TPU v7x, 32 devices: a whole 2x2x4 slice. The times are simulated.
32 devices in a mesh: tm: 4 (over z), space: 8 (over y, x, core).
Axes of the slice: x: 2, y: 2, z: 4, core: 2. Of those that a mesh axis runs over, the one named last changes fastest.
Arguments:
- queries: bfloat16 [512, 1024], P('tm', 'space'), may hold values from -150 to 150
- keys: bfloat16 [4096, 1024], P('tm', 'space'), may hold values from -6 to 6
- values: bfloat16 [4096, 1024], P('tm', 'space'), may hold values from -6 to 6
- saved_out: bfloat16 [512, 1024], P('tm', 'space'), may hold values from -6 to 6
- out_grad: bfloat16 [512, 5120], P('tm', 'space'), may hold values from -6 to 6
- proj_weight: bfloat16 [1024, 5120], P('space'), may hold values from -0.1875 to 0.1875
- gate_table: float32 [16, 5120], replicated, may hold values from 0.1 to 1.9
- noise_levels: int32 [8], replicated, may hold values from 0 to 15
- clip_lengths: int32 [4], replicated, may hold values from 1 to 4, 8 in all
Outputs:
- query_grad: bfloat16 [512, 1024], P('tm', 'space')
- key_grad: bfloat16 [4096, 1024], P('tm', 'space')
- value_grad: bfloat16 [4096, 1024], P('tm', 'space')
- weight_grad: float32 [1024, 5120], P('space', 'tm')
- gate_grad: float32 [16, 5120], replicated
All inputs are finite; a program needn't handle non-finite values.
Results may differ from a plain program's by a relative error of at most 0.0065.
Values may be sent and summed in bfloat16 or wider, within the bound.
No kernel may reach another device: no remote copies, remote signals or barrier semaphores. Data moves between devices by JAX's collectives and lax.ppermute only.
A program may use at most 64 MiB of HBM per device.

v0:
```python
import math

import jax
import jax.numpy as jnp
from jax import lax
from jax.sharding import PartitionSpec as P

HD = 128
FR = 2
SPF = 512
QF = 64
LEVELS = 16


NEG_BIG = -1e30


def merged(array, axis, combine):
    everything = jax.tree.map(lambda part: lax.all_gather(part, axis), array)
    leading = jax.tree.map(lambda part: part[0], everything)

    def lap(k, so_far):
        return combine(so_far, jax.tree.map(lambda part: part[k], everything))

    return lax.fori_loop(1, lax.axis_size(axis), lap, leading)


def clip_index(clip_lengths, frame_ids):
    bounds = jnp.cumsum(clip_lengths)
    return jnp.sum((frame_ids[:, None] >= bounds[None, :]).astype(jnp.int32), axis=1)


def lookup_small(indices, table_ids, table):
    hot = (indices[:, None] == table_ids[None, :]).astype(jnp.int32)
    return jnp.sum(hot * table[None, :], axis=1)


def merge_stats(first, second):
    top = jnp.maximum(first[0], second[0])
    total = first[1] * jnp.exp(first[0] - top) + second[1] * jnp.exp(second[0] - top)
    return (top, total)


def body(
    queries, keys, values, saved_out, out_grad, proj_weight, gate_table, noise_levels, clip_lengths
):
    rank = lax.axis_index("tm")
    q_rows = queries.shape[0]
    k_rows = keys.shape[0]
    heads = queries.shape[1] // HD
    scale = 1.0 / math.sqrt(HD)
    frame_count = noise_levels.shape[0]
    frame_ids = jnp.arange(frame_count, dtype=jnp.int32)
    clip_of = clip_index(clip_lengths, frame_ids)
    my_frames = rank * FR + jnp.arange(q_rows, dtype=jnp.int32) // QF
    my_levels = lookup_small(my_frames, frame_ids, noise_levels)
    level_hot = (my_levels[:, None] == jnp.arange(LEVELS, dtype=jnp.int32)[None, :]).astype(
        jnp.float32
    )
    gate_rows = jnp.dot(level_hot, gate_table, precision=lax.Precision.HIGHEST)
    full_grad = lax.all_gather(out_grad, "space", axis=1, tiled=True)
    grad_wide = full_grad.astype(jnp.float32)
    gated = (gate_rows * grad_wide).astype(jnp.bfloat16)
    head_grad = lax.dot_general(
        gated, proj_weight, (((1,), (1,)), ((), ())), preferred_element_type=jnp.float32
    ).astype(jnp.bfloat16)
    mixed = jnp.dot(saved_out, proj_weight, preferred_element_type=jnp.float32)
    gate_part = jnp.dot(level_hot.T, grad_wide * mixed, precision=lax.Precision.HIGHEST)
    gate_grad = lax.psum(gate_part, ("tm", "space"))
    all_queries, all_grads, all_saved = (
        lax.all_gather(queries, "tm", axis=0, tiled=True),
        lax.all_gather(head_grad, "tm", axis=0, tiled=True),
        lax.all_gather(saved_out, "tm", axis=0, tiled=True),
    )
    total_rows = all_queries.shape[0]
    q_heads = all_queries.reshape(total_rows, heads, HD)
    g_heads = all_grads.reshape(total_rows, heads, HD)
    delta = jnp.sum(
        g_heads.astype(jnp.float32) * all_saved.reshape(total_rows, heads, HD).astype(jnp.float32),
        axis=2,
    )
    k_heads = keys.reshape(k_rows, heads, HD)
    v_heads = values.reshape(k_rows, heads, HD)
    key_frames = rank * FR + jnp.arange(k_rows, dtype=jnp.int32) // SPF
    key_clips = lookup_small(key_frames, frame_ids, clip_of)
    block = min(512, total_rows)
    blocks = total_rows // block
    last_frame = rank * FR + FR - 1

    def block_setup(start):
        query_frames = (start + jnp.arange(block, dtype=jnp.int32)) // QF
        query_clips = lookup_small(query_frames, frame_ids, clip_of)
        visible = (key_frames[None, :] >= query_frames[:, None]) & (
            key_clips[None, :] == query_clips[:, None]
        )
        q_block = lax.slice_in_dim(q_heads, start, start + block, axis=0)
        scores = (
            jnp.einsum("qhd,khd->hqk", q_block, k_heads, preferred_element_type=jnp.float32) * scale
        )
        masked = jnp.where(visible[None, :, :], scores, NEG_BIG)
        return (visible, q_block, masked)

    top_list = []
    total_list = []
    for index in range(blocks):
        start = index * block
        needed = start // QF <= last_frame

        def live_stats(start=start):
            visible, q_block, masked = block_setup(start)
            top = jnp.max(masked, axis=2)
            total = jnp.sum(
                jnp.where(visible[None, :, :], jnp.exp(masked - top[:, :, None]), 0.0), axis=2
            )
            return (top.T, total.T)

        def dead_stats():
            return (
                jnp.full((block, heads), NEG_BIG, jnp.float32),
                jnp.zeros((block, heads), jnp.float32),
            )

        top_block, total_block = lax.cond(needed, live_stats, dead_stats)
        top_list.append(top_block)
        total_list.append(total_block)
    top_part = jnp.concatenate(top_list, axis=0)
    total_part = jnp.concatenate(total_list, axis=0)
    top_all, total_all = merged((top_part, total_part), "tm", merge_stats)
    lse = top_all + jnp.log(total_all)
    key_acc = jnp.zeros((k_rows, heads, HD), jnp.float32)
    value_acc = jnp.zeros((k_rows, heads, HD), jnp.float32)
    query_list = []
    for index in range(blocks):
        start = index * block
        needed = start // QF <= last_frame

        def live_grads(start=start):
            visible, q_block, masked = block_setup(start)
            lse_block = lax.slice_in_dim(lse, start, start + block, axis=0).T
            delta_block = lax.slice_in_dim(delta, start, start + block, axis=0).T
            g_block = lax.slice_in_dim(g_heads, start, start + block, axis=0)
            probs = jnp.where(visible[None, :, :], jnp.exp(masked - lse_block[:, :, None]), 0.0)
            probs_low = probs.astype(jnp.bfloat16)
            value_add = jnp.einsum(
                "hqk,qhd->khd", probs_low, g_block, preferred_element_type=jnp.float32
            )
            prob_grad = jnp.einsum(
                "qhd,khd->hqk", g_block, v_heads, preferred_element_type=jnp.float32
            )
            score_grad = (probs * (prob_grad - delta_block[:, :, None])).astype(jnp.bfloat16)
            query_part = (
                jnp.einsum("hqk,khd->qhd", score_grad, k_heads, preferred_element_type=jnp.float32)
                * scale
            )
            key_add = (
                jnp.einsum("hqk,qhd->khd", score_grad, q_block, preferred_element_type=jnp.float32)
                * scale
            )
            return (key_add, value_add, query_part)

        def dead_grads():
            return (
                jnp.zeros((k_rows, heads, HD), jnp.float32),
                jnp.zeros((k_rows, heads, HD), jnp.float32),
                jnp.zeros((block, heads, HD), jnp.float32),
            )

        key_add, value_add, query_part = lax.cond(needed, live_grads, dead_grads)
        key_acc = key_acc + key_add
        value_acc = value_acc + value_add
        query_list.append(query_part)
    query_terms = jnp.concatenate(query_list, axis=0).reshape(total_rows, heads * HD)
    query_full = lax.psum_scatter(query_terms, "tm", scatter_dimension=0, tiled=True)
    weight_terms = lax.dot_general(
        saved_out, gated, (((0,), (0,)), ((), ())), preferred_element_type=jnp.float32
    )
    weight_grad = lax.psum_scatter(weight_terms, "tm", scatter_dimension=1, tiled=True)
    query_grad = query_full.astype(jnp.bfloat16)
    key_grad = key_acc.reshape(k_rows, heads * HD).astype(jnp.bfloat16)
    value_grad = value_acc.reshape(k_rows, heads * HD).astype(jnp.bfloat16)
    return (query_grad, key_grad, value_grad, weight_grad, gate_grad)


def solution(mesh):
    return jax.shard_map(
        body,
        mesh=mesh,
        in_specs=(
            P("tm", "space"),
            P("tm", "space"),
            P("tm", "space"),
            P("tm", "space"),
            P("tm", "space"),
            P("space", None),
            P(),
            P(),
            P(),
        ),
        out_specs=(P("tm", "space"), P("tm", "space"), P("tm", "space"), P("space", "tm"), P()),
        check_vma=False,
    )
```

profile of v0, /device:TPU:0, one launch (start us, length us, event | category | flops | bytes accessed | tf_op | source)
XLA Modules:
  0.0 299.0 jit_solution(17682861243445928828)
XLA Ops:
  8.0 0.8 reduce-window.8
  8.8 15.3 %all_gather.24 = bf16[512,128]{1,0:T(8,128)(2,1)S(1)} all-gather(bf16[128,128]{1,0:T(8,128)(2,1)} %param.15), channel_id=1, replica_groups=mesh['tm'=4,'space'=8] {'tm'}, dimensions={0}, use_global_device_ids=true | all-gather | bytes 163840 | tf_op jit(solution)/shard_map/all_gather | solution.py:71
  24.3 3.9 %conditional.2 = (f32[512,1]{0,1:T(1,128)}, f32[512,1]{0,1:T(1,128)S(1)}) conditional(s32[]{:T(128)} %convert_element_type.59, () %tuple.54, (s32[1024]{0:T(1024)S(1)}, s32[1024]{0:T(1024)S(1)}, s32[8]{0:T(128)S(1)}, s32[8]{0:T(128)S(1)}, bf16[512,1,128]{2,0,1:T(8,128)(2,1)S(1)}, /*index=5*/bf16[1024,1,128]{2,0,1:T(8,128)(2,1)}) %tuple.93), branch_computations={%region_3.4_spmd, %region_4.8_spmd} | conditional | flops 141572608 | bytes 4624464 | solution.py:123
  24.4 2.3 fusion
  26.7 1.5 select_reduce_fusion
  28.1 12.0 %all-gather = f32[2048,1]{0,1:T(1,128)S(1)} all-gather(f32[512,1]{0,1:T(1,128)} %get-tuple-element.231), channel_id=2, replica_groups=mesh['tm'=4,'space'=8] {'tm'}, dimensions={0}, use_global_device_ids=true | all-gather | bytes 10240 | tf_op jit(solution)/shard_map/all_gather | solution.py:19
  40.2 11.9 %all-gather.1 = f32[2048,1]{0,1:T(1,128)S(1)} all-gather(f32[512,1]{0,1:T(1,128)S(1)} %get-tuple-element.232), channel_id=3, replica_groups=mesh['tm'=4,'space'=8] {'tm'}, dimensions={0}, use_global_device_ids=true | all-gather | bytes 10240 | tf_op jit(solution)/shard_map/all_gather | solution.py:19
  52.0 13.3 %all_gather.31 = bf16[512,128]{1,0:T(8,128)(2,1)S(1)} all-gather(bf16[128,128]{1,0:T(8,128)(2,1)S(1)} %copy-done.4), channel_id=1, replica_groups=mesh['tm'=4,'space'=8] {'tm'}, dimensions={0}, use_global_device_ids=true | all-gather | bytes 163840 | tf_op jit(solution)/shard_map/all_gather | solution.py:73
  65.7 2.6 fusion.19
  68.8 13.3 %all_gather.30 = bf16[512,128]{1,0:T(8,128)(2,1)S(1)} all-gather(bf16[128,128]{1,0:T(8,128)(2,1)S(1)} %convolution_convert_fusion.1), channel_id=1, replica_groups=mesh['tm'=4,'space'=8] {'tm'}, dimensions={0}, use_global_device_ids=true | all-gather | bytes 163840 | tf_op jit(solution)/shard_map/all_gather | solution.py:72
  82.2 4.3 %conditional.3 = (f32[512,1,128]{2,0,1:T(8,128)S(1)}, bf16[1024,128]{1,0:T(8,128)(2,1)}, bf16[1024,128]{1,0:T(8,128)(2,1)}) conditional(s32[]{:T(128)} %convert_element_type.59, () %tuple.53, (s32[1024]{0:T(1024)S(1)}, s32[1024]{0:T(1024)S(1)}, s32[8]{0:T(128)S(1)}, s32[8]{0:T(128)S(1)}, bf16[512,1,128]{2,0,1:T(8,128)(2,1)S(1)}, ...), branch_computations={%region_11.12_spmd, %region_12.15_spmd} | conditional | flops 677461504 | bytes 12089432 | solution.py:168
  82.5 0.8 exponential_select_fusion
  83.3 1.2 convolution_convert_fusion
  84.9 1.2 fusion.9
  86.6 0.7 copy-done.2
  87.4 2.1 convolution_bitcast_fusion
  89.5 1.2 copy-done.1
  91.2 1.7 fusion.20
  93.0 13.0 %reduce-scatter.3.cloned.1.call-done = f32[128,128]{1,0:T(8,128)} async-done(((f32[512,128]{1,0:T(8,128)}), f32[128,128]{1,0:T(8,128)}) %reduce-scatter.3.cloned.1.call-update) | async-done | bytes 65552 | tf_op jit(solution)/shard_map/reduce_scatter | solution.py:173
  106.0 1.5 convert_element_type.66
  107.4 51.4 %reduce-scatter.5.cloned.1.call-done = f32[128,1280]{0,1:T(8,128)} async-done(((f32[128,5120]{0,1:T(8,128)}), f32[128,1280]{0,1:T(8,128)}) %reduce-scatter.5.cloned.1.call-update) | async-done | bytes 655376 | tf_op jit(solution)/shard_map/reduce_scatter | solution.py:177
  158.8 2.2 copy.19
  161.0 129.8 %all-reduce.2.cloned.1.call-done = f32[16,5120]{1,0:T(8,128)} async-done(((f32[16,5120]{1,0:T(8,128)}), f32[16,5120]{1,0:T(8,128)}) %all-reduce.2.cloned.1.call-update) | async-done | bytes 327696 | tf_op jit(solution)/shard_map/psum | solution.py:69
  290.8 1.7 copy.40
  (48 shorter events, 3.7 us)
Async XLA Ops:
  7.2 61.1 %copy-start = (bf16[128,5120]{1,0:T(8,128)(2,1)S(1)}, bf16[128,5120]{1,0:T(8,128)(2,1)}, u32[]{:S(2)}) copy-start(bf16[128,5120]{1,0:T(8,128)(2,1)} %param.20) | copy-start | bytes 3932164
  7.2 58.5 %all-gather.4.cloned.1.call-start = ((), (), s32[]{:S(2)}) async-start(), calls=%async_computation.2 | async-start | bytes 1474560 | tf_op jit(solution)/shard_map/all_gather | solution.py:61
  7.9 98.1 %reduce-scatter.3.cloned.1.call-start = ((), (), s32[]{:S(2)}) async-start(), calls=%async_computation.3 | async-start | bytes 327680 | tf_op jit(solution)/shard_map/reduce_scatter | solution.py:173
  24.2 27.8 %copy-start.4 = (bf16[128,128]{1,0:T(8,128)(2,1)S(1)}, bf16[128,128]{1,0:T(8,128)(2,1)}, u32[]{:S(2)}) copy-start(bf16[128,128]{1,0:T(8,128)(2,1)} %param.18) | copy-start | bytes 98308
  24.3 41.1 %copy-start.7 = (s32[8]{0:T(128)S(1)}, s32[8]{0:T(128)}, u32[]{:S(2)}) copy-start(s32[8]{0:T(128)} %param.22) | copy-start | bytes 100
  24.3 41.4 %copy-start.3 = (f32[16,5120]{1,0:T(8,128)S(1)}, f32[16,5120]{1,0:T(8,128)}, u32[]{:S(2)}) copy-start(f32[16,5120]{1,0:T(8,128)} %param.21) | copy-start | bytes 983044
  68.3 13.9 %copy-start.5 = (bf16[1024,128]{1,0:T(8,128)(2,1)S(1)}, bf16[1024,128]{1,0:T(8,128)(2,1)}, u32[]{:S(2)}) copy-start(bf16[1024,128]{1,0:T(8,128)(2,1)} %param.17) | copy-start | bytes 786436
  68.3 13.9 %copy-start.6 = (bf16[1024,128]{1,0:T(8,128)(2,1)S(1)}, bf16[1024,128]{1,0:T(8,128)(2,1)}, u32[]{:S(2)}) copy-start(bf16[1024,128]{1,0:T(8,128)(2,1)} %param.16) | copy-start | bytes 786436
  86.6 0.7 copy-start.2
  87.3 71.5 %reduce-scatter.5.cloned.1.call-start = ((), (), s32[]{:S(2)}) async-start(), calls=%async_computation.4 | async-start | bytes 3276800 | tf_op jit(solution)/shard_map/reduce_scatter | solution.py:177
  89.4 1.3 copy-start.1
  89.4 201.3 %all-reduce.2.cloned.1.call-start = ((), (), s32[]{:S(2)}) async-start(), calls=%async_computation.5 | async-start | bytes 655360 | tf_op jit(solution)/shard_map/psum | solution.py:69
Sparse Core Ops, SparseCore 0:
  9.9 27.3 all-gather.3
  87.4 18.5 reduce-scatter.2
  108.4 50.3 reduce-scatter.4
  165.5 125.2 all-reduce.1
where the time goes:
time: 300 us; the launch traced here: 299 us
  waiting for transfers between devices  195 us (65%)
  blocking collectives  65.8 us (22%)
  between operations  14 us (5%)
  matrix products  13.7 us (5%)
  local copies, waits for them, and re-layouts  5.86 us (2%)
  other arithmetic  4.5 us (2%)
    psum x1, waiting for transfers between devices, body(): gate_grad = lax.psum(gate_part, ('tm', 'space'))  130 us
    reduce_scatter x1, waiting for transfers between devices, body(): lax.psum_scatter(weight_terms, 'tm', scatter_dimension=1, tiled=True)  51.4 us
    all_gather x2, blocking collectives, merged(): everything = jax.tree.map(lambda part: lax.all_gather(part, axis), array)  23.9 us
    all_gather x1, blocking collectives, body(): lax.all_gather(queries, 'tm', axis=0, tiled=True)  15.3 us
    all_gather x1, blocking collectives, body(): lax.all_gather(head_grad, 'tm', axis=0, tiled=True)  13.3 us
    all_gather x1, blocking collectives, body(): lax.all_gather(saved_out, 'tm', axis=0, tiled=True)  13.3 us
    reduce_scatter x1, waiting for transfers between devices, body(): lax.psum_scatter(query_terms, 'tm', scatter_dimension=0, tiled=True)  13 us
  transfers between devices with their start and end apart: 4, of which 3 were waited for; matrix products, arithmetic and copies ran while one was open for 4% of the time, Pallas kernels for 0%

commit v1 on v0

v1 whole, which is shorter than its diff:
```python
import functools
import math

import jax
import jax.numpy as jnp
from jax import lax
from jax.experimental import pallas as pl
from jax.experimental.pallas import tpu as pltpu
from jax.sharding import PartitionSpec as P

HD = 128
SPF = 512
QF = 64
NEG_BIG = -1e30
SCALE = 1.0 / math.sqrt(HD)
VMEM_LIMIT = 48 * 1024 * 1024


def dot(a, b, on_a, on_b):
    return lax.dot_general(
        a, b, (((on_a,), (on_b,)), ((), ())), preferred_element_type=jnp.float32
    )


def take_columns(ref, shard, width):
    if len(ref.shape) == 3:
        return ref[shard]
    return ref[:, pl.ds(pl.multiple_of(shard * width, 128), width)]


def gate_row(gate_ref, shard, width, level):
    if len(gate_ref.shape) == 3:
        return gate_ref[shard, pl.ds(level, 1), :]
    return gate_ref[pl.ds(level, 1), pl.ds(pl.multiple_of(shard * width, 128), width)]


def gate_rows(piece, levels_ref, gate_ref, owner, shard, frames):
    wide = piece.astype(jnp.float32)
    rows = []
    for r in range(frames):
        row = gate_row(gate_ref, shard, piece.shape[1], levels_ref[owner * frames + r])
        rows.append((wide[r * QF : (r + 1) * QF] * row).astype(jnp.bfloat16))
    return wide, jnp.concatenate(rows, axis=0)


def head_kernel(n_s, frames, levels_ref, saved_ref, w_ref, gate_ref, *refs):
    pieces, (head_ref, terms_ref) = refs[:n_s], refs[n_s:]
    t, s = lax.axis_index("tm"), lax.axis_index("space")
    width = pieces[0].shape[1]
    saved = saved_ref[...]
    head = jnp.zeros(head_ref.shape, jnp.float32)
    for j in range(n_s):
        shard = s ^ j
        weight = take_columns(w_ref, shard, width)
        wide, gated = gate_rows(pieces[j][...], levels_ref, gate_ref, t, shard, frames)
        head = head + dot(gated, weight, 1, 1)
        product = wide * dot(saved, weight, 1, 0)
        for r in range(frames):
            term = jnp.sum(product[r * QF : (r + 1) * QF], axis=0, keepdims=True)
            if len(terms_ref.shape) == 3:
                terms_ref[shard, r : r + 1, :] = term
            else:
                terms_ref[r : r + 1, pl.ds(pl.multiple_of(shard * width, 128), width)] = term
    head_ref[...] = head.astype(jnp.bfloat16)


def heads_sum_kernel(n_s, *refs):
    pieces, out_ref, held = refs[:n_s], refs[n_s], refs[n_s + 1]
    s = lax.axis_index("space")
    for j in range(n_s):
        held[s ^ j] = pieces[j][...]
    total = held[0]
    for j in range(1, n_s):
        total = total + held[j]
    out_ref[...] = total


def levels_kernel(n_t, frames, levels_ref, *refs):
    pieces, out_ref, held = refs[:n_t], refs[n_t], refs[n_t + 1]
    t = lax.axis_index("tm")
    for k in range(n_t):
        held[t ^ k] = pieces[k][...]
    spot = lax.broadcasted_iota(jnp.int32, out_ref.shape, len(out_ref.shape) - 2)
    total = jnp.zeros(out_ref.shape, jnp.float32)
    for f in range(n_t * frames):
        r = f % frames
        row = held[f // frames, ..., r : r + 1, :]
        total = total + jnp.where(spot == levels_ref[f], row, 0.0)
    out_ref[...] = total


def weight_kernel(n_t, frames, levels_ref, gate_ref, *refs):
    n_s = 2 * n_t
    saved_refs, pieces = refs[:n_t], refs[n_t : n_t + n_s]
    out_ref, held = refs[n_t + n_s], refs[n_t + n_s + 1]
    t, s = lax.axis_index("tm"), lax.axis_index("space")
    chip, core = s // 2, s % 2
    width = pieces[0].shape[1]
    for k in range(n_t):
        held[k] = saved_refs[k][...]
    saved = jnp.concatenate([held[chip ^ k] for k in range(n_t)], axis=0)
    for f in range(2):
        half = core ^ f
        rows = [
            gate_rows(pieces[2 * k + f][...], levels_ref, gate_ref, t ^ chip ^ k, 2 * t + half, frames)[1]
            for k in range(n_t)
        ]
        result = dot(saved, jnp.concatenate(rows, axis=0), 0, 0)
        for h in range(2):

            @pl.when(half == h)
            def _():
                out_ref[:, h * width : (h + 1) * width] = result


def clip_numbers(clips_ref):
    bounds = []
    so_far = 0
    for c in range(clips_ref.shape[0]):
        so_far = so_far + clips_ref[c]
        bounds.append(so_far)
    return lambda frame: sum((frame >= bound).astype(jnp.int32) for bound in bounds)


def bias_row(clip_of, t, k, key_frame, frames, rows):
    lane = lax.broadcasted_iota(jnp.int32, (1, rows), 1)
    row = jnp.full((1, rows), NEG_BIG, jnp.float32)
    for r in range(frames):
        frame = (t ^ k) * frames + r
        visible = (key_frame >= frame) & (clip_of(key_frame) == clip_of(frame))
        value = jnp.where(visible, 0.0, NEG_BIG).astype(jnp.float32)
        row = jnp.where((lane >= r * QF) & (lane < (r + 1) * QF), value, row)
    return row


def stats_kernel(n_t, frames, clips_ref, keys_ref, *refs):
    queries, stats_ref = refs[:n_t], refs[n_t]
    t = lax.axis_index("tm")
    clip_of = clip_numbers(clips_ref)
    rows = queries[0].shape[0]
    for p in range(0, n_t, 2):
        q = jnp.concatenate([queries[p][...], queries[p + 1][...]], axis=0)
        scores = []
        for kf in range(frames):
            bias = jnp.concatenate(
                [bias_row(clip_of, t, k, t * frames + kf, frames, rows) for k in (p, p + 1)], axis=1
            )
            scores.append(dot(keys_ref[kf * SPF : (kf + 1) * SPF, :], q, 1, 1) * SCALE + bias)
        top = functools.reduce(jnp.maximum, [jnp.max(x, axis=0, keepdims=True) for x in scores])
        total = sum(jnp.sum(jnp.exp(x - top), axis=0, keepdims=True) for x in scores)
        stats_ref[0:1, p * rows : (p + 2) * rows] = top
        stats_ref[1:2, p * rows : (p + 2) * rows] = total


def grads_kernel(n_t, frames, clips_ref, keys_ref, values_ref, *refs):
    queries, grads, saved, stats = (refs[i * n_t : (i + 1) * n_t] for i in range(4))
    key_ref, value_ref = refs[4 * n_t : 4 * n_t + 2]
    query_refs = refs[4 * n_t + 2 : 5 * n_t + 2]
    key_acc, value_acc = refs[5 * n_t + 2 :]
    t = lax.axis_index("tm")
    clip_of = clip_numbers(clips_ref)
    rows = queries[0].shape[0]
    ones = jnp.ones((8, HD), jnp.float32)
    keys_t = jnp.transpose(keys_ref[...])
    for p in range(0, n_t, 2):
        q = jnp.concatenate([queries[p][...], queries[p + 1][...]], axis=0)
        g = jnp.concatenate([grads[p][...], grads[p + 1][...]], axis=0)
        o = jnp.concatenate([saved[p][...], saved[p + 1][...]], axis=0)
        delta = lax.dot_general(
            ones,
            g.astype(jnp.float32) * o.astype(jnp.float32),
            (((1,), (1,)), ((), ())),
            precision=lax.Precision.HIGHEST,
            preferred_element_type=jnp.float32,
        )[0:1]
        lse = []
        for i in (p, p + 1):
            tops = [stats[k][0:1, (i ^ k) * rows : ((i ^ k) + 1) * rows] for k in range(n_t)]
            sums = [stats[k][1:2, (i ^ k) * rows : ((i ^ k) + 1) * rows] for k in range(n_t)]
            top = functools.reduce(jnp.maximum, tops)
            lse.append(top + jnp.log(sum(b * jnp.exp(a - top) for a, b in zip(tops, sums))))
        lse = jnp.concatenate(lse, axis=1)
        query_part = None
        for kf in range(frames):
            span = slice(kf * SPF, (kf + 1) * SPF)
            bias = jnp.concatenate(
                [bias_row(clip_of, t, k, t * frames + kf, frames, rows) for k in (p, p + 1)], axis=1
            )
            probs = jnp.exp(dot(keys_ref[span, :], q, 1, 1) * SCALE + (bias - lse))
            score_grad = (probs * (dot(values_ref[span, :], g, 1, 1) - delta)).astype(jnp.bfloat16)
            value_add = dot(probs.astype(jnp.bfloat16), g, 1, 0)
            key_add = dot(score_grad, q, 1, 0)
            if p > 0:
                value_add = value_add + value_acc[span, :]
                key_add = key_add + key_acc[span, :]
            if p + 2 < n_t:
                value_acc[span, :] = value_add
                key_acc[span, :] = key_add
            else:
                value_ref[span, :] = value_add.astype(jnp.bfloat16)
                key_ref[span, :] = (key_add * SCALE).astype(jnp.bfloat16)
            part = dot(keys_t[:, span], score_grad, 1, 0)
            query_part = part if query_part is None else query_part + part
        query_refs[p][...] = query_part[:, :rows]
        query_refs[p + 1][...] = query_part[:, rows:]


def query_kernel(n_t, *refs):
    total = refs[0][...]
    for k in range(1, n_t):
        total = total + refs[k][...]
    refs[n_t][...] = jnp.transpose(total * SCALE).astype(jnp.bfloat16)


def call(kernel, in_smem, args, out_shape, scratch=(), flops=0):
    whole = pl.BlockSpec(memory_space=pltpu.VMEM)
    single = not isinstance(out_shape, (list, tuple))
    nbytes = sum(a.size * a.dtype.itemsize for a in args)
    return pl.pallas_call(
        kernel,
        out_shape=out_shape,
        in_specs=[pl.BlockSpec(memory_space=pltpu.SMEM)] * in_smem + [whole] * (len(args) - in_smem),
        out_specs=whole if single else [whole] * len(out_shape),
        scratch_shapes=list(scratch),
        compiler_params=pltpu.CompilerParams(vmem_limit_bytes=VMEM_LIMIT),
        cost_estimate=pl.CostEstimate(flops=flops, bytes_accessed=nbytes, transcendentals=0),
    )(*args)


def body(
    queries, keys, values, saved_out, out_grad, proj_weight, gate_table, noise_levels, clip_lengths
):
    n_t, n_s = lax.axis_size("tm"), lax.axis_size("space")
    chips = n_s // 2
    rows, width = out_grad.shape
    k_rows = keys.shape[0]
    frames = rows // QF
    levels, columns = gate_table.shape
    shape = jax.ShapeDtypeStruct

    def over_chips(x, k):
        return lax.ppermute(x, "space", [(s, s ^ (2 * k)) for s in range(n_s)])

    def over_cores(x):
        return lax.ppermute(x, "space", [(s, s ^ 1) for s in range(n_s)])

    def over_time(x, k, up_only=False, down_only=False):
        pairs = [(t, t ^ k) for t in range(n_t)]
        if up_only:
            pairs = [(a, b) for a, b in pairs if a < b]
        if down_only:
            pairs = [(a, b) for a, b in pairs if a > b]
        return lax.ppermute(x, "tm", pairs)

    def plane_gather(x):
        same_core = [x] + [over_chips(x, k) for k in range(1, chips)]
        return [y for piece in same_core for y in (piece, over_cores(piece))]

    pieces = plane_gather(out_grad)
    queries_all = [queries] + [over_time(queries, k, up_only=True) for k in range(1, n_t)]
    saved_all = [saved_out] + [over_time(saved_out, k) for k in range(1, n_t)]
    moves = [
        (t * n_s + 2 * c + e, c * n_s + 2 * (c ^ t) + e)
        for t in range(n_t)
        for c in range(chips)
        for e in range(2)
    ]
    moved = lax.ppermute(out_grad, ("tm", "space"), moves)
    row_pieces = plane_gather(moved)

    cut = width % 128 != 0
    w_table, g_table = proj_weight, gate_table
    if cut:
        w_table = proj_weight.reshape(HD, n_s, width).transpose(1, 0, 2)
        g_table = gate_table.reshape(levels, n_s, width).transpose(1, 0, 2)
    terms_shape = (n_s, frames, width) if cut else (frames, columns)

    stats = call(
        functools.partial(stats_kernel, n_t, frames),
        1,
        [clip_lengths, keys] + queries_all,
        shape((2, n_t * rows), jnp.float32),
        flops=2 * n_t * rows * k_rows * HD,
    )
    stats_all = [stats] + [over_time(stats, k) for k in range(1, n_t)]

    head_grad, terms = call(
        functools.partial(head_kernel, n_s, frames),
        1,
        [noise_levels, saved_out, w_table, g_table] + pieces,
        [shape((rows, HD), jnp.bfloat16), shape(terms_shape, jnp.float32)],
        flops=4 * rows * columns * HD,
    )
    grads_all = [head_grad] + [over_time(head_grad, k, up_only=True) for k in range(1, n_t)]
    terms_all = [terms] + [
        lax.ppermute(terms, "space", [(s, s ^ j) for s in range(n_s)]) for j in range(1, n_s)
    ]
    terms_sum = call(
        functools.partial(heads_sum_kernel, n_s),
        0,
        terms_all,
        shape(terms_shape, jnp.float32),
        [pltpu.VMEM((n_s,) + terms_shape, jnp.float32)],
    )
    sums_all = [terms_sum] + [over_time(terms_sum, k) for k in range(1, n_t)]

    outs = call(
        functools.partial(grads_kernel, n_t, frames),
        1,
        [clip_lengths, keys, values] + queries_all + grads_all + saved_all + stats_all,
        [shape((k_rows, HD), jnp.bfloat16)] * 2 + [shape((HD, rows), jnp.float32)] * n_t,
        [pltpu.VMEM((k_rows, HD), jnp.float32)] * 2,
        flops=10 * n_t * rows * k_rows * HD,
    )
    key_grad, value_grad, query_parts = outs[0], outs[1], outs[2:]
    query_terms = [query_parts[0]] + [
        over_time(query_parts[k], k, down_only=True) for k in range(1, n_t)
    ]

    weight_grad = call(
        functools.partial(weight_kernel, n_t, frames),
        1,
        [noise_levels, g_table] + saved_all + row_pieces,
        shape((HD, 2 * width), jnp.float32),
        [pltpu.VMEM((n_t, rows, HD), jnp.bfloat16)],
        flops=4 * n_t * rows * width * HD,
    )
    gate_grad = call(
        functools.partial(levels_kernel, n_t, frames),
        1,
        [noise_levels] + sums_all,
        shape((n_s, levels, width) if cut else (levels, columns), jnp.float32),
        [pltpu.VMEM((n_t,) + terms_shape, jnp.float32)],
    )
    if cut:
        gate_grad = gate_grad.transpose(1, 0, 2).reshape(levels, columns)
    query_grad = call(
        functools.partial(query_kernel, n_t),
        0,
        query_terms,
        shape((rows, HD), jnp.bfloat16),
    )
    return (query_grad, key_grad, value_grad, weight_grad, gate_grad)


def solution(mesh):
    return jax.shard_map(
        body,
        mesh=mesh,
        in_specs=(
            P("tm", "space"),
            P("tm", "space"),
            P("tm", "space"),
            P("tm", "space"),
            P("tm", "space"),
            P("space", None),
            P(),
            P(),
            P(),
        ),
        out_specs=(P("tm", "space"), P("tm", "space"), P("tm", "space"), P("space", "tm"), P()),
        check_vma=False,
    )
```

time: 300 us -> 104 us (0.35)
  waiting for transfers between devices: 195 us -> 22.7 us
  blocking collectives: 65.8 us -> 0 us
  starting transfers between devices: 0.16 us -> 63 us
  matrix products: 13.7 us -> 0 us
  between operations: 14 us -> 0.9 us
  Pallas kernels: 0 us -> 10.3 us
  other arithmetic: 4.5 us -> 0 us
    psum x1 -> x0, waiting for transfers between devices: 130 us -> none  [body(): gate_grad = lax.psum(gate_part, ('tm', 'space'))]
    all_gather x5 -> x0, blocking collectives: 65.8 us -> none  [the longest x2 23.9 us: merged(): everything = jax.tree.map(lambda part: lax.all_gather(part, axis), array)]
    reduce_scatter x2 -> x0, waiting for transfers between devices: 64.4 us -> none  [the longest x1 51.4 us: body(): lax.psum_scatter(weight_terms, 'tm', scatter_dimension=1, tiled=True)]
    ppermute x0 -> x40, starting transfers between devices: none -> 63 us  [the longest x18 45 us: over_time(): return lax.ppermute(x, 'tm', pairs)]
    ppermute x0 -> x40, waiting for transfers between devices: none -> 22.7 us  [the longest x18 22.3 us: over_time(): return lax.ppermute(x, 'tm', pairs)]
    dot_general x11 -> x0, matrix products: 13.7 us -> none  [the longest x2 3.05 us: block_setup(): jnp.einsum('qhd,khd->hqk', q_block, k_heads, preferred_element_type=jnp.f...]
    pallas_call x0 -> x7, Pallas kernels: none -> 10.3 us  [call(): pl.pallas_call(kernel, out_shape=out_shape, in_specs=[pl.BlockSpec(memory...]
    unnamed x18 -> x30, local copies, waits for them, and re-layouts: 5.86 us -> 7.01 us
  transfers between devices with their start and end apart: 4 -> 40, of which waited for: 3 -> 9; matrix products, arithmetic and copies ran while one was open for 4% -> 0% of each run, Pallas kernels for 0% -> 8%
where the time goes in v1:
time: 104 us
  starting transfers between devices  63 us (61%)
  waiting for transfers between devices  22.7 us (22%)
  Pallas kernels  10.3 us (10%)
  local copies, waits for them, and re-layouts  7.01 us (7%)
    ppermute x18, starting transfers between devices, over_time(): return lax.ppermute(x, 'tm', pairs)  45 us
    ppermute x18, waiting for transfers between devices, over_time(): return lax.ppermute(x, 'tm', pairs)  22.3 us
    pallas_call x7, Pallas kernels, call(): pl.pallas_call(kernel, out_shape=out_shape, in_specs=[pl.BlockSpec(memory...  10.3 us
    ppermute x6, starting transfers between devices, over_chips(): return lax.ppermute(x, 'space', [(s, s ^ 2 * k) for s in range(n_s)])  7.77 us
    unnamed x30, local copies, waits for them, and re-layouts  7.01 us
    ppermute x7, starting transfers between devices, body(): lax.ppermute(terms, 'space', [(s, s ^ j) for s in range(n_s)])  6.55 us
    ppermute x8, starting transfers between devices, over_cores(): return lax.ppermute(x, 'space', [(s, s ^ 1) for s in range(n_s)])  2.09 us
  transfers between devices with their start and end apart: 40, of which 9 were waited for; matrix products, arithmetic and copies ran while one was open for 0% of the time, Pallas kernels for 8%

profile of v1, /device:TPU:0, one launch (start us, length us, event | category | flops | bytes accessed | tf_op | source)
XLA Modules:
  0.0 103.9 jit_solution(17621278174086416548)
XLA Ops:
  0.6 4.0 %collective-permute-start.8 = (bf16[128,640]{1,0:T(8,128)(2,1)}, bf16[128,640]{1,0:T(8,128)(2,1)S(1)}, u32[]{:S(2)}, u32[]{:S(2)}) collective-permute-start(bf16[128,640]{1,0:T(8,128)(2,1)} %refs_0_.4), channel_id=1, source_target_pairs={{0,6},{1,7},{2,4},{3,5},{4,2},{5,3},{6,0},{7,1},{8,14},{9,15},{10,... | collective-permute-start | bytes 491528 | tf_op jit(solution)/shard_map/ppermute | solution.py:242
  5.2 5.9 %collective-permute-start.2 = (bf16[128,128]{1,0:T(8,128)(2,1)}, bf16[128,128]{1,0:T(8,128)(2,1)S(1)}, u32[]{:S(2)}, u32[]{:S(2)}) collective-permute-start(bf16[128,128]{1,0:T(8,128)(2,1)} %refs_0_.6), channel_id=1, source_target_pairs={{0,24},{8,16},{1,25},{9,17},{2,26},{10,18},{3,27},{11,19},{4,28},{... | collective-permute-start | bytes 98312 | tf_op jit(solution)/shard_map/ppermute | solution.py:253
  13.0 5.8 %collective-permute-start.1 = (bf16[128,128]{1,0:T(8,128)(2,1)}, bf16[128,128]{1,0:T(8,128)(2,1)S(1)}, u32[]{:S(2)}, u32[]{:S(2)}) collective-permute-start(bf16[128,128]{1,0:T(8,128)(2,1)} %refs_0_.6), channel_id=1, source_target_pairs={{0,16},{8,24},{1,17},{9,25},{2,18},{10,26},{3,19},{11,27},{4,20},{... | collective-permute-start | bytes 98312 | tf_op jit(solution)/shard_map/ppermute | solution.py:253
  18.9 1.9 %collective-permute-done.1.refs_2_ = bf16[128,128]{1,0:T(8,128)(2,1)S(1)} collective-permute-done((bf16[128,128]{1,0:T(8,128)(2,1)}, bf16[128,128]{1,0:T(8,128)(2,1)S(1)}, u32[]{:S(2)}, u32[]{:S(2)}) %collective-permute-start.1) | collective-permute-done | bytes 32800 | tf_op jit(solution)/shard_map/ppermute | solution.py:253
  20.8 4.3 %collective-permute-start = (bf16[128,128]{1,0:T(8,128)(2,1)}, bf16[128,128]{1,0:T(8,128)(2,1)S(1)}, u32[]{:S(2)}, u32[]{:S(2)}) collective-permute-start(bf16[128,128]{1,0:T(8,128)(2,1)} %refs_0_.6), channel_id=1, source_target_pairs={{0,8},{16,24},{1,9},{17,25},{2,10},{18,26},{3,11},{19,27},{4,12},{... | collective-permute-start | bytes 98312 | tf_op jit(solution)/shard_map/ppermute | solution.py:253
  25.0 1.9 %collective-permute-done.refs_1_ = bf16[128,128]{1,0:T(8,128)(2,1)S(1)} collective-permute-done((bf16[128,128]{1,0:T(8,128)(2,1)}, bf16[128,128]{1,0:T(8,128)(2,1)S(1)}, u32[]{:S(2)}, u32[]{:S(2)}) %collective-permute-start) | collective-permute-done | bytes 32800 | tf_op jit(solution)/shard_map/ppermute | solution.py:253
  26.9 4.8 %collective-permute-start.15 = (bf16[128,128]{1,0:T(8,128)(2,1)}, bf16[128,128]{1,0:T(8,128)(2,1)S(1)}, u32[]{:S(2)}, u32[]{:S(2)}) collective-permute-start(bf16[128,128]{1,0:T(8,128)(2,1)} %refs_0_.7), channel_id=1, source_target_pairs={{0,24},{8,16},{16,8},{24,0},{1,25},{9,17},{17,9},{25,1},{2,26},{10... | collective-permute-start | bytes 98312 | tf_op jit(solution)/shard_map/ppermute | solution.py:253
  31.7 2.1 %collective-permute-done.15.refs_11_.refs_3_ = bf16[128,128]{1,0:T(8,128)(2,1)S(1)} collective-permute-done((bf16[128,128]{1,0:T(8,128)(2,1)}, bf16[128,128]{1,0:T(8,128)(2,1)S(1)}, u32[]{:S(2)}, u32[]{:S(2)}) %collective-permute-start.15) | collective-permute-done | bytes 32800 | tf_op jit(solution)/shard_map/ppermute | solution.py:253
  36.4 4.0 %collective-permute-start.13 = (bf16[128,128]{1,0:T(8,128)(2,1)}, bf16[128,128]{1,0:T(8,128)(2,1)S(1)}, u32[]{:S(2)}, u32[]{:S(2)}) collective-permute-start(bf16[128,128]{1,0:T(8,128)(2,1)} %refs_0_.7), channel_id=1, source_target_pairs={{0,8},{8,0},{16,24},{24,16},{1,9},{9,1},{17,25},{25,17},{2,10},{10... | collective-permute-start | bytes 98312 | tf_op jit(solution)/shard_map/ppermute | solution.py:253
  54.7 2.9 %collective-permute-start.16 = (f32[2,512]{1,0:T(2,128)S(1)}, f32[2,512]{1,0:T(2,128)S(1)}, u32[]{:S(2)}, u32[]{:S(2)}) collective-permute-start(f32[2,512]{1,0:T(2,128)S(1)} %shard_map.129.refs_12_), channel_id=1, source_target_pairs={{0,8},{8,0},{16,24},{24,16},{1,9},{9,1},{17,25},{25,17},{2,10},{10... | collective-permute-start | bytes 12296 | tf_op jit(solution)/shard_map/ppermute | solution.py:253
  57.6 1.6 %collective-permute-done.16.refs_13_ = f32[2,512]{1,0:T(2,128)S(1)} collective-permute-done((f32[2,512]{1,0:T(2,128)S(1)}, f32[2,512]{1,0:T(2,128)S(1)}, u32[]{:S(2)}, u32[]{:S(2)}) %collective-permute-start.16) | collective-permute-done | bytes 4128 | tf_op jit(solution)/shard_map/ppermute | solution.py:253
  59.2 1.6 %collective-permute-start.33 = (f32[2,5120]{1,0:T(2,128)S(1)}, f32[2,5120]{1,0:T(2,128)S(1)}, u32[]{:S(2)}, u32[]{:S(2)}) collective-permute-start(f32[2,5120]{1,0:T(2,128)S(1)} %get-tuple-element.20.refs_0_), channel_id=1, source_target_pairs={{0,4},{1,5},{2,6},{3,7},{4,0},{5,1},{6,2},{7,3},{8,12},{9,13},{10,... | collective-permute-start | bytes 122888 | tf_op jit(solution)/shard_map/ppermute | solution.py:296
  61.2 2.0 %collective-permute-start.31 = (f32[2,5120]{1,0:T(2,128)S(1)}, f32[2,5120]{1,0:T(2,128)S(1)}, u32[]{:S(2)}, u32[]{:S(2)}) collective-permute-start(f32[2,5120]{1,0:T(2,128)S(1)} %get-tuple-element.20.refs_0_), channel_id=1, source_target_pairs={{0,2},{1,3},{2,0},{3,1},{4,6},{5,7},{6,4},{7,5},{8,10},{9,11},{10,... | collective-permute-start | bytes 122888 | tf_op jit(solution)/shard_map/ppermute | solution.py:296
  63.6 1.6 %collective-permute-start.24 = (bf16[128,640]{1,0:T(8,128)(2,1)S(1)}, bf16[128,640]{1,0:T(8,128)(2,1)S(1)}, u32[]{:S(2)}, u32[]{:S(2)}) collective-permute-start(bf16[128,640]{1,0:T(8,128)(2,1)S(1)} %collective-permute-done.22.refs_4_), channel_id=1, source_target_pairs={{0,2},{1,3},{2,0},{3,1},{4,6},{5,7},{6,4},{7,5},{8,10},{9,11},{10,... | collective-permute-start | bytes 491528 | tf_op jit(solution)/shard_map/ppermute | solution.py:242
  65.2 3.4 %collective-permute-start.12 = (bf16[128,128]{1,0:T(8,128)(2,1)S(1)}, bf16[128,128]{1,0:T(8,128)(2,1)S(1)}, u32[]{:S(2)}, u32[]{:S(2)}) collective-permute-start(bf16[128,128]{1,0:T(8,128)(2,1)S(1)} %get-tuple-element.13.refs_4_), channel_id=1, source_target_pairs={{0,24},{8,16},{1,25},{9,17},{2,26},{10,18},{3,27},{11,19},{4,28},{... | collective-permute-start | bytes 98312 | tf_op jit(solution)/shard_map/ppermute | solution.py:253
  69.9 2.5 %collective-permute-start.10 = (bf16[128,128]{1,0:T(8,128)(2,1)S(1)}, bf16[128,128]{1,0:T(8,128)(2,1)S(1)}, u32[]{:S(2)}, u32[]{:S(2)}) collective-permute-start(bf16[128,128]{1,0:T(8,128)(2,1)S(1)} %get-tuple-element.13.refs_4_), channel_id=1, source_target_pairs={{0,8},{16,24},{1,9},{17,25},{2,10},{18,26},{3,11},{19,27},{4,12},{... | collective-permute-start | bytes 98312 | tf_op jit(solution)/shard_map/ppermute | solution.py:253
  72.5 1.9 %collective-permute-start.39 = (f32[2,5120]{1,0:T(2,128)S(1)}, f32[2,5120]{1,0:T(2,128)S(1)}, u32[]{:S(2)}, u32[]{:S(2)}) collective-permute-start(f32[2,5120]{1,0:T(2,128)S(1)} %shard_map.133.refs_0_), channel_id=1, source_target_pairs={{0,24},{8,16},{16,8},{24,0},{1,25},{9,17},{17,9},{25,1},{2,26},{10... | collective-permute-start | bytes 122888 | tf_op jit(solution)/shard_map/ppermute | solution.py:253
  74.8 2.1 %collective-permute-start.37 = (f32[2,5120]{1,0:T(2,128)S(1)}, f32[2,5120]{1,0:T(2,128)S(1)}, u32[]{:S(2)}, u32[]{:S(2)}) collective-permute-start(f32[2,5120]{1,0:T(2,128)S(1)} %shard_map.133.refs_0_), channel_id=1, source_target_pairs={{0,8},{8,0},{16,24},{24,16},{1,9},{9,1},{17,25},{25,17},{2,10},{10... | collective-permute-start | bytes 122888 | tf_op jit(solution)/shard_map/ppermute | solution.py:253
  77.0 3.0 %shard_map.130 = (bf16[1024,128]{1,0:T(8,128)(2,1)}, bf16[1024,128]{1,0:T(8,128)(2,1)}, f32[128,128]{1,0:T(8,128)S(1)}, f32[128,128]{1,0:T(8,128)S(1)}, f32[128,128]{1,0:T(8,128)S(1)}, /*index=5*/f32[128,128]{1,0:T(8,128)S(1)}) custom-call(s32[4]{0:T(128)S(1)} %copy-done.14, bf16[1024,128]{1,0:T(8,128)(2,1)S(1)} %copy-done.9, ...), custom_call_target="tpu_custom_call" | custom-call | flops 671088640 | bytes 933904 | tf_op jit(solution)/shard_map/pallas_call | solution.py:219
  82.4 3.8 %collective-permute-done.19.refs_1_ = f32[128,128]{1,0:T(8,128)S(1)} collective-permute-done((f32[128,128]{1,0:T(8,128)S(1)}, f32[128,128]{1,0:T(8,128)S(1)}, u32[]{:S(2)}, u32[]{:S(2)}) %collective-permute-start.19) | collective-permute-done | bytes 65568 | tf_op jit(solution)/shard_map/ppermute | solution.py:253
  87.4 5.8 %collective-permute-done.20.refs_2_ = f32[128,128]{1,0:T(8,128)S(1)} collective-permute-done((f32[128,128]{1,0:T(8,128)S(1)}, f32[128,128]{1,0:T(8,128)S(1)}, u32[]{:S(2)}, u32[]{:S(2)}) %collective-permute-start.20) | collective-permute-done | bytes 65568 | tf_op jit(solution)/shard_map/ppermute | solution.py:253
  94.5 1.7 %shard_map.134 = f32[16,5120]{1,0:T(8,128)} custom-call(s32[8]{0:T(128)S(1)} %copy-done.7, f32[2,5120]{1,0:T(2,128)S(1)} %shard_map.133.refs_0_, f32[2,5120]{1,0:T(2,128)S(1)} %collective-permute-done.37.refs_1_, f32[2,5120]{1,0:T(2,128)S(1)} %collective-permute-done.38.refs_2_, f32[2,5120]{1,0:T(2,128)S(1)} %collective-permute-done.39.refs_3_), custom_call_target="tpu_custom_call" | custom-call | bytes 163872 | tf_op jit(solution)/shard_map/pallas_call | solution.py:219
  96.1 5.0 %collective-permute-done.21.refs_3_ = f32[128,128]{1,0:T(8,128)S(1)} collective-permute-done((f32[128,128]{1,0:T(8,128)S(1)}, f32[128,128]{1,0:T(8,128)S(1)}, u32[]{:S(2)}, u32[]{:S(2)}) %collective-permute-start.21) | collective-permute-done | bytes 65568 | tf_op jit(solution)/shard_map/ppermute | solution.py:253
  101.9 2.0 %shard_map.132 = f32[128,1280]{1,0:T(8,128)} custom-call(s32[8]{0:T(128)S(1)} %copy-done.7, f32[16,5120]{1,0:T(8,128)S(1)} %copy-done.2, bf16[128,128]{1,0:T(8,128)(2,1)S(1)} %copy-done.5, bf16[128,128]{1,0:T(8,128)(2,1)S(1)} %collective-permute-done.13.refs_9_.refs_1_, bf16[128,128]{1,0:T(8,128)(2,1)S(1)} %collective-permute-done.14.refs_10_.refs_2_, ...), custom_call_target="tpu_custom_call" | custom-call | flops 167772160 | bytes 1769504 | tf_op jit(solution)/shard_map/pallas_call | solution.py:219
  (93 shorter events, 27.6 us)
Async XLA Ops:
  0.6 33.2 %collective-permute-start.8 = (bf16[128,640]{1,0:T(8,128)(2,1)}, bf16[128,640]{1,0:T(8,128)(2,1)S(1)}, u32[]{:S(2)}, u32[]{:S(2)}) collective-permute-start(bf16[128,640]{1,0:T(8,128)(2,1)} %refs_0_.4), channel_id=1, source_target_pairs={{0,6},{1,7},{2,4},{3,5},{4,2},{5,3},{6,0},{7,1},{8,14},{9,15},{10,... | collective-permute-start | bytes 491528 | tf_op jit(solution)/shard_map/ppermute | solution.py:242
  4.6 29.7 %collective-permute-start.6 = (bf16[128,640]{1,0:T(8,128)(2,1)}, bf16[128,640]{1,0:T(8,128)(2,1)S(1)}, u32[]{:S(2)}, u32[]{:S(2)}) collective-permute-start(bf16[128,640]{1,0:T(8,128)(2,1)} %refs_0_.4), channel_id=1, source_target_pairs={{0,4},{1,5},{2,6},{3,7},{4,0},{5,1},{6,2},{7,3},{8,12},{9,13},{10,... | collective-permute-start | bytes 491528 | tf_op jit(solution)/shard_map/ppermute | solution.py:242
  5.1 29.3 %collective-permute-start.4 = (bf16[128,640]{1,0:T(8,128)(2,1)}, bf16[128,640]{1,0:T(8,128)(2,1)S(1)}, u32[]{:S(2)}, u32[]{:S(2)}) collective-permute-start(bf16[128,640]{1,0:T(8,128)(2,1)} %refs_0_.4), channel_id=1, source_target_pairs={{0,2},{1,3},{2,0},{3,1},{4,6},{5,7},{6,4},{7,5},{8,10},{9,11},{10,... | collective-permute-start | bytes 491528 | tf_op jit(solution)/shard_map/ppermute | solution.py:242
  5.2 7.8 %collective-permute-start.2 = (bf16[128,128]{1,0:T(8,128)(2,1)}, bf16[128,128]{1,0:T(8,128)(2,1)S(1)}, u32[]{:S(2)}, u32[]{:S(2)}) collective-permute-start(bf16[128,128]{1,0:T(8,128)(2,1)} %refs_0_.6), channel_id=1, source_target_pairs={{0,24},{8,16},{1,25},{9,17},{2,26},{10,18},{3,27},{11,19},{4,28},{... | collective-permute-start | bytes 98312 | tf_op jit(solution)/shard_map/ppermute | solution.py:253
  11.1 23.7 %collective-permute-start.22 = (bf16[128,640]{1,0:T(8,128)(2,1)}, bf16[128,640]{1,0:T(8,128)(2,1)S(1)}, u32[]{:S(2)}, u32[]{:S(2)}) collective-permute-start(bf16[128,640]{1,0:T(8,128)(2,1)} %refs_0_.4), channel_id=1, source_target_pairs={{0,0},{1,1},{2,10},{3,11},{4,20},{5,21},{6,30},{7,31},{8,2},{9,3},... | collective-permute-start | bytes 491528 | tf_op jit(solution)/shard_map/ppermute | solution.py:268
  13.0 7.7 %collective-permute-start.1 = (bf16[128,128]{1,0:T(8,128)(2,1)}, bf16[128,128]{1,0:T(8,128)(2,1)S(1)}, u32[]{:S(2)}, u32[]{:S(2)}) collective-permute-start(bf16[128,128]{1,0:T(8,128)(2,1)} %refs_0_.6), channel_id=1, source_target_pairs={{0,16},{8,24},{1,17},{9,25},{2,18},{10,26},{3,19},{11,27},{4,20},{... | collective-permute-start | bytes 98312 | tf_op jit(solution)/shard_map/ppermute | solution.py:253
  34.3 9.8 %collective-permute-start.7 = (bf16[128,640]{1,0:T(8,128)(2,1)S(1)}, bf16[128,640]{1,0:T(8,128)(2,1)S(1)}, u32[]{:S(2)}, u32[]{:S(2)}) collective-permute-start(bf16[128,640]{1,0:T(8,128)(2,1)S(1)} %collective-permute-done.6.refs_4_), channel_id=1, source_target_pairs={{0,1},{1,0},{2,3},{3,2},{4,5},{5,4},{6,7},{7,6},{8,9},{9,8},{10,11... | collective-permute-start | bytes 491528 | tf_op jit(solution)/shard_map/ppermute | solution.py:245
  34.4 9.8 %collective-permute-start.5 = (bf16[128,640]{1,0:T(8,128)(2,1)S(1)}, bf16[128,640]{1,0:T(8,128)(2,1)S(1)}, u32[]{:S(2)}, u32[]{:S(2)}) collective-permute-start(bf16[128,640]{1,0:T(8,128)(2,1)S(1)} %collective-permute-done.4.refs_2_), channel_id=1, source_target_pairs={{0,1},{1,0},{2,3},{3,2},{4,5},{5,4},{6,7},{7,6},{8,9},{9,8},{10,11... | collective-permute-start | bytes 491528 | tf_op jit(solution)/shard_map/ppermute | solution.py:245
  34.8 26.0 %collective-permute-start.28 = (bf16[128,640]{1,0:T(8,128)(2,1)S(1)}, bf16[128,640]{1,0:T(8,128)(2,1)S(1)}, u32[]{:S(2)}, u32[]{:S(2)}) collective-permute-start(bf16[128,640]{1,0:T(8,128)(2,1)S(1)} %collective-permute-done.22.refs_4_), channel_id=1, source_target_pairs={{0,6},{1,7},{2,4},{3,5},{4,2},{5,3},{6,0},{7,1},{8,14},{9,15},{10,... | collective-permute-start | bytes 491528 | tf_op jit(solution)/shard_map/ppermute | solution.py:242
  36.0 15.8 %collective-permute-start.14 = (bf16[128,128]{1,0:T(8,128)(2,1)}, bf16[128,128]{1,0:T(8,128)(2,1)S(1)}, u32[]{:S(2)}, u32[]{:S(2)}) collective-permute-start(bf16[128,128]{1,0:T(8,128)(2,1)} %refs_0_.7), channel_id=1, source_target_pairs={{0,16},{8,24},{16,0},{24,8},{1,17},{9,25},{17,1},{25,9},{2,18},{10... | collective-permute-start | bytes 98312 | tf_op jit(solution)/shard_map/ppermute | solution.py:253
  36.4 15.8 %collective-permute-start.13 = (bf16[128,128]{1,0:T(8,128)(2,1)}, bf16[128,128]{1,0:T(8,128)(2,1)S(1)}, u32[]{:S(2)}, u32[]{:S(2)}) collective-permute-start(bf16[128,128]{1,0:T(8,128)(2,1)} %refs_0_.7), channel_id=1, source_target_pairs={{0,8},{8,0},{16,24},{24,16},{1,9},{9,1},{17,25},{25,17},{2,10},{10... | collective-permute-start | bytes 98312 | tf_op jit(solution)/shard_map/ppermute | solution.py:253
  44.1 9.7 %collective-permute-start.18 = (f32[2,512]{1,0:T(2,128)S(1)}, f32[2,512]{1,0:T(2,128)S(1)}, u32[]{:S(2)}, u32[]{:S(2)}) collective-permute-start(f32[2,512]{1,0:T(2,128)S(1)} %shard_map.129.refs_12_), channel_id=1, source_target_pairs={{0,24},{8,16},{16,8},{24,0},{1,25},{9,17},{17,9},{25,1},{2,26},{10... | collective-permute-start | bytes 12296 | tf_op jit(solution)/shard_map/ppermute | solution.py:253
  44.2 10.5 %collective-permute-start.17 = (f32[2,512]{1,0:T(2,128)S(1)}, f32[2,512]{1,0:T(2,128)S(1)}, u32[]{:S(2)}, u32[]{:S(2)}) collective-permute-start(f32[2,512]{1,0:T(2,128)S(1)} %shard_map.129.refs_12_), channel_id=1, source_target_pairs={{0,16},{8,24},{16,0},{24,8},{1,17},{9,25},{17,1},{25,9},{2,18},{10... | collective-permute-start | bytes 12296 | tf_op jit(solution)/shard_map/ppermute | solution.py:253
  51.8 9.4 %collective-permute-start.36 = (f32[2,5120]{1,0:T(2,128)S(1)}, f32[2,5120]{1,0:T(2,128)S(1)}, u32[]{:S(2)}, u32[]{:S(2)}) collective-permute-start(f32[2,5120]{1,0:T(2,128)S(1)} %get-tuple-element.20.refs_0_), channel_id=1, source_target_pairs={{0,7},{1,6},{2,5},{3,4},{4,3},{5,2},{6,1},{7,0},{8,15},{9,14},{10,... | collective-permute-start | bytes 122888 | tf_op jit(solution)/shard_map/ppermute | solution.py:296
  52.2 9.0 %collective-permute-start.35 = (f32[2,5120]{1,0:T(2,128)S(1)}, f32[2,5120]{1,0:T(2,128)S(1)}, u32[]{:S(2)}, u32[]{:S(2)}) collective-permute-start(f32[2,5120]{1,0:T(2,128)S(1)} %get-tuple-element.20.refs_0_), channel_id=1, source_target_pairs={{0,6},{1,7},{2,4},{3,5},{4,2},{5,3},{6,0},{7,1},{8,14},{9,15},{10,... | collective-permute-start | bytes 122888 | tf_op jit(solution)/shard_map/ppermute | solution.py:296
  53.8 9.5 %collective-permute-start.34 = (f32[2,5120]{1,0:T(2,128)S(1)}, f32[2,5120]{1,0:T(2,128)S(1)}, u32[]{:S(2)}, u32[]{:S(2)}) collective-permute-start(f32[2,5120]{1,0:T(2,128)S(1)} %get-tuple-element.20.refs_0_), channel_id=1, source_target_pairs={{0,5},{1,4},{2,7},{3,6},{4,1},{5,0},{6,3},{7,2},{8,13},{9,12},{10,... | collective-permute-start | bytes 122888 | tf_op jit(solution)/shard_map/ppermute | solution.py:296
  60.8 19.2 %collective-permute-start.26 = (bf16[128,640]{1,0:T(8,128)(2,1)S(1)}, bf16[128,640]{1,0:T(8,128)(2,1)S(1)}, u32[]{:S(2)}, u32[]{:S(2)}) collective-permute-start(bf16[128,640]{1,0:T(8,128)(2,1)S(1)} %collective-permute-done.22.refs_4_), channel_id=1, source_target_pairs={{0,4},{1,5},{2,6},{3,7},{4,0},{5,1},{6,2},{7,3},{8,12},{9,13},{10,... | collective-permute-start | bytes 491528 | tf_op jit(solution)/shard_map/ppermute | solution.py:242
  63.6 17.6 %collective-permute-start.24 = (bf16[128,640]{1,0:T(8,128)(2,1)S(1)}, bf16[128,640]{1,0:T(8,128)(2,1)S(1)}, u32[]{:S(2)}, u32[]{:S(2)}) collective-permute-start(bf16[128,640]{1,0:T(8,128)(2,1)S(1)} %collective-permute-done.22.refs_4_), channel_id=1, source_target_pairs={{0,2},{1,3},{2,0},{3,1},{4,6},{5,7},{6,4},{7,5},{8,10},{9,11},{10,... | collective-permute-start | bytes 491528 | tf_op jit(solution)/shard_map/ppermute | solution.py:242
  72.5 8.9 %collective-permute-start.39 = (f32[2,5120]{1,0:T(2,128)S(1)}, f32[2,5120]{1,0:T(2,128)S(1)}, u32[]{:S(2)}, u32[]{:S(2)}) collective-permute-start(f32[2,5120]{1,0:T(2,128)S(1)} %shard_map.133.refs_0_), channel_id=1, source_target_pairs={{0,24},{8,16},{16,8},{24,0},{1,25},{9,17},{17,9},{25,1},{2,26},{10... | collective-permute-start | bytes 122888 | tf_op jit(solution)/shard_map/ppermute | solution.py:253
  81.3 20.6 %collective-permute-start.23 = (bf16[128,640]{1,0:T(8,128)(2,1)S(1)}, bf16[128,640]{1,0:T(8,128)(2,1)S(1)}, u32[]{:S(2)}, u32[]{:S(2)}) collective-permute-start(bf16[128,640]{1,0:T(8,128)(2,1)S(1)} %collective-permute-done.22.refs_4_), channel_id=1, source_target_pairs={{0,1},{1,0},{2,3},{3,2},{4,5},{5,4},{6,7},{7,6},{8,9},{9,8},{10,11... | collective-permute-start | bytes 491528 | tf_op jit(solution)/shard_map/ppermute | solution.py:245
  81.4 20.5 %collective-permute-start.29 = (bf16[128,640]{1,0:T(8,128)(2,1)S(1)}, bf16[128,640]{1,0:T(8,128)(2,1)S(1)}, u32[]{:S(2)}, u32[]{:S(2)}) collective-permute-start(bf16[128,640]{1,0:T(8,128)(2,1)S(1)} %collective-permute-done.28.refs_10_), channel_id=1, source_target_pairs={{0,1},{1,0},{2,3},{3,2},{4,5},{5,4},{6,7},{7,6},{8,9},{9,8},{10,11... | collective-permute-start | bytes 491528 | tf_op jit(solution)/shard_map/ppermute | solution.py:245
  81.8 20.0 %collective-permute-start.27 = (bf16[128,640]{1,0:T(8,128)(2,1)S(1)}, bf16[128,640]{1,0:T(8,128)(2,1)S(1)}, u32[]{:S(2)}, u32[]{:S(2)}) collective-permute-start(bf16[128,640]{1,0:T(8,128)(2,1)S(1)} %collective-permute-done.26.refs_8_), channel_id=1, source_target_pairs={{0,1},{1,0},{2,3},{3,2},{4,5},{5,4},{6,7},{7,6},{8,9},{9,8},{10,11... | collective-permute-start | bytes 491528 | tf_op jit(solution)/shard_map/ppermute | solution.py:245
  81.9 19.9 %collective-permute-start.25 = (bf16[128,640]{1,0:T(8,128)(2,1)S(1)}, bf16[128,640]{1,0:T(8,128)(2,1)S(1)}, u32[]{:S(2)}, u32[]{:S(2)}) collective-permute-start(bf16[128,640]{1,0:T(8,128)(2,1)S(1)} %collective-permute-done.24.refs_6_), channel_id=1, source_target_pairs={{0,1},{1,0},{2,3},{3,2},{4,5},{5,4},{6,7},{7,6},{8,9},{9,8},{10,11... | collective-permute-start | bytes 491528 | tf_op jit(solution)/shard_map/ppermute | solution.py:245
  93.2 7.9 %collective-permute-start.21 = (f32[128,128]{1,0:T(8,128)S(1)}, f32[128,128]{1,0:T(8,128)S(1)}, u32[]{:S(2)}, u32[]{:S(2)}) collective-permute-start(f32[128,128]{1,0:T(8,128)S(1)} %get-tuple-element.17), channel_id=1, source_target_pairs={{16,8},{24,0},{17,9},{25,1},{18,10},{26,2},{19,11},{27,3},{20,12},... | collective-permute-start | bytes 196616 | tf_op jit(solution)/shard_map/ppermute | solution.py:253
  (31 other events, 312.4 us)

commit v2 on v1

v2 whole, which is shorter than its diff:
```python
import functools
import math

import jax
import jax.numpy as jnp
from jax import lax
from jax.experimental import pallas as pl
from jax.experimental.pallas import tpu as pltpu
from jax.sharding import PartitionSpec as P

HD = 128
SPF = 512
QF = 64
NEG_BIG = -1e30
SCALE = 1.0 / math.sqrt(HD)
VMEM_LIMIT = 48 * 1024 * 1024


def dot(a, b, on_a, on_b):
    return lax.dot_general(
        a, b, (((on_a,), (on_b,)), ((), ())), preferred_element_type=jnp.float32
    )


def take_columns(ref, shard, width):
    if len(ref.shape) == 3:
        return ref[shard]
    return ref[:, pl.ds(pl.multiple_of(shard * width, 128), width)]


def gate_row(gate_ref, shard, width, level):
    if len(gate_ref.shape) == 3:
        return gate_ref[shard, pl.ds(level, 1), :]
    return gate_ref[pl.ds(level, 1), pl.ds(pl.multiple_of(shard * width, 128), width)]


def gate_rows(piece, levels_ref, gate_ref, owner, shard, frames):
    wide = piece.astype(jnp.float32)
    rows = []
    for r in range(frames):
        row = gate_row(gate_ref, shard, piece.shape[1], levels_ref[owner * frames + r])
        rows.append((wide[r * QF : (r + 1) * QF] * row).astype(jnp.bfloat16))
    return wide, jnp.concatenate(rows, axis=0)


def pack_kernel(queries_ref, saved_ref, out_ref):
    for i in range(out_ref.shape[0]):
        out_ref[i, 0] = queries_ref[...]
        out_ref[i, 1] = saved_ref[...]


def head_kernel(n_s, frames, levels_ref, saved_ref, w_ref, gate_ref, *refs):
    pieces, (head_out, terms_out, terms_ref) = refs[:n_s], refs[n_s:]
    t, s = lax.axis_index("tm"), lax.axis_index("space")
    width = pieces[0].shape[1]
    saved = saved_ref[...]
    head = jnp.zeros(head_out.shape[1:], jnp.float32)
    for j in range(n_s):
        shard = s ^ j
        weight = take_columns(w_ref, shard, width)
        wide, gated = gate_rows(pieces[j][...], levels_ref, gate_ref, t, shard, frames)
        head = head + dot(gated, weight, 1, 1)
        product = wide * dot(saved, weight, 1, 0)
        for r in range(frames):
            term = jnp.sum(product[r * QF : (r + 1) * QF], axis=0, keepdims=True)
            if len(terms_ref.shape) == 3:
                terms_ref[shard, r : r + 1, :] = term
            else:
                terms_ref[r : r + 1, pl.ds(pl.multiple_of(shard * width, 128), width)] = term
    for i in range(head_out.shape[0]):
        head_out[i] = head.astype(jnp.bfloat16)
    for i in range(n_s):
        terms_out[i] = terms_ref[...]


def heads_sum_kernel(terms_ref, out_ref):
    total = terms_ref[0]
    for j in range(1, terms_ref.shape[0]):
        total = total + terms_ref[j]
    for i in range(out_ref.shape[0]):
        out_ref[i] = total


def levels_kernel(n_t, frames, levels_ref, held, out_ref):
    spot = lax.broadcasted_iota(jnp.int32, out_ref.shape, len(out_ref.shape) - 2)
    total = jnp.zeros(out_ref.shape, jnp.float32)
    for f in range(n_t * frames):
        r = f % frames
        row = held[f // frames, ..., r : r + 1, :]
        total = total + jnp.where(spot == levels_ref[f], row, 0.0)
    out_ref[...] = total


def weight_kernel(n_t, frames, levels_ref, gate_ref, packed_ref, *refs):
    n_s = 2 * n_t
    pieces, out_ref = refs[:n_s], refs[n_s]
    t, s = lax.axis_index("tm"), lax.axis_index("space")
    chip, core = s // 2, s % 2
    width = pieces[0].shape[1]
    saved = jnp.concatenate([packed_ref[t ^ chip ^ k, 1] for k in range(n_t)], axis=0)
    for f in range(2):
        half = core ^ f
        rows = [
            gate_rows(pieces[2 * k + f][...], levels_ref, gate_ref, t ^ chip ^ k, 2 * t + half, frames)[1]
            for k in range(n_t)
        ]
        result = dot(saved, jnp.concatenate(rows, axis=0), 0, 0)
        for h in range(2):

            @pl.when(half == h)
            def _():
                out_ref[:, h * width : (h + 1) * width] = result


def clip_numbers(clips_ref):
    bounds = []
    so_far = 0
    for c in range(clips_ref.shape[0]):
        so_far = so_far + clips_ref[c]
        bounds.append(so_far)
    return lambda frame: sum((frame >= bound).astype(jnp.int32) for bound in bounds)


def bias_row(clip_of, owner, key_frame, frames, rows):
    lane = lax.broadcasted_iota(jnp.int32, (1, rows), 1)
    row = jnp.full((1, rows), NEG_BIG, jnp.float32)
    for r in range(frames):
        frame = owner * frames + r
        visible = (key_frame >= frame) & (clip_of(key_frame) == clip_of(frame))
        value = jnp.where(visible, 0.0, NEG_BIG).astype(jnp.float32)
        row = jnp.where((lane >= r * QF) & (lane < (r + 1) * QF), value, row)
    return row


def stats_kernel(n_t, frames, clips_ref, keys_ref, packed_ref, stats_ref):
    t = lax.axis_index("tm")
    clip_of = clip_numbers(clips_ref)
    rows = packed_ref.shape[2]
    for p in range(0, n_t, 2):
        q = jnp.concatenate([packed_ref[p, 0], packed_ref[p + 1, 0]], axis=0)
        scores = []
        for kf in range(frames):
            bias = jnp.concatenate(
                [bias_row(clip_of, k, t * frames + kf, frames, rows) for k in (p, p + 1)], axis=1
            )
            scores.append(dot(keys_ref[kf * SPF : (kf + 1) * SPF, :], q, 1, 1) * SCALE + bias)
        top = functools.reduce(jnp.maximum, [jnp.max(x, axis=0, keepdims=True) for x in scores])
        total = sum(jnp.sum(jnp.exp(x - top), axis=0, keepdims=True) for x in scores)
        for i in range(n_t):
            stats_ref[i, 0:1, p * rows : (p + 2) * rows] = top
            stats_ref[i, 1:2, p * rows : (p + 2) * rows] = total


def grads_kernel(
    n_t, frames, clips_ref, keys_ref, values_ref, packed_ref, grads_ref, stats_ref,
    key_ref, value_ref, query_ref, key_acc, value_acc,
):
    t = lax.axis_index("tm")
    clip_of = clip_numbers(clips_ref)
    rows = packed_ref.shape[2]
    ones = jnp.ones((8, HD), jnp.float32)
    keys_t = jnp.transpose(keys_ref[...])
    for p in range(0, n_t, 2):
        q = jnp.concatenate([packed_ref[p, 0], packed_ref[p + 1, 0]], axis=0)
        g = jnp.concatenate([grads_ref[p], grads_ref[p + 1]], axis=0)
        o = jnp.concatenate([packed_ref[p, 1], packed_ref[p + 1, 1]], axis=0)
        delta = lax.dot_general(
            ones,
            g.astype(jnp.float32) * o.astype(jnp.float32),
            (((1,), (1,)), ((), ())),
            precision=lax.Precision.HIGHEST,
            preferred_element_type=jnp.float32,
        )[0:1]
        span = slice(p * rows, (p + 2) * rows)
        tops = [stats_ref[i, 0:1, span] for i in range(n_t)]
        sums = [stats_ref[i, 1:2, span] for i in range(n_t)]
        top = functools.reduce(jnp.maximum, tops)
        lse = top + jnp.log(sum(b * jnp.exp(a - top) for a, b in zip(tops, sums)))
        query_part = None
        for kf in range(frames):
            span = slice(kf * SPF, (kf + 1) * SPF)
            bias = jnp.concatenate(
                [bias_row(clip_of, k, t * frames + kf, frames, rows) for k in (p, p + 1)], axis=1
            )
            probs = jnp.exp(dot(keys_ref[span, :], q, 1, 1) * SCALE + (bias - lse))
            score_grad = (probs * (dot(values_ref[span, :], g, 1, 1) - delta)).astype(jnp.bfloat16)
            value_add = dot(probs.astype(jnp.bfloat16), g, 1, 0)
            key_add = dot(score_grad, q, 1, 0)
            if p > 0:
                value_add = value_add + value_acc[span, :]
                key_add = key_add + key_acc[span, :]
            if p + 2 < n_t:
                value_acc[span, :] = value_add
                key_acc[span, :] = key_add
            else:
                value_ref[span, :] = value_add.astype(jnp.bfloat16)
                key_ref[span, :] = (key_add * SCALE).astype(jnp.bfloat16)
            part = dot(keys_t[:, span], score_grad, 1, 0)
            query_part = part if query_part is None else query_part + part
        query_ref[p] = query_part[:, :rows]
        query_ref[p + 1] = query_part[:, rows:]


def query_kernel(parts_ref, out_ref):
    total = parts_ref[0]
    for k in range(1, parts_ref.shape[0]):
        total = total + parts_ref[k]
    out_ref[...] = jnp.transpose(total * SCALE).astype(jnp.bfloat16)


def call(kernel, in_smem, args, out_shape, scratch=(), flops=0):
    whole = pl.BlockSpec(memory_space=pltpu.VMEM)
    single = not isinstance(out_shape, (list, tuple))
    nbytes = sum(a.size * a.dtype.itemsize for a in args)
    return pl.pallas_call(
        kernel,
        out_shape=out_shape,
        in_specs=[pl.BlockSpec(memory_space=pltpu.SMEM)] * in_smem + [whole] * (len(args) - in_smem),
        out_specs=whole if single else [whole] * len(out_shape),
        scratch_shapes=list(scratch),
        compiler_params=pltpu.CompilerParams(vmem_limit_bytes=VMEM_LIMIT),
        cost_estimate=pl.CostEstimate(flops=flops, bytes_accessed=nbytes, transcendentals=0),
    )(*args)


def body(
    queries, keys, values, saved_out, out_grad, proj_weight, gate_table, noise_levels, clip_lengths
):
    n_t, n_s = lax.axis_size("tm"), lax.axis_size("space")
    chips = n_s // 2
    rows, width = out_grad.shape
    k_rows = keys.shape[0]
    frames = rows // QF
    levels, columns = gate_table.shape
    shape = jax.ShapeDtypeStruct

    def over_chips(x, k):
        return lax.ppermute(x, "space", [(s, s ^ (2 * k)) for s in range(n_s)])

    def over_cores(x):
        return lax.ppermute(x, "space", [(s, s ^ 1) for s in range(n_s)])

    def swap(x, axis):
        return lax.all_to_all(x, axis, 0, 0)

    def plane_gather(x):
        same_core = [x] + [over_chips(x, k) for k in range(1, chips)]
        return [y for piece in same_core for y in (piece, over_cores(piece))]

    pieces = plane_gather(out_grad)
    packed = swap(
        call(pack_kernel, 0, [queries, saved_out], shape((n_t, 2, rows, HD), jnp.bfloat16)), "tm"
    )
    moves = [
        (t * n_s + 2 * c + e, c * n_s + 2 * (c ^ t) + e)
        for t in range(n_t)
        for c in range(chips)
        for e in range(2)
    ]
    moved = lax.ppermute(out_grad, ("tm", "space"), moves)
    row_pieces = plane_gather(moved)

    cut = width % 128 != 0
    w_table, g_table = proj_weight, gate_table
    if cut:
        w_table = proj_weight.reshape(HD, n_s, width).transpose(1, 0, 2)
        g_table = gate_table.reshape(levels, n_s, width).transpose(1, 0, 2)
    terms_shape = (n_s, frames, width) if cut else (frames, columns)

    stats = call(
        functools.partial(stats_kernel, n_t, frames),
        1,
        [clip_lengths, keys, packed],
        shape((n_t, 2, n_t * rows), jnp.float32),
        flops=2 * n_t * rows * k_rows * HD,
    )
    stats = swap(stats, "tm")

    head_grad, terms = call(
        functools.partial(head_kernel, n_s, frames),
        1,
        [noise_levels, saved_out, w_table, g_table] + pieces,
        [shape((n_t, rows, HD), jnp.bfloat16), shape((n_s,) + terms_shape, jnp.float32)],
        [pltpu.VMEM(terms_shape, jnp.float32)],
        flops=4 * rows * columns * HD,
    )
    grads_all = swap(head_grad, "tm")
    terms_sum = call(
        heads_sum_kernel, 0, [swap(terms, "space")], shape((n_t,) + terms_shape, jnp.float32)
    )
    terms_sum = swap(terms_sum, "tm")

    key_grad, value_grad, query_parts = call(
        functools.partial(grads_kernel, n_t, frames),
        1,
        [clip_lengths, keys, values, packed, grads_all, stats],
        [shape((k_rows, HD), jnp.bfloat16)] * 2 + [shape((n_t, HD, rows), jnp.float32)],
        [pltpu.VMEM((k_rows, HD), jnp.float32)] * 2,
        flops=10 * n_t * rows * k_rows * HD,
    )
    query_parts = swap(query_parts, "tm")

    weight_grad = call(
        functools.partial(weight_kernel, n_t, frames),
        1,
        [noise_levels, g_table, packed] + row_pieces,
        shape((HD, 2 * width), jnp.float32),
        flops=4 * n_t * rows * width * HD,
    )
    gate_grad = call(
        functools.partial(levels_kernel, n_t, frames),
        1,
        [noise_levels, terms_sum],
        shape((n_s, levels, width) if cut else (levels, columns), jnp.float32),
    )
    if cut:
        gate_grad = gate_grad.transpose(1, 0, 2).reshape(levels, columns)
    query_grad = call(query_kernel, 0, [query_parts], shape((rows, HD), jnp.bfloat16))
    return (query_grad, key_grad, value_grad, weight_grad, gate_grad)


def solution(mesh):
    return jax.shard_map(
        body,
        mesh=mesh,
        in_specs=(
            P("tm", "space"),
            P("tm", "space"),
            P("tm", "space"),
            P("tm", "space"),
            P("tm", "space"),
            P("space", None),
            P(),
            P(),
            P(),
        ),
        out_specs=(P("tm", "space"), P("tm", "space"), P("tm", "space"), P("space", "tm"), P()),
        check_vma=False,
    )
```

time: 104 us -> 92.1 us (0.89)
  starting transfers between devices: 63 us -> 34.4 us
  blocking collectives: 0 us -> 10.1 us
  waiting for transfers between devices: 22.7 us -> 26.5 us
  Pallas kernels: 10.3 us -> 12.8 us
    ppermute x25 -> x0, starting transfers between devices: 51.6 us -> none  [the longest x18 45 us: over_time(): return lax.ppermute(x, 'tm', pairs)]
    all_to_all x0 -> x5, starting transfers between devices: none -> 23.2 us  [swap(): return lax.all_to_all(x, axis, 0, 0)]
    ppermute x25 -> x0, waiting for transfers between devices: 22.6 us -> none  [the longest x18 22.3 us: over_time(): return lax.ppermute(x, 'tm', pairs)]
    ppermute x6, waiting for transfers between devices: 0.02 us -> 13.1 us  [over_chips(): return lax.ppermute(x, 'space', [(s, s ^ 2 * k) for s in range(n_s)])]
    all_to_all x0 -> x5, waiting for transfers between devices: none -> 12.3 us  [swap(): return lax.all_to_all(x, axis, 0, 0)]
    all_to_all x0 -> x1, blocking collectives: none -> 10.1 us  [swap(): return lax.all_to_all(x, axis, 0, 0)]
    pallas_call x7 -> x8, Pallas kernels: 10.3 us -> 12.8 us  [call(): pl.pallas_call(kernel, out_shape=out_shape, in_specs=[pl.BlockSpec(memory...]
    ppermute x6, starting transfers between devices: 7.77 us -> 9.45 us  [over_chips(): return lax.ppermute(x, 'space', [(s, s ^ 2 * k) for s in range(n_s)])]
  transfers between devices with their start and end apart: 40 -> 20, of which waited for: 9 -> 9; matrix products, arithmetic and copies ran while one was open for 0% -> 0% of each run, Pallas kernels for 8% -> 12%
where the time goes in v2:
time: 92.1 us; the launch traced here: 91.2 us
  starting transfers between devices  34.4 us (37%)
  waiting for transfers between devices  26.5 us (29%)
  Pallas kernels  12.8 us (14%)
  blocking collectives  10.1 us (11%)
  local copies, waits for them, and re-layouts  6.54 us (7%)
    all_to_all x5, starting transfers between devices, swap(): return lax.all_to_all(x, axis, 0, 0)  23.2 us
    ppermute x6, waiting for transfers between devices, over_chips(): return lax.ppermute(x, 'space', [(s, s ^ 2 * k) for s in range(n_s)])  13.1 us
    pallas_call x8, Pallas kernels, call(): pl.pallas_call(kernel, out_shape=out_shape, in_specs=[pl.BlockSpec(memory...  12.8 us
    all_to_all x5, waiting for transfers between devices, swap(): return lax.all_to_all(x, axis, 0, 0)  12.3 us
    all_to_all x1, blocking collectives, swap(): return lax.all_to_all(x, axis, 0, 0)  10.1 us
    ppermute x6, starting transfers between devices, over_chips(): return lax.ppermute(x, 'space', [(s, s ^ 2 * k) for s in range(n_s)])  9.45 us
    unnamed x30, local copies, waits for them, and re-layouts  6.54 us
  transfers between devices with their start and end apart: 20, of which 9 were waited for; matrix products, arithmetic and copies ran while one was open for 0% of the time, Pallas kernels for 12%

profile of v2, /device:TPU:0, one launch (start us, length us, event | category | flops | bytes accessed | tf_op | source)
XLA Modules:
  0.0 91.2 jit_solution(15937320778000587026)
XLA Ops:
  3.0 6.3 %all-to-all-start = ((bf16[4,2,128,128]{3,2,1,0:T(8,128)(2,1)}), bf16[4,2,128,128]{3,2,1,0:T(8,128)(2,1)S(1)}, u32[]{:S(2)}, u32[]{:S(2)}) async-start(bf16[4,2,128,128]{3,2,1,0:T(8,128)(2,1)} %shard_map.128), calls=%async_computation | async-start | bytes 524288 | tf_op jit(solution)/shard_map/all_to_all | solution.py:244
  9.3 1.5 %collective-permute-start.1 = (bf16[128,640]{1,0:T(8,128)(2,1)}, bf16[128,640]{1,0:T(8,128)(2,1)S(1)}, u32[]{:S(2)}, u32[]{:S(2)}) collective-permute-start(bf16[128,640]{1,0:T(8,128)(2,1)} %refs_0_.1), channel_id=1, source_target_pairs={{0,2},{1,3},{2,0},{3,1},{4,6},{5,7},{6,4},{7,5},{8,10},{9,11},{10,... | collective-permute-start | bytes 491528 | tf_op jit(solution)/shard_map/ppermute | solution.py:238
  10.8 1.5 %collective-permute-start.3 = (bf16[128,640]{1,0:T(8,128)(2,1)}, bf16[128,640]{1,0:T(8,128)(2,1)S(1)}, u32[]{:S(2)}, u32[]{:S(2)}) collective-permute-start(bf16[128,640]{1,0:T(8,128)(2,1)} %refs_0_.1), channel_id=1, source_target_pairs={{0,4},{1,5},{2,6},{3,7},{4,0},{5,1},{6,2},{7,3},{8,12},{9,13},{10,... | collective-permute-start | bytes 491528 | tf_op jit(solution)/shard_map/ppermute | solution.py:238
  12.8 3.5 %collective-permute-done.1.refs_2_ = bf16[128,640]{1,0:T(8,128)(2,1)S(1)} collective-permute-done((bf16[128,640]{1,0:T(8,128)(2,1)}, bf16[128,640]{1,0:T(8,128)(2,1)S(1)}, u32[]{:S(2)}, u32[]{:S(2)}) %collective-permute-start.1) | collective-permute-done | bytes 163872 | tf_op jit(solution)/shard_map/ppermute | solution.py:238
  16.3 3.6 %collective-permute-done.3.refs_4_ = bf16[128,640]{1,0:T(8,128)(2,1)S(1)} collective-permute-done((bf16[128,640]{1,0:T(8,128)(2,1)}, bf16[128,640]{1,0:T(8,128)(2,1)S(1)}, u32[]{:S(2)}, u32[]{:S(2)}) %collective-permute-start.3) | collective-permute-done | bytes 163872 | tf_op jit(solution)/shard_map/ppermute | solution.py:238
  20.4 0.9 %copy-done.3 = bf16[1024,128]{1,0:T(8,128)(2,1)S(1)} copy-done((bf16[1024,128]{1,0:T(8,128)(2,1)S(1)}, bf16[1024,128]{1,0:T(8,128)(2,1)}, u32[]{:S(2)}) %copy-start.3) | copy-done | bytes 262168
  22.0 1.9 %shard_map.130 = f32[4,2,512]{2,1,0:T(2,128)} custom-call(s32[4]{0:T(128)S(1)} %copy-done.12, bf16[1024,128]{1,0:T(8,128)(2,1)S(1)} %copy-done.3, bf16[4,2,128,128]{3,2,1,0:T(8,128)(2,1)S(1)} %all-to-all-done.packed_ref), custom_call_target="tpu_custom_call" | custom-call | flops 134217728 | bytes 524304 | tf_op jit(solution)/shard_map/pallas_call | solution.py:215
  23.9 5.0 %all-to-all-start.2 = ((f32[4,2,512]{2,1,0:T(2,128)}), f32[4,2,512]{2,1,0:T(2,128)S(1)}, u32[]{:S(2)}, u32[]{:S(2)}) async-start(f32[4,2,512]{2,1,0:T(2,128)} %shard_map.130), calls=%async_computation.2 | async-start | bytes 32768 | tf_op jit(solution)/shard_map/all_to_all | solution.py:244
  29.0 1.0 %copy-done.1 = f32[16,5120]{1,0:T(8,128)S(1)} copy-done((f32[16,5120]{1,0:T(8,128)S(1)}, f32[16,5120]{1,0:T(8,128)}, u32[]{:S(2)}) %copy-start.1) | copy-done | bytes 327704
  30.0 0.9 %copy-done.5 = bf16[128,640]{1,0:T(8,128)(2,1)S(1)} copy-done((bf16[128,640]{1,0:T(8,128)(2,1)S(1)}, bf16[128,640]{1,0:T(8,128)(2,1)}, u32[]{:S(2)}) %copy-start.5) | copy-done | bytes 163864
  32.3 2.2 %shard_map.129 = (bf16[4,128,128]{2,1,0:T(8,128)(2,1)}, f32[8,2,5120]{2,1,0:T(2,128)S(1)}) custom-call(s32[8]{0:T(128)S(1)} %copy-done.10, bf16[128,128]{1,0:T(8,128)(2,1)S(1)} %copy-done.8, bf16[128,5120]{1,0:T(8,128)(2,1)S(1)} %copy-done, f32[16,5120]{1,0:T(8,128)S(1)} %copy-done.1, bf16[128,640]{1,0:T(8,128)(2,1)S(1)} %copy-done.5, ...), custom_call_target="tpu_custom_call" | custom-call | flops 335544320 | bytes 2981920 | tf_op jit(solution)/shard_map/pallas_call | solution.py:215
  34.6 10.1 %all_to_all.30.terms_ref = f32[8,2,5120]{2,1,0:T(2,128)S(1)} all-to-all(f32[8,2,5120]{2,1,0:T(2,128)S(1)} %get-tuple-element.14), channel_id=1, replica_groups=mesh['tm'=4,'space'=8] {'space'}, dimensions={0} | all-to-all | bytes 655360 | tf_op jit(solution)/shard_map/all_to_all | solution.py:244
  44.7 5.0 %all-to-all-start.1 = ((bf16[4,128,128]{2,1,0:T(8,128)(2,1)}), bf16[4,128,128]{2,1,0:T(8,128)(2,1)S(1)}, u32[]{:S(2)}, u32[]{:S(2)}) async-start(bf16[4,128,128]{2,1,0:T(8,128)(2,1)} %get-tuple-element.10), calls=%async_computation.1 | async-start | bytes 262144 | tf_op jit(solution)/shard_map/all_to_all | solution.py:244
  50.5 5.4 %all-to-all-done.1.grads_ref = bf16[4,128,128]{2,1,0:T(8,128)(2,1)S(1)} async-done(((bf16[4,128,128]{2,1,0:T(8,128)(2,1)}), bf16[4,128,128]{2,1,0:T(8,128)(2,1)S(1)}, u32[]{:S(2)}, u32[]{:S(2)}) %all-to-all-start.1) | async-done | bytes 131104 | tf_op jit(solution)/shard_map/all_to_all | solution.py:244
  55.9 3.3 %all-to-all-start.5 = ((f32[4,2,5120]{2,1,0:T(2,128)}), f32[4,2,5120]{2,1,0:T(2,128)S(1)}, u32[]{:S(2)}, u32[]{:S(2)}) async-start(f32[4,2,5120]{2,1,0:T(2,128)} %shard_map.134), calls=%async_computation.5 | async-start | bytes 327680 | tf_op jit(solution)/shard_map/all_to_all | solution.py:244
  60.1 3.0 %shard_map.131 = (bf16[1024,128]{1,0:T(8,128)(2,1)}, bf16[1024,128]{1,0:T(8,128)(2,1)}, f32[4,128,128]{2,1,0:T(8,128)}) custom-call(s32[4]{0:T(128)S(1)} %copy-done.13, bf16[1024,128]{1,0:T(8,128)(2,1)S(1)} %copy-done.4, bf16[1024,128]{1,0:T(8,128)(2,1)S(1)} %copy-done.14, bf16[4,2,128,128]{3,2,1,0:T(8,128)(2,1)S(1)} %all-to-all-done.packed_ref, ...), custom_call_target="tpu_custom_call" | custom-call | flops 671088640 | bytes 933904 | tf_op jit(solution)/shard_map/pallas_call | solution.py:215
  63.1 6.8 %all-to-all-done.5.held = f32[4,2,5120]{2,1,0:T(2,128)S(1)} async-done(((f32[4,2,5120]{2,1,0:T(2,128)}), f32[4,2,5120]{2,1,0:T(2,128)S(1)}, u32[]{:S(2)}, u32[]{:S(2)}) %all-to-all-start.5) | async-done | bytes 163872 | tf_op jit(solution)/shard_map/all_to_all | solution.py:244
  69.9 3.4 %all-to-all-start.3 = ((f32[4,128,128]{2,1,0:T(8,128)}), f32[4,128,128]{2,1,0:T(8,128)S(1)}, u32[]{:S(2)}, u32[]{:S(2)}) async-start(f32[4,128,128]{2,1,0:T(8,128)} %get-tuple-element.11), calls=%async_computation.3 | async-start | bytes 524288 | tf_op jit(solution)/shard_map/all_to_all | solution.py:244
  73.4 4.5 %collective-permute-start.9 = (bf16[128,640]{1,0:T(8,128)(2,1)S(1)}, bf16[128,640]{1,0:T(8,128)(2,1)S(1)}, u32[]{:S(2)}, u32[]{:S(2)}) collective-permute-start(bf16[128,640]{1,0:T(8,128)(2,1)S(1)} %collective-permute-done.7.refs_0_), channel_id=1, source_target_pairs={{0,2},{1,3},{2,0},{3,1},{4,6},{5,7},{6,4},{7,5},{8,10},{9,11},{10,... | collective-permute-start | bytes 491528 | tf_op jit(solution)/shard_map/ppermute | solution.py:238
  77.9 1.5 %collective-permute-start.13 = (bf16[128,640]{1,0:T(8,128)(2,1)S(1)}, bf16[128,640]{1,0:T(8,128)(2,1)S(1)}, u32[]{:S(2)}, u32[]{:S(2)}) collective-permute-start(bf16[128,640]{1,0:T(8,128)(2,1)S(1)} %collective-permute-done.7.refs_0_), channel_id=1, source_target_pairs={{0,6},{1,7},{2,4},{3,5},{4,2},{5,3},{6,0},{7,1},{8,14},{9,15},{10,... | collective-permute-start | bytes 491528 | tf_op jit(solution)/shard_map/ppermute | solution.py:238
  79.3 3.3 %collective-permute-done.9.refs_2_ = bf16[128,640]{1,0:T(8,128)(2,1)S(1)} collective-permute-done((bf16[128,640]{1,0:T(8,128)(2,1)S(1)}, bf16[128,640]{1,0:T(8,128)(2,1)S(1)}, u32[]{:S(2)}, u32[]{:S(2)}) %collective-permute-start.9) | collective-permute-done | bytes 163872 | tf_op jit(solution)/shard_map/ppermute | solution.py:238
  82.7 2.7 %collective-permute-done.11.refs_4_ = bf16[128,640]{1,0:T(8,128)(2,1)S(1)} collective-permute-done((bf16[128,640]{1,0:T(8,128)(2,1)S(1)}, bf16[128,640]{1,0:T(8,128)(2,1)S(1)}, u32[]{:S(2)}, u32[]{:S(2)}) %collective-permute-start.11) | collective-permute-done | bytes 163872 | tf_op jit(solution)/shard_map/ppermute | solution.py:238
  87.0 2.1 %shard_map.133 = f32[128,1280]{1,0:T(8,128)} custom-call(s32[8]{0:T(128)S(1)} %copy-done.11, f32[16,5120]{1,0:T(8,128)S(1)} %copy-done.2, bf16[4,2,128,128]{3,2,1,0:T(8,128)(2,1)S(1)} %all-to-all-done.packed_ref, bf16[128,640]{1,0:T(8,128)(2,1)S(1)} %collective-permute-done.7.refs_0_, bf16[128,640]{1,0:T(8,128)(2,1)S(1)} %collective-permute-done.8.refs_1_, ...), custom_call_target="tpu_custom_call" | custom-call | flops 167772160 | bytes 1900576 | tf_op jit(solution)/shard_map/pallas_call | solution.py:215
  89.0 1.5 %shard_map.135 = f32[16,5120]{1,0:T(8,128)} custom-call(s32[8]{0:T(128)S(1)} %copy-done.11, f32[4,2,5120]{2,1,0:T(2,128)S(1)} %all-to-all-done.5.held), custom_call_target="tpu_custom_call" | custom-call | bytes 163872 | tf_op jit(solution)/shard_map/pallas_call | solution.py:215
  (55 shorter events, 9.4 us)
Async XLA Ops:
  0.6 28.4 %copy-start = (bf16[128,5120]{1,0:T(8,128)(2,1)S(1)}, bf16[128,5120]{1,0:T(8,128)(2,1)}, u32[]{:S(2)}) copy-start(bf16[128,5120]{1,0:T(8,128)(2,1)} %w_ref.1) | copy-start | bytes 3932164
  3.0 17.4 %all-to-all-start = ((bf16[4,2,128,128]{3,2,1,0:T(8,128)(2,1)}), bf16[4,2,128,128]{3,2,1,0:T(8,128)(2,1)S(1)}, u32[]{:S(2)}, u32[]{:S(2)}) async-start(bf16[4,2,128,128]{3,2,1,0:T(8,128)(2,1)} %shard_map.128), calls=%async_computation | async-start | bytes 524288 | tf_op jit(solution)/shard_map/all_to_all | solution.py:244
  9.3 7.0 %collective-permute-start.1 = (bf16[128,640]{1,0:T(8,128)(2,1)}, bf16[128,640]{1,0:T(8,128)(2,1)S(1)}, u32[]{:S(2)}, u32[]{:S(2)}) collective-permute-start(bf16[128,640]{1,0:T(8,128)(2,1)} %refs_0_.1), channel_id=1, source_target_pairs={{0,2},{1,3},{2,0},{3,1},{4,6},{5,7},{6,4},{7,5},{8,10},{9,11},{10,... | collective-permute-start | bytes 491528 | tf_op jit(solution)/shard_map/ppermute | solution.py:238
  10.8 9.1 %collective-permute-start.3 = (bf16[128,640]{1,0:T(8,128)(2,1)}, bf16[128,640]{1,0:T(8,128)(2,1)S(1)}, u32[]{:S(2)}, u32[]{:S(2)}) collective-permute-start(bf16[128,640]{1,0:T(8,128)(2,1)} %refs_0_.1), channel_id=1, source_target_pairs={{0,4},{1,5},{2,6},{3,7},{4,0},{5,1},{6,2},{7,3},{8,12},{9,13},{10,... | collective-permute-start | bytes 491528 | tf_op jit(solution)/shard_map/ppermute | solution.py:238
  12.3 7.6 %collective-permute-start.5 = (bf16[128,640]{1,0:T(8,128)(2,1)}, bf16[128,640]{1,0:T(8,128)(2,1)S(1)}, u32[]{:S(2)}, u32[]{:S(2)}) collective-permute-start(bf16[128,640]{1,0:T(8,128)(2,1)} %refs_0_.1), channel_id=1, source_target_pairs={{0,6},{1,7},{2,4},{3,5},{4,2},{5,3},{6,0},{7,1},{8,14},{9,15},{10,... | collective-permute-start | bytes 491528 | tf_op jit(solution)/shard_map/ppermute | solution.py:238
  12.8 16.2 %collective-permute-start = (bf16[128,640]{1,0:T(8,128)(2,1)}, bf16[128,640]{1,0:T(8,128)(2,1)S(1)}, u32[]{:S(2)}, u32[]{:S(2)}) collective-permute-start(bf16[128,640]{1,0:T(8,128)(2,1)} %refs_0_.1), channel_id=1, source_target_pairs={{0,1},{1,0},{2,3},{3,2},{4,5},{5,4},{6,7},{7,6},{8,9},{9,8},{10,11... | collective-permute-start | bytes 491528 | tf_op jit(solution)/shard_map/ppermute | solution.py:241
  16.3 12.7 %collective-permute-start.2 = (bf16[128,640]{1,0:T(8,128)(2,1)S(1)}, bf16[128,640]{1,0:T(8,128)(2,1)S(1)}, u32[]{:S(2)}, u32[]{:S(2)}) collective-permute-start(bf16[128,640]{1,0:T(8,128)(2,1)S(1)} %collective-permute-done.1.refs_2_), channel_id=1, source_target_pairs={{0,1},{1,0},{2,3},{3,2},{4,5},{5,4},{6,7},{7,6},{8,9},{9,8},{10,11... | collective-permute-start | bytes 491528 | tf_op jit(solution)/shard_map/ppermute | solution.py:241
  19.9 9.1 %collective-permute-start.4 = (bf16[128,640]{1,0:T(8,128)(2,1)S(1)}, bf16[128,640]{1,0:T(8,128)(2,1)S(1)}, u32[]{:S(2)}, u32[]{:S(2)}) collective-permute-start(bf16[128,640]{1,0:T(8,128)(2,1)S(1)} %collective-permute-done.3.refs_4_), channel_id=1, source_target_pairs={{0,1},{1,0},{2,3},{3,2},{4,5},{5,4},{6,7},{7,6},{8,9},{9,8},{10,11... | collective-permute-start | bytes 491528 | tf_op jit(solution)/shard_map/ppermute | solution.py:241
  19.9 9.1 %collective-permute-start.6 = (bf16[128,640]{1,0:T(8,128)(2,1)S(1)}, bf16[128,640]{1,0:T(8,128)(2,1)S(1)}, u32[]{:S(2)}, u32[]{:S(2)}) collective-permute-start(bf16[128,640]{1,0:T(8,128)(2,1)S(1)} %collective-permute-done.5.refs_6_), channel_id=1, source_target_pairs={{0,1},{1,0},{2,3},{3,2},{4,5},{5,4},{6,7},{7,6},{8,9},{9,8},{10,11... | collective-permute-start | bytes 491528 | tf_op jit(solution)/shard_map/ppermute | solution.py:241
  23.9 10.6 %all-to-all-start.2 = ((f32[4,2,512]{2,1,0:T(2,128)}), f32[4,2,512]{2,1,0:T(2,128)S(1)}, u32[]{:S(2)}, u32[]{:S(2)}) async-start(f32[4,2,512]{2,1,0:T(2,128)} %shard_map.130), calls=%async_computation.2 | async-start | bytes 32768 | tf_op jit(solution)/shard_map/all_to_all | solution.py:244
  34.5 25.5 %copy-start.14 = (bf16[1024,128]{1,0:T(8,128)(2,1)S(1)}, bf16[1024,128]{1,0:T(8,128)(2,1)}, u32[]{:S(2)}) copy-start(bf16[1024,128]{1,0:T(8,128)(2,1)} %values_ref.1) | copy-start | bytes 786436
  44.7 11.1 %all-to-all-start.1 = ((bf16[4,128,128]{2,1,0:T(8,128)(2,1)}), bf16[4,128,128]{2,1,0:T(8,128)(2,1)S(1)}, u32[]{:S(2)}, u32[]{:S(2)}) async-start(bf16[4,128,128]{2,1,0:T(8,128)(2,1)} %get-tuple-element.10), calls=%async_computation.1 | async-start | bytes 262144 | tf_op jit(solution)/shard_map/all_to_all | solution.py:244
  55.9 14.1 %all-to-all-start.5 = ((f32[4,2,5120]{2,1,0:T(2,128)}), f32[4,2,5120]{2,1,0:T(2,128)S(1)}, u32[]{:S(2)}, u32[]{:S(2)}) async-start(f32[4,2,5120]{2,1,0:T(2,128)} %shard_map.134), calls=%async_computation.5 | async-start | bytes 327680 | tf_op jit(solution)/shard_map/all_to_all | solution.py:244
  59.2 27.8 %copy-start.2 = (f32[16,5120]{1,0:T(8,128)S(1)}, f32[16,5120]{1,0:T(8,128)}, u32[]{:S(2)}) copy-start(f32[16,5120]{1,0:T(8,128)} %gate_ref.3) | copy-start | bytes 983044
  59.2 27.8 %copy-start.11 = (s32[8]{0:T(128)S(1)}, s32[8]{0:T(128)}, u32[]{:S(2)}) copy-start(s32[8]{0:T(128)} %levels_ref.5) | copy-start | bytes 100
  59.2 14.1 %collective-permute-start.7 = (bf16[128,640]{1,0:T(8,128)(2,1)S(1)}, bf16[128,640]{1,0:T(8,128)(2,1)S(1)}, u32[]{:S(2)}, u32[]{:S(2)}) collective-permute-start(bf16[128,640]{1,0:T(8,128)(2,1)S(1)} %copy-done.6), channel_id=1, source_target_pairs={{0,0},{1,1},{2,10},{3,11},{4,20},{5,21},{6,30},{7,31},{8,2},{9,3},... | collective-permute-start | bytes 491528 | tf_op jit(solution)/shard_map/ppermute | solution.py:260
  69.9 20.6 %all-to-all-start.3 = ((f32[4,128,128]{2,1,0:T(8,128)}), f32[4,128,128]{2,1,0:T(8,128)S(1)}, u32[]{:S(2)}, u32[]{:S(2)}) async-start(f32[4,128,128]{2,1,0:T(8,128)} %get-tuple-element.11), calls=%async_computation.3 | async-start | bytes 524288 | tf_op jit(solution)/shard_map/all_to_all | solution.py:244
  73.4 9.3 %collective-permute-start.9 = (bf16[128,640]{1,0:T(8,128)(2,1)S(1)}, bf16[128,640]{1,0:T(8,128)(2,1)S(1)}, u32[]{:S(2)}, u32[]{:S(2)}) collective-permute-start(bf16[128,640]{1,0:T(8,128)(2,1)S(1)} %collective-permute-done.7.refs_0_), channel_id=1, source_target_pairs={{0,2},{1,3},{2,0},{3,1},{4,6},{5,7},{6,4},{7,5},{8,10},{9,11},{10,... | collective-permute-start | bytes 491528 | tf_op jit(solution)/shard_map/ppermute | solution.py:238
  77.9 7.5 %collective-permute-start.11 = (bf16[128,640]{1,0:T(8,128)(2,1)S(1)}, bf16[128,640]{1,0:T(8,128)(2,1)S(1)}, u32[]{:S(2)}, u32[]{:S(2)}) collective-permute-start(bf16[128,640]{1,0:T(8,128)(2,1)S(1)} %collective-permute-done.7.refs_0_), channel_id=1, source_target_pairs={{0,4},{1,5},{2,6},{3,7},{4,0},{5,1},{6,2},{7,3},{8,12},{9,13},{10,... | collective-permute-start | bytes 491528 | tf_op jit(solution)/shard_map/ppermute | solution.py:238
  77.9 7.5 %collective-permute-start.13 = (bf16[128,640]{1,0:T(8,128)(2,1)S(1)}, bf16[128,640]{1,0:T(8,128)(2,1)S(1)}, u32[]{:S(2)}, u32[]{:S(2)}) collective-permute-start(bf16[128,640]{1,0:T(8,128)(2,1)S(1)} %collective-permute-done.7.refs_0_), channel_id=1, source_target_pairs={{0,6},{1,7},{2,4},{3,5},{4,2},{5,3},{6,0},{7,1},{8,14},{9,15},{10,... | collective-permute-start | bytes 491528 | tf_op jit(solution)/shard_map/ppermute | solution.py:238
  79.3 6.5 %collective-permute-start.8 = (bf16[128,640]{1,0:T(8,128)(2,1)S(1)}, bf16[128,640]{1,0:T(8,128)(2,1)S(1)}, u32[]{:S(2)}, u32[]{:S(2)}) collective-permute-start(bf16[128,640]{1,0:T(8,128)(2,1)S(1)} %collective-permute-done.7.refs_0_), channel_id=1, source_target_pairs={{0,1},{1,0},{2,3},{3,2},{4,5},{5,4},{6,7},{7,6},{8,9},{9,8},{10,11... | collective-permute-start | bytes 491528 | tf_op jit(solution)/shard_map/ppermute | solution.py:241
  82.7 3.2 %collective-permute-start.10 = (bf16[128,640]{1,0:T(8,128)(2,1)S(1)}, bf16[128,640]{1,0:T(8,128)(2,1)S(1)}, u32[]{:S(2)}, u32[]{:S(2)}) collective-permute-start(bf16[128,640]{1,0:T(8,128)(2,1)S(1)} %collective-permute-done.9.refs_2_), channel_id=1, source_target_pairs={{0,1},{1,0},{2,3},{3,2},{4,5},{5,4},{6,7},{7,6},{8,9},{9,8},{10,11... | collective-permute-start | bytes 491528 | tf_op jit(solution)/shard_map/ppermute | solution.py:241
  85.3 1.4 %collective-permute-start.12 = (bf16[128,640]{1,0:T(8,128)(2,1)S(1)}, bf16[128,640]{1,0:T(8,128)(2,1)S(1)}, u32[]{:S(2)}, u32[]{:S(2)}) collective-permute-start(bf16[128,640]{1,0:T(8,128)(2,1)S(1)} %collective-permute-done.11.refs_4_), channel_id=1, source_target_pairs={{0,1},{1,0},{2,3},{3,2},{4,5},{5,4},{6,7},{7,6},{8,9},{9,8},{10,11... | collective-permute-start | bytes 491528 | tf_op jit(solution)/shard_map/ppermute | solution.py:241
  85.4 1.6 %collective-permute-start.14 = (bf16[128,640]{1,0:T(8,128)(2,1)S(1)}, bf16[128,640]{1,0:T(8,128)(2,1)S(1)}, u32[]{:S(2)}, u32[]{:S(2)}) collective-permute-start(bf16[128,640]{1,0:T(8,128)(2,1)S(1)} %collective-permute-done.13.refs_6_), channel_id=1, source_target_pairs={{0,1},{1,0},{2,3},{3,2},{4,5},{5,4},{6,7},{7,6},{8,9},{9,8},{10,11... | collective-permute-start | bytes 491528 | tf_op jit(solution)/shard_map/ppermute | solution.py:241
  (11 other events, 82.3 us)

commit v3 on v2

v3 whole, which is shorter than its diff:
```python
import functools
import math

import jax
import jax.numpy as jnp
from jax import lax
from jax.experimental import pallas as pl
from jax.experimental.pallas import tpu as pltpu
from jax.sharding import PartitionSpec as P

HD = 128
SPF = 512
QF = 64
LANES = 128
NEG_BIG = -1e30
SCALE = 1.0 / math.sqrt(HD)
VMEM_LIMIT = 32 * 1024 * 1024
SPLIT = 3


def dot(a, b, on_a, on_b):
    return lax.dot_general(
        a, b, (((on_a,), (on_b,)), ((), ())), preferred_element_type=jnp.float32
    )


def place():
    s = lax.axis_index("space")
    return lax.axis_index("tm"), s // 2, s % 2


def clip_numbers(clips_ref):
    bounds = []
    so_far = 0
    for c in range(clips_ref.shape[0]):
        so_far = so_far + clips_ref[c]
        bounds.append(so_far)
    return lambda frame: sum((frame >= bound).astype(jnp.int32) for bound in bounds)


def prep_kernel(
    n_t, chips, frames, levels_in, clips_in, queries_in, saved_in, keys_in, values_in, grad_in,
    weight_in, gate_in, packed, kept, sent, keys, values, grad, bias, gate_a, gate_b, hot,
    gate, levels, clips, sems,
):
    t, chip, core = place()
    rows = grad.shape[0]
    width = grad.shape[1]

    def columns(k, c):
        return pl.ds(pl.multiple_of((2 * (chip ^ k) + c) * width, LANES), width)

    moves = [(levels_in, levels), (clips_in, clips), (queries_in, packed.at[0]), (saved_in, packed.at[1])]
    for k in range(chips):
        moves.append((weight_in.at[:, columns(k, 1 - core)], sent.at[:, k * width : (k + 1) * width]))
    moves.append((saved_in, sent.at[:, chips * width : chips * width + HD]))
    moves.append((gate_in, gate))
    moves.append((keys_in, keys))
    for k in range(chips):
        moves.append((weight_in.at[:, columns(k, core)], kept.at[k]))
    moves.append((grad_in, grad))
    moves.append((values_in, values))
    copies = [pltpu.make_async_copy(a, b, sems.at[i]) for i, (a, b) in enumerate(moves)]
    for copy in copies:
        copy.start()
    copies[0].wait()
    copies[1].wait()
    clip_of = clip_numbers(clips)
    lane = lax.broadcasted_iota(jnp.int32, (1, rows), 1)
    for kf in range(frames):
        key_frame = t * frames + kf
        key_clip = clip_of(key_frame)
        for k in range(n_t):
            row = jnp.full((1, rows), NEG_BIG, jnp.float32)
            for r in range(frames):
                frame = (t ^ k) * frames + r
                visible = (key_frame >= frame) & (clip_of(frame) == key_clip)
                value = jnp.where(visible, 0.0, NEG_BIG).astype(jnp.float32)
                row = jnp.where((lane >= r * QF) & (lane < (r + 1) * QF), value, row)
            bias[kf : kf + 1, k * rows : (k + 1) * rows] = row
    spot = lax.broadcasted_iota(jnp.int32, hot.shape[1:], 0)
    for f in range(n_t * frames):
        hot[f] = (spot == levels[f]).astype(jnp.float32)
    for copy in copies[2:]:
        copy.wait()
    for r in range(frames):
        level = levels[t * frames + r]
        for k in range(chips):
            gate_a[k, r : r + 1, :] = gate[pl.ds(level, 1), columns(k, core)]
        for k in range(n_t):
            level = levels[(t ^ chip ^ k) * frames + r]
            mine = pl.ds(pl.multiple_of((2 * t + core) * width, LANES), width)
            gate_b[k, r : r + 1, :] = gate[pl.ds(level, 1), mine]


def stats_kernel(n_t, bias, keys, *refs):
    packed, out = refs[:n_t], refs[n_t]
    rows = packed[0].shape[1]
    for p in range(0, n_t, 2):
        q = jnp.concatenate([packed[p][0], packed[p + 1][0]], axis=0)
        scores = []
        for kf in range(bias.shape[0]):
            mask = bias[kf : kf + 1, p * rows : (p + 2) * rows]
            scores.append(dot(keys[kf * SPF : (kf + 1) * SPF, :], q, 1, 1) * SCALE + mask)
        top = functools.reduce(jnp.maximum, [jnp.max(x, axis=0, keepdims=True) for x in scores])
        total = sum(jnp.sum(jnp.exp(x - top), axis=0, keepdims=True) for x in scores)
        for i in range(2):
            out[p + i : p + i + 1, :] = top[:, i * rows : (i + 1) * rows]
            out[n_t + p + i : n_t + p + i + 1, :] = total[:, i * rows : (i + 1) * rows]


def head_kernel(chips, frames, packed, kept, received, gate_a, *refs):
    pieces, (mine, other, terms) = refs[:chips], refs[chips:]
    _, chip, _ = place()
    width = pieces[0].shape[1]
    saved = jnp.concatenate([packed[1], received[:, chips * width : chips * width + HD]], axis=1)
    head = None
    for k in range(chips):
        weight = jnp.concatenate([kept[k], received[:, k * width : (k + 1) * width]], axis=0)
        wide = pieces[k][...].astype(jnp.float32)
        gated = jnp.concatenate(
            [
                (wide[r * QF : (r + 1) * QF] * gate_a[k, r : r + 1, :]).astype(jnp.bfloat16)
                for r in range(frames)
            ],
            axis=0,
        )
        part = dot(gated, weight, 1, 1)
        head = part if head is None else head + part
        product = wide * dot(saved, weight, 1, 0)
        for r in range(frames):
            term = jnp.sum(product[r * QF : (r + 1) * QF], axis=0, keepdims=True)
            terms[chip ^ k, r : r + 1, :] = term
    mine[...] = head[:, :HD]
    other[...] = head[:, HD:]


def join_kernel(mine, received, stats, out):
    rows = mine.shape[0]
    out[:rows, :] = (mine[...] + received[...]).astype(jnp.bfloat16)
    rest = stats[...]
    parts = []
    for _ in range(SPLIT):
        part = rest.astype(jnp.bfloat16).astype(jnp.float32)
        parts.append(part)
        rest = rest - part
    pad = out.shape[0] - rows - SPLIT * rest.shape[0]
    if pad:
        parts.append(jnp.zeros((pad, LANES), jnp.float32))
    out[rows:, :] = jnp.concatenate(parts, axis=0).astype(jnp.bfloat16)


def terms_kernel(chips, *refs):
    pieces, out, held = refs[:chips], refs[chips], refs[chips + 1]
    _, chip, _ = place()
    for k in range(chips):
        held[chip ^ k] = pieces[k][...]
    total = held[0]
    for k in range(1, chips):
        total = total + held[k]
    row = 0
    for a in range(total.shape[0]):
        for r in range(total.shape[1]):
            for j in range(0, total.shape[2], LANES):
                out[row : row + 1, :] = total[a, r : r + 1, j : j + LANES]
                row += 1


def grads_kernel(n_t, bias, keys, values, own_terms, other_terms, *refs):
    packed, heads = refs[:n_t], refs[n_t : 2 * n_t]
    key_out, value_out = refs[2 * n_t : 2 * n_t + 2]
    outs = refs[2 * n_t + 2 : 3 * n_t + 2]
    key_acc, value_acc = refs[3 * n_t + 2 :]
    core = place()[2]
    rows = packed[0].shape[1]
    count = own_terms.shape[0]
    ones = jnp.ones((8, HD), jnp.float32)
    keys_t = jnp.transpose(keys[...])
    stats = []
    for k in range(n_t):
        parts = heads[k][rows:, :].astype(jnp.float32)
        stats.append(sum(parts[i * 2 * n_t : (i + 1) * 2 * n_t] for i in range(SPLIT)))
    own, other = own_terms[...], other_terms[...]
    first, second = jnp.where(core == 0, own, other), jnp.where(core == 0, other, own)
    for k in range(n_t):
        outs[k][rows : rows + count, :] = first
        outs[k][rows + count :, :] = second
    for p in range(0, n_t, 2):
        q = jnp.concatenate([packed[p][0], packed[p + 1][0]], axis=0)
        o = jnp.concatenate([packed[p][1], packed[p + 1][1]], axis=0)
        g = jnp.concatenate([heads[p][:rows, :], heads[p + 1][:rows, :]], axis=0)
        delta = lax.dot_general(
            ones,
            g.astype(jnp.float32) * o.astype(jnp.float32),
            (((1,), (1,)), ((), ())),
            precision=lax.Precision.HIGHEST,
            preferred_element_type=jnp.float32,
        )[0:1]
        lse = []
        for i in (p, p + 1):
            tops = [stats[k][i ^ k : (i ^ k) + 1] for k in range(n_t)]
            sums = [stats[k][n_t + (i ^ k) : n_t + (i ^ k) + 1] for k in range(n_t)]
            top = functools.reduce(jnp.maximum, tops)
            lse.append(top + jnp.log(sum(b * jnp.exp(a - top) for a, b in zip(tops, sums))))
        lse = jnp.concatenate(lse, axis=1)
        query_part = None
        for kf in range(bias.shape[0]):
            span = slice(kf * SPF, (kf + 1) * SPF)
            shift = bias[kf : kf + 1, p * rows : (p + 2) * rows] - lse
            probs = jnp.exp(dot(keys[span, :], q, 1, 1) * SCALE + shift)
            score_grad = (probs * (dot(values[span, :], g, 1, 1) - delta)).astype(jnp.bfloat16)
            value_add = dot(probs.astype(jnp.bfloat16), g, 1, 0)
            key_add = dot(score_grad, q, 1, 0)
            if p > 0:
                value_add = value_add + value_acc[span, :]
                key_add = key_add + key_acc[span, :]
            if p + 2 < n_t:
                value_acc[span, :] = value_add
                key_acc[span, :] = key_add
            else:
                value_out[span, :] = value_add.astype(jnp.bfloat16)
                key_out[span, :] = (key_add * SCALE).astype(jnp.bfloat16)
            part = dot(keys_t[:, span], score_grad, 1, 0)
            query_part = part if query_part is None else query_part + part
        outs[p][:rows, :] = query_part[:, :rows]
        outs[p + 1][:rows, :] = query_part[:, rows:]


def finish_kernel(n_t, chips, frames, hot, *refs):
    parts, (query_out, gate_out, held) = refs[:n_t], refs[n_t:]
    t = lax.axis_index("tm")
    rows = query_out.shape[0]
    total = parts[0][:rows, :]
    for k in range(1, n_t):
        total = total + parts[k][:rows, :]
    query_out[...] = jnp.transpose(total * SCALE).astype(jnp.bfloat16)
    for k in range(n_t):
        held[t ^ k] = parts[k][rows:, :]
    tiles = gate_out.shape[1] // (2 * chips * LANES)
    for core in range(2):
        for a in range(chips):
            for j in range(tiles):
                total = jnp.zeros(hot.shape[1:], jnp.float32)
                for f in range(n_t * frames):
                    row = ((core * chips + a) * frames + f % frames) * tiles + j
                    total = total + hot[f] * held[f // frames, row : row + 1, :]
                column = ((2 * a + core) * tiles + j) * LANES
                gate_out[:, column : column + LANES] = total


def gated_kernel(n_t, frames, gate_b, *refs):
    pieces, out = refs[:n_t], refs[n_t]
    for k in range(n_t):
        for r in range(frames):
            span = slice(r * QF, (r + 1) * QF)
            wide = pieces[k][span, :].astype(jnp.float32)
            out[k, span, :] = (wide * gate_b[k, r : r + 1, :]).astype(jnp.bfloat16)


def weight_kernel(n_t, own, other, *refs):
    packed, out, held = refs[:n_t], refs[n_t], refs[n_t + 1]
    _, chip, core = place()
    width = own.shape[2]
    for k in range(n_t):
        held[k] = packed[k][1]
    saved = jnp.concatenate([held[chip ^ k] for k in range(n_t)], axis=0)
    for ref, half in ((own, core), (other, 1 - core)):
        gated = jnp.concatenate([ref[k] for k in range(n_t)], axis=0)
        result = dot(saved, gated, 0, 0)
        for h in range(2):

            @pl.when(half == h)
            def _():
                out[:, h * width : (h + 1) * width] = result


def call(kernel, args, out_shape, scratch=(), flops=0, in_place=False):
    vmem = pl.BlockSpec(memory_space=pltpu.VMEM)
    single = not isinstance(out_shape, (list, tuple))
    nbytes = sum(a.size * a.dtype.itemsize for a in args)
    return pl.pallas_call(
        kernel,
        out_shape=out_shape,
        in_specs=[pl.BlockSpec(memory_space=pltpu.HBM) if in_place else vmem] * len(args),
        out_specs=vmem if single else [vmem] * len(out_shape),
        scratch_shapes=list(scratch),
        compiler_params=pltpu.CompilerParams(vmem_limit_bytes=VMEM_LIMIT),
        cost_estimate=pl.CostEstimate(flops=flops, bytes_accessed=nbytes, transcendentals=0),
    )(*args)


def padded_shards(table, n_s, width):
    rows, columns = table.shape
    cut = table.reshape(rows, n_s, columns // n_s)
    cut = jnp.pad(cut, ((0, 0), (0, 0), (0, width - columns // n_s)))
    return cut.reshape(rows, n_s * width)


def without_padding(table, shards, shard):
    rows, columns = table.shape
    return table.reshape(rows, shards, columns // shards)[:, :, :shard].reshape(rows, shards * shard)


def body(
    queries, keys, values, saved_out, out_grad, proj_weight, gate_table, noise_levels, clip_lengths
):
    n_t, n_s = lax.axis_size("tm"), lax.axis_size("space")
    chips = n_s // 2
    rows, shard = out_grad.shape
    k_rows = keys.shape[0]
    frames = rows // QF
    levels = gate_table.shape[0]
    bf16, f32 = jnp.bfloat16, jnp.float32
    width = -(-shard // LANES) * LANES
    if width != shard:
        out_grad = jnp.pad(out_grad, ((0, 0), (0, width - shard)))
        proj_weight = padded_shards(proj_weight, n_s, width)
        gate_table = padded_shards(gate_table, n_s, width)

    def shape(dtype, *dims):
        return jax.ShapeDtypeStruct(dims, dtype)

    def over_chips(x):
        return [x] + [
            lax.ppermute(x, "space", [(s, s ^ (2 * k)) for s in range(n_s)]) for k in range(1, chips)
        ]

    def over_cores(x):
        return lax.ppermute(x, "space", [(s, s ^ 1) for s in range(n_s)])

    def over_time(x, k):
        return lax.ppermute(x, "tm", [(t, t ^ k) for t in range(n_t)])

    pieces = over_chips(out_grad)
    moves = [
        (t * n_s + 2 * c + e, c * n_s + 2 * (c ^ t) + e)
        for t in range(n_t)
        for c in range(chips)
        for e in range(2)
    ]
    moved = lax.ppermute(out_grad, ("tm", "space"), moves)
    packed, kept, sent, keys, values, own_grad, bias, gate_a, gate_b, hot = call(
        functools.partial(prep_kernel, n_t, chips, frames),
        [noise_levels, clip_lengths, queries, saved_out, keys, values, out_grad, proj_weight, gate_table],
        [
            shape(bf16, 2, rows, HD),
            shape(bf16, chips, HD, width),
            shape(bf16, HD, chips * width + HD),
            shape(bf16, k_rows, HD),
            shape(bf16, k_rows, HD),
            shape(bf16, rows, width),
            shape(f32, frames, n_t * rows),
            shape(f32, chips, frames, width),
            shape(f32, n_t, frames, width),
            shape(f32, n_t * frames, levels, LANES),
        ],
        [
            pltpu.VMEM((levels, n_s * width), f32),
            pltpu.SMEM(noise_levels.shape, jnp.int32),
            pltpu.SMEM(clip_lengths.shape, jnp.int32),
            pltpu.SemaphoreType.DMA((2 * chips + 9,)),
        ],
        in_place=True,
    )
    received = over_cores(sent)
    packed_all = [packed] + [over_time(packed, k) for k in range(1, n_t)]
    stats = call(
        functools.partial(stats_kernel, n_t),
        [bias, keys] + packed_all,
        shape(f32, 2 * n_t, LANES),
        flops=2 * n_t * rows * k_rows * HD,
    )
    gate_a, _ = lax.optimization_barrier((gate_a, stats))
    mine, other, terms = call(
        functools.partial(head_kernel, chips, frames),
        [packed, kept, received, gate_a, own_grad] + pieces[1:],
        [shape(f32, rows, HD), shape(f32, rows, HD), shape(f32, chips, frames, width)],
        flops=4 * rows * chips * width * 2 * HD,
    )
    extra = -(-SPLIT * 2 * n_t // 16) * 16
    joined = call(join_kernel, [mine, over_cores(other), stats], shape(bf16, rows + extra, HD))
    moved, joined = lax.optimization_barrier((moved, joined))
    row_pieces = over_chips(moved)
    heads_all = [joined] + [over_time(joined, k) for k in range(1, n_t)]

    count = chips * frames * width // LANES
    own_terms = call(
        functools.partial(terms_kernel, chips),
        over_chips(terms),
        shape(f32, count, LANES),
        [pltpu.VMEM((chips, chips, frames, width), f32)],
    )
    outs = call(
        functools.partial(grads_kernel, n_t),
        [bias, keys, values, own_terms, over_cores(own_terms)] + packed_all + heads_all,
        [shape(bf16, k_rows, HD)] * 2 + [shape(f32, rows + 2 * count, LANES)] * n_t,
        [pltpu.VMEM((k_rows, HD), f32)] * 2,
        flops=10 * n_t * rows * k_rows * HD,
    )
    key_grad, value_grad, parts = outs[0], outs[1], outs[2:]
    row_pieces, _ = lax.optimization_barrier((row_pieces, parts[0]))
    parts = [parts[0]] + [over_time(parts[k], k) for k in range(1, n_t)]

    gated = call(
        functools.partial(gated_kernel, n_t, frames),
        [gate_b] + row_pieces,
        shape(bf16, n_t, rows, width),
    )
    weight_grad = call(
        functools.partial(weight_kernel, n_t),
        [gated, over_cores(gated)] + packed_all,
        shape(f32, HD, 2 * width),
        [pltpu.VMEM((n_t, rows, HD), bf16)],
        flops=4 * n_t * rows * width * HD,
    )
    query_grad, gate_grad = call(
        functools.partial(finish_kernel, n_t, chips, frames),
        [hot] + parts,
        [shape(bf16, rows, HD), shape(f32, levels, n_s * width)],
        [pltpu.VMEM((n_t, 2 * count, LANES), f32)],
    )
    if width != shard:
        weight_grad = without_padding(weight_grad, 2, shard)
        gate_grad = without_padding(gate_grad, n_s, shard)
    return (query_grad, key_grad, value_grad, weight_grad, gate_grad)


def solution(mesh):
    return jax.shard_map(
        body,
        mesh=mesh,
        in_specs=(
            P("tm", "space"),
            P("tm", "space"),
            P("tm", "space"),
            P("tm", "space"),
            P("tm", "space"),
            P("space", None),
            P(),
            P(),
            P(),
        ),
        out_specs=(P("tm", "space"), P("tm", "space"), P("tm", "space"), P("space", "tm"), P()),
        check_vma=False,
    )
```

time: 92.1 us -> 72.1 us (0.78)
  blocking collectives: 10.1 us -> 0 us
  waiting for transfers between devices: 26.5 us -> 19.8 us
  Pallas kernels: 12.8 us -> 8.01 us
  starting transfers between devices: 34.4 us -> 35.9 us
    ppermute x6 -> x18, starting transfers between devices: 9.45 us -> 33.6 us  [the longest x9 18.3 us: over_chips(): lax.ppermute(x, 'space', [(s, s ^ 2 * k) for s in range(n_s)])]
    all_to_all x5 -> x0, starting transfers between devices: 23.2 us -> none  [swap(): return lax.all_to_all(x, axis, 0, 0)]
    all_to_all x5 -> x0, waiting for transfers between devices: 12.3 us -> none  [swap(): return lax.all_to_all(x, axis, 0, 0)]
    all_to_all x1 -> x0, blocking collectives: 10.1 us -> none  [swap(): return lax.all_to_all(x, axis, 0, 0)]
    ppermute x6 -> x18, waiting for transfers between devices: 13.1 us -> 18.6 us  [the longest x9 15 us: over_time(): return lax.ppermute(x, 'tm', [(t, t ^ k) for t in range(n_t)])]
    pallas_call x8 -> x9, Pallas kernels: 12.8 us -> 8.01 us  [call(): pl.pallas_call(kernel, out_shape=out_shape, in_specs=[pl.BlockSpec(memory...]
    unnamed x30 -> x16, local copies, waits for them, and re-layouts: 6.54 us -> 7 us
  transfers between devices with their start and end apart: 20 -> 23, of which waited for: 9 -> 8; matrix products, arithmetic and copies ran while one was open for 0% -> 0% of each run, Pallas kernels for 12% -> 7%
where the time goes in v3:
time: 72.1 us; the launch traced here: 71.5 us
  starting transfers between devices  35.9 us (50%)
  waiting for transfers between devices  19.8 us (27%)
  Pallas kernels  8.01 us (11%)
  local copies, waits for them, and re-layouts  7 us (10%)
  between operations  0.76 us (1%)
    ppermute x9, starting transfers between devices, over_chips(): lax.ppermute(x, 'space', [(s, s ^ 2 * k) for s in range(n_s)])  18.3 us
    ppermute x9, starting transfers between devices, over_time(): return lax.ppermute(x, 'tm', [(t, t ^ k) for t in range(n_t)])  15.4 us
    ppermute x9, waiting for transfers between devices, over_time(): return lax.ppermute(x, 'tm', [(t, t ^ k) for t in range(n_t)])  15 us
    pallas_call x9, Pallas kernels, call(): pl.pallas_call(kernel, out_shape=out_shape, in_specs=[pl.BlockSpec(memory...  8.01 us
    unnamed x16, local copies, waits for them, and re-layouts  7 us
    ppermute x9, waiting for transfers between devices, over_chips(): lax.ppermute(x, 'space', [(s, s ^ 2 * k) for s in range(n_s)])  3.63 us
    ppermute x1, starting transfers between devices, body(): moved = lax.ppermute(out_grad, ('tm', 'space'), moves)  1.56 us
  transfers between devices with their start and end apart: 23, of which 8 were waited for; matrix products, arithmetic and copies ran while one was open for 0% of the time, Pallas kernels for 7%

profile of v3, /device:TPU:0, one launch (start us, length us, event | category | flops | bytes accessed | tf_op | source)
XLA Modules:
  0.0 71.5 jit_solution(6287480758672950351)
XLA Ops:
  0.6 1.3 %copy-done = bf16[128,5120]{1,0:T(8,128)(2,1)S(1)} copy-done((bf16[128,5120]{1,0:T(8,128)(2,1)S(1)}, bf16[128,5120]{1,0:T(8,128)(2,1)}, u32[]{:S(2)}) %copy-start) | copy-done | bytes 1310744
  7.7 1.5 %shard_map.128 = (bf16[2,128,128]{2,1,0:T(8,128)(2,1)S(1)}, bf16[4,128,640]{2,1,0:T(8,128)(2,1)S(1)}, bf16[128,2688]{1,0:T(8,128)(2,1)S(1)}, bf16[1024,128]{1,0:...) custom-call(s32[8]{0:T(128)S(1)} %copy-done.6, ...), custom_call_target="tpu_custom_call" | custom-call | bytes 2392112 | tf_op jit(solution)/shard_map/pallas_call | solution.py:281
  9.7 2.6 %collective-permute-start.1 = (bf16[2,128,128]{2,1,0:T(8,128)(2,1)S(1)}, bf16[2,128,128]{2,1,0:T(8,128)(2,1)S(1)}, u32[]{:S(2)}, u32[]{:S(2)}) collective-permute-start(bf16[2,128,128]{2,1,0:T(8,128)(2,1)S(1)} %get-tuple-element.37.refs_0_.packed), channel_id=1, source_target_pairs={{0,8},{8,0},{16,24},{24,16},{1,9},{9,1},{17,25},{25,17},{2,10},{10... | collective-permute-start | bytes 196616 | tf_op jit(solution)/shard_map/ppermute | solution.py:332
  12.3 2.6 %collective-permute-start.2 = (bf16[2,128,128]{2,1,0:T(8,128)(2,1)S(1)}, bf16[2,128,128]{2,1,0:T(8,128)(2,1)S(1)}, u32[]{:S(2)}, u32[]{:S(2)}) collective-permute-start(bf16[2,128,128]{2,1,0:T(8,128)(2,1)S(1)} %get-tuple-element.37.refs_0_.packed), channel_id=1, source_target_pairs={{0,16},{8,24},{16,0},{24,8},{1,17},{9,25},{17,1},{25,9},{2,18},{10... | collective-permute-start | bytes 196616 | tf_op jit(solution)/shard_map/ppermute | solution.py:332
  14.9 1.5 %collective-permute-start.4 = (bf16[128,640]{1,0:T(8,128)(2,1)}, bf16[128,640]{1,0:T(8,128)(2,1)S(1)}, u32[]{:S(2)}, u32[]{:S(2)}) collective-permute-start(bf16[128,640]{1,0:T(8,128)(2,1)} %grad_in.1), channel_id=1, source_target_pairs={{0,2},{1,3},{2,0},{3,1},{4,6},{5,7},{6,4},{7,5},{8,10},{9,11},{10,... | collective-permute-start | bytes 491528 | tf_op jit(solution)/shard_map/ppermute | solution.py:325
  16.4 1.5 %collective-permute-start.5 = (bf16[128,640]{1,0:T(8,128)(2,1)}, bf16[128,640]{1,0:T(8,128)(2,1)S(1)}, u32[]{:S(2)}, u32[]{:S(2)}) collective-permute-start(bf16[128,640]{1,0:T(8,128)(2,1)} %grad_in.1), channel_id=1, source_target_pairs={{0,4},{1,5},{2,6},{3,7},{4,0},{5,1},{6,2},{7,3},{8,12},{9,13},{10,... | collective-permute-start | bytes 491528 | tf_op jit(solution)/shard_map/ppermute | solution.py:325
  18.9 3.4 %collective-permute-start.3 = (bf16[2,128,128]{2,1,0:T(8,128)(2,1)S(1)}, bf16[2,128,128]{2,1,0:T(8,128)(2,1)S(1)}, u32[]{:S(2)}, u32[]{:S(2)}) collective-permute-start(bf16[2,128,128]{2,1,0:T(8,128)(2,1)S(1)} %get-tuple-element.37.refs_0_.packed), channel_id=1, source_target_pairs={{0,24},{8,16},{16,8},{24,0},{1,25},{9,17},{17,9},{25,1},{2,26},{10... | collective-permute-start | bytes 196616 | tf_op jit(solution)/shard_map/ppermute | solution.py:332
  22.3 2.7 %collective-permute-done.3.refs_3_ = bf16[2,128,128]{2,1,0:T(8,128)(2,1)S(1)} collective-permute-done((bf16[2,128,128]{2,1,0:T(8,128)(2,1)S(1)}, bf16[2,128,128]{2,1,0:T(8,128)(2,1)S(1)}, u32[]{:S(2)}, u32[]{:S(2)}) %collective-permute-start.3) | collective-permute-done | bytes 65568 | tf_op jit(solution)/shard_map/ppermute | solution.py:332
  24.9 1.6 %collective-permute-start.11 = (bf16[128,640]{1,0:T(8,128)(2,1)}, bf16[128,640]{1,0:T(8,128)(2,1)S(1)}, u32[]{:S(2)}, u32[]{:S(2)}) collective-permute-start(bf16[128,640]{1,0:T(8,128)(2,1)} %grad_in.1), channel_id=1, source_target_pairs={{0,0},{1,1},{2,10},{3,11},{4,20},{5,21},{6,30},{7,31},{8,2},{9,3},... | collective-permute-start | bytes 491528 | tf_op jit(solution)/shard_map/ppermute | solution.py:341
  28.2 1.9 %collective-permute-start.7 = (f32[4,2,640]{2,1,0:T(2,128)S(1)}, f32[4,2,640]{2,1,0:T(2,128)S(1)}, u32[]{:S(2)}, u32[]{:S(2)}) collective-permute-start(f32[4,2,640]{2,1,0:T(2,128)S(1)} %get-tuple-element.43.refs_0_), channel_id=1, source_target_pairs={{0,2},{1,3},{2,0},{3,1},{4,6},{5,7},{6,4},{7,5},{8,10},{9,11},{10,... | collective-permute-start | bytes 61448 | tf_op jit(solution)/shard_map/ppermute | solution.py:325
  30.1 4.0 %collective-permute-start.8 = (f32[4,2,640]{2,1,0:T(2,128)S(1)}, f32[4,2,640]{2,1,0:T(2,128)S(1)}, u32[]{:S(2)}, u32[]{:S(2)}) collective-permute-start(f32[4,2,640]{2,1,0:T(2,128)S(1)} %get-tuple-element.43.refs_0_), channel_id=1, source_target_pairs={{0,4},{1,5},{2,6},{3,7},{4,0},{5,1},{6,2},{7,3},{8,12},{9,13},{10,... | collective-permute-start | bytes 61448 | tf_op jit(solution)/shard_map/ppermute | solution.py:325
  34.1 5.9 %collective-permute-start.19 = (bf16[128,640]{1,0:T(8,128)(2,1)S(1)}, bf16[128,640]{1,0:T(8,128)(2,1)S(1)}, u32[]{:S(2)}, u32[]{:S(2)}) collective-permute-start(bf16[128,640]{1,0:T(8,128)(2,1)S(1)} %collective-permute-done.11.refs_0_), channel_id=1, source_target_pairs={{0,2},{1,3},{2,0},{3,1},{4,6},{5,7},{6,4},{7,5},{8,10},{9,11},{10,... | collective-permute-start | bytes 491528 | tf_op jit(solution)/shard_map/ppermute | solution.py:325
  40.1 1.5 %collective-permute-start.21 = (bf16[128,640]{1,0:T(8,128)(2,1)S(1)}, bf16[128,640]{1,0:T(8,128)(2,1)S(1)}, u32[]{:S(2)}, u32[]{:S(2)}) collective-permute-start(bf16[128,640]{1,0:T(8,128)(2,1)S(1)} %collective-permute-done.11.refs_0_), channel_id=1, source_target_pairs={{0,6},{1,7},{2,4},{3,5},{4,2},{5,3},{6,0},{7,1},{8,14},{9,15},{10,... | collective-permute-start | bytes 491528 | tf_op jit(solution)/shard_map/ppermute | solution.py:325
  41.5 1.5 %collective-permute-start.9 = (f32[4,2,640]{2,1,0:T(2,128)S(1)}, f32[4,2,640]{2,1,0:T(2,128)S(1)}, u32[]{:S(2)}, u32[]{:S(2)}) collective-permute-start(f32[4,2,640]{2,1,0:T(2,128)S(1)} %get-tuple-element.43.refs_0_), channel_id=1, source_target_pairs={{0,6},{1,7},{2,4},{3,5},{4,2},{5,3},{6,0},{7,1},{8,14},{9,15},{10,... | collective-permute-start | bytes 61448 | tf_op jit(solution)/shard_map/ppermute | solution.py:325
  43.0 3.6 %collective-permute-done.9.refs_3_ = f32[4,2,640]{2,1,0:T(2,128)S(1)} collective-permute-done((f32[4,2,640]{2,1,0:T(2,128)S(1)}, f32[4,2,640]{2,1,0:T(2,128)S(1)}, u32[]{:S(2)}, u32[]{:S(2)}) %collective-permute-start.9) | collective-permute-done | bytes 20512 | tf_op jit(solution)/shard_map/ppermute | solution.py:325
  47.9 1.3 %collective-permute-start.14 = (bf16[160,128]{1,0:T(8,128)(2,1)S(1)}, bf16[160,128]{1,0:T(8,128)(2,1)S(1)}, u32[]{:S(2)}, u32[]{:S(2)}) collective-permute-start(bf16[160,128]{1,0:T(8,128)(2,1)S(1)} %shard_map.132.refs_4_), channel_id=1, source_target_pairs={{0,16},{8,24},{16,0},{24,8},{1,17},{9,25},{17,1},{25,9},{2,18},{10... | collective-permute-start | bytes 122888 | tf_op jit(solution)/shard_map/ppermute | solution.py:332
  50.2 3.0 %collective-permute-done.14.refs_6_ = bf16[160,128]{1,0:T(8,128)(2,1)S(1)} collective-permute-done((bf16[160,128]{1,0:T(8,128)(2,1)S(1)}, bf16[160,128]{1,0:T(8,128)(2,1)S(1)}, u32[]{:S(2)}, u32[]{:S(2)}) %collective-permute-start.14) | collective-permute-done | bytes 40992 | tf_op jit(solution)/shard_map/ppermute | solution.py:332
  53.2 1.8 %collective-permute-done.15.refs_7_ = bf16[160,128]{1,0:T(8,128)(2,1)S(1)} collective-permute-done((bf16[160,128]{1,0:T(8,128)(2,1)S(1)}, bf16[160,128]{1,0:T(8,128)(2,1)S(1)}, u32[]{:S(2)}, u32[]{:S(2)}) %collective-permute-start.15) | collective-permute-done | bytes 40992 | tf_op jit(solution)/shard_map/ppermute | solution.py:332
  55.0 2.4 %shard_map.133 = (bf16[1024,128]{1,0:T(8,128)(2,1)}, bf16[1024,128]{1,0:T(8,128)(2,1)}, f32[208,128]{1,0:T(8,128)S(1)}, f32[208,128]{1,0:T(8,128)S(1)}, f32[208,128]{1,0:T(8,128)S(1)}, /*index=5*/f32[208,128]{1,0:T(8,128)S(1)}) custom-call(f32[2,512]{1,0:T(2,128)S(1)} %get-tuple-element.34.bias, bf16[1024,128]{1,0:T(8,128)(2,1)S(1)} %get-tuple-element.35.keys, ...), custom_call_target="tpu_custom_call" | custom-call | flops 671088640 | bytes 995328 | tf_op jit(solution)/shard_map/pallas_call | solution.py:281
  57.8 2.3 %collective-permute-start.17 = (f32[208,128]{1,0:T(8,128)S(1)}, f32[208,128]{1,0:T(8,128)S(1)}, u32[]{:S(2)}, u32[]{:S(2)}) collective-permute-start(f32[208,128]{1,0:T(8,128)S(1)} %get-tuple-element.49), channel_id=1, source_target_pairs={{0,16},{8,24},{16,0},{24,8},{1,17},{9,25},{17,1},{25,9},{2,18},{10... | collective-permute-start | bytes 319496 | tf_op jit(solution)/shard_map/ppermute | solution.py:332
  60.0 2.1 %collective-permute-start.18 = (f32[208,128]{1,0:T(8,128)S(1)}, f32[208,128]{1,0:T(8,128)S(1)}, u32[]{:S(2)}, u32[]{:S(2)}) collective-permute-start(f32[208,128]{1,0:T(8,128)S(1)} %get-tuple-element.50), channel_id=1, source_target_pairs={{0,24},{8,16},{16,8},{24,0},{1,25},{9,17},{17,9},{25,1},{2,26},{10... | collective-permute-start | bytes 319496 | tf_op jit(solution)/shard_map/ppermute | solution.py:332
  62.1 2.9 %collective-permute-done.16.refs_1_ = f32[208,128]{1,0:T(8,128)S(1)} collective-permute-done((f32[208,128]{1,0:T(8,128)S(1)}, f32[208,128]{1,0:T(8,128)S(1)}, u32[]{:S(2)}, u32[]{:S(2)}) %collective-permute-start.16) | collective-permute-done | bytes 106528 | tf_op jit(solution)/shard_map/ppermute | solution.py:332
  65.1 4.1 %collective-permute-done.17.refs_2_ = f32[208,128]{1,0:T(8,128)S(1)} collective-permute-done((f32[208,128]{1,0:T(8,128)S(1)}, f32[208,128]{1,0:T(8,128)S(1)}, u32[]{:S(2)}, u32[]{:S(2)}) %collective-permute-start.17) | collective-permute-done | bytes 106528 | tf_op jit(solution)/shard_map/ppermute | solution.py:332
  70.1 1.4 %shard_map.136 = f32[128,1280]{1,0:T(8,128)} custom-call(bf16[4,128,640]{2,1,0:T(8,128)(2,1)S(1)} %shard_map.135.own, bf16[4,128,640]{2,1,0:T(8,128)(2,1)S(1)} %collective-permute-done.22.other, bf16[2,128,128]{2,1,0:T(8,128)(2,1)S(1)} %get-tuple-element.37.refs_0_.packed, bf16[2,128,128]{2,1,0:T(8,128)(2,1)S(1)} %collective-permute-done.1.refs_1_, ...), custom_call_target="tpu_custom_call" | custom-call | flops 167772160 | bytes 1572864 | tf_op jit(solution)/shard_map/pallas_call | solution.py:281
  (47 shorter events, 12.3 us)
Async XLA Ops:
  0.6 1.3 %copy-start = (bf16[128,5120]{1,0:T(8,128)(2,1)S(1)}, bf16[128,5120]{1,0:T(8,128)(2,1)}, u32[]{:S(2)}) copy-start(bf16[128,5120]{1,0:T(8,128)(2,1)} %weight_in.1) | copy-start | bytes 3932164
  9.2 18.2 %collective-permute-start = (bf16[128,2688]{1,0:T(8,128)(2,1)S(1)}, bf16[128,2688]{1,0:T(8,128)(2,1)S(1)}, u32[]{:S(2)}, u32[]{:S(2)}) collective-permute-start(bf16[128,2688]{1,0:T(8,128)(2,1)S(1)} %get-tuple-element.39), channel_id=1, source_target_pairs={{0,1},{1,0},{2,3},{3,2},{4,5},{5,4},{6,7},{7,6},{8,9},{9,8},{10,11... | collective-permute-start | bytes 2064392 | tf_op jit(solution)/shard_map/ppermute | solution.py:329
  9.7 8.3 %collective-permute-start.1 = (bf16[2,128,128]{2,1,0:T(8,128)(2,1)S(1)}, bf16[2,128,128]{2,1,0:T(8,128)(2,1)S(1)}, u32[]{:S(2)}, u32[]{:S(2)}) collective-permute-start(bf16[2,128,128]{2,1,0:T(8,128)(2,1)S(1)} %get-tuple-element.37.refs_0_.packed), channel_id=1, source_target_pairs={{0,8},{8,0},{16,24},{24,16},{1,9},{9,1},{17,25},{25,17},{2,10},{10... | collective-permute-start | bytes 196616 | tf_op jit(solution)/shard_map/ppermute | solution.py:332
  12.3 6.6 %collective-permute-start.2 = (bf16[2,128,128]{2,1,0:T(8,128)(2,1)S(1)}, bf16[2,128,128]{2,1,0:T(8,128)(2,1)S(1)}, u32[]{:S(2)}, u32[]{:S(2)}) collective-permute-start(bf16[2,128,128]{2,1,0:T(8,128)(2,1)S(1)} %get-tuple-element.37.refs_0_.packed), channel_id=1, source_target_pairs={{0,16},{8,24},{16,0},{24,8},{1,17},{9,25},{17,1},{25,9},{2,18},{10... | collective-permute-start | bytes 196616 | tf_op jit(solution)/shard_map/ppermute | solution.py:332
  14.9 12.4 %collective-permute-start.4 = (bf16[128,640]{1,0:T(8,128)(2,1)}, bf16[128,640]{1,0:T(8,128)(2,1)S(1)}, u32[]{:S(2)}, u32[]{:S(2)}) collective-permute-start(bf16[128,640]{1,0:T(8,128)(2,1)} %grad_in.1), channel_id=1, source_target_pairs={{0,2},{1,3},{2,0},{3,1},{4,6},{5,7},{6,4},{7,5},{8,10},{9,11},{10,... | collective-permute-start | bytes 491528 | tf_op jit(solution)/shard_map/ppermute | solution.py:325
  16.4 10.9 %collective-permute-start.5 = (bf16[128,640]{1,0:T(8,128)(2,1)}, bf16[128,640]{1,0:T(8,128)(2,1)S(1)}, u32[]{:S(2)}, u32[]{:S(2)}) collective-permute-start(bf16[128,640]{1,0:T(8,128)(2,1)} %grad_in.1), channel_id=1, source_target_pairs={{0,4},{1,5},{2,6},{3,7},{4,0},{5,1},{6,2},{7,3},{8,12},{9,13},{10,... | collective-permute-start | bytes 491528 | tf_op jit(solution)/shard_map/ppermute | solution.py:325
  17.9 9.4 %collective-permute-start.6 = (bf16[128,640]{1,0:T(8,128)(2,1)}, bf16[128,640]{1,0:T(8,128)(2,1)S(1)}, u32[]{:S(2)}, u32[]{:S(2)}) collective-permute-start(bf16[128,640]{1,0:T(8,128)(2,1)} %grad_in.1), channel_id=1, source_target_pairs={{0,6},{1,7},{2,4},{3,5},{4,2},{5,3},{6,0},{7,1},{8,14},{9,15},{10,... | collective-permute-start | bytes 491528 | tf_op jit(solution)/shard_map/ppermute | solution.py:325
  18.9 6.1 %collective-permute-start.3 = (bf16[2,128,128]{2,1,0:T(8,128)(2,1)S(1)}, bf16[2,128,128]{2,1,0:T(8,128)(2,1)S(1)}, u32[]{:S(2)}, u32[]{:S(2)}) collective-permute-start(bf16[2,128,128]{2,1,0:T(8,128)(2,1)S(1)} %get-tuple-element.37.refs_0_.packed), channel_id=1, source_target_pairs={{0,24},{8,16},{16,8},{24,0},{1,25},{9,17},{17,9},{25,1},{2,26},{10... | collective-permute-start | bytes 196616 | tf_op jit(solution)/shard_map/ppermute | solution.py:332
  24.9 9.2 %collective-permute-start.11 = (bf16[128,640]{1,0:T(8,128)(2,1)}, bf16[128,640]{1,0:T(8,128)(2,1)S(1)}, u32[]{:S(2)}, u32[]{:S(2)}) collective-permute-start(bf16[128,640]{1,0:T(8,128)(2,1)} %grad_in.1), channel_id=1, source_target_pairs={{0,0},{1,1},{2,10},{3,11},{4,20},{5,21},{6,30},{7,31},{8,2},{9,3},... | collective-permute-start | bytes 491528 | tf_op jit(solution)/shard_map/ppermute | solution.py:341
  28.1 6.0 %collective-permute-start.12 = (f32[128,128]{1,0:T(8,128)S(1)}, f32[128,128]{1,0:T(8,128)S(1)}, u32[]{:S(2)}, u32[]{:S(2)}) collective-permute-start(f32[128,128]{1,0:T(8,128)S(1)} %get-tuple-element.45), channel_id=1, source_target_pairs={{0,1},{1,0},{2,3},{3,2},{4,5},{5,4},{6,7},{7,6},{8,9},{9,8},{10,11... | collective-permute-start | bytes 196616 | tf_op jit(solution)/shard_map/ppermute | solution.py:329
  28.2 13.3 %collective-permute-start.7 = (f32[4,2,640]{2,1,0:T(2,128)S(1)}, f32[4,2,640]{2,1,0:T(2,128)S(1)}, u32[]{:S(2)}, u32[]{:S(2)}) collective-permute-start(f32[4,2,640]{2,1,0:T(2,128)S(1)} %get-tuple-element.43.refs_0_), channel_id=1, source_target_pairs={{0,2},{1,3},{2,0},{3,1},{4,6},{5,7},{6,4},{7,5},{8,10},{9,11},{10,... | collective-permute-start | bytes 61448 | tf_op jit(solution)/shard_map/ppermute | solution.py:325
  30.1 12.9 %collective-permute-start.8 = (f32[4,2,640]{2,1,0:T(2,128)S(1)}, f32[4,2,640]{2,1,0:T(2,128)S(1)}, u32[]{:S(2)}, u32[]{:S(2)}) collective-permute-start(f32[4,2,640]{2,1,0:T(2,128)S(1)} %get-tuple-element.43.refs_0_), channel_id=1, source_target_pairs={{0,4},{1,5},{2,6},{3,7},{4,0},{5,1},{6,2},{7,3},{8,12},{9,13},{10,... | collective-permute-start | bytes 61448 | tf_op jit(solution)/shard_map/ppermute | solution.py:325
  34.1 23.4 %collective-permute-start.19 = (bf16[128,640]{1,0:T(8,128)(2,1)S(1)}, bf16[128,640]{1,0:T(8,128)(2,1)S(1)}, u32[]{:S(2)}, u32[]{:S(2)}) collective-permute-start(bf16[128,640]{1,0:T(8,128)(2,1)S(1)} %collective-permute-done.11.refs_0_), channel_id=1, source_target_pairs={{0,2},{1,3},{2,0},{3,1},{4,6},{5,7},{6,4},{7,5},{8,10},{9,11},{10,... | collective-permute-start | bytes 491528 | tf_op jit(solution)/shard_map/ppermute | solution.py:325
  40.1 17.4 %collective-permute-start.20 = (bf16[128,640]{1,0:T(8,128)(2,1)S(1)}, bf16[128,640]{1,0:T(8,128)(2,1)S(1)}, u32[]{:S(2)}, u32[]{:S(2)}) collective-permute-start(bf16[128,640]{1,0:T(8,128)(2,1)S(1)} %collective-permute-done.11.refs_0_), channel_id=1, source_target_pairs={{0,4},{1,5},{2,6},{3,7},{4,0},{5,1},{6,2},{7,3},{8,12},{9,13},{10,... | collective-permute-start | bytes 491528 | tf_op jit(solution)/shard_map/ppermute | solution.py:325
  40.1 17.4 %collective-permute-start.21 = (bf16[128,640]{1,0:T(8,128)(2,1)S(1)}, bf16[128,640]{1,0:T(8,128)(2,1)S(1)}, u32[]{:S(2)}, u32[]{:S(2)}) collective-permute-start(bf16[128,640]{1,0:T(8,128)(2,1)S(1)} %collective-permute-done.11.refs_0_), channel_id=1, source_target_pairs={{0,6},{1,7},{2,4},{3,5},{4,2},{5,3},{6,0},{7,1},{8,14},{9,15},{10,... | collective-permute-start | bytes 491528 | tf_op jit(solution)/shard_map/ppermute | solution.py:325
  41.5 5.1 %collective-permute-start.9 = (f32[4,2,640]{2,1,0:T(2,128)S(1)}, f32[4,2,640]{2,1,0:T(2,128)S(1)}, u32[]{:S(2)}, u32[]{:S(2)}) collective-permute-start(f32[4,2,640]{2,1,0:T(2,128)S(1)} %get-tuple-element.43.refs_0_), channel_id=1, source_target_pairs={{0,6},{1,7},{2,4},{3,5},{4,2},{5,3},{6,0},{7,1},{8,14},{9,15},{10,... | collective-permute-start | bytes 61448 | tf_op jit(solution)/shard_map/ppermute | solution.py:325
  43.0 6.3 %collective-permute-start.13 = (bf16[160,128]{1,0:T(8,128)(2,1)S(1)}, bf16[160,128]{1,0:T(8,128)(2,1)S(1)}, u32[]{:S(2)}, u32[]{:S(2)}) collective-permute-start(bf16[160,128]{1,0:T(8,128)(2,1)S(1)} %shard_map.132.refs_4_), channel_id=1, source_target_pairs={{0,8},{8,0},{16,24},{24,16},{1,9},{9,1},{17,25},{25,17},{2,10},{10... | collective-permute-start | bytes 122888 | tf_op jit(solution)/shard_map/ppermute | solution.py:332
  46.6 1.3 %collective-permute-start.10 = (f32[40,128]{1,0:T(8,128)S(1)}, f32[40,128]{1,0:T(8,128)S(1)}, u32[]{:S(2)}, u32[]{:S(2)}) collective-permute-start(f32[40,128]{1,0:T(8,128)S(1)} %shard_map.131.own_terms), channel_id=1, source_target_pairs={{0,1},{1,0},{2,3},{3,2},{4,5},{5,4},{6,7},{7,6},{8,9},{9,8},{10,11... | collective-permute-start | bytes 61448 | tf_op jit(solution)/shard_map/ppermute | solution.py:329
  47.9 5.3 %collective-permute-start.14 = (bf16[160,128]{1,0:T(8,128)(2,1)S(1)}, bf16[160,128]{1,0:T(8,128)(2,1)S(1)}, u32[]{:S(2)}, u32[]{:S(2)}) collective-permute-start(bf16[160,128]{1,0:T(8,128)(2,1)S(1)} %shard_map.132.refs_4_), channel_id=1, source_target_pairs={{0,16},{8,24},{16,0},{24,8},{1,17},{9,25},{17,1},{25,9},{2,18},{10... | collective-permute-start | bytes 122888 | tf_op jit(solution)/shard_map/ppermute | solution.py:332
  49.2 5.8 %collective-permute-start.15 = (bf16[160,128]{1,0:T(8,128)(2,1)S(1)}, bf16[160,128]{1,0:T(8,128)(2,1)S(1)}, u32[]{:S(2)}, u32[]{:S(2)}) collective-permute-start(bf16[160,128]{1,0:T(8,128)(2,1)S(1)} %shard_map.132.refs_4_), channel_id=1, source_target_pairs={{0,24},{8,16},{16,8},{24,0},{1,25},{9,17},{17,9},{25,1},{2,26},{10... | collective-permute-start | bytes 122888 | tf_op jit(solution)/shard_map/ppermute | solution.py:332
  57.6 12.5 %collective-permute-start.22 = (bf16[4,128,640]{2,1,0:T(8,128)(2,1)S(1)}, bf16[4,128,640]{2,1,0:T(8,128)(2,1)S(1)}, u32[]{:S(2)}, u32[]{:S(2)}) collective-permute-start(bf16[4,128,640]{2,1,0:T(8,128)(2,1)S(1)} %shard_map.135.own), channel_id=1, source_target_pairs={{0,1},{1,0},{2,3},{3,2},{4,5},{5,4},{6,7},{7,6},{8,9},{9,8},{10,11... | collective-permute-start | bytes 1966088 | tf_op jit(solution)/shard_map/ppermute | solution.py:329
  57.7 7.4 %collective-permute-start.16 = (f32[208,128]{1,0:T(8,128)S(1)}, f32[208,128]{1,0:T(8,128)S(1)}, u32[]{:S(2)}, u32[]{:S(2)}) collective-permute-start(f32[208,128]{1,0:T(8,128)S(1)} %get-tuple-element.48), channel_id=1, source_target_pairs={{0,8},{8,0},{16,24},{24,16},{1,9},{9,1},{17,25},{25,17},{2,10},{10... | collective-permute-start | bytes 319496 | tf_op jit(solution)/shard_map/ppermute | solution.py:332
  57.8 11.4 %collective-permute-start.17 = (f32[208,128]{1,0:T(8,128)S(1)}, f32[208,128]{1,0:T(8,128)S(1)}, u32[]{:S(2)}, u32[]{:S(2)}) collective-permute-start(f32[208,128]{1,0:T(8,128)S(1)} %get-tuple-element.49), channel_id=1, source_target_pairs={{0,16},{8,24},{16,0},{24,8},{1,17},{9,25},{17,1},{25,9},{2,18},{10... | collective-permute-start | bytes 319496 | tf_op jit(solution)/shard_map/ppermute | solution.py:332
  60.0 9.1 %collective-permute-start.18 = (f32[208,128]{1,0:T(8,128)S(1)}, f32[208,128]{1,0:T(8,128)S(1)}, u32[]{:S(2)}, u32[]{:S(2)}) collective-permute-start(f32[208,128]{1,0:T(8,128)S(1)} %get-tuple-element.50), channel_id=1, source_target_pairs={{0,24},{8,16},{16,8},{24,0},{1,25},{9,17},{17,9},{25,1},{2,26},{10... | collective-permute-start | bytes 319496 | tf_op jit(solution)/shard_map/ppermute | solution.py:332
  (7 other events, 5.7 us)

commit v4 on v3

--- a/solution.py
+++ b/solution.py
@@ -15,6 +15,7 @@
 NEG_BIG = -1e30
 SCALE = 1.0 / math.sqrt(HD)
 VMEM_LIMIT = 32 * 1024 * 1024
+PREP_VMEM = 52 * 1024 * 1024
 SPLIT = 3
 
 
@@ -38,33 +39,25 @@
     return lambda frame: sum((frame >= bound).astype(jnp.int32) for bound in bounds)
 
 
-def prep_kernel(
-    n_t, chips, frames, levels_in, clips_in, queries_in, saved_in, keys_in, values_in, grad_in,
-    weight_in, gate_in, packed, kept, sent, keys, values, grad, bias, gate_a, gate_b, hot,
-    gate, levels, clips, sems,
-):
-    t, chip, core = place()
-    rows = grad.shape[0]
-    width = grad.shape[1]
-
-    def columns(k, c):
-        return pl.ds(pl.multiple_of((2 * (chip ^ k) + c) * width, LANES), width)
-
-    moves = [(levels_in, levels), (clips_in, clips), (queries_in, packed.at[0]), (saved_in, packed.at[1])]
+def cut_kernel(chips, weight_in, kept, sent, sems):
+    _, chip, core = place()
+    width = kept.shape[2]
+    copies = []
     for k in range(chips):
-        moves.append((weight_in.at[:, columns(k, 1 - core)], sent.at[:, k * width : (k + 1) * width]))
-    moves.append((saved_in, sent.at[:, chips * width : chips * width + HD]))
-    moves.append((gate_in, gate))
-    moves.append((keys_in, keys))
-    for k in range(chips):
-        moves.append((weight_in.at[:, columns(k, core)], kept.at[k]))
-    moves.append((grad_in, grad))
-    moves.append((values_in, values))
-    copies = [pltpu.make_async_copy(a, b, sems.at[i]) for i, (a, b) in enumerate(moves)]
+        for c, out in ((1 - core, sent), (core, kept)):
+            columns = pl.ds(pl.multiple_of((2 * (chip ^ k) + c) * width, LANES), width)
+            copies.append(
+                pltpu.make_async_copy(weight_in.at[:, columns], out.at[k], sems.at[len(copies)])
+            )
     for copy in copies:
         copy.start()
-    copies[0].wait()
-    copies[1].wait()
+    for copy in copies:
+        copy.wait()
+
+
+def masks_kernel(n_t, chips, frames, rows, levels, clips, gate, bias, gate_a, gate_b, hot):
+    t, chip, core = place()
+    width = gate_a.shape[2]
     clip_of = clip_numbers(clips)
     lane = lax.broadcasted_iota(jnp.int32, (1, rows), 1)
     for kf in range(frames):
@@ -81,12 +74,11 @@
     spot = lax.broadcasted_iota(jnp.int32, hot.shape[1:], 0)
     for f in range(n_t * frames):
         hot[f] = (spot == levels[f]).astype(jnp.float32)
-    for copy in copies[2:]:
-        copy.wait()
     for r in range(frames):
         level = levels[t * frames + r]
         for k in range(chips):
-            gate_a[k, r : r + 1, :] = gate[pl.ds(level, 1), columns(k, core)]
+            columns = pl.ds(pl.multiple_of((2 * (chip ^ k) + core) * width, LANES), width)
+            gate_a[k, r : r + 1, :] = gate[pl.ds(level, 1), columns]
         for k in range(n_t):
             level = levels[(t ^ chip ^ k) * frames + r]
             mine = pl.ds(pl.multiple_of((2 * t + core) * width, LANES), width)
@@ -109,14 +101,15 @@
             out[n_t + p + i : n_t + p + i + 1, :] = total[:, i * rows : (i + 1) * rows]
 
 
-def head_kernel(chips, frames, packed, kept, received, gate_a, *refs):
-    pieces, (mine, other, terms) = refs[:chips], refs[chips:]
+def head_kernel(chips, frames, packed, other_saved, kept, received, gate_a, *refs):
+    pieces, (mine, other) = refs[:chips], refs[chips:]
     _, chip, _ = place()
-    width = pieces[0].shape[1]
-    saved = jnp.concatenate([packed[1], received[:, chips * width : chips * width + HD]], axis=1)
+    rows = mine.shape[0]
+    tiles = pieces[0].shape[1] // LANES
+    saved = jnp.concatenate([packed[1], other_saved[...]], axis=1)
     head = None
     for k in range(chips):
-        weight = jnp.concatenate([kept[k], received[:, k * width : (k + 1) * width]], axis=0)
+        weight = jnp.concatenate([kept[k], received[k]], axis=0)
         wide = pieces[k][...].astype(jnp.float32)
         gated = jnp.concatenate(
             [
@@ -130,14 +123,21 @@
         product = wide * dot(saved, weight, 1, 0)
         for r in range(frames):
             term = jnp.sum(product[r * QF : (r + 1) * QF], axis=0, keepdims=True)
-            terms[chip ^ k, r : r + 1, :] = term
+            for j in range(tiles):
+                row = rows + ((chip ^ k) * frames + r) * tiles + j
+                other[pl.ds(row, 1), :] = term[:, j * LANES : (j + 1) * LANES]
     mine[...] = head[:, :HD]
-    other[...] = head[:, HD:]
-
-
-def join_kernel(mine, received, stats, out):
+    other[:rows, :] = head[:, HD:]
+
+
+def join_kernel(mine, sent, received, stats, out, terms):
+    core = place()[2]
     rows = mine.shape[0]
-    out[:rows, :] = (mine[...] + received[...]).astype(jnp.bfloat16)
+    out[:rows, :] = (mine[...] + received[:rows, :]).astype(jnp.bfloat16)
+    own, other = sent[rows:, :], received[rows:, :]
+    count = own.shape[0]
+    terms[:count, :] = jnp.where(core == 0, own, other)
+    terms[count:, :] = jnp.where(core == 0, other, own)
     rest = stats[...]
     parts = []
     for _ in range(SPLIT):
@@ -150,41 +150,27 @@
     out[rows:, :] = jnp.concatenate(parts, axis=0).astype(jnp.bfloat16)
 
 
-def terms_kernel(chips, *refs):
-    pieces, out, held = refs[:chips], refs[chips], refs[chips + 1]
-    _, chip, _ = place()
-    for k in range(chips):
-        held[chip ^ k] = pieces[k][...]
-    total = held[0]
-    for k in range(1, chips):
-        total = total + held[k]
-    row = 0
-    for a in range(total.shape[0]):
-        for r in range(total.shape[1]):
-            for j in range(0, total.shape[2], LANES):
-                out[row : row + 1, :] = total[a, r : r + 1, j : j + LANES]
-                row += 1
-
-
-def grads_kernel(n_t, bias, keys, values, own_terms, other_terms, *refs):
+def grads_kernel(n_t, chips, bias, keys, values, *refs):
+    terms, refs = refs[:chips], refs[chips:]
     packed, heads = refs[:n_t], refs[n_t : 2 * n_t]
     key_out, value_out = refs[2 * n_t : 2 * n_t + 2]
     outs = refs[2 * n_t + 2 : 3 * n_t + 2]
-    key_acc, value_acc = refs[3 * n_t + 2 :]
-    core = place()[2]
+    key_acc, value_acc, held = refs[3 * n_t + 2 :]
+    chip = place()[1]
     rows = packed[0].shape[1]
-    count = own_terms.shape[0]
     ones = jnp.ones((8, HD), jnp.float32)
     keys_t = jnp.transpose(keys[...])
     stats = []
     for k in range(n_t):
         parts = heads[k][rows:, :].astype(jnp.float32)
         stats.append(sum(parts[i * 2 * n_t : (i + 1) * 2 * n_t] for i in range(SPLIT)))
-    own, other = own_terms[...], other_terms[...]
-    first, second = jnp.where(core == 0, own, other), jnp.where(core == 0, other, own)
+    for k in range(chips):
+        held[chip ^ k] = terms[k][...]
+    total = held[0]
+    for k in range(1, chips):
+        total = total + held[k]
     for k in range(n_t):
-        outs[k][rows : rows + count, :] = first
-        outs[k][rows + count :, :] = second
+        outs[k][rows:, :] = total.astype(jnp.bfloat16)
     for p in range(0, n_t, 2):
         q = jnp.concatenate([packed[p][0], packed[p + 1][0]], axis=0)
         o = jnp.concatenate([packed[p][1], packed[p + 1][1]], axis=0)
@@ -222,20 +208,20 @@
                 key_out[span, :] = (key_add * SCALE).astype(jnp.bfloat16)
             part = dot(keys_t[:, span], score_grad, 1, 0)
             query_part = part if query_part is None else query_part + part
-        outs[p][:rows, :] = query_part[:, :rows]
-        outs[p + 1][:rows, :] = query_part[:, rows:]
+        outs[p][:rows, :] = query_part[:, :rows].astype(jnp.bfloat16)
+        outs[p + 1][:rows, :] = query_part[:, rows:].astype(jnp.bfloat16)
 
 
 def finish_kernel(n_t, chips, frames, hot, *refs):
     parts, (query_out, gate_out, held) = refs[:n_t], refs[n_t:]
     t = lax.axis_index("tm")
     rows = query_out.shape[0]
-    total = parts[0][:rows, :]
+    total = parts[0][:rows, :].astype(jnp.float32)
     for k in range(1, n_t):
-        total = total + parts[k][:rows, :]
+        total = total + parts[k][:rows, :].astype(jnp.float32)
     query_out[...] = jnp.transpose(total * SCALE).astype(jnp.bfloat16)
     for k in range(n_t):
-        held[t ^ k] = parts[k][rows:, :]
+        held[t ^ k] = parts[k][rows:, :].astype(jnp.float32)
     tiles = gate_out.shape[1] // (2 * chips * LANES)
     for core in range(2):
         for a in range(chips):
@@ -274,17 +260,18 @@
                 out[:, h * width : (h + 1) * width] = result
 
 
-def call(kernel, args, out_shape, scratch=(), flops=0, in_place=False):
+def call(kernel, args, out_shape, scratch=(), flops=0, in_place=False, in_smem=0):
     vmem = pl.BlockSpec(memory_space=pltpu.VMEM)
     single = not isinstance(out_shape, (list, tuple))
     nbytes = sum(a.size * a.dtype.itemsize for a in args)
     return pl.pallas_call(
         kernel,
         out_shape=out_shape,
-        in_specs=[pl.BlockSpec(memory_space=pltpu.HBM) if in_place else vmem] * len(args),
+        in_specs=[pl.BlockSpec(memory_space=pltpu.SMEM)] * in_smem
+        + [pl.BlockSpec(memory_space=pltpu.HBM) if in_place else vmem] * (len(args) - in_smem),
         out_specs=vmem if single else [vmem] * len(out_shape),
         scratch_shapes=list(scratch),
-        compiler_params=pltpu.CompilerParams(vmem_limit_bytes=VMEM_LIMIT),
+        compiler_params=pltpu.CompilerParams(vmem_limit_bytes=PREP_VMEM if in_place else VMEM_LIMIT),
         cost_estimate=pl.CostEstimate(flops=flops, bytes_accessed=nbytes, transcendentals=0),
     )(*args)
 
@@ -332,74 +319,74 @@
         return lax.ppermute(x, "tm", [(t, t ^ k) for t in range(n_t)])
 
     pieces = over_chips(out_grad)
+    kept, sent = call(
+        functools.partial(cut_kernel, chips),
+        [proj_weight],
+        [shape(bf16, chips, HD, width)] * 2,
+        [pltpu.SemaphoreType.DMA((2 * chips,))],
+        in_place=True,
+    )
+    received, other_saved = over_cores(sent), over_cores(saved_out)
+    packed, _ = lax.optimization_barrier((jnp.stack([queries, saved_out]), (received, other_saved)))
+    packed_all = [packed]
+    for k in range(1, n_t):
+        high = 1 << (k.bit_length() - 1)
+        packed_all.append(over_time(packed_all[k - high], high))
     moves = [
         (t * n_s + 2 * c + e, c * n_s + 2 * (c ^ t) + e)
         for t in range(n_t)
         for c in range(chips)
         for e in range(2)
     ]
-    moved = lax.ppermute(out_grad, ("tm", "space"), moves)
-    packed, kept, sent, keys, values, own_grad, bias, gate_a, gate_b, hot = call(
-        functools.partial(prep_kernel, n_t, chips, frames),
-        [noise_levels, clip_lengths, queries, saved_out, keys, values, out_grad, proj_weight, gate_table],
+    to_move, _ = lax.optimization_barrier((out_grad, packed_all[n_t // 2]))
+    moved = lax.ppermute(to_move, ("tm", "space"), moves)
+    gate_table, _ = lax.optimization_barrier((gate_table, received))
+    bias, gate_a, gate_b, hot = call(
+        functools.partial(masks_kernel, n_t, chips, frames, rows),
+        [noise_levels, clip_lengths, gate_table],
         [
-            shape(bf16, 2, rows, HD),
-            shape(bf16, chips, HD, width),
-            shape(bf16, HD, chips * width + HD),
-            shape(bf16, k_rows, HD),
-            shape(bf16, k_rows, HD),
-            shape(bf16, rows, width),
             shape(f32, frames, n_t * rows),
             shape(f32, chips, frames, width),
             shape(f32, n_t, frames, width),
             shape(f32, n_t * frames, levels, LANES),
         ],
-        [
-            pltpu.VMEM((levels, n_s * width), f32),
-            pltpu.SMEM(noise_levels.shape, jnp.int32),
-            pltpu.SMEM(clip_lengths.shape, jnp.int32),
-            pltpu.SemaphoreType.DMA((2 * chips + 9,)),
-        ],
-        in_place=True,
-    )
-    received = over_cores(sent)
-    packed_all = [packed] + [over_time(packed, k) for k in range(1, n_t)]
+        in_smem=2,
+    )
+    kept, _ = lax.optimization_barrier((kept, packed_all))
+    count = chips * frames * width // LANES
+    mine, other = call(
+        functools.partial(head_kernel, chips, frames),
+        [packed, other_saved, kept, received, gate_a] + pieces,
+        [shape(f32, rows, HD), shape(f32, rows + count, HD)],
+        flops=4 * rows * chips * width * 2 * HD,
+    )
+    later_bias, _ = lax.optimization_barrier((bias, mine))
     stats = call(
         functools.partial(stats_kernel, n_t),
-        [bias, keys] + packed_all,
+        [later_bias, keys] + packed_all,
         shape(f32, 2 * n_t, LANES),
         flops=2 * n_t * rows * k_rows * HD,
     )
-    gate_a, _ = lax.optimization_barrier((gate_a, stats))
-    mine, other, terms = call(
-        functools.partial(head_kernel, chips, frames),
-        [packed, kept, received, gate_a, own_grad] + pieces[1:],
-        [shape(f32, rows, HD), shape(f32, rows, HD), shape(f32, chips, frames, width)],
-        flops=4 * rows * chips * width * 2 * HD,
-    )
     extra = -(-SPLIT * 2 * n_t // 16) * 16
-    joined = call(join_kernel, [mine, over_cores(other), stats], shape(bf16, rows + extra, HD))
-    moved, joined = lax.optimization_barrier((moved, joined))
+    joined, terms = call(
+        join_kernel,
+        [mine, other, over_cores(other), stats],
+        [shape(bf16, rows + extra, HD), shape(f32, 2 * count, LANES)],
+    )
+    heads_all = [joined] + [over_time(joined, k) for k in range(1, n_t)]
+    terms_all = over_chips(terms)
+    moved, _ = lax.optimization_barrier((moved, terms_all))
     row_pieces = over_chips(moved)
-    heads_all = [joined] + [over_time(joined, k) for k in range(1, n_t)]
-
-    count = chips * frames * width // LANES
-    own_terms = call(
-        functools.partial(terms_kernel, chips),
-        over_chips(terms),
-        shape(f32, count, LANES),
-        [pltpu.VMEM((chips, chips, frames, width), f32)],
-    )
     outs = call(
-        functools.partial(grads_kernel, n_t),
-        [bias, keys, values, own_terms, over_cores(own_terms)] + packed_all + heads_all,
-        [shape(bf16, k_rows, HD)] * 2 + [shape(f32, rows + 2 * count, LANES)] * n_t,
-        [pltpu.VMEM((k_rows, HD), f32)] * 2,
+        functools.partial(grads_kernel, n_t, chips),
+        [bias, keys, values] + terms_all + packed_all + heads_all,
+        [shape(bf16, k_rows, HD)] * 2 + [shape(bf16, rows + 2 * count, LANES)] * n_t,
+        [pltpu.VMEM((k_rows, HD), f32)] * 2 + [pltpu.VMEM((chips, 2 * count, LANES), f32)],
         flops=10 * n_t * rows * k_rows * HD,
     )
     key_grad, value_grad, parts = outs[0], outs[1], outs[2:]
-    row_pieces, _ = lax.optimization_barrier((row_pieces, parts[0]))
     parts = [parts[0]] + [over_time(parts[k], k) for k in range(1, n_t)]
+    row_pieces, _ = lax.optimization_barrier((row_pieces, parts))
 
     gated = call(
         functools.partial(gated_kernel, n_t, frames),

time: 72.1 us -> 53.9 us (0.75)
  waiting for transfers between devices: 19.8 us -> 11 us
  local copies, waits for them, and re-layouts: 7 us -> 0.04 us
  starting transfers between devices: 35.9 us -> 33.1 us
    unnamed x16, local copies, waits for them, and re-layouts: 7 us -> 0.04 us
    ppermute x9, waiting for transfers between devices: 15 us -> 8.12 us  [over_time(): return lax.ppermute(x, 'tm', [(t, t ^ k) for t in range(n_t)])]
    ppermute x9, waiting for transfers between devices: 3.63 us -> 0.02 us  [over_chips(): lax.ppermute(x, 'space', [(s, s ^ 2 * k) for s in range(n_s)])]
    ppermute x9, starting transfers between devices: 18.3 us -> 15 us  [over_chips(): lax.ppermute(x, 'space', [(s, s ^ 2 * k) for s in range(n_s)])]
    ppermute x4, waiting for transfers between devices: 1.18 us -> 2.84 us  [over_cores(): return lax.ppermute(x, 'space', [(s, s ^ 1) for s in range(n_s)])]
    ppermute x9, starting transfers between devices: 15.4 us -> 16.9 us  [over_time(): return lax.ppermute(x, 'tm', [(t, t ^ k) for t in range(n_t)])]
    ppermute x1, starting transfers between devices: 1.56 us -> 0.66 us  [body(): moved = lax.ppermute(to_move, ('tm', 'space'), moves)]
  transfers between devices with their start and end apart: 23 -> 23, of which waited for: 8 -> 7; matrix products, arithmetic and copies ran while one was open for 0% -> 0% of each run, Pallas kernels for 7% -> 10%
where the time goes in v4:
time: 53.9 us; the launch traced here: 53.7 us
  starting transfers between devices  33.1 us (61%)
  waiting for transfers between devices  11 us (20%)
  Pallas kernels  8.71 us (16%)
  between operations  0.82 us (2%)
    ppermute x9, starting transfers between devices, over_time(): return lax.ppermute(x, 'tm', [(t, t ^ k) for t in range(n_t)])  16.9 us
    ppermute x9, starting transfers between devices, over_chips(): lax.ppermute(x, 'space', [(s, s ^ 2 * k) for s in range(n_s)])  15 us
    pallas_call x9, Pallas kernels, call(): pl.pallas_call(kernel, out_shape=out_shape, in_specs=[pl.BlockSpec(memory...  8.71 us
    ppermute x9, waiting for transfers between devices, over_time(): return lax.ppermute(x, 'tm', [(t, t ^ k) for t in range(n_t)])  8.12 us
    ppermute x4, waiting for transfers between devices, over_cores(): return lax.ppermute(x, 'space', [(s, s ^ 1) for s in range(n_s)])  2.84 us
  transfers between devices with their start and end apart: 23, of which 7 were waited for; matrix products, arithmetic and copies ran while one was open for 0% of the time, Pallas kernels for 10%

profile of v4, /device:TPU:0, one launch (start us, length us, event | category | flops | bytes accessed | tf_op | source)
XLA Modules:
  0.0 53.7 jit_solution(11690250015288802869)
XLA Ops:
  0.7 1.5 %shard_map.128 = (bf16[4,128,640]{2,1,0:T(8,128)(2,1)S(1)}, bf16[4,128,640]{2,1,0:T(8,128)(2,1)S(1)}) custom-call(bf16[128,5120]{1,0:T(8,128)(2,1)} %weight_in.1), custom_call_target="tpu_custom_call" | custom-call | bytes 1310720 | tf_op jit(solution)/shard_map/pallas_call | solution.py:267
  2.8 2.6 %collective-permute-start.5 = (bf16[128,640]{1,0:T(8,128)(2,1)S(1)}, bf16[128,640]{1,0:T(8,128)(2,1)S(1)}, u32[]{:S(2)}, u32[]{:S(2)}) collective-permute-start(bf16[128,640]{1,0:T(8,128)(2,1)S(1)} %copy-done.2), channel_id=1, source_target_pairs={{0,2},{1,3},{2,0},{3,1},{4,6},{5,7},{6,4},{7,5},{8,10},{9,11},{10,... | collective-permute-start | bytes 491528 | tf_op jit(solution)/shard_map/ppermute | solution.py:312
  5.4 1.5 %collective-permute-start.6 = (bf16[128,640]{1,0:T(8,128)(2,1)S(1)}, bf16[128,640]{1,0:T(8,128)(2,1)S(1)}, u32[]{:S(2)}, u32[]{:S(2)}) collective-permute-start(bf16[128,640]{1,0:T(8,128)(2,1)S(1)} %copy-done.2), channel_id=1, source_target_pairs={{0,4},{1,5},{2,6},{3,7},{4,0},{5,1},{6,2},{7,3},{8,12},{9,13},{10,... | collective-permute-start | bytes 491528 | tf_op jit(solution)/shard_map/ppermute | solution.py:312
  6.9 1.2 %collective-permute-done.1.other_saved = bf16[128,128]{1,0:T(8,128)(2,1)S(1)} collective-permute-done((bf16[128,128]{1,0:T(8,128)(2,1)S(1)}, bf16[128,128]{1,0:T(8,128)(2,1)S(1)}, u32[]{:S(2)}, u32[]{:S(2)}) %collective-permute-start.1) | collective-permute-done | bytes 32800 | tf_op jit(solution)/shard_map/ppermute | solution.py:316
  8.1 2.0 %collective-permute-start.2 = (bf16[2,128,128]{2,1,0:T(8,128)(2,1)S(1)}, bf16[2,128,128]{2,1,0:T(8,128)(2,1)S(1)}, u32[]{:S(2)}, u32[]{:S(2)}) collective-permute-start(bf16[2,128,128]{2,1,0:T(8,128)(2,1)S(1)} %pad_maximum_fusion.packed.refs_0_.refs_4_), channel_id=1, source_target_pairs={{0,8},{8,0},{16,24},{24,16},{1,9},{9,1},{17,25},{25,17},{2,10},{10... | collective-permute-start | bytes 196616 | tf_op jit(solution)/shard_map/ppermute | solution.py:319
  10.1 2.6 %collective-permute-start.3 = (bf16[2,128,128]{2,1,0:T(8,128)(2,1)S(1)}, bf16[2,128,128]{2,1,0:T(8,128)(2,1)S(1)}, u32[]{:S(2)}, u32[]{:S(2)}) collective-permute-start(bf16[2,128,128]{2,1,0:T(8,128)(2,1)S(1)} %pad_maximum_fusion.packed.refs_0_.refs_4_), channel_id=1, source_target_pairs={{0,16},{8,24},{16,0},{24,8},{1,17},{9,25},{17,1},{25,9},{2,18},{10... | collective-permute-start | bytes 196616 | tf_op jit(solution)/shard_map/ppermute | solution.py:319
  12.7 3.3 %collective-permute-start.4 = (bf16[2,128,128]{2,1,0:T(8,128)(2,1)S(1)}, bf16[2,128,128]{2,1,0:T(8,128)(2,1)S(1)}, u32[]{:S(2)}, u32[]{:S(2)}) collective-permute-start(bf16[2,128,128]{2,1,0:T(8,128)(2,1)S(1)} %collective-permute-done.2.refs_1_.refs_5_), channel_id=1, source_target_pairs={{0,16},{8,24},{16,0},{24,8},{1,17},{9,25},{17,1},{25,9},{2,18},{10... | collective-permute-start | bytes 196616 | tf_op jit(solution)/shard_map/ppermute | solution.py:319
  18.5 0.8 %shard_map.130 = (f32[128,128]{1,0:T(8,128)S(1)}, f32[168,128]{1,0:T(8,128)S(1)}) custom-call(bf16[2,128,128]{2,1,0:T(8,128)(2,1)S(1)} %pad_maximum_fusion.packed.refs_0_.refs_4_, bf16[128,128]{1,0:T(8,128)(2,1)S(1)} %collective-permute-done.1.other_saved, bf16[4,128,640]{2,1,0:T(8,128)(2,1)S(1)} %get-tuple-element.39.kept, ...), custom_call_target="tpu_custom_call" | custom-call | flops 335544320 | bytes 2084864 | tf_op jit(solution)/shard_map/pallas_call | solution.py:267
  19.4 0.8 %shard_map.131.stats = f32[8,128]{1,0:T(8,128)S(1)} custom-call(f32[2,512]{1,0:T(2,128)S(1)} %get-tuple-element.43.bias, bf16[1024,128]{1,0:T(8,128)(2,1)S(1)} %copy-done.1, bf16[2,128,128]{2,1,0:T(8,128)(2,1)S(1)} %pad_maximum_fusion.packed.refs_0_.refs_4_, bf16[2,128,128]{2,1,0:T(8,128)(2,1)S(1)} %collective-permute-done.2.refs_1_.refs_5_, ...), custom_call_target="tpu_custom_call" | custom-call | flops 134217728 | bytes 528384 | tf_op jit(solution)/shard_map/pallas_call | solution.py:267
  20.7 3.6 %collective-permute-start.10 = (f32[80,128]{1,0:T(8,128)S(1)}, f32[80,128]{1,0:T(8,128)S(1)}, u32[]{:S(2)}, u32[]{:S(2)}) collective-permute-start(f32[80,128]{1,0:T(8,128)S(1)} %get-tuple-element.44.refs_0_), channel_id=1, source_target_pairs={{0,4},{1,5},{2,6},{3,7},{4,0},{5,1},{6,2},{7,3},{8,12},{9,13},{10,... | collective-permute-start | bytes 122888 | tf_op jit(solution)/shard_map/ppermute | solution.py:312
  24.3 2.2 %collective-permute-start.11 = (f32[80,128]{1,0:T(8,128)S(1)}, f32[80,128]{1,0:T(8,128)S(1)}, u32[]{:S(2)}, u32[]{:S(2)}) collective-permute-start(f32[80,128]{1,0:T(8,128)S(1)} %get-tuple-element.44.refs_0_), channel_id=1, source_target_pairs={{0,6},{1,7},{2,4},{3,5},{4,2},{5,3},{6,0},{7,1},{8,14},{9,15},{10,... | collective-permute-start | bytes 122888 | tf_op jit(solution)/shard_map/ppermute | solution.py:312
  27.0 0.9 %collective-permute-start.12 = (bf16[160,128]{1,0:T(8,128)(2,1)S(1)}, bf16[160,128]{1,0:T(8,128)(2,1)S(1)}, u32[]{:S(2)}, u32[]{:S(2)}) collective-permute-start(bf16[160,128]{1,0:T(8,128)(2,1)S(1)} %get-tuple-element.45.refs_8_), channel_id=1, source_target_pairs={{0,8},{8,0},{16,24},{24,16},{1,9},{9,1},{17,25},{25,17},{2,10},{10... | collective-permute-start | bytes 122888 | tf_op jit(solution)/shard_map/ppermute | solution.py:319
  27.9 3.3 %collective-permute-start.13 = (bf16[160,128]{1,0:T(8,128)(2,1)S(1)}, bf16[160,128]{1,0:T(8,128)(2,1)S(1)}, u32[]{:S(2)}, u32[]{:S(2)}) collective-permute-start(bf16[160,128]{1,0:T(8,128)(2,1)S(1)} %get-tuple-element.45.refs_8_), channel_id=1, source_target_pairs={{0,16},{8,24},{16,0},{24,8},{1,17},{9,25},{17,1},{25,9},{2,18},{10... | collective-permute-start | bytes 122888 | tf_op jit(solution)/shard_map/ppermute | solution.py:319
  31.3 1.7 %collective-permute-start.14 = (bf16[160,128]{1,0:T(8,128)(2,1)S(1)}, bf16[160,128]{1,0:T(8,128)(2,1)S(1)}, u32[]{:S(2)}, u32[]{:S(2)}) collective-permute-start(bf16[160,128]{1,0:T(8,128)(2,1)S(1)} %get-tuple-element.45.refs_8_), channel_id=1, source_target_pairs={{0,24},{8,16},{16,8},{24,0},{1,25},{9,17},{17,9},{25,1},{2,26},{10... | collective-permute-start | bytes 122888 | tf_op jit(solution)/shard_map/ppermute | solution.py:319
  32.9 3.0 %collective-permute-start.19 = (bf16[128,640]{1,0:T(8,128)(2,1)S(1)}, bf16[128,640]{1,0:T(8,128)(2,1)S(1)}, u32[]{:S(2)}, u32[]{:S(2)}) collective-permute-start(bf16[128,640]{1,0:T(8,128)(2,1)S(1)} %collective-permute-done.18.refs_0_), channel_id=1, source_target_pairs={{0,2},{1,3},{2,0},{3,1},{4,6},{5,7},{6,4},{7,5},{8,10},{9,11},{10,... | collective-permute-start | bytes 491528 | tf_op jit(solution)/shard_map/ppermute | solution.py:312
  35.9 1.5 %collective-permute-start.21 = (bf16[128,640]{1,0:T(8,128)(2,1)S(1)}, bf16[128,640]{1,0:T(8,128)(2,1)S(1)}, u32[]{:S(2)}, u32[]{:S(2)}) collective-permute-start(bf16[128,640]{1,0:T(8,128)(2,1)S(1)} %collective-permute-done.18.refs_0_), channel_id=1, source_target_pairs={{0,6},{1,7},{2,4},{3,5},{4,2},{5,3},{6,0},{7,1},{8,14},{9,15},{10,... | collective-permute-start | bytes 491528 | tf_op jit(solution)/shard_map/ppermute | solution.py:312
  37.5 2.4 %shard_map.133 = (bf16[1024,128]{1,0:T(8,128)(2,1)}, bf16[1024,128]{1,0:T(8,128)(2,1)}, bf16[208,128]{1,0:T(8,128)(2,1)S(1)}, bf16[208,128]{1,0:T(8,128)(2,1)S(1...) custom-call(f32[2,512]{1,0:T(2,128)S(1)} %get-tuple-element.43.bias, bf16[1024,128]{1,0:T(8,128)(2,1)S(1)} %copy-done.1, ...), custom_call_target="tpu_custom_call" | custom-call | flops 671088640 | bytes 1118208 | tf_op jit(solution)/shard_map/pallas_call | solution.py:267
  40.2 1.6 %collective-permute-start.16 = (bf16[208,128]{1,0:T(8,128)(2,1)S(1)}, bf16[208,128]{1,0:T(8,128)(2,1)S(1)}, u32[]{:S(2)}, u32[]{:S(2)}) collective-permute-start(bf16[208,128]{1,0:T(8,128)(2,1)S(1)} %get-tuple-element.48), channel_id=1, source_target_pairs={{0,16},{8,24},{16,0},{24,8},{1,17},{9,25},{17,1},{25,9},{2,18},{10... | collective-permute-start | bytes 159752 | tf_op jit(solution)/shard_map/ppermute | solution.py:319
  41.7 2.3 %collective-permute-done.15.refs_1_ = bf16[208,128]{1,0:T(8,128)(2,1)S(1)} collective-permute-done((bf16[208,128]{1,0:T(8,128)(2,1)S(1)}, bf16[208,128]{1,0:T(8,128)(2,1)S(1)}, u32[]{:S(2)}, u32[]{:S(2)}) %collective-permute-start.15) | collective-permute-done | bytes 53280 | tf_op jit(solution)/shard_map/ppermute | solution.py:319
  44.0 1.3 %collective-permute-start.17 = (bf16[208,128]{1,0:T(8,128)(2,1)S(1)}, bf16[208,128]{1,0:T(8,128)(2,1)S(1)}, u32[]{:S(2)}, u32[]{:S(2)}) collective-permute-start(bf16[208,128]{1,0:T(8,128)(2,1)S(1)} %get-tuple-element.49), channel_id=1, source_target_pairs={{0,24},{8,16},{16,8},{24,0},{1,25},{9,17},{17,9},{25,1},{2,26},{10... | collective-permute-start | bytes 159752 | tf_op jit(solution)/shard_map/ppermute | solution.py:319
  45.3 4.7 %collective-permute-done.17.refs_3_ = bf16[208,128]{1,0:T(8,128)(2,1)S(1)} collective-permute-done((bf16[208,128]{1,0:T(8,128)(2,1)S(1)}, bf16[208,128]{1,0:T(8,128)(2,1)S(1)}, u32[]{:S(2)}, u32[]{:S(2)}) %collective-permute-start.17) | collective-permute-done | bytes 53280 | tf_op jit(solution)/shard_map/ppermute | solution.py:319
  50.2 0.9 %shard_map.134 = (bf16[128,128]{1,0:T(8,128)(2,1)}, f32[16,5120]{1,0:T(8,128)}) custom-call(f32[8,16,128]{2,1,0:T(8,128)S(1)} %get-tuple-element.35.hot, bf16[208,128]{1,0:T(8,128)(2,1)S(1)} %get-tuple-element.46.refs_0_, bf16[208,128]{1,0:T(8,128)(2,1)S(1)} %collective-permute-done.15.refs_1_, bf16[208,128]{1,0:T(8,128)(2,1)S(1)} %collective-permute-done.16.refs_2_, ...), custom_call_target="tpu_custom_call" | custom-call | bytes 278528 | tf_op jit(solution)/shard_map/pallas_call | solution.py:267
  51.1 1.2 %collective-permute-done.22.other = bf16[4,128,640]{2,1,0:T(8,128)(2,1)S(1)} collective-permute-done((bf16[4,128,640]{2,1,0:T(8,128)(2,1)S(1)}, bf16[4,128,640]{2,1,0:T(8,128)(2,1)S(1)}, u32[]{:S(2)}, u32[]{:S(2)}) %collective-permute-start.22) | collective-permute-done | bytes 655392 | tf_op jit(solution)/shard_map/ppermute | solution.py:316
  52.3 1.4 %shard_map.136 = f32[128,1280]{1,0:T(8,128)} custom-call(bf16[4,128,640]{2,1,0:T(8,128)(2,1)S(1)} %shard_map.135.own, bf16[4,128,640]{2,1,0:T(8,128)(2,1)S(1)} %collective-permute-done.22.other, bf16[2,128,128]{2,1,0:T(8,128)(2,1)S(1)} %pad_maximum_fusion.packed.refs_0_.refs_4_, bf16[2,128,128]{2,1,0:T(8,128)(2,1)S(1)} %collective-permute-done.2.refs_1_.refs_5_, ...), custom_call_target="tpu_custom_call" | custom-call | flops 167772160 | bytes 1572864 | tf_op jit(solution)/shard_map/pallas_call | solution.py:267
  (48 shorter events, 4.6 us)
Async XLA Ops:
  2.3 5.8 %collective-permute-start = (bf16[4,128,640]{2,1,0:T(8,128)(2,1)S(1)}, bf16[4,128,640]{2,1,0:T(8,128)(2,1)S(1)}, u32[]{:S(2)}, u32[]{:S(2)}) collective-permute-start(bf16[4,128,640]{2,1,0:T(8,128)(2,1)S(1)} %get-tuple-element.33), channel_id=1, source_target_pairs={{0,1},{1,0},{2,3},{3,2},{4,5},{5,4},{6,7},{7,6},{8,9},{9,8},{10,11... | collective-permute-start | bytes 1966088 | tf_op jit(solution)/shard_map/ppermute | solution.py:316
  2.8 15.7 %collective-permute-start.5 = (bf16[128,640]{1,0:T(8,128)(2,1)S(1)}, bf16[128,640]{1,0:T(8,128)(2,1)S(1)}, u32[]{:S(2)}, u32[]{:S(2)}) collective-permute-start(bf16[128,640]{1,0:T(8,128)(2,1)S(1)} %copy-done.2), channel_id=1, source_target_pairs={{0,2},{1,3},{2,0},{3,1},{4,6},{5,7},{6,4},{7,5},{8,10},{9,11},{10,... | collective-permute-start | bytes 491528 | tf_op jit(solution)/shard_map/ppermute | solution.py:312
  5.4 13.2 %collective-permute-start.6 = (bf16[128,640]{1,0:T(8,128)(2,1)S(1)}, bf16[128,640]{1,0:T(8,128)(2,1)S(1)}, u32[]{:S(2)}, u32[]{:S(2)}) collective-permute-start(bf16[128,640]{1,0:T(8,128)(2,1)S(1)} %copy-done.2), channel_id=1, source_target_pairs={{0,4},{1,5},{2,6},{3,7},{4,0},{5,1},{6,2},{7,3},{8,12},{9,13},{10,... | collective-permute-start | bytes 491528 | tf_op jit(solution)/shard_map/ppermute | solution.py:312
  6.9 11.6 %collective-permute-start.7 = (bf16[128,640]{1,0:T(8,128)(2,1)S(1)}, bf16[128,640]{1,0:T(8,128)(2,1)S(1)}, u32[]{:S(2)}, u32[]{:S(2)}) collective-permute-start(bf16[128,640]{1,0:T(8,128)(2,1)S(1)} %copy-done.2), channel_id=1, source_target_pairs={{0,6},{1,7},{2,4},{3,5},{4,2},{5,3},{6,0},{7,1},{8,14},{9,15},{10,... | collective-permute-start | bytes 491528 | tf_op jit(solution)/shard_map/ppermute | solution.py:312
  6.9 1.2 %collective-permute-start.1 = (bf16[128,128]{1,0:T(8,128)(2,1)S(1)}, bf16[128,128]{1,0:T(8,128)(2,1)S(1)}, u32[]{:S(2)}, u32[]{:S(2)}) collective-permute-start(bf16[128,128]{1,0:T(8,128)(2,1)S(1)} %copy-done.7), channel_id=1, source_target_pairs={{0,1},{1,0},{2,3},{3,2},{4,5},{5,4},{6,7},{7,6},{8,9},{9,8},{10,11... | collective-permute-start | bytes 98312 | tf_op jit(solution)/shard_map/ppermute | solution.py:316
  8.1 4.6 %collective-permute-start.2 = (bf16[2,128,128]{2,1,0:T(8,128)(2,1)S(1)}, bf16[2,128,128]{2,1,0:T(8,128)(2,1)S(1)}, u32[]{:S(2)}, u32[]{:S(2)}) collective-permute-start(bf16[2,128,128]{2,1,0:T(8,128)(2,1)S(1)} %pad_maximum_fusion.packed.refs_0_.refs_4_), channel_id=1, source_target_pairs={{0,8},{8,0},{16,24},{24,16},{1,9},{9,1},{17,25},{25,17},{2,10},{10... | collective-permute-start | bytes 196616 | tf_op jit(solution)/shard_map/ppermute | solution.py:319
  10.1 6.5 %collective-permute-start.3 = (bf16[2,128,128]{2,1,0:T(8,128)(2,1)S(1)}, bf16[2,128,128]{2,1,0:T(8,128)(2,1)S(1)}, u32[]{:S(2)}, u32[]{:S(2)}) collective-permute-start(bf16[2,128,128]{2,1,0:T(8,128)(2,1)S(1)} %pad_maximum_fusion.packed.refs_0_.refs_4_), channel_id=1, source_target_pairs={{0,16},{8,24},{16,0},{24,8},{1,17},{9,25},{17,1},{25,9},{2,18},{10... | collective-permute-start | bytes 196616 | tf_op jit(solution)/shard_map/ppermute | solution.py:319
  12.7 5.8 %collective-permute-start.4 = (bf16[2,128,128]{2,1,0:T(8,128)(2,1)S(1)}, bf16[2,128,128]{2,1,0:T(8,128)(2,1)S(1)}, u32[]{:S(2)}, u32[]{:S(2)}) collective-permute-start(bf16[2,128,128]{2,1,0:T(8,128)(2,1)S(1)} %collective-permute-done.2.refs_1_.refs_5_), channel_id=1, source_target_pairs={{0,16},{8,24},{16,0},{24,8},{1,17},{9,25},{17,1},{25,9},{2,18},{10... | collective-permute-start | bytes 196616 | tf_op jit(solution)/shard_map/ppermute | solution.py:319
  16.6 11.3 %collective-permute-start.18 = (bf16[128,640]{1,0:T(8,128)(2,1)S(1)}, bf16[128,640]{1,0:T(8,128)(2,1)S(1)}, u32[]{:S(2)}, u32[]{:S(2)}) collective-permute-start(bf16[128,640]{1,0:T(8,128)(2,1)S(1)} %copy-done.2), channel_id=1, source_target_pairs={{0,0},{1,1},{2,10},{3,11},{4,20},{5,21},{6,30},{7,31},{8,2},{9,3},... | collective-permute-start | bytes 491528 | tf_op jit(solution)/shard_map/ppermute | solution.py:342
  18.5 18.9 %copy-start.5 = (bf16[1024,128]{1,0:T(8,128)(2,1)S(1)}, bf16[1024,128]{1,0:T(8,128)(2,1)}, u32[]{:S(2)}) copy-start(bf16[1024,128]{1,0:T(8,128)(2,1)} %values.1) | copy-start | bytes 786436
  19.3 1.3 %collective-permute-start.8 = (f32[168,128]{1,0:T(8,128)S(1)}, f32[168,128]{1,0:T(8,128)S(1)}, u32[]{:S(2)}, u32[]{:S(2)}) collective-permute-start(f32[168,128]{1,0:T(8,128)S(1)} %get-tuple-element.42.sent), channel_id=1, source_target_pairs={{0,1},{1,0},{2,3},{3,2},{4,5},{5,4},{6,7},{7,6},{8,9},{9,8},{10,11... | collective-permute-start | bytes 258056 | tf_op jit(solution)/shard_map/ppermute | solution.py:316
  20.7 10.6 %collective-permute-start.10 = (f32[80,128]{1,0:T(8,128)S(1)}, f32[80,128]{1,0:T(8,128)S(1)}, u32[]{:S(2)}, u32[]{:S(2)}) collective-permute-start(f32[80,128]{1,0:T(8,128)S(1)} %get-tuple-element.44.refs_0_), channel_id=1, source_target_pairs={{0,4},{1,5},{2,6},{3,7},{4,0},{5,1},{6,2},{7,3},{8,12},{9,13},{10,... | collective-permute-start | bytes 122888 | tf_op jit(solution)/shard_map/ppermute | solution.py:312
  24.3 8.6 %collective-permute-start.11 = (f32[80,128]{1,0:T(8,128)S(1)}, f32[80,128]{1,0:T(8,128)S(1)}, u32[]{:S(2)}, u32[]{:S(2)}) collective-permute-start(f32[80,128]{1,0:T(8,128)S(1)} %get-tuple-element.44.refs_0_), channel_id=1, source_target_pairs={{0,6},{1,7},{2,4},{3,5},{4,2},{5,3},{6,0},{7,1},{8,14},{9,15},{10,... | collective-permute-start | bytes 122888 | tf_op jit(solution)/shard_map/ppermute | solution.py:312
  26.5 6.4 %collective-permute-start.9 = (f32[80,128]{1,0:T(8,128)S(1)}, f32[80,128]{1,0:T(8,128)S(1)}, u32[]{:S(2)}, u32[]{:S(2)}) collective-permute-start(f32[80,128]{1,0:T(8,128)S(1)} %get-tuple-element.44.refs_0_), channel_id=1, source_target_pairs={{0,2},{1,3},{2,0},{3,1},{4,6},{5,7},{6,4},{7,5},{8,10},{9,11},{10,... | collective-permute-start | bytes 122888 | tf_op jit(solution)/shard_map/ppermute | solution.py:312
  27.0 8.9 %collective-permute-start.12 = (bf16[160,128]{1,0:T(8,128)(2,1)S(1)}, bf16[160,128]{1,0:T(8,128)(2,1)S(1)}, u32[]{:S(2)}, u32[]{:S(2)}) collective-permute-start(bf16[160,128]{1,0:T(8,128)(2,1)S(1)} %get-tuple-element.45.refs_8_), channel_id=1, source_target_pairs={{0,8},{8,0},{16,24},{24,16},{1,9},{9,1},{17,25},{25,17},{2,10},{10... | collective-permute-start | bytes 122888 | tf_op jit(solution)/shard_map/ppermute | solution.py:319
  27.9 9.5 %collective-permute-start.13 = (bf16[160,128]{1,0:T(8,128)(2,1)S(1)}, bf16[160,128]{1,0:T(8,128)(2,1)S(1)}, u32[]{:S(2)}, u32[]{:S(2)}) collective-permute-start(bf16[160,128]{1,0:T(8,128)(2,1)S(1)} %get-tuple-element.45.refs_8_), channel_id=1, source_target_pairs={{0,16},{8,24},{16,0},{24,8},{1,17},{9,25},{17,1},{25,9},{2,18},{10... | collective-permute-start | bytes 122888 | tf_op jit(solution)/shard_map/ppermute | solution.py:319
  31.3 6.2 %collective-permute-start.14 = (bf16[160,128]{1,0:T(8,128)(2,1)S(1)}, bf16[160,128]{1,0:T(8,128)(2,1)S(1)}, u32[]{:S(2)}, u32[]{:S(2)}) collective-permute-start(bf16[160,128]{1,0:T(8,128)(2,1)S(1)} %get-tuple-element.45.refs_8_), channel_id=1, source_target_pairs={{0,24},{8,16},{16,8},{24,0},{1,25},{9,17},{17,9},{25,1},{2,26},{10... | collective-permute-start | bytes 122888 | tf_op jit(solution)/shard_map/ppermute | solution.py:319
  32.9 17.1 %collective-permute-start.19 = (bf16[128,640]{1,0:T(8,128)(2,1)S(1)}, bf16[128,640]{1,0:T(8,128)(2,1)S(1)}, u32[]{:S(2)}, u32[]{:S(2)}) collective-permute-start(bf16[128,640]{1,0:T(8,128)(2,1)S(1)} %collective-permute-done.18.refs_0_), channel_id=1, source_target_pairs={{0,2},{1,3},{2,0},{3,1},{4,6},{5,7},{6,4},{7,5},{8,10},{9,11},{10,... | collective-permute-start | bytes 491528 | tf_op jit(solution)/shard_map/ppermute | solution.py:312
  35.9 14.1 %collective-permute-start.20 = (bf16[128,640]{1,0:T(8,128)(2,1)S(1)}, bf16[128,640]{1,0:T(8,128)(2,1)S(1)}, u32[]{:S(2)}, u32[]{:S(2)}) collective-permute-start(bf16[128,640]{1,0:T(8,128)(2,1)S(1)} %collective-permute-done.18.refs_0_), channel_id=1, source_target_pairs={{0,4},{1,5},{2,6},{3,7},{4,0},{5,1},{6,2},{7,3},{8,12},{9,13},{10,... | collective-permute-start | bytes 491528 | tf_op jit(solution)/shard_map/ppermute | solution.py:312
  35.9 14.1 %collective-permute-start.21 = (bf16[128,640]{1,0:T(8,128)(2,1)S(1)}, bf16[128,640]{1,0:T(8,128)(2,1)S(1)}, u32[]{:S(2)}, u32[]{:S(2)}) collective-permute-start(bf16[128,640]{1,0:T(8,128)(2,1)S(1)} %collective-permute-done.18.refs_0_), channel_id=1, source_target_pairs={{0,6},{1,7},{2,4},{3,5},{4,2},{5,3},{6,0},{7,1},{8,14},{9,15},{10,... | collective-permute-start | bytes 491528 | tf_op jit(solution)/shard_map/ppermute | solution.py:312
  39.9 4.1 %collective-permute-start.15 = (bf16[208,128]{1,0:T(8,128)(2,1)S(1)}, bf16[208,128]{1,0:T(8,128)(2,1)S(1)}, u32[]{:S(2)}, u32[]{:S(2)}) collective-permute-start(bf16[208,128]{1,0:T(8,128)(2,1)S(1)} %get-tuple-element.47), channel_id=1, source_target_pairs={{0,8},{8,0},{16,24},{24,16},{1,9},{9,1},{17,25},{25,17},{2,10},{10... | collective-permute-start | bytes 159752 | tf_op jit(solution)/shard_map/ppermute | solution.py:319
  40.2 5.1 %collective-permute-start.16 = (bf16[208,128]{1,0:T(8,128)(2,1)S(1)}, bf16[208,128]{1,0:T(8,128)(2,1)S(1)}, u32[]{:S(2)}, u32[]{:S(2)}) collective-permute-start(bf16[208,128]{1,0:T(8,128)(2,1)S(1)} %get-tuple-element.48), channel_id=1, source_target_pairs={{0,16},{8,24},{16,0},{24,8},{1,17},{9,25},{17,1},{25,9},{2,18},{10... | collective-permute-start | bytes 159752 | tf_op jit(solution)/shard_map/ppermute | solution.py:319
  44.0 5.9 %collective-permute-start.17 = (bf16[208,128]{1,0:T(8,128)(2,1)S(1)}, bf16[208,128]{1,0:T(8,128)(2,1)S(1)}, u32[]{:S(2)}, u32[]{:S(2)}) collective-permute-start(bf16[208,128]{1,0:T(8,128)(2,1)S(1)} %get-tuple-element.49), channel_id=1, source_target_pairs={{0,24},{8,16},{16,8},{24,0},{1,25},{9,17},{17,9},{25,1},{2,26},{10... | collective-permute-start | bytes 159752 | tf_op jit(solution)/shard_map/ppermute | solution.py:319
  50.1 2.2 %collective-permute-start.22 = (bf16[4,128,640]{2,1,0:T(8,128)(2,1)S(1)}, bf16[4,128,640]{2,1,0:T(8,128)(2,1)S(1)}, u32[]{:S(2)}, u32[]{:S(2)}) collective-permute-start(bf16[4,128,640]{2,1,0:T(8,128)(2,1)S(1)} %shard_map.135.own), channel_id=1, source_target_pairs={{0,1},{1,0},{2,3},{3,2},{4,5},{5,4},{6,7},{7,6},{8,9},{9,8},{10,11... | collective-permute-start | bytes 1966088 | tf_op jit(solution)/shard_map/ppermute | solution.py:316
  (7 other events, 81.6 us)

commit v5 on v4

--- a/solution.py
+++ b/solution.py
@@ -39,16 +39,15 @@
     return lambda frame: sum((frame >= bound).astype(jnp.int32) for bound in bounds)
 
 
-def cut_kernel(chips, weight_in, kept, sent, sems):
+def cut_kernel(chips, weight_in, saved_in, kept, sent, sems):
     _, chip, core = place()
     width = kept.shape[2]
-    copies = []
+    moves = [(saved_in, sent.at[:, chips * width : chips * width + HD])]
     for k in range(chips):
-        for c, out in ((1 - core, sent), (core, kept)):
+        for c, out in ((1 - core, sent.at[:, k * width : (k + 1) * width]), (core, kept.at[k])):
             columns = pl.ds(pl.multiple_of((2 * (chip ^ k) + c) * width, LANES), width)
-            copies.append(
-                pltpu.make_async_copy(weight_in.at[:, columns], out.at[k], sems.at[len(copies)])
-            )
+            moves.append((weight_in.at[:, columns], out))
+    copies = [pltpu.make_async_copy(a, b, sems.at[i]) for i, (a, b) in enumerate(moves)]
     for copy in copies:
         copy.start()
     for copy in copies:
@@ -79,10 +78,10 @@
         for k in range(chips):
             columns = pl.ds(pl.multiple_of((2 * (chip ^ k) + core) * width, LANES), width)
             gate_a[k, r : r + 1, :] = gate[pl.ds(level, 1), columns]
-        for k in range(n_t):
-            level = levels[(t ^ chip ^ k) * frames + r]
-            mine = pl.ds(pl.multiple_of((2 * t + core) * width, LANES), width)
-            gate_b[k, r : r + 1, :] = gate[pl.ds(level, 1), mine]
+    mine = pl.ds(pl.multiple_of((2 * t + core) * width, LANES), width)
+    for k in range(n_t):
+        level = levels[(t ^ k) * frames + chip * (rows // chips) // QF]
+        gate_b[k] = gate[pl.ds(level, 1), mine]
 
 
 def stats_kernel(n_t, bias, keys, *refs):
@@ -101,15 +100,15 @@
             out[n_t + p + i : n_t + p + i + 1, :] = total[:, i * rows : (i + 1) * rows]
 
 
-def head_kernel(chips, frames, packed, other_saved, kept, received, gate_a, *refs):
-    pieces, (mine, other) = refs[:chips], refs[chips:]
+def head_kernel(chips, frames, packed, kept, received, gate_a, *refs):
+    pieces, (mine, other, terms) = refs[:chips], refs[chips:]
     _, chip, _ = place()
-    rows = mine.shape[0]
-    tiles = pieces[0].shape[1] // LANES
-    saved = jnp.concatenate([packed[1], other_saved[...]], axis=1)
+    width = pieces[0].shape[1]
+    tiles = width // LANES
+    saved = jnp.concatenate([packed[1], received[:, chips * width : chips * width + HD]], axis=1)
     head = None
     for k in range(chips):
-        weight = jnp.concatenate([kept[k], received[k]], axis=0)
+        weight = jnp.concatenate([kept[k], received[:, k * width : (k + 1) * width]], axis=0)
         wide = pieces[k][...].astype(jnp.float32)
         gated = jnp.concatenate(
             [
@@ -124,53 +123,96 @@
         for r in range(frames):
             term = jnp.sum(product[r * QF : (r + 1) * QF], axis=0, keepdims=True)
             for j in range(tiles):
-                row = rows + ((chip ^ k) * frames + r) * tiles + j
-                other[pl.ds(row, 1), :] = term[:, j * LANES : (j + 1) * LANES]
+                row = ((chip ^ k) * frames + r) * tiles + j
+                terms[pl.ds(row, 1), :] = term[:, j * LANES : (j + 1) * LANES]
     mine[...] = head[:, :HD]
-    other[:rows, :] = head[:, HD:]
-
-
-def join_kernel(mine, sent, received, stats, out, terms):
-    core = place()[2]
-    rows = mine.shape[0]
-    out[:rows, :] = (mine[...] + received[:rows, :]).astype(jnp.bfloat16)
-    own, other = sent[rows:, :], received[rows:, :]
-    count = own.shape[0]
-    terms[:count, :] = jnp.where(core == 0, own, other)
-    terms[count:, :] = jnp.where(core == 0, other, own)
+    other[...] = head[:, HD:]
+
+
+def sections(rows, chips, tiles, n_t, count):
+    starts = [0, rows]
+    starts.append(starts[-1] + -(-SPLIT * 2 * n_t // 16) * 16)
+    starts.append(starts[-1] + tiles * (rows // chips))
+    starts.append(starts[-1] + -(-count // 16) * 16)
+    return starts
+
+
+def padded(x, rows):
+    if x.shape[0] == rows:
+        return x
+    return jnp.concatenate([x, jnp.zeros((rows - x.shape[0], x.shape[1]), x.dtype)], axis=0)
+
+
+def join_kernel(n_t, chips, starts, mine, received, stats, terms, *refs):
+    pieces, outs, (wide, held) = refs[:chips], refs[chips : chips + n_t][::-1], refs[chips + n_t :]
+    t, chip, _ = place()
+    part, tiles = held.shape[1], held.shape[2] // LANES
+    for k in range(chips):
+        wide[...] = pieces[k][...].astype(jnp.float32)
+        held[k] = wide[pl.ds(pl.multiple_of(chip * part, part), part), :]
+    head = (mine[...] + received[...]).astype(jnp.bfloat16)
     rest = stats[...]
-    parts = []
+    split = []
     for _ in range(SPLIT):
-        part = rest.astype(jnp.bfloat16).astype(jnp.float32)
-        parts.append(part)
-        rest = rest - part
-    pad = out.shape[0] - rows - SPLIT * rest.shape[0]
-    if pad:
-        parts.append(jnp.zeros((pad, LANES), jnp.float32))
-    out[rows:, :] = jnp.concatenate(parts, axis=0).astype(jnp.bfloat16)
-
-
-def grads_kernel(n_t, chips, bias, keys, values, *refs):
-    terms, refs = refs[:chips], refs[chips:]
-    packed, heads = refs[:n_t], refs[n_t : 2 * n_t]
+        piece = rest.astype(jnp.bfloat16).astype(jnp.float32)
+        split.append(piece)
+        rest = rest - piece
+    split = padded(jnp.concatenate(split, axis=0), starts[2] - starts[1]).astype(jnp.bfloat16)
+    last = padded(terms[...], starts[4] - starts[3]).astype(jnp.bfloat16)
+    for k in range(n_t):
+        rows = held[chip ^ t ^ k]
+        rows = jnp.concatenate([rows[:, j * LANES : (j + 1) * LANES] for j in range(tiles)], axis=0)
+        outs[k][: starts[1], :] = head
+        outs[k][starts[1] : starts[2], :] = split
+        outs[k][starts[2] : starts[3], :] = rows.astype(jnp.bfloat16)
+        outs[k][starts[3] :, :] = last
+
+
+def bundle_kernel(n_t, starts, count, gate_b, *refs):
+    heads, out = refs[:n_t][::-1], refs[n_t]
+    tiles = gate_b.shape[2] // LANES
+    part = (starts[3] - starts[2]) // tiles
+    wide = [heads[k][starts[2] : starts[3], :].astype(jnp.float32) for k in range(n_t)]
+    for j in range(tiles):
+        gated = jnp.concatenate(
+            [
+                wide[k][j * part : (j + 1) * part] * gate_b[k, :, j * LANES : (j + 1) * LANES]
+                for k in range(n_t)
+            ],
+            axis=0,
+        )
+        out[j * n_t * part : (j + 1) * n_t * part, :] = gated.astype(jnp.bfloat16)
+    terms = [heads[k][starts[3] :, :].astype(jnp.float32)[:count] for k in range(n_t)]
+    out[tiles * n_t * part :, :] = jnp.concatenate(terms, axis=0).astype(jnp.bfloat16)
+
+
+def collect_kernel(chips, base, *refs):
+    pieces, out, held = refs[:chips], refs[chips], refs[chips + 1]
+    chip = place()[1]
+    for k in range(chips):
+        out[k * base : (k + 1) * base, :] = pieces[k][:base, :]
+        held[chip ^ k] = pieces[k][base:, :].astype(jnp.float32)
+    total = held[0]
+    for k in range(1, chips):
+        total = total + held[k]
+    high = total.astype(jnp.bfloat16)
+    count = total.shape[0]
+    out[chips * base : chips * base + count, :] = high
+    out[chips * base + count :, :] = (total - high.astype(jnp.float32)).astype(jnp.bfloat16)
+
+
+def grads_kernel(n_t, bias, keys, values, *refs):
+    packed, heads = refs[:n_t], refs[n_t : 2 * n_t][::-1]
     key_out, value_out = refs[2 * n_t : 2 * n_t + 2]
-    outs = refs[2 * n_t + 2 : 3 * n_t + 2]
-    key_acc, value_acc, held = refs[3 * n_t + 2 :]
-    chip = place()[1]
+    outs = refs[2 * n_t + 2 : 3 * n_t + 2][::-1]
+    key_acc, value_acc = refs[3 * n_t + 2 :]
     rows = packed[0].shape[1]
     ones = jnp.ones((8, HD), jnp.float32)
     keys_t = jnp.transpose(keys[...])
     stats = []
     for k in range(n_t):
-        parts = heads[k][rows:, :].astype(jnp.float32)
+        parts = heads[k][rows : rows + -(-SPLIT * 2 * n_t // 16) * 16, :].astype(jnp.float32)
         stats.append(sum(parts[i * 2 * n_t : (i + 1) * 2 * n_t] for i in range(SPLIT)))
-    for k in range(chips):
-        held[chip ^ k] = terms[k][...]
-    total = held[0]
-    for k in range(1, chips):
-        total = total + held[k]
-    for k in range(n_t):
-        outs[k][rows:, :] = total.astype(jnp.bfloat16)
     for p in range(0, n_t, 2):
         q = jnp.concatenate([packed[p][0], packed[p + 1][0]], axis=0)
         o = jnp.concatenate([packed[p][1], packed[p + 1][1]], axis=0)
@@ -208,56 +250,68 @@
                 key_out[span, :] = (key_add * SCALE).astype(jnp.bfloat16)
             part = dot(keys_t[:, span], score_grad, 1, 0)
             query_part = part if query_part is None else query_part + part
-        outs[p][:rows, :] = query_part[:, :rows].astype(jnp.bfloat16)
-        outs[p + 1][:rows, :] = query_part[:, rows:].astype(jnp.bfloat16)
-
-
-def finish_kernel(n_t, chips, frames, hot, *refs):
-    parts, (query_out, gate_out, held) = refs[:n_t], refs[n_t:]
-    t = lax.axis_index("tm")
-    rows = query_out.shape[0]
-    total = parts[0][:rows, :].astype(jnp.float32)
+        outs[p][...] = query_part[:, :rows].astype(jnp.bfloat16)
+        outs[p + 1][...] = query_part[:, rows:].astype(jnp.bfloat16)
+
+
+def query_kernel(n_t, *refs):
+    total = refs[0][...].astype(jnp.float32)
     for k in range(1, n_t):
-        total = total + parts[k][:rows, :].astype(jnp.float32)
-    query_out[...] = jnp.transpose(total * SCALE).astype(jnp.bfloat16)
+        total = total + refs[k][...].astype(jnp.float32)
+    refs[n_t][...] = jnp.transpose(total * SCALE).astype(jnp.bfloat16)
+
+
+def final_kernel(n_t, chips, frames, hot, own, other, *refs):
+    packed, (weight_out, gate_out, saved, held) = refs[:n_t], refs[n_t:]
+    t, chip, core = place()
+    width = weight_out.shape[1] // 2
+    tiles = width // LANES
+    rows = saved.shape[1]
+    part = rows // chips
+    base = tiles * n_t * part
     for k in range(n_t):
-        held[t ^ k] = parts[k][rows:, :].astype(jnp.float32)
-    tiles = gate_out.shape[1] // (2 * chips * LANES)
-    for core in range(2):
+        saved[k] = packed[k][1].astype(jnp.float32)
+    ordered = []
+    for c in range(chips):
+        mine = pl.ds(pl.multiple_of((chip ^ c) * part, part), part)
+        ordered += [saved[k, mine, :] for k in range(n_t)]
+    ordered = jnp.transpose(jnp.concatenate(ordered, axis=0)).astype(jnp.bfloat16)
+    count = (own.shape[0] - chips * base) // 2
+    each = count // n_t
+    for ref, half in ((own, core), (other, 1 - core)):
+        gated = jnp.concatenate(
+            [
+                jnp.concatenate(
+                    [
+                        ref[c * base + j * n_t * part : c * base + (j + 1) * n_t * part, :]
+                        for c in range(chips)
+                    ],
+                    axis=0,
+                )
+                for j in range(tiles)
+            ],
+            axis=1,
+        )
+        result = dot(ordered, gated, 1, 0)
+        terms = ref[chips * base : chips * base + count, :].astype(jnp.float32)
+        terms = terms + ref[chips * base + count :, :].astype(jnp.float32)
+        for k in range(n_t):
+            held[half, t ^ k] = terms[k * each : (k + 1) * each]
+        for h in range(2):
+
+            @pl.when(half == h)
+            def _():
+                weight_out[:, h * width : (h + 1) * width] = result
+
+    for half in range(2):
         for a in range(chips):
             for j in range(tiles):
                 total = jnp.zeros(hot.shape[1:], jnp.float32)
                 for f in range(n_t * frames):
-                    row = ((core * chips + a) * frames + f % frames) * tiles + j
-                    total = total + hot[f] * held[f // frames, row : row + 1, :]
-                column = ((2 * a + core) * tiles + j) * LANES
+                    row = (a * frames + f % frames) * tiles + j
+                    total = total + hot[f] * held[half, f // frames, row : row + 1, :]
+                column = ((2 * a + half) * tiles + j) * LANES
                 gate_out[:, column : column + LANES] = total
-
-
-def gated_kernel(n_t, frames, gate_b, *refs):
-    pieces, out = refs[:n_t], refs[n_t]
-    for k in range(n_t):
-        for r in range(frames):
-            span = slice(r * QF, (r + 1) * QF)
-            wide = pieces[k][span, :].astype(jnp.float32)
-            out[k, span, :] = (wide * gate_b[k, r : r + 1, :]).astype(jnp.bfloat16)
-
-
-def weight_kernel(n_t, own, other, *refs):
-    packed, out, held = refs[:n_t], refs[n_t], refs[n_t + 1]
-    _, chip, core = place()
-    width = own.shape[2]
-    for k in range(n_t):
-        held[k] = packed[k][1]
-    saved = jnp.concatenate([held[chip ^ k] for k in range(n_t)], axis=0)
-    for ref, half in ((own, core), (other, 1 - core)):
-        gated = jnp.concatenate([ref[k] for k in range(n_t)], axis=0)
-        result = dot(saved, gated, 0, 0)
-        for h in range(2):
-
-            @pl.when(half == h)
-            def _():
-                out[:, h * width : (h + 1) * width] = result
 
 
 def call(kernel, args, out_shape, scratch=(), flops=0, in_place=False, in_smem=0):
@@ -318,28 +372,29 @@
     def over_time(x, k):
         return lax.ppermute(x, "tm", [(t, t ^ k) for t in range(n_t)])
 
+    tiles = width // LANES
+    part = rows // chips
+    count = chips * frames * tiles
+    starts = sections(rows, chips, tiles, n_t, count)
+
+    def time_swaps(messages):
+        got = {k: over_time(messages[k], k) for k in range(n_t - 1, 0, -1)}
+        return [messages[0]] + [got[k] for k in range(1, n_t)]
+
     pieces = over_chips(out_grad)
     kept, sent = call(
         functools.partial(cut_kernel, chips),
-        [proj_weight],
-        [shape(bf16, chips, HD, width)] * 2,
-        [pltpu.SemaphoreType.DMA((2 * chips,))],
+        [proj_weight, saved_out],
+        [shape(bf16, chips, HD, width), shape(bf16, HD, chips * width + HD)],
+        [pltpu.SemaphoreType.DMA((2 * chips + 1,))],
         in_place=True,
     )
-    received, other_saved = over_cores(sent), over_cores(saved_out)
-    packed, _ = lax.optimization_barrier((jnp.stack([queries, saved_out]), (received, other_saved)))
+    received = over_cores(sent)
+    packed, _ = lax.optimization_barrier((jnp.stack([queries, saved_out]), received))
     packed_all = [packed]
     for k in range(1, n_t):
         high = 1 << (k.bit_length() - 1)
         packed_all.append(over_time(packed_all[k - high], high))
-    moves = [
-        (t * n_s + 2 * c + e, c * n_s + 2 * (c ^ t) + e)
-        for t in range(n_t)
-        for c in range(chips)
-        for e in range(2)
-    ]
-    to_move, _ = lax.optimization_barrier((out_grad, packed_all[n_t // 2]))
-    moved = lax.ppermute(to_move, ("tm", "space"), moves)
     gate_table, _ = lax.optimization_barrier((gate_table, received))
     bias, gate_a, gate_b, hot = call(
         functools.partial(masks_kernel, n_t, chips, frames, rows),
@@ -347,17 +402,15 @@
         [
             shape(f32, frames, n_t * rows),
             shape(f32, chips, frames, width),
-            shape(f32, n_t, frames, width),
+            shape(f32, n_t, 1, width),
             shape(f32, n_t * frames, levels, LANES),
         ],
         in_smem=2,
     )
-    kept, _ = lax.optimization_barrier((kept, packed_all))
-    count = chips * frames * width // LANES
-    mine, other = call(
+    mine, other, terms = call(
         functools.partial(head_kernel, chips, frames),
-        [packed, other_saved, kept, received, gate_a] + pieces,
-        [shape(f32, rows, HD), shape(f32, rows + count, HD)],
+        [packed, kept, received, gate_a] + pieces,
+        [shape(f32, rows, HD), shape(f32, rows, HD), shape(f32, count, LANES)],
         flops=4 * rows * chips * width * 2 * HD,
     )
     later_bias, _ = lax.optimization_barrier((bias, mine))
@@ -367,44 +420,44 @@
         shape(f32, 2 * n_t, LANES),
         flops=2 * n_t * rows * k_rows * HD,
     )
-    extra = -(-SPLIT * 2 * n_t // 16) * 16
-    joined, terms = call(
-        join_kernel,
-        [mine, other, over_cores(other), stats],
-        [shape(bf16, rows + extra, HD), shape(f32, 2 * count, LANES)],
-    )
-    heads_all = [joined] + [over_time(joined, k) for k in range(1, n_t)]
-    terms_all = over_chips(terms)
-    moved, _ = lax.optimization_barrier((moved, terms_all))
-    row_pieces = over_chips(moved)
+    heads = call(
+        functools.partial(join_kernel, n_t, chips, starts),
+        [mine, over_cores(other), stats, terms] + pieces,
+        [shape(bf16, starts[-1], LANES)] * n_t,
+        [pltpu.VMEM((rows, width), f32), pltpu.VMEM((chips, part, width), f32)],
+    )
+    heads_all = time_swaps(heads[::-1])
+    base = tiles * n_t * part
+    bundle = call(
+        functools.partial(bundle_kernel, n_t, starts, count),
+        [gate_b] + heads_all[::-1],
+        shape(bf16, base + n_t * count, LANES),
+    )
+    bundles = over_chips(bundle)
+    later_bias, _ = lax.optimization_barrier((bias, bundle))
     outs = call(
-        functools.partial(grads_kernel, n_t, chips),
-        [bias, keys, values] + terms_all + packed_all + heads_all,
-        [shape(bf16, k_rows, HD)] * 2 + [shape(bf16, rows + 2 * count, LANES)] * n_t,
-        [pltpu.VMEM((k_rows, HD), f32)] * 2 + [pltpu.VMEM((chips, 2 * count, LANES), f32)],
+        functools.partial(grads_kernel, n_t),
+        [later_bias, keys, values] + packed_all + heads_all[::-1],
+        [shape(bf16, k_rows, HD)] * 2 + [shape(bf16, HD, rows)] * n_t,
+        [pltpu.VMEM((k_rows, HD), f32)] * 2,
         flops=10 * n_t * rows * k_rows * HD,
     )
-    key_grad, value_grad, parts = outs[0], outs[1], outs[2:]
-    parts = [parts[0]] + [over_time(parts[k], k) for k in range(1, n_t)]
-    row_pieces, _ = lax.optimization_barrier((row_pieces, parts))
-
-    gated = call(
-        functools.partial(gated_kernel, n_t, frames),
-        [gate_b] + row_pieces,
-        shape(bf16, n_t, rows, width),
-    )
-    weight_grad = call(
-        functools.partial(weight_kernel, n_t),
-        [gated, over_cores(gated)] + packed_all,
-        shape(f32, HD, 2 * width),
-        [pltpu.VMEM((n_t, rows, HD), bf16)],
+    key_grad, value_grad = outs[:2]
+    parts = time_swaps(outs[2:][::-1])
+    bundles, _ = lax.optimization_barrier((bundles, parts[::-1]))
+    collected = call(
+        functools.partial(collect_kernel, chips, base),
+        bundles,
+        shape(bf16, chips * base + 2 * n_t * count, LANES),
+        [pltpu.VMEM((chips, n_t * count, LANES), f32)],
+    )
+    query_grad = call(functools.partial(query_kernel, n_t), parts[::-1], shape(bf16, rows, HD))
+    weight_grad, gate_grad = call(
+        functools.partial(final_kernel, n_t, chips, frames),
+        [hot, collected, over_cores(collected)] + packed_all,
+        [shape(f32, HD, 2 * width), shape(f32, levels, n_s * width)],
+        [pltpu.VMEM((n_t, rows, HD), f32), pltpu.VMEM((2, n_t, count, LANES), f32)],
         flops=4 * n_t * rows * width * HD,
-    )
-    query_grad, gate_grad = call(
-        functools.partial(finish_kernel, n_t, chips, frames),
-        [hot] + parts,
-        [shape(bf16, rows, HD), shape(f32, levels, n_s * width)],
-        [pltpu.VMEM((n_t, 2 * count, LANES), f32)],
     )
     if width != shard:
         weight_grad = without_padding(weight_grad, 2, shard)

time: 53.9 us -> 49.6 us (0.920)
  starting transfers between devices: 33.1 us -> 22.1 us
  waiting for transfers between devices: 11 us -> 17.1 us
  local copies, waits for them, and re-layouts: 0.04 us -> 0.84 us
    ppermute x9 -> x6, starting transfers between devices: 15 us -> 7.72 us  [over_chips(): lax.ppermute(x, 'space', [(s, s ^ 2 * k) for s in range(n_s)])]
    ppermute x9, waiting for transfers between devices: 8.12 us -> 15 us  [over_time(): return lax.ppermute(x, 'tm', [(t, t ^ k) for t in range(n_t)])]
    ppermute x9, starting transfers between devices: 16.9 us -> 13.7 us  [over_time(): return lax.ppermute(x, 'tm', [(t, t ^ k) for t in range(n_t)])]
    ppermute x4 -> x3, waiting for transfers between devices: 2.84 us -> 1.48 us  [over_cores(): return lax.ppermute(x, 'space', [(s, s ^ 1) for s in range(n_s)])]
    unnamed x16, local copies, waits for them, and re-layouts: 0.04 us -> 0.84 us
    ppermute x1 -> x0, starting transfers between devices: 0.66 us -> none  [body(): moved = lax.ppermute(to_move, ('tm', 'space'), moves)]
    ppermute x9 -> x6, waiting for transfers between devices: 0.02 us -> 0.59 us  [over_chips(): lax.ppermute(x, 'space', [(s, s ^ 2 * k) for s in range(n_s)])]
    pallas_call x9 -> x10, Pallas kernels: 8.71 us -> 8.69 us  [call(): pl.pallas_call(kernel, out_shape=out_shape, in_specs=[pl.BlockSpec(memory...]
  transfers between devices with their start and end apart: 23 -> 18, of which waited for: 7 -> 9; matrix products, arithmetic and copies ran while one was open for 0% -> 0% of each run, Pallas kernels for 10% -> 11%
where the time goes in v5:
time: 49.6 us; the launch traced here: 49.4 us
  starting transfers between devices  22.1 us (45%)
  waiting for transfers between devices  17.1 us (34%)
  Pallas kernels  8.69 us (18%)
  local copies, waits for them, and re-layouts  0.84 us (2%)
  between operations  0.78 us (2%)
    ppermute x9, waiting for transfers between devices, over_time(): return lax.ppermute(x, 'tm', [(t, t ^ k) for t in range(n_t)])  15 us
    ppermute x9, starting transfers between devices, over_time(): return lax.ppermute(x, 'tm', [(t, t ^ k) for t in range(n_t)])  13.7 us
    pallas_call x10, Pallas kernels, call(): pl.pallas_call(kernel, out_shape=out_shape, in_specs=[pl.BlockSpec(memory...  8.69 us
    ppermute x6, starting transfers between devices, over_chips(): lax.ppermute(x, 'space', [(s, s ^ 2 * k) for s in range(n_s)])  7.72 us
    ppermute x3, waiting for transfers between devices, over_cores(): return lax.ppermute(x, 'space', [(s, s ^ 1) for s in range(n_s)])  1.48 us
  transfers between devices with their start and end apart: 18, of which 9 were waited for; matrix products, arithmetic and copies ran while one was open for 0% of the time, Pallas kernels for 11%

profile of v5, /device:TPU:0, one launch (start us, length us, event | category | flops | bytes accessed | tf_op | source)
XLA Modules:
  0.0 49.4 jit_solution(17048294554841038222)
XLA Ops:
  0.7 0.8 %copy-done.3 = bf16[128,128]{1,0:T(8,128)(2,1)S(1)} copy-done((bf16[128,128]{1,0:T(8,128)(2,1)S(1)}, bf16[128,128]{1,0:T(8,128)(2,1)}, u32[]{:S(2)}) %copy-start.3) | copy-done | bytes 32792
  1.5 1.5 %shard_map.128 = (bf16[4,128,640]{2,1,0:T(8,128)(2,1)S(1)}, bf16[128,2688]{1,0:T(8,128)(2,1)S(1)}) custom-call(bf16[128,5120]{1,0:T(8,128)(2,1)} %weight_in.1, bf16[128,128]{1,0:T(8,128)(2,1)S(1)} %copy-done.3), custom_call_target="tpu_custom_call" | custom-call | bytes 1343488 | tf_op jit(solution)/shard_map/pallas_call | solution.py:321
  3.5 3.5 %collective-permute-start.3 = (bf16[128,640]{1,0:T(8,128)(2,1)S(1)}, bf16[128,640]{1,0:T(8,128)(2,1)S(1)}, u32[]{:S(2)}, u32[]{:S(2)}) collective-permute-start(bf16[128,640]{1,0:T(8,128)(2,1)S(1)} %copy-done), channel_id=1, source_target_pairs={{0,6},{1,7},{2,4},{3,5},{4,2},{5,3},{6,0},{7,1},{8,14},{9,15},{10,... | collective-permute-start | bytes 491528 | tf_op jit(solution)/shard_map/ppermute | solution.py:366
  7.7 2.0 %collective-permute-start.5 = (bf16[2,128,128]{2,1,0:T(8,128)(2,1)S(1)}, bf16[2,128,128]{2,1,0:T(8,128)(2,1)S(1)}, u32[]{:S(2)}, u32[]{:S(2)}) collective-permute-start(bf16[2,128,128]{2,1,0:T(8,128)(2,1)S(1)} %pad_maximum_fusion.packed.refs_0_), channel_id=1, source_target_pairs={{0,8},{8,0},{16,24},{24,16},{1,9},{9,1},{17,25},{25,17},{2,10},{10... | collective-permute-start | bytes 196616 | tf_op jit(solution)/shard_map/ppermute | solution.py:373
  9.8 2.6 %collective-permute-start.6 = (bf16[2,128,128]{2,1,0:T(8,128)(2,1)S(1)}, bf16[2,128,128]{2,1,0:T(8,128)(2,1)S(1)}, u32[]{:S(2)}, u32[]{:S(2)}) collective-permute-start(bf16[2,128,128]{2,1,0:T(8,128)(2,1)S(1)} %pad_maximum_fusion.packed.refs_0_), channel_id=1, source_target_pairs={{0,16},{8,24},{16,0},{24,8},{1,17},{9,25},{17,1},{25,9},{2,18},{10... | collective-permute-start | bytes 196616 | tf_op jit(solution)/shard_map/ppermute | solution.py:373
  12.4 0.6 %shard_map.129 = (f32[2,512]{1,0:T(2,128)S(1)}, f32[4,2,640]{2,1,0:T(2,128)S(1)}, f32[4,1,640]{2,1,0:T(1,128)S(1)}, f32[8,16,128]{2,1,0:T(8,128)S(1)}) custom-call(s32[8]{0:T(128)S(1)} %copy-done.4, s32[4]{0:T(128)S(1)} %copy-done.5, f32[16,5120]{1,0:T(8,128)S(1)} %copy-done.1), custom_call_target="tpu_custom_call" | custom-call | bytes 327728 | tf_op jit(solution)/shard_map/pallas_call | solution.py:321
  13.0 2.0 %collective-permute-start.7 = (bf16[2,128,128]{2,1,0:T(8,128)(2,1)S(1)}, bf16[2,128,128]{2,1,0:T(8,128)(2,1)S(1)}, u32[]{:S(2)}, u32[]{:S(2)}) collective-permute-start(bf16[2,128,128]{2,1,0:T(8,128)(2,1)S(1)} %collective-permute-done.5.refs_1_), channel_id=1, source_target_pairs={{0,16},{8,24},{16,0},{24,8},{1,17},{9,25},{17,1},{25,9},{2,18},{10... | collective-permute-start | bytes 196616 | tf_op jit(solution)/shard_map/ppermute | solution.py:373
  15.7 0.8 %shard_map.130 = (f32[128,128]{1,0:T(8,128)S(1)}, f32[128,128]{1,0:T(8,128)S(1)}, f32[40,128]{1,0:T(8,128)S(1)}) custom-call(bf16[2,128,128]{2,1,0:T(8,128)(2,1)S(1)} %pad_maximum_fusion.packed.refs_0_, bf16[4,128,640]{2,1,0:T(8,128)(2,1)S(1)} %get-tuple-element.39.kept, bf16[128,2688]{1,0:T(8,128)(2,1)S(1)} %collective-permute-done.received, ...), custom_call_target="tpu_custom_call" | custom-call | flops 335544320 | bytes 2084864 | tf_op jit(solution)/shard_map/pallas_call | solution.py:321
  16.5 2.4 %collective-permute-done.7.refs_3_ = bf16[2,128,128]{2,1,0:T(8,128)(2,1)S(1)} collective-permute-done((bf16[2,128,128]{2,1,0:T(8,128)(2,1)S(1)}, bf16[2,128,128]{2,1,0:T(8,128)(2,1)S(1)}, u32[]{:S(2)}, u32[]{:S(2)}) %collective-permute-start.7) | collective-permute-done | bytes 65568 | tf_op jit(solution)/shard_map/ppermute | solution.py:373
  19.0 0.8 %shard_map.131.stats = f32[8,128]{1,0:T(8,128)S(1)} custom-call(f32[2,512]{1,0:T(2,128)S(1)} %get-tuple-element.49.bias, bf16[1024,128]{1,0:T(8,128)(2,1)S(1)} %copy-done.2, bf16[2,128,128]{2,1,0:T(8,128)(2,1)S(1)} %pad_maximum_fusion.packed.refs_0_, bf16[2,128,128]{2,1,0:T(8,128)(2,1)S(1)} %collective-permute-done.5.refs_1_, ...), custom_call_target="tpu_custom_call" | custom-call | flops 134217728 | bytes 528384 | tf_op jit(solution)/shard_map/pallas_call | solution.py:321
  19.9 2.9 %collective-permute-start.8 = (bf16[368,128]{1,0:T(8,128)(2,1)S(1)}, bf16[368,128]{1,0:T(8,128)(2,1)S(1)}, u32[]{:S(2)}, u32[]{:S(2)}) collective-permute-start(bf16[368,128]{1,0:T(8,128)(2,1)S(1)} %get-tuple-element.45), channel_id=1, source_target_pairs={{0,24},{8,16},{16,8},{24,0},{1,25},{9,17},{17,9},{25,1},{2,26},{10... | collective-permute-start | bytes 282632 | tf_op jit(solution)/shard_map/ppermute | solution.py:373
  22.8 1.5 %collective-permute-start.10 = (bf16[368,128]{1,0:T(8,128)(2,1)S(1)}, bf16[368,128]{1,0:T(8,128)(2,1)S(1)}, u32[]{:S(2)}, u32[]{:S(2)}) collective-permute-start(bf16[368,128]{1,0:T(8,128)(2,1)S(1)} %get-tuple-element.47), channel_id=1, source_target_pairs={{0,8},{8,0},{16,24},{24,16},{1,9},{9,1},{17,25},{25,17},{2,10},{10... | collective-permute-start | bytes 282632 | tf_op jit(solution)/shard_map/ppermute | solution.py:373
  24.3 2.2 %collective-permute-done.8.refs_0_.refs_4_ = bf16[368,128]{1,0:T(8,128)(2,1)S(1)} collective-permute-done((bf16[368,128]{1,0:T(8,128)(2,1)S(1)}, bf16[368,128]{1,0:T(8,128)(2,1)S(1)}, u32[]{:S(2)}, u32[]{:S(2)}) %collective-permute-start.8) | collective-permute-done | bytes 94240 | tf_op jit(solution)/shard_map/ppermute | solution.py:373
  26.5 3.3 %collective-permute-done.9.refs_1_.refs_5_ = bf16[368,128]{1,0:T(8,128)(2,1)S(1)} collective-permute-done((bf16[368,128]{1,0:T(8,128)(2,1)S(1)}, bf16[368,128]{1,0:T(8,128)(2,1)S(1)}, u32[]{:S(2)}, u32[]{:S(2)}) %collective-permute-start.9) | collective-permute-done | bytes 94240 | tf_op jit(solution)/shard_map/ppermute | solution.py:373
  29.9 2.3 %collective-permute-start.16 = (bf16[800,128]{1,0:T(8,128)(2,1)S(1)}, bf16[800,128]{1,0:T(8,128)(2,1)S(1)}, u32[]{:S(2)}, u32[]{:S(2)}) collective-permute-start(bf16[800,128]{1,0:T(8,128)(2,1)S(1)} %shard_map.133.refs_0_), channel_id=1, source_target_pairs={{0,6},{1,7},{2,4},{3,5},{4,2},{5,3},{6,0},{7,1},{8,14},{9,15},{10,... | collective-permute-start | bytes 614408 | tf_op jit(solution)/shard_map/ppermute | solution.py:366
  32.2 0.7 %collective-permute-start.15 = (bf16[800,128]{1,0:T(8,128)(2,1)S(1)}, bf16[800,128]{1,0:T(8,128)(2,1)S(1)}, u32[]{:S(2)}, u32[]{:S(2)}) collective-permute-start(bf16[800,128]{1,0:T(8,128)(2,1)S(1)} %shard_map.133.refs_0_), channel_id=1, source_target_pairs={{0,4},{1,5},{2,6},{3,7},{4,0},{5,1},{6,2},{7,3},{8,12},{9,13},{10,... | collective-permute-start | bytes 614408 | tf_op jit(solution)/shard_map/ppermute | solution.py:366
  33.4 2.4 %shard_map.134 = (bf16[1024,128]{1,0:T(8,128)(2,1)}, bf16[1024,128]{1,0:T(8,128)(2,1)}, bf16[128,128]{1,0:T(8,128)(2,1)S(1)}, bf16[128,128]{1,0:T(8,128)(2,1)S(1...) custom-call(f32[2,512]{1,0:T(2,128)S(1)} %get-tuple-element.49.bias, bf16[1024,128]{1,0:T(8,128)(2,1)S(1)} %copy-done.2, ...), custom_call_target="tpu_custom_call" | custom-call | flops 671088640 | bytes 1167360 | tf_op jit(solution)/shard_map/pallas_call | solution.py:321
  35.8 2.6 %collective-permute-start.11 = (bf16[128,128]{1,0:T(8,128)(2,1)S(1)}, bf16[128,128]{1,0:T(8,128)(2,1)S(1)}, u32[]{:S(2)}, u32[]{:S(2)}) collective-permute-start(bf16[128,128]{1,0:T(8,128)(2,1)S(1)} %get-tuple-element.50), channel_id=1, source_target_pairs={{0,24},{8,16},{16,8},{24,0},{1,25},{9,17},{17,9},{25,1},{2,26},{10... | collective-permute-start | bytes 98312 | tf_op jit(solution)/shard_map/ppermute | solution.py:373
  38.4 3.2 %collective-permute-done.11.refs_0_ = bf16[128,128]{1,0:T(8,128)(2,1)S(1)} collective-permute-done((bf16[128,128]{1,0:T(8,128)(2,1)S(1)}, bf16[128,128]{1,0:T(8,128)(2,1)S(1)}, u32[]{:S(2)}, u32[]{:S(2)}) %collective-permute-start.11) | collective-permute-done | bytes 32800 | tf_op jit(solution)/shard_map/ppermute | solution.py:373
  41.6 1.7 %collective-permute-done.12.refs_1_ = bf16[128,128]{1,0:T(8,128)(2,1)S(1)} collective-permute-done((bf16[128,128]{1,0:T(8,128)(2,1)S(1)}, bf16[128,128]{1,0:T(8,128)(2,1)S(1)}, u32[]{:S(2)}, u32[]{:S(2)}) %collective-permute-start.12) | collective-permute-done | bytes 32800 | tf_op jit(solution)/shard_map/ppermute | solution.py:373
  43.2 2.3 %collective-permute-done.13.refs_2_ = bf16[128,128]{1,0:T(8,128)(2,1)S(1)} collective-permute-done((bf16[128,128]{1,0:T(8,128)(2,1)S(1)}, bf16[128,128]{1,0:T(8,128)(2,1)S(1)}, u32[]{:S(2)}, u32[]{:S(2)}) %collective-permute-start.13) | collective-permute-done | bytes 32800 | tf_op jit(solution)/shard_map/ppermute | solution.py:373
  45.7 0.7 %shard_map.135 = bf16[128,128]{1,0:T(8,128)(2,1)} custom-call(bf16[128,128]{1,0:T(8,128)(2,1)S(1)} %collective-permute-done.11.refs_0_, bf16[128,128]{1,0:T(8,128)(2,1)S(1)} %collective-permute-done.12.refs_1_, bf16[128,128]{1,0:T(8,128)(2,1)S(1)} %collective-permute-done.13.refs_2_, bf16[128,128]{1,0:T(8,128)(2,1)S(1)} %get-tuple-element.53.refs_3_), custom_call_target="tpu_custom_call" | custom-call | bytes 131072 | tf_op jit(solution)/shard_map/pallas_call | solution.py:321
  46.4 1.5 %collective-permute-done.17.other = bf16[2880,128]{1,0:T(8,128)(2,1)S(1)} collective-permute-done((bf16[2880,128]{1,0:T(8,128)(2,1)S(1)}, bf16[2880,128]{1,0:T(8,128)(2,1)S(1)}, u32[]{:S(2)}, u32[]{:S(2)}) %collective-permute-start.17) | collective-permute-done | bytes 737312 | tf_op jit(solution)/shard_map/ppermute | solution.py:370
  47.9 1.6 %shard_map.137 = (f32[128,1280]{1,0:T(8,128)}, f32[16,5120]{1,0:T(8,128)}) custom-call(f32[8,16,128]{2,1,0:T(8,128)S(1)} %get-tuple-element.56.hot, bf16[2880,128]{1,0:T(8,128)(2,1)S(1)} %shard_map.136.own, bf16[2880,128]{1,0:T(8,128)(2,1)S(1)} %collective-permute-done.17.other, bf16[2,128,128]{2,1,0:T(8,128)(2,1)S(1)} %pad_maximum_fusion.packed.refs_0_, ...), custom_call_target="tpu_custom_call" | custom-call | flops 167772160 | bytes 1802240 | tf_op jit(solution)/shard_map/pallas_call | solution.py:321
  (39 shorter events, 2.8 us)
Async XLA Ops:
  0.6 11.7 %copy-start.1 = (f32[16,5120]{1,0:T(8,128)S(1)}, f32[16,5120]{1,0:T(8,128)}, u32[]{:S(2)}) copy-start(f32[16,5120]{1,0:T(8,128)} %gate) | copy-start | bytes 983044
  1.5 6.2 %copy-start.7 = (bf16[128,128]{1,0:T(8,128)(2,1)S(1)}, bf16[128,128]{1,0:T(8,128)(2,1)}, u32[]{:S(2)}) copy-start(bf16[128,128]{1,0:T(8,128)(2,1)} %param.9) | copy-start | bytes 98308
  1.5 10.9 %copy-start.4 = (s32[8]{0:T(128)S(1)}, s32[8]{0:T(128)}, u32[]{:S(2)}) copy-start(s32[8]{0:T(128)} %levels.1) | copy-start | bytes 100
  1.5 10.9 %copy-start.5 = (s32[4]{0:T(128)S(1)}, s32[4]{0:T(128)}, u32[]{:S(2)}) copy-start(s32[4]{0:T(128)} %clips.1) | copy-start | bytes 52
  3.0 16.0 %copy-start.2 = (bf16[1024,128]{1,0:T(8,128)(2,1)S(1)}, bf16[1024,128]{1,0:T(8,128)(2,1)}, u32[]{:S(2)}) copy-start(bf16[1024,128]{1,0:T(8,128)(2,1)} %keys.3) | copy-start | bytes 786436
  3.0 4.7 %collective-permute-start = (bf16[128,2688]{1,0:T(8,128)(2,1)S(1)}, bf16[128,2688]{1,0:T(8,128)(2,1)S(1)}, u32[]{:S(2)}, u32[]{:S(2)}) collective-permute-start(bf16[128,2688]{1,0:T(8,128)(2,1)S(1)} %get-tuple-element.34), channel_id=1, source_target_pairs={{0,1},{1,0},{2,3},{3,2},{4,5},{5,4},{6,7},{7,6},{8,9},{9,8},{10,11... | collective-permute-start | bytes 2064392 | tf_op jit(solution)/shard_map/ppermute | solution.py:370
  3.5 11.6 %collective-permute-start.3 = (bf16[128,640]{1,0:T(8,128)(2,1)S(1)}, bf16[128,640]{1,0:T(8,128)(2,1)S(1)}, u32[]{:S(2)}, u32[]{:S(2)}) collective-permute-start(bf16[128,640]{1,0:T(8,128)(2,1)S(1)} %copy-done), channel_id=1, source_target_pairs={{0,6},{1,7},{2,4},{3,5},{4,2},{5,3},{6,0},{7,1},{8,14},{9,15},{10,... | collective-permute-start | bytes 491528 | tf_op jit(solution)/shard_map/ppermute | solution.py:366
  7.1 8.3 %collective-permute-start.2 = (bf16[128,640]{1,0:T(8,128)(2,1)S(1)}, bf16[128,640]{1,0:T(8,128)(2,1)S(1)}, u32[]{:S(2)}, u32[]{:S(2)}) collective-permute-start(bf16[128,640]{1,0:T(8,128)(2,1)S(1)} %copy-done), channel_id=1, source_target_pairs={{0,4},{1,5},{2,6},{3,7},{4,0},{5,1},{6,2},{7,3},{8,12},{9,13},{10,... | collective-permute-start | bytes 491528 | tf_op jit(solution)/shard_map/ppermute | solution.py:366
  7.6 8.1 %collective-permute-start.1 = (bf16[128,640]{1,0:T(8,128)(2,1)S(1)}, bf16[128,640]{1,0:T(8,128)(2,1)S(1)}, u32[]{:S(2)}, u32[]{:S(2)}) collective-permute-start(bf16[128,640]{1,0:T(8,128)(2,1)S(1)} %copy-done), channel_id=1, source_target_pairs={{0,2},{1,3},{2,0},{3,1},{4,6},{5,7},{6,4},{7,5},{8,10},{9,11},{10,... | collective-permute-start | bytes 491528 | tf_op jit(solution)/shard_map/ppermute | solution.py:366
  7.7 5.3 %collective-permute-start.5 = (bf16[2,128,128]{2,1,0:T(8,128)(2,1)S(1)}, bf16[2,128,128]{2,1,0:T(8,128)(2,1)S(1)}, u32[]{:S(2)}, u32[]{:S(2)}) collective-permute-start(bf16[2,128,128]{2,1,0:T(8,128)(2,1)S(1)} %pad_maximum_fusion.packed.refs_0_), channel_id=1, source_target_pairs={{0,8},{8,0},{16,24},{24,16},{1,9},{9,1},{17,25},{25,17},{2,10},{10... | collective-permute-start | bytes 196616 | tf_op jit(solution)/shard_map/ppermute | solution.py:373
  9.8 6.8 %collective-permute-start.6 = (bf16[2,128,128]{2,1,0:T(8,128)(2,1)S(1)}, bf16[2,128,128]{2,1,0:T(8,128)(2,1)S(1)}, u32[]{:S(2)}, u32[]{:S(2)}) collective-permute-start(bf16[2,128,128]{2,1,0:T(8,128)(2,1)S(1)} %pad_maximum_fusion.packed.refs_0_), channel_id=1, source_target_pairs={{0,16},{8,24},{16,0},{24,8},{1,17},{9,25},{17,1},{25,9},{2,18},{10... | collective-permute-start | bytes 196616 | tf_op jit(solution)/shard_map/ppermute | solution.py:373
  13.0 5.9 %collective-permute-start.7 = (bf16[2,128,128]{2,1,0:T(8,128)(2,1)S(1)}, bf16[2,128,128]{2,1,0:T(8,128)(2,1)S(1)}, u32[]{:S(2)}, u32[]{:S(2)}) collective-permute-start(bf16[2,128,128]{2,1,0:T(8,128)(2,1)S(1)} %collective-permute-done.5.refs_1_), channel_id=1, source_target_pairs={{0,16},{8,24},{16,0},{24,8},{1,17},{9,25},{17,1},{25,9},{2,18},{10... | collective-permute-start | bytes 196616 | tf_op jit(solution)/shard_map/ppermute | solution.py:373
  16.4 17.0 %copy-start.6 = (bf16[1024,128]{1,0:T(8,128)(2,1)S(1)}, bf16[1024,128]{1,0:T(8,128)(2,1)}, u32[]{:S(2)}) copy-start(bf16[1024,128]{1,0:T(8,128)(2,1)} %values.1) | copy-start | bytes 786436
  16.4 3.3 %collective-permute-start.4 = (f32[128,128]{1,0:T(8,128)S(1)}, f32[128,128]{1,0:T(8,128)S(1)}, u32[]{:S(2)}, u32[]{:S(2)}) collective-permute-start(f32[128,128]{1,0:T(8,128)S(1)} %get-tuple-element.42), channel_id=1, source_target_pairs={{0,1},{1,0},{2,3},{3,2},{4,5},{5,4},{6,7},{7,6},{8,9},{9,8},{10,11... | collective-permute-start | bytes 196616 | tf_op jit(solution)/shard_map/ppermute | solution.py:370
  19.9 6.7 %collective-permute-start.8 = (bf16[368,128]{1,0:T(8,128)(2,1)S(1)}, bf16[368,128]{1,0:T(8,128)(2,1)S(1)}, u32[]{:S(2)}, u32[]{:S(2)}) collective-permute-start(bf16[368,128]{1,0:T(8,128)(2,1)S(1)} %get-tuple-element.45), channel_id=1, source_target_pairs={{0,24},{8,16},{16,8},{24,0},{1,25},{9,17},{17,9},{25,1},{2,26},{10... | collective-permute-start | bytes 282632 | tf_op jit(solution)/shard_map/ppermute | solution.py:373
  22.8 7.0 %collective-permute-start.9 = (bf16[368,128]{1,0:T(8,128)(2,1)S(1)}, bf16[368,128]{1,0:T(8,128)(2,1)S(1)}, u32[]{:S(2)}, u32[]{:S(2)}) collective-permute-start(bf16[368,128]{1,0:T(8,128)(2,1)S(1)} %get-tuple-element.46), channel_id=1, source_target_pairs={{0,16},{8,24},{16,0},{24,8},{1,17},{9,25},{17,1},{25,9},{2,18},{10... | collective-permute-start | bytes 282632 | tf_op jit(solution)/shard_map/ppermute | solution.py:373
  22.8 7.0 %collective-permute-start.10 = (bf16[368,128]{1,0:T(8,128)(2,1)S(1)}, bf16[368,128]{1,0:T(8,128)(2,1)S(1)}, u32[]{:S(2)}, u32[]{:S(2)}) collective-permute-start(bf16[368,128]{1,0:T(8,128)(2,1)S(1)} %get-tuple-element.47), channel_id=1, source_target_pairs={{0,8},{8,0},{16,24},{24,16},{1,9},{9,1},{17,25},{25,17},{2,10},{10... | collective-permute-start | bytes 282632 | tf_op jit(solution)/shard_map/ppermute | solution.py:373
  29.9 15.6 %collective-permute-start.16 = (bf16[800,128]{1,0:T(8,128)(2,1)S(1)}, bf16[800,128]{1,0:T(8,128)(2,1)S(1)}, u32[]{:S(2)}, u32[]{:S(2)}) collective-permute-start(bf16[800,128]{1,0:T(8,128)(2,1)S(1)} %shard_map.133.refs_0_), channel_id=1, source_target_pairs={{0,6},{1,7},{2,4},{3,5},{4,2},{5,3},{6,0},{7,1},{8,14},{9,15},{10,... | collective-permute-start | bytes 614408 | tf_op jit(solution)/shard_map/ppermute | solution.py:366
  32.2 13.3 %collective-permute-start.15 = (bf16[800,128]{1,0:T(8,128)(2,1)S(1)}, bf16[800,128]{1,0:T(8,128)(2,1)S(1)}, u32[]{:S(2)}, u32[]{:S(2)}) collective-permute-start(bf16[800,128]{1,0:T(8,128)(2,1)S(1)} %shard_map.133.refs_0_), channel_id=1, source_target_pairs={{0,4},{1,5},{2,6},{3,7},{4,0},{5,1},{6,2},{7,3},{8,12},{9,13},{10,... | collective-permute-start | bytes 614408 | tf_op jit(solution)/shard_map/ppermute | solution.py:366
  32.9 12.6 %collective-permute-start.14 = (bf16[800,128]{1,0:T(8,128)(2,1)S(1)}, bf16[800,128]{1,0:T(8,128)(2,1)S(1)}, u32[]{:S(2)}, u32[]{:S(2)}) collective-permute-start(bf16[800,128]{1,0:T(8,128)(2,1)S(1)} %shard_map.133.refs_0_), channel_id=1, source_target_pairs={{0,2},{1,3},{2,0},{3,1},{4,6},{5,7},{6,4},{7,5},{8,10},{9,11},{10,... | collective-permute-start | bytes 614408 | tf_op jit(solution)/shard_map/ppermute | solution.py:366
  35.8 5.7 %collective-permute-start.11 = (bf16[128,128]{1,0:T(8,128)(2,1)S(1)}, bf16[128,128]{1,0:T(8,128)(2,1)S(1)}, u32[]{:S(2)}, u32[]{:S(2)}) collective-permute-start(bf16[128,128]{1,0:T(8,128)(2,1)S(1)} %get-tuple-element.50), channel_id=1, source_target_pairs={{0,24},{8,16},{16,8},{24,0},{1,25},{9,17},{17,9},{25,1},{2,26},{10... | collective-permute-start | bytes 98312 | tf_op jit(solution)/shard_map/ppermute | solution.py:373
  38.4 4.8 %collective-permute-start.12 = (bf16[128,128]{1,0:T(8,128)(2,1)S(1)}, bf16[128,128]{1,0:T(8,128)(2,1)S(1)}, u32[]{:S(2)}, u32[]{:S(2)}) collective-permute-start(bf16[128,128]{1,0:T(8,128)(2,1)S(1)} %get-tuple-element.51), channel_id=1, source_target_pairs={{0,16},{8,24},{16,0},{24,8},{1,17},{9,25},{17,1},{25,9},{2,18},{10... | collective-permute-start | bytes 98312 | tf_op jit(solution)/shard_map/ppermute | solution.py:373
  41.6 3.9 %collective-permute-start.13 = (bf16[128,128]{1,0:T(8,128)(2,1)S(1)}, bf16[128,128]{1,0:T(8,128)(2,1)S(1)}, u32[]{:S(2)}, u32[]{:S(2)}) collective-permute-start(bf16[128,128]{1,0:T(8,128)(2,1)S(1)} %get-tuple-element.52), channel_id=1, source_target_pairs={{0,8},{8,0},{16,24},{24,16},{1,9},{9,1},{17,25},{25,17},{2,10},{10... | collective-permute-start | bytes 98312 | tf_op jit(solution)/shard_map/ppermute | solution.py:373
  45.6 2.3 %collective-permute-start.17 = (bf16[2880,128]{1,0:T(8,128)(2,1)S(1)}, bf16[2880,128]{1,0:T(8,128)(2,1)S(1)}, u32[]{:S(2)}, u32[]{:S(2)}) collective-permute-start(bf16[2880,128]{1,0:T(8,128)(2,1)S(1)} %shard_map.136.own), channel_id=1, source_target_pairs={{0,1},{1,0},{2,3},{3,2},{4,5},{5,4},{6,7},{7,6},{8,9},{9,8},{10,11... | collective-permute-start | bytes 2211848 | tf_op jit(solution)/shard_map/ppermute | solution.py:370
  (2 other events, 3.7 us)

commit v6 on v4

--- a/solution.py
+++ b/solution.py
@@ -25,6 +25,11 @@
     )
 
 
+def piece(refs, k):
+    each = refs[0].shape[0]
+    return refs[k // each][k % each]
+
+
 def place():
     s = lax.axis_index("space")
     return lax.axis_index("tm"), s // 2, s % 2
@@ -39,16 +44,15 @@
     return lambda frame: sum((frame >= bound).astype(jnp.int32) for bound in bounds)
 
 
-def cut_kernel(chips, weight_in, kept, sent, sems):
+def cut_kernel(chips, weight_in, saved_in, kept, sent, sems):
     _, chip, core = place()
     width = kept.shape[2]
-    copies = []
+    moves = [(saved_in, sent.at[:, chips * width : chips * width + HD])]
     for k in range(chips):
-        for c, out in ((1 - core, sent), (core, kept)):
+        for c, out in ((1 - core, sent.at[:, k * width : (k + 1) * width]), (core, kept.at[k])):
             columns = pl.ds(pl.multiple_of((2 * (chip ^ k) + c) * width, LANES), width)
-            copies.append(
-                pltpu.make_async_copy(weight_in.at[:, columns], out.at[k], sems.at[len(copies)])
-            )
+            moves.append((weight_in.at[:, columns], out))
+    copies = [pltpu.make_async_copy(a, b, sems.at[i]) for i, (a, b) in enumerate(moves)]
     for copy in copies:
         copy.start()
     for copy in copies:
@@ -79,17 +83,17 @@
         for k in range(chips):
             columns = pl.ds(pl.multiple_of((2 * (chip ^ k) + core) * width, LANES), width)
             gate_a[k, r : r + 1, :] = gate[pl.ds(level, 1), columns]
-        for k in range(n_t):
-            level = levels[(t ^ chip ^ k) * frames + r]
-            mine = pl.ds(pl.multiple_of((2 * t + core) * width, LANES), width)
-            gate_b[k, r : r + 1, :] = gate[pl.ds(level, 1), mine]
+    mine = pl.ds(pl.multiple_of((2 * t + core) * width, LANES), width)
+    for r in range(frames):
+        level = levels[(t ^ chip) * frames + r]
+        gate_b[r : r + 1, :] = gate[pl.ds(level, 1), mine]
 
 
 def stats_kernel(n_t, bias, keys, *refs):
-    packed, out = refs[:n_t], refs[n_t]
-    rows = packed[0].shape[1]
+    packed, out = refs[:-1], refs[-1]
+    rows = packed[0].shape[2]
     for p in range(0, n_t, 2):
-        q = jnp.concatenate([packed[p][0], packed[p + 1][0]], axis=0)
+        q = jnp.concatenate([piece(packed, p)[0], piece(packed, p + 1)[0]], axis=0)
         scores = []
         for kf in range(bias.shape[0]):
             mask = bias[kf : kf + 1, p * rows : (p + 2) * rows]
@@ -101,15 +105,15 @@
             out[n_t + p + i : n_t + p + i + 1, :] = total[:, i * rows : (i + 1) * rows]
 
 
-def head_kernel(chips, frames, packed, other_saved, kept, received, gate_a, *refs):
+def head_kernel(chips, frames, packed, kept, received, gate_a, *refs):
     pieces, (mine, other) = refs[:chips], refs[chips:]
     _, chip, _ = place()
-    rows = mine.shape[0]
-    tiles = pieces[0].shape[1] // LANES
-    saved = jnp.concatenate([packed[1], other_saved[...]], axis=1)
+    rows, width = pieces[0].shape
+    tiles = width // LANES
+    saved = jnp.concatenate([packed[0, 1], received[:, chips * width : chips * width + HD]], axis=1)
     head = None
     for k in range(chips):
-        weight = jnp.concatenate([kept[k], received[k]], axis=0)
+        weight = jnp.concatenate([kept[k], received[:, k * width : (k + 1) * width]], axis=0)
         wide = pieces[k][...].astype(jnp.float32)
         gated = jnp.concatenate(
             [
@@ -130,51 +134,79 @@
     other[:rows, :] = head[:, HD:]
 
 
-def join_kernel(mine, sent, received, stats, out, terms):
+def rows_of_split(n_t):
+    return -(-SPLIT * 2 * n_t // 16) * 16
+
+
+def split_up(x, count):
+    terms = []
+    for _ in range(count):
+        term = x.astype(jnp.bfloat16).astype(jnp.float32)
+        terms.append(term)
+        x = x - term
+    return jnp.concatenate(terms, axis=0)
+
+
+def padded(x, rows):
+    if x.shape[0] == rows:
+        return x
+    return jnp.concatenate([x, jnp.zeros((rows - x.shape[0], x.shape[1]), x.dtype)], axis=0)
+
+
+def join_kernel(mine, received, stats, out):
+    rows = mine.shape[0]
+    out[0, :rows, :] = (mine[...] + received[:rows, :]).astype(jnp.bfloat16)
+    split = padded(split_up(stats[...], SPLIT), out.shape[1] - rows)
+    out[0, rows:, :] = split.astype(jnp.bfloat16)
+
+
+def bundle_kernel(frames, gate_b, moved, sent, received, out):
     core = place()[2]
-    rows = mine.shape[0]
-    out[:rows, :] = (mine[...] + received[:rows, :]).astype(jnp.bfloat16)
+    rows, width = moved.shape
+    wide = moved[...].astype(jnp.float32)
+    gated = jnp.concatenate(
+        [wide[r * QF : (r + 1) * QF] * gate_b[r : r + 1, :] for r in range(frames)], axis=0
+    ).astype(jnp.bfloat16)
+    base = rows * (width // LANES)
+    for j in range(width // LANES):
+        out[j * rows : (j + 1) * rows, :] = gated[:, j * LANES : (j + 1) * LANES]
     own, other = sent[rows:, :], received[rows:, :]
-    count = own.shape[0]
-    terms[:count, :] = jnp.where(core == 0, own, other)
-    terms[count:, :] = jnp.where(core == 0, other, own)
-    rest = stats[...]
-    parts = []
-    for _ in range(SPLIT):
-        part = rest.astype(jnp.bfloat16).astype(jnp.float32)
-        parts.append(part)
-        rest = rest - part
-    pad = out.shape[0] - rows - SPLIT * rest.shape[0]
-    if pad:
-        parts.append(jnp.zeros((pad, LANES), jnp.float32))
-    out[rows:, :] = jnp.concatenate(parts, axis=0).astype(jnp.bfloat16)
-
-
-def grads_kernel(n_t, chips, bias, keys, values, *refs):
-    terms, refs = refs[:chips], refs[chips:]
-    packed, heads = refs[:n_t], refs[n_t : 2 * n_t]
-    key_out, value_out = refs[2 * n_t : 2 * n_t + 2]
-    outs = refs[2 * n_t + 2 : 3 * n_t + 2]
-    key_acc, value_acc, held = refs[3 * n_t + 2 :]
+    terms = [jnp.where(core == 0, own, other), jnp.where(core == 0, other, own)]
+    out[base:, :] = split_up(jnp.concatenate(terms, axis=0), 2).astype(jnp.bfloat16)
+
+
+def collect_kernel(chips, base, *refs):
+    pieces, (gated, terms_out, held) = refs[:chips], refs[chips:]
     chip = place()[1]
-    rows = packed[0].shape[1]
+    count = held.shape[1]
+    for k in range(chips):
+        gated[k * base : (k + 1) * base, :] = pieces[k][:base, :]
+        terms = pieces[k][base:, :].astype(jnp.float32)
+        held[chip ^ k] = terms[:count] + terms[count:]
+    total = held[0]
+    for k in range(1, chips):
+        total = total + held[k]
+    terms_out[...] = total.astype(jnp.bfloat16)
+
+
+def grads_kernel(n_t, parts, bias, keys, values, terms, *refs):
+    packed, heads = refs[:parts], refs[parts : 2 * parts]
+    key_out, value_out = refs[2 * parts : 2 * parts + 2]
+    outs = refs[2 * parts + 2 : 2 * parts + 2 + n_t][::-1]
+    key_acc, value_acc = refs[2 * parts + 2 + n_t :]
+    rows = packed[0].shape[2]
     ones = jnp.ones((8, HD), jnp.float32)
     keys_t = jnp.transpose(keys[...])
     stats = []
     for k in range(n_t):
-        parts = heads[k][rows:, :].astype(jnp.float32)
-        stats.append(sum(parts[i * 2 * n_t : (i + 1) * 2 * n_t] for i in range(SPLIT)))
-    for k in range(chips):
-        held[chip ^ k] = terms[k][...]
-    total = held[0]
-    for k in range(1, chips):
-        total = total + held[k]
+        split = piece(heads, k)[rows:].astype(jnp.float32)
+        stats.append(sum(split[i * 2 * n_t : (i + 1) * 2 * n_t] for i in range(SPLIT)))
     for k in range(n_t):
-        outs[k][rows:, :] = total.astype(jnp.bfloat16)
+        outs[k][rows:, :] = terms[...]
     for p in range(0, n_t, 2):
-        q = jnp.concatenate([packed[p][0], packed[p + 1][0]], axis=0)
-        o = jnp.concatenate([packed[p][1], packed[p + 1][1]], axis=0)
-        g = jnp.concatenate([heads[p][:rows, :], heads[p + 1][:rows, :]], axis=0)
+        q = jnp.concatenate([piece(packed, p)[0], piece(packed, p + 1)[0]], axis=0)
+        o = jnp.concatenate([piece(packed, p)[1], piece(packed, p + 1)[1]], axis=0)
+        g = jnp.concatenate([piece(heads, p)[:rows], piece(heads, p + 1)[:rows]], axis=0)
         delta = lax.dot_general(
             ones,
             g.astype(jnp.float32) * o.astype(jnp.float32),
@@ -213,7 +245,7 @@
 
 
 def finish_kernel(n_t, chips, frames, hot, *refs):
-    parts, (query_out, gate_out, held) = refs[:n_t], refs[n_t:]
+    parts, (query_out, gate_out, held) = refs[:n_t][::-1], refs[n_t:]
     t = lax.axis_index("tm")
     rows = query_out.shape[0]
     total = parts[0][:rows, :].astype(jnp.float32)
@@ -234,25 +266,29 @@
                 gate_out[:, column : column + LANES] = total
 
 
-def gated_kernel(n_t, frames, gate_b, *refs):
-    pieces, out = refs[:n_t], refs[n_t]
+def weight_kernel(n_t, own, other, *refs):
+    packed, (out, saved) = refs[:-2], refs[-2:]
+    _, chip, core = place()
+    rows = saved.shape[1]
+    width = out.shape[1] // 2
+    tiles = width // LANES
+    base = tiles * rows
     for k in range(n_t):
-        for r in range(frames):
-            span = slice(r * QF, (r + 1) * QF)
-            wide = pieces[k][span, :].astype(jnp.float32)
-            out[k, span, :] = (wide * gate_b[k, r : r + 1, :]).astype(jnp.bfloat16)
-
-
-def weight_kernel(n_t, own, other, *refs):
-    packed, out, held = refs[:n_t], refs[n_t], refs[n_t + 1]
-    _, chip, core = place()
-    width = own.shape[2]
-    for k in range(n_t):
-        held[k] = packed[k][1]
-    saved = jnp.concatenate([held[chip ^ k] for k in range(n_t)], axis=0)
+        saved[k] = piece(packed, k)[1].astype(jnp.float32)
+    ordered = jnp.concatenate([saved[chip ^ k] for k in range(n_t)], axis=0)
+    ordered = jnp.transpose(ordered).astype(jnp.bfloat16)
     for ref, half in ((own, core), (other, 1 - core)):
-        gated = jnp.concatenate([ref[k] for k in range(n_t)], axis=0)
-        result = dot(saved, gated, 0, 0)
+        gated = jnp.concatenate(
+            [
+                jnp.concatenate(
+                    [ref[k * base + j * rows : k * base + (j + 1) * rows, :] for k in range(n_t)],
+                    axis=0,
+                )
+                for j in range(tiles)
+            ],
+            axis=1,
+        )
+        result = dot(ordered, gated, 1, 0)
         for h in range(2):
 
             @pl.when(half == h)
@@ -318,28 +354,41 @@
     def over_time(x, k):
         return lax.ppermute(x, "tm", [(t, t ^ k) for t in range(n_t)])
 
+    tiles = width // LANES
+    count = chips * frames * tiles
+    base = tiles * rows
+
+    def time_swaps(messages):
+        got = {k: over_time(messages[k], k) for k in range(n_t - 1, 0, -1)}
+        return [messages[0]] + [got[k] for k in range(1, n_t)]
+
+    def time_gather(x):
+        step = 1
+        while True:
+            got = over_time(x, step)
+            step *= 2
+            if step >= n_t:
+                return [x, got]
+            x = jnp.concatenate([x, got], axis=0)
+
     pieces = over_chips(out_grad)
-    kept, sent = call(
-        functools.partial(cut_kernel, chips),
-        [proj_weight],
-        [shape(bf16, chips, HD, width)] * 2,
-        [pltpu.SemaphoreType.DMA((2 * chips,))],
-        in_place=True,
-    )
-    received, other_saved = over_cores(sent), over_cores(saved_out)
-    packed, _ = lax.optimization_barrier((jnp.stack([queries, saved_out]), (received, other_saved)))
-    packed_all = [packed]
-    for k in range(1, n_t):
-        high = 1 << (k.bit_length() - 1)
-        packed_all.append(over_time(packed_all[k - high], high))
     moves = [
         (t * n_s + 2 * c + e, c * n_s + 2 * (c ^ t) + e)
         for t in range(n_t)
         for c in range(chips)
         for e in range(2)
     ]
-    to_move, _ = lax.optimization_barrier((out_grad, packed_all[n_t // 2]))
-    moved = lax.ppermute(to_move, ("tm", "space"), moves)
+    moved = lax.ppermute(out_grad, ("tm", "space"), moves)
+    kept, sent = call(
+        functools.partial(cut_kernel, chips),
+        [proj_weight, saved_out],
+        [shape(bf16, chips, HD, width), shape(bf16, HD, chips * width + HD)],
+        [pltpu.SemaphoreType.DMA((2 * chips + 1,))],
+        in_place=True,
+    )
+    received = over_cores(sent)
+    packed, _ = lax.optimization_barrier((jnp.stack([queries, saved_out])[None], received))
+    packed_all = time_gather(packed)
     gate_table, _ = lax.optimization_barrier((gate_table, received))
     bias, gate_a, gate_b, hot = call(
         functools.partial(masks_kernel, n_t, chips, frames, rows),
@@ -347,16 +396,14 @@
         [
             shape(f32, frames, n_t * rows),
             shape(f32, chips, frames, width),
-            shape(f32, n_t, frames, width),
+            shape(f32, frames, width),
             shape(f32, n_t * frames, levels, LANES),
         ],
         in_smem=2,
     )
-    kept, _ = lax.optimization_barrier((kept, packed_all))
-    count = chips * frames * width // LANES
     mine, other = call(
         functools.partial(head_kernel, chips, frames),
-        [packed, other_saved, kept, received, gate_a] + pieces,
+        [packed, kept, received, gate_a] + pieces,
         [shape(f32, rows, HD), shape(f32, rows + count, HD)],
         flops=4 * rows * chips * width * 2 * HD,
     )
@@ -367,42 +414,48 @@
         shape(f32, 2 * n_t, LANES),
         flops=2 * n_t * rows * k_rows * HD,
     )
-    extra = -(-SPLIT * 2 * n_t // 16) * 16
-    joined, terms = call(
+    from_core = over_cores(other)
+    joined = call(
         join_kernel,
-        [mine, other, over_cores(other), stats],
-        [shape(bf16, rows + extra, HD), shape(f32, 2 * count, LANES)],
-    )
-    heads_all = [joined] + [over_time(joined, k) for k in range(1, n_t)]
-    terms_all = over_chips(terms)
-    moved, _ = lax.optimization_barrier((moved, terms_all))
-    row_pieces = over_chips(moved)
+        [mine, from_core, stats],
+        shape(bf16, 1, rows + rows_of_split(n_t), HD),
+    )
+    heads_all = time_gather(joined)
+    bundle = call(
+        functools.partial(bundle_kernel, frames),
+        [gate_b, moved, other, from_core],
+        shape(bf16, base + 4 * count, LANES),
+    )
+    bundles, _ = lax.optimization_barrier((over_chips(bundle), heads_all[1]))
+    collected, terms = call(
+        functools.partial(collect_kernel, chips, base),
+        bundles,
+        [shape(bf16, chips * base, LANES), shape(bf16, 2 * count, LANES)],
+        [pltpu.VMEM((chips, 2 * count, LANES), f32)],
+    )
     outs = call(
-        functools.partial(grads_kernel, n_t, chips),
-        [bias, keys, values] + terms_all + packed_all + heads_all,
-        [shape(bf16, k_rows, HD)] * 2 + [shape(bf16, rows + 2 * count, LANES)] * n_t,
-        [pltpu.VMEM((k_rows, HD), f32)] * 2 + [pltpu.VMEM((chips, 2 * count, LANES), f32)],
+        functools.partial(grads_kernel, n_t, len(packed_all)),
+        [bias, keys, values, terms] + packed_all + heads_all,
+        [shape(bf16, k_rows, HD)] * 2 + [shape(bf16, HD + 2 * count, rows)] * n_t,
+        [pltpu.VMEM((k_rows, HD), f32)] * 2,
         flops=10 * n_t * rows * k_rows * HD,
     )
-    key_grad, value_grad, parts = outs[0], outs[1], outs[2:]
-    parts = [parts[0]] + [over_time(parts[k], k) for k in range(1, n_t)]
-    row_pieces, _ = lax.optimization_barrier((row_pieces, parts))
-
-    gated = call(
-        functools.partial(gated_kernel, n_t, frames),
-        [gate_b] + row_pieces,
-        shape(bf16, n_t, rows, width),
-    )
+    key_grad, value_grad = outs[:2]
+    parts = time_swaps(outs[2:][::-1])
+    to_core, _ = lax.optimization_barrier((collected, outs[2]))
+    exchanged = over_cores(to_core)
+    later, _ = lax.optimization_barrier((collected, parts[n_t - 1]))
     weight_grad = call(
         functools.partial(weight_kernel, n_t),
-        [gated, over_cores(gated)] + packed_all,
+        [later, exchanged] + packed_all,
         shape(f32, HD, 2 * width),
-        [pltpu.VMEM((n_t, rows, HD), bf16)],
+        [pltpu.VMEM((n_t, rows, HD), f32)],
         flops=4 * n_t * rows * width * HD,
     )
+    hot, _ = lax.optimization_barrier((hot, weight_grad))
     query_grad, gate_grad = call(
         functools.partial(finish_kernel, n_t, chips, frames),
-        [hot] + parts,
+        [hot] + parts[::-1],
         [shape(bf16, rows, HD), shape(f32, levels, n_s * width)],
         [pltpu.VMEM((n_t, 2 * count, LANES), f32)],
     )

time: 53.9 us -> 52.9 us (0.981)
  starting transfers between devices: 33.1 us -> 27.7 us
  waiting for transfers between devices: 11 us -> 14.7 us
  local copies, waits for them, and re-layouts: 0.04 us -> 0.86 us
    ppermute x9 -> x6, waiting for transfers between devices: 0.02 us -> 6.6 us  [over_chips(): lax.ppermute(x, 'space', [(s, s ^ 2 * k) for s in range(n_s)])]
    ppermute x9 -> x7, starting transfers between devices: 16.9 us -> 11.4 us  [over_time(): return lax.ppermute(x, 'tm', [(t, t ^ k) for t in range(n_t)])]
    ppermute x4 -> x3, waiting for transfers between devices: 2.84 us -> 0.01 us  [over_cores(): return lax.ppermute(x, 'space', [(s, s ^ 1) for s in range(n_s)])]
    unnamed x16 -> x17, local copies, waits for them, and re-layouts: 0.04 us -> 0.84 us
    ppermute x9 -> x6, starting transfers between devices: 15 us -> 15 us  [over_chips(): lax.ppermute(x, 'space', [(s, s ^ 2 * k) for s in range(n_s)])]
    pallas_call x9 -> x10, Pallas kernels: 8.71 us -> 8.66 us  [call(): pl.pallas_call(kernel, out_shape=out_shape, in_specs=[pl.BlockSpec(memory...]
    ppermute x9 -> x7, waiting for transfers between devices: 8.12 us -> 8.13 us  [over_time(): return lax.ppermute(x, 'tm', [(t, t ^ k) for t in range(n_t)])]
  transfers between devices with their start and end apart: 23 -> 17, of which waited for: 7 -> 7; matrix products, arithmetic and copies ran while one was open for 0% -> 0% of each run, Pallas kernels for 10% -> 7%
where the time goes in v6:
time: 52.9 us; the launch traced here: 52.8 us
  starting transfers between devices  27.7 us (52%)
  waiting for transfers between devices  14.7 us (28%)
  Pallas kernels  8.66 us (16%)
  local copies, waits for them, and re-layouts  0.86 us (2%)
  between operations  0.81 us (2%)
    ppermute x6, starting transfers between devices, over_chips(): lax.ppermute(x, 'space', [(s, s ^ 2 * k) for s in range(n_s)])  15 us
    ppermute x7, starting transfers between devices, over_time(): return lax.ppermute(x, 'tm', [(t, t ^ k) for t in range(n_t)])  11.4 us
    pallas_call x10, Pallas kernels, call(): pl.pallas_call(kernel, out_shape=out_shape, in_specs=[pl.BlockSpec(memory...  8.66 us
    ppermute x7, waiting for transfers between devices, over_time(): return lax.ppermute(x, 'tm', [(t, t ^ k) for t in range(n_t)])  8.13 us
    ppermute x6, waiting for transfers between devices, over_chips(): lax.ppermute(x, 'space', [(s, s ^ 2 * k) for s in range(n_s)])  6.6 us
  transfers between devices with their start and end apart: 17, of which 7 were waited for; matrix products, arithmetic and copies ran while one was open for 0% of the time, Pallas kernels for 7%

profile of v6, /device:TPU:0, one launch (start us, length us, event | category | flops | bytes accessed | tf_op | source)
XLA Modules:
  0.0 52.8 jit_solution(5233990646143567735)
XLA Ops:
  0.7 0.8 %copy-done.3 = bf16[128,128]{1,0:T(8,128)(2,1)S(1)} copy-done((bf16[128,128]{1,0:T(8,128)(2,1)S(1)}, bf16[128,128]{1,0:T(8,128)(2,1)}, u32[]{:S(2)}) %copy-start.3) | copy-done | bytes 32792
  1.5 1.5 %shard_map.128 = (bf16[4,128,640]{2,1,0:T(8,128)(2,1)S(1)}, bf16[128,2688]{1,0:T(8,128)(2,1)S(1)}) custom-call(bf16[128,5120]{1,0:T(8,128)(2,1)} %weight_in.1, bf16[128,128]{1,0:T(8,128)(2,1)S(1)} %copy-done.3), custom_call_target="tpu_custom_call" | custom-call | bytes 1343488 | tf_op jit(solution)/shard_map/pallas_call | solution.py:303
  3.5 2.6 %collective-permute-start.3 = (bf16[128,640]{1,0:T(8,128)(2,1)S(1)}, bf16[128,640]{1,0:T(8,128)(2,1)S(1)}, u32[]{:S(2)}, u32[]{:S(2)}) collective-permute-start(bf16[128,640]{1,0:T(8,128)(2,1)S(1)} %copy-done.2), channel_id=1, source_target_pairs={{0,4},{1,5},{2,6},{3,7},{4,0},{5,1},{6,2},{7,3},{8,12},{9,13},{10,... | collective-permute-start | bytes 491528 | tf_op jit(solution)/shard_map/ppermute | solution.py:348
  6.1 1.5 %collective-permute-start.2 = (bf16[128,640]{1,0:T(8,128)(2,1)S(1)}, bf16[128,640]{1,0:T(8,128)(2,1)S(1)}, u32[]{:S(2)}, u32[]{:S(2)}) collective-permute-start(bf16[128,640]{1,0:T(8,128)(2,1)S(1)} %copy-done.2), channel_id=1, source_target_pairs={{0,2},{1,3},{2,0},{3,1},{4,6},{5,7},{6,4},{7,5},{8,10},{9,11},{10,... | collective-permute-start | bytes 491528 | tf_op jit(solution)/shard_map/ppermute | solution.py:348
  7.7 2.1 %collective-permute-start.9 = (bf16[1,2,128,128]{3,2,1,0:T(8,128)(2,1)S(1)}, bf16[1,2,128,128]{3,2,1,0:T(8,128)(2,1)S(1)}, u32[]{:S(2)}, u32[]{:S(2)}) collective-permute-start(bf16[1,2,128,128]{3,2,1,0:T(8,128)(2,1)S(1)} %maximum_bitcast_fusion.packed), channel_id=1, source_target_pairs={{0,8},{8,0},{16,24},{24,16},{1,9},{9,1},{17,25},{25,17},{2,10},{10... | collective-permute-start | bytes 196616 | tf_op jit(solution)/shard_map/ppermute | solution.py:355
  9.8 2.3 %collective-permute-done.9 = bf16[1,2,128,128]{3,2,1,0:T(8,128)(2,1)S(1)} collective-permute-done((bf16[1,2,128,128]{3,2,1,0:T(8,128)(2,1)S(1)}, bf16[1,2,128,128]{3,2,1,0:T(8,128)(2,1)S(1)}, u32[]{:S(2)}, u32[]{:S(2)}) %collective-permute-start.9) | collective-permute-done | bytes 65568 | tf_op jit(solution)/shard_map/ppermute | solution.py:355
  12.0 3.1 %collective-permute-start.10 = (bf16[2,2,128,128]{3,2,1,0:T(8,128)(2,1)S(1)}, bf16[2,2,128,128]{3,2,1,0:T(8,128)(2,1)S(1)}, u32[]{:S(2)}, u32[]{:S(2)}) collective-permute-start(bf16[2,2,128,128]{3,2,1,0:T(8,128)(2,1)S(1)} %constant_dynamic-update-slice_fusion.refs_0_), channel_id=1, source_target_pairs={{0,16},{8,24},{16,0},{24,8},{1,17},{9,25},{17,1},{25,9},{2,18},{10... | collective-permute-start | bytes 393224 | tf_op jit(solution)/shard_map/ppermute | solution.py:355
  15.1 0.7 %collective-permute-start.1 = (bf16[128,640]{1,0:T(8,128)(2,1)S(1)}, bf16[128,640]{1,0:T(8,128)(2,1)S(1)}, u32[]{:S(2)}, u32[]{:S(2)}) collective-permute-start(bf16[128,640]{1,0:T(8,128)(2,1)S(1)} %copy-done.2), channel_id=1, source_target_pairs={{0,0},{1,1},{2,10},{3,11},{4,20},{5,21},{6,30},{7,31},{8,2},{9,3},... | collective-permute-start | bytes 491528 | tf_op jit(solution)/shard_map/ppermute | solution.py:381
  15.8 0.6 %shard_map.129 = (f32[2,512]{1,0:T(2,128)S(1)}, f32[4,2,640]{2,1,0:T(2,128)S(1)}, f32[2,640]{1,0:T(2,128)S(1)}, f32[8,16,128]{2,1,0:T(8,128)S(1)}) custom-call(s32[8]{0:T(128)S(1)} %copy-done.4, s32[4]{0:T(128)S(1)} %copy-done.5, f32[16,5120]{1,0:T(8,128)S(1)} %copy-done), custom_call_target="tpu_custom_call" | custom-call | bytes 327728 | tf_op jit(solution)/shard_map/pallas_call | solution.py:303
  16.5 0.8 %shard_map.130 = (f32[128,128]{1,0:T(8,128)S(1)}, f32[168,128]{1,0:T(8,128)S(1)}) custom-call(bf16[1,2,128,128]{3,2,1,0:T(8,128)(2,1)S(1)} %maximum_bitcast_fusion.packed, bf16[4,128,640]{2,1,0:T(8,128)(2,1)S(1)} %get-tuple-element.38.kept, bf16[128,2688]{1,0:T(8,128)(2,1)S(1)} %collective-permute-done.received, f32[4,2,640]{2,1,0:T(2,128)S(1)} %get-tuple-element.39.gate_a, ...), custom_call_target="tpu_custom_call" | custom-call | flops 335544320 | bytes 2084864 | tf_op jit(solution)/shard_map/pallas_call | solution.py:303
  17.4 3.4 %collective-permute-done.10.refs_1_ = bf16[2,2,128,128]{3,2,1,0:T(8,128)(2,1)S(1)} collective-permute-done((bf16[2,2,128,128]{3,2,1,0:T(8,128)(2,1)S(1)}, bf16[2,2,128,128]{3,2,1,0:T(8,128)(2,1)S(1)}, u32[]{:S(2)}, u32[]{:S(2)}) %collective-permute-start.10) | collective-permute-done | bytes 131104 | tf_op jit(solution)/shard_map/ppermute | solution.py:355
  20.8 0.8 %shard_map.132.stats = f32[8,128]{1,0:T(8,128)S(1)} custom-call(f32[2,512]{1,0:T(2,128)S(1)} %get-tuple-element.43.bias, bf16[1024,128]{1,0:T(8,128)(2,1)S(1)} %copy-done.1, bf16[2,2,128,128]{3,2,1,0:T(8,128)(2,1)S(1)} %constant_dynamic-update-slice_fusion.refs_0_, bf16[2,2,128,128]{3,2,1,0:T(8,128)(2,1)S(1)} %collective-permute-done.10.refs_1_), custom_call_target="tpu_custom_call" | custom-call | flops 134217728 | bytes 528384 | tf_op jit(solution)/shard_map/pallas_call | solution.py:303
  21.6 1.3 %collective-permute-start.11 = (bf16[1,160,128]{2,1,0:T(8,128)(2,1)S(1)}, bf16[1,160,128]{2,1,0:T(8,128)(2,1)S(1)}, u32[]{:S(2)}, u32[]{:S(2)}) collective-permute-start(bf16[1,160,128]{2,1,0:T(8,128)(2,1)S(1)} %shard_map.133), channel_id=1, source_target_pairs={{0,8},{8,0},{16,24},{24,16},{1,9},{9,1},{17,25},{25,17},{2,10},{10... | collective-permute-start | bytes 122888 | tf_op jit(solution)/shard_map/ppermute | solution.py:355
  23.0 6.0 %collective-permute-start.8 = (bf16[800,128]{1,0:T(8,128)(2,1)S(1)}, bf16[800,128]{1,0:T(8,128)(2,1)S(1)}, u32[]{:S(2)}, u32[]{:S(2)}) collective-permute-start(bf16[800,128]{1,0:T(8,128)(2,1)S(1)} %shard_map.131.refs_0_), channel_id=1, source_target_pairs={{0,6},{1,7},{2,4},{3,5},{4,2},{5,3},{6,0},{7,1},{8,14},{9,15},{10,... | collective-permute-start | bytes 614408 | tf_op jit(solution)/shard_map/ppermute | solution.py:348
  29.0 4.9 %collective-permute-start.7 = (bf16[800,128]{1,0:T(8,128)(2,1)S(1)}, bf16[800,128]{1,0:T(8,128)(2,1)S(1)}, u32[]{:S(2)}, u32[]{:S(2)}) collective-permute-start(bf16[800,128]{1,0:T(8,128)(2,1)S(1)} %shard_map.131.refs_0_), channel_id=1, source_target_pairs={{0,4},{1,5},{2,6},{3,7},{4,0},{5,1},{6,2},{7,3},{8,12},{9,13},{10,... | collective-permute-start | bytes 614408 | tf_op jit(solution)/shard_map/ppermute | solution.py:348
  33.9 0.5 %collective-permute-start.12 = (bf16[2,160,128]{2,1,0:T(8,128)(2,1)S(1)}, bf16[2,160,128]{2,1,0:T(8,128)(2,1)S(1)}, u32[]{:S(2)}, u32[]{:S(2)}) collective-permute-start(bf16[2,160,128]{2,1,0:T(8,128)(2,1)S(1)} %pad_maximum_fusion.refs_2_), channel_id=1, source_target_pairs={{0,16},{8,24},{16,0},{24,8},{1,17},{9,25},{17,1},{25,9},{2,18},{10... | collective-permute-start | bytes 245768 | tf_op jit(solution)/shard_map/ppermute | solution.py:355
  34.6 5.4 %collective-permute-done.7.refs_2_ = bf16[800,128]{1,0:T(8,128)(2,1)S(1)} collective-permute-done((bf16[800,128]{1,0:T(8,128)(2,1)S(1)}, bf16[800,128]{1,0:T(8,128)(2,1)S(1)}, u32[]{:S(2)}, u32[]{:S(2)}) %collective-permute-start.7) | collective-permute-done | bytes 204832 | tf_op jit(solution)/shard_map/ppermute | solution.py:348
  40.0 1.0 %collective-permute-done.6.refs_1_ = bf16[800,128]{1,0:T(8,128)(2,1)S(1)} collective-permute-done((bf16[800,128]{1,0:T(8,128)(2,1)S(1)}, bf16[800,128]{1,0:T(8,128)(2,1)S(1)}, u32[]{:S(2)}, u32[]{:S(2)}) %collective-permute-start.6) | collective-permute-done | bytes 204832 | tf_op jit(solution)/shard_map/ppermute | solution.py:348
  41.1 2.4 %shard_map.135 = (bf16[1024,128]{1,0:T(8,128)(2,1)}, bf16[1024,128]{1,0:T(8,128)(2,1)}, bf16[208,128]{1,0:T(8,128)(2,1)S(1)}, bf16[208,128]{1,0:T(8,128)(2,1)S(1...) custom-call(f32[2,512]{1,0:T(2,128)S(1)} %get-tuple-element.43.bias, bf16[1024,128]{1,0:T(8,128)(2,1)S(1)} %copy-done.1, ...), custom_call_target="tpu_custom_call" | custom-call | flops 671088640 | bytes 974848 | tf_op jit(solution)/shard_map/pallas_call | solution.py:303
  43.5 2.7 %collective-permute-start.13 = (bf16[208,128]{1,0:T(8,128)(2,1)S(1)}, bf16[208,128]{1,0:T(8,128)(2,1)S(1)}, u32[]{:S(2)}, u32[]{:S(2)}) collective-permute-start(bf16[208,128]{1,0:T(8,128)(2,1)S(1)} %get-tuple-element.50), channel_id=1, source_target_pairs={{0,24},{8,16},{16,8},{24,0},{1,25},{9,17},{17,9},{25,1},{2,26},{10... | collective-permute-start | bytes 159752 | tf_op jit(solution)/shard_map/ppermute | solution.py:355
  46.2 1.7 %collective-permute-start.16 = (bf16[208,128]{1,0:T(8,128)(2,1)S(1)}, bf16[208,128]{1,0:T(8,128)(2,1)S(1)}, u32[]{:S(2)}, u32[]{:S(2)}) collective-permute-start(bf16[208,128]{1,0:T(8,128)(2,1)S(1)} %get-tuple-element.55), channel_id=1, source_target_pairs={{0,8},{8,0},{16,24},{24,16},{1,9},{9,1},{17,25},{25,17},{2,10},{10... | collective-permute-start | bytes 159752 | tf_op jit(solution)/shard_map/ppermute | solution.py:355
  47.9 2.0 %collective-permute-done.13.refs_0_ = bf16[208,128]{1,0:T(8,128)(2,1)S(1)} collective-permute-done((bf16[208,128]{1,0:T(8,128)(2,1)S(1)}, bf16[208,128]{1,0:T(8,128)(2,1)S(1)}, u32[]{:S(2)}, u32[]{:S(2)}) %collective-permute-start.13) | collective-permute-done | bytes 53280 | tf_op jit(solution)/shard_map/ppermute | solution.py:355
  49.9 1.5 %shard_map.136 = f32[128,1280]{1,0:T(8,128)} custom-call(bf16[2560,128]{1,0:T(8,128)(2,1)S(1)} %get-tuple-element.52.own, bf16[2560,128]{1,0:T(8,128)(2,1)S(1)} %collective-permute-done.14.other, bf16[2,2,128,128]{3,2,1,0:T(8,128)(2,1)S(1)} %constant_dynamic-update-slice_fusion.refs_0_, bf16[2,2,128,128]{3,2,1,0:T(8,128)(2,1)S(1)} %collective-permute-done.10.refs_1_), custom_call_target="tpu_custom_call" | custom-call | flops 167772160 | bytes 1572864 | tf_op jit(solution)/shard_map/pallas_call | solution.py:303
  51.8 0.9 %shard_map.137 = (bf16[128,128]{1,0:T(8,128)(2,1)}, f32[16,5120]{1,0:T(8,128)}) custom-call(f32[8,16,128]{2,1,0:T(8,128)S(1)} %get-tuple-element.53.hot, bf16[208,128]{1,0:T(8,128)(2,1)S(1)} %collective-permute-done.13.refs_0_, bf16[208,128]{1,0:T(8,128)(2,1)S(1)} %collective-permute-done.15.refs_1_, bf16[208,128]{1,0:T(8,128)(2,1)S(1)} %collective-permute-done.16.refs_2_, ...), custom_call_target="tpu_custom_call" | custom-call | bytes 278528 | tf_op jit(solution)/shard_map/pallas_call | solution.py:303
  (40 shorter events, 1.4 us)
Async XLA Ops:
  0.6 2.9 %copy-start.2 = (bf16[128,640]{1,0:T(8,128)(2,1)S(1)}, bf16[128,640]{1,0:T(8,128)(2,1)}, u32[]{:S(2)}) copy-start(bf16[128,640]{1,0:T(8,128)(2,1)} %refs_0_.1) | copy-start | bytes 491524
  0.6 15.1 %copy-start = (f32[16,5120]{1,0:T(8,128)S(1)}, f32[16,5120]{1,0:T(8,128)}, u32[]{:S(2)}) copy-start(f32[16,5120]{1,0:T(8,128)} %gate) | copy-start | bytes 983044
  1.5 6.2 %copy-start.7 = (bf16[128,128]{1,0:T(8,128)(2,1)S(1)}, bf16[128,128]{1,0:T(8,128)(2,1)}, u32[]{:S(2)}) copy-start(bf16[128,128]{1,0:T(8,128)(2,1)} %param.9) | copy-start | bytes 98308
  1.5 14.3 %copy-start.4 = (s32[8]{0:T(128)S(1)}, s32[8]{0:T(128)}, u32[]{:S(2)}) copy-start(s32[8]{0:T(128)} %levels.1) | copy-start | bytes 100
  1.5 14.3 %copy-start.5 = (s32[4]{0:T(128)S(1)}, s32[4]{0:T(128)}, u32[]{:S(2)}) copy-start(s32[4]{0:T(128)} %clips.1) | copy-start | bytes 52
  3.0 4.7 %collective-permute-start = (bf16[128,2688]{1,0:T(8,128)(2,1)S(1)}, bf16[128,2688]{1,0:T(8,128)(2,1)S(1)}, u32[]{:S(2)}, u32[]{:S(2)}) collective-permute-start(bf16[128,2688]{1,0:T(8,128)(2,1)S(1)} %get-tuple-element.33), channel_id=1, source_target_pairs={{0,1},{1,0},{2,3},{3,2},{4,5},{5,4},{6,7},{7,6},{8,9},{9,8},{10,11... | collective-permute-start | bytes 2064392 | tf_op jit(solution)/shard_map/ppermute | solution.py:352
  3.5 13.0 %collective-permute-start.3 = (bf16[128,640]{1,0:T(8,128)(2,1)S(1)}, bf16[128,640]{1,0:T(8,128)(2,1)S(1)}, u32[]{:S(2)}, u32[]{:S(2)}) collective-permute-start(bf16[128,640]{1,0:T(8,128)(2,1)S(1)} %copy-done.2), channel_id=1, source_target_pairs={{0,4},{1,5},{2,6},{3,7},{4,0},{5,1},{6,2},{7,3},{8,12},{9,13},{10,... | collective-permute-start | bytes 491528 | tf_op jit(solution)/shard_map/ppermute | solution.py:348
  6.1 10.4 %collective-permute-start.2 = (bf16[128,640]{1,0:T(8,128)(2,1)S(1)}, bf16[128,640]{1,0:T(8,128)(2,1)S(1)}, u32[]{:S(2)}, u32[]{:S(2)}) collective-permute-start(bf16[128,640]{1,0:T(8,128)(2,1)S(1)} %copy-done.2), channel_id=1, source_target_pairs={{0,2},{1,3},{2,0},{3,1},{4,6},{5,7},{6,4},{7,5},{8,10},{9,11},{10,... | collective-permute-start | bytes 491528 | tf_op jit(solution)/shard_map/ppermute | solution.py:348
  7.6 8.9 %collective-permute-start.4 = (bf16[128,640]{1,0:T(8,128)(2,1)S(1)}, bf16[128,640]{1,0:T(8,128)(2,1)S(1)}, u32[]{:S(2)}, u32[]{:S(2)}) collective-permute-start(bf16[128,640]{1,0:T(8,128)(2,1)S(1)} %copy-done.2), channel_id=1, source_target_pairs={{0,6},{1,7},{2,4},{3,5},{4,2},{5,3},{6,0},{7,1},{8,14},{9,15},{10,... | collective-permute-start | bytes 491528 | tf_op jit(solution)/shard_map/ppermute | solution.py:348
  7.7 13.1 %copy-start.1 = (bf16[1024,128]{1,0:T(8,128)(2,1)S(1)}, bf16[1024,128]{1,0:T(8,128)(2,1)}, u32[]{:S(2)}) copy-start(bf16[1024,128]{1,0:T(8,128)(2,1)} %keys.3) | copy-start | bytes 786436
  7.7 4.3 %collective-permute-start.9 = (bf16[1,2,128,128]{3,2,1,0:T(8,128)(2,1)S(1)}, bf16[1,2,128,128]{3,2,1,0:T(8,128)(2,1)S(1)}, u32[]{:S(2)}, u32[]{:S(2)}) collective-permute-start(bf16[1,2,128,128]{3,2,1,0:T(8,128)(2,1)S(1)} %maximum_bitcast_fusion.packed), channel_id=1, source_target_pairs={{0,8},{8,0},{16,24},{24,16},{1,9},{9,1},{17,25},{25,17},{2,10},{10... | collective-permute-start | bytes 196616 | tf_op jit(solution)/shard_map/ppermute | solution.py:355
  12.0 8.7 %collective-permute-start.10 = (bf16[2,2,128,128]{3,2,1,0:T(8,128)(2,1)S(1)}, bf16[2,2,128,128]{3,2,1,0:T(8,128)(2,1)S(1)}, u32[]{:S(2)}, u32[]{:S(2)}) collective-permute-start(bf16[2,2,128,128]{3,2,1,0:T(8,128)(2,1)S(1)} %constant_dynamic-update-slice_fusion.refs_0_), channel_id=1, source_target_pairs={{0,16},{8,24},{16,0},{24,8},{1,17},{9,25},{17,1},{25,9},{2,18},{10... | collective-permute-start | bytes 393224 | tf_op jit(solution)/shard_map/ppermute | solution.py:355
  15.1 7.8 %collective-permute-start.1 = (bf16[128,640]{1,0:T(8,128)(2,1)S(1)}, bf16[128,640]{1,0:T(8,128)(2,1)S(1)}, u32[]{:S(2)}, u32[]{:S(2)}) collective-permute-start(bf16[128,640]{1,0:T(8,128)(2,1)S(1)} %copy-done.2), channel_id=1, source_target_pairs={{0,0},{1,1},{2,10},{3,11},{4,20},{5,21},{6,30},{7,31},{8,2},{9,3},... | collective-permute-start | bytes 491528 | tf_op jit(solution)/shard_map/ppermute | solution.py:381
  17.3 23.8 %copy-start.6 = (bf16[1024,128]{1,0:T(8,128)(2,1)S(1)}, bf16[1024,128]{1,0:T(8,128)(2,1)}, u32[]{:S(2)}) copy-start(bf16[1024,128]{1,0:T(8,128)(2,1)} %values.1) | copy-start | bytes 786436
  17.3 4.3 %collective-permute-start.5 = (f32[168,128]{1,0:T(8,128)S(1)}, f32[168,128]{1,0:T(8,128)S(1)}, u32[]{:S(2)}, u32[]{:S(2)}) collective-permute-start(f32[168,128]{1,0:T(8,128)S(1)} %get-tuple-element.40.sent), channel_id=1, source_target_pairs={{0,1},{1,0},{2,3},{3,2},{4,5},{5,4},{6,7},{7,6},{8,9},{9,8},{10,11... | collective-permute-start | bytes 258056 | tf_op jit(solution)/shard_map/ppermute | solution.py:352
  21.6 12.3 %collective-permute-start.11 = (bf16[1,160,128]{2,1,0:T(8,128)(2,1)S(1)}, bf16[1,160,128]{2,1,0:T(8,128)(2,1)S(1)}, u32[]{:S(2)}, u32[]{:S(2)}) collective-permute-start(bf16[1,160,128]{2,1,0:T(8,128)(2,1)S(1)} %shard_map.133), channel_id=1, source_target_pairs={{0,8},{8,0},{16,24},{24,16},{1,9},{9,1},{17,25},{25,17},{2,10},{10... | collective-permute-start | bytes 122888 | tf_op jit(solution)/shard_map/ppermute | solution.py:355
  23.0 11.6 %collective-permute-start.8 = (bf16[800,128]{1,0:T(8,128)(2,1)S(1)}, bf16[800,128]{1,0:T(8,128)(2,1)S(1)}, u32[]{:S(2)}, u32[]{:S(2)}) collective-permute-start(bf16[800,128]{1,0:T(8,128)(2,1)S(1)} %shard_map.131.refs_0_), channel_id=1, source_target_pairs={{0,6},{1,7},{2,4},{3,5},{4,2},{5,3},{6,0},{7,1},{8,14},{9,15},{10,... | collective-permute-start | bytes 614408 | tf_op jit(solution)/shard_map/ppermute | solution.py:348
  29.0 11.0 %collective-permute-start.7 = (bf16[800,128]{1,0:T(8,128)(2,1)S(1)}, bf16[800,128]{1,0:T(8,128)(2,1)S(1)}, u32[]{:S(2)}, u32[]{:S(2)}) collective-permute-start(bf16[800,128]{1,0:T(8,128)(2,1)S(1)} %shard_map.131.refs_0_), channel_id=1, source_target_pairs={{0,4},{1,5},{2,6},{3,7},{4,0},{5,1},{6,2},{7,3},{8,12},{9,13},{10,... | collective-permute-start | bytes 614408 | tf_op jit(solution)/shard_map/ppermute | solution.py:348
  33.8 7.2 %collective-permute-start.6 = (bf16[800,128]{1,0:T(8,128)(2,1)S(1)}, bf16[800,128]{1,0:T(8,128)(2,1)S(1)}, u32[]{:S(2)}, u32[]{:S(2)}) collective-permute-start(bf16[800,128]{1,0:T(8,128)(2,1)S(1)} %shard_map.131.refs_0_), channel_id=1, source_target_pairs={{0,2},{1,3},{2,0},{3,1},{4,6},{5,7},{6,4},{7,5},{8,10},{9,11},{10,... | collective-permute-start | bytes 614408 | tf_op jit(solution)/shard_map/ppermute | solution.py:348
  33.9 7.1 %collective-permute-start.12 = (bf16[2,160,128]{2,1,0:T(8,128)(2,1)S(1)}, bf16[2,160,128]{2,1,0:T(8,128)(2,1)S(1)}, u32[]{:S(2)}, u32[]{:S(2)}) collective-permute-start(bf16[2,160,128]{2,1,0:T(8,128)(2,1)S(1)} %pad_maximum_fusion.refs_2_), channel_id=1, source_target_pairs={{0,16},{8,24},{16,0},{24,8},{1,17},{9,25},{17,1},{25,9},{2,18},{10... | collective-permute-start | bytes 245768 | tf_op jit(solution)/shard_map/ppermute | solution.py:355
  43.5 6.4 %collective-permute-start.14 = (bf16[2560,128]{1,0:T(8,128)(2,1)S(1)}, bf16[2560,128]{1,0:T(8,128)(2,1)S(1)}, u32[]{:S(2)}, u32[]{:S(2)}) collective-permute-start(bf16[2560,128]{1,0:T(8,128)(2,1)S(1)} %get-tuple-element.52.own), channel_id=1, source_target_pairs={{0,1},{1,0},{2,3},{3,2},{4,5},{5,4},{6,7},{7,6},{8,9},{9,8},{10,11... | collective-permute-start | bytes 1966088 | tf_op jit(solution)/shard_map/ppermute | solution.py:352
  43.5 6.4 %collective-permute-start.13 = (bf16[208,128]{1,0:T(8,128)(2,1)S(1)}, bf16[208,128]{1,0:T(8,128)(2,1)S(1)}, u32[]{:S(2)}, u32[]{:S(2)}) collective-permute-start(bf16[208,128]{1,0:T(8,128)(2,1)S(1)} %get-tuple-element.50), channel_id=1, source_target_pairs={{0,24},{8,16},{16,8},{24,0},{1,25},{9,17},{17,9},{25,1},{2,26},{10... | collective-permute-start | bytes 159752 | tf_op jit(solution)/shard_map/ppermute | solution.py:355
  46.2 5.6 %collective-permute-start.15 = (bf16[208,128]{1,0:T(8,128)(2,1)S(1)}, bf16[208,128]{1,0:T(8,128)(2,1)S(1)}, u32[]{:S(2)}, u32[]{:S(2)}) collective-permute-start(bf16[208,128]{1,0:T(8,128)(2,1)S(1)} %get-tuple-element.54), channel_id=1, source_target_pairs={{0,16},{8,24},{16,0},{24,8},{1,17},{9,25},{17,1},{25,9},{2,18},{10... | collective-permute-start | bytes 159752 | tf_op jit(solution)/shard_map/ppermute | solution.py:355
  46.2 5.6 %collective-permute-start.16 = (bf16[208,128]{1,0:T(8,128)(2,1)S(1)}, bf16[208,128]{1,0:T(8,128)(2,1)S(1)}, u32[]{:S(2)}, u32[]{:S(2)}) collective-permute-start(bf16[208,128]{1,0:T(8,128)(2,1)S(1)} %get-tuple-element.55), channel_id=1, source_target_pairs={{0,8},{8,0},{16,24},{24,16},{1,9},{9,1},{17,25},{25,17},{2,10},{10... | collective-permute-start | bytes 159752 | tf_op jit(solution)/shard_map/ppermute | solution.py:355
  (1 other events, 0.8 us)

commit v7 on v5

v7 whole, which is shorter than its diff:
```python
import functools
import math

import jax
import jax.numpy as jnp
from jax import lax
from jax.experimental import pallas as pl
from jax.experimental.pallas import tpu as pltpu
from jax.sharding import PartitionSpec as P

HD = 128
SPF = 512
QF = 64
LANES = 128
NEG_BIG = -1e30
SCALE = 1.0 / math.sqrt(HD)
VMEM_LIMIT = 32 * 1024 * 1024
PREP_VMEM = 52 * 1024 * 1024
SPLIT = 3


def dot(a, b, on_a, on_b):
    return lax.dot_general(
        a, b, (((on_a,), (on_b,)), ((), ())), preferred_element_type=jnp.float32
    )


def place():
    s = lax.axis_index("space")
    return lax.axis_index("tm"), s // 2, s % 2


def clip_numbers(clips_ref):
    bounds = []
    so_far = 0
    for c in range(clips_ref.shape[0]):
        so_far = so_far + clips_ref[c]
        bounds.append(so_far)
    return lambda frame: sum((frame >= bound).astype(jnp.int32) for bound in bounds)


def masks_kernel(
    n_t, n_s, frames, rows, levels, clips, gate, grad_in, bias, gate_a, gate_b, hot, grad
):
    grad[...] = grad_in[...]
    t, chip, core = place()
    width = gate_a.shape[2]
    clip_of = clip_numbers(clips)
    lane = lax.broadcasted_iota(jnp.int32, (1, rows), 1)
    for kf in range(frames):
        key_frame = t * frames + kf
        key_clip = clip_of(key_frame)
        for k in range(n_t):
            row = jnp.full((1, rows), NEG_BIG, jnp.float32)
            for r in range(frames):
                frame = (t ^ k) * frames + r
                visible = (key_frame >= frame) & (clip_of(frame) == key_clip)
                value = jnp.where(visible, 0.0, NEG_BIG).astype(jnp.float32)
                row = jnp.where((lane >= r * QF) & (lane < (r + 1) * QF), value, row)
            bias[kf : kf + 1, k * rows : (k + 1) * rows] = row
    spot = lax.broadcasted_iota(jnp.int32, hot.shape[1:], 0)
    for f in range(n_t * frames):
        hot[f] = (spot == levels[f]).astype(jnp.float32)
    for r in range(frames):
        level = levels[t * frames + r]
        for k in range(n_s):
            shard = (2 * chip + core) ^ k
            columns = pl.ds(pl.multiple_of(shard * width, LANES), width)
            gate_a[k, r : r + 1, :] = gate[pl.ds(level, 1), columns]
    mine = pl.ds(pl.multiple_of((2 * t + core) * width, LANES), width)
    for k in range(n_t):
        level = levels[(t ^ k) * frames + chip * (rows // (n_s // 2)) // QF]
        gate_b[k] = gate[pl.ds(level, 1), mine]


def stats_kernel(n_t, bias, keys, *refs):
    packed, out = refs[:n_t], refs[n_t]
    rows = packed[0].shape[1]
    for p in range(0, n_t, 2):
        q = jnp.concatenate([packed[p][0], packed[p + 1][0]], axis=0)
        scores = []
        for kf in range(bias.shape[0]):
            mask = bias[kf : kf + 1, p * rows : (p + 2) * rows]
            scores.append(dot(keys[kf * SPF : (kf + 1) * SPF, :], q, 1, 1) * SCALE + mask)
        top = functools.reduce(jnp.maximum, [jnp.max(x, axis=0, keepdims=True) for x in scores])
        total = sum(jnp.sum(jnp.exp(x - top), axis=0, keepdims=True) for x in scores)
        for i in range(2):
            out[p + i : p + i + 1, :] = top[:, i * rows : (i + 1) * rows]
            out[n_t + p + i : n_t + p + i + 1, :] = total[:, i * rows : (i + 1) * rows]


def head_kernel(n_s, frames, weight_in, packed, gate_a, *refs):
    pieces, (head_out, terms, weight_ref, sems) = refs[:n_s], refs[n_s:]
    s = lax.axis_index("space")
    width = pieces[0].shape[1]
    copies = []
    for k in range(n_s):
        columns = pl.ds(pl.multiple_of((s ^ k) * width, LANES), width)
        copies.append(pltpu.make_async_copy(weight_in.at[:, columns], weight_ref.at[k], sems.at[k]))
    for copy in copies:
        copy.start()
    tiles = width // LANES
    saved = packed[1]
    head = None
    for k in range(n_s):
        shard = s ^ k
        copies[k].wait()
        weight = weight_ref[k]
        wide = pieces[k][...].astype(jnp.float32)
        gated = jnp.concatenate(
            [
                (wide[r * QF : (r + 1) * QF] * gate_a[k, r : r + 1, :]).astype(jnp.bfloat16)
                for r in range(frames)
            ],
            axis=0,
        )
        part = dot(gated, weight, 1, 1)
        head = part if head is None else head + part
        product = wide * dot(saved, weight, 1, 0)
        place_of = (shard % 2) * (n_s // 2) + shard // 2
        for r in range(frames):
            term = jnp.sum(product[r * QF : (r + 1) * QF], axis=0, keepdims=True)
            for j in range(tiles):
                row = (place_of * frames + r) * tiles + j
                terms[pl.ds(row, 1), :] = term[:, j * LANES : (j + 1) * LANES]
    head_out[...] = head.astype(jnp.bfloat16)


def sections(rows, chips, tiles, n_t):
    starts = [0, rows]
    starts.append(starts[-1] + -(-SPLIT * 2 * n_t // 16) * 16)
    starts.append(starts[-1] + tiles * (rows // chips))
    return starts


def padded(x, rows):
    if x.shape[0] == rows:
        return x
    return jnp.concatenate([x, jnp.zeros((rows - x.shape[0], x.shape[1]), x.dtype)], axis=0)


def join_kernel(n_t, chips, starts, head, stats, *refs):
    pieces, outs, (wide, held) = refs[:chips], refs[chips : chips + n_t][::-1], refs[chips + n_t :]
    t, chip, _ = place()
    part, tiles = held.shape[1], held.shape[2] // LANES
    for k in range(chips):
        wide[...] = pieces[k][...].astype(jnp.float32)
        held[k] = wide[pl.ds(pl.multiple_of(chip * part, part), part), :]
    rest = stats[...]
    split = []
    for _ in range(SPLIT):
        piece = rest.astype(jnp.bfloat16).astype(jnp.float32)
        split.append(piece)
        rest = rest - piece
    split = padded(jnp.concatenate(split, axis=0), starts[2] - starts[1]).astype(jnp.bfloat16)
    for k in range(n_t):
        rows = held[chip ^ t ^ k]
        rows = jnp.concatenate([rows[:, j * LANES : (j + 1) * LANES] for j in range(tiles)], axis=0)
        outs[k][: starts[1], :] = head[...]
        outs[k][starts[1] : starts[2], :] = split
        outs[k][starts[2] : starts[3], :] = rows.astype(jnp.bfloat16)


def bundle_kernel(n_t, starts, gate_b, *refs):
    heads, out = refs[:n_t][::-1], refs[n_t]
    tiles = gate_b.shape[2] // LANES
    part = (starts[3] - starts[2]) // tiles
    wide = [heads[k][starts[2] : starts[3], :].astype(jnp.float32) for k in range(n_t)]
    for j in range(tiles):
        gated = jnp.concatenate(
            [
                wide[k][j * part : (j + 1) * part] * gate_b[k, :, j * LANES : (j + 1) * LANES]
                for k in range(n_t)
            ],
            axis=0,
        )
        out[j * n_t * part : (j + 1) * n_t * part, :] = gated.astype(jnp.bfloat16)


def collect_kernel(chips, *refs):
    base = refs[0].shape[0]
    for k in range(chips):
        refs[chips][k * base : (k + 1) * base, :] = refs[k][...]


def grads_kernel(n_t, bias, keys, values, terms, *refs):
    packed, heads = refs[:n_t], refs[n_t : 2 * n_t][::-1]
    key_out, value_out = refs[2 * n_t : 2 * n_t + 2]
    outs = refs[2 * n_t + 2 : 3 * n_t + 2][::-1]
    key_acc, value_acc = refs[3 * n_t + 2 :]
    rows = packed[0].shape[1]
    ones = jnp.ones((8, HD), jnp.float32)
    keys_t = jnp.transpose(keys[...])
    stats = []
    for k in range(n_t):
        parts = heads[k][rows : rows + -(-SPLIT * 2 * n_t // 16) * 16, :].astype(jnp.float32)
        stats.append(sum(parts[i * 2 * n_t : (i + 1) * 2 * n_t] for i in range(SPLIT)))
    for k in range(n_t):
        outs[k][rows:, :] = terms[...].astype(jnp.bfloat16)
    for p in range(0, n_t, 2):
        q = jnp.concatenate([packed[p][0], packed[p + 1][0]], axis=0)
        o = jnp.concatenate([packed[p][1], packed[p + 1][1]], axis=0)
        g = jnp.concatenate([heads[p][:rows, :], heads[p + 1][:rows, :]], axis=0)
        delta = lax.dot_general(
            ones,
            g.astype(jnp.float32) * o.astype(jnp.float32),
            (((1,), (1,)), ((), ())),
            precision=lax.Precision.HIGHEST,
            preferred_element_type=jnp.float32,
        )[0:1]
        lse = []
        for i in (p, p + 1):
            tops = [stats[k][i ^ k : (i ^ k) + 1] for k in range(n_t)]
            sums = [stats[k][n_t + (i ^ k) : n_t + (i ^ k) + 1] for k in range(n_t)]
            top = functools.reduce(jnp.maximum, tops)
            lse.append(top + jnp.log(sum(b * jnp.exp(a - top) for a, b in zip(tops, sums))))
        lse = jnp.concatenate(lse, axis=1)
        query_part = None
        for kf in range(bias.shape[0]):
            span = slice(kf * SPF, (kf + 1) * SPF)
            shift = bias[kf : kf + 1, p * rows : (p + 2) * rows] - lse
            probs = jnp.exp(dot(keys[span, :], q, 1, 1) * SCALE + shift)
            score_grad = (probs * (dot(values[span, :], g, 1, 1) - delta)).astype(jnp.bfloat16)
            value_add = dot(probs.astype(jnp.bfloat16), g, 1, 0)
            key_add = dot(score_grad, q, 1, 0)
            if p > 0:
                value_add = value_add + value_acc[span, :]
                key_add = key_add + key_acc[span, :]
            if p + 2 < n_t:
                value_acc[span, :] = value_add
                key_acc[span, :] = key_add
            else:
                value_out[span, :] = value_add.astype(jnp.bfloat16)
                key_out[span, :] = (key_add * SCALE).astype(jnp.bfloat16)
            part = dot(keys_t[:, span], score_grad, 1, 0)
            query_part = part if query_part is None else query_part + part
        outs[p][:rows, :] = query_part[:, :rows].astype(jnp.bfloat16)
        outs[p + 1][:rows, :] = query_part[:, rows:].astype(jnp.bfloat16)


def finish_kernel(n_t, chips, frames, hot, *refs):
    parts, (query_out, gate_out, held) = refs[:n_t][::-1], refs[n_t:]
    t = lax.axis_index("tm")
    rows = query_out.shape[0]
    total = parts[0][:rows, :].astype(jnp.float32)
    for k in range(1, n_t):
        total = total + parts[k][:rows, :].astype(jnp.float32)
    query_out[...] = jnp.transpose(total * SCALE).astype(jnp.bfloat16)
    for k in range(n_t):
        held[t ^ k] = parts[k][rows:, :].astype(jnp.float32)
    tiles = gate_out.shape[1] // (2 * chips * LANES)
    for core in range(2):
        for a in range(chips):
            for j in range(tiles):
                total = jnp.zeros(hot.shape[1:], jnp.float32)
                for f in range(n_t * frames):
                    row = ((core * chips + a) * frames + f % frames) * tiles + j
                    total = total + hot[f] * held[f // frames, row : row + 1, :]
                column = ((2 * a + core) * tiles + j) * LANES
                gate_out[:, column : column + LANES] = total


def weight_kernel(n_t, chips, own, other, *refs):
    packed, (out, saved) = refs[:n_t], refs[n_t:]
    _, chip, core = place()
    width = out.shape[1] // 2
    tiles = width // LANES
    rows = saved.shape[1]
    part = rows // chips
    base = tiles * n_t * part
    for k in range(n_t):
        saved[k] = packed[k][1].astype(jnp.float32)
    ordered = []
    for c in range(chips):
        mine = pl.ds(pl.multiple_of((chip ^ c) * part, part), part)
        ordered += [saved[k, mine, :] for k in range(n_t)]
    ordered = jnp.transpose(jnp.concatenate(ordered, axis=0)).astype(jnp.bfloat16)
    for ref, half in ((own, core), (other, 1 - core)):
        gated = jnp.concatenate(
            [
                jnp.concatenate(
                    [
                        ref[c * base + j * n_t * part : c * base + (j + 1) * n_t * part, :]
                        for c in range(chips)
                    ],
                    axis=0,
                )
                for j in range(tiles)
            ],
            axis=1,
        )
        result = dot(ordered, gated, 1, 0)
        for h in range(2):

            @pl.when(half == h)
            def _():
                out[:, h * width : (h + 1) * width] = result


def call(kernel, args, out_shape, scratch=(), flops=0, in_place=0, in_smem=0):
    vmem = pl.BlockSpec(memory_space=pltpu.VMEM)
    single = not isinstance(out_shape, (list, tuple))
    nbytes = sum(a.size * a.dtype.itemsize for a in args)
    return pl.pallas_call(
        kernel,
        out_shape=out_shape,
        in_specs=[pl.BlockSpec(memory_space=pltpu.SMEM)] * in_smem
        + [pl.BlockSpec(memory_space=pltpu.HBM)] * in_place
        + [vmem] * (len(args) - in_smem - in_place),
        out_specs=vmem if single else [vmem] * len(out_shape),
        scratch_shapes=list(scratch),
        compiler_params=pltpu.CompilerParams(vmem_limit_bytes=PREP_VMEM if in_place else VMEM_LIMIT),
        cost_estimate=pl.CostEstimate(flops=flops, bytes_accessed=nbytes, transcendentals=0),
    )(*args)


def padded_shards(table, n_s, width):
    rows, columns = table.shape
    cut = table.reshape(rows, n_s, columns // n_s)
    cut = jnp.pad(cut, ((0, 0), (0, 0), (0, width - columns // n_s)))
    return cut.reshape(rows, n_s * width)


def without_padding(table, shards, shard):
    rows, columns = table.shape
    return table.reshape(rows, shards, columns // shards)[:, :, :shard].reshape(rows, shards * shard)


def body(
    queries, keys, values, saved_out, out_grad, proj_weight, gate_table, noise_levels, clip_lengths
):
    n_t, n_s = lax.axis_size("tm"), lax.axis_size("space")
    chips = n_s // 2
    rows, shard = out_grad.shape
    k_rows = keys.shape[0]
    frames = rows // QF
    levels = gate_table.shape[0]
    bf16, f32 = jnp.bfloat16, jnp.float32
    width = -(-shard // LANES) * LANES
    if width != shard:
        out_grad = jnp.pad(out_grad, ((0, 0), (0, width - shard)))
        proj_weight = padded_shards(proj_weight, n_s, width)
        gate_table = padded_shards(gate_table, n_s, width)

    def shape(dtype, *dims):
        return jax.ShapeDtypeStruct(dims, dtype)

    def over_chips(x):
        return [x] + [
            lax.ppermute(x, "space", [(s, s ^ (2 * k)) for s in range(n_s)]) for k in range(1, chips)
        ]

    def over_space(x, k):
        return lax.ppermute(x, "space", [(s, s ^ k) for s in range(n_s)])

    def over_cores(x):
        return lax.ppermute(x, "space", [(s, s ^ 1) for s in range(n_s)])

    def over_time(x, k):
        return lax.ppermute(x, "tm", [(t, t ^ k) for t in range(n_t)])

    tiles = width // LANES
    part = rows // chips
    count = chips * frames * tiles
    starts = sections(rows, chips, tiles, n_t)

    def time_swaps(messages):
        got = {k: over_time(messages[k], k) for k in range(n_t - 1, 0, -1)}
        return [messages[0]] + [got[k] for k in range(1, n_t)]

    packed = jnp.stack([queries, saved_out])
    packed_all = [packed]
    for k in range(1, n_t):
        high = 1 << (k.bit_length() - 1)
        packed_all.append(over_time(packed_all[k - high], high))
    pieces = over_chips(out_grad)
    bias, gate_a, gate_b, hot, own_piece = call(
        functools.partial(masks_kernel, n_t, n_s, frames, rows),
        [noise_levels, clip_lengths, gate_table, out_grad],
        [
            shape(f32, frames, n_t * rows),
            shape(f32, n_s, frames, width),
            shape(f32, n_t, 1, width),
            shape(f32, n_t * frames, levels, LANES),
            shape(bf16, rows, width),
        ],
        in_smem=2,
    )
    pieces[1:], _ = lax.optimization_barrier((pieces[1:], (packed_all[1:], gate_a)))
    pieces = [y for x in pieces for y in (x, over_cores(x))]
    pieces[0] = own_piece
    head, terms = call(
        functools.partial(head_kernel, n_s, frames),
        [proj_weight, packed, gate_a] + pieces,
        [shape(bf16, rows, HD), shape(f32, 2 * count, LANES)],
        [
            pltpu.VMEM((n_s, HD, width), bf16),
            pltpu.SemaphoreType.DMA((n_s,)),
        ],
        in_place=1,
        flops=4 * rows * n_s * width * HD,
    )
    later_bias, _ = lax.optimization_barrier((bias, head))
    stats = call(
        functools.partial(stats_kernel, n_t),
        [later_bias, keys] + packed_all,
        shape(f32, 2 * n_t, LANES),
        flops=2 * n_t * rows * k_rows * HD,
    )
    messages = call(
        functools.partial(join_kernel, n_t, chips, starts),
        [head, stats] + pieces[::2],
        [shape(bf16, starts[-1], LANES)] * n_t,
        [pltpu.VMEM((rows, width), f32), pltpu.VMEM((chips, part, width), f32)],
    )
    heads_all = time_swaps(messages[::-1])
    step = 1
    while step < n_s:
        terms = terms + over_space(terms, step)
        step *= 2
    base = tiles * n_t * part
    bundle = call(
        functools.partial(bundle_kernel, n_t, starts),
        [gate_b] + heads_all[::-1],
        shape(bf16, base, LANES),
    )
    bundles = over_chips(bundle)
    later_bias, _ = lax.optimization_barrier((bias, bundle))
    outs = call(
        functools.partial(grads_kernel, n_t),
        [later_bias, keys, values, terms] + packed_all + heads_all[::-1],
        [shape(bf16, k_rows, HD)] * 2 + [shape(bf16, HD + 2 * count, rows)] * n_t,
        [pltpu.VMEM((k_rows, HD), f32)] * 2,
        flops=10 * n_t * rows * k_rows * HD,
    )
    key_grad, value_grad = outs[:2]
    parts = time_swaps(outs[2:][::-1])
    bundles, _ = lax.optimization_barrier((bundles, parts[::-1]))
    collected = call(
        functools.partial(collect_kernel, chips), bundles, shape(bf16, chips * base, LANES)
    )
    weight_grad = call(
        functools.partial(weight_kernel, n_t, chips),
        [collected, over_cores(collected)] + packed_all,
        shape(f32, HD, 2 * width),
        [pltpu.VMEM((n_t, rows, HD), f32)],
        flops=4 * n_t * rows * width * HD,
    )
    query_grad, gate_grad = call(
        functools.partial(finish_kernel, n_t, chips, frames),
        [hot] + parts[::-1],
        [shape(bf16, rows, HD), shape(f32, levels, n_s * width)],
        [pltpu.VMEM((n_t, 2 * count, LANES), f32)],
    )
    if width != shard:
        weight_grad = without_padding(weight_grad, 2, shard)
        gate_grad = without_padding(gate_grad, n_s, shard)
    return (query_grad, key_grad, value_grad, weight_grad, gate_grad)


def solution(mesh):
    return jax.shard_map(
        body,
        mesh=mesh,
        in_specs=(
            P("tm", "space"),
            P("tm", "space"),
            P("tm", "space"),
            P("tm", "space"),
            P("tm", "space"),
            P("space", None),
            P(),
            P(),
            P(),
        ),
        out_specs=(P("tm", "space"), P("tm", "space"), P("tm", "space"), P("space", "tm"), P()),
        check_vma=False,
    )
```

time: 49.6 us -> 55 us (1.11)
  starting transfers between devices: 22.1 us -> 26.2 us
  waiting for transfers between devices: 17.1 us -> 14.1 us
  local copies, waits for them, and re-layouts: 0.84 us -> 3.21 us
  Pallas kernels: 8.69 us -> 9.64 us
  other arithmetic: 0.01 us -> 0.8 us
    ppermute x9, waiting for transfers between devices: 15 us -> 9.28 us  [over_time(): return lax.ppermute(x, 'tm', [(t, t ^ k) for t in range(n_t)])]
    ppermute x0 -> x3, starting transfers between devices: none -> 3.42 us  [over_space(): return lax.ppermute(x, 'space', [(s, s ^ k) for s in range(n_s)])]
    ppermute x0 -> x3, waiting for transfers between devices: none -> 2.51 us  [over_space(): return lax.ppermute(x, 'space', [(s, s ^ k) for s in range(n_s)])]
    unnamed x16 -> x12, local copies, waits for them, and re-layouts: 0.84 us -> 3.21 us
    pallas_call x10 -> x9, Pallas kernels: 8.69 us -> 9.64 us  [call(): pl.pallas_call(kernel, out_shape=out_shape, in_specs=[pl.BlockSpec(memory...]
    ppermute x3 -> x5, waiting for transfers between devices: 1.48 us -> 2.27 us  [over_cores(): return lax.ppermute(x, 'space', [(s, s ^ 1) for s in range(n_s)])]
    another operation x1, other arithmetic: 0.01 us -> 0.78 us  [body(): packed = jnp.stack([queries, saved_out])]
    ppermute x6, waiting for transfers between devices: 0.59 us -> 0.02 us  [over_chips(): lax.ppermute(x, 'space', [(s, s ^ 2 * k) for s in range(n_s)])]
  transfers between devices with their start and end apart: 18 -> 23, of which waited for: 9 -> 10; matrix products, arithmetic and copies ran while one was open for 0% -> 1% of each run, Pallas kernels for 11% -> 9%
where the time goes in v7:
time: 55 us; the launch traced here: 54.7 us
  starting transfers between devices  26.2 us (48%)
  waiting for transfers between devices  14.1 us (26%)
  Pallas kernels  9.64 us (18%)
  local copies, waits for them, and re-layouts  3.21 us (6%)
  other arithmetic  0.8 us (1%)
  between operations  0.77 us (1%)
    ppermute x9, starting transfers between devices, over_time(): return lax.ppermute(x, 'tm', [(t, t ^ k) for t in range(n_t)])  13.5 us
    pallas_call x9, Pallas kernels, call(): pl.pallas_call(kernel, out_shape=out_shape, in_specs=[pl.BlockSpec(memory...  9.64 us
    ppermute x9, waiting for transfers between devices, over_time(): return lax.ppermute(x, 'tm', [(t, t ^ k) for t in range(n_t)])  9.28 us
    ppermute x6, starting transfers between devices, over_chips(): lax.ppermute(x, 'space', [(s, s ^ 2 * k) for s in range(n_s)])  8.1 us
    ppermute x3, starting transfers between devices, over_space(): return lax.ppermute(x, 'space', [(s, s ^ k) for s in range(n_s)])  3.42 us
    unnamed x12, local copies, waits for them, and re-layouts  3.21 us
    ppermute x3, waiting for transfers between devices, over_space(): return lax.ppermute(x, 'space', [(s, s ^ k) for s in range(n_s)])  2.51 us
    ppermute x5, waiting for transfers between devices, over_cores(): return lax.ppermute(x, 'space', [(s, s ^ 1) for s in range(n_s)])  2.27 us
  transfers between devices with their start and end apart: 23, of which 10 were waited for; matrix products, arithmetic and copies ran while one was open for 1% of the time, Pallas kernels for 9%

profile of v7, /device:TPU:0, one launch (start us, length us, event | category | flops | bytes accessed | tf_op | source)
XLA Modules:
  0.0 54.7 jit_solution(4830368505648431706)
XLA Ops:
  0.6 3.0 %collective-permute-start.1 = (bf16[128,640]{1,0:T(8,128)(2,1)}, bf16[128,640]{1,0:T(8,128)(2,1)S(1)}, u32[]{:S(2)}, u32[]{:S(2)}) collective-permute-start(bf16[128,640]{1,0:T(8,128)(2,1)} %grad_in.1), channel_id=1, source_target_pairs={{0,2},{1,3},{2,0},{3,1},{4,6},{5,7},{6,4},{7,5},{8,10},{9,11},{10,... | collective-permute-start | bytes 491528 | tf_op jit(solution)/shard_map/ppermute | solution.py:350
  3.6 1.5 %collective-permute-start.2 = (bf16[128,640]{1,0:T(8,128)(2,1)}, bf16[128,640]{1,0:T(8,128)(2,1)S(1)}, u32[]{:S(2)}, u32[]{:S(2)}) collective-permute-start(bf16[128,640]{1,0:T(8,128)(2,1)} %grad_in.1), channel_id=1, source_target_pairs={{0,4},{1,5},{2,6},{3,7},{4,0},{5,1},{6,2},{7,3},{8,12},{9,13},{10,... | collective-permute-start | bytes 491528 | tf_op jit(solution)/shard_map/ppermute | solution.py:350
  6.0 2.1 %collective-permute-start.4 = (bf16[2,128,128]{2,1,0:T(8,128)(2,1)S(1)}, bf16[2,128,128]{2,1,0:T(8,128)(2,1)S(1)}, u32[]{:S(2)}, u32[]{:S(2)}) collective-permute-start(bf16[2,128,128]{2,1,0:T(8,128)(2,1)S(1)} %pad_maximum_fusion.packed.refs_0_), channel_id=1, source_target_pairs={{0,8},{8,0},{16,24},{24,16},{1,9},{9,1},{17,25},{25,17},{2,10},{10... | collective-permute-start | bytes 196616 | tf_op jit(solution)/shard_map/ppermute | solution.py:360
  8.0 2.6 %collective-permute-start.5 = (bf16[2,128,128]{2,1,0:T(8,128)(2,1)S(1)}, bf16[2,128,128]{2,1,0:T(8,128)(2,1)S(1)}, u32[]{:S(2)}, u32[]{:S(2)}) collective-permute-start(bf16[2,128,128]{2,1,0:T(8,128)(2,1)S(1)} %pad_maximum_fusion.packed.refs_0_), channel_id=1, source_target_pairs={{0,16},{8,24},{16,0},{24,8},{1,17},{9,25},{17,1},{25,9},{2,18},{10... | collective-permute-start | bytes 196616 | tf_op jit(solution)/shard_map/ppermute | solution.py:360
  10.6 2.7 %collective-permute-start.6 = (bf16[2,128,128]{2,1,0:T(8,128)(2,1)S(1)}, bf16[2,128,128]{2,1,0:T(8,128)(2,1)S(1)}, u32[]{:S(2)}, u32[]{:S(2)}) collective-permute-start(bf16[2,128,128]{2,1,0:T(8,128)(2,1)S(1)} %collective-permute-done.4.refs_1_), channel_id=1, source_target_pairs={{0,16},{8,24},{16,0},{24,8},{1,17},{9,25},{17,1},{25,9},{2,18},{10... | collective-permute-start | bytes 196616 | tf_op jit(solution)/shard_map/ppermute | solution.py:360
  13.3 1.0 %copy-done = f32[16,5120]{1,0:T(8,128)S(1)} copy-done((f32[16,5120]{1,0:T(8,128)S(1)}, f32[16,5120]{1,0:T(8,128)}, u32[]{:S(2)}) %copy-start) | copy-done | bytes 327704
  14.3 0.9 %copy-done.2 = bf16[128,640]{1,0:T(8,128)(2,1)S(1)} copy-done((bf16[128,640]{1,0:T(8,128)(2,1)S(1)}, bf16[128,640]{1,0:T(8,128)(2,1)}, u32[]{:S(2)}) %copy-start.2) | copy-done | bytes 163864
  19.5 3.1 %shard_map.129 = (bf16[128,128]{1,0:T(8,128)(2,1)S(1)}, f32[80,128]{1,0:T(8,128)S(1)}) custom-call(bf16[128,5120]{1,0:T(8,128)(2,1)} %weight_in.1, bf16[2,128,128]{2,1,0:T(8,128)(2,1)S(1)} %pad_maximum_fusion.packed.refs_0_, f32[8,2,640]{2,1,0:T(2,128)S(1)} %get-tuple-element.36.gate_a, bf16[128,640]{1,0:T(8,128)(2,1)S(1)} %get-tuple-element.37.refs_0_, ...), custom_call_target="tpu_custom_call" | custom-call | flops 335544320 | bytes 2727936 | tf_op jit(solution)/shard_map/pallas_call | solution.py:304
  23.9 2.6 %collective-permute-start.10 = (bf16[320,128]{1,0:T(8,128)(2,1)S(1)}, bf16[320,128]{1,0:T(8,128)(2,1)S(1)}, u32[]{:S(2)}, u32[]{:S(2)}) collective-permute-start(bf16[320,128]{1,0:T(8,128)(2,1)S(1)} %get-tuple-element.43), channel_id=1, source_target_pairs={{0,24},{8,16},{16,8},{24,0},{1,25},{9,17},{17,9},{25,1},{2,26},{10... | collective-permute-start | bytes 245768 | tf_op jit(solution)/shard_map/ppermute | solution.py:360
  27.0 1.4 %collective-permute-start.12 = (bf16[320,128]{1,0:T(8,128)(2,1)S(1)}, bf16[320,128]{1,0:T(8,128)(2,1)S(1)}, u32[]{:S(2)}, u32[]{:S(2)}) collective-permute-start(bf16[320,128]{1,0:T(8,128)(2,1)S(1)} %get-tuple-element.45), channel_id=1, source_target_pairs={{0,8},{8,0},{16,24},{24,16},{1,9},{9,1},{17,25},{25,17},{2,10},{10... | collective-permute-start | bytes 245768 | tf_op jit(solution)/shard_map/ppermute | solution.py:360
  28.4 1.6 %collective-permute-start.14 = (f32[80,128]{1,0:T(8,128)S(1)}, f32[80,128]{1,0:T(8,128)S(1)}, u32[]{:S(2)}, u32[]{:S(2)}) collective-permute-start(f32[80,128]{1,0:T(8,128)S(1)} %add.9), channel_id=1, source_target_pairs={{0,2},{1,3},{2,0},{3,1},{4,6},{5,7},{6,4},{7,5},{8,10},{9,11},{10,... | collective-permute-start | bytes 122888 | tf_op jit(solution)/shard_map/ppermute | solution.py:354
  30.0 2.5 %collective-permute-done.14 = f32[80,128]{1,0:T(8,128)S(1)} collective-permute-done((f32[80,128]{1,0:T(8,128)S(1)}, f32[80,128]{1,0:T(8,128)S(1)}, u32[]{:S(2)}, u32[]{:S(2)}) %collective-permute-start.14) | collective-permute-done | bytes 40992 | tf_op jit(solution)/shard_map/ppermute | solution.py:354
  32.5 1.5 %collective-permute-start.15 = (f32[80,128]{1,0:T(8,128)S(1)}, f32[80,128]{1,0:T(8,128)S(1)}, u32[]{:S(2)}, u32[]{:S(2)}) collective-permute-start(f32[80,128]{1,0:T(8,128)S(1)} %add.10), channel_id=1, source_target_pairs={{0,4},{1,5},{2,6},{3,7},{4,0},{5,1},{6,2},{7,3},{8,12},{9,13},{10,... | collective-permute-start | bytes 122888 | tf_op jit(solution)/shard_map/ppermute | solution.py:354
  34.0 0.9 %collective-permute-done.11.refs_1_.refs_5_ = bf16[320,128]{1,0:T(8,128)(2,1)S(1)} collective-permute-done((bf16[320,128]{1,0:T(8,128)(2,1)S(1)}, bf16[320,128]{1,0:T(8,128)(2,1)S(1)}, u32[]{:S(2)}, u32[]{:S(2)}) %collective-permute-start.11) | collective-permute-done | bytes 81952 | tf_op jit(solution)/shard_map/ppermute | solution.py:360
  34.9 1.6 %collective-permute-start.19 = (bf16[640,128]{1,0:T(8,128)(2,1)S(1)}, bf16[640,128]{1,0:T(8,128)(2,1)S(1)}, u32[]{:S(2)}, u32[]{:S(2)}) collective-permute-start(bf16[640,128]{1,0:T(8,128)(2,1)S(1)} %shard_map.132.refs_0_), channel_id=1, source_target_pairs={{0,2},{1,3},{2,0},{3,1},{4,6},{5,7},{6,4},{7,5},{8,10},{9,11},{10,... | collective-permute-start | bytes 491528 | tf_op jit(solution)/shard_map/ppermute | solution.py:350
  36.5 1.5 %collective-permute-start.20 = (bf16[640,128]{1,0:T(8,128)(2,1)S(1)}, bf16[640,128]{1,0:T(8,128)(2,1)S(1)}, u32[]{:S(2)}, u32[]{:S(2)}) collective-permute-start(bf16[640,128]{1,0:T(8,128)(2,1)S(1)} %shard_map.132.refs_0_), channel_id=1, source_target_pairs={{0,4},{1,5},{2,6},{3,7},{4,0},{5,1},{6,2},{7,3},{8,12},{9,13},{10,... | collective-permute-start | bytes 491528 | tf_op jit(solution)/shard_map/ppermute | solution.py:350
  38.5 2.4 %shard_map.133 = (bf16[1024,128]{1,0:T(8,128)(2,1)}, bf16[1024,128]{1,0:T(8,128)(2,1)}, bf16[208,128]{1,0:T(8,128)(2,1)S(1)}, bf16[208,128]{1,0:T(8,128)(2,1)S(1...) custom-call(f32[2,512]{1,0:T(2,128)S(1)} %get-tuple-element.47.bias, bf16[1024,128]{1,0:T(8,128)(2,1)S(1)} %copy-done.1, ...), custom_call_target="tpu_custom_call" | custom-call | flops 671088640 | bytes 1159168 | tf_op jit(solution)/shard_map/pallas_call | solution.py:304
  40.9 1.7 %collective-permute-start.16 = (bf16[208,128]{1,0:T(8,128)(2,1)S(1)}, bf16[208,128]{1,0:T(8,128)(2,1)S(1)}, u32[]{:S(2)}, u32[]{:S(2)}) collective-permute-start(bf16[208,128]{1,0:T(8,128)(2,1)S(1)} %get-tuple-element.49), channel_id=1, source_target_pairs={{0,24},{8,16},{16,8},{24,0},{1,25},{9,17},{17,9},{25,1},{2,26},{10... | collective-permute-start | bytes 159752 | tf_op jit(solution)/shard_map/ppermute | solution.py:360
  42.6 4.3 %collective-permute-done.16.refs_0_ = bf16[208,128]{1,0:T(8,128)(2,1)S(1)} collective-permute-done((bf16[208,128]{1,0:T(8,128)(2,1)S(1)}, bf16[208,128]{1,0:T(8,128)(2,1)S(1)}, u32[]{:S(2)}, u32[]{:S(2)}) %collective-permute-start.16) | collective-permute-done | bytes 53280 | tf_op jit(solution)/shard_map/ppermute | solution.py:360
  46.9 1.2 %collective-permute-done.17.refs_1_ = bf16[208,128]{1,0:T(8,128)(2,1)S(1)} collective-permute-done((bf16[208,128]{1,0:T(8,128)(2,1)S(1)}, bf16[208,128]{1,0:T(8,128)(2,1)S(1)}, u32[]{:S(2)}, u32[]{:S(2)}) %collective-permute-start.17) | collective-permute-done | bytes 53280 | tf_op jit(solution)/shard_map/ppermute | solution.py:360
  48.1 2.9 %collective-permute-done.18.refs_2_ = bf16[208,128]{1,0:T(8,128)(2,1)S(1)} collective-permute-done((bf16[208,128]{1,0:T(8,128)(2,1)S(1)}, bf16[208,128]{1,0:T(8,128)(2,1)S(1)}, u32[]{:S(2)}, u32[]{:S(2)}) %collective-permute-start.18) | collective-permute-done | bytes 53280 | tf_op jit(solution)/shard_map/ppermute | solution.py:360
  51.1 0.9 %shard_map.134 = (bf16[128,128]{1,0:T(8,128)(2,1)}, f32[16,5120]{1,0:T(8,128)}) custom-call(f32[8,16,128]{2,1,0:T(8,128)S(1)} %get-tuple-element.33.hot, bf16[208,128]{1,0:T(8,128)(2,1)S(1)} %collective-permute-done.16.refs_0_, bf16[208,128]{1,0:T(8,128)(2,1)S(1)} %collective-permute-done.17.refs_1_, bf16[208,128]{1,0:T(8,128)(2,1)S(1)} %collective-permute-done.18.refs_2_, ...), custom_call_target="tpu_custom_call" | custom-call | bytes 278528 | tf_op jit(solution)/shard_map/pallas_call | solution.py:304
  52.1 1.2 %collective-permute-done.22.other = bf16[2560,128]{1,0:T(8,128)(2,1)S(1)} collective-permute-done((bf16[2560,128]{1,0:T(8,128)(2,1)S(1)}, bf16[2560,128]{1,0:T(8,128)(2,1)S(1)}, u32[]{:S(2)}, u32[]{:S(2)}) %collective-permute-start.22) | collective-permute-done | bytes 655392 | tf_op jit(solution)/shard_map/ppermute | solution.py:357
  53.2 1.5 %shard_map.136 = f32[128,1280]{1,0:T(8,128)} custom-call(bf16[2560,128]{1,0:T(8,128)(2,1)S(1)} %shard_map.135.own, bf16[2560,128]{1,0:T(8,128)(2,1)S(1)} %collective-permute-done.22.other, bf16[2,128,128]{2,1,0:T(8,128)(2,1)S(1)} %pad_maximum_fusion.packed.refs_0_, bf16[2,128,128]{2,1,0:T(8,128)(2,1)S(1)} %collective-permute-done.4.refs_1_, ...), custom_call_target="tpu_custom_call" | custom-call | flops 167772160 | bytes 1572864 | tf_op jit(solution)/shard_map/pallas_call | solution.py:304
  (47 shorter events, 7.5 us)
Async XLA Ops:
  0.6 16.7 %collective-permute-start.1 = (bf16[128,640]{1,0:T(8,128)(2,1)}, bf16[128,640]{1,0:T(8,128)(2,1)S(1)}, u32[]{:S(2)}, u32[]{:S(2)}) collective-permute-start(bf16[128,640]{1,0:T(8,128)(2,1)} %grad_in.1), channel_id=1, source_target_pairs={{0,2},{1,3},{2,0},{3,1},{4,6},{5,7},{6,4},{7,5},{8,10},{9,11},{10,... | collective-permute-start | bytes 491528 | tf_op jit(solution)/shard_map/ppermute | solution.py:350
  3.6 13.7 %collective-permute-start.2 = (bf16[128,640]{1,0:T(8,128)(2,1)}, bf16[128,640]{1,0:T(8,128)(2,1)S(1)}, u32[]{:S(2)}, u32[]{:S(2)}) collective-permute-start(bf16[128,640]{1,0:T(8,128)(2,1)} %grad_in.1), channel_id=1, source_target_pairs={{0,4},{1,5},{2,6},{3,7},{4,0},{5,1},{6,2},{7,3},{8,12},{9,13},{10,... | collective-permute-start | bytes 491528 | tf_op jit(solution)/shard_map/ppermute | solution.py:350
  5.2 12.2 %collective-permute-start.3 = (bf16[128,640]{1,0:T(8,128)(2,1)}, bf16[128,640]{1,0:T(8,128)(2,1)S(1)}, u32[]{:S(2)}, u32[]{:S(2)}) collective-permute-start(bf16[128,640]{1,0:T(8,128)(2,1)} %grad_in.1), channel_id=1, source_target_pairs={{0,6},{1,7},{2,4},{3,5},{4,2},{5,3},{6,0},{7,1},{8,14},{9,15},{10,... | collective-permute-start | bytes 491528 | tf_op jit(solution)/shard_map/ppermute | solution.py:350
  6.0 4.7 %collective-permute-start.4 = (bf16[2,128,128]{2,1,0:T(8,128)(2,1)S(1)}, bf16[2,128,128]{2,1,0:T(8,128)(2,1)S(1)}, u32[]{:S(2)}, u32[]{:S(2)}) collective-permute-start(bf16[2,128,128]{2,1,0:T(8,128)(2,1)S(1)} %pad_maximum_fusion.packed.refs_0_), channel_id=1, source_target_pairs={{0,8},{8,0},{16,24},{24,16},{1,9},{9,1},{17,25},{25,17},{2,10},{10... | collective-permute-start | bytes 196616 | tf_op jit(solution)/shard_map/ppermute | solution.py:360
  8.0 9.2 %collective-permute-start.5 = (bf16[2,128,128]{2,1,0:T(8,128)(2,1)S(1)}, bf16[2,128,128]{2,1,0:T(8,128)(2,1)S(1)}, u32[]{:S(2)}, u32[]{:S(2)}) collective-permute-start(bf16[2,128,128]{2,1,0:T(8,128)(2,1)S(1)} %pad_maximum_fusion.packed.refs_0_), channel_id=1, source_target_pairs={{0,16},{8,24},{16,0},{24,8},{1,17},{9,25},{17,1},{25,9},{2,18},{10... | collective-permute-start | bytes 196616 | tf_op jit(solution)/shard_map/ppermute | solution.py:360
  10.6 6.7 %collective-permute-start.6 = (bf16[2,128,128]{2,1,0:T(8,128)(2,1)S(1)}, bf16[2,128,128]{2,1,0:T(8,128)(2,1)S(1)}, u32[]{:S(2)}, u32[]{:S(2)}) collective-permute-start(bf16[2,128,128]{2,1,0:T(8,128)(2,1)S(1)} %collective-permute-done.4.refs_1_), channel_id=1, source_target_pairs={{0,16},{8,24},{16,0},{24,8},{1,17},{9,25},{17,1},{25,9},{2,18},{10... | collective-permute-start | bytes 196616 | tf_op jit(solution)/shard_map/ppermute | solution.py:360
  17.2 1.5 %collective-permute-start = (bf16[128,640]{1,0:T(8,128)(2,1)S(1)}, bf16[128,640]{1,0:T(8,128)(2,1)S(1)}, u32[]{:S(2)}, u32[]{:S(2)}) collective-permute-start(bf16[128,640]{1,0:T(8,128)(2,1)S(1)} %copy-done.2), channel_id=1, source_target_pairs={{0,1},{1,0},{2,3},{3,2},{4,5},{5,4},{6,7},{7,6},{8,9},{9,8},{10,11... | collective-permute-start | bytes 491528 | tf_op jit(solution)/shard_map/ppermute | solution.py:357
  17.3 1.6 %collective-permute-start.7 = (bf16[128,640]{1,0:T(8,128)(2,1)S(1)}, bf16[128,640]{1,0:T(8,128)(2,1)S(1)}, u32[]{:S(2)}, u32[]{:S(2)}) collective-permute-start(bf16[128,640]{1,0:T(8,128)(2,1)S(1)} %collective-permute-done.1.refs_2_.refs_1_), channel_id=1, source_target_pairs={{0,1},{1,0},{2,3},{3,2},{4,5},{5,4},{6,7},{7,6},{8,9},{9,8},{10,11... | collective-permute-start | bytes 491528 | tf_op jit(solution)/shard_map/ppermute | solution.py:357
  17.9 1.4 %collective-permute-start.8 = (bf16[128,640]{1,0:T(8,128)(2,1)S(1)}, bf16[128,640]{1,0:T(8,128)(2,1)S(1)}, u32[]{:S(2)}, u32[]{:S(2)}) collective-permute-start(bf16[128,640]{1,0:T(8,128)(2,1)S(1)} %collective-permute-done.2.refs_4_.refs_2_), channel_id=1, source_target_pairs={{0,1},{1,0},{2,3},{3,2},{4,5},{5,4},{6,7},{7,6},{8,9},{9,8},{10,11... | collective-permute-start | bytes 491528 | tf_op jit(solution)/shard_map/ppermute | solution.py:357
  17.9 1.6 %collective-permute-start.9 = (bf16[128,640]{1,0:T(8,128)(2,1)S(1)}, bf16[128,640]{1,0:T(8,128)(2,1)S(1)}, u32[]{:S(2)}, u32[]{:S(2)}) collective-permute-start(bf16[128,640]{1,0:T(8,128)(2,1)S(1)} %collective-permute-done.3.refs_6_.refs_3_), channel_id=1, source_target_pairs={{0,1},{1,0},{2,3},{3,2},{4,5},{5,4},{6,7},{7,6},{8,9},{9,8},{10,11... | collective-permute-start | bytes 491528 | tf_op jit(solution)/shard_map/ppermute | solution.py:357
  22.7 15.8 %copy-start.5 = (bf16[1024,128]{1,0:T(8,128)(2,1)S(1)}, bf16[1024,128]{1,0:T(8,128)(2,1)}, u32[]{:S(2)}) copy-start(bf16[1024,128]{1,0:T(8,128)(2,1)} %values.1) | copy-start | bytes 786436
  22.7 5.7 %collective-permute-start.13 = (f32[80,128]{1,0:T(8,128)S(1)}, f32[80,128]{1,0:T(8,128)S(1)}, u32[]{:S(2)}, u32[]{:S(2)}) collective-permute-start(f32[80,128]{1,0:T(8,128)S(1)} %get-tuple-element.48), channel_id=1, source_target_pairs={{0,1},{1,0},{2,3},{3,2},{4,5},{5,4},{6,7},{7,6},{8,9},{9,8},{10,11... | collective-permute-start | bytes 122888 | tf_op jit(solution)/shard_map/ppermute | solution.py:354
  23.9 10.1 %collective-permute-start.10 = (bf16[320,128]{1,0:T(8,128)(2,1)S(1)}, bf16[320,128]{1,0:T(8,128)(2,1)S(1)}, u32[]{:S(2)}, u32[]{:S(2)}) collective-permute-start(bf16[320,128]{1,0:T(8,128)(2,1)S(1)} %get-tuple-element.43), channel_id=1, source_target_pairs={{0,24},{8,16},{16,8},{24,0},{1,25},{9,17},{17,9},{25,1},{2,26},{10... | collective-permute-start | bytes 245768 | tf_op jit(solution)/shard_map/ppermute | solution.py:360
  26.5 8.3 %collective-permute-start.11 = (bf16[320,128]{1,0:T(8,128)(2,1)S(1)}, bf16[320,128]{1,0:T(8,128)(2,1)S(1)}, u32[]{:S(2)}, u32[]{:S(2)}) collective-permute-start(bf16[320,128]{1,0:T(8,128)(2,1)S(1)} %get-tuple-element.44), channel_id=1, source_target_pairs={{0,16},{8,24},{16,0},{24,8},{1,17},{9,25},{17,1},{25,9},{2,18},{10... | collective-permute-start | bytes 245768 | tf_op jit(solution)/shard_map/ppermute | solution.py:360
  27.0 7.8 %collective-permute-start.12 = (bf16[320,128]{1,0:T(8,128)(2,1)S(1)}, bf16[320,128]{1,0:T(8,128)(2,1)S(1)}, u32[]{:S(2)}, u32[]{:S(2)}) collective-permute-start(bf16[320,128]{1,0:T(8,128)(2,1)S(1)} %get-tuple-element.45), channel_id=1, source_target_pairs={{0,8},{8,0},{16,24},{24,16},{1,9},{9,1},{17,25},{25,17},{2,10},{10... | collective-permute-start | bytes 245768 | tf_op jit(solution)/shard_map/ppermute | solution.py:360
  28.4 4.1 %collective-permute-start.14 = (f32[80,128]{1,0:T(8,128)S(1)}, f32[80,128]{1,0:T(8,128)S(1)}, u32[]{:S(2)}, u32[]{:S(2)}) collective-permute-start(f32[80,128]{1,0:T(8,128)S(1)} %add.9), channel_id=1, source_target_pairs={{0,2},{1,3},{2,0},{3,1},{4,6},{5,7},{6,4},{7,5},{8,10},{9,11},{10,... | collective-permute-start | bytes 122888 | tf_op jit(solution)/shard_map/ppermute | solution.py:354
  32.5 6.0 %collective-permute-start.15 = (f32[80,128]{1,0:T(8,128)S(1)}, f32[80,128]{1,0:T(8,128)S(1)}, u32[]{:S(2)}, u32[]{:S(2)}) collective-permute-start(f32[80,128]{1,0:T(8,128)S(1)} %add.10), channel_id=1, source_target_pairs={{0,4},{1,5},{2,6},{3,7},{4,0},{5,1},{6,2},{7,3},{8,12},{9,13},{10,... | collective-permute-start | bytes 122888 | tf_op jit(solution)/shard_map/ppermute | solution.py:354
  34.9 16.1 %collective-permute-start.19 = (bf16[640,128]{1,0:T(8,128)(2,1)S(1)}, bf16[640,128]{1,0:T(8,128)(2,1)S(1)}, u32[]{:S(2)}, u32[]{:S(2)}) collective-permute-start(bf16[640,128]{1,0:T(8,128)(2,1)S(1)} %shard_map.132.refs_0_), channel_id=1, source_target_pairs={{0,2},{1,3},{2,0},{3,1},{4,6},{5,7},{6,4},{7,5},{8,10},{9,11},{10,... | collective-permute-start | bytes 491528 | tf_op jit(solution)/shard_map/ppermute | solution.py:350
  36.5 14.5 %collective-permute-start.20 = (bf16[640,128]{1,0:T(8,128)(2,1)S(1)}, bf16[640,128]{1,0:T(8,128)(2,1)S(1)}, u32[]{:S(2)}, u32[]{:S(2)}) collective-permute-start(bf16[640,128]{1,0:T(8,128)(2,1)S(1)} %shard_map.132.refs_0_), channel_id=1, source_target_pairs={{0,4},{1,5},{2,6},{3,7},{4,0},{5,1},{6,2},{7,3},{8,12},{9,13},{10,... | collective-permute-start | bytes 491528 | tf_op jit(solution)/shard_map/ppermute | solution.py:350
  38.0 13.0 %collective-permute-start.21 = (bf16[640,128]{1,0:T(8,128)(2,1)S(1)}, bf16[640,128]{1,0:T(8,128)(2,1)S(1)}, u32[]{:S(2)}, u32[]{:S(2)}) collective-permute-start(bf16[640,128]{1,0:T(8,128)(2,1)S(1)} %shard_map.132.refs_0_), channel_id=1, source_target_pairs={{0,6},{1,7},{2,4},{3,5},{4,2},{5,3},{6,0},{7,1},{8,14},{9,15},{10,... | collective-permute-start | bytes 491528 | tf_op jit(solution)/shard_map/ppermute | solution.py:350
  40.9 5.9 %collective-permute-start.16 = (bf16[208,128]{1,0:T(8,128)(2,1)S(1)}, bf16[208,128]{1,0:T(8,128)(2,1)S(1)}, u32[]{:S(2)}, u32[]{:S(2)}) collective-permute-start(bf16[208,128]{1,0:T(8,128)(2,1)S(1)} %get-tuple-element.49), channel_id=1, source_target_pairs={{0,24},{8,16},{16,8},{24,0},{1,25},{9,17},{17,9},{25,1},{2,26},{10... | collective-permute-start | bytes 159752 | tf_op jit(solution)/shard_map/ppermute | solution.py:360
  42.6 5.5 %collective-permute-start.17 = (bf16[208,128]{1,0:T(8,128)(2,1)S(1)}, bf16[208,128]{1,0:T(8,128)(2,1)S(1)}, u32[]{:S(2)}, u32[]{:S(2)}) collective-permute-start(bf16[208,128]{1,0:T(8,128)(2,1)S(1)} %get-tuple-element.50), channel_id=1, source_target_pairs={{0,16},{8,24},{16,0},{24,8},{1,17},{9,25},{17,1},{25,9},{2,18},{10... | collective-permute-start | bytes 159752 | tf_op jit(solution)/shard_map/ppermute | solution.py:360
  46.9 4.1 %collective-permute-start.18 = (bf16[208,128]{1,0:T(8,128)(2,1)S(1)}, bf16[208,128]{1,0:T(8,128)(2,1)S(1)}, u32[]{:S(2)}, u32[]{:S(2)}) collective-permute-start(bf16[208,128]{1,0:T(8,128)(2,1)S(1)} %get-tuple-element.51), channel_id=1, source_target_pairs={{0,8},{8,0},{16,24},{24,16},{1,9},{9,1},{17,25},{25,17},{2,10},{10... | collective-permute-start | bytes 159752 | tf_op jit(solution)/shard_map/ppermute | solution.py:360
  51.1 2.2 %collective-permute-start.22 = (bf16[2560,128]{1,0:T(8,128)(2,1)S(1)}, bf16[2560,128]{1,0:T(8,128)(2,1)S(1)}, u32[]{:S(2)}, u32[]{:S(2)}) collective-permute-start(bf16[2560,128]{1,0:T(8,128)(2,1)S(1)} %shard_map.135.own), channel_id=1, source_target_pairs={{0,1},{1,0},{2,3},{3,2},{4,5},{5,4},{6,7},{7,6},{8,9},{9,8},{10,11... | collective-permute-start | bytes 1966088 | tf_op jit(solution)/shard_map/ppermute | solution.py:357
  (5 other events, 6.7 us)

commit v8 on v5

--- a/solution.py
+++ b/solution.py
@@ -79,9 +79,9 @@
             columns = pl.ds(pl.multiple_of((2 * (chip ^ k) + core) * width, LANES), width)
             gate_a[k, r : r + 1, :] = gate[pl.ds(level, 1), columns]
     mine = pl.ds(pl.multiple_of((2 * t + core) * width, LANES), width)
-    for k in range(n_t):
-        level = levels[(t ^ k) * frames + chip * (rows // chips) // QF]
-        gate_b[k] = gate[pl.ds(level, 1), mine]
+    for r in range(frames):
+        level = levels[(t ^ chip) * frames + r]
+        gate_b[r : r + 1, :] = gate[pl.ds(level, 1), mine]
 
 
 def stats_kernel(n_t, bias, keys, *refs):
@@ -101,8 +101,14 @@
 
 
 def head_kernel(chips, frames, packed, kept, received, gate_a, *refs):
-    pieces, (mine, other, terms) = refs[:chips], refs[chips:]
-    _, chip, _ = place()
+    pieces, (mine, other, terms, move) = refs[:chips], refs[chips:]
+    t, chip, _ = place()
+    for k in range(chips):
+
+        @pl.when(t == k)
+        def _():
+            move[...] = pieces[k][...]
+
     width = pieces[0].shape[1]
     tiles = width // LANES
     saved = jnp.concatenate([packed[1], received[:, chips * width : chips * width + HD]], axis=1)
@@ -129,10 +135,9 @@
     other[...] = head[:, HD:]
 
 
-def sections(rows, chips, tiles, n_t, count):
+def sections(rows, n_t, count):
     starts = [0, rows]
     starts.append(starts[-1] + -(-SPLIT * 2 * n_t // 16) * 16)
-    starts.append(starts[-1] + tiles * (rows // chips))
     starts.append(starts[-1] + -(-count // 16) * 16)
     return starts
 
@@ -143,47 +148,31 @@
     return jnp.concatenate([x, jnp.zeros((rows - x.shape[0], x.shape[1]), x.dtype)], axis=0)
 
 
-def join_kernel(n_t, chips, starts, mine, received, stats, terms, *refs):
-    pieces, outs, (wide, held) = refs[:chips], refs[chips : chips + n_t][::-1], refs[chips + n_t :]
-    t, chip, _ = place()
-    part, tiles = held.shape[1], held.shape[2] // LANES
-    for k in range(chips):
-        wide[...] = pieces[k][...].astype(jnp.float32)
-        held[k] = wide[pl.ds(pl.multiple_of(chip * part, part), part), :]
-    head = (mine[...] + received[...]).astype(jnp.bfloat16)
+def join_kernel(starts, mine, received, stats, terms, out):
+    out[: starts[1], :] = (mine[...] + received[...]).astype(jnp.bfloat16)
     rest = stats[...]
     split = []
     for _ in range(SPLIT):
         piece = rest.astype(jnp.bfloat16).astype(jnp.float32)
         split.append(piece)
         rest = rest - piece
-    split = padded(jnp.concatenate(split, axis=0), starts[2] - starts[1]).astype(jnp.bfloat16)
-    last = padded(terms[...], starts[4] - starts[3]).astype(jnp.bfloat16)
-    for k in range(n_t):
-        rows = held[chip ^ t ^ k]
-        rows = jnp.concatenate([rows[:, j * LANES : (j + 1) * LANES] for j in range(tiles)], axis=0)
-        outs[k][: starts[1], :] = head
-        outs[k][starts[1] : starts[2], :] = split
-        outs[k][starts[2] : starts[3], :] = rows.astype(jnp.bfloat16)
-        outs[k][starts[3] :, :] = last
-
-
-def bundle_kernel(n_t, starts, count, gate_b, *refs):
-    heads, out = refs[:n_t][::-1], refs[n_t]
-    tiles = gate_b.shape[2] // LANES
-    part = (starts[3] - starts[2]) // tiles
-    wide = [heads[k][starts[2] : starts[3], :].astype(jnp.float32) for k in range(n_t)]
+    split = padded(jnp.concatenate(split, axis=0), starts[2] - starts[1])
+    out[starts[1] : starts[2], :] = split.astype(jnp.bfloat16)
+    out[starts[2] :, :] = padded(terms[...], starts[3] - starts[2]).astype(jnp.bfloat16)
+
+
+def bundle_kernel(n_t, frames, starts, count, gate_b, moved, *refs):
+    heads, out = refs[:n_t], refs[n_t]
+    rows, width = moved.shape
+    tiles = width // LANES
+    wide = moved[...].astype(jnp.float32)
+    gated = jnp.concatenate(
+        [wide[r * QF : (r + 1) * QF] * gate_b[r : r + 1, :] for r in range(frames)], axis=0
+    ).astype(jnp.bfloat16)
     for j in range(tiles):
-        gated = jnp.concatenate(
-            [
-                wide[k][j * part : (j + 1) * part] * gate_b[k, :, j * LANES : (j + 1) * LANES]
-                for k in range(n_t)
-            ],
-            axis=0,
-        )
-        out[j * n_t * part : (j + 1) * n_t * part, :] = gated.astype(jnp.bfloat16)
-    terms = [heads[k][starts[3] :, :].astype(jnp.float32)[:count] for k in range(n_t)]
-    out[tiles * n_t * part :, :] = jnp.concatenate(terms, axis=0).astype(jnp.bfloat16)
+        out[j * rows : (j + 1) * rows, :] = gated[:, j * LANES : (j + 1) * LANES]
+    terms = [heads[k][starts[2] :, :].astype(jnp.float32)[:count] for k in range(n_t)]
+    out[tiles * rows :, :] = jnp.concatenate(terms, axis=0).astype(jnp.bfloat16)
 
 
 def collect_kernel(chips, base, *refs):
@@ -202,7 +191,7 @@
 
 
 def grads_kernel(n_t, bias, keys, values, *refs):
-    packed, heads = refs[:n_t], refs[n_t : 2 * n_t][::-1]
+    packed, heads = refs[:n_t], refs[n_t : 2 * n_t]
     key_out, value_out = refs[2 * n_t : 2 * n_t + 2]
     outs = refs[2 * n_t + 2 : 3 * n_t + 2][::-1]
     key_acc, value_acc = refs[3 * n_t + 2 :]
@@ -267,15 +256,11 @@
     width = weight_out.shape[1] // 2
     tiles = width // LANES
     rows = saved.shape[1]
-    part = rows // chips
-    base = tiles * n_t * part
+    base = tiles * rows
     for k in range(n_t):
         saved[k] = packed[k][1].astype(jnp.float32)
-    ordered = []
-    for c in range(chips):
-        mine = pl.ds(pl.multiple_of((chip ^ c) * part, part), part)
-        ordered += [saved[k, mine, :] for k in range(n_t)]
-    ordered = jnp.transpose(jnp.concatenate(ordered, axis=0)).astype(jnp.bfloat16)
+    ordered = jnp.concatenate([saved[chip ^ c] for c in range(chips)], axis=0)
+    ordered = jnp.transpose(ordered).astype(jnp.bfloat16)
     count = (own.shape[0] - chips * base) // 2
     each = count // n_t
     for ref, half in ((own, core), (other, 1 - core)):
@@ -283,7 +268,7 @@
             [
                 jnp.concatenate(
                     [
-                        ref[c * base + j * n_t * part : c * base + (j + 1) * n_t * part, :]
+                        ref[c * base + j * rows : c * base + (j + 1) * rows, :]
                         for c in range(chips)
                     ],
                     axis=0,
@@ -373,9 +358,8 @@
         return lax.ppermute(x, "tm", [(t, t ^ k) for t in range(n_t)])
 
     tiles = width // LANES
-    part = rows // chips
     count = chips * frames * tiles
-    starts = sections(rows, chips, tiles, n_t, count)
+    starts = sections(rows, n_t, count)
 
     def time_swaps(messages):
         got = {k: over_time(messages[k], k) for k in range(n_t - 1, 0, -1)}
@@ -402,15 +386,21 @@
         [
             shape(f32, frames, n_t * rows),
             shape(f32, chips, frames, width),
-            shape(f32, n_t, 1, width),
+            shape(f32, frames, width),
             shape(f32, n_t * frames, levels, LANES),
         ],
         in_smem=2,
     )
-    mine, other, terms = call(
+    kept, _ = lax.optimization_barrier((kept, packed_all[1 : n_t // 2 + 1]))
+    mine, other, terms, to_move = call(
         functools.partial(head_kernel, chips, frames),
         [packed, kept, received, gate_a] + pieces,
-        [shape(f32, rows, HD), shape(f32, rows, HD), shape(f32, count, LANES)],
+        [
+            shape(f32, rows, HD),
+            shape(f32, rows, HD),
+            shape(f32, count, LANES),
+            shape(bf16, rows, width),
+        ],
         flops=4 * rows * chips * width * 2 * HD,
     )
     later_bias, _ = lax.optimization_barrier((bias, mine))
@@ -420,24 +410,27 @@
         shape(f32, 2 * n_t, LANES),
         flops=2 * n_t * rows * k_rows * HD,
     )
-    heads = call(
-        functools.partial(join_kernel, n_t, chips, starts),
-        [mine, over_cores(other), stats, terms] + pieces,
-        [shape(bf16, starts[-1], LANES)] * n_t,
-        [pltpu.VMEM((rows, width), f32), pltpu.VMEM((chips, part, width), f32)],
-    )
-    heads_all = time_swaps(heads[::-1])
-    base = tiles * n_t * part
+    moves = [
+        (t * n_s + s, (t ^ (s // 2)) * n_s + s) for t in range(n_t) for s in range(n_s)
+    ]
+    moved = lax.ppermute(to_move, ("tm", "space"), moves)
+    message = call(
+        functools.partial(join_kernel, starts),
+        [mine, over_cores(other), stats, terms],
+        shape(bf16, starts[-1], LANES),
+    )
+    heads_all = time_swaps([message] * n_t)
+    base = tiles * rows
     bundle = call(
-        functools.partial(bundle_kernel, n_t, starts, count),
-        [gate_b] + heads_all[::-1],
+        functools.partial(bundle_kernel, n_t, frames, starts, count),
+        [gate_b, moved] + heads_all,
         shape(bf16, base + n_t * count, LANES),
     )
     bundles = over_chips(bundle)
     later_bias, _ = lax.optimization_barrier((bias, bundle))
     outs = call(
         functools.partial(grads_kernel, n_t),
-        [later_bias, keys, values] + packed_all + heads_all[::-1],
+        [later_bias, keys, values] + packed_all + heads_all,
         [shape(bf16, k_rows, HD)] * 2 + [shape(bf16, HD, rows)] * n_t,
         [pltpu.VMEM((k_rows, HD), f32)] * 2,
         flops=10 * n_t * rows * k_rows * HD,

time: 49.6 us -> 60 us (1.21)
  starting transfers between devices: 22.1 us -> 31.2 us
  waiting for transfers between devices: 17.1 us -> 18.4 us
    ppermute x6, starting transfers between devices: 7.72 us -> 15.1 us  [over_chips(): lax.ppermute(x, 'space', [(s, s ^ 2 * k) for s in range(n_s)])]
    ppermute x9, waiting for transfers between devices: 15 us -> 16.3 us  [over_time(): return lax.ppermute(x, 'tm', [(t, t ^ k) for t in range(n_t)])]
    ppermute x9, starting transfers between devices: 13.7 us -> 14.8 us  [over_time(): return lax.ppermute(x, 'tm', [(t, t ^ k) for t in range(n_t)])]
    ppermute x0 -> x1, starting transfers between devices: none -> 0.67 us  [body(): moved = lax.ppermute(to_move, ('tm', 'space'), moves)]
  transfers between devices with their start and end apart: 18 -> 19, of which waited for: 9 -> 10; matrix products, arithmetic and copies ran while one was open for 0% -> 0% of each run, Pallas kernels for 11% -> 8%
where the time goes in v8:
time: 60 us; the launch traced here: 59.8 us
  starting transfers between devices  31.2 us (52%)
  waiting for transfers between devices  18.4 us (31%)
  Pallas kernels  8.57 us (14%)
  local copies, waits for them, and re-layouts  0.84 us (1%)
  between operations  0.76 us (1%)
    ppermute x9, waiting for transfers between devices, over_time(): return lax.ppermute(x, 'tm', [(t, t ^ k) for t in range(n_t)])  16.3 us
    ppermute x6, starting transfers between devices, over_chips(): lax.ppermute(x, 'space', [(s, s ^ 2 * k) for s in range(n_s)])  15.1 us
    ppermute x9, starting transfers between devices, over_time(): return lax.ppermute(x, 'tm', [(t, t ^ k) for t in range(n_t)])  14.8 us
    pallas_call x10, Pallas kernels, call(): pl.pallas_call(kernel, out_shape=out_shape, in_specs=[pl.BlockSpec(memory...  8.57 us
    ppermute x3, waiting for transfers between devices, over_cores(): return lax.ppermute(x, 'space', [(s, s ^ 1) for s in range(n_s)])  1.48 us
  transfers between devices with their start and end apart: 19, of which 10 were waited for; matrix products, arithmetic and copies ran while one was open for 0% of the time, Pallas kernels for 8%

profile of v8, /device:TPU:0, one launch (start us, length us, event | category | flops | bytes accessed | tf_op | source)
XLA Modules:
  0.0 59.8 jit_solution(14413099167530173805)
XLA Ops:
  0.7 0.8 %copy-done.3 = bf16[128,128]{1,0:T(8,128)(2,1)S(1)} copy-done((bf16[128,128]{1,0:T(8,128)(2,1)S(1)}, bf16[128,128]{1,0:T(8,128)(2,1)}, u32[]{:S(2)}) %copy-start.3) | copy-done | bytes 32792
  1.5 1.5 %shard_map.128 = (bf16[4,128,640]{2,1,0:T(8,128)(2,1)S(1)}, bf16[128,2688]{1,0:T(8,128)(2,1)S(1)}) custom-call(bf16[128,5120]{1,0:T(8,128)(2,1)} %weight_in.1, bf16[128,128]{1,0:T(8,128)(2,1)S(1)} %copy-done.3), custom_call_target="tpu_custom_call" | custom-call | bytes 1343488 | tf_op jit(solution)/shard_map/pallas_call | solution.py:306
  3.5 2.6 %collective-permute-start.4 = (bf16[128,640]{1,0:T(8,128)(2,1)S(1)}, bf16[128,640]{1,0:T(8,128)(2,1)S(1)}, u32[]{:S(2)}, u32[]{:S(2)}) collective-permute-start(bf16[128,640]{1,0:T(8,128)(2,1)S(1)} %copy-done.2), channel_id=1, source_target_pairs={{0,4},{1,5},{2,6},{3,7},{4,0},{5,1},{6,2},{7,3},{8,12},{9,13},{10,... | collective-permute-start | bytes 491528 | tf_op jit(solution)/shard_map/ppermute | solution.py:351
  6.1 1.5 %collective-permute-start.3 = (bf16[128,640]{1,0:T(8,128)(2,1)S(1)}, bf16[128,640]{1,0:T(8,128)(2,1)S(1)}, u32[]{:S(2)}, u32[]{:S(2)}) collective-permute-start(bf16[128,640]{1,0:T(8,128)(2,1)S(1)} %copy-done.2), channel_id=1, source_target_pairs={{0,2},{1,3},{2,0},{3,1},{4,6},{5,7},{6,4},{7,5},{8,10},{9,11},{10,... | collective-permute-start | bytes 491528 | tf_op jit(solution)/shard_map/ppermute | solution.py:351
  7.7 3.1 %collective-permute-start.2 = (bf16[2,128,128]{2,1,0:T(8,128)(2,1)S(1)}, bf16[2,128,128]{2,1,0:T(8,128)(2,1)S(1)}, u32[]{:S(2)}, u32[]{:S(2)}) collective-permute-start(bf16[2,128,128]{2,1,0:T(8,128)(2,1)S(1)} %pad_maximum_fusion.packed.refs_0_), channel_id=1, source_target_pairs={{0,16},{8,24},{16,0},{24,8},{1,17},{9,25},{17,1},{25,9},{2,18},{10... | collective-permute-start | bytes 196616 | tf_op jit(solution)/shard_map/ppermute | solution.py:358
  10.8 1.6 %collective-permute-start.1 = (bf16[2,128,128]{2,1,0:T(8,128)(2,1)S(1)}, bf16[2,128,128]{2,1,0:T(8,128)(2,1)S(1)}, u32[]{:S(2)}, u32[]{:S(2)}) collective-permute-start(bf16[2,128,128]{2,1,0:T(8,128)(2,1)S(1)} %pad_maximum_fusion.packed.refs_0_), channel_id=1, source_target_pairs={{0,8},{8,0},{16,24},{24,16},{1,9},{9,1},{17,25},{25,17},{2,10},{10... | collective-permute-start | bytes 196616 | tf_op jit(solution)/shard_map/ppermute | solution.py:358
  13.0 0.8 %collective-permute-done.2.refs_2_ = bf16[2,128,128]{2,1,0:T(8,128)(2,1)S(1)} collective-permute-done((bf16[2,128,128]{2,1,0:T(8,128)(2,1)S(1)}, bf16[2,128,128]{2,1,0:T(8,128)(2,1)S(1)}, u32[]{:S(2)}, u32[]{:S(2)}) %collective-permute-start.2) | collective-permute-done | bytes 65568 | tf_op jit(solution)/shard_map/ppermute | solution.py:358
  13.8 1.2 %collective-permute-done.1.refs_1_ = bf16[2,128,128]{2,1,0:T(8,128)(2,1)S(1)} collective-permute-done((bf16[2,128,128]{2,1,0:T(8,128)(2,1)S(1)}, bf16[2,128,128]{2,1,0:T(8,128)(2,1)S(1)}, u32[]{:S(2)}, u32[]{:S(2)}) %collective-permute-start.1) | collective-permute-done | bytes 65568 | tf_op jit(solution)/shard_map/ppermute | solution.py:358
  15.6 0.8 %shard_map.130 = (f32[128,128]{1,0:T(8,128)S(1)}, f32[128,128]{1,0:T(8,128)S(1)}, f32[40,128]{1,0:T(8,128)S(1)}, bf16[128,640]{1,0:T(8,128)(2,1)S(1)}) custom-call(bf16[2,128,128]{2,1,0:T(8,128)(2,1)S(1)} %pad_maximum_fusion.packed.refs_0_, bf16[4,128,640]{2,1,0:T(8,128)(2,1)S(1)} %get-tuple-element.38.kept, ...), custom_call_target="tpu_custom_call" | custom-call | flops 335544320 | bytes 2084864 | tf_op jit(solution)/shard_map/pallas_call | solution.py:306
  17.1 2.9 %collective-permute-start.8 = (bf16[2,128,128]{2,1,0:T(8,128)(2,1)S(1)}, bf16[2,128,128]{2,1,0:T(8,128)(2,1)S(1)}, u32[]{:S(2)}, u32[]{:S(2)}) collective-permute-start(bf16[2,128,128]{2,1,0:T(8,128)(2,1)S(1)} %collective-permute-done.1.refs_1_), channel_id=1, source_target_pairs={{0,16},{8,24},{16,0},{24,8},{1,17},{9,25},{17,1},{25,9},{2,18},{10... | collective-permute-start | bytes 196616 | tf_op jit(solution)/shard_map/ppermute | solution.py:358
  20.0 2.6 %collective-permute-done.8.refs_3_ = bf16[2,128,128]{2,1,0:T(8,128)(2,1)S(1)} collective-permute-done((bf16[2,128,128]{2,1,0:T(8,128)(2,1)S(1)}, bf16[2,128,128]{2,1,0:T(8,128)(2,1)S(1)}, u32[]{:S(2)}, u32[]{:S(2)}) %collective-permute-start.8) | collective-permute-done | bytes 65568 | tf_op jit(solution)/shard_map/ppermute | solution.py:358
  22.6 0.8 %shard_map.131.stats = f32[8,128]{1,0:T(8,128)S(1)} custom-call(f32[2,512]{1,0:T(2,128)S(1)} %get-tuple-element.45.bias, bf16[1024,128]{1,0:T(8,128)(2,1)S(1)} %copy-done.1, bf16[2,128,128]{2,1,0:T(8,128)(2,1)S(1)} %pad_maximum_fusion.packed.refs_0_, bf16[2,128,128]{2,1,0:T(8,128)(2,1)S(1)} %collective-permute-done.1.refs_1_, ...), custom_call_target="tpu_custom_call" | custom-call | flops 134217728 | bytes 528384 | tf_op jit(solution)/shard_map/pallas_call | solution.py:306
  23.4 4.2 %collective-permute-start.11 = (bf16[208,128]{1,0:T(8,128)(2,1)S(1)}, bf16[208,128]{1,0:T(8,128)(2,1)S(1)}, u32[]{:S(2)}, u32[]{:S(2)}) collective-permute-start(bf16[208,128]{1,0:T(8,128)(2,1)S(1)} %shard_map.132.refs_0_.refs_4_), channel_id=1, source_target_pairs={{0,24},{8,16},{16,8},{24,0},{1,25},{9,17},{17,9},{25,1},{2,26},{10... | collective-permute-start | bytes 159752 | tf_op jit(solution)/shard_map/ppermute | solution.py:358
  28.2 1.6 %collective-permute-done.11.refs_3_.refs_7_ = bf16[208,128]{1,0:T(8,128)(2,1)S(1)} collective-permute-done((bf16[208,128]{1,0:T(8,128)(2,1)S(1)}, bf16[208,128]{1,0:T(8,128)(2,1)S(1)}, u32[]{:S(2)}, u32[]{:S(2)}) %collective-permute-start.11) | collective-permute-done | bytes 53280 | tf_op jit(solution)/shard_map/ppermute | solution.py:358
  29.8 2.8 %collective-permute-done.10.refs_2_.refs_6_ = bf16[208,128]{1,0:T(8,128)(2,1)S(1)} collective-permute-done((bf16[208,128]{1,0:T(8,128)(2,1)S(1)}, bf16[208,128]{1,0:T(8,128)(2,1)S(1)}, u32[]{:S(2)}, u32[]{:S(2)}) %collective-permute-start.10) | collective-permute-done | bytes 53280 | tf_op jit(solution)/shard_map/ppermute | solution.py:358
  32.7 9.6 %collective-permute-start.17 = (bf16[800,128]{1,0:T(8,128)(2,1)S(1)}, bf16[800,128]{1,0:T(8,128)(2,1)S(1)}, u32[]{:S(2)}, u32[]{:S(2)}) collective-permute-start(bf16[800,128]{1,0:T(8,128)(2,1)S(1)} %shard_map.133.refs_0_), channel_id=1, source_target_pairs={{0,6},{1,7},{2,4},{3,5},{4,2},{5,3},{6,0},{7,1},{8,14},{9,15},{10,... | collective-permute-start | bytes 614408 | tf_op jit(solution)/shard_map/ppermute | solution.py:351
  42.3 1.4 %collective-permute-start.15 = (bf16[800,128]{1,0:T(8,128)(2,1)S(1)}, bf16[800,128]{1,0:T(8,128)(2,1)S(1)}, u32[]{:S(2)}, u32[]{:S(2)}) collective-permute-start(bf16[800,128]{1,0:T(8,128)(2,1)S(1)} %shard_map.133.refs_0_), channel_id=1, source_target_pairs={{0,2},{1,3},{2,0},{3,1},{4,6},{5,7},{6,4},{7,5},{8,10},{9,11},{10,... | collective-permute-start | bytes 614408 | tf_op jit(solution)/shard_map/ppermute | solution.py:351
  43.7 2.4 %shard_map.134 = (bf16[1024,128]{1,0:T(8,128)(2,1)}, bf16[1024,128]{1,0:T(8,128)(2,1)}, bf16[128,128]{1,0:T(8,128)(2,1)S(1)}, bf16[128,128]{1,0:T(8,128)(2,1)S(1...) custom-call(f32[2,512]{1,0:T(2,128)S(1)} %get-tuple-element.45.bias, bf16[1024,128]{1,0:T(8,128)(2,1)S(1)} %copy-done.1, ...), custom_call_target="tpu_custom_call" | custom-call | flops 671088640 | bytes 1003520 | tf_op jit(solution)/shard_map/pallas_call | solution.py:306
  46.1 2.2 %collective-permute-start.12 = (bf16[128,128]{1,0:T(8,128)(2,1)S(1)}, bf16[128,128]{1,0:T(8,128)(2,1)S(1)}, u32[]{:S(2)}, u32[]{:S(2)}) collective-permute-start(bf16[128,128]{1,0:T(8,128)(2,1)S(1)} %get-tuple-element.46), channel_id=1, source_target_pairs={{0,24},{8,16},{16,8},{24,0},{1,25},{9,17},{17,9},{25,1},{2,26},{10... | collective-permute-start | bytes 98312 | tf_op jit(solution)/shard_map/ppermute | solution.py:358
  48.5 3.4 %collective-permute-done.12.refs_0_ = bf16[128,128]{1,0:T(8,128)(2,1)S(1)} collective-permute-done((bf16[128,128]{1,0:T(8,128)(2,1)S(1)}, bf16[128,128]{1,0:T(8,128)(2,1)S(1)}, u32[]{:S(2)}, u32[]{:S(2)}) %collective-permute-start.12) | collective-permute-done | bytes 32800 | tf_op jit(solution)/shard_map/ppermute | solution.py:358
  51.9 1.4 %collective-permute-done.13.refs_1_ = bf16[128,128]{1,0:T(8,128)(2,1)S(1)} collective-permute-done((bf16[128,128]{1,0:T(8,128)(2,1)S(1)}, bf16[128,128]{1,0:T(8,128)(2,1)S(1)}, u32[]{:S(2)}, u32[]{:S(2)}) %collective-permute-start.13) | collective-permute-done | bytes 32800 | tf_op jit(solution)/shard_map/ppermute | solution.py:358
  53.3 2.5 %collective-permute-done.14.refs_2_ = bf16[128,128]{1,0:T(8,128)(2,1)S(1)} collective-permute-done((bf16[128,128]{1,0:T(8,128)(2,1)S(1)}, bf16[128,128]{1,0:T(8,128)(2,1)S(1)}, u32[]{:S(2)}, u32[]{:S(2)}) %collective-permute-start.14) | collective-permute-done | bytes 32800 | tf_op jit(solution)/shard_map/ppermute | solution.py:358
  56.7 1.5 %collective-permute-done.18.other = bf16[2880,128]{1,0:T(8,128)(2,1)S(1)} collective-permute-done((bf16[2880,128]{1,0:T(8,128)(2,1)S(1)}, bf16[2880,128]{1,0:T(8,128)(2,1)S(1)}, u32[]{:S(2)}, u32[]{:S(2)}) %collective-permute-start.18) | collective-permute-done | bytes 737312 | tf_op jit(solution)/shard_map/ppermute | solution.py:355
  58.2 1.6 %shard_map.137 = (f32[128,1280]{1,0:T(8,128)}, f32[16,5120]{1,0:T(8,128)}) custom-call(f32[8,16,128]{2,1,0:T(8,128)S(1)} %get-tuple-element.52.hot, bf16[2880,128]{1,0:T(8,128)(2,1)S(1)} %shard_map.136.own, bf16[2880,128]{1,0:T(8,128)(2,1)S(1)} %collective-permute-done.18.other, bf16[2,128,128]{2,1,0:T(8,128)(2,1)S(1)} %pad_maximum_fusion.packed.refs_0_, ...), custom_call_target="tpu_custom_call" | custom-call | flops 167772160 | bytes 1802240 | tf_op jit(solution)/shard_map/pallas_call | solution.py:306
  (41 shorter events, 4.4 us)
Async XLA Ops:
  0.6 11.7 %copy-start = (f32[16,5120]{1,0:T(8,128)S(1)}, f32[16,5120]{1,0:T(8,128)}, u32[]{:S(2)}) copy-start(f32[16,5120]{1,0:T(8,128)} %gate) | copy-start | bytes 983044
  1.5 10.9 %copy-start.4 = (s32[8]{0:T(128)S(1)}, s32[8]{0:T(128)}, u32[]{:S(2)}) copy-start(s32[8]{0:T(128)} %levels.1) | copy-start | bytes 100
  1.5 10.9 %copy-start.5 = (s32[4]{0:T(128)S(1)}, s32[4]{0:T(128)}, u32[]{:S(2)}) copy-start(s32[4]{0:T(128)} %clips.1) | copy-start | bytes 52
  3.0 19.6 %copy-start.1 = (bf16[1024,128]{1,0:T(8,128)(2,1)S(1)}, bf16[1024,128]{1,0:T(8,128)(2,1)}, u32[]{:S(2)}) copy-start(bf16[1024,128]{1,0:T(8,128)(2,1)} %keys.3) | copy-start | bytes 786436
  3.0 4.7 %collective-permute-start = (bf16[128,2688]{1,0:T(8,128)(2,1)S(1)}, bf16[128,2688]{1,0:T(8,128)(2,1)S(1)}, u32[]{:S(2)}, u32[]{:S(2)}) collective-permute-start(bf16[128,2688]{1,0:T(8,128)(2,1)S(1)} %get-tuple-element.32), channel_id=1, source_target_pairs={{0,1},{1,0},{2,3},{3,2},{4,5},{5,4},{6,7},{7,6},{8,9},{9,8},{10,11... | collective-permute-start | bytes 2064392 | tf_op jit(solution)/shard_map/ppermute | solution.py:355
  3.5 11.5 %collective-permute-start.4 = (bf16[128,640]{1,0:T(8,128)(2,1)S(1)}, bf16[128,640]{1,0:T(8,128)(2,1)S(1)}, u32[]{:S(2)}, u32[]{:S(2)}) collective-permute-start(bf16[128,640]{1,0:T(8,128)(2,1)S(1)} %copy-done.2), channel_id=1, source_target_pairs={{0,4},{1,5},{2,6},{3,7},{4,0},{5,1},{6,2},{7,3},{8,12},{9,13},{10,... | collective-permute-start | bytes 491528 | tf_op jit(solution)/shard_map/ppermute | solution.py:351
  6.1 8.9 %collective-permute-start.3 = (bf16[128,640]{1,0:T(8,128)(2,1)S(1)}, bf16[128,640]{1,0:T(8,128)(2,1)S(1)}, u32[]{:S(2)}, u32[]{:S(2)}) collective-permute-start(bf16[128,640]{1,0:T(8,128)(2,1)S(1)} %copy-done.2), channel_id=1, source_target_pairs={{0,2},{1,3},{2,0},{3,1},{4,6},{5,7},{6,4},{7,5},{8,10},{9,11},{10,... | collective-permute-start | bytes 491528 | tf_op jit(solution)/shard_map/ppermute | solution.py:351
  7.6 8.0 %collective-permute-start.5 = (bf16[128,640]{1,0:T(8,128)(2,1)S(1)}, bf16[128,640]{1,0:T(8,128)(2,1)S(1)}, u32[]{:S(2)}, u32[]{:S(2)}) collective-permute-start(bf16[128,640]{1,0:T(8,128)(2,1)S(1)} %copy-done.2), channel_id=1, source_target_pairs={{0,6},{1,7},{2,4},{3,5},{4,2},{5,3},{6,0},{7,1},{8,14},{9,15},{10,... | collective-permute-start | bytes 491528 | tf_op jit(solution)/shard_map/ppermute | solution.py:351
  7.7 6.1 %collective-permute-start.2 = (bf16[2,128,128]{2,1,0:T(8,128)(2,1)S(1)}, bf16[2,128,128]{2,1,0:T(8,128)(2,1)S(1)}, u32[]{:S(2)}, u32[]{:S(2)}) collective-permute-start(bf16[2,128,128]{2,1,0:T(8,128)(2,1)S(1)} %pad_maximum_fusion.packed.refs_0_), channel_id=1, source_target_pairs={{0,16},{8,24},{16,0},{24,8},{1,17},{9,25},{17,1},{25,9},{2,18},{10... | collective-permute-start | bytes 196616 | tf_op jit(solution)/shard_map/ppermute | solution.py:358
  10.8 4.3 %collective-permute-start.1 = (bf16[2,128,128]{2,1,0:T(8,128)(2,1)S(1)}, bf16[2,128,128]{2,1,0:T(8,128)(2,1)S(1)}, u32[]{:S(2)}, u32[]{:S(2)}) collective-permute-start(bf16[2,128,128]{2,1,0:T(8,128)(2,1)S(1)} %pad_maximum_fusion.packed.refs_0_), channel_id=1, source_target_pairs={{0,8},{8,0},{16,24},{24,16},{1,9},{9,1},{17,25},{25,17},{2,10},{10... | collective-permute-start | bytes 196616 | tf_op jit(solution)/shard_map/ppermute | solution.py:358
  15.6 28.1 %copy-start.6 = (bf16[1024,128]{1,0:T(8,128)(2,1)S(1)}, bf16[1024,128]{1,0:T(8,128)(2,1)}, u32[]{:S(2)}) copy-start(bf16[1024,128]{1,0:T(8,128)(2,1)} %values.1) | copy-start | bytes 786436
  16.4 16.2 %collective-permute-start.6 = (bf16[128,640]{1,0:T(8,128)(2,1)S(1)}, bf16[128,640]{1,0:T(8,128)(2,1)S(1)}, u32[]{:S(2)}, u32[]{:S(2)}) collective-permute-start(bf16[128,640]{1,0:T(8,128)(2,1)S(1)} %get-tuple-element.40), channel_id=1, source_target_pairs={{0,0},{1,1},{2,10},{3,11},{4,20},{5,21},{6,30},{7,31},{8,8},{9,9},... | collective-permute-start | bytes 491528 | tf_op jit(solution)/shard_map/ppermute | solution.py:416
  17.1 5.5 %collective-permute-start.8 = (bf16[2,128,128]{2,1,0:T(8,128)(2,1)S(1)}, bf16[2,128,128]{2,1,0:T(8,128)(2,1)S(1)}, u32[]{:S(2)}, u32[]{:S(2)}) collective-permute-start(bf16[2,128,128]{2,1,0:T(8,128)(2,1)S(1)} %collective-permute-done.1.refs_1_), channel_id=1, source_target_pairs={{0,16},{8,24},{16,0},{24,8},{1,17},{9,25},{17,1},{25,9},{2,18},{10... | collective-permute-start | bytes 196616 | tf_op jit(solution)/shard_map/ppermute | solution.py:358
  20.0 3.4 %collective-permute-start.7 = (f32[128,128]{1,0:T(8,128)S(1)}, f32[128,128]{1,0:T(8,128)S(1)}, u32[]{:S(2)}, u32[]{:S(2)}) collective-permute-start(f32[128,128]{1,0:T(8,128)S(1)} %get-tuple-element.42), channel_id=1, source_target_pairs={{0,1},{1,0},{2,3},{3,2},{4,5},{5,4},{6,7},{7,6},{8,9},{9,8},{10,11... | collective-permute-start | bytes 196616 | tf_op jit(solution)/shard_map/ppermute | solution.py:355
  23.4 6.4 %collective-permute-start.11 = (bf16[208,128]{1,0:T(8,128)(2,1)S(1)}, bf16[208,128]{1,0:T(8,128)(2,1)S(1)}, u32[]{:S(2)}, u32[]{:S(2)}) collective-permute-start(bf16[208,128]{1,0:T(8,128)(2,1)S(1)} %shard_map.132.refs_0_.refs_4_), channel_id=1, source_target_pairs={{0,24},{8,16},{16,8},{24,0},{1,25},{9,17},{17,9},{25,1},{2,26},{10... | collective-permute-start | bytes 159752 | tf_op jit(solution)/shard_map/ppermute | solution.py:358
  27.6 5.0 %collective-permute-start.10 = (bf16[208,128]{1,0:T(8,128)(2,1)S(1)}, bf16[208,128]{1,0:T(8,128)(2,1)S(1)}, u32[]{:S(2)}, u32[]{:S(2)}) collective-permute-start(bf16[208,128]{1,0:T(8,128)(2,1)S(1)} %shard_map.132.refs_0_.refs_4_), channel_id=1, source_target_pairs={{0,16},{8,24},{16,0},{24,8},{1,17},{9,25},{17,1},{25,9},{2,18},{10... | collective-permute-start | bytes 159752 | tf_op jit(solution)/shard_map/ppermute | solution.py:358
  27.6 5.0 %collective-permute-start.9 = (bf16[208,128]{1,0:T(8,128)(2,1)S(1)}, bf16[208,128]{1,0:T(8,128)(2,1)S(1)}, u32[]{:S(2)}, u32[]{:S(2)}) collective-permute-start(bf16[208,128]{1,0:T(8,128)(2,1)S(1)} %shard_map.132.refs_0_.refs_4_), channel_id=1, source_target_pairs={{0,8},{8,0},{16,24},{24,16},{1,9},{9,1},{17,25},{25,17},{2,10},{10... | collective-permute-start | bytes 159752 | tf_op jit(solution)/shard_map/ppermute | solution.py:358
  32.7 23.2 %collective-permute-start.17 = (bf16[800,128]{1,0:T(8,128)(2,1)S(1)}, bf16[800,128]{1,0:T(8,128)(2,1)S(1)}, u32[]{:S(2)}, u32[]{:S(2)}) collective-permute-start(bf16[800,128]{1,0:T(8,128)(2,1)S(1)} %shard_map.133.refs_0_), channel_id=1, source_target_pairs={{0,6},{1,7},{2,4},{3,5},{4,2},{5,3},{6,0},{7,1},{8,14},{9,15},{10,... | collective-permute-start | bytes 614408 | tf_op jit(solution)/shard_map/ppermute | solution.py:351
  42.2 13.6 %collective-permute-start.16 = (bf16[800,128]{1,0:T(8,128)(2,1)S(1)}, bf16[800,128]{1,0:T(8,128)(2,1)S(1)}, u32[]{:S(2)}, u32[]{:S(2)}) collective-permute-start(bf16[800,128]{1,0:T(8,128)(2,1)S(1)} %shard_map.133.refs_0_), channel_id=1, source_target_pairs={{0,4},{1,5},{2,6},{3,7},{4,0},{5,1},{6,2},{7,3},{8,12},{9,13},{10,... | collective-permute-start | bytes 614408 | tf_op jit(solution)/shard_map/ppermute | solution.py:351
  42.3 13.6 %collective-permute-start.15 = (bf16[800,128]{1,0:T(8,128)(2,1)S(1)}, bf16[800,128]{1,0:T(8,128)(2,1)S(1)}, u32[]{:S(2)}, u32[]{:S(2)}) collective-permute-start(bf16[800,128]{1,0:T(8,128)(2,1)S(1)} %shard_map.133.refs_0_), channel_id=1, source_target_pairs={{0,2},{1,3},{2,0},{3,1},{4,6},{5,7},{6,4},{7,5},{8,10},{9,11},{10,... | collective-permute-start | bytes 614408 | tf_op jit(solution)/shard_map/ppermute | solution.py:351
  46.1 5.8 %collective-permute-start.12 = (bf16[128,128]{1,0:T(8,128)(2,1)S(1)}, bf16[128,128]{1,0:T(8,128)(2,1)S(1)}, u32[]{:S(2)}, u32[]{:S(2)}) collective-permute-start(bf16[128,128]{1,0:T(8,128)(2,1)S(1)} %get-tuple-element.46), channel_id=1, source_target_pairs={{0,24},{8,16},{16,8},{24,0},{1,25},{9,17},{17,9},{25,1},{2,26},{10... | collective-permute-start | bytes 98312 | tf_op jit(solution)/shard_map/ppermute | solution.py:358
  48.3 5.0 %collective-permute-start.13 = (bf16[128,128]{1,0:T(8,128)(2,1)S(1)}, bf16[128,128]{1,0:T(8,128)(2,1)S(1)}, u32[]{:S(2)}, u32[]{:S(2)}) collective-permute-start(bf16[128,128]{1,0:T(8,128)(2,1)S(1)} %get-tuple-element.47), channel_id=1, source_target_pairs={{0,16},{8,24},{16,0},{24,8},{1,17},{9,25},{17,1},{25,9},{2,18},{10... | collective-permute-start | bytes 98312 | tf_op jit(solution)/shard_map/ppermute | solution.py:358
  51.9 3.9 %collective-permute-start.14 = (bf16[128,128]{1,0:T(8,128)(2,1)S(1)}, bf16[128,128]{1,0:T(8,128)(2,1)S(1)}, u32[]{:S(2)}, u32[]{:S(2)}) collective-permute-start(bf16[128,128]{1,0:T(8,128)(2,1)S(1)} %get-tuple-element.48), channel_id=1, source_target_pairs={{0,8},{8,0},{16,24},{24,16},{1,9},{9,1},{17,25},{25,17},{2,10},{10... | collective-permute-start | bytes 98312 | tf_op jit(solution)/shard_map/ppermute | solution.py:358
  55.9 2.3 %collective-permute-start.18 = (bf16[2880,128]{1,0:T(8,128)(2,1)S(1)}, bf16[2880,128]{1,0:T(8,128)(2,1)S(1)}, u32[]{:S(2)}, u32[]{:S(2)}) collective-permute-start(bf16[2880,128]{1,0:T(8,128)(2,1)S(1)} %shard_map.136.own), channel_id=1, source_target_pairs={{0,1},{1,0},{2,3},{3,2},{4,5},{5,4},{6,7},{7,6},{8,9},{9,8},{10,11... | collective-permute-start | bytes 2211848 | tf_op jit(solution)/shard_map/ppermute | solution.py:355
  (3 other events, 9.9 us)

commit v9 on v5

--- a/solution.py
+++ b/solution.py
@@ -131,9 +131,8 @@
 
 def sections(rows, chips, tiles, n_t, count):
     starts = [0, rows]
-    starts.append(starts[-1] + -(-SPLIT * 2 * n_t // 16) * 16)
     starts.append(starts[-1] + tiles * (rows // chips))
-    starts.append(starts[-1] + -(-count // 16) * 16)
+    starts.append(starts[-1] + -(-(SPLIT * 2 * n_t + count) // 16) * 16)
     return starts
 
 
@@ -157,22 +156,21 @@
         piece = rest.astype(jnp.bfloat16).astype(jnp.float32)
         split.append(piece)
         rest = rest - piece
-    split = padded(jnp.concatenate(split, axis=0), starts[2] - starts[1]).astype(jnp.bfloat16)
-    last = padded(terms[...], starts[4] - starts[3]).astype(jnp.bfloat16)
+    last = padded(jnp.concatenate(split + [terms[...]], axis=0), starts[3] - starts[2])
+    last = last.astype(jnp.bfloat16)
     for k in range(n_t):
         rows = held[chip ^ t ^ k]
         rows = jnp.concatenate([rows[:, j * LANES : (j + 1) * LANES] for j in range(tiles)], axis=0)
         outs[k][: starts[1], :] = head
-        outs[k][starts[1] : starts[2], :] = split
-        outs[k][starts[2] : starts[3], :] = rows.astype(jnp.bfloat16)
-        outs[k][starts[3] :, :] = last
+        outs[k][starts[1] : starts[2], :] = rows.astype(jnp.bfloat16)
+        outs[k][starts[2] :, :] = last
 
 
 def bundle_kernel(n_t, starts, count, gate_b, *refs):
     heads, out = refs[:n_t][::-1], refs[n_t]
     tiles = gate_b.shape[2] // LANES
-    part = (starts[3] - starts[2]) // tiles
-    wide = [heads[k][starts[2] : starts[3], :].astype(jnp.float32) for k in range(n_t)]
+    part = (starts[2] - starts[1]) // tiles
+    wide = [heads[k][starts[1] : starts[2], :].astype(jnp.float32) for k in range(n_t)]
     for j in range(tiles):
         gated = jnp.concatenate(
             [
@@ -182,7 +180,8 @@
             axis=0,
         )
         out[j * n_t * part : (j + 1) * n_t * part, :] = gated.astype(jnp.bfloat16)
-    terms = [heads[k][starts[3] :, :].astype(jnp.float32)[:count] for k in range(n_t)]
+    first = SPLIT * 2 * n_t
+    terms = [heads[k][starts[2] :, :].astype(jnp.float32)[first : first + count] for k in range(n_t)]
     out[tiles * n_t * part :, :] = jnp.concatenate(terms, axis=0).astype(jnp.bfloat16)
 
 
@@ -201,7 +200,7 @@
     out[chips * base + count :, :] = (total - high.astype(jnp.float32)).astype(jnp.bfloat16)
 
 
-def grads_kernel(n_t, bias, keys, values, *refs):
+def grads_kernel(n_t, starts, bias, keys, values, *refs):
     packed, heads = refs[:n_t], refs[n_t : 2 * n_t][::-1]
     key_out, value_out = refs[2 * n_t : 2 * n_t + 2]
     outs = refs[2 * n_t + 2 : 3 * n_t + 2][::-1]
@@ -211,7 +210,7 @@
     keys_t = jnp.transpose(keys[...])
     stats = []
     for k in range(n_t):
-        parts = heads[k][rows : rows + -(-SPLIT * 2 * n_t // 16) * 16, :].astype(jnp.float32)
+        parts = heads[k][starts[2] :, :].astype(jnp.float32)
         stats.append(sum(parts[i * 2 * n_t : (i + 1) * 2 * n_t] for i in range(SPLIT)))
     for p in range(0, n_t, 2):
         q = jnp.concatenate([packed[p][0], packed[p + 1][0]], axis=0)
@@ -261,11 +260,8 @@
     refs[n_t][...] = jnp.transpose(total * SCALE).astype(jnp.bfloat16)
 
 
-def final_kernel(n_t, chips, frames, hot, own, other, *refs):
-    packed, (weight_out, gate_out, saved, held) = refs[:n_t], refs[n_t:]
-    t, chip, core = place()
-    width = weight_out.shape[1] // 2
-    tiles = width // LANES
+def half_results(n_t, chips, frames, hot, ref, packed, saved, held, tiles):
+    t, chip, _ = place()
     rows = saved.shape[1]
     part = rows // chips
     base = tiles * n_t * part
@@ -276,42 +272,63 @@
         mine = pl.ds(pl.multiple_of((chip ^ c) * part, part), part)
         ordered += [saved[k, mine, :] for k in range(n_t)]
     ordered = jnp.transpose(jnp.concatenate(ordered, axis=0)).astype(jnp.bfloat16)
-    count = (own.shape[0] - chips * base) // 2
+    gated = jnp.concatenate(
+        [
+            jnp.concatenate(
+                [
+                    ref[c * base + j * n_t * part : c * base + (j + 1) * n_t * part, :]
+                    for c in range(chips)
+                ],
+                axis=0,
+            )
+            for j in range(tiles)
+        ],
+        axis=1,
+    )
+    count = (ref.shape[0] - chips * base) // 2
     each = count // n_t
-    for ref, half in ((own, core), (other, 1 - core)):
-        gated = jnp.concatenate(
-            [
-                jnp.concatenate(
-                    [
-                        ref[c * base + j * n_t * part : c * base + (j + 1) * n_t * part, :]
-                        for c in range(chips)
-                    ],
-                    axis=0,
-                )
-                for j in range(tiles)
-            ],
-            axis=1,
-        )
-        result = dot(ordered, gated, 1, 0)
-        terms = ref[chips * base : chips * base + count, :].astype(jnp.float32)
-        terms = terms + ref[chips * base + count :, :].astype(jnp.float32)
-        for k in range(n_t):
-            held[half, t ^ k] = terms[k * each : (k + 1) * each]
-        for h in range(2):
-
-            @pl.when(half == h)
-            def _():
-                weight_out[:, h * width : (h + 1) * width] = result
-
-    for half in range(2):
-        for a in range(chips):
-            for j in range(tiles):
-                total = jnp.zeros(hot.shape[1:], jnp.float32)
-                for f in range(n_t * frames):
-                    row = (a * frames + f % frames) * tiles + j
-                    total = total + hot[f] * held[half, f // frames, row : row + 1, :]
-                column = ((2 * a + half) * tiles + j) * LANES
-                gate_out[:, column : column + LANES] = total
+    terms = ref[chips * base : chips * base + count, :].astype(jnp.float32)
+    terms = terms + ref[chips * base + count :, :].astype(jnp.float32)
+    for k in range(n_t):
+        held[t ^ k] = terms[k * each : (k + 1) * each]
+
+    def gate_tile(a, j):
+        total = jnp.zeros(hot.shape[1:], jnp.float32)
+        for f in range(n_t * frames):
+            row = (a * frames + f % frames) * tiles + j
+            total = total + hot[f] * held[f // frames, row : row + 1, :]
+        return total
+
+    return dot(ordered, gated, 1, 0), gate_tile
+
+
+def own_kernel(n_t, chips, frames, hot, own, *refs):
+    packed, (weight_out, gate_out, saved, held) = refs[:n_t], refs[n_t:]
+    tiles = weight_out.shape[1] // LANES
+    result, gate_tile = half_results(n_t, chips, frames, hot, own, packed, saved, held, tiles)
+    weight_out[...] = result
+    for a in range(chips):
+        for j in range(tiles):
+            gate_out[:, (a * tiles + j) * LANES : (a * tiles + j + 1) * LANES] = gate_tile(a, j)
+
+
+def final_kernel(n_t, chips, frames, hot, other, own_weight, own_gate, *refs):
+    packed, (weight_out, gate_out, saved, held) = refs[:n_t], refs[n_t:]
+    core = place()[2]
+    width = own_weight.shape[1]
+    tiles = width // LANES
+    result, gate_tile = half_results(n_t, chips, frames, hot, other, packed, saved, held, tiles)
+    mine = own_weight[...]
+    weight_out[:, :width] = jnp.where(core == 0, mine, result)
+    weight_out[:, width:] = jnp.where(core == 0, result, mine)
+    for a in range(chips):
+        for j in range(tiles):
+            first = gate_tile(a, j)
+            second = own_gate[:, (a * tiles + j) * LANES : (a * tiles + j + 1) * LANES]
+            column = 2 * a * width + j * LANES
+            gate_out[:, column : column + LANES] = jnp.where(core == 0, second, first)
+            column += width
+            gate_out[:, column : column + LANES] = jnp.where(core == 0, first, second)
 
 
 def call(kernel, args, out_shape, scratch=(), flops=0, in_place=False, in_smem=0):
@@ -393,8 +410,8 @@
     packed, _ = lax.optimization_barrier((jnp.stack([queries, saved_out]), received))
     packed_all = [packed]
     for k in range(1, n_t):
-        high = 1 << (k.bit_length() - 1)
-        packed_all.append(over_time(packed_all[k - high], high))
+        low = k & -k
+        packed_all.append(over_time(packed_all[k - low], low))
     gate_table, _ = lax.optimization_barrier((gate_table, received))
     bias, gate_a, gate_b, hot = call(
         functools.partial(masks_kernel, n_t, chips, frames, rows),
@@ -436,7 +453,7 @@
     bundles = over_chips(bundle)
     later_bias, _ = lax.optimization_barrier((bias, bundle))
     outs = call(
-        functools.partial(grads_kernel, n_t),
+        functools.partial(grads_kernel, n_t, starts),
         [later_bias, keys, values] + packed_all + heads_all[::-1],
         [shape(bf16, k_rows, HD)] * 2 + [shape(bf16, HD, rows)] * n_t,
         [pltpu.VMEM((k_rows, HD), f32)] * 2,
@@ -452,12 +469,20 @@
         [pltpu.VMEM((chips, n_t * count, LANES), f32)],
     )
     query_grad = call(functools.partial(query_kernel, n_t), parts[::-1], shape(bf16, rows, HD))
+    scratch = [pltpu.VMEM((n_t, rows, HD), f32), pltpu.VMEM((n_t, count, LANES), f32)]
+    own_halves = call(
+        functools.partial(own_kernel, n_t, chips, frames),
+        [hot, collected] + packed_all,
+        [shape(f32, HD, width), shape(f32, levels, chips * width)],
+        scratch,
+        flops=2 * n_t * rows * width * HD,
+    )
     weight_grad, gate_grad = call(
         functools.partial(final_kernel, n_t, chips, frames),
-        [hot, collected, over_cores(collected)] + packed_all,
+        [hot, over_cores(collected), *own_halves] + packed_all,
         [shape(f32, HD, 2 * width), shape(f32, levels, n_s * width)],
-        [pltpu.VMEM((n_t, rows, HD), f32), pltpu.VMEM((2, n_t, count, LANES), f32)],
-        flops=4 * n_t * rows * width * HD,
+        scratch,
+        flops=2 * n_t * rows * width * HD,
     )
     if width != shard:
         weight_grad = without_padding(weight_grad, 2, shard)

time: 49.6 us -> 49.4 us (level)
  starting transfers between devices: 22.1 us -> 21.3 us
    ppermute x9, starting transfers between devices: 13.7 us -> 12.9 us  [over_time(): return lax.ppermute(x, 'tm', [(t, t ^ k) for t in range(n_t)])]
    ppermute x9, waiting for transfers between devices: 15 us -> 15.7 us  [over_time(): return lax.ppermute(x, 'tm', [(t, t ^ k) for t in range(n_t)])]
    pallas_call x10 -> x11, Pallas kernels: 8.69 us -> 8.77 us  [call(): pl.pallas_call(kernel, out_shape=out_shape, in_specs=[pl.BlockSpec(memory...]
  transfers between devices with their start and end apart: 18 -> 18, of which waited for: 9 -> 10; matrix products, arithmetic and copies ran while one was open for 0% -> 0% of each run, Pallas kernels for 11% -> 12%
where the time goes in v9:
time: 49.4 us; the launch traced here: 49.2 us
  starting transfers between devices  21.3 us (43%)
  waiting for transfers between devices  17.5 us (35%)
  Pallas kernels  8.77 us (18%)
  local copies, waits for them, and re-layouts  0.84 us (2%)
  between operations  0.78 us (2%)
    ppermute x9, waiting for transfers between devices, over_time(): return lax.ppermute(x, 'tm', [(t, t ^ k) for t in range(n_t)])  15.7 us
    ppermute x9, starting transfers between devices, over_time(): return lax.ppermute(x, 'tm', [(t, t ^ k) for t in range(n_t)])  12.9 us
    pallas_call x11, Pallas kernels, call(): pl.pallas_call(kernel, out_shape=out_shape, in_specs=[pl.BlockSpec(memory...  8.77 us
    ppermute x6, starting transfers between devices, over_chips(): lax.ppermute(x, 'space', [(s, s ^ 2 * k) for s in range(n_s)])  7.72 us
    ppermute x3, waiting for transfers between devices, over_cores(): return lax.ppermute(x, 'space', [(s, s ^ 1) for s in range(n_s)])  1.09 us
  transfers between devices with their start and end apart: 18, of which 10 were waited for; matrix products, arithmetic and copies ran while one was open for 0% of the time, Pallas kernels for 12%

profile of v9, /device:TPU:0, one launch (start us, length us, event | category | flops | bytes accessed | tf_op | source)
XLA Modules:
  0.0 49.2 jit_solution(2489827080072674981)
XLA Ops:
  0.7 0.8 %copy-done.3 = bf16[128,128]{1,0:T(8,128)(2,1)S(1)} copy-done((bf16[128,128]{1,0:T(8,128)(2,1)S(1)}, bf16[128,128]{1,0:T(8,128)(2,1)}, u32[]{:S(2)}) %copy-start.3) | copy-done | bytes 32792
  1.5 1.5 %shard_map.128 = (bf16[4,128,640]{2,1,0:T(8,128)(2,1)S(1)}, bf16[128,2688]{1,0:T(8,128)(2,1)S(1)}) custom-call(bf16[128,5120]{1,0:T(8,128)(2,1)} %weight_in.1, bf16[128,128]{1,0:T(8,128)(2,1)S(1)} %copy-done.3), custom_call_target="tpu_custom_call" | custom-call | bytes 1343488 | tf_op jit(solution)/shard_map/pallas_call | solution.py:338
  3.5 3.5 %collective-permute-start.3 = (bf16[128,640]{1,0:T(8,128)(2,1)S(1)}, bf16[128,640]{1,0:T(8,128)(2,1)S(1)}, u32[]{:S(2)}, u32[]{:S(2)}) collective-permute-start(bf16[128,640]{1,0:T(8,128)(2,1)S(1)} %copy-done), channel_id=1, source_target_pairs={{0,6},{1,7},{2,4},{3,5},{4,2},{5,3},{6,0},{7,1},{8,14},{9,15},{10,... | collective-permute-start | bytes 491528 | tf_op jit(solution)/shard_map/ppermute | solution.py:383
  7.7 3.1 %collective-permute-start.6 = (bf16[2,128,128]{2,1,0:T(8,128)(2,1)S(1)}, bf16[2,128,128]{2,1,0:T(8,128)(2,1)S(1)}, u32[]{:S(2)}, u32[]{:S(2)}) collective-permute-start(bf16[2,128,128]{2,1,0:T(8,128)(2,1)S(1)} %pad_maximum_fusion.packed.refs_0_), channel_id=1, source_target_pairs={{0,16},{8,24},{16,0},{24,8},{1,17},{9,25},{17,1},{25,9},{2,18},{10... | collective-permute-start | bytes 196616 | tf_op jit(solution)/shard_map/ppermute | solution.py:390
  10.8 1.6 %collective-permute-start.5 = (bf16[2,128,128]{2,1,0:T(8,128)(2,1)S(1)}, bf16[2,128,128]{2,1,0:T(8,128)(2,1)S(1)}, u32[]{:S(2)}, u32[]{:S(2)}) collective-permute-start(bf16[2,128,128]{2,1,0:T(8,128)(2,1)S(1)} %pad_maximum_fusion.packed.refs_0_), channel_id=1, source_target_pairs={{0,8},{8,0},{16,24},{24,16},{1,9},{9,1},{17,25},{25,17},{2,10},{10... | collective-permute-start | bytes 196616 | tf_op jit(solution)/shard_map/ppermute | solution.py:390
  12.4 0.6 %shard_map.129 = (f32[2,512]{1,0:T(2,128)S(1)}, f32[4,2,640]{2,1,0:T(2,128)S(1)}, f32[4,1,640]{2,1,0:T(1,128)S(1)}, f32[8,16,128]{2,1,0:T(8,128)S(1)}) custom-call(s32[8]{0:T(128)S(1)} %copy-done.4, s32[4]{0:T(128)S(1)} %copy-done.5, f32[16,5120]{1,0:T(8,128)S(1)} %copy-done.1), custom_call_target="tpu_custom_call" | custom-call | bytes 327728 | tf_op jit(solution)/shard_map/pallas_call | solution.py:338
  13.0 0.8 %collective-permute-done.6.refs_2_ = bf16[2,128,128]{2,1,0:T(8,128)(2,1)S(1)} collective-permute-done((bf16[2,128,128]{2,1,0:T(8,128)(2,1)S(1)}, bf16[2,128,128]{2,1,0:T(8,128)(2,1)S(1)}, u32[]{:S(2)}, u32[]{:S(2)}) %collective-permute-start.6) | collective-permute-done | bytes 65568 | tf_op jit(solution)/shard_map/ppermute | solution.py:390
  13.8 1.2 %collective-permute-start.7 = (bf16[2,128,128]{2,1,0:T(8,128)(2,1)S(1)}, bf16[2,128,128]{2,1,0:T(8,128)(2,1)S(1)}, u32[]{:S(2)}, u32[]{:S(2)}) collective-permute-start(bf16[2,128,128]{2,1,0:T(8,128)(2,1)S(1)} %collective-permute-done.6.refs_2_), channel_id=1, source_target_pairs={{0,8},{8,0},{16,24},{24,16},{1,9},{9,1},{17,25},{25,17},{2,10},{10... | collective-permute-start | bytes 196616 | tf_op jit(solution)/shard_map/ppermute | solution.py:390
  15.7 0.8 %shard_map.130 = (f32[128,128]{1,0:T(8,128)S(1)}, f32[128,128]{1,0:T(8,128)S(1)}, f32[40,128]{1,0:T(8,128)S(1)}) custom-call(bf16[2,128,128]{2,1,0:T(8,128)(2,1)S(1)} %pad_maximum_fusion.packed.refs_0_, bf16[4,128,640]{2,1,0:T(8,128)(2,1)S(1)} %get-tuple-element.41.kept, bf16[128,2688]{1,0:T(8,128)(2,1)S(1)} %collective-permute-done.received, ...), custom_call_target="tpu_custom_call" | custom-call | flops 335544320 | bytes 2084864 | tf_op jit(solution)/shard_map/pallas_call | solution.py:338
  16.5 1.5 %collective-permute-done.7.refs_3_ = bf16[2,128,128]{2,1,0:T(8,128)(2,1)S(1)} collective-permute-done((bf16[2,128,128]{2,1,0:T(8,128)(2,1)S(1)}, bf16[2,128,128]{2,1,0:T(8,128)(2,1)S(1)}, u32[]{:S(2)}, u32[]{:S(2)}) %collective-permute-start.7) | collective-permute-done | bytes 65568 | tf_op jit(solution)/shard_map/ppermute | solution.py:390
  18.1 0.8 %shard_map.131.stats = f32[8,128]{1,0:T(8,128)S(1)} custom-call(f32[2,512]{1,0:T(2,128)S(1)} %get-tuple-element.51.bias, bf16[1024,128]{1,0:T(8,128)(2,1)S(1)} %copy-done.2, bf16[2,128,128]{2,1,0:T(8,128)(2,1)S(1)} %pad_maximum_fusion.packed.refs_0_, bf16[2,128,128]{2,1,0:T(8,128)(2,1)S(1)} %collective-permute-done.5.refs_1_, ...), custom_call_target="tpu_custom_call" | custom-call | flops 134217728 | bytes 528384 | tf_op jit(solution)/shard_map/pallas_call | solution.py:338
  19.0 3.9 %collective-permute-start.8 = (bf16[352,128]{1,0:T(8,128)(2,1)S(1)}, bf16[352,128]{1,0:T(8,128)(2,1)S(1)}, u32[]{:S(2)}, u32[]{:S(2)}) collective-permute-start(bf16[352,128]{1,0:T(8,128)(2,1)S(1)} %get-tuple-element.47), channel_id=1, source_target_pairs={{0,24},{8,16},{16,8},{24,0},{1,25},{9,17},{17,9},{25,1},{2,26},{10... | collective-permute-start | bytes 270344 | tf_op jit(solution)/shard_map/ppermute | solution.py:390
  23.5 2.5 %collective-permute-done.8.refs_0_.refs_4_ = bf16[352,128]{1,0:T(8,128)(2,1)S(1)} collective-permute-done((bf16[352,128]{1,0:T(8,128)(2,1)S(1)}, bf16[352,128]{1,0:T(8,128)(2,1)S(1)}, u32[]{:S(2)}, u32[]{:S(2)}) %collective-permute-start.8) | collective-permute-done | bytes 90144 | tf_op jit(solution)/shard_map/ppermute | solution.py:390
  26.0 3.5 %collective-permute-done.9.refs_1_.refs_5_ = bf16[352,128]{1,0:T(8,128)(2,1)S(1)} collective-permute-done((bf16[352,128]{1,0:T(8,128)(2,1)S(1)}, bf16[352,128]{1,0:T(8,128)(2,1)S(1)}, u32[]{:S(2)}, u32[]{:S(2)}) %collective-permute-start.9) | collective-permute-done | bytes 90144 | tf_op jit(solution)/shard_map/ppermute | solution.py:390
  29.5 2.3 %collective-permute-start.16 = (bf16[800,128]{1,0:T(8,128)(2,1)S(1)}, bf16[800,128]{1,0:T(8,128)(2,1)S(1)}, u32[]{:S(2)}, u32[]{:S(2)}) collective-permute-start(bf16[800,128]{1,0:T(8,128)(2,1)S(1)} %shard_map.133.refs_0_), channel_id=1, source_target_pairs={{0,6},{1,7},{2,4},{3,5},{4,2},{5,3},{6,0},{7,1},{8,14},{9,15},{10,... | collective-permute-start | bytes 614408 | tf_op jit(solution)/shard_map/ppermute | solution.py:383
  31.8 0.7 %collective-permute-start.15 = (bf16[800,128]{1,0:T(8,128)(2,1)S(1)}, bf16[800,128]{1,0:T(8,128)(2,1)S(1)}, u32[]{:S(2)}, u32[]{:S(2)}) collective-permute-start(bf16[800,128]{1,0:T(8,128)(2,1)S(1)} %shard_map.133.refs_0_), channel_id=1, source_target_pairs={{0,4},{1,5},{2,6},{3,7},{4,0},{5,1},{6,2},{7,3},{8,12},{9,13},{10,... | collective-permute-start | bytes 614408 | tf_op jit(solution)/shard_map/ppermute | solution.py:383
  33.1 2.4 %shard_map.134 = (bf16[1024,128]{1,0:T(8,128)(2,1)}, bf16[1024,128]{1,0:T(8,128)(2,1)}, bf16[128,128]{1,0:T(8,128)(2,1)S(1)}, bf16[128,128]{1,0:T(8,128)(2,1)S(1...) custom-call(f32[2,512]{1,0:T(2,128)S(1)} %get-tuple-element.51.bias, bf16[1024,128]{1,0:T(8,128)(2,1)S(1)} %copy-done.2, ...), custom_call_target="tpu_custom_call" | custom-call | flops 671088640 | bytes 1150976 | tf_op jit(solution)/shard_map/pallas_call | solution.py:338
  35.5 2.6 %collective-permute-start.11 = (bf16[128,128]{1,0:T(8,128)(2,1)S(1)}, bf16[128,128]{1,0:T(8,128)(2,1)S(1)}, u32[]{:S(2)}, u32[]{:S(2)}) collective-permute-start(bf16[128,128]{1,0:T(8,128)(2,1)S(1)} %get-tuple-element.52), channel_id=1, source_target_pairs={{0,24},{8,16},{16,8},{24,0},{1,25},{9,17},{17,9},{25,1},{2,26},{10... | collective-permute-start | bytes 98312 | tf_op jit(solution)/shard_map/ppermute | solution.py:390
  38.1 3.5 %collective-permute-done.11.refs_0_ = bf16[128,128]{1,0:T(8,128)(2,1)S(1)} collective-permute-done((bf16[128,128]{1,0:T(8,128)(2,1)S(1)}, bf16[128,128]{1,0:T(8,128)(2,1)S(1)}, u32[]{:S(2)}, u32[]{:S(2)}) %collective-permute-start.11) | collective-permute-done | bytes 32800 | tf_op jit(solution)/shard_map/ppermute | solution.py:390
  41.6 1.3 %collective-permute-done.12.refs_1_ = bf16[128,128]{1,0:T(8,128)(2,1)S(1)} collective-permute-done((bf16[128,128]{1,0:T(8,128)(2,1)S(1)}, bf16[128,128]{1,0:T(8,128)(2,1)S(1)}, u32[]{:S(2)}, u32[]{:S(2)}) %collective-permute-start.12) | collective-permute-done | bytes 32800 | tf_op jit(solution)/shard_map/ppermute | solution.py:390
  42.9 2.6 %collective-permute-done.13.refs_2_ = bf16[128,128]{1,0:T(8,128)(2,1)S(1)} collective-permute-done((bf16[128,128]{1,0:T(8,128)(2,1)S(1)}, bf16[128,128]{1,0:T(8,128)(2,1)S(1)}, u32[]{:S(2)}, u32[]{:S(2)}) %collective-permute-start.13) | collective-permute-done | bytes 32800 | tf_op jit(solution)/shard_map/ppermute | solution.py:390
  45.7 0.7 %shard_map.135 = bf16[128,128]{1,0:T(8,128)(2,1)} custom-call(bf16[128,128]{1,0:T(8,128)(2,1)S(1)} %collective-permute-done.11.refs_0_, bf16[128,128]{1,0:T(8,128)(2,1)S(1)} %collective-permute-done.12.refs_1_, bf16[128,128]{1,0:T(8,128)(2,1)S(1)} %collective-permute-done.13.refs_2_, bf16[128,128]{1,0:T(8,128)(2,1)S(1)} %get-tuple-element.55.refs_3_), custom_call_target="tpu_custom_call" | custom-call | bytes 131072 | tf_op jit(solution)/shard_map/pallas_call | solution.py:338
  46.8 1.1 %collective-permute-done.17.other = bf16[2880,128]{1,0:T(8,128)(2,1)S(1)} collective-permute-done((bf16[2880,128]{1,0:T(8,128)(2,1)S(1)}, bf16[2880,128]{1,0:T(8,128)(2,1)S(1)}, u32[]{:S(2)}, u32[]{:S(2)}) %collective-permute-start.17) | collective-permute-done | bytes 737312 | tf_op jit(solution)/shard_map/ppermute | solution.py:387
  47.9 1.3 %shard_map.138 = (f32[128,1280]{1,0:T(8,128)}, f32[16,5120]{1,0:T(8,128)}) custom-call(f32[8,16,128]{2,1,0:T(8,128)S(1)} %get-tuple-element.58.hot, bf16[2880,128]{1,0:T(8,128)(2,1)S(1)} %collective-permute-done.17.other, f32[128,640]{1,0:T(8,128)S(1)} %get-tuple-element.63.own_weight, f32[16,2560]{1,0:T(8,128)S(1)} %get-tuple-element.64.own_gate, ...), custom_call_target="tpu_custom_call" | custom-call | flops 83886080 | bytes 1556480 | tf_op jit(solution)/shard_map/pallas_call | solution.py:338
  (40 shorter events, 3.9 us)
Async XLA Ops:
  0.6 11.7 %copy-start.1 = (f32[16,5120]{1,0:T(8,128)S(1)}, f32[16,5120]{1,0:T(8,128)}, u32[]{:S(2)}) copy-start(f32[16,5120]{1,0:T(8,128)} %gate) | copy-start | bytes 983044
  1.5 6.2 %copy-start.7 = (bf16[128,128]{1,0:T(8,128)(2,1)S(1)}, bf16[128,128]{1,0:T(8,128)(2,1)}, u32[]{:S(2)}) copy-start(bf16[128,128]{1,0:T(8,128)(2,1)} %param.9) | copy-start | bytes 98308
  1.5 10.9 %copy-start.4 = (s32[8]{0:T(128)S(1)}, s32[8]{0:T(128)}, u32[]{:S(2)}) copy-start(s32[8]{0:T(128)} %levels.1) | copy-start | bytes 100
  1.5 10.9 %copy-start.5 = (s32[4]{0:T(128)S(1)}, s32[4]{0:T(128)}, u32[]{:S(2)}) copy-start(s32[4]{0:T(128)} %clips.1) | copy-start | bytes 52
  3.0 15.1 %copy-start.2 = (bf16[1024,128]{1,0:T(8,128)(2,1)S(1)}, bf16[1024,128]{1,0:T(8,128)(2,1)}, u32[]{:S(2)}) copy-start(bf16[1024,128]{1,0:T(8,128)(2,1)} %keys.3) | copy-start | bytes 786436
  3.0 4.7 %collective-permute-start = (bf16[128,2688]{1,0:T(8,128)(2,1)S(1)}, bf16[128,2688]{1,0:T(8,128)(2,1)S(1)}, u32[]{:S(2)}, u32[]{:S(2)}) collective-permute-start(bf16[128,2688]{1,0:T(8,128)(2,1)S(1)} %get-tuple-element.36), channel_id=1, source_target_pairs={{0,1},{1,0},{2,3},{3,2},{4,5},{5,4},{6,7},{7,6},{8,9},{9,8},{10,11... | collective-permute-start | bytes 2064392 | tf_op jit(solution)/shard_map/ppermute | solution.py:387
  3.5 11.4 %collective-permute-start.3 = (bf16[128,640]{1,0:T(8,128)(2,1)S(1)}, bf16[128,640]{1,0:T(8,128)(2,1)S(1)}, u32[]{:S(2)}, u32[]{:S(2)}) collective-permute-start(bf16[128,640]{1,0:T(8,128)(2,1)S(1)} %copy-done), channel_id=1, source_target_pairs={{0,6},{1,7},{2,4},{3,5},{4,2},{5,3},{6,0},{7,1},{8,14},{9,15},{10,... | collective-permute-start | bytes 491528 | tf_op jit(solution)/shard_map/ppermute | solution.py:383
  7.1 8.3 %collective-permute-start.2 = (bf16[128,640]{1,0:T(8,128)(2,1)S(1)}, bf16[128,640]{1,0:T(8,128)(2,1)S(1)}, u32[]{:S(2)}, u32[]{:S(2)}) collective-permute-start(bf16[128,640]{1,0:T(8,128)(2,1)S(1)} %copy-done), channel_id=1, source_target_pairs={{0,4},{1,5},{2,6},{3,7},{4,0},{5,1},{6,2},{7,3},{8,12},{9,13},{10,... | collective-permute-start | bytes 491528 | tf_op jit(solution)/shard_map/ppermute | solution.py:383
  7.6 8.1 %collective-permute-start.1 = (bf16[128,640]{1,0:T(8,128)(2,1)S(1)}, bf16[128,640]{1,0:T(8,128)(2,1)S(1)}, u32[]{:S(2)}, u32[]{:S(2)}) collective-permute-start(bf16[128,640]{1,0:T(8,128)(2,1)S(1)} %copy-done), channel_id=1, source_target_pairs={{0,2},{1,3},{2,0},{3,1},{4,6},{5,7},{6,4},{7,5},{8,10},{9,11},{10,... | collective-permute-start | bytes 491528 | tf_op jit(solution)/shard_map/ppermute | solution.py:383
  7.7 6.1 %collective-permute-start.6 = (bf16[2,128,128]{2,1,0:T(8,128)(2,1)S(1)}, bf16[2,128,128]{2,1,0:T(8,128)(2,1)S(1)}, u32[]{:S(2)}, u32[]{:S(2)}) collective-permute-start(bf16[2,128,128]{2,1,0:T(8,128)(2,1)S(1)} %pad_maximum_fusion.packed.refs_0_), channel_id=1, source_target_pairs={{0,16},{8,24},{16,0},{24,8},{1,17},{9,25},{17,1},{25,9},{2,18},{10... | collective-permute-start | bytes 196616 | tf_op jit(solution)/shard_map/ppermute | solution.py:390
  10.8 5.7 %collective-permute-start.5 = (bf16[2,128,128]{2,1,0:T(8,128)(2,1)S(1)}, bf16[2,128,128]{2,1,0:T(8,128)(2,1)S(1)}, u32[]{:S(2)}, u32[]{:S(2)}) collective-permute-start(bf16[2,128,128]{2,1,0:T(8,128)(2,1)S(1)} %pad_maximum_fusion.packed.refs_0_), channel_id=1, source_target_pairs={{0,8},{8,0},{16,24},{24,16},{1,9},{9,1},{17,25},{25,17},{2,10},{10... | collective-permute-start | bytes 196616 | tf_op jit(solution)/shard_map/ppermute | solution.py:390
  13.8 4.3 %collective-permute-start.7 = (bf16[2,128,128]{2,1,0:T(8,128)(2,1)S(1)}, bf16[2,128,128]{2,1,0:T(8,128)(2,1)S(1)}, u32[]{:S(2)}, u32[]{:S(2)}) collective-permute-start(bf16[2,128,128]{2,1,0:T(8,128)(2,1)S(1)} %collective-permute-done.6.refs_2_), channel_id=1, source_target_pairs={{0,8},{8,0},{16,24},{24,16},{1,9},{9,1},{17,25},{25,17},{2,10},{10... | collective-permute-start | bytes 196616 | tf_op jit(solution)/shard_map/ppermute | solution.py:390
  16.4 16.6 %copy-start.6 = (bf16[1024,128]{1,0:T(8,128)(2,1)S(1)}, bf16[1024,128]{1,0:T(8,128)(2,1)}, u32[]{:S(2)}) copy-start(bf16[1024,128]{1,0:T(8,128)(2,1)} %values.1) | copy-start | bytes 786436
  16.4 2.4 %collective-permute-start.4 = (f32[128,128]{1,0:T(8,128)S(1)}, f32[128,128]{1,0:T(8,128)S(1)}, u32[]{:S(2)}, u32[]{:S(2)}) collective-permute-start(f32[128,128]{1,0:T(8,128)S(1)} %get-tuple-element.44), channel_id=1, source_target_pairs={{0,1},{1,0},{2,3},{3,2},{4,5},{5,4},{6,7},{7,6},{8,9},{9,8},{10,11... | collective-permute-start | bytes 196616 | tf_op jit(solution)/shard_map/ppermute | solution.py:387
  19.0 7.0 %collective-permute-start.8 = (bf16[352,128]{1,0:T(8,128)(2,1)S(1)}, bf16[352,128]{1,0:T(8,128)(2,1)S(1)}, u32[]{:S(2)}, u32[]{:S(2)}) collective-permute-start(bf16[352,128]{1,0:T(8,128)(2,1)S(1)} %get-tuple-element.47), channel_id=1, source_target_pairs={{0,24},{8,16},{16,8},{24,0},{1,25},{9,17},{17,9},{25,1},{2,26},{10... | collective-permute-start | bytes 270344 | tf_op jit(solution)/shard_map/ppermute | solution.py:390
  22.9 6.6 %collective-permute-start.9 = (bf16[352,128]{1,0:T(8,128)(2,1)S(1)}, bf16[352,128]{1,0:T(8,128)(2,1)S(1)}, u32[]{:S(2)}, u32[]{:S(2)}) collective-permute-start(bf16[352,128]{1,0:T(8,128)(2,1)S(1)} %get-tuple-element.48), channel_id=1, source_target_pairs={{0,16},{8,24},{16,0},{24,8},{1,17},{9,25},{17,1},{25,9},{2,18},{10... | collective-permute-start | bytes 270344 | tf_op jit(solution)/shard_map/ppermute | solution.py:390
  22.9 6.6 %collective-permute-start.10 = (bf16[352,128]{1,0:T(8,128)(2,1)S(1)}, bf16[352,128]{1,0:T(8,128)(2,1)S(1)}, u32[]{:S(2)}, u32[]{:S(2)}) collective-permute-start(bf16[352,128]{1,0:T(8,128)(2,1)S(1)} %get-tuple-element.49), channel_id=1, source_target_pairs={{0,8},{8,0},{16,24},{24,16},{1,9},{9,1},{17,25},{25,17},{2,10},{10... | collective-permute-start | bytes 270344 | tf_op jit(solution)/shard_map/ppermute | solution.py:390
  29.5 16.0 %collective-permute-start.16 = (bf16[800,128]{1,0:T(8,128)(2,1)S(1)}, bf16[800,128]{1,0:T(8,128)(2,1)S(1)}, u32[]{:S(2)}, u32[]{:S(2)}) collective-permute-start(bf16[800,128]{1,0:T(8,128)(2,1)S(1)} %shard_map.133.refs_0_), channel_id=1, source_target_pairs={{0,6},{1,7},{2,4},{3,5},{4,2},{5,3},{6,0},{7,1},{8,14},{9,15},{10,... | collective-permute-start | bytes 614408 | tf_op jit(solution)/shard_map/ppermute | solution.py:383
  31.8 13.7 %collective-permute-start.15 = (bf16[800,128]{1,0:T(8,128)(2,1)S(1)}, bf16[800,128]{1,0:T(8,128)(2,1)S(1)}, u32[]{:S(2)}, u32[]{:S(2)}) collective-permute-start(bf16[800,128]{1,0:T(8,128)(2,1)S(1)} %shard_map.133.refs_0_), channel_id=1, source_target_pairs={{0,4},{1,5},{2,6},{3,7},{4,0},{5,1},{6,2},{7,3},{8,12},{9,13},{10,... | collective-permute-start | bytes 614408 | tf_op jit(solution)/shard_map/ppermute | solution.py:383
  32.5 13.0 %collective-permute-start.14 = (bf16[800,128]{1,0:T(8,128)(2,1)S(1)}, bf16[800,128]{1,0:T(8,128)(2,1)S(1)}, u32[]{:S(2)}, u32[]{:S(2)}) collective-permute-start(bf16[800,128]{1,0:T(8,128)(2,1)S(1)} %shard_map.133.refs_0_), channel_id=1, source_target_pairs={{0,2},{1,3},{2,0},{3,1},{4,6},{5,7},{6,4},{7,5},{8,10},{9,11},{10,... | collective-permute-start | bytes 614408 | tf_op jit(solution)/shard_map/ppermute | solution.py:383
  35.5 6.1 %collective-permute-start.11 = (bf16[128,128]{1,0:T(8,128)(2,1)S(1)}, bf16[128,128]{1,0:T(8,128)(2,1)S(1)}, u32[]{:S(2)}, u32[]{:S(2)}) collective-permute-start(bf16[128,128]{1,0:T(8,128)(2,1)S(1)} %get-tuple-element.52), channel_id=1, source_target_pairs={{0,24},{8,16},{16,8},{24,0},{1,25},{9,17},{17,9},{25,1},{2,26},{10... | collective-permute-start | bytes 98312 | tf_op jit(solution)/shard_map/ppermute | solution.py:390
  38.1 4.8 %collective-permute-start.12 = (bf16[128,128]{1,0:T(8,128)(2,1)S(1)}, bf16[128,128]{1,0:T(8,128)(2,1)S(1)}, u32[]{:S(2)}, u32[]{:S(2)}) collective-permute-start(bf16[128,128]{1,0:T(8,128)(2,1)S(1)} %get-tuple-element.53), channel_id=1, source_target_pairs={{0,16},{8,24},{16,0},{24,8},{1,17},{9,25},{17,1},{25,9},{2,18},{10... | collective-permute-start | bytes 98312 | tf_op jit(solution)/shard_map/ppermute | solution.py:390
  41.6 3.9 %collective-permute-start.13 = (bf16[128,128]{1,0:T(8,128)(2,1)S(1)}, bf16[128,128]{1,0:T(8,128)(2,1)S(1)}, u32[]{:S(2)}, u32[]{:S(2)}) collective-permute-start(bf16[128,128]{1,0:T(8,128)(2,1)S(1)} %get-tuple-element.54), channel_id=1, source_target_pairs={{0,8},{8,0},{16,24},{24,16},{1,9},{9,1},{17,25},{25,17},{2,10},{10... | collective-permute-start | bytes 98312 | tf_op jit(solution)/shard_map/ppermute | solution.py:390
  45.6 2.3 %collective-permute-start.17 = (bf16[2880,128]{1,0:T(8,128)(2,1)S(1)}, bf16[2880,128]{1,0:T(8,128)(2,1)S(1)}, u32[]{:S(2)}, u32[]{:S(2)}) collective-permute-start(bf16[2880,128]{1,0:T(8,128)(2,1)S(1)} %shard_map.136.own), channel_id=1, source_target_pairs={{0,1},{1,0},{2,3},{3,2},{4,5},{5,4},{6,7},{7,6},{8,9},{9,8},{10,11... | collective-permute-start | bytes 2211848 | tf_op jit(solution)/shard_map/ppermute | solution.py:387
  (2 other events, 3.7 us)

commit v10 on v9

--- a/solution.py
+++ b/solution.py
@@ -101,15 +101,19 @@
 
 
 def head_kernel(chips, frames, packed, kept, received, gate_a, *refs):
-    pieces, (mine, other, terms) = refs[:chips], refs[chips:]
-    _, chip, _ = place()
+    pieces, (mine, other) = refs[:chips], refs[chips : chips + 2]
+    messages, (terms, whole, held) = refs[chips + 2 : -3][::-1], refs[-3:]
+    t, chip, _ = place()
     width = pieces[0].shape[1]
     tiles = width // LANES
+    part = held.shape[1]
     saved = jnp.concatenate([packed[1], received[:, chips * width : chips * width + HD]], axis=1)
     head = None
     for k in range(chips):
         weight = jnp.concatenate([kept[k], received[:, k * width : (k + 1) * width]], axis=0)
         wide = pieces[k][...].astype(jnp.float32)
+        whole[...] = wide
+        held[k] = whole[pl.ds(pl.multiple_of(chip * part, part), part), :]
         gated = jnp.concatenate(
             [
                 (wide[r * QF : (r + 1) * QF] * gate_a[k, r : r + 1, :]).astype(jnp.bfloat16)
@@ -117,8 +121,8 @@
             ],
             axis=0,
         )
-        part = dot(gated, weight, 1, 1)
-        head = part if head is None else head + part
+        add = dot(gated, weight, 1, 1)
+        head = add if head is None else head + add
         product = wide * dot(saved, weight, 1, 0)
         for r in range(frames):
             term = jnp.sum(product[r * QF : (r + 1) * QF], axis=0, keepdims=True)
@@ -127,13 +131,11 @@
                 terms[pl.ds(row, 1), :] = term[:, j * LANES : (j + 1) * LANES]
     mine[...] = head[:, :HD]
     other[...] = head[:, HD:]
-
-
-def sections(rows, chips, tiles, n_t, count):
-    starts = [0, rows]
-    starts.append(starts[-1] + tiles * (rows // chips))
-    starts.append(starts[-1] + -(-(SPLIT * 2 * n_t + count) // 16) * 16)
-    return starts
+    for k in range(chips):
+        rows = held[chip ^ t ^ k]
+        rows = [rows[:, j * LANES : (j + 1) * LANES] for j in range(tiles)]
+        out = padded(jnp.concatenate(rows + [terms[...]], axis=0), messages[k].shape[0])
+        messages[k][...] = out.astype(jnp.bfloat16)
 
 
 def padded(x, rows):
@@ -142,35 +144,23 @@
     return jnp.concatenate([x, jnp.zeros((rows - x.shape[0], x.shape[1]), x.dtype)], axis=0)
 
 
-def join_kernel(n_t, chips, starts, mine, received, stats, terms, *refs):
-    pieces, outs, (wide, held) = refs[:chips], refs[chips : chips + n_t][::-1], refs[chips + n_t :]
-    t, chip, _ = place()
-    part, tiles = held.shape[1], held.shape[2] // LANES
-    for k in range(chips):
-        wide[...] = pieces[k][...].astype(jnp.float32)
-        held[k] = wide[pl.ds(pl.multiple_of(chip * part, part), part), :]
-    head = (mine[...] + received[...]).astype(jnp.bfloat16)
+def join_kernel(mine, received, stats, out):
+    rows = mine.shape[0]
+    out[:rows, :] = (mine[...] + received[...]).astype(jnp.bfloat16)
     rest = stats[...]
     split = []
     for _ in range(SPLIT):
         piece = rest.astype(jnp.bfloat16).astype(jnp.float32)
         split.append(piece)
         rest = rest - piece
-    last = padded(jnp.concatenate(split + [terms[...]], axis=0), starts[3] - starts[2])
-    last = last.astype(jnp.bfloat16)
-    for k in range(n_t):
-        rows = held[chip ^ t ^ k]
-        rows = jnp.concatenate([rows[:, j * LANES : (j + 1) * LANES] for j in range(tiles)], axis=0)
-        outs[k][: starts[1], :] = head
-        outs[k][starts[1] : starts[2], :] = rows.astype(jnp.bfloat16)
-        outs[k][starts[2] :, :] = last
-
-
-def bundle_kernel(n_t, starts, count, gate_b, *refs):
-    heads, out = refs[:n_t][::-1], refs[n_t]
+    split = padded(jnp.concatenate(split, axis=0), out.shape[0] - rows)
+    out[rows:, :] = split.astype(jnp.bfloat16)
+
+
+def bundle_kernel(n_t, part, count, gate_b, *refs):
+    messages, out = refs[:n_t], refs[n_t]
     tiles = gate_b.shape[2] // LANES
-    part = (starts[2] - starts[1]) // tiles
-    wide = [heads[k][starts[1] : starts[2], :].astype(jnp.float32) for k in range(n_t)]
+    wide = [messages[k][...].astype(jnp.float32) for k in range(n_t)]
     for j in range(tiles):
         gated = jnp.concatenate(
             [
@@ -180,8 +170,7 @@
             axis=0,
         )
         out[j * n_t * part : (j + 1) * n_t * part, :] = gated.astype(jnp.bfloat16)
-    first = SPLIT * 2 * n_t
-    terms = [heads[k][starts[2] :, :].astype(jnp.float32)[first : first + count] for k in range(n_t)]
+    terms = [wide[k][tiles * part : tiles * part + count] for k in range(n_t)]
     out[tiles * n_t * part :, :] = jnp.concatenate(terms, axis=0).astype(jnp.bfloat16)
 
 
@@ -200,8 +189,8 @@
     out[chips * base + count :, :] = (total - high.astype(jnp.float32)).astype(jnp.bfloat16)
 
 
-def grads_kernel(n_t, starts, bias, keys, values, *refs):
-    packed, heads = refs[:n_t], refs[n_t : 2 * n_t][::-1]
+def grads_kernel(n_t, bias, keys, values, *refs):
+    packed, heads = refs[:n_t], refs[n_t : 2 * n_t]
     key_out, value_out = refs[2 * n_t : 2 * n_t + 2]
     outs = refs[2 * n_t + 2 : 3 * n_t + 2][::-1]
     key_acc, value_acc = refs[3 * n_t + 2 :]
@@ -210,7 +199,7 @@
     keys_t = jnp.transpose(keys[...])
     stats = []
     for k in range(n_t):
-        parts = heads[k][starts[2] :, :].astype(jnp.float32)
+        parts = heads[k][rows:, :].astype(jnp.float32)
         stats.append(sum(parts[i * 2 * n_t : (i + 1) * 2 * n_t] for i in range(SPLIT)))
     for p in range(0, n_t, 2):
         q = jnp.concatenate([packed[p][0], packed[p + 1][0]], axis=0)
@@ -392,7 +381,6 @@
     tiles = width // LANES
     part = rows // chips
     count = chips * frames * tiles
-    starts = sections(rows, chips, tiles, n_t, count)
 
     def time_swaps(messages):
         got = {k: over_time(messages[k], k) for k in range(n_t - 1, 0, -1)}
@@ -424,12 +412,20 @@
         ],
         in_smem=2,
     )
-    mine, other, terms = call(
+    base = tiles * n_t * part
+    length = -(-(tiles * part + count) // 16) * 16
+    mine, other, *shares = call(
         functools.partial(head_kernel, chips, frames),
         [packed, kept, received, gate_a] + pieces,
-        [shape(f32, rows, HD), shape(f32, rows, HD), shape(f32, count, LANES)],
+        [shape(f32, rows, HD)] * 2 + [shape(bf16, length, LANES)] * n_t,
+        [
+            pltpu.VMEM((count, LANES), f32),
+            pltpu.VMEM((rows, width), f32),
+            pltpu.VMEM((chips, part, width), f32),
+        ],
         flops=4 * rows * chips * width * 2 * HD,
     )
+    shares = time_swaps(shares[::-1])
     later_bias, _ = lax.optimization_barrier((bias, mine))
     stats = call(
         functools.partial(stats_kernel, n_t),
@@ -437,24 +433,22 @@
         shape(f32, 2 * n_t, LANES),
         flops=2 * n_t * rows * k_rows * HD,
     )
-    heads = call(
-        functools.partial(join_kernel, n_t, chips, starts),
-        [mine, over_cores(other), stats, terms] + pieces,
-        [shape(bf16, starts[-1], LANES)] * n_t,
-        [pltpu.VMEM((rows, width), f32), pltpu.VMEM((chips, part, width), f32)],
-    )
-    heads_all = time_swaps(heads[::-1])
-    base = tiles * n_t * part
+    message = call(
+        join_kernel,
+        [mine, over_cores(other), stats],
+        shape(bf16, rows + -(-SPLIT * 2 * n_t // 16) * 16, LANES),
+    )
+    heads_all = time_swaps([message] * n_t)
     bundle = call(
-        functools.partial(bundle_kernel, n_t, starts, count),
-        [gate_b] + heads_all[::-1],
+        functools.partial(bundle_kernel, n_t, part, count),
+        [gate_b] + shares,
         shape(bf16, base + n_t * count, LANES),
     )
     bundles = over_chips(bundle)
     later_bias, _ = lax.optimization_barrier((bias, bundle))
     outs = call(
-        functools.partial(grads_kernel, n_t, starts),
-        [later_bias, keys, values] + packed_all + heads_all[::-1],
+        functools.partial(grads_kernel, n_t),
+        [later_bias, keys, values] + packed_all + heads_all,
         [shape(bf16, k_rows, HD)] * 2 + [shape(bf16, HD, rows)] * n_t,
         [pltpu.VMEM((k_rows, HD), f32)] * 2,
         flops=10 * n_t * rows * k_rows * HD,

time: 49.4 us -> 52.2 us (1.057)
  starting transfers between devices: 21.3 us -> 26.8 us
  waiting for transfers between devices: 17.5 us -> 14.8 us
    ppermute x9 -> x12, starting transfers between devices: 12.9 us -> 18.4 us  [over_time(): return lax.ppermute(x, 'tm', [(t, t ^ k) for t in range(n_t)])]
    ppermute x9 -> x12, waiting for transfers between devices: 15.7 us -> 13.1 us  [over_time(): return lax.ppermute(x, 'tm', [(t, t ^ k) for t in range(n_t)])]
  transfers between devices with their start and end apart: 18 -> 21, of which waited for: 10 -> 9; matrix products, arithmetic and copies ran while one was open for 0% -> 0% of each run, Pallas kernels for 12% -> 11%
where the time goes in v10:
time: 52.2 us; the launch traced here: 52.1 us
  starting transfers between devices  26.8 us (51%)
  waiting for transfers between devices  14.8 us (28%)
  Pallas kernels  8.84 us (17%)
  local copies, waits for them, and re-layouts  0.84 us (2%)
  between operations  0.78 us (1%)
    ppermute x12, starting transfers between devices, over_time(): return lax.ppermute(x, 'tm', [(t, t ^ k) for t in range(n_t)])  18.4 us
    ppermute x12, waiting for transfers between devices, over_time(): return lax.ppermute(x, 'tm', [(t, t ^ k) for t in range(n_t)])  13.1 us
    pallas_call x11, Pallas kernels, call(): pl.pallas_call(kernel, out_shape=out_shape, in_specs=[pl.BlockSpec(memory...  8.84 us
    ppermute x6, starting transfers between devices, over_chips(): lax.ppermute(x, 'space', [(s, s ^ 2 * k) for s in range(n_s)])  7.69 us
    ppermute x3, waiting for transfers between devices, over_cores(): return lax.ppermute(x, 'space', [(s, s ^ 1) for s in range(n_s)])  1.08 us
  transfers between devices with their start and end apart: 21, of which 9 were waited for; matrix products, arithmetic and copies ran while one was open for 0% of the time, Pallas kernels for 11%

profile of v10, /device:TPU:0, one launch (start us, length us, event | category | flops | bytes accessed | tf_op | source)
XLA Modules:
  0.0 52.1 jit_solution(15814459162975909616)
XLA Ops:
  0.7 0.8 %copy-done.3 = bf16[128,128]{1,0:T(8,128)(2,1)S(1)} copy-done((bf16[128,128]{1,0:T(8,128)(2,1)S(1)}, bf16[128,128]{1,0:T(8,128)(2,1)}, u32[]{:S(2)}) %copy-start.3) | copy-done | bytes 32792
  1.5 1.5 %shard_map.128 = (bf16[4,128,640]{2,1,0:T(8,128)(2,1)S(1)}, bf16[128,2688]{1,0:T(8,128)(2,1)S(1)}) custom-call(bf16[128,5120]{1,0:T(8,128)(2,1)} %weight_in.1, bf16[128,128]{1,0:T(8,128)(2,1)S(1)} %copy-done.3), custom_call_target="tpu_custom_call" | custom-call | bytes 1343488 | tf_op jit(solution)/shard_map/pallas_call | solution.py:327
  3.5 2.6 %collective-permute-start.2 = (bf16[128,640]{1,0:T(8,128)(2,1)S(1)}, bf16[128,640]{1,0:T(8,128)(2,1)S(1)}, u32[]{:S(2)}, u32[]{:S(2)}) collective-permute-start(bf16[128,640]{1,0:T(8,128)(2,1)S(1)} %copy-done.2), channel_id=1, source_target_pairs={{0,4},{1,5},{2,6},{3,7},{4,0},{5,1},{6,2},{7,3},{8,12},{9,13},{10,... | collective-permute-start | bytes 491528 | tf_op jit(solution)/shard_map/ppermute | solution.py:372
  6.1 1.5 %collective-permute-start.1 = (bf16[128,640]{1,0:T(8,128)(2,1)S(1)}, bf16[128,640]{1,0:T(8,128)(2,1)S(1)}, u32[]{:S(2)}, u32[]{:S(2)}) collective-permute-start(bf16[128,640]{1,0:T(8,128)(2,1)S(1)} %copy-done.2), channel_id=1, source_target_pairs={{0,2},{1,3},{2,0},{3,1},{4,6},{5,7},{6,4},{7,5},{8,10},{9,11},{10,... | collective-permute-start | bytes 491528 | tf_op jit(solution)/shard_map/ppermute | solution.py:372
  7.7 3.1 %collective-permute-start.8 = (bf16[2,128,128]{2,1,0:T(8,128)(2,1)S(1)}, bf16[2,128,128]{2,1,0:T(8,128)(2,1)S(1)}, u32[]{:S(2)}, u32[]{:S(2)}) collective-permute-start(bf16[2,128,128]{2,1,0:T(8,128)(2,1)S(1)} %pad_maximum_fusion.packed.refs_0_), channel_id=1, source_target_pairs={{0,16},{8,24},{16,0},{24,8},{1,17},{9,25},{17,1},{25,9},{2,18},{10... | collective-permute-start | bytes 196616 | tf_op jit(solution)/shard_map/ppermute | solution.py:379
  10.8 1.6 %collective-permute-start.7 = (bf16[2,128,128]{2,1,0:T(8,128)(2,1)S(1)}, bf16[2,128,128]{2,1,0:T(8,128)(2,1)S(1)}, u32[]{:S(2)}, u32[]{:S(2)}) collective-permute-start(bf16[2,128,128]{2,1,0:T(8,128)(2,1)S(1)} %pad_maximum_fusion.packed.refs_0_), channel_id=1, source_target_pairs={{0,8},{8,0},{16,24},{24,16},{1,9},{9,1},{17,25},{25,17},{2,10},{10... | collective-permute-start | bytes 196616 | tf_op jit(solution)/shard_map/ppermute | solution.py:379
  13.0 0.8 %collective-permute-done.8.refs_2_ = bf16[2,128,128]{2,1,0:T(8,128)(2,1)S(1)} collective-permute-done((bf16[2,128,128]{2,1,0:T(8,128)(2,1)S(1)}, bf16[2,128,128]{2,1,0:T(8,128)(2,1)S(1)}, u32[]{:S(2)}, u32[]{:S(2)}) %collective-permute-start.8) | collective-permute-done | bytes 65568 | tf_op jit(solution)/shard_map/ppermute | solution.py:379
  13.8 1.2 %collective-permute-start.9 = (bf16[2,128,128]{2,1,0:T(8,128)(2,1)S(1)}, bf16[2,128,128]{2,1,0:T(8,128)(2,1)S(1)}, u32[]{:S(2)}, u32[]{:S(2)}) collective-permute-start(bf16[2,128,128]{2,1,0:T(8,128)(2,1)S(1)} %collective-permute-done.8.refs_2_), channel_id=1, source_target_pairs={{0,8},{8,0},{16,24},{24,16},{1,9},{9,1},{17,25},{25,17},{2,10},{10... | collective-permute-start | bytes 196616 | tf_op jit(solution)/shard_map/ppermute | solution.py:379
  15.6 0.9 %shard_map.130 = (f32[128,128]{1,0:T(8,128)S(1)}, f32[128,128]{1,0:T(8,128)S(1)}, bf16[208,128]{1,0:T(8,128)(2,1)S(1)}, bf16[208,128]{1,0:T(8,128)(2,1)S(1)}, bf...) custom-call(bf16[2,128,128]{2,1,0:T(8,128)(2,1)S(1)} %pad_maximum_fusion.packed.refs_0_, ...), custom_call_target="tpu_custom_call" | custom-call | flops 335544320 | bytes 2084864 | tf_op jit(solution)/shard_map/pallas_call | solution.py:327
  16.6 1.9 %collective-permute-start.4 = (bf16[208,128]{1,0:T(8,128)(2,1)S(1)}, bf16[208,128]{1,0:T(8,128)(2,1)S(1)}, u32[]{:S(2)}, u32[]{:S(2)}) collective-permute-start(bf16[208,128]{1,0:T(8,128)(2,1)S(1)} %get-tuple-element.43), channel_id=1, source_target_pairs={{0,8},{8,0},{16,24},{24,16},{1,9},{9,1},{17,25},{25,17},{2,10},{10... | collective-permute-start | bytes 159752 | tf_op jit(solution)/shard_map/ppermute | solution.py:379
  18.5 2.6 %collective-permute-start.5 = (bf16[208,128]{1,0:T(8,128)(2,1)S(1)}, bf16[208,128]{1,0:T(8,128)(2,1)S(1)}, u32[]{:S(2)}, u32[]{:S(2)}) collective-permute-start(bf16[208,128]{1,0:T(8,128)(2,1)S(1)} %get-tuple-element.44), channel_id=1, source_target_pairs={{0,16},{8,24},{16,0},{24,8},{1,17},{9,25},{17,1},{25,9},{2,18},{10... | collective-permute-start | bytes 159752 | tf_op jit(solution)/shard_map/ppermute | solution.py:379
  21.1 0.8 %shard_map.132.stats = f32[8,128]{1,0:T(8,128)S(1)} custom-call(f32[2,512]{1,0:T(2,128)S(1)} %get-tuple-element.49.bias, bf16[1024,128]{1,0:T(8,128)(2,1)S(1)} %copy-done.1, bf16[2,128,128]{2,1,0:T(8,128)(2,1)S(1)} %pad_maximum_fusion.packed.refs_0_, bf16[2,128,128]{2,1,0:T(8,128)(2,1)S(1)} %collective-permute-done.7.refs_1_, ...), custom_call_target="tpu_custom_call" | custom-call | flops 134217728 | bytes 528384 | tf_op jit(solution)/shard_map/pallas_call | solution.py:327
  21.9 3.9 %collective-permute-start.13 = (bf16[160,128]{1,0:T(8,128)(2,1)S(1)}, bf16[160,128]{1,0:T(8,128)(2,1)S(1)}, u32[]{:S(2)}, u32[]{:S(2)}) collective-permute-start(bf16[160,128]{1,0:T(8,128)(2,1)S(1)} %shard_map.133.refs_4_), channel_id=1, source_target_pairs={{0,24},{8,16},{16,8},{24,0},{1,25},{9,17},{17,9},{25,1},{2,26},{10... | collective-permute-start | bytes 122888 | tf_op jit(solution)/shard_map/ppermute | solution.py:379
  25.8 1.5 %collective-permute-done.6.refs_3_ = bf16[208,128]{1,0:T(8,128)(2,1)S(1)} collective-permute-done((bf16[208,128]{1,0:T(8,128)(2,1)S(1)}, bf16[208,128]{1,0:T(8,128)(2,1)S(1)}, u32[]{:S(2)}, u32[]{:S(2)}) %collective-permute-start.6) | collective-permute-done | bytes 53280 | tf_op jit(solution)/shard_map/ppermute | solution.py:379
  27.4 2.5 %collective-permute-start.19 = (bf16[800,128]{1,0:T(8,128)(2,1)S(1)}, bf16[800,128]{1,0:T(8,128)(2,1)S(1)}, u32[]{:S(2)}, u32[]{:S(2)}) collective-permute-start(bf16[800,128]{1,0:T(8,128)(2,1)S(1)} %shard_map.131.refs_0_), channel_id=1, source_target_pairs={{0,6},{1,7},{2,4},{3,5},{4,2},{5,3},{6,0},{7,1},{8,14},{9,15},{10,... | collective-permute-start | bytes 614408 | tf_op jit(solution)/shard_map/ppermute | solution.py:372
  30.9 1.4 %collective-permute-start.12 = (bf16[160,128]{1,0:T(8,128)(2,1)S(1)}, bf16[160,128]{1,0:T(8,128)(2,1)S(1)}, u32[]{:S(2)}, u32[]{:S(2)}) collective-permute-start(bf16[160,128]{1,0:T(8,128)(2,1)S(1)} %shard_map.133.refs_4_), channel_id=1, source_target_pairs={{0,16},{8,24},{16,0},{24,8},{1,17},{9,25},{17,1},{25,9},{2,18},{10... | collective-permute-start | bytes 122888 | tf_op jit(solution)/shard_map/ppermute | solution.py:379
  33.0 2.8 %collective-permute-done.12.refs_6_ = bf16[160,128]{1,0:T(8,128)(2,1)S(1)} collective-permute-done((bf16[160,128]{1,0:T(8,128)(2,1)S(1)}, bf16[160,128]{1,0:T(8,128)(2,1)S(1)}, u32[]{:S(2)}, u32[]{:S(2)}) %collective-permute-start.12) | collective-permute-done | bytes 40992 | tf_op jit(solution)/shard_map/ppermute | solution.py:379
  36.3 2.4 %shard_map.134 = (bf16[1024,128]{1,0:T(8,128)(2,1)}, bf16[1024,128]{1,0:T(8,128)(2,1)}, bf16[128,128]{1,0:T(8,128)(2,1)S(1)}, bf16[128,128]{1,0:T(8,128)(2,1)S(1...) custom-call(f32[2,512]{1,0:T(2,128)S(1)} %get-tuple-element.49.bias, bf16[1024,128]{1,0:T(8,128)(2,1)S(1)} %copy-done.1, ...), custom_call_target="tpu_custom_call" | custom-call | flops 671088640 | bytes 954368 | tf_op jit(solution)/shard_map/pallas_call | solution.py:327
  38.8 2.2 %collective-permute-start.14 = (bf16[128,128]{1,0:T(8,128)(2,1)S(1)}, bf16[128,128]{1,0:T(8,128)(2,1)S(1)}, u32[]{:S(2)}, u32[]{:S(2)}) collective-permute-start(bf16[128,128]{1,0:T(8,128)(2,1)S(1)} %get-tuple-element.50), channel_id=1, source_target_pairs={{0,24},{8,16},{16,8},{24,0},{1,25},{9,17},{17,9},{25,1},{2,26},{10... | collective-permute-start | bytes 98312 | tf_op jit(solution)/shard_map/ppermute | solution.py:379
  41.0 3.5 %collective-permute-done.14.refs_0_ = bf16[128,128]{1,0:T(8,128)(2,1)S(1)} collective-permute-done((bf16[128,128]{1,0:T(8,128)(2,1)S(1)}, bf16[128,128]{1,0:T(8,128)(2,1)S(1)}, u32[]{:S(2)}, u32[]{:S(2)}) %collective-permute-start.14) | collective-permute-done | bytes 32800 | tf_op jit(solution)/shard_map/ppermute | solution.py:379
  44.5 1.3 %collective-permute-done.15.refs_1_ = bf16[128,128]{1,0:T(8,128)(2,1)S(1)} collective-permute-done((bf16[128,128]{1,0:T(8,128)(2,1)S(1)}, bf16[128,128]{1,0:T(8,128)(2,1)S(1)}, u32[]{:S(2)}, u32[]{:S(2)}) %collective-permute-start.15) | collective-permute-done | bytes 32800 | tf_op jit(solution)/shard_map/ppermute | solution.py:379
  45.8 2.6 %collective-permute-done.16.refs_2_ = bf16[128,128]{1,0:T(8,128)(2,1)S(1)} collective-permute-done((bf16[128,128]{1,0:T(8,128)(2,1)S(1)}, bf16[128,128]{1,0:T(8,128)(2,1)S(1)}, u32[]{:S(2)}, u32[]{:S(2)}) %collective-permute-start.16) | collective-permute-done | bytes 32800 | tf_op jit(solution)/shard_map/ppermute | solution.py:379
  49.7 1.1 %collective-permute-done.20.other = bf16[2880,128]{1,0:T(8,128)(2,1)S(1)} collective-permute-done((bf16[2880,128]{1,0:T(8,128)(2,1)S(1)}, bf16[2880,128]{1,0:T(8,128)(2,1)S(1)}, u32[]{:S(2)}, u32[]{:S(2)}) %collective-permute-start.20) | collective-permute-done | bytes 737312 | tf_op jit(solution)/shard_map/ppermute | solution.py:376
  50.8 1.3 %shard_map.138 = (f32[128,1280]{1,0:T(8,128)}, f32[16,5120]{1,0:T(8,128)}) custom-call(f32[8,16,128]{2,1,0:T(8,128)S(1)} %get-tuple-element.56.hot, bf16[2880,128]{1,0:T(8,128)(2,1)S(1)} %collective-permute-done.20.other, f32[128,640]{1,0:T(8,128)S(1)} %get-tuple-element.61.own_weight, f32[16,2560]{1,0:T(8,128)S(1)} %get-tuple-element.62.own_gate, ...), custom_call_target="tpu_custom_call" | custom-call | flops 83886080 | bytes 1556480 | tf_op jit(solution)/shard_map/pallas_call | solution.py:327
  (46 shorter events, 5.6 us)
Async XLA Ops:
  0.6 11.7 %copy-start = (f32[16,5120]{1,0:T(8,128)S(1)}, f32[16,5120]{1,0:T(8,128)}, u32[]{:S(2)}) copy-start(f32[16,5120]{1,0:T(8,128)} %gate) | copy-start | bytes 983044
  3.0 18.1 %copy-start.1 = (bf16[1024,128]{1,0:T(8,128)(2,1)S(1)}, bf16[1024,128]{1,0:T(8,128)(2,1)}, u32[]{:S(2)}) copy-start(bf16[1024,128]{1,0:T(8,128)(2,1)} %keys.3) | copy-start | bytes 786436
  3.0 4.7 %collective-permute-start = (bf16[128,2688]{1,0:T(8,128)(2,1)S(1)}, bf16[128,2688]{1,0:T(8,128)(2,1)S(1)}, u32[]{:S(2)}, u32[]{:S(2)}) collective-permute-start(bf16[128,2688]{1,0:T(8,128)(2,1)S(1)} %get-tuple-element.35), channel_id=1, source_target_pairs={{0,1},{1,0},{2,3},{3,2},{4,5},{5,4},{6,7},{7,6},{8,9},{9,8},{10,11... | collective-permute-start | bytes 2064392 | tf_op jit(solution)/shard_map/ppermute | solution.py:376
  3.5 11.4 %collective-permute-start.2 = (bf16[128,640]{1,0:T(8,128)(2,1)S(1)}, bf16[128,640]{1,0:T(8,128)(2,1)S(1)}, u32[]{:S(2)}, u32[]{:S(2)}) collective-permute-start(bf16[128,640]{1,0:T(8,128)(2,1)S(1)} %copy-done.2), channel_id=1, source_target_pairs={{0,4},{1,5},{2,6},{3,7},{4,0},{5,1},{6,2},{7,3},{8,12},{9,13},{10,... | collective-permute-start | bytes 491528 | tf_op jit(solution)/shard_map/ppermute | solution.py:372
  6.1 8.8 %collective-permute-start.1 = (bf16[128,640]{1,0:T(8,128)(2,1)S(1)}, bf16[128,640]{1,0:T(8,128)(2,1)S(1)}, u32[]{:S(2)}, u32[]{:S(2)}) collective-permute-start(bf16[128,640]{1,0:T(8,128)(2,1)S(1)} %copy-done.2), channel_id=1, source_target_pairs={{0,2},{1,3},{2,0},{3,1},{4,6},{5,7},{6,4},{7,5},{8,10},{9,11},{10,... | collective-permute-start | bytes 491528 | tf_op jit(solution)/shard_map/ppermute | solution.py:372
  7.6 8.0 %collective-permute-start.3 = (bf16[128,640]{1,0:T(8,128)(2,1)S(1)}, bf16[128,640]{1,0:T(8,128)(2,1)S(1)}, u32[]{:S(2)}, u32[]{:S(2)}) collective-permute-start(bf16[128,640]{1,0:T(8,128)(2,1)S(1)} %copy-done.2), channel_id=1, source_target_pairs={{0,6},{1,7},{2,4},{3,5},{4,2},{5,3},{6,0},{7,1},{8,14},{9,15},{10,... | collective-permute-start | bytes 491528 | tf_op jit(solution)/shard_map/ppermute | solution.py:372
  7.7 6.1 %collective-permute-start.8 = (bf16[2,128,128]{2,1,0:T(8,128)(2,1)S(1)}, bf16[2,128,128]{2,1,0:T(8,128)(2,1)S(1)}, u32[]{:S(2)}, u32[]{:S(2)}) collective-permute-start(bf16[2,128,128]{2,1,0:T(8,128)(2,1)S(1)} %pad_maximum_fusion.packed.refs_0_), channel_id=1, source_target_pairs={{0,16},{8,24},{16,0},{24,8},{1,17},{9,25},{17,1},{25,9},{2,18},{10... | collective-permute-start | bytes 196616 | tf_op jit(solution)/shard_map/ppermute | solution.py:379
  10.8 10.3 %collective-permute-start.7 = (bf16[2,128,128]{2,1,0:T(8,128)(2,1)S(1)}, bf16[2,128,128]{2,1,0:T(8,128)(2,1)S(1)}, u32[]{:S(2)}, u32[]{:S(2)}) collective-permute-start(bf16[2,128,128]{2,1,0:T(8,128)(2,1)S(1)} %pad_maximum_fusion.packed.refs_0_), channel_id=1, source_target_pairs={{0,8},{8,0},{16,24},{24,16},{1,9},{9,1},{17,25},{25,17},{2,10},{10... | collective-permute-start | bytes 196616 | tf_op jit(solution)/shard_map/ppermute | solution.py:379
  13.8 7.3 %collective-permute-start.9 = (bf16[2,128,128]{2,1,0:T(8,128)(2,1)S(1)}, bf16[2,128,128]{2,1,0:T(8,128)(2,1)S(1)}, u32[]{:S(2)}, u32[]{:S(2)}) collective-permute-start(bf16[2,128,128]{2,1,0:T(8,128)(2,1)S(1)} %collective-permute-done.8.refs_2_), channel_id=1, source_target_pairs={{0,8},{8,0},{16,24},{24,16},{1,9},{9,1},{17,25},{25,17},{2,10},{10... | collective-permute-start | bytes 196616 | tf_op jit(solution)/shard_map/ppermute | solution.py:379
  15.6 20.7 %copy-start.6 = (bf16[1024,128]{1,0:T(8,128)(2,1)S(1)}, bf16[1024,128]{1,0:T(8,128)(2,1)}, u32[]{:S(2)}) copy-start(bf16[1024,128]{1,0:T(8,128)(2,1)} %values.1) | copy-start | bytes 786436
  16.5 5.3 %collective-permute-start.10 = (f32[128,128]{1,0:T(8,128)S(1)}, f32[128,128]{1,0:T(8,128)S(1)}, u32[]{:S(2)}, u32[]{:S(2)}) collective-permute-start(f32[128,128]{1,0:T(8,128)S(1)} %get-tuple-element.48), channel_id=1, source_target_pairs={{0,1},{1,0},{2,3},{3,2},{4,5},{5,4},{6,7},{7,6},{8,9},{9,8},{10,11... | collective-permute-start | bytes 196616 | tf_op jit(solution)/shard_map/ppermute | solution.py:376
  16.6 9.2 %collective-permute-start.4 = (bf16[208,128]{1,0:T(8,128)(2,1)S(1)}, bf16[208,128]{1,0:T(8,128)(2,1)S(1)}, u32[]{:S(2)}, u32[]{:S(2)}) collective-permute-start(bf16[208,128]{1,0:T(8,128)(2,1)S(1)} %get-tuple-element.43), channel_id=1, source_target_pairs={{0,8},{8,0},{16,24},{24,16},{1,9},{9,1},{17,25},{25,17},{2,10},{10... | collective-permute-start | bytes 159752 | tf_op jit(solution)/shard_map/ppermute | solution.py:379
  18.5 7.3 %collective-permute-start.5 = (bf16[208,128]{1,0:T(8,128)(2,1)S(1)}, bf16[208,128]{1,0:T(8,128)(2,1)S(1)}, u32[]{:S(2)}, u32[]{:S(2)}) collective-permute-start(bf16[208,128]{1,0:T(8,128)(2,1)S(1)} %get-tuple-element.44), channel_id=1, source_target_pairs={{0,16},{8,24},{16,0},{24,8},{1,17},{9,25},{17,1},{25,9},{2,18},{10... | collective-permute-start | bytes 159752 | tf_op jit(solution)/shard_map/ppermute | solution.py:379
  21.1 6.2 %collective-permute-start.6 = (bf16[208,128]{1,0:T(8,128)(2,1)S(1)}, bf16[208,128]{1,0:T(8,128)(2,1)S(1)}, u32[]{:S(2)}, u32[]{:S(2)}) collective-permute-start(bf16[208,128]{1,0:T(8,128)(2,1)S(1)} %get-tuple-element.45), channel_id=1, source_target_pairs={{0,24},{8,16},{16,8},{24,0},{1,25},{9,17},{17,9},{25,1},{2,26},{10... | collective-permute-start | bytes 159752 | tf_op jit(solution)/shard_map/ppermute | solution.py:379
  21.9 10.4 %collective-permute-start.13 = (bf16[160,128]{1,0:T(8,128)(2,1)S(1)}, bf16[160,128]{1,0:T(8,128)(2,1)S(1)}, u32[]{:S(2)}, u32[]{:S(2)}) collective-permute-start(bf16[160,128]{1,0:T(8,128)(2,1)S(1)} %shard_map.133.refs_4_), channel_id=1, source_target_pairs={{0,24},{8,16},{16,8},{24,0},{1,25},{9,17},{17,9},{25,1},{2,26},{10... | collective-permute-start | bytes 122888 | tf_op jit(solution)/shard_map/ppermute | solution.py:379
  27.4 21.0 %collective-permute-start.19 = (bf16[800,128]{1,0:T(8,128)(2,1)S(1)}, bf16[800,128]{1,0:T(8,128)(2,1)S(1)}, u32[]{:S(2)}, u32[]{:S(2)}) collective-permute-start(bf16[800,128]{1,0:T(8,128)(2,1)S(1)} %shard_map.131.refs_0_), channel_id=1, source_target_pairs={{0,6},{1,7},{2,4},{3,5},{4,2},{5,3},{6,0},{7,1},{8,14},{9,15},{10,... | collective-permute-start | bytes 614408 | tf_op jit(solution)/shard_map/ppermute | solution.py:372
  29.9 18.5 %collective-permute-start.18 = (bf16[800,128]{1,0:T(8,128)(2,1)S(1)}, bf16[800,128]{1,0:T(8,128)(2,1)S(1)}, u32[]{:S(2)}, u32[]{:S(2)}) collective-permute-start(bf16[800,128]{1,0:T(8,128)(2,1)S(1)} %shard_map.131.refs_0_), channel_id=1, source_target_pairs={{0,4},{1,5},{2,6},{3,7},{4,0},{5,1},{6,2},{7,3},{8,12},{9,13},{10,... | collective-permute-start | bytes 614408 | tf_op jit(solution)/shard_map/ppermute | solution.py:372
  30.4 18.0 %collective-permute-start.17 = (bf16[800,128]{1,0:T(8,128)(2,1)S(1)}, bf16[800,128]{1,0:T(8,128)(2,1)S(1)}, u32[]{:S(2)}, u32[]{:S(2)}) collective-permute-start(bf16[800,128]{1,0:T(8,128)(2,1)S(1)} %shard_map.131.refs_0_), channel_id=1, source_target_pairs={{0,2},{1,3},{2,0},{3,1},{4,6},{5,7},{6,4},{7,5},{8,10},{9,11},{10,... | collective-permute-start | bytes 614408 | tf_op jit(solution)/shard_map/ppermute | solution.py:372
  30.9 4.9 %collective-permute-start.12 = (bf16[160,128]{1,0:T(8,128)(2,1)S(1)}, bf16[160,128]{1,0:T(8,128)(2,1)S(1)}, u32[]{:S(2)}, u32[]{:S(2)}) collective-permute-start(bf16[160,128]{1,0:T(8,128)(2,1)S(1)} %shard_map.133.refs_4_), channel_id=1, source_target_pairs={{0,16},{8,24},{16,0},{24,8},{1,17},{9,25},{17,1},{25,9},{2,18},{10... | collective-permute-start | bytes 122888 | tf_op jit(solution)/shard_map/ppermute | solution.py:379
  32.3 4.0 %collective-permute-start.11 = (bf16[160,128]{1,0:T(8,128)(2,1)S(1)}, bf16[160,128]{1,0:T(8,128)(2,1)S(1)}, u32[]{:S(2)}, u32[]{:S(2)}) collective-permute-start(bf16[160,128]{1,0:T(8,128)(2,1)S(1)} %shard_map.133.refs_4_), channel_id=1, source_target_pairs={{0,8},{8,0},{16,24},{24,16},{1,9},{9,1},{17,25},{25,17},{2,10},{10... | collective-permute-start | bytes 122888 | tf_op jit(solution)/shard_map/ppermute | solution.py:379
  38.8 5.7 %collective-permute-start.14 = (bf16[128,128]{1,0:T(8,128)(2,1)S(1)}, bf16[128,128]{1,0:T(8,128)(2,1)S(1)}, u32[]{:S(2)}, u32[]{:S(2)}) collective-permute-start(bf16[128,128]{1,0:T(8,128)(2,1)S(1)} %get-tuple-element.50), channel_id=1, source_target_pairs={{0,24},{8,16},{16,8},{24,0},{1,25},{9,17},{17,9},{25,1},{2,26},{10... | collective-permute-start | bytes 98312 | tf_op jit(solution)/shard_map/ppermute | solution.py:379
  41.0 4.8 %collective-permute-start.15 = (bf16[128,128]{1,0:T(8,128)(2,1)S(1)}, bf16[128,128]{1,0:T(8,128)(2,1)S(1)}, u32[]{:S(2)}, u32[]{:S(2)}) collective-permute-start(bf16[128,128]{1,0:T(8,128)(2,1)S(1)} %get-tuple-element.51), channel_id=1, source_target_pairs={{0,16},{8,24},{16,0},{24,8},{1,17},{9,25},{17,1},{25,9},{2,18},{10... | collective-permute-start | bytes 98312 | tf_op jit(solution)/shard_map/ppermute | solution.py:379
  44.5 3.9 %collective-permute-start.16 = (bf16[128,128]{1,0:T(8,128)(2,1)S(1)}, bf16[128,128]{1,0:T(8,128)(2,1)S(1)}, u32[]{:S(2)}, u32[]{:S(2)}) collective-permute-start(bf16[128,128]{1,0:T(8,128)(2,1)S(1)} %get-tuple-element.52), channel_id=1, source_target_pairs={{0,8},{8,0},{16,24},{24,16},{1,9},{9,1},{17,25},{25,17},{2,10},{10... | collective-permute-start | bytes 98312 | tf_op jit(solution)/shard_map/ppermute | solution.py:379
  48.5 2.3 %collective-permute-start.20 = (bf16[2880,128]{1,0:T(8,128)(2,1)S(1)}, bf16[2880,128]{1,0:T(8,128)(2,1)S(1)}, u32[]{:S(2)}, u32[]{:S(2)}) collective-permute-start(bf16[2880,128]{1,0:T(8,128)(2,1)S(1)} %shard_map.136.own), channel_id=1, source_target_pairs={{0,1},{1,0},{2,3},{3,2},{4,5},{5,4},{6,7},{7,6},{8,9},{9,8},{10,11... | collective-permute-start | bytes 2211848 | tf_op jit(solution)/shard_map/ppermute | solution.py:376
  (5 other events, 31.7 us)

commit v11 on v9

--- a/solution.py
+++ b/solution.py
@@ -461,14 +461,13 @@
     )
     key_grad, value_grad = outs[:2]
     parts = time_swaps(outs[2:][::-1])
-    bundles, _ = lax.optimization_barrier((bundles, parts[::-1]))
+    bundles, _ = lax.optimization_barrier((bundles, parts[: n_t // 2 - 1 : -1]))
     collected = call(
         functools.partial(collect_kernel, chips, base),
         bundles,
         shape(bf16, chips * base + 2 * n_t * count, LANES),
         [pltpu.VMEM((chips, n_t * count, LANES), f32)],
     )
-    query_grad = call(functools.partial(query_kernel, n_t), parts[::-1], shape(bf16, rows, HD))
     scratch = [pltpu.VMEM((n_t, rows, HD), f32), pltpu.VMEM((n_t, count, LANES), f32)]
     own_halves = call(
         functools.partial(own_kernel, n_t, chips, frames),
@@ -484,6 +483,8 @@
         scratch,
         flops=2 * n_t * rows * width * HD,
     )
+    parts[0], _ = lax.optimization_barrier((parts[0], gate_grad))
+    query_grad = call(functools.partial(query_kernel, n_t), parts[::-1], shape(bf16, rows, HD))
     if width != shard:
         weight_grad = without_padding(weight_grad, 2, shard)
         gate_grad = without_padding(gate_grad, n_s, shard)

time: 49.4 us -> 48 us (0.972)
  waiting for transfers between devices: 17.5 us -> 16 us
    ppermute x9, waiting for transfers between devices: 15.7 us -> 13.6 us  [over_time(): return lax.ppermute(x, 'tm', [(t, t ^ k) for t in range(n_t)])]
    ppermute x3, waiting for transfers between devices: 1.09 us -> 1.73 us  [over_cores(): return lax.ppermute(x, 'space', [(s, s ^ 1) for s in range(n_s)])]
  transfers between devices with their start and end apart: 18 -> 18, of which waited for: 10 -> 10; matrix products, arithmetic and copies ran while one was open for 0% -> 0% of each run, Pallas kernels for 12% -> 13%
where the time goes in v11:
time: 48 us; the launch traced here: 47.8 us
  starting transfers between devices  21.4 us (45%)
  waiting for transfers between devices  16 us (33%)
  Pallas kernels  8.78 us (18%)
  local copies, waits for them, and re-layouts  0.84 us (2%)
  between operations  0.79 us (2%)
    ppermute x9, waiting for transfers between devices, over_time(): return lax.ppermute(x, 'tm', [(t, t ^ k) for t in range(n_t)])  13.6 us
    ppermute x9, starting transfers between devices, over_time(): return lax.ppermute(x, 'tm', [(t, t ^ k) for t in range(n_t)])  13 us
    pallas_call x11, Pallas kernels, call(): pl.pallas_call(kernel, out_shape=out_shape, in_specs=[pl.BlockSpec(memory...  8.78 us
    ppermute x6, starting transfers between devices, over_chips(): lax.ppermute(x, 'space', [(s, s ^ 2 * k) for s in range(n_s)])  7.72 us
    ppermute x3, waiting for transfers between devices, over_cores(): return lax.ppermute(x, 'space', [(s, s ^ 1) for s in range(n_s)])  1.73 us
  transfers between devices with their start and end apart: 18, of which 10 were waited for; matrix products, arithmetic and copies ran while one was open for 0% of the time, Pallas kernels for 13%

profile of v11, /device:TPU:0, one launch (start us, length us, event | category | flops | bytes accessed | tf_op | source)
XLA Modules:
  0.0 47.8 jit_solution(9857883978658921569)
XLA Ops:
  0.7 0.8 %copy-done.3 = bf16[128,128]{1,0:T(8,128)(2,1)S(1)} copy-done((bf16[128,128]{1,0:T(8,128)(2,1)S(1)}, bf16[128,128]{1,0:T(8,128)(2,1)}, u32[]{:S(2)}) %copy-start.3) | copy-done | bytes 32792
  1.5 1.5 %shard_map.128 = (bf16[4,128,640]{2,1,0:T(8,128)(2,1)S(1)}, bf16[128,2688]{1,0:T(8,128)(2,1)S(1)}) custom-call(bf16[128,5120]{1,0:T(8,128)(2,1)} %weight_in.1, bf16[128,128]{1,0:T(8,128)(2,1)S(1)} %copy-done.3), custom_call_target="tpu_custom_call" | custom-call | bytes 1343488 | tf_op jit(solution)/shard_map/pallas_call | solution.py:338
  3.5 3.5 %collective-permute-start.3 = (bf16[128,640]{1,0:T(8,128)(2,1)S(1)}, bf16[128,640]{1,0:T(8,128)(2,1)S(1)}, u32[]{:S(2)}, u32[]{:S(2)}) collective-permute-start(bf16[128,640]{1,0:T(8,128)(2,1)S(1)} %copy-done), channel_id=1, source_target_pairs={{0,6},{1,7},{2,4},{3,5},{4,2},{5,3},{6,0},{7,1},{8,14},{9,15},{10,... | collective-permute-start | bytes 491528 | tf_op jit(solution)/shard_map/ppermute | solution.py:383
  7.7 3.1 %collective-permute-start.6 = (bf16[2,128,128]{2,1,0:T(8,128)(2,1)S(1)}, bf16[2,128,128]{2,1,0:T(8,128)(2,1)S(1)}, u32[]{:S(2)}, u32[]{:S(2)}) collective-permute-start(bf16[2,128,128]{2,1,0:T(8,128)(2,1)S(1)} %pad_maximum_fusion.packed.refs_0_), channel_id=1, source_target_pairs={{0,16},{8,24},{16,0},{24,8},{1,17},{9,25},{17,1},{25,9},{2,18},{10... | collective-permute-start | bytes 196616 | tf_op jit(solution)/shard_map/ppermute | solution.py:390
  10.8 1.6 %collective-permute-start.5 = (bf16[2,128,128]{2,1,0:T(8,128)(2,1)S(1)}, bf16[2,128,128]{2,1,0:T(8,128)(2,1)S(1)}, u32[]{:S(2)}, u32[]{:S(2)}) collective-permute-start(bf16[2,128,128]{2,1,0:T(8,128)(2,1)S(1)} %pad_maximum_fusion.packed.refs_0_), channel_id=1, source_target_pairs={{0,8},{8,0},{16,24},{24,16},{1,9},{9,1},{17,25},{25,17},{2,10},{10... | collective-permute-start | bytes 196616 | tf_op jit(solution)/shard_map/ppermute | solution.py:390
  12.4 0.6 %shard_map.129 = (f32[2,512]{1,0:T(2,128)S(1)}, f32[4,2,640]{2,1,0:T(2,128)S(1)}, f32[4,1,640]{2,1,0:T(1,128)S(1)}, f32[8,16,128]{2,1,0:T(8,128)S(1)}) custom-call(s32[8]{0:T(128)S(1)} %copy-done.4, s32[4]{0:T(128)S(1)} %copy-done.5, f32[16,5120]{1,0:T(8,128)S(1)} %copy-done.1), custom_call_target="tpu_custom_call" | custom-call | bytes 327728 | tf_op jit(solution)/shard_map/pallas_call | solution.py:338
  13.0 0.8 %collective-permute-done.6.refs_2_ = bf16[2,128,128]{2,1,0:T(8,128)(2,1)S(1)} collective-permute-done((bf16[2,128,128]{2,1,0:T(8,128)(2,1)S(1)}, bf16[2,128,128]{2,1,0:T(8,128)(2,1)S(1)}, u32[]{:S(2)}, u32[]{:S(2)}) %collective-permute-start.6) | collective-permute-done | bytes 65568 | tf_op jit(solution)/shard_map/ppermute | solution.py:390
  13.8 1.2 %collective-permute-start.7 = (bf16[2,128,128]{2,1,0:T(8,128)(2,1)S(1)}, bf16[2,128,128]{2,1,0:T(8,128)(2,1)S(1)}, u32[]{:S(2)}, u32[]{:S(2)}) collective-permute-start(bf16[2,128,128]{2,1,0:T(8,128)(2,1)S(1)} %collective-permute-done.6.refs_2_), channel_id=1, source_target_pairs={{0,8},{8,0},{16,24},{24,16},{1,9},{9,1},{17,25},{25,17},{2,10},{10... | collective-permute-start | bytes 196616 | tf_op jit(solution)/shard_map/ppermute | solution.py:390
  15.7 0.8 %shard_map.130 = (f32[128,128]{1,0:T(8,128)S(1)}, f32[128,128]{1,0:T(8,128)S(1)}, f32[40,128]{1,0:T(8,128)S(1)}) custom-call(bf16[2,128,128]{2,1,0:T(8,128)(2,1)S(1)} %pad_maximum_fusion.packed.refs_0_, bf16[4,128,640]{2,1,0:T(8,128)(2,1)S(1)} %get-tuple-element.42.kept, bf16[128,2688]{1,0:T(8,128)(2,1)S(1)} %collective-permute-done.received, ...), custom_call_target="tpu_custom_call" | custom-call | flops 335544320 | bytes 2084864 | tf_op jit(solution)/shard_map/pallas_call | solution.py:338
  16.5 1.5 %collective-permute-done.7.refs_3_ = bf16[2,128,128]{2,1,0:T(8,128)(2,1)S(1)} collective-permute-done((bf16[2,128,128]{2,1,0:T(8,128)(2,1)S(1)}, bf16[2,128,128]{2,1,0:T(8,128)(2,1)S(1)}, u32[]{:S(2)}, u32[]{:S(2)}) %collective-permute-start.7) | collective-permute-done | bytes 65568 | tf_op jit(solution)/shard_map/ppermute | solution.py:390
  18.1 0.8 %shard_map.131.stats = f32[8,128]{1,0:T(8,128)S(1)} custom-call(f32[2,512]{1,0:T(2,128)S(1)} %get-tuple-element.52.bias, bf16[1024,128]{1,0:T(8,128)(2,1)S(1)} %copy-done.2, bf16[2,128,128]{2,1,0:T(8,128)(2,1)S(1)} %pad_maximum_fusion.packed.refs_0_, bf16[2,128,128]{2,1,0:T(8,128)(2,1)S(1)} %collective-permute-done.5.refs_1_, ...), custom_call_target="tpu_custom_call" | custom-call | flops 134217728 | bytes 528384 | tf_op jit(solution)/shard_map/pallas_call | solution.py:338
  19.0 3.9 %collective-permute-start.8 = (bf16[352,128]{1,0:T(8,128)(2,1)S(1)}, bf16[352,128]{1,0:T(8,128)(2,1)S(1)}, u32[]{:S(2)}, u32[]{:S(2)}) collective-permute-start(bf16[352,128]{1,0:T(8,128)(2,1)S(1)} %get-tuple-element.48), channel_id=1, source_target_pairs={{0,24},{8,16},{16,8},{24,0},{1,25},{9,17},{17,9},{25,1},{2,26},{10... | collective-permute-start | bytes 270344 | tf_op jit(solution)/shard_map/ppermute | solution.py:390
  22.9 0.6 %collective-permute-start.10 = (bf16[352,128]{1,0:T(8,128)(2,1)S(1)}, bf16[352,128]{1,0:T(8,128)(2,1)S(1)}, u32[]{:S(2)}, u32[]{:S(2)}) collective-permute-start(bf16[352,128]{1,0:T(8,128)(2,1)S(1)} %get-tuple-element.50), channel_id=1, source_target_pairs={{0,8},{8,0},{16,24},{24,16},{1,9},{9,1},{17,25},{25,17},{2,10},{10... | collective-permute-start | bytes 270344 | tf_op jit(solution)/shard_map/ppermute | solution.py:390
  23.5 2.5 %collective-permute-done.8.refs_0_.refs_4_ = bf16[352,128]{1,0:T(8,128)(2,1)S(1)} collective-permute-done((bf16[352,128]{1,0:T(8,128)(2,1)S(1)}, bf16[352,128]{1,0:T(8,128)(2,1)S(1)}, u32[]{:S(2)}, u32[]{:S(2)}) %collective-permute-start.8) | collective-permute-done | bytes 90144 | tf_op jit(solution)/shard_map/ppermute | solution.py:390
  26.0 3.5 %collective-permute-done.9.refs_1_.refs_5_ = bf16[352,128]{1,0:T(8,128)(2,1)S(1)} collective-permute-done((bf16[352,128]{1,0:T(8,128)(2,1)S(1)}, bf16[352,128]{1,0:T(8,128)(2,1)S(1)}, u32[]{:S(2)}, u32[]{:S(2)}) %collective-permute-start.9) | collective-permute-done | bytes 90144 | tf_op jit(solution)/shard_map/ppermute | solution.py:390
  29.5 2.3 %collective-permute-start.16 = (bf16[800,128]{1,0:T(8,128)(2,1)S(1)}, bf16[800,128]{1,0:T(8,128)(2,1)S(1)}, u32[]{:S(2)}, u32[]{:S(2)}) collective-permute-start(bf16[800,128]{1,0:T(8,128)(2,1)S(1)} %shard_map.133.refs_0_), channel_id=1, source_target_pairs={{0,6},{1,7},{2,4},{3,5},{4,2},{5,3},{6,0},{7,1},{8,14},{9,15},{10,... | collective-permute-start | bytes 614408 | tf_op jit(solution)/shard_map/ppermute | solution.py:383
  31.8 0.7 %collective-permute-start.15 = (bf16[800,128]{1,0:T(8,128)(2,1)S(1)}, bf16[800,128]{1,0:T(8,128)(2,1)S(1)}, u32[]{:S(2)}, u32[]{:S(2)}) collective-permute-start(bf16[800,128]{1,0:T(8,128)(2,1)S(1)} %shard_map.133.refs_0_), channel_id=1, source_target_pairs={{0,4},{1,5},{2,6},{3,7},{4,0},{5,1},{6,2},{7,3},{8,12},{9,13},{10,... | collective-permute-start | bytes 614408 | tf_op jit(solution)/shard_map/ppermute | solution.py:383
  33.1 2.4 %shard_map.134 = (bf16[1024,128]{1,0:T(8,128)(2,1)}, bf16[1024,128]{1,0:T(8,128)(2,1)}, bf16[128,128]{1,0:T(8,128)(2,1)S(1)}, bf16[128,128]{1,0:T(8,128)(2,1)S(1...) custom-call(f32[2,512]{1,0:T(2,128)S(1)} %get-tuple-element.52.bias, bf16[1024,128]{1,0:T(8,128)(2,1)S(1)} %copy-done.2, ...), custom_call_target="tpu_custom_call" | custom-call | flops 671088640 | bytes 1150976 | tf_op jit(solution)/shard_map/pallas_call | solution.py:338
  35.5 2.6 %collective-permute-start.11 = (bf16[128,128]{1,0:T(8,128)(2,1)S(1)}, bf16[128,128]{1,0:T(8,128)(2,1)S(1)}, u32[]{:S(2)}, u32[]{:S(2)}) collective-permute-start(bf16[128,128]{1,0:T(8,128)(2,1)S(1)} %get-tuple-element.53), channel_id=1, source_target_pairs={{0,24},{8,16},{16,8},{24,0},{1,25},{9,17},{17,9},{25,1},{2,26},{10... | collective-permute-start | bytes 98312 | tf_op jit(solution)/shard_map/ppermute | solution.py:390
  38.1 3.1 %collective-permute-done.11.refs_0_ = bf16[128,128]{1,0:T(8,128)(2,1)S(1)} collective-permute-done((bf16[128,128]{1,0:T(8,128)(2,1)S(1)}, bf16[128,128]{1,0:T(8,128)(2,1)S(1)}, u32[]{:S(2)}, u32[]{:S(2)}) %collective-permute-start.11) | collective-permute-done | bytes 32800 | tf_op jit(solution)/shard_map/ppermute | solution.py:390
  41.2 1.7 %collective-permute-done.12.refs_1_ = bf16[128,128]{1,0:T(8,128)(2,1)S(1)} collective-permute-done((bf16[128,128]{1,0:T(8,128)(2,1)S(1)}, bf16[128,128]{1,0:T(8,128)(2,1)S(1)}, u32[]{:S(2)}, u32[]{:S(2)}) %collective-permute-start.12) | collective-permute-done | bytes 32800 | tf_op jit(solution)/shard_map/ppermute | solution.py:390
  43.6 1.7 %collective-permute-done.17.other = bf16[2880,128]{1,0:T(8,128)(2,1)S(1)} collective-permute-done((bf16[2880,128]{1,0:T(8,128)(2,1)S(1)}, bf16[2880,128]{1,0:T(8,128)(2,1)S(1)}, u32[]{:S(2)}, u32[]{:S(2)}) %collective-permute-start.17) | collective-permute-done | bytes 737312 | tf_op jit(solution)/shard_map/ppermute | solution.py:387
  45.3 1.3 %shard_map.137 = (f32[128,1280]{1,0:T(8,128)}, f32[16,5120]{1,0:T(8,128)}) custom-call(f32[8,16,128]{2,1,0:T(8,128)S(1)} %get-tuple-element.57.hot, bf16[2880,128]{1,0:T(8,128)(2,1)S(1)} %collective-permute-done.17.other, f32[128,640]{1,0:T(8,128)S(1)} %get-tuple-element.62.own_weight, f32[16,2560]{1,0:T(8,128)S(1)} %get-tuple-element.63.own_gate, ...), custom_call_target="tpu_custom_call" | custom-call | flops 83886080 | bytes 1556480 | tf_op jit(solution)/shard_map/pallas_call | solution.py:338
  47.1 0.7 %shard_map.138 = bf16[128,128]{1,0:T(8,128)(2,1)} custom-call(bf16[128,128]{1,0:T(8,128)(2,1)S(1)} %collective-permute-done.11.refs_0_, bf16[128,128]{1,0:T(8,128)(2,1)S(1)} %collective-permute-done.12.refs_1_, bf16[128,128]{1,0:T(8,128)(2,1)S(1)} %collective-permute-done.13.refs_2_, bf16[128,128]{1,0:T(8,128)(2,1)S(1)} %get-tuple-element.65.refs_3_), custom_call_target="tpu_custom_call" | custom-call | bytes 131072 | tf_op jit(solution)/shard_map/pallas_call | solution.py:338
  (40 shorter events, 3.8 us)
Async XLA Ops:
  0.6 11.7 %copy-start.1 = (f32[16,5120]{1,0:T(8,128)S(1)}, f32[16,5120]{1,0:T(8,128)}, u32[]{:S(2)}) copy-start(f32[16,5120]{1,0:T(8,128)} %gate) | copy-start | bytes 983044
  1.5 6.2 %copy-start.7 = (bf16[128,128]{1,0:T(8,128)(2,1)S(1)}, bf16[128,128]{1,0:T(8,128)(2,1)}, u32[]{:S(2)}) copy-start(bf16[128,128]{1,0:T(8,128)(2,1)} %param.9) | copy-start | bytes 98308
  1.5 10.9 %copy-start.4 = (s32[8]{0:T(128)S(1)}, s32[8]{0:T(128)}, u32[]{:S(2)}) copy-start(s32[8]{0:T(128)} %levels.1) | copy-start | bytes 100
  1.5 10.9 %copy-start.5 = (s32[4]{0:T(128)S(1)}, s32[4]{0:T(128)}, u32[]{:S(2)}) copy-start(s32[4]{0:T(128)} %clips.1) | copy-start | bytes 52
  3.0 15.1 %copy-start.2 = (bf16[1024,128]{1,0:T(8,128)(2,1)S(1)}, bf16[1024,128]{1,0:T(8,128)(2,1)}, u32[]{:S(2)}) copy-start(bf16[1024,128]{1,0:T(8,128)(2,1)} %keys.3) | copy-start | bytes 786436
  3.0 4.7 %collective-permute-start = (bf16[128,2688]{1,0:T(8,128)(2,1)S(1)}, bf16[128,2688]{1,0:T(8,128)(2,1)S(1)}, u32[]{:S(2)}, u32[]{:S(2)}) collective-permute-start(bf16[128,2688]{1,0:T(8,128)(2,1)S(1)} %get-tuple-element.37), channel_id=1, source_target_pairs={{0,1},{1,0},{2,3},{3,2},{4,5},{5,4},{6,7},{7,6},{8,9},{9,8},{10,11... | collective-permute-start | bytes 2064392 | tf_op jit(solution)/shard_map/ppermute | solution.py:387
  3.5 11.4 %collective-permute-start.3 = (bf16[128,640]{1,0:T(8,128)(2,1)S(1)}, bf16[128,640]{1,0:T(8,128)(2,1)S(1)}, u32[]{:S(2)}, u32[]{:S(2)}) collective-permute-start(bf16[128,640]{1,0:T(8,128)(2,1)S(1)} %copy-done), channel_id=1, source_target_pairs={{0,6},{1,7},{2,4},{3,5},{4,2},{5,3},{6,0},{7,1},{8,14},{9,15},{10,... | collective-permute-start | bytes 491528 | tf_op jit(solution)/shard_map/ppermute | solution.py:383
  7.1 8.3 %collective-permute-start.2 = (bf16[128,640]{1,0:T(8,128)(2,1)S(1)}, bf16[128,640]{1,0:T(8,128)(2,1)S(1)}, u32[]{:S(2)}, u32[]{:S(2)}) collective-permute-start(bf16[128,640]{1,0:T(8,128)(2,1)S(1)} %copy-done), channel_id=1, source_target_pairs={{0,4},{1,5},{2,6},{3,7},{4,0},{5,1},{6,2},{7,3},{8,12},{9,13},{10,... | collective-permute-start | bytes 491528 | tf_op jit(solution)/shard_map/ppermute | solution.py:383
  7.6 8.1 %collective-permute-start.1 = (bf16[128,640]{1,0:T(8,128)(2,1)S(1)}, bf16[128,640]{1,0:T(8,128)(2,1)S(1)}, u32[]{:S(2)}, u32[]{:S(2)}) collective-permute-start(bf16[128,640]{1,0:T(8,128)(2,1)S(1)} %copy-done), channel_id=1, source_target_pairs={{0,2},{1,3},{2,0},{3,1},{4,6},{5,7},{6,4},{7,5},{8,10},{9,11},{10,... | collective-permute-start | bytes 491528 | tf_op jit(solution)/shard_map/ppermute | solution.py:383
  7.7 6.1 %collective-permute-start.6 = (bf16[2,128,128]{2,1,0:T(8,128)(2,1)S(1)}, bf16[2,128,128]{2,1,0:T(8,128)(2,1)S(1)}, u32[]{:S(2)}, u32[]{:S(2)}) collective-permute-start(bf16[2,128,128]{2,1,0:T(8,128)(2,1)S(1)} %pad_maximum_fusion.packed.refs_0_), channel_id=1, source_target_pairs={{0,16},{8,24},{16,0},{24,8},{1,17},{9,25},{17,1},{25,9},{2,18},{10... | collective-permute-start | bytes 196616 | tf_op jit(solution)/shard_map/ppermute | solution.py:390
  10.8 5.7 %collective-permute-start.5 = (bf16[2,128,128]{2,1,0:T(8,128)(2,1)S(1)}, bf16[2,128,128]{2,1,0:T(8,128)(2,1)S(1)}, u32[]{:S(2)}, u32[]{:S(2)}) collective-permute-start(bf16[2,128,128]{2,1,0:T(8,128)(2,1)S(1)} %pad_maximum_fusion.packed.refs_0_), channel_id=1, source_target_pairs={{0,8},{8,0},{16,24},{24,16},{1,9},{9,1},{17,25},{25,17},{2,10},{10... | collective-permute-start | bytes 196616 | tf_op jit(solution)/shard_map/ppermute | solution.py:390
  13.8 4.3 %collective-permute-start.7 = (bf16[2,128,128]{2,1,0:T(8,128)(2,1)S(1)}, bf16[2,128,128]{2,1,0:T(8,128)(2,1)S(1)}, u32[]{:S(2)}, u32[]{:S(2)}) collective-permute-start(bf16[2,128,128]{2,1,0:T(8,128)(2,1)S(1)} %collective-permute-done.6.refs_2_), channel_id=1, source_target_pairs={{0,8},{8,0},{16,24},{24,16},{1,9},{9,1},{17,25},{25,17},{2,10},{10... | collective-permute-start | bytes 196616 | tf_op jit(solution)/shard_map/ppermute | solution.py:390
  16.4 16.6 %copy-start.6 = (bf16[1024,128]{1,0:T(8,128)(2,1)S(1)}, bf16[1024,128]{1,0:T(8,128)(2,1)}, u32[]{:S(2)}) copy-start(bf16[1024,128]{1,0:T(8,128)(2,1)} %values.1) | copy-start | bytes 786436
  16.4 2.4 %collective-permute-start.4 = (f32[128,128]{1,0:T(8,128)S(1)}, f32[128,128]{1,0:T(8,128)S(1)}, u32[]{:S(2)}, u32[]{:S(2)}) collective-permute-start(f32[128,128]{1,0:T(8,128)S(1)} %get-tuple-element.45), channel_id=1, source_target_pairs={{0,1},{1,0},{2,3},{3,2},{4,5},{5,4},{6,7},{7,6},{8,9},{9,8},{10,11... | collective-permute-start | bytes 196616 | tf_op jit(solution)/shard_map/ppermute | solution.py:387
  19.0 7.0 %collective-permute-start.8 = (bf16[352,128]{1,0:T(8,128)(2,1)S(1)}, bf16[352,128]{1,0:T(8,128)(2,1)S(1)}, u32[]{:S(2)}, u32[]{:S(2)}) collective-permute-start(bf16[352,128]{1,0:T(8,128)(2,1)S(1)} %get-tuple-element.48), channel_id=1, source_target_pairs={{0,24},{8,16},{16,8},{24,0},{1,25},{9,17},{17,9},{25,1},{2,26},{10... | collective-permute-start | bytes 270344 | tf_op jit(solution)/shard_map/ppermute | solution.py:390
  22.9 6.6 %collective-permute-start.9 = (bf16[352,128]{1,0:T(8,128)(2,1)S(1)}, bf16[352,128]{1,0:T(8,128)(2,1)S(1)}, u32[]{:S(2)}, u32[]{:S(2)}) collective-permute-start(bf16[352,128]{1,0:T(8,128)(2,1)S(1)} %get-tuple-element.49), channel_id=1, source_target_pairs={{0,16},{8,24},{16,0},{24,8},{1,17},{9,25},{17,1},{25,9},{2,18},{10... | collective-permute-start | bytes 270344 | tf_op jit(solution)/shard_map/ppermute | solution.py:390
  22.9 6.6 %collective-permute-start.10 = (bf16[352,128]{1,0:T(8,128)(2,1)S(1)}, bf16[352,128]{1,0:T(8,128)(2,1)S(1)}, u32[]{:S(2)}, u32[]{:S(2)}) collective-permute-start(bf16[352,128]{1,0:T(8,128)(2,1)S(1)} %get-tuple-element.50), channel_id=1, source_target_pairs={{0,8},{8,0},{16,24},{24,16},{1,9},{9,1},{17,25},{25,17},{2,10},{10... | collective-permute-start | bytes 270344 | tf_op jit(solution)/shard_map/ppermute | solution.py:390
  29.5 13.4 %collective-permute-start.16 = (bf16[800,128]{1,0:T(8,128)(2,1)S(1)}, bf16[800,128]{1,0:T(8,128)(2,1)S(1)}, u32[]{:S(2)}, u32[]{:S(2)}) collective-permute-start(bf16[800,128]{1,0:T(8,128)(2,1)S(1)} %shard_map.133.refs_0_), channel_id=1, source_target_pairs={{0,6},{1,7},{2,4},{3,5},{4,2},{5,3},{6,0},{7,1},{8,14},{9,15},{10,... | collective-permute-start | bytes 614408 | tf_op jit(solution)/shard_map/ppermute | solution.py:383
  31.8 11.1 %collective-permute-start.15 = (bf16[800,128]{1,0:T(8,128)(2,1)S(1)}, bf16[800,128]{1,0:T(8,128)(2,1)S(1)}, u32[]{:S(2)}, u32[]{:S(2)}) collective-permute-start(bf16[800,128]{1,0:T(8,128)(2,1)S(1)} %shard_map.133.refs_0_), channel_id=1, source_target_pairs={{0,4},{1,5},{2,6},{3,7},{4,0},{5,1},{6,2},{7,3},{8,12},{9,13},{10,... | collective-permute-start | bytes 614408 | tf_op jit(solution)/shard_map/ppermute | solution.py:383
  32.5 10.4 %collective-permute-start.14 = (bf16[800,128]{1,0:T(8,128)(2,1)S(1)}, bf16[800,128]{1,0:T(8,128)(2,1)S(1)}, u32[]{:S(2)}, u32[]{:S(2)}) collective-permute-start(bf16[800,128]{1,0:T(8,128)(2,1)S(1)} %shard_map.133.refs_0_), channel_id=1, source_target_pairs={{0,2},{1,3},{2,0},{3,1},{4,6},{5,7},{6,4},{7,5},{8,10},{9,11},{10,... | collective-permute-start | bytes 614408 | tf_op jit(solution)/shard_map/ppermute | solution.py:383
  35.5 5.7 %collective-permute-start.11 = (bf16[128,128]{1,0:T(8,128)(2,1)S(1)}, bf16[128,128]{1,0:T(8,128)(2,1)S(1)}, u32[]{:S(2)}, u32[]{:S(2)}) collective-permute-start(bf16[128,128]{1,0:T(8,128)(2,1)S(1)} %get-tuple-element.53), channel_id=1, source_target_pairs={{0,24},{8,16},{16,8},{24,0},{1,25},{9,17},{17,9},{25,1},{2,26},{10... | collective-permute-start | bytes 98312 | tf_op jit(solution)/shard_map/ppermute | solution.py:390
  38.1 4.8 %collective-permute-start.12 = (bf16[128,128]{1,0:T(8,128)(2,1)S(1)}, bf16[128,128]{1,0:T(8,128)(2,1)S(1)}, u32[]{:S(2)}, u32[]{:S(2)}) collective-permute-start(bf16[128,128]{1,0:T(8,128)(2,1)S(1)} %get-tuple-element.54), channel_id=1, source_target_pairs={{0,16},{8,24},{16,0},{24,8},{1,17},{9,25},{17,1},{25,9},{2,18},{10... | collective-permute-start | bytes 98312 | tf_op jit(solution)/shard_map/ppermute | solution.py:390
  43.0 2.3 %collective-permute-start.17 = (bf16[2880,128]{1,0:T(8,128)(2,1)S(1)}, bf16[2880,128]{1,0:T(8,128)(2,1)S(1)}, u32[]{:S(2)}, u32[]{:S(2)}) collective-permute-start(bf16[2880,128]{1,0:T(8,128)(2,1)S(1)} %shard_map.135.own), channel_id=1, source_target_pairs={{0,1},{1,0},{2,3},{3,2},{4,5},{5,4},{6,7},{7,6},{8,9},{9,8},{10,11... | collective-permute-start | bytes 2211848 | tf_op jit(solution)/shard_map/ppermute | solution.py:387
  43.1 4.0 %collective-permute-start.13 = (bf16[128,128]{1,0:T(8,128)(2,1)S(1)}, bf16[128,128]{1,0:T(8,128)(2,1)S(1)}, u32[]{:S(2)}, u32[]{:S(2)}) collective-permute-start(bf16[128,128]{1,0:T(8,128)(2,1)S(1)} %get-tuple-element.55), channel_id=1, source_target_pairs={{0,8},{8,0},{16,24},{24,16},{1,9},{9,1},{17,25},{25,17},{2,10},{10... | collective-permute-start | bytes 98312 | tf_op jit(solution)/shard_map/ppermute | solution.py:390
  (2 other events, 3.7 us)

commit v12 on v11

--- a/solution.py
+++ b/solution.py
@@ -200,11 +200,14 @@
     out[chips * base + count :, :] = (total - high.astype(jnp.float32)).astype(jnp.bfloat16)
 
 
-def grads_kernel(n_t, starts, bias, keys, values, *refs):
+def grads_kernel(n_t, starts, first, last, bias, keys, values, *refs):
     packed, heads = refs[:n_t], refs[n_t : 2 * n_t][::-1]
-    key_out, value_out = refs[2 * n_t : 2 * n_t + 2]
-    outs = refs[2 * n_t + 2 : 3 * n_t + 2][::-1]
-    key_acc, value_acc = refs[3 * n_t + 2 :]
+    refs = refs[2 * n_t :]
+    if first == 0:
+        sums, refs = refs[:2], refs[2:]
+    key_out, value_out = refs[:2]
+    outs = refs[2 : 2 + last - first][::-1]
+    accs = refs[2 + last - first :]
     rows = packed[0].shape[1]
     ones = jnp.ones((8, HD), jnp.float32)
     keys_t = jnp.transpose(keys[...])
@@ -212,7 +215,7 @@
     for k in range(n_t):
         parts = heads[k][starts[2] :, :].astype(jnp.float32)
         stats.append(sum(parts[i * 2 * n_t : (i + 1) * 2 * n_t] for i in range(SPLIT)))
-    for p in range(0, n_t, 2):
+    for p in range(first, last, 2):
         q = jnp.concatenate([packed[p][0], packed[p + 1][0]], axis=0)
         o = jnp.concatenate([packed[p][1], packed[p + 1][1]], axis=0)
         g = jnp.concatenate([heads[p][:rows, :], heads[p + 1][:rows, :]], axis=0)
@@ -226,9 +229,9 @@
         lse = []
         for i in (p, p + 1):
             tops = [stats[k][i ^ k : (i ^ k) + 1] for k in range(n_t)]
-            sums = [stats[k][n_t + (i ^ k) : n_t + (i ^ k) + 1] for k in range(n_t)]
+            sums_of = [stats[k][n_t + (i ^ k) : n_t + (i ^ k) + 1] for k in range(n_t)]
             top = functools.reduce(jnp.maximum, tops)
-            lse.append(top + jnp.log(sum(b * jnp.exp(a - top) for a, b in zip(tops, sums))))
+            lse.append(top + jnp.log(sum(b * jnp.exp(a - top) for a, b in zip(tops, sums_of))))
         lse = jnp.concatenate(lse, axis=1)
         query_part = None
         for kf in range(bias.shape[0]):
@@ -238,19 +241,22 @@
             score_grad = (probs * (dot(values[span, :], g, 1, 1) - delta)).astype(jnp.bfloat16)
             value_add = dot(probs.astype(jnp.bfloat16), g, 1, 0)
             key_add = dot(score_grad, q, 1, 0)
-            if p > 0:
-                value_add = value_add + value_acc[span, :]
-                key_add = key_add + key_acc[span, :]
-            if p + 2 < n_t:
-                value_acc[span, :] = value_add
-                key_acc[span, :] = key_add
+            if p > first:
+                value_add = value_add + accs[1][span, :]
+                key_add = key_add + accs[0][span, :]
+            if p + 2 < last:
+                accs[1][span, :] = value_add
+                accs[0][span, :] = key_add
+            elif first:
+                value_out[span, :] = value_add
+                key_out[span, :] = key_add
             else:
-                value_out[span, :] = value_add.astype(jnp.bfloat16)
-                key_out[span, :] = (key_add * SCALE).astype(jnp.bfloat16)
+                value_out[span, :] = (value_add + sums[1][span, :]).astype(jnp.bfloat16)
+                key_out[span, :] = ((key_add + sums[0][span, :]) * SCALE).astype(jnp.bfloat16)
             part = dot(keys_t[:, span], score_grad, 1, 0)
             query_part = part if query_part is None else query_part + part
-        outs[p][...] = query_part[:, :rows].astype(jnp.bfloat16)
-        outs[p + 1][...] = query_part[:, rows:].astype(jnp.bfloat16)
+        outs[p - first][...] = query_part[:, :rows].astype(jnp.bfloat16)
+        outs[p + 1 - first][...] = query_part[:, rows:].astype(jnp.bfloat16)
 
 
 def query_kernel(n_t, *refs):
@@ -452,16 +458,26 @@
     )
     bundles = over_chips(bundle)
     later_bias, _ = lax.optimization_barrier((bias, bundle))
-    outs = call(
-        functools.partial(grads_kernel, n_t, starts),
+    accs = [pltpu.VMEM((k_rows, HD), f32)] * 2
+    far = call(
+        functools.partial(grads_kernel, n_t, starts, 2, n_t),
         [later_bias, keys, values] + packed_all + heads_all[::-1],
-        [shape(bf16, k_rows, HD)] * 2 + [shape(bf16, HD, rows)] * n_t,
-        [pltpu.VMEM((k_rows, HD), f32)] * 2,
-        flops=10 * n_t * rows * k_rows * HD,
-    )
-    key_grad, value_grad = outs[:2]
-    parts = time_swaps(outs[2:][::-1])
-    bundles, _ = lax.optimization_barrier((bundles, parts[: n_t // 2 - 1 : -1]))
+        [shape(f32, k_rows, HD)] * 2 + [shape(bf16, HD, rows)] * (n_t - 2),
+        accs,
+        flops=10 * (n_t - 2) * rows * k_rows * HD,
+    )
+    parts = {k: over_time(far[1 + n_t - k], k) for k in range(n_t - 1, 1, -1)}
+    near_bias, _ = lax.optimization_barrier((bias, parts[n_t - 1]))
+    near = call(
+        functools.partial(grads_kernel, n_t, starts, 0, 2),
+        [near_bias, keys, values] + packed_all + heads_all[::-1] + list(far[:2]),
+        [shape(bf16, k_rows, HD)] * 2 + [shape(bf16, HD, rows)] * 2,
+        flops=20 * rows * k_rows * HD,
+    )
+    key_grad, value_grad = near[:2]
+    parts[0], parts[1] = near[3], over_time(near[2], 1)
+    parts = [parts[k] for k in range(n_t)]
+    bundles, _ = lax.optimization_barrier((bundles, (key_grad, parts[: n_t // 2 - 1 : -1])))
     collected = call(
         functools.partial(collect_kernel, chips, base),
         bundles,

time: 48 us -> 48 us (level)
    pallas_call x11 -> x12, Pallas kernels: 8.78 us -> 8.99 us  [call(): pl.pallas_call(kernel, out_shape=out_shape, in_specs=[pl.BlockSpec(memory...]
  transfers between devices with their start and end apart: 18 -> 18, of which waited for: 10 -> 10; matrix products, arithmetic and copies ran while one was open for 0% -> 0% of each run, Pallas kernels for 13% -> 14%
where the time goes in v12:
time: 48 us; the launch traced here: 47.8 us
  starting transfers between devices  21.4 us (45%)
  waiting for transfers between devices  15.8 us (33%)
  Pallas kernels  8.99 us (19%)
  local copies, waits for them, and re-layouts  0.84 us (2%)
  between operations  0.79 us (2%)
    ppermute x9, waiting for transfers between devices, over_time(): return lax.ppermute(x, 'tm', [(t, t ^ k) for t in range(n_t)])  13.2 us
    ppermute x9, starting transfers between devices, over_time(): return lax.ppermute(x, 'tm', [(t, t ^ k) for t in range(n_t)])  13.1 us
    pallas_call x12, Pallas kernels, call(): pl.pallas_call(kernel, out_shape=out_shape, in_specs=[pl.BlockSpec(memory...  8.99 us
    ppermute x6, starting transfers between devices, over_chips(): lax.ppermute(x, 'space', [(s, s ^ 2 * k) for s in range(n_s)])  7.67 us
    ppermute x3, waiting for transfers between devices, over_cores(): return lax.ppermute(x, 'space', [(s, s ^ 1) for s in range(n_s)])  1.73 us
  transfers between devices with their start and end apart: 18, of which 10 were waited for; matrix products, arithmetic and copies ran while one was open for 0% of the time, Pallas kernels for 14%

profile of v12, /device:TPU:0, one launch (start us, length us, event | category | flops | bytes accessed | tf_op | source)
XLA Modules:
  0.0 47.8 jit_solution(15399528729147708189)
XLA Ops:
  0.7 0.8 %copy-done.4 = bf16[128,128]{1,0:T(8,128)(2,1)S(1)} copy-done((bf16[128,128]{1,0:T(8,128)(2,1)S(1)}, bf16[128,128]{1,0:T(8,128)(2,1)}, u32[]{:S(2)}) %copy-start.4) | copy-done | bytes 32792
  1.5 1.5 %shard_map.128 = (bf16[4,128,640]{2,1,0:T(8,128)(2,1)S(1)}, bf16[128,2688]{1,0:T(8,128)(2,1)S(1)}) custom-call(bf16[128,5120]{1,0:T(8,128)(2,1)} %weight_in.1, bf16[128,128]{1,0:T(8,128)(2,1)S(1)} %copy-done.4), custom_call_target="tpu_custom_call" | custom-call | bytes 1343488 | tf_op jit(solution)/shard_map/pallas_call | solution.py:344
  3.5 2.6 %collective-permute-start.1 = (bf16[128,640]{1,0:T(8,128)(2,1)S(1)}, bf16[128,640]{1,0:T(8,128)(2,1)S(1)}, u32[]{:S(2)}, u32[]{:S(2)}) collective-permute-start(bf16[128,640]{1,0:T(8,128)(2,1)S(1)} %copy-done.1), channel_id=1, source_target_pairs={{0,2},{1,3},{2,0},{3,1},{4,6},{5,7},{6,4},{7,5},{8,10},{9,11},{10,... | collective-permute-start | bytes 491528 | tf_op jit(solution)/shard_map/ppermute | solution.py:389
  6.1 1.5 %collective-permute-start.2 = (bf16[128,640]{1,0:T(8,128)(2,1)S(1)}, bf16[128,640]{1,0:T(8,128)(2,1)S(1)}, u32[]{:S(2)}, u32[]{:S(2)}) collective-permute-start(bf16[128,640]{1,0:T(8,128)(2,1)S(1)} %copy-done.1), channel_id=1, source_target_pairs={{0,4},{1,5},{2,6},{3,7},{4,0},{5,1},{6,2},{7,3},{8,12},{9,13},{10,... | collective-permute-start | bytes 491528 | tf_op jit(solution)/shard_map/ppermute | solution.py:389
  7.7 3.1 %collective-permute-start.6 = (bf16[2,128,128]{2,1,0:T(8,128)(2,1)S(1)}, bf16[2,128,128]{2,1,0:T(8,128)(2,1)S(1)}, u32[]{:S(2)}, u32[]{:S(2)}) collective-permute-start(bf16[2,128,128]{2,1,0:T(8,128)(2,1)S(1)} %pad_maximum_fusion.packed.refs_0_), channel_id=1, source_target_pairs={{0,16},{8,24},{16,0},{24,8},{1,17},{9,25},{17,1},{25,9},{2,18},{10... | collective-permute-start | bytes 196616 | tf_op jit(solution)/shard_map/ppermute | solution.py:396
  10.8 1.6 %collective-permute-start.5 = (bf16[2,128,128]{2,1,0:T(8,128)(2,1)S(1)}, bf16[2,128,128]{2,1,0:T(8,128)(2,1)S(1)}, u32[]{:S(2)}, u32[]{:S(2)}) collective-permute-start(bf16[2,128,128]{2,1,0:T(8,128)(2,1)S(1)} %pad_maximum_fusion.packed.refs_0_), channel_id=1, source_target_pairs={{0,8},{8,0},{16,24},{24,16},{1,9},{9,1},{17,25},{25,17},{2,10},{10... | collective-permute-start | bytes 196616 | tf_op jit(solution)/shard_map/ppermute | solution.py:396
  13.0 0.8 %collective-permute-done.6.refs_2_ = bf16[2,128,128]{2,1,0:T(8,128)(2,1)S(1)} collective-permute-done((bf16[2,128,128]{2,1,0:T(8,128)(2,1)S(1)}, bf16[2,128,128]{2,1,0:T(8,128)(2,1)S(1)}, u32[]{:S(2)}, u32[]{:S(2)}) %collective-permute-start.6) | collective-permute-done | bytes 65568 | tf_op jit(solution)/shard_map/ppermute | solution.py:396
  13.8 1.2 %collective-permute-start.7 = (bf16[2,128,128]{2,1,0:T(8,128)(2,1)S(1)}, bf16[2,128,128]{2,1,0:T(8,128)(2,1)S(1)}, u32[]{:S(2)}, u32[]{:S(2)}) collective-permute-start(bf16[2,128,128]{2,1,0:T(8,128)(2,1)S(1)} %collective-permute-done.6.refs_2_), channel_id=1, source_target_pairs={{0,8},{8,0},{16,24},{24,16},{1,9},{9,1},{17,25},{25,17},{2,10},{10... | collective-permute-start | bytes 196616 | tf_op jit(solution)/shard_map/ppermute | solution.py:396
  15.0 0.9 %collective-permute-done.2.refs_2_ = bf16[128,640]{1,0:T(8,128)(2,1)S(1)} collective-permute-done((bf16[128,640]{1,0:T(8,128)(2,1)S(1)}, bf16[128,640]{1,0:T(8,128)(2,1)S(1)}, u32[]{:S(2)}, u32[]{:S(2)}) %collective-permute-start.2) | collective-permute-done | bytes 163872 | tf_op jit(solution)/shard_map/ppermute | solution.py:389
  15.9 0.8 %shard_map.130 = (f32[128,128]{1,0:T(8,128)S(1)}, f32[128,128]{1,0:T(8,128)S(1)}, f32[40,128]{1,0:T(8,128)S(1)}) custom-call(bf16[2,128,128]{2,1,0:T(8,128)(2,1)S(1)} %pad_maximum_fusion.packed.refs_0_, bf16[4,128,640]{2,1,0:T(8,128)(2,1)S(1)} %get-tuple-element.45.kept, bf16[128,2688]{1,0:T(8,128)(2,1)S(1)} %collective-permute-done.received, ...), custom_call_target="tpu_custom_call" | custom-call | flops 335544320 | bytes 2084864 | tf_op jit(solution)/shard_map/pallas_call | solution.py:344
  16.7 1.3 %collective-permute-done.7.refs_3_ = bf16[2,128,128]{2,1,0:T(8,128)(2,1)S(1)} collective-permute-done((bf16[2,128,128]{2,1,0:T(8,128)(2,1)S(1)}, bf16[2,128,128]{2,1,0:T(8,128)(2,1)S(1)}, u32[]{:S(2)}, u32[]{:S(2)}) %collective-permute-start.7) | collective-permute-done | bytes 65568 | tf_op jit(solution)/shard_map/ppermute | solution.py:396
  19.0 1.2 %collective-permute-start.10 = (bf16[352,128]{1,0:T(8,128)(2,1)S(1)}, bf16[352,128]{1,0:T(8,128)(2,1)S(1)}, u32[]{:S(2)}, u32[]{:S(2)}) collective-permute-start(bf16[352,128]{1,0:T(8,128)(2,1)S(1)} %get-tuple-element.53), channel_id=1, source_target_pairs={{0,8},{8,0},{16,24},{24,16},{1,9},{9,1},{17,25},{25,17},{2,10},{10... | collective-permute-start | bytes 270344 | tf_op jit(solution)/shard_map/ppermute | solution.py:396
  20.2 3.2 %collective-permute-start.8 = (bf16[352,128]{1,0:T(8,128)(2,1)S(1)}, bf16[352,128]{1,0:T(8,128)(2,1)S(1)}, u32[]{:S(2)}, u32[]{:S(2)}) collective-permute-start(bf16[352,128]{1,0:T(8,128)(2,1)S(1)} %get-tuple-element.51), channel_id=1, source_target_pairs={{0,24},{8,16},{16,8},{24,0},{1,25},{9,17},{17,9},{25,1},{2,26},{10... | collective-permute-start | bytes 270344 | tf_op jit(solution)/shard_map/ppermute | solution.py:396
  23.6 4.3 %collective-permute-done.8.refs_0_.refs_4_ = bf16[352,128]{1,0:T(8,128)(2,1)S(1)} collective-permute-done((bf16[352,128]{1,0:T(8,128)(2,1)S(1)}, bf16[352,128]{1,0:T(8,128)(2,1)S(1)}, u32[]{:S(2)}, u32[]{:S(2)}) %collective-permute-start.8) | collective-permute-done | bytes 90144 | tf_op jit(solution)/shard_map/ppermute | solution.py:396
  27.9 2.9 %collective-permute-done.9.refs_1_.refs_5_ = bf16[352,128]{1,0:T(8,128)(2,1)S(1)} collective-permute-done((bf16[352,128]{1,0:T(8,128)(2,1)S(1)}, bf16[352,128]{1,0:T(8,128)(2,1)S(1)}, u32[]{:S(2)}, u32[]{:S(2)}) %collective-permute-start.9) | collective-permute-done | bytes 90144 | tf_op jit(solution)/shard_map/ppermute | solution.py:396
  30.9 1.5 %collective-permute-start.14 = (bf16[800,128]{1,0:T(8,128)(2,1)S(1)}, bf16[800,128]{1,0:T(8,128)(2,1)S(1)}, u32[]{:S(2)}, u32[]{:S(2)}) collective-permute-start(bf16[800,128]{1,0:T(8,128)(2,1)S(1)} %shard_map.133.refs_0_), channel_id=1, source_target_pairs={{0,2},{1,3},{2,0},{3,1},{4,6},{5,7},{6,4},{7,5},{8,10},{9,11},{10,... | collective-permute-start | bytes 614408 | tf_op jit(solution)/shard_map/ppermute | solution.py:389
  32.4 1.2 %collective-permute-start.15 = (bf16[800,128]{1,0:T(8,128)(2,1)S(1)}, bf16[800,128]{1,0:T(8,128)(2,1)S(1)}, u32[]{:S(2)}, u32[]{:S(2)}) collective-permute-start(bf16[800,128]{1,0:T(8,128)(2,1)S(1)} %shard_map.133.refs_0_), channel_id=1, source_target_pairs={{0,4},{1,5},{2,6},{3,7},{4,0},{5,1},{6,2},{7,3},{8,12},{9,13},{10,... | collective-permute-start | bytes 614408 | tf_op jit(solution)/shard_map/ppermute | solution.py:389
  33.5 0.9 %collective-permute-start.16 = (bf16[800,128]{1,0:T(8,128)(2,1)S(1)}, bf16[800,128]{1,0:T(8,128)(2,1)S(1)}, u32[]{:S(2)}, u32[]{:S(2)}) collective-permute-start(bf16[800,128]{1,0:T(8,128)(2,1)S(1)} %shard_map.133.refs_0_), channel_id=1, source_target_pairs={{0,6},{1,7},{2,4},{3,5},{4,2},{5,3},{6,0},{7,1},{8,14},{9,15},{10,... | collective-permute-start | bytes 614408 | tf_op jit(solution)/shard_map/ppermute | solution.py:389
  34.4 1.0 %shard_map.134 = (f32[1024,128]{1,0:T(8,128)S(1)}, f32[1024,128]{1,0:T(8,128)S(1)}, bf16[128,128]{1,0:T(8,128)(2,1)S(1)}, bf16[128,128]{1,0:T(8,128)(2,1)S(1)}) custom-call(f32[2,512]{1,0:T(2,128)S(1)} %get-tuple-element.58.bias, bf16[1024,128]{1,0:T(8,128)(2,1)S(1)} %copy-done, bf16[1024,128]{1,0:T(8,128)(2,1)S(1)} %copy-done.3, ...), custom_call_target="tpu_custom_call" | custom-call | flops 335544320 | bytes 1150976 | tf_op jit(solution)/shard_map/pallas_call | solution.py:344
  35.4 2.7 %collective-permute-start.11 = (bf16[128,128]{1,0:T(8,128)(2,1)S(1)}, bf16[128,128]{1,0:T(8,128)(2,1)S(1)}, u32[]{:S(2)}, u32[]{:S(2)}) collective-permute-start(bf16[128,128]{1,0:T(8,128)(2,1)S(1)} %get-tuple-element.56), channel_id=1, source_target_pairs={{0,24},{8,16},{16,8},{24,0},{1,25},{9,17},{17,9},{25,1},{2,26},{10... | collective-permute-start | bytes 98312 | tf_op jit(solution)/shard_map/ppermute | solution.py:396
  38.1 3.1 %collective-permute-done.11.refs_0_ = bf16[128,128]{1,0:T(8,128)(2,1)S(1)} collective-permute-done((bf16[128,128]{1,0:T(8,128)(2,1)S(1)}, bf16[128,128]{1,0:T(8,128)(2,1)S(1)}, u32[]{:S(2)}, u32[]{:S(2)}) %collective-permute-start.11) | collective-permute-done | bytes 32800 | tf_op jit(solution)/shard_map/ppermute | solution.py:396
  41.2 1.7 %shard_map.135 = (bf16[1024,128]{1,0:T(8,128)(2,1)}, bf16[1024,128]{1,0:T(8,128)(2,1)}, bf16[128,128]{1,0:T(8,128)(2,1)S(1)}, bf16[128,128]{1,0:T(8,128)(2,1)S(1)}) custom-call(f32[2,512]{1,0:T(2,128)S(1)} %get-tuple-element.58.bias, bf16[1024,128]{1,0:T(8,128)(2,1)S(1)} %copy-done, bf16[1024,128]{1,0:T(8,128)(2,1)S(1)} %copy-done.3, ...), custom_call_target="tpu_custom_call" | custom-call | flops 335544320 | bytes 2199552 | tf_op jit(solution)/shard_map/pallas_call | solution.py:344
  43.6 1.7 %collective-permute-done.17.other = bf16[2880,128]{1,0:T(8,128)(2,1)S(1)} collective-permute-done((bf16[2880,128]{1,0:T(8,128)(2,1)S(1)}, bf16[2880,128]{1,0:T(8,128)(2,1)S(1)}, u32[]{:S(2)}, u32[]{:S(2)}) %collective-permute-start.17) | collective-permute-done | bytes 737312 | tf_op jit(solution)/shard_map/ppermute | solution.py:393
  45.3 1.3 %shard_map.138 = (f32[128,1280]{1,0:T(8,128)}, f32[16,5120]{1,0:T(8,128)}) custom-call(f32[8,16,128]{2,1,0:T(8,128)S(1)} %get-tuple-element.63.hot, bf16[2880,128]{1,0:T(8,128)(2,1)S(1)} %collective-permute-done.17.other, f32[128,640]{1,0:T(8,128)S(1)} %get-tuple-element.69.own_weight, f32[16,2560]{1,0:T(8,128)S(1)} %get-tuple-element.70.own_gate, ...), custom_call_target="tpu_custom_call" | custom-call | flops 83886080 | bytes 1556480 | tf_op jit(solution)/shard_map/pallas_call | solution.py:344
  (41 shorter events, 4.4 us)
Async XLA Ops:
  0.6 11.7 %copy-start.2 = (f32[16,5120]{1,0:T(8,128)S(1)}, f32[16,5120]{1,0:T(8,128)}, u32[]{:S(2)}) copy-start(f32[16,5120]{1,0:T(8,128)} %gate) | copy-start | bytes 983044
  1.5 6.2 %copy-start.7 = (bf16[128,128]{1,0:T(8,128)(2,1)S(1)}, bf16[128,128]{1,0:T(8,128)(2,1)}, u32[]{:S(2)}) copy-start(bf16[128,128]{1,0:T(8,128)(2,1)} %param.9) | copy-start | bytes 98308
  1.5 10.9 %copy-start.5 = (s32[8]{0:T(128)S(1)}, s32[8]{0:T(128)}, u32[]{:S(2)}) copy-start(s32[8]{0:T(128)} %levels.1) | copy-start | bytes 100
  1.5 10.9 %copy-start.6 = (s32[4]{0:T(128)S(1)}, s32[4]{0:T(128)}, u32[]{:S(2)}) copy-start(s32[4]{0:T(128)} %clips.1) | copy-start | bytes 52
  3.0 15.1 %copy-start = (bf16[1024,128]{1,0:T(8,128)(2,1)S(1)}, bf16[1024,128]{1,0:T(8,128)(2,1)}, u32[]{:S(2)}) copy-start(bf16[1024,128]{1,0:T(8,128)(2,1)} %keys.5) | copy-start | bytes 786436
  3.0 4.7 %collective-permute-start = (bf16[128,2688]{1,0:T(8,128)(2,1)S(1)}, bf16[128,2688]{1,0:T(8,128)(2,1)S(1)}, u32[]{:S(2)}, u32[]{:S(2)}) collective-permute-start(bf16[128,2688]{1,0:T(8,128)(2,1)S(1)} %get-tuple-element.40), channel_id=1, source_target_pairs={{0,1},{1,0},{2,3},{3,2},{4,5},{5,4},{6,7},{7,6},{8,9},{9,8},{10,11... | collective-permute-start | bytes 2064392 | tf_op jit(solution)/shard_map/ppermute | solution.py:393
  3.5 11.4 %collective-permute-start.1 = (bf16[128,640]{1,0:T(8,128)(2,1)S(1)}, bf16[128,640]{1,0:T(8,128)(2,1)S(1)}, u32[]{:S(2)}, u32[]{:S(2)}) collective-permute-start(bf16[128,640]{1,0:T(8,128)(2,1)S(1)} %copy-done.1), channel_id=1, source_target_pairs={{0,2},{1,3},{2,0},{3,1},{4,6},{5,7},{6,4},{7,5},{8,10},{9,11},{10,... | collective-permute-start | bytes 491528 | tf_op jit(solution)/shard_map/ppermute | solution.py:389
  6.1 9.8 %collective-permute-start.2 = (bf16[128,640]{1,0:T(8,128)(2,1)S(1)}, bf16[128,640]{1,0:T(8,128)(2,1)S(1)}, u32[]{:S(2)}, u32[]{:S(2)}) collective-permute-start(bf16[128,640]{1,0:T(8,128)(2,1)S(1)} %copy-done.1), channel_id=1, source_target_pairs={{0,4},{1,5},{2,6},{3,7},{4,0},{5,1},{6,2},{7,3},{8,12},{9,13},{10,... | collective-permute-start | bytes 491528 | tf_op jit(solution)/shard_map/ppermute | solution.py:389
  7.6 8.3 %collective-permute-start.3 = (bf16[128,640]{1,0:T(8,128)(2,1)S(1)}, bf16[128,640]{1,0:T(8,128)(2,1)S(1)}, u32[]{:S(2)}, u32[]{:S(2)}) collective-permute-start(bf16[128,640]{1,0:T(8,128)(2,1)S(1)} %copy-done.1), channel_id=1, source_target_pairs={{0,6},{1,7},{2,4},{3,5},{4,2},{5,3},{6,0},{7,1},{8,14},{9,15},{10,... | collective-permute-start | bytes 491528 | tf_op jit(solution)/shard_map/ppermute | solution.py:389
  7.7 6.1 %collective-permute-start.6 = (bf16[2,128,128]{2,1,0:T(8,128)(2,1)S(1)}, bf16[2,128,128]{2,1,0:T(8,128)(2,1)S(1)}, u32[]{:S(2)}, u32[]{:S(2)}) collective-permute-start(bf16[2,128,128]{2,1,0:T(8,128)(2,1)S(1)} %pad_maximum_fusion.packed.refs_0_), channel_id=1, source_target_pairs={{0,16},{8,24},{16,0},{24,8},{1,17},{9,25},{17,1},{25,9},{2,18},{10... | collective-permute-start | bytes 196616 | tf_op jit(solution)/shard_map/ppermute | solution.py:396
  10.8 6.0 %collective-permute-start.5 = (bf16[2,128,128]{2,1,0:T(8,128)(2,1)S(1)}, bf16[2,128,128]{2,1,0:T(8,128)(2,1)S(1)}, u32[]{:S(2)}, u32[]{:S(2)}) collective-permute-start(bf16[2,128,128]{2,1,0:T(8,128)(2,1)S(1)} %pad_maximum_fusion.packed.refs_0_), channel_id=1, source_target_pairs={{0,8},{8,0},{16,24},{24,16},{1,9},{9,1},{17,25},{25,17},{2,10},{10... | collective-permute-start | bytes 196616 | tf_op jit(solution)/shard_map/ppermute | solution.py:396
  13.8 4.3 %collective-permute-start.7 = (bf16[2,128,128]{2,1,0:T(8,128)(2,1)S(1)}, bf16[2,128,128]{2,1,0:T(8,128)(2,1)S(1)}, u32[]{:S(2)}, u32[]{:S(2)}) collective-permute-start(bf16[2,128,128]{2,1,0:T(8,128)(2,1)S(1)} %collective-permute-done.6.refs_2_), channel_id=1, source_target_pairs={{0,8},{8,0},{16,24},{24,16},{1,9},{9,1},{17,25},{25,17},{2,10},{10... | collective-permute-start | bytes 196616 | tf_op jit(solution)/shard_map/ppermute | solution.py:396
  16.6 17.8 %copy-start.3 = (bf16[1024,128]{1,0:T(8,128)(2,1)S(1)}, bf16[1024,128]{1,0:T(8,128)(2,1)}, u32[]{:S(2)}) copy-start(bf16[1024,128]{1,0:T(8,128)(2,1)} %values.3) | copy-start | bytes 786436
  16.7 2.2 %collective-permute-start.4 = (f32[128,128]{1,0:T(8,128)S(1)}, f32[128,128]{1,0:T(8,128)S(1)}, u32[]{:S(2)}, u32[]{:S(2)}) collective-permute-start(f32[128,128]{1,0:T(8,128)S(1)} %get-tuple-element.48), channel_id=1, source_target_pairs={{0,1},{1,0},{2,3},{3,2},{4,5},{5,4},{6,7},{7,6},{8,9},{9,8},{10,11... | collective-permute-start | bytes 196616 | tf_op jit(solution)/shard_map/ppermute | solution.py:393
  19.0 4.6 %collective-permute-start.10 = (bf16[352,128]{1,0:T(8,128)(2,1)S(1)}, bf16[352,128]{1,0:T(8,128)(2,1)S(1)}, u32[]{:S(2)}, u32[]{:S(2)}) collective-permute-start(bf16[352,128]{1,0:T(8,128)(2,1)S(1)} %get-tuple-element.53), channel_id=1, source_target_pairs={{0,8},{8,0},{16,24},{24,16},{1,9},{9,1},{17,25},{25,17},{2,10},{10... | collective-permute-start | bytes 270344 | tf_op jit(solution)/shard_map/ppermute | solution.py:396
  20.2 7.7 %collective-permute-start.8 = (bf16[352,128]{1,0:T(8,128)(2,1)S(1)}, bf16[352,128]{1,0:T(8,128)(2,1)S(1)}, u32[]{:S(2)}, u32[]{:S(2)}) collective-permute-start(bf16[352,128]{1,0:T(8,128)(2,1)S(1)} %get-tuple-element.51), channel_id=1, source_target_pairs={{0,24},{8,16},{16,8},{24,0},{1,25},{9,17},{17,9},{25,1},{2,26},{10... | collective-permute-start | bytes 270344 | tf_op jit(solution)/shard_map/ppermute | solution.py:396
  23.4 7.4 %collective-permute-start.9 = (bf16[352,128]{1,0:T(8,128)(2,1)S(1)}, bf16[352,128]{1,0:T(8,128)(2,1)S(1)}, u32[]{:S(2)}, u32[]{:S(2)}) collective-permute-start(bf16[352,128]{1,0:T(8,128)(2,1)S(1)} %get-tuple-element.52), channel_id=1, source_target_pairs={{0,16},{8,24},{16,0},{24,8},{1,17},{9,25},{17,1},{25,9},{2,18},{10... | collective-permute-start | bytes 270344 | tf_op jit(solution)/shard_map/ppermute | solution.py:396
  30.9 12.1 %collective-permute-start.14 = (bf16[800,128]{1,0:T(8,128)(2,1)S(1)}, bf16[800,128]{1,0:T(8,128)(2,1)S(1)}, u32[]{:S(2)}, u32[]{:S(2)}) collective-permute-start(bf16[800,128]{1,0:T(8,128)(2,1)S(1)} %shard_map.133.refs_0_), channel_id=1, source_target_pairs={{0,2},{1,3},{2,0},{3,1},{4,6},{5,7},{6,4},{7,5},{8,10},{9,11},{10,... | collective-permute-start | bytes 614408 | tf_op jit(solution)/shard_map/ppermute | solution.py:389
  32.4 10.6 %collective-permute-start.15 = (bf16[800,128]{1,0:T(8,128)(2,1)S(1)}, bf16[800,128]{1,0:T(8,128)(2,1)S(1)}, u32[]{:S(2)}, u32[]{:S(2)}) collective-permute-start(bf16[800,128]{1,0:T(8,128)(2,1)S(1)} %shard_map.133.refs_0_), channel_id=1, source_target_pairs={{0,4},{1,5},{2,6},{3,7},{4,0},{5,1},{6,2},{7,3},{8,12},{9,13},{10,... | collective-permute-start | bytes 614408 | tf_op jit(solution)/shard_map/ppermute | solution.py:389
  33.5 9.4 %collective-permute-start.16 = (bf16[800,128]{1,0:T(8,128)(2,1)S(1)}, bf16[800,128]{1,0:T(8,128)(2,1)S(1)}, u32[]{:S(2)}, u32[]{:S(2)}) collective-permute-start(bf16[800,128]{1,0:T(8,128)(2,1)S(1)} %shard_map.133.refs_0_), channel_id=1, source_target_pairs={{0,6},{1,7},{2,4},{3,5},{4,2},{5,3},{6,0},{7,1},{8,14},{9,15},{10,... | collective-permute-start | bytes 614408 | tf_op jit(solution)/shard_map/ppermute | solution.py:389
  35.4 5.8 %collective-permute-start.11 = (bf16[128,128]{1,0:T(8,128)(2,1)S(1)}, bf16[128,128]{1,0:T(8,128)(2,1)S(1)}, u32[]{:S(2)}, u32[]{:S(2)}) collective-permute-start(bf16[128,128]{1,0:T(8,128)(2,1)S(1)} %get-tuple-element.56), channel_id=1, source_target_pairs={{0,24},{8,16},{16,8},{24,0},{1,25},{9,17},{17,9},{25,1},{2,26},{10... | collective-permute-start | bytes 98312 | tf_op jit(solution)/shard_map/ppermute | solution.py:396
  38.1 4.8 %collective-permute-start.12 = (bf16[128,128]{1,0:T(8,128)(2,1)S(1)}, bf16[128,128]{1,0:T(8,128)(2,1)S(1)}, u32[]{:S(2)}, u32[]{:S(2)}) collective-permute-start(bf16[128,128]{1,0:T(8,128)(2,1)S(1)} %get-tuple-element.57), channel_id=1, source_target_pairs={{0,16},{8,24},{16,0},{24,8},{1,17},{9,25},{17,1},{25,9},{2,18},{10... | collective-permute-start | bytes 98312 | tf_op jit(solution)/shard_map/ppermute | solution.py:396
  43.0 2.3 %collective-permute-start.17 = (bf16[2880,128]{1,0:T(8,128)(2,1)S(1)}, bf16[2880,128]{1,0:T(8,128)(2,1)S(1)}, u32[]{:S(2)}, u32[]{:S(2)}) collective-permute-start(bf16[2880,128]{1,0:T(8,128)(2,1)S(1)} %shard_map.136.own), channel_id=1, source_target_pairs={{0,1},{1,0},{2,3},{3,2},{4,5},{5,4},{6,7},{7,6},{8,9},{9,8},{10,11... | collective-permute-start | bytes 2211848 | tf_op jit(solution)/shard_map/ppermute | solution.py:393
  43.1 4.0 %collective-permute-start.13 = (bf16[128,128]{1,0:T(8,128)(2,1)S(1)}, bf16[128,128]{1,0:T(8,128)(2,1)S(1)}, u32[]{:S(2)}, u32[]{:S(2)}) collective-permute-start(bf16[128,128]{1,0:T(8,128)(2,1)S(1)} %get-tuple-element.61), channel_id=1, source_target_pairs={{0,8},{8,0},{16,24},{24,16},{1,9},{9,1},{17,25},{25,17},{2,10},{10... | collective-permute-start | bytes 98312 | tf_op jit(solution)/shard_map/ppermute | solution.py:396
  (2 other events, 3.7 us)

commit v13 on v12

--- a/solution.py
+++ b/solution.py
@@ -23,6 +23,11 @@
     return lax.dot_general(
         a, b, (((on_a,), (on_b,)), ((), ())), preferred_element_type=jnp.float32
     )
+
+
+def two_first(blocks):
+    blocks = list(blocks)
+    return blocks[:1] + blocks[2:3] + blocks[1:2] + blocks[3:]
 
 
 def place():
@@ -167,7 +172,7 @@
 
 
 def bundle_kernel(n_t, starts, count, gate_b, *refs):
-    heads, out = refs[:n_t][::-1], refs[n_t]
+    heads, out = two_first(refs[:n_t]), refs[n_t]
     tiles = gate_b.shape[2] // LANES
     part = (starts[2] - starts[1]) // tiles
     wide = [heads[k][starts[1] : starts[2], :].astype(jnp.float32) for k in range(n_t)]
@@ -453,7 +458,7 @@
     base = tiles * n_t * part
     bundle = call(
         functools.partial(bundle_kernel, n_t, starts, count),
-        [gate_b] + heads_all[::-1],
+        [gate_b] + two_first(heads_all),
         shape(bf16, base + n_t * count, LANES),
     )
     bundles = over_chips(bundle)
@@ -467,10 +472,9 @@
         flops=10 * (n_t - 2) * rows * k_rows * HD,
     )
     parts = {k: over_time(far[1 + n_t - k], k) for k in range(n_t - 1, 1, -1)}
-    near_bias, _ = lax.optimization_barrier((bias, parts[n_t - 1]))
     near = call(
         functools.partial(grads_kernel, n_t, starts, 0, 2),
-        [near_bias, keys, values] + packed_all + heads_all[::-1] + list(far[:2]),
+        [bias, keys, values] + packed_all + heads_all[::-1] + list(far[:2]),
         [shape(bf16, k_rows, HD)] * 2 + [shape(bf16, HD, rows)] * 2,
         flops=20 * rows * k_rows * HD,
     )

time: 48 us -> 46.8 us (0.975)
  waiting for transfers between devices: 15.8 us -> 14.6 us
    ppermute x9, waiting for transfers between devices: 13.2 us -> 11.9 us  [over_time(): return lax.ppermute(x, 'tm', [(t, t ^ k) for t in range(n_t)])]
  transfers between devices with their start and end apart: 18 -> 18, of which waited for: 10 -> 9; matrix products, arithmetic and copies ran while one was open for 0% -> 0% of each run, Pallas kernels for 14% -> 14%
where the time goes in v13:
time: 46.8 us; the launch traced here: 46.6 us
  starting transfers between devices  21.4 us (46%)
  waiting for transfers between devices  14.6 us (31%)
  Pallas kernels  8.98 us (19%)
  local copies, waits for them, and re-layouts  0.84 us (2%)
  between operations  0.8 us (2%)
    ppermute x9, starting transfers between devices, over_time(): return lax.ppermute(x, 'tm', [(t, t ^ k) for t in range(n_t)])  13.1 us
    ppermute x9, waiting for transfers between devices, over_time(): return lax.ppermute(x, 'tm', [(t, t ^ k) for t in range(n_t)])  11.9 us
    pallas_call x12, Pallas kernels, call(): pl.pallas_call(kernel, out_shape=out_shape, in_specs=[pl.BlockSpec(memory...  8.98 us
    ppermute x6, starting transfers between devices, over_chips(): lax.ppermute(x, 'space', [(s, s ^ 2 * k) for s in range(n_s)])  7.67 us
    ppermute x3, waiting for transfers between devices, over_cores(): return lax.ppermute(x, 'space', [(s, s ^ 1) for s in range(n_s)])  1.73 us
  transfers between devices with their start and end apart: 18, of which 9 were waited for; matrix products, arithmetic and copies ran while one was open for 0% of the time, Pallas kernels for 14%

profile of v13, /device:TPU:0, one launch (start us, length us, event | category | flops | bytes accessed | tf_op | source)
XLA Modules:
  0.0 46.6 jit_solution(12092788358505015021)
XLA Ops:
  0.7 0.8 %copy-done.4 = bf16[128,128]{1,0:T(8,128)(2,1)S(1)} copy-done((bf16[128,128]{1,0:T(8,128)(2,1)S(1)}, bf16[128,128]{1,0:T(8,128)(2,1)}, u32[]{:S(2)}) %copy-start.4) | copy-done | bytes 32792
  1.5 1.5 %shard_map.128 = (bf16[4,128,640]{2,1,0:T(8,128)(2,1)S(1)}, bf16[128,2688]{1,0:T(8,128)(2,1)S(1)}) custom-call(bf16[128,5120]{1,0:T(8,128)(2,1)} %weight_in.1, bf16[128,128]{1,0:T(8,128)(2,1)S(1)} %copy-done.4), custom_call_target="tpu_custom_call" | custom-call | bytes 1343488 | tf_op jit(solution)/shard_map/pallas_call | solution.py:349
  3.5 2.6 %collective-permute-start.1 = (bf16[128,640]{1,0:T(8,128)(2,1)S(1)}, bf16[128,640]{1,0:T(8,128)(2,1)S(1)}, u32[]{:S(2)}, u32[]{:S(2)}) collective-permute-start(bf16[128,640]{1,0:T(8,128)(2,1)S(1)} %copy-done.1), channel_id=1, source_target_pairs={{0,2},{1,3},{2,0},{3,1},{4,6},{5,7},{6,4},{7,5},{8,10},{9,11},{10,... | collective-permute-start | bytes 491528 | tf_op jit(solution)/shard_map/ppermute | solution.py:394
  6.1 1.5 %collective-permute-start.2 = (bf16[128,640]{1,0:T(8,128)(2,1)S(1)}, bf16[128,640]{1,0:T(8,128)(2,1)S(1)}, u32[]{:S(2)}, u32[]{:S(2)}) collective-permute-start(bf16[128,640]{1,0:T(8,128)(2,1)S(1)} %copy-done.1), channel_id=1, source_target_pairs={{0,4},{1,5},{2,6},{3,7},{4,0},{5,1},{6,2},{7,3},{8,12},{9,13},{10,... | collective-permute-start | bytes 491528 | tf_op jit(solution)/shard_map/ppermute | solution.py:394
  7.7 3.1 %collective-permute-start.6 = (bf16[2,128,128]{2,1,0:T(8,128)(2,1)S(1)}, bf16[2,128,128]{2,1,0:T(8,128)(2,1)S(1)}, u32[]{:S(2)}, u32[]{:S(2)}) collective-permute-start(bf16[2,128,128]{2,1,0:T(8,128)(2,1)S(1)} %pad_maximum_fusion.packed.refs_0_), channel_id=1, source_target_pairs={{0,16},{8,24},{16,0},{24,8},{1,17},{9,25},{17,1},{25,9},{2,18},{10... | collective-permute-start | bytes 196616 | tf_op jit(solution)/shard_map/ppermute | solution.py:401
  10.8 1.6 %collective-permute-start.5 = (bf16[2,128,128]{2,1,0:T(8,128)(2,1)S(1)}, bf16[2,128,128]{2,1,0:T(8,128)(2,1)S(1)}, u32[]{:S(2)}, u32[]{:S(2)}) collective-permute-start(bf16[2,128,128]{2,1,0:T(8,128)(2,1)S(1)} %pad_maximum_fusion.packed.refs_0_), channel_id=1, source_target_pairs={{0,8},{8,0},{16,24},{24,16},{1,9},{9,1},{17,25},{25,17},{2,10},{10... | collective-permute-start | bytes 196616 | tf_op jit(solution)/shard_map/ppermute | solution.py:401
  13.0 0.8 %collective-permute-done.6.refs_2_ = bf16[2,128,128]{2,1,0:T(8,128)(2,1)S(1)} collective-permute-done((bf16[2,128,128]{2,1,0:T(8,128)(2,1)S(1)}, bf16[2,128,128]{2,1,0:T(8,128)(2,1)S(1)}, u32[]{:S(2)}, u32[]{:S(2)}) %collective-permute-start.6) | collective-permute-done | bytes 65568 | tf_op jit(solution)/shard_map/ppermute | solution.py:401
  13.8 1.2 %collective-permute-start.7 = (bf16[2,128,128]{2,1,0:T(8,128)(2,1)S(1)}, bf16[2,128,128]{2,1,0:T(8,128)(2,1)S(1)}, u32[]{:S(2)}, u32[]{:S(2)}) collective-permute-start(bf16[2,128,128]{2,1,0:T(8,128)(2,1)S(1)} %collective-permute-done.6.refs_2_), channel_id=1, source_target_pairs={{0,8},{8,0},{16,24},{24,16},{1,9},{9,1},{17,25},{25,17},{2,10},{10... | collective-permute-start | bytes 196616 | tf_op jit(solution)/shard_map/ppermute | solution.py:401
  15.0 0.9 %collective-permute-done.2.refs_2_ = bf16[128,640]{1,0:T(8,128)(2,1)S(1)} collective-permute-done((bf16[128,640]{1,0:T(8,128)(2,1)S(1)}, bf16[128,640]{1,0:T(8,128)(2,1)S(1)}, u32[]{:S(2)}, u32[]{:S(2)}) %collective-permute-start.2) | collective-permute-done | bytes 163872 | tf_op jit(solution)/shard_map/ppermute | solution.py:394
  15.9 0.8 %shard_map.130 = (f32[128,128]{1,0:T(8,128)S(1)}, f32[128,128]{1,0:T(8,128)S(1)}, f32[40,128]{1,0:T(8,128)S(1)}) custom-call(bf16[2,128,128]{2,1,0:T(8,128)(2,1)S(1)} %pad_maximum_fusion.packed.refs_0_, bf16[4,128,640]{2,1,0:T(8,128)(2,1)S(1)} %get-tuple-element.44.kept, bf16[128,2688]{1,0:T(8,128)(2,1)S(1)} %collective-permute-done.received, ...), custom_call_target="tpu_custom_call" | custom-call | flops 335544320 | bytes 2084864 | tf_op jit(solution)/shard_map/pallas_call | solution.py:349
  16.7 1.3 %collective-permute-done.7.refs_3_ = bf16[2,128,128]{2,1,0:T(8,128)(2,1)S(1)} collective-permute-done((bf16[2,128,128]{2,1,0:T(8,128)(2,1)S(1)}, bf16[2,128,128]{2,1,0:T(8,128)(2,1)S(1)}, u32[]{:S(2)}, u32[]{:S(2)}) %collective-permute-start.7) | collective-permute-done | bytes 65568 | tf_op jit(solution)/shard_map/ppermute | solution.py:401
  19.0 3.9 %collective-permute-start.10 = (bf16[352,128]{1,0:T(8,128)(2,1)S(1)}, bf16[352,128]{1,0:T(8,128)(2,1)S(1)}, u32[]{:S(2)}, u32[]{:S(2)}) collective-permute-start(bf16[352,128]{1,0:T(8,128)(2,1)S(1)} %get-tuple-element.53), channel_id=1, source_target_pairs={{0,24},{8,16},{16,8},{24,0},{1,25},{9,17},{17,9},{25,1},{2,26},{10... | collective-permute-start | bytes 270344 | tf_op jit(solution)/shard_map/ppermute | solution.py:401
  23.5 2.7 %collective-permute-done.10.refs_3_.refs_4_ = bf16[352,128]{1,0:T(8,128)(2,1)S(1)} collective-permute-done((bf16[352,128]{1,0:T(8,128)(2,1)S(1)}, bf16[352,128]{1,0:T(8,128)(2,1)S(1)}, u32[]{:S(2)}, u32[]{:S(2)}) %collective-permute-start.10) | collective-permute-done | bytes 90144 | tf_op jit(solution)/shard_map/ppermute | solution.py:401
  26.2 3.5 %collective-permute-done.8.refs_1_.refs_5_ = bf16[352,128]{1,0:T(8,128)(2,1)S(1)} collective-permute-done((bf16[352,128]{1,0:T(8,128)(2,1)S(1)}, bf16[352,128]{1,0:T(8,128)(2,1)S(1)}, u32[]{:S(2)}, u32[]{:S(2)}) %collective-permute-start.8) | collective-permute-done | bytes 90144 | tf_op jit(solution)/shard_map/ppermute | solution.py:401
  29.7 1.3 %collective-permute-start.14 = (bf16[800,128]{1,0:T(8,128)(2,1)S(1)}, bf16[800,128]{1,0:T(8,128)(2,1)S(1)}, u32[]{:S(2)}, u32[]{:S(2)}) collective-permute-start(bf16[800,128]{1,0:T(8,128)(2,1)S(1)} %shard_map.133.refs_0_), channel_id=1, source_target_pairs={{0,2},{1,3},{2,0},{3,1},{4,6},{5,7},{6,4},{7,5},{8,10},{9,11},{10,... | collective-permute-start | bytes 614408 | tf_op jit(solution)/shard_map/ppermute | solution.py:394
  31.0 1.4 %collective-permute-start.15 = (bf16[800,128]{1,0:T(8,128)(2,1)S(1)}, bf16[800,128]{1,0:T(8,128)(2,1)S(1)}, u32[]{:S(2)}, u32[]{:S(2)}) collective-permute-start(bf16[800,128]{1,0:T(8,128)(2,1)S(1)} %shard_map.133.refs_0_), channel_id=1, source_target_pairs={{0,4},{1,5},{2,6},{3,7},{4,0},{5,1},{6,2},{7,3},{8,12},{9,13},{10,... | collective-permute-start | bytes 614408 | tf_op jit(solution)/shard_map/ppermute | solution.py:394
  32.4 0.9 %collective-permute-start.16 = (bf16[800,128]{1,0:T(8,128)(2,1)S(1)}, bf16[800,128]{1,0:T(8,128)(2,1)S(1)}, u32[]{:S(2)}, u32[]{:S(2)}) collective-permute-start(bf16[800,128]{1,0:T(8,128)(2,1)S(1)} %shard_map.133.refs_0_), channel_id=1, source_target_pairs={{0,6},{1,7},{2,4},{3,5},{4,2},{5,3},{6,0},{7,1},{8,14},{9,15},{10,... | collective-permute-start | bytes 614408 | tf_op jit(solution)/shard_map/ppermute | solution.py:394
  33.3 1.0 %shard_map.134 = (f32[1024,128]{1,0:T(8,128)S(1)}, f32[1024,128]{1,0:T(8,128)S(1)}, bf16[128,128]{1,0:T(8,128)(2,1)S(1)}, bf16[128,128]{1,0:T(8,128)(2,1)S(1)}) custom-call(f32[2,512]{1,0:T(2,128)S(1)} %get-tuple-element.54.bias, bf16[1024,128]{1,0:T(8,128)(2,1)S(1)} %copy-done, bf16[1024,128]{1,0:T(8,128)(2,1)S(1)} %copy-done.3, ...), custom_call_target="tpu_custom_call" | custom-call | flops 335544320 | bytes 1150976 | tf_op jit(solution)/shard_map/pallas_call | solution.py:349
  34.3 2.7 %collective-permute-start.11 = (bf16[128,128]{1,0:T(8,128)(2,1)S(1)}, bf16[128,128]{1,0:T(8,128)(2,1)S(1)}, u32[]{:S(2)}, u32[]{:S(2)}) collective-permute-start(bf16[128,128]{1,0:T(8,128)(2,1)S(1)} %get-tuple-element.55), channel_id=1, source_target_pairs={{0,24},{8,16},{16,8},{24,0},{1,25},{9,17},{17,9},{25,1},{2,26},{10... | collective-permute-start | bytes 98312 | tf_op jit(solution)/shard_map/ppermute | solution.py:401
  36.9 1.7 %shard_map.135 = (bf16[1024,128]{1,0:T(8,128)(2,1)}, bf16[1024,128]{1,0:T(8,128)(2,1)}, bf16[128,128]{1,0:T(8,128)(2,1)S(1)}, bf16[128,128]{1,0:T(8,128)(2,1)S(1)}) custom-call(f32[2,512]{1,0:T(2,128)S(1)} %get-tuple-element.54.bias, bf16[1024,128]{1,0:T(8,128)(2,1)S(1)} %copy-done, bf16[1024,128]{1,0:T(8,128)(2,1)S(1)} %copy-done.3, ...), custom_call_target="tpu_custom_call" | custom-call | flops 335544320 | bytes 2199552 | tf_op jit(solution)/shard_map/pallas_call | solution.py:349
  38.6 1.4 %collective-permute-done.11.refs_0_ = bf16[128,128]{1,0:T(8,128)(2,1)S(1)} collective-permute-done((bf16[128,128]{1,0:T(8,128)(2,1)S(1)}, bf16[128,128]{1,0:T(8,128)(2,1)S(1)}, u32[]{:S(2)}, u32[]{:S(2)}) %collective-permute-start.11) | collective-permute-done | bytes 32800 | tf_op jit(solution)/shard_map/ppermute | solution.py:401
  40.0 1.7 %collective-permute-done.12.refs_1_ = bf16[128,128]{1,0:T(8,128)(2,1)S(1)} collective-permute-done((bf16[128,128]{1,0:T(8,128)(2,1)S(1)}, bf16[128,128]{1,0:T(8,128)(2,1)S(1)}, u32[]{:S(2)}, u32[]{:S(2)}) %collective-permute-start.12) | collective-permute-done | bytes 32800 | tf_op jit(solution)/shard_map/ppermute | solution.py:401
  42.4 1.7 %collective-permute-done.17.other = bf16[2880,128]{1,0:T(8,128)(2,1)S(1)} collective-permute-done((bf16[2880,128]{1,0:T(8,128)(2,1)S(1)}, bf16[2880,128]{1,0:T(8,128)(2,1)S(1)}, u32[]{:S(2)}, u32[]{:S(2)}) %collective-permute-start.17) | collective-permute-done | bytes 737312 | tf_op jit(solution)/shard_map/ppermute | solution.py:398
  44.1 1.3 %shard_map.138 = (f32[128,1280]{1,0:T(8,128)}, f32[16,5120]{1,0:T(8,128)}) custom-call(f32[8,16,128]{2,1,0:T(8,128)S(1)} %get-tuple-element.61.hot, bf16[2880,128]{1,0:T(8,128)(2,1)S(1)} %collective-permute-done.17.other, f32[128,640]{1,0:T(8,128)S(1)} %get-tuple-element.67.own_weight, f32[16,2560]{1,0:T(8,128)S(1)} %get-tuple-element.68.own_gate, ...), custom_call_target="tpu_custom_call" | custom-call | flops 83886080 | bytes 1556480 | tf_op jit(solution)/shard_map/pallas_call | solution.py:349
  (41 shorter events, 4.8 us)
Async XLA Ops:
  0.6 11.7 %copy-start.2 = (f32[16,5120]{1,0:T(8,128)S(1)}, f32[16,5120]{1,0:T(8,128)}, u32[]{:S(2)}) copy-start(f32[16,5120]{1,0:T(8,128)} %gate) | copy-start | bytes 983044
  1.5 6.2 %copy-start.7 = (bf16[128,128]{1,0:T(8,128)(2,1)S(1)}, bf16[128,128]{1,0:T(8,128)(2,1)}, u32[]{:S(2)}) copy-start(bf16[128,128]{1,0:T(8,128)(2,1)} %param.9) | copy-start | bytes 98308
  1.5 10.9 %copy-start.5 = (s32[8]{0:T(128)S(1)}, s32[8]{0:T(128)}, u32[]{:S(2)}) copy-start(s32[8]{0:T(128)} %levels.1) | copy-start | bytes 100
  1.5 10.9 %copy-start.6 = (s32[4]{0:T(128)S(1)}, s32[4]{0:T(128)}, u32[]{:S(2)}) copy-start(s32[4]{0:T(128)} %clips.1) | copy-start | bytes 52
  3.0 15.1 %copy-start = (bf16[1024,128]{1,0:T(8,128)(2,1)S(1)}, bf16[1024,128]{1,0:T(8,128)(2,1)}, u32[]{:S(2)}) copy-start(bf16[1024,128]{1,0:T(8,128)(2,1)} %keys.5) | copy-start | bytes 786436
  3.0 4.7 %collective-permute-start = (bf16[128,2688]{1,0:T(8,128)(2,1)S(1)}, bf16[128,2688]{1,0:T(8,128)(2,1)S(1)}, u32[]{:S(2)}, u32[]{:S(2)}) collective-permute-start(bf16[128,2688]{1,0:T(8,128)(2,1)S(1)} %get-tuple-element.39), channel_id=1, source_target_pairs={{0,1},{1,0},{2,3},{3,2},{4,5},{5,4},{6,7},{7,6},{8,9},{9,8},{10,11... | collective-permute-start | bytes 2064392 | tf_op jit(solution)/shard_map/ppermute | solution.py:398
  3.5 11.4 %collective-permute-start.1 = (bf16[128,640]{1,0:T(8,128)(2,1)S(1)}, bf16[128,640]{1,0:T(8,128)(2,1)S(1)}, u32[]{:S(2)}, u32[]{:S(2)}) collective-permute-start(bf16[128,640]{1,0:T(8,128)(2,1)S(1)} %copy-done.1), channel_id=1, source_target_pairs={{0,2},{1,3},{2,0},{3,1},{4,6},{5,7},{6,4},{7,5},{8,10},{9,11},{10,... | collective-permute-start | bytes 491528 | tf_op jit(solution)/shard_map/ppermute | solution.py:394
  6.1 9.8 %collective-permute-start.2 = (bf16[128,640]{1,0:T(8,128)(2,1)S(1)}, bf16[128,640]{1,0:T(8,128)(2,1)S(1)}, u32[]{:S(2)}, u32[]{:S(2)}) collective-permute-start(bf16[128,640]{1,0:T(8,128)(2,1)S(1)} %copy-done.1), channel_id=1, source_target_pairs={{0,4},{1,5},{2,6},{3,7},{4,0},{5,1},{6,2},{7,3},{8,12},{9,13},{10,... | collective-permute-start | bytes 491528 | tf_op jit(solution)/shard_map/ppermute | solution.py:394
  7.6 8.3 %collective-permute-start.3 = (bf16[128,640]{1,0:T(8,128)(2,1)S(1)}, bf16[128,640]{1,0:T(8,128)(2,1)S(1)}, u32[]{:S(2)}, u32[]{:S(2)}) collective-permute-start(bf16[128,640]{1,0:T(8,128)(2,1)S(1)} %copy-done.1), channel_id=1, source_target_pairs={{0,6},{1,7},{2,4},{3,5},{4,2},{5,3},{6,0},{7,1},{8,14},{9,15},{10,... | collective-permute-start | bytes 491528 | tf_op jit(solution)/shard_map/ppermute | solution.py:394
  7.7 6.1 %collective-permute-start.6 = (bf16[2,128,128]{2,1,0:T(8,128)(2,1)S(1)}, bf16[2,128,128]{2,1,0:T(8,128)(2,1)S(1)}, u32[]{:S(2)}, u32[]{:S(2)}) collective-permute-start(bf16[2,128,128]{2,1,0:T(8,128)(2,1)S(1)} %pad_maximum_fusion.packed.refs_0_), channel_id=1, source_target_pairs={{0,16},{8,24},{16,0},{24,8},{1,17},{9,25},{17,1},{25,9},{2,18},{10... | collective-permute-start | bytes 196616 | tf_op jit(solution)/shard_map/ppermute | solution.py:401
  10.8 6.0 %collective-permute-start.5 = (bf16[2,128,128]{2,1,0:T(8,128)(2,1)S(1)}, bf16[2,128,128]{2,1,0:T(8,128)(2,1)S(1)}, u32[]{:S(2)}, u32[]{:S(2)}) collective-permute-start(bf16[2,128,128]{2,1,0:T(8,128)(2,1)S(1)} %pad_maximum_fusion.packed.refs_0_), channel_id=1, source_target_pairs={{0,8},{8,0},{16,24},{24,16},{1,9},{9,1},{17,25},{25,17},{2,10},{10... | collective-permute-start | bytes 196616 | tf_op jit(solution)/shard_map/ppermute | solution.py:401
  13.8 4.3 %collective-permute-start.7 = (bf16[2,128,128]{2,1,0:T(8,128)(2,1)S(1)}, bf16[2,128,128]{2,1,0:T(8,128)(2,1)S(1)}, u32[]{:S(2)}, u32[]{:S(2)}) collective-permute-start(bf16[2,128,128]{2,1,0:T(8,128)(2,1)S(1)} %collective-permute-done.6.refs_2_), channel_id=1, source_target_pairs={{0,8},{8,0},{16,24},{24,16},{1,9},{9,1},{17,25},{25,17},{2,10},{10... | collective-permute-start | bytes 196616 | tf_op jit(solution)/shard_map/ppermute | solution.py:401
  16.6 16.6 %copy-start.3 = (bf16[1024,128]{1,0:T(8,128)(2,1)S(1)}, bf16[1024,128]{1,0:T(8,128)(2,1)}, u32[]{:S(2)}) copy-start(bf16[1024,128]{1,0:T(8,128)(2,1)} %values.3) | copy-start | bytes 786436
  16.7 2.2 %collective-permute-start.4 = (f32[128,128]{1,0:T(8,128)S(1)}, f32[128,128]{1,0:T(8,128)S(1)}, u32[]{:S(2)}, u32[]{:S(2)}) collective-permute-start(f32[128,128]{1,0:T(8,128)S(1)} %get-tuple-element.47), channel_id=1, source_target_pairs={{0,1},{1,0},{2,3},{3,2},{4,5},{5,4},{6,7},{7,6},{8,9},{9,8},{10,11... | collective-permute-start | bytes 196616 | tf_op jit(solution)/shard_map/ppermute | solution.py:398
  19.0 7.2 %collective-permute-start.10 = (bf16[352,128]{1,0:T(8,128)(2,1)S(1)}, bf16[352,128]{1,0:T(8,128)(2,1)S(1)}, u32[]{:S(2)}, u32[]{:S(2)}) collective-permute-start(bf16[352,128]{1,0:T(8,128)(2,1)S(1)} %get-tuple-element.53), channel_id=1, source_target_pairs={{0,24},{8,16},{16,8},{24,0},{1,25},{9,17},{17,9},{25,1},{2,26},{10... | collective-permute-start | bytes 270344 | tf_op jit(solution)/shard_map/ppermute | solution.py:401
  22.9 6.8 %collective-permute-start.8 = (bf16[352,128]{1,0:T(8,128)(2,1)S(1)}, bf16[352,128]{1,0:T(8,128)(2,1)S(1)}, u32[]{:S(2)}, u32[]{:S(2)}) collective-permute-start(bf16[352,128]{1,0:T(8,128)(2,1)S(1)} %get-tuple-element.51), channel_id=1, source_target_pairs={{0,16},{8,24},{16,0},{24,8},{1,17},{9,25},{17,1},{25,9},{2,18},{10... | collective-permute-start | bytes 270344 | tf_op jit(solution)/shard_map/ppermute | solution.py:401
  22.9 6.8 %collective-permute-start.9 = (bf16[352,128]{1,0:T(8,128)(2,1)S(1)}, bf16[352,128]{1,0:T(8,128)(2,1)S(1)}, u32[]{:S(2)}, u32[]{:S(2)}) collective-permute-start(bf16[352,128]{1,0:T(8,128)(2,1)S(1)} %get-tuple-element.52), channel_id=1, source_target_pairs={{0,8},{8,0},{16,24},{24,16},{1,9},{9,1},{17,25},{25,17},{2,10},{10... | collective-permute-start | bytes 270344 | tf_op jit(solution)/shard_map/ppermute | solution.py:401
  29.7 12.0 %collective-permute-start.14 = (bf16[800,128]{1,0:T(8,128)(2,1)S(1)}, bf16[800,128]{1,0:T(8,128)(2,1)S(1)}, u32[]{:S(2)}, u32[]{:S(2)}) collective-permute-start(bf16[800,128]{1,0:T(8,128)(2,1)S(1)} %shard_map.133.refs_0_), channel_id=1, source_target_pairs={{0,2},{1,3},{2,0},{3,1},{4,6},{5,7},{6,4},{7,5},{8,10},{9,11},{10,... | collective-permute-start | bytes 614408 | tf_op jit(solution)/shard_map/ppermute | solution.py:394
  31.0 10.7 %collective-permute-start.15 = (bf16[800,128]{1,0:T(8,128)(2,1)S(1)}, bf16[800,128]{1,0:T(8,128)(2,1)S(1)}, u32[]{:S(2)}, u32[]{:S(2)}) collective-permute-start(bf16[800,128]{1,0:T(8,128)(2,1)S(1)} %shard_map.133.refs_0_), channel_id=1, source_target_pairs={{0,4},{1,5},{2,6},{3,7},{4,0},{5,1},{6,2},{7,3},{8,12},{9,13},{10,... | collective-permute-start | bytes 614408 | tf_op jit(solution)/shard_map/ppermute | solution.py:394
  32.4 9.4 %collective-permute-start.16 = (bf16[800,128]{1,0:T(8,128)(2,1)S(1)}, bf16[800,128]{1,0:T(8,128)(2,1)S(1)}, u32[]{:S(2)}, u32[]{:S(2)}) collective-permute-start(bf16[800,128]{1,0:T(8,128)(2,1)S(1)} %shard_map.133.refs_0_), channel_id=1, source_target_pairs={{0,6},{1,7},{2,4},{3,5},{4,2},{5,3},{6,0},{7,1},{8,14},{9,15},{10,... | collective-permute-start | bytes 614408 | tf_op jit(solution)/shard_map/ppermute | solution.py:394
  34.3 5.8 %collective-permute-start.11 = (bf16[128,128]{1,0:T(8,128)(2,1)S(1)}, bf16[128,128]{1,0:T(8,128)(2,1)S(1)}, u32[]{:S(2)}, u32[]{:S(2)}) collective-permute-start(bf16[128,128]{1,0:T(8,128)(2,1)S(1)} %get-tuple-element.55), channel_id=1, source_target_pairs={{0,24},{8,16},{16,8},{24,0},{1,25},{9,17},{17,9},{25,1},{2,26},{10... | collective-permute-start | bytes 98312 | tf_op jit(solution)/shard_map/ppermute | solution.py:401
  36.9 4.8 %collective-permute-start.12 = (bf16[128,128]{1,0:T(8,128)(2,1)S(1)}, bf16[128,128]{1,0:T(8,128)(2,1)S(1)}, u32[]{:S(2)}, u32[]{:S(2)}) collective-permute-start(bf16[128,128]{1,0:T(8,128)(2,1)S(1)} %get-tuple-element.56), channel_id=1, source_target_pairs={{0,16},{8,24},{16,0},{24,8},{1,17},{9,25},{17,1},{25,9},{2,18},{10... | collective-permute-start | bytes 98312 | tf_op jit(solution)/shard_map/ppermute | solution.py:401
  41.9 2.3 %collective-permute-start.17 = (bf16[2880,128]{1,0:T(8,128)(2,1)S(1)}, bf16[2880,128]{1,0:T(8,128)(2,1)S(1)}, u32[]{:S(2)}, u32[]{:S(2)}) collective-permute-start(bf16[2880,128]{1,0:T(8,128)(2,1)S(1)} %shard_map.136.own), channel_id=1, source_target_pairs={{0,1},{1,0},{2,3},{3,2},{4,5},{5,4},{6,7},{7,6},{8,9},{9,8},{10,11... | collective-permute-start | bytes 2211848 | tf_op jit(solution)/shard_map/ppermute | solution.py:398
  41.9 4.0 %collective-permute-start.13 = (bf16[128,128]{1,0:T(8,128)(2,1)S(1)}, bf16[128,128]{1,0:T(8,128)(2,1)S(1)}, u32[]{:S(2)}, u32[]{:S(2)}) collective-permute-start(bf16[128,128]{1,0:T(8,128)(2,1)S(1)} %get-tuple-element.59), channel_id=1, source_target_pairs={{0,8},{8,0},{16,24},{24,16},{1,9},{9,1},{17,25},{25,17},{2,10},{10... | collective-permute-start | bytes 98312 | tf_op jit(solution)/shard_map/ppermute | solution.py:401
  (2 other events, 3.7 us)

commit v14 on v13

--- a/solution.py
+++ b/solution.py
@@ -25,9 +25,9 @@
     )
 
 
-def two_first(blocks):
+def far_first(blocks):
     blocks = list(blocks)
-    return blocks[:1] + blocks[2:3] + blocks[1:2] + blocks[3:]
+    return blocks[:1] + blocks[:0:-1]
 
 
 def place():
@@ -172,7 +172,7 @@
 
 
 def bundle_kernel(n_t, starts, count, gate_b, *refs):
-    heads, out = two_first(refs[:n_t]), refs[n_t]
+    heads, out = far_first(refs[:n_t]), refs[n_t]
     tiles = gate_b.shape[2] // LANES
     part = (starts[2] - starts[1]) // tiles
     wide = [heads[k][starts[1] : starts[2], :].astype(jnp.float32) for k in range(n_t)]
@@ -458,7 +458,7 @@
     base = tiles * n_t * part
     bundle = call(
         functools.partial(bundle_kernel, n_t, starts, count),
-        [gate_b] + two_first(heads_all),
+        [gate_b] + far_first(heads_all),
         shape(bf16, base + n_t * count, LANES),
     )
     bundles = over_chips(bundle)
@@ -481,7 +481,7 @@
     key_grad, value_grad = near[:2]
     parts[0], parts[1] = near[3], over_time(near[2], 1)
     parts = [parts[k] for k in range(n_t)]
-    bundles, _ = lax.optimization_barrier((bundles, (key_grad, parts[: n_t // 2 - 1 : -1])))
+    bundles, _ = lax.optimization_barrier((bundles, (key_grad, parts[n_t - 1])))
     collected = call(
         functools.partial(collect_kernel, chips, base),
         bundles,

time: 46.8 us -> 47.5 us (1.015)
  starting transfers between devices: 21.4 us -> 23.5 us
  waiting for transfers between devices: 14.6 us -> 13.3 us
    ppermute x9, starting transfers between devices: 13.1 us -> 15.2 us  [over_time(): return lax.ppermute(x, 'tm', [(t, t ^ k) for t in range(n_t)])]
    ppermute x3, waiting for transfers between devices: 1.73 us -> 0.01 us  [over_cores(): return lax.ppermute(x, 'space', [(s, s ^ 1) for s in range(n_s)])]
    ppermute x6, waiting for transfers between devices: 0.92 us -> 2.45 us  [over_chips(): lax.ppermute(x, 'space', [(s, s ^ 2 * k) for s in range(n_s)])]
    ppermute x9, waiting for transfers between devices: 11.9 us -> 10.8 us  [over_time(): return lax.ppermute(x, 'tm', [(t, t ^ k) for t in range(n_t)])]
where the time goes in v14:
time: 47.5 us; the launch traced here: 47.4 us
  starting transfers between devices  23.5 us (49%)
  waiting for transfers between devices  13.3 us (28%)
  Pallas kernels  8.98 us (19%)
  local copies, waits for them, and re-layouts  0.84 us (2%)
  between operations  0.8 us (2%)
    ppermute x9, starting transfers between devices, over_time(): return lax.ppermute(x, 'tm', [(t, t ^ k) for t in range(n_t)])  15.2 us
    ppermute x9, waiting for transfers between devices, over_time(): return lax.ppermute(x, 'tm', [(t, t ^ k) for t in range(n_t)])  10.8 us
    pallas_call x12, Pallas kernels, call(): pl.pallas_call(kernel, out_shape=out_shape, in_specs=[pl.BlockSpec(memory...  8.98 us
    ppermute x6, starting transfers between devices, over_chips(): lax.ppermute(x, 'space', [(s, s ^ 2 * k) for s in range(n_s)])  7.67 us
    ppermute x6, waiting for transfers between devices, over_chips(): lax.ppermute(x, 'space', [(s, s ^ 2 * k) for s in range(n_s)])  2.45 us
  transfers between devices with their start and end apart: 18, of which 9 were waited for; matrix products, arithmetic and copies ran while one was open for 0% of the time, Pallas kernels for 14%

profile of v14, /device:TPU:0, one launch (start us, length us, event | category | flops | bytes accessed | tf_op | source)
XLA Modules:
  0.0 47.4 jit_solution(6341086932753911170)
XLA Ops:
  0.7 0.8 %copy-done.4 = bf16[128,128]{1,0:T(8,128)(2,1)S(1)} copy-done((bf16[128,128]{1,0:T(8,128)(2,1)S(1)}, bf16[128,128]{1,0:T(8,128)(2,1)}, u32[]{:S(2)}) %copy-start.4) | copy-done | bytes 32792
  1.5 1.5 %shard_map.128 = (bf16[4,128,640]{2,1,0:T(8,128)(2,1)S(1)}, bf16[128,2688]{1,0:T(8,128)(2,1)S(1)}) custom-call(bf16[128,5120]{1,0:T(8,128)(2,1)} %weight_in.1, bf16[128,128]{1,0:T(8,128)(2,1)S(1)} %copy-done.4), custom_call_target="tpu_custom_call" | custom-call | bytes 1343488 | tf_op jit(solution)/shard_map/pallas_call | solution.py:349
  3.5 2.6 %collective-permute-start.1 = (bf16[128,640]{1,0:T(8,128)(2,1)S(1)}, bf16[128,640]{1,0:T(8,128)(2,1)S(1)}, u32[]{:S(2)}, u32[]{:S(2)}) collective-permute-start(bf16[128,640]{1,0:T(8,128)(2,1)S(1)} %copy-done.1), channel_id=1, source_target_pairs={{0,2},{1,3},{2,0},{3,1},{4,6},{5,7},{6,4},{7,5},{8,10},{9,11},{10,... | collective-permute-start | bytes 491528 | tf_op jit(solution)/shard_map/ppermute | solution.py:394
  6.1 1.5 %collective-permute-start.2 = (bf16[128,640]{1,0:T(8,128)(2,1)S(1)}, bf16[128,640]{1,0:T(8,128)(2,1)S(1)}, u32[]{:S(2)}, u32[]{:S(2)}) collective-permute-start(bf16[128,640]{1,0:T(8,128)(2,1)S(1)} %copy-done.1), channel_id=1, source_target_pairs={{0,4},{1,5},{2,6},{3,7},{4,0},{5,1},{6,2},{7,3},{8,12},{9,13},{10,... | collective-permute-start | bytes 491528 | tf_op jit(solution)/shard_map/ppermute | solution.py:394
  7.7 3.1 %collective-permute-start.6 = (bf16[2,128,128]{2,1,0:T(8,128)(2,1)S(1)}, bf16[2,128,128]{2,1,0:T(8,128)(2,1)S(1)}, u32[]{:S(2)}, u32[]{:S(2)}) collective-permute-start(bf16[2,128,128]{2,1,0:T(8,128)(2,1)S(1)} %pad_maximum_fusion.packed.refs_0_), channel_id=1, source_target_pairs={{0,16},{8,24},{16,0},{24,8},{1,17},{9,25},{17,1},{25,9},{2,18},{10... | collective-permute-start | bytes 196616 | tf_op jit(solution)/shard_map/ppermute | solution.py:401
  10.8 1.6 %collective-permute-start.5 = (bf16[2,128,128]{2,1,0:T(8,128)(2,1)S(1)}, bf16[2,128,128]{2,1,0:T(8,128)(2,1)S(1)}, u32[]{:S(2)}, u32[]{:S(2)}) collective-permute-start(bf16[2,128,128]{2,1,0:T(8,128)(2,1)S(1)} %pad_maximum_fusion.packed.refs_0_), channel_id=1, source_target_pairs={{0,8},{8,0},{16,24},{24,16},{1,9},{9,1},{17,25},{25,17},{2,10},{10... | collective-permute-start | bytes 196616 | tf_op jit(solution)/shard_map/ppermute | solution.py:401
  13.0 0.8 %collective-permute-done.6.refs_2_ = bf16[2,128,128]{2,1,0:T(8,128)(2,1)S(1)} collective-permute-done((bf16[2,128,128]{2,1,0:T(8,128)(2,1)S(1)}, bf16[2,128,128]{2,1,0:T(8,128)(2,1)S(1)}, u32[]{:S(2)}, u32[]{:S(2)}) %collective-permute-start.6) | collective-permute-done | bytes 65568 | tf_op jit(solution)/shard_map/ppermute | solution.py:401
  13.8 1.2 %collective-permute-start.7 = (bf16[2,128,128]{2,1,0:T(8,128)(2,1)S(1)}, bf16[2,128,128]{2,1,0:T(8,128)(2,1)S(1)}, u32[]{:S(2)}, u32[]{:S(2)}) collective-permute-start(bf16[2,128,128]{2,1,0:T(8,128)(2,1)S(1)} %collective-permute-done.6.refs_2_), channel_id=1, source_target_pairs={{0,8},{8,0},{16,24},{24,16},{1,9},{9,1},{17,25},{25,17},{2,10},{10... | collective-permute-start | bytes 196616 | tf_op jit(solution)/shard_map/ppermute | solution.py:401
  15.0 0.9 %collective-permute-done.2.refs_2_ = bf16[128,640]{1,0:T(8,128)(2,1)S(1)} collective-permute-done((bf16[128,640]{1,0:T(8,128)(2,1)S(1)}, bf16[128,640]{1,0:T(8,128)(2,1)S(1)}, u32[]{:S(2)}, u32[]{:S(2)}) %collective-permute-start.2) | collective-permute-done | bytes 163872 | tf_op jit(solution)/shard_map/ppermute | solution.py:394
  16.7 1.3 %collective-permute-done.7.refs_3_ = bf16[2,128,128]{2,1,0:T(8,128)(2,1)S(1)} collective-permute-done((bf16[2,128,128]{2,1,0:T(8,128)(2,1)S(1)}, bf16[2,128,128]{2,1,0:T(8,128)(2,1)S(1)}, u32[]{:S(2)}, u32[]{:S(2)}) %collective-permute-start.7) | collective-permute-done | bytes 65568 | tf_op jit(solution)/shard_map/ppermute | solution.py:401
  19.0 3.9 %collective-permute-start.8 = (bf16[352,128]{1,0:T(8,128)(2,1)S(1)}, bf16[352,128]{1,0:T(8,128)(2,1)S(1)}, u32[]{:S(2)}, u32[]{:S(2)}) collective-permute-start(bf16[352,128]{1,0:T(8,128)(2,1)S(1)} %get-tuple-element.51), channel_id=1, source_target_pairs={{0,24},{8,16},{16,8},{24,0},{1,25},{9,17},{17,9},{25,1},{2,26},{10... | collective-permute-start | bytes 270344 | tf_op jit(solution)/shard_map/ppermute | solution.py:401
  23.5 2.7 %collective-permute-done.8.refs_1_.refs_4_ = bf16[352,128]{1,0:T(8,128)(2,1)S(1)} collective-permute-done((bf16[352,128]{1,0:T(8,128)(2,1)S(1)}, bf16[352,128]{1,0:T(8,128)(2,1)S(1)}, u32[]{:S(2)}, u32[]{:S(2)}) %collective-permute-start.8) | collective-permute-done | bytes 90144 | tf_op jit(solution)/shard_map/ppermute | solution.py:401
  26.2 3.5 %collective-permute-done.9.refs_2_.refs_5_ = bf16[352,128]{1,0:T(8,128)(2,1)S(1)} collective-permute-done((bf16[352,128]{1,0:T(8,128)(2,1)S(1)}, bf16[352,128]{1,0:T(8,128)(2,1)S(1)}, u32[]{:S(2)}, u32[]{:S(2)}) %collective-permute-start.9) | collective-permute-done | bytes 90144 | tf_op jit(solution)/shard_map/ppermute | solution.py:401
  29.7 1.3 %collective-permute-start.14 = (bf16[800,128]{1,0:T(8,128)(2,1)S(1)}, bf16[800,128]{1,0:T(8,128)(2,1)S(1)}, u32[]{:S(2)}, u32[]{:S(2)}) collective-permute-start(bf16[800,128]{1,0:T(8,128)(2,1)S(1)} %shard_map.133.refs_0_), channel_id=1, source_target_pairs={{0,2},{1,3},{2,0},{3,1},{4,6},{5,7},{6,4},{7,5},{8,10},{9,11},{10,... | collective-permute-start | bytes 614408 | tf_op jit(solution)/shard_map/ppermute | solution.py:394
  31.0 1.4 %collective-permute-start.15 = (bf16[800,128]{1,0:T(8,128)(2,1)S(1)}, bf16[800,128]{1,0:T(8,128)(2,1)S(1)}, u32[]{:S(2)}, u32[]{:S(2)}) collective-permute-start(bf16[800,128]{1,0:T(8,128)(2,1)S(1)} %shard_map.133.refs_0_), channel_id=1, source_target_pairs={{0,4},{1,5},{2,6},{3,7},{4,0},{5,1},{6,2},{7,3},{8,12},{9,13},{10,... | collective-permute-start | bytes 614408 | tf_op jit(solution)/shard_map/ppermute | solution.py:394
  32.4 0.9 %collective-permute-start.16 = (bf16[800,128]{1,0:T(8,128)(2,1)S(1)}, bf16[800,128]{1,0:T(8,128)(2,1)S(1)}, u32[]{:S(2)}, u32[]{:S(2)}) collective-permute-start(bf16[800,128]{1,0:T(8,128)(2,1)S(1)} %shard_map.133.refs_0_), channel_id=1, source_target_pairs={{0,6},{1,7},{2,4},{3,5},{4,2},{5,3},{6,0},{7,1},{8,14},{9,15},{10,... | collective-permute-start | bytes 614408 | tf_op jit(solution)/shard_map/ppermute | solution.py:394
  33.3 1.0 %shard_map.134 = (f32[1024,128]{1,0:T(8,128)S(1)}, f32[1024,128]{1,0:T(8,128)S(1)}, bf16[128,128]{1,0:T(8,128)(2,1)S(1)}, bf16[128,128]{1,0:T(8,128)(2,1)S(1)}) custom-call(f32[2,512]{1,0:T(2,128)S(1)} %get-tuple-element.54.bias, bf16[1024,128]{1,0:T(8,128)(2,1)S(1)} %copy-done, bf16[1024,128]{1,0:T(8,128)(2,1)S(1)} %copy-done.3, ...), custom_call_target="tpu_custom_call" | custom-call | flops 335544320 | bytes 1150976 | tf_op jit(solution)/shard_map/pallas_call | solution.py:349
  34.3 2.7 %collective-permute-start.11 = (bf16[128,128]{1,0:T(8,128)(2,1)S(1)}, bf16[128,128]{1,0:T(8,128)(2,1)S(1)}, u32[]{:S(2)}, u32[]{:S(2)}) collective-permute-start(bf16[128,128]{1,0:T(8,128)(2,1)S(1)} %get-tuple-element.55), channel_id=1, source_target_pairs={{0,24},{8,16},{16,8},{24,0},{1,25},{9,17},{17,9},{25,1},{2,26},{10... | collective-permute-start | bytes 98312 | tf_op jit(solution)/shard_map/ppermute | solution.py:401
  36.9 1.7 %shard_map.135 = (bf16[1024,128]{1,0:T(8,128)(2,1)}, bf16[1024,128]{1,0:T(8,128)(2,1)}, bf16[128,128]{1,0:T(8,128)(2,1)S(1)}, bf16[128,128]{1,0:T(8,128)(2,1)S(1)}) custom-call(f32[2,512]{1,0:T(2,128)S(1)} %get-tuple-element.54.bias, bf16[1024,128]{1,0:T(8,128)(2,1)S(1)} %copy-done, bf16[1024,128]{1,0:T(8,128)(2,1)S(1)} %copy-done.3, ...), custom_call_target="tpu_custom_call" | custom-call | flops 335544320 | bytes 2199552 | tf_op jit(solution)/shard_map/pallas_call | solution.py:349
  38.6 1.4 %collective-permute-done.11.refs_0_ = bf16[128,128]{1,0:T(8,128)(2,1)S(1)} collective-permute-done((bf16[128,128]{1,0:T(8,128)(2,1)S(1)}, bf16[128,128]{1,0:T(8,128)(2,1)S(1)}, u32[]{:S(2)}, u32[]{:S(2)}) %collective-permute-start.11) | collective-permute-done | bytes 32800 | tf_op jit(solution)/shard_map/ppermute | solution.py:401
  40.6 1.0 %collective-permute-done.16.refs_3_ = bf16[800,128]{1,0:T(8,128)(2,1)S(1)} collective-permute-done((bf16[800,128]{1,0:T(8,128)(2,1)S(1)}, bf16[800,128]{1,0:T(8,128)(2,1)S(1)}, u32[]{:S(2)}, u32[]{:S(2)}) %collective-permute-start.16) | collective-permute-done | bytes 204832 | tf_op jit(solution)/shard_map/ppermute | solution.py:394
  41.8 2.1 %collective-permute-start.13 = (bf16[128,128]{1,0:T(8,128)(2,1)S(1)}, bf16[128,128]{1,0:T(8,128)(2,1)S(1)}, u32[]{:S(2)}, u32[]{:S(2)}) collective-permute-start(bf16[128,128]{1,0:T(8,128)(2,1)S(1)} %get-tuple-element.59), channel_id=1, source_target_pairs={{0,8},{8,0},{16,24},{24,16},{1,9},{9,1},{17,25},{25,17},{2,10},{10... | collective-permute-start | bytes 98312 | tf_op jit(solution)/shard_map/ppermute | solution.py:401
  44.3 1.3 %shard_map.138 = (f32[128,1280]{1,0:T(8,128)}, f32[16,5120]{1,0:T(8,128)}) custom-call(f32[8,16,128]{2,1,0:T(8,128)S(1)} %get-tuple-element.61.hot, bf16[2880,128]{1,0:T(8,128)(2,1)S(1)} %collective-permute-done.17.other, f32[128,640]{1,0:T(8,128)S(1)} %get-tuple-element.67.own_weight, f32[16,2560]{1,0:T(8,128)S(1)} %get-tuple-element.68.own_gate, ...), custom_call_target="tpu_custom_call" | custom-call | flops 83886080 | bytes 1556480 | tf_op jit(solution)/shard_map/pallas_call | solution.py:349
  45.6 1.0 %collective-permute-done.12.refs_1_ = bf16[128,128]{1,0:T(8,128)(2,1)S(1)} collective-permute-done((bf16[128,128]{1,0:T(8,128)(2,1)S(1)}, bf16[128,128]{1,0:T(8,128)(2,1)S(1)}, u32[]{:S(2)}, u32[]{:S(2)}) %collective-permute-start.12) | collective-permute-done | bytes 32800 | tf_op jit(solution)/shard_map/ppermute | solution.py:401
  (41 shorter events, 5.6 us)
Async XLA Ops:
  0.6 11.7 %copy-start.2 = (f32[16,5120]{1,0:T(8,128)S(1)}, f32[16,5120]{1,0:T(8,128)}, u32[]{:S(2)}) copy-start(f32[16,5120]{1,0:T(8,128)} %gate) | copy-start | bytes 983044
  1.5 6.2 %copy-start.7 = (bf16[128,128]{1,0:T(8,128)(2,1)S(1)}, bf16[128,128]{1,0:T(8,128)(2,1)}, u32[]{:S(2)}) copy-start(bf16[128,128]{1,0:T(8,128)(2,1)} %param.9) | copy-start | bytes 98308
  1.5 10.9 %copy-start.5 = (s32[8]{0:T(128)S(1)}, s32[8]{0:T(128)}, u32[]{:S(2)}) copy-start(s32[8]{0:T(128)} %levels.1) | copy-start | bytes 100
  1.5 10.9 %copy-start.6 = (s32[4]{0:T(128)S(1)}, s32[4]{0:T(128)}, u32[]{:S(2)}) copy-start(s32[4]{0:T(128)} %clips.1) | copy-start | bytes 52
  3.0 15.1 %copy-start = (bf16[1024,128]{1,0:T(8,128)(2,1)S(1)}, bf16[1024,128]{1,0:T(8,128)(2,1)}, u32[]{:S(2)}) copy-start(bf16[1024,128]{1,0:T(8,128)(2,1)} %keys.5) | copy-start | bytes 786436
  3.0 4.7 %collective-permute-start = (bf16[128,2688]{1,0:T(8,128)(2,1)S(1)}, bf16[128,2688]{1,0:T(8,128)(2,1)S(1)}, u32[]{:S(2)}, u32[]{:S(2)}) collective-permute-start(bf16[128,2688]{1,0:T(8,128)(2,1)S(1)} %get-tuple-element.39), channel_id=1, source_target_pairs={{0,1},{1,0},{2,3},{3,2},{4,5},{5,4},{6,7},{7,6},{8,9},{9,8},{10,11... | collective-permute-start | bytes 2064392 | tf_op jit(solution)/shard_map/ppermute | solution.py:398
  3.5 11.4 %collective-permute-start.1 = (bf16[128,640]{1,0:T(8,128)(2,1)S(1)}, bf16[128,640]{1,0:T(8,128)(2,1)S(1)}, u32[]{:S(2)}, u32[]{:S(2)}) collective-permute-start(bf16[128,640]{1,0:T(8,128)(2,1)S(1)} %copy-done.1), channel_id=1, source_target_pairs={{0,2},{1,3},{2,0},{3,1},{4,6},{5,7},{6,4},{7,5},{8,10},{9,11},{10,... | collective-permute-start | bytes 491528 | tf_op jit(solution)/shard_map/ppermute | solution.py:394
  6.1 9.8 %collective-permute-start.2 = (bf16[128,640]{1,0:T(8,128)(2,1)S(1)}, bf16[128,640]{1,0:T(8,128)(2,1)S(1)}, u32[]{:S(2)}, u32[]{:S(2)}) collective-permute-start(bf16[128,640]{1,0:T(8,128)(2,1)S(1)} %copy-done.1), channel_id=1, source_target_pairs={{0,4},{1,5},{2,6},{3,7},{4,0},{5,1},{6,2},{7,3},{8,12},{9,13},{10,... | collective-permute-start | bytes 491528 | tf_op jit(solution)/shard_map/ppermute | solution.py:394
  7.6 8.3 %collective-permute-start.3 = (bf16[128,640]{1,0:T(8,128)(2,1)S(1)}, bf16[128,640]{1,0:T(8,128)(2,1)S(1)}, u32[]{:S(2)}, u32[]{:S(2)}) collective-permute-start(bf16[128,640]{1,0:T(8,128)(2,1)S(1)} %copy-done.1), channel_id=1, source_target_pairs={{0,6},{1,7},{2,4},{3,5},{4,2},{5,3},{6,0},{7,1},{8,14},{9,15},{10,... | collective-permute-start | bytes 491528 | tf_op jit(solution)/shard_map/ppermute | solution.py:394
  7.7 6.1 %collective-permute-start.6 = (bf16[2,128,128]{2,1,0:T(8,128)(2,1)S(1)}, bf16[2,128,128]{2,1,0:T(8,128)(2,1)S(1)}, u32[]{:S(2)}, u32[]{:S(2)}) collective-permute-start(bf16[2,128,128]{2,1,0:T(8,128)(2,1)S(1)} %pad_maximum_fusion.packed.refs_0_), channel_id=1, source_target_pairs={{0,16},{8,24},{16,0},{24,8},{1,17},{9,25},{17,1},{25,9},{2,18},{10... | collective-permute-start | bytes 196616 | tf_op jit(solution)/shard_map/ppermute | solution.py:401
  10.8 6.0 %collective-permute-start.5 = (bf16[2,128,128]{2,1,0:T(8,128)(2,1)S(1)}, bf16[2,128,128]{2,1,0:T(8,128)(2,1)S(1)}, u32[]{:S(2)}, u32[]{:S(2)}) collective-permute-start(bf16[2,128,128]{2,1,0:T(8,128)(2,1)S(1)} %pad_maximum_fusion.packed.refs_0_), channel_id=1, source_target_pairs={{0,8},{8,0},{16,24},{24,16},{1,9},{9,1},{17,25},{25,17},{2,10},{10... | collective-permute-start | bytes 196616 | tf_op jit(solution)/shard_map/ppermute | solution.py:401
  13.8 4.3 %collective-permute-start.7 = (bf16[2,128,128]{2,1,0:T(8,128)(2,1)S(1)}, bf16[2,128,128]{2,1,0:T(8,128)(2,1)S(1)}, u32[]{:S(2)}, u32[]{:S(2)}) collective-permute-start(bf16[2,128,128]{2,1,0:T(8,128)(2,1)S(1)} %collective-permute-done.6.refs_2_), channel_id=1, source_target_pairs={{0,8},{8,0},{16,24},{24,16},{1,9},{9,1},{17,25},{25,17},{2,10},{10... | collective-permute-start | bytes 196616 | tf_op jit(solution)/shard_map/ppermute | solution.py:401
  16.6 16.6 %copy-start.3 = (bf16[1024,128]{1,0:T(8,128)(2,1)S(1)}, bf16[1024,128]{1,0:T(8,128)(2,1)}, u32[]{:S(2)}) copy-start(bf16[1024,128]{1,0:T(8,128)(2,1)} %values.3) | copy-start | bytes 786436
  16.7 2.2 %collective-permute-start.4 = (f32[128,128]{1,0:T(8,128)S(1)}, f32[128,128]{1,0:T(8,128)S(1)}, u32[]{:S(2)}, u32[]{:S(2)}) collective-permute-start(f32[128,128]{1,0:T(8,128)S(1)} %get-tuple-element.47), channel_id=1, source_target_pairs={{0,1},{1,0},{2,3},{3,2},{4,5},{5,4},{6,7},{7,6},{8,9},{9,8},{10,11... | collective-permute-start | bytes 196616 | tf_op jit(solution)/shard_map/ppermute | solution.py:398
  19.0 7.2 %collective-permute-start.8 = (bf16[352,128]{1,0:T(8,128)(2,1)S(1)}, bf16[352,128]{1,0:T(8,128)(2,1)S(1)}, u32[]{:S(2)}, u32[]{:S(2)}) collective-permute-start(bf16[352,128]{1,0:T(8,128)(2,1)S(1)} %get-tuple-element.51), channel_id=1, source_target_pairs={{0,24},{8,16},{16,8},{24,0},{1,25},{9,17},{17,9},{25,1},{2,26},{10... | collective-permute-start | bytes 270344 | tf_op jit(solution)/shard_map/ppermute | solution.py:401
  22.9 6.8 %collective-permute-start.9 = (bf16[352,128]{1,0:T(8,128)(2,1)S(1)}, bf16[352,128]{1,0:T(8,128)(2,1)S(1)}, u32[]{:S(2)}, u32[]{:S(2)}) collective-permute-start(bf16[352,128]{1,0:T(8,128)(2,1)S(1)} %get-tuple-element.52), channel_id=1, source_target_pairs={{0,16},{8,24},{16,0},{24,8},{1,17},{9,25},{17,1},{25,9},{2,18},{10... | collective-permute-start | bytes 270344 | tf_op jit(solution)/shard_map/ppermute | solution.py:401
  22.9 6.8 %collective-permute-start.10 = (bf16[352,128]{1,0:T(8,128)(2,1)S(1)}, bf16[352,128]{1,0:T(8,128)(2,1)S(1)}, u32[]{:S(2)}, u32[]{:S(2)}) collective-permute-start(bf16[352,128]{1,0:T(8,128)(2,1)S(1)} %get-tuple-element.53), channel_id=1, source_target_pairs={{0,8},{8,0},{16,24},{24,16},{1,9},{9,1},{17,25},{25,17},{2,10},{10... | collective-permute-start | bytes 270344 | tf_op jit(solution)/shard_map/ppermute | solution.py:401
  29.7 10.3 %collective-permute-start.14 = (bf16[800,128]{1,0:T(8,128)(2,1)S(1)}, bf16[800,128]{1,0:T(8,128)(2,1)S(1)}, u32[]{:S(2)}, u32[]{:S(2)}) collective-permute-start(bf16[800,128]{1,0:T(8,128)(2,1)S(1)} %shard_map.133.refs_0_), channel_id=1, source_target_pairs={{0,2},{1,3},{2,0},{3,1},{4,6},{5,7},{6,4},{7,5},{8,10},{9,11},{10,... | collective-permute-start | bytes 614408 | tf_op jit(solution)/shard_map/ppermute | solution.py:394
  31.0 9.6 %collective-permute-start.15 = (bf16[800,128]{1,0:T(8,128)(2,1)S(1)}, bf16[800,128]{1,0:T(8,128)(2,1)S(1)}, u32[]{:S(2)}, u32[]{:S(2)}) collective-permute-start(bf16[800,128]{1,0:T(8,128)(2,1)S(1)} %shard_map.133.refs_0_), channel_id=1, source_target_pairs={{0,4},{1,5},{2,6},{3,7},{4,0},{5,1},{6,2},{7,3},{8,12},{9,13},{10,... | collective-permute-start | bytes 614408 | tf_op jit(solution)/shard_map/ppermute | solution.py:394
  32.4 9.2 %collective-permute-start.16 = (bf16[800,128]{1,0:T(8,128)(2,1)S(1)}, bf16[800,128]{1,0:T(8,128)(2,1)S(1)}, u32[]{:S(2)}, u32[]{:S(2)}) collective-permute-start(bf16[800,128]{1,0:T(8,128)(2,1)S(1)} %shard_map.133.refs_0_), channel_id=1, source_target_pairs={{0,6},{1,7},{2,4},{3,5},{4,2},{5,3},{6,0},{7,1},{8,14},{9,15},{10,... | collective-permute-start | bytes 614408 | tf_op jit(solution)/shard_map/ppermute | solution.py:394
  34.3 5.8 %collective-permute-start.11 = (bf16[128,128]{1,0:T(8,128)(2,1)S(1)}, bf16[128,128]{1,0:T(8,128)(2,1)S(1)}, u32[]{:S(2)}, u32[]{:S(2)}) collective-permute-start(bf16[128,128]{1,0:T(8,128)(2,1)S(1)} %get-tuple-element.55), channel_id=1, source_target_pairs={{0,24},{8,16},{16,8},{24,0},{1,25},{9,17},{17,9},{25,1},{2,26},{10... | collective-permute-start | bytes 98312 | tf_op jit(solution)/shard_map/ppermute | solution.py:401
  41.7 2.6 %collective-permute-start.17 = (bf16[2880,128]{1,0:T(8,128)(2,1)S(1)}, bf16[2880,128]{1,0:T(8,128)(2,1)S(1)}, u32[]{:S(2)}, u32[]{:S(2)}) collective-permute-start(bf16[2880,128]{1,0:T(8,128)(2,1)S(1)} %shard_map.136.own), channel_id=1, source_target_pairs={{0,1},{1,0},{2,3},{3,2},{4,5},{5,4},{6,7},{7,6},{8,9},{9,8},{10,11... | collective-permute-start | bytes 2211848 | tf_op jit(solution)/shard_map/ppermute | solution.py:398
  41.7 4.9 %collective-permute-start.12 = (bf16[128,128]{1,0:T(8,128)(2,1)S(1)}, bf16[128,128]{1,0:T(8,128)(2,1)S(1)}, u32[]{:S(2)}, u32[]{:S(2)}) collective-permute-start(bf16[128,128]{1,0:T(8,128)(2,1)S(1)} %get-tuple-element.56), channel_id=1, source_target_pairs={{0,16},{8,24},{16,0},{24,8},{1,17},{9,25},{17,1},{25,9},{2,18},{10... | collective-permute-start | bytes 98312 | tf_op jit(solution)/shard_map/ppermute | solution.py:401
  41.8 4.8 %collective-permute-start.13 = (bf16[128,128]{1,0:T(8,128)(2,1)S(1)}, bf16[128,128]{1,0:T(8,128)(2,1)S(1)}, u32[]{:S(2)}, u32[]{:S(2)}) collective-permute-start(bf16[128,128]{1,0:T(8,128)(2,1)S(1)} %get-tuple-element.59), channel_id=1, source_target_pairs={{0,8},{8,0},{16,24},{24,16},{1,9},{9,1},{17,25},{25,17},{2,10},{10... | collective-permute-start | bytes 98312 | tf_op jit(solution)/shard_map/ppermute | solution.py:401
  (2 other events, 3.7 us)

commit v15 on v14

--- a/solution.py
+++ b/solution.py
@@ -134,10 +134,10 @@
     other[...] = head[:, HD:]
 
 
-def sections(rows, chips, tiles, n_t, count):
+def sections(rows, chips, tiles, n_t):
     starts = [0, rows]
     starts.append(starts[-1] + tiles * (rows // chips))
-    starts.append(starts[-1] + -(-(SPLIT * 2 * n_t + count) // 16) * 16)
+    starts.append(starts[-1] + -(-SPLIT * 2 * n_t // 16) * 16)
     return starts
 
 
@@ -147,9 +147,13 @@
     return jnp.concatenate([x, jnp.zeros((rows - x.shape[0], x.shape[1]), x.dtype)], axis=0)
 
 
-def join_kernel(n_t, chips, starts, mine, received, stats, terms, *refs):
-    pieces, outs, (wide, held) = refs[:chips], refs[chips : chips + n_t][::-1], refs[chips + n_t :]
-    t, chip, _ = place()
+def join_kernel(n_t, chips, starts, mine, received, stats, own_terms, other_terms, *refs):
+    pieces, outs, (both, wide, held) = refs[:chips], refs[chips : chips + n_t][::-1], refs[chips + n_t :]
+    t, chip, core = place()
+    own, other = own_terms[...], other_terms[...]
+    count = own.shape[0]
+    both[:count, :] = jnp.where(core == 0, own, other)
+    both[count:, :] = jnp.where(core == 0, other, own)
     part, tiles = held.shape[1], held.shape[2] // LANES
     for k in range(chips):
         wide[...] = pieces[k][...].astype(jnp.float32)
@@ -161,7 +165,7 @@
         piece = rest.astype(jnp.bfloat16).astype(jnp.float32)
         split.append(piece)
         rest = rest - piece
-    last = padded(jnp.concatenate(split + [terms[...]], axis=0), starts[3] - starts[2])
+    last = padded(jnp.concatenate(split, axis=0), starts[3] - starts[2])
     last = last.astype(jnp.bfloat16)
     for k in range(n_t):
         rows = held[chip ^ t ^ k]
@@ -171,7 +175,7 @@
         outs[k][starts[2] :, :] = last
 
 
-def bundle_kernel(n_t, starts, count, gate_b, *refs):
+def bundle_kernel(n_t, starts, gate_b, *refs):
     heads, out = far_first(refs[:n_t]), refs[n_t]
     tiles = gate_b.shape[2] // LANES
     part = (starts[2] - starts[1]) // tiles
@@ -185,27 +189,15 @@
             axis=0,
         )
         out[j * n_t * part : (j + 1) * n_t * part, :] = gated.astype(jnp.bfloat16)
-    first = SPLIT * 2 * n_t
-    terms = [heads[k][starts[2] :, :].astype(jnp.float32)[first : first + count] for k in range(n_t)]
-    out[tiles * n_t * part :, :] = jnp.concatenate(terms, axis=0).astype(jnp.bfloat16)
-
-
-def collect_kernel(chips, base, *refs):
-    pieces, out, held = refs[:chips], refs[chips], refs[chips + 1]
-    chip = place()[1]
+
+
+def collect_kernel(chips, *refs):
+    base = refs[0].shape[0]
     for k in range(chips):
-        out[k * base : (k + 1) * base, :] = pieces[k][:base, :]
-        held[chip ^ k] = pieces[k][base:, :].astype(jnp.float32)
-    total = held[0]
-    for k in range(1, chips):
-        total = total + held[k]
-    high = total.astype(jnp.bfloat16)
-    count = total.shape[0]
-    out[chips * base : chips * base + count, :] = high
-    out[chips * base + count :, :] = (total - high.astype(jnp.float32)).astype(jnp.bfloat16)
-
-
-def grads_kernel(n_t, starts, first, last, bias, keys, values, *refs):
+        refs[chips][k * base : (k + 1) * base, :] = refs[k][...]
+
+
+def grads_kernel(n_t, starts, first, last, bias, keys, values, terms, *refs):
     packed, heads = refs[:n_t], refs[n_t : 2 * n_t][::-1]
     refs = refs[2 * n_t :]
     if first == 0:
@@ -220,6 +212,8 @@
     for k in range(n_t):
         parts = heads[k][starts[2] :, :].astype(jnp.float32)
         stats.append(sum(parts[i * 2 * n_t : (i + 1) * 2 * n_t] for i in range(SPLIT)))
+    for out in outs:
+        out[rows:, :] = terms[...].astype(jnp.bfloat16)
     for p in range(first, last, 2):
         q = jnp.concatenate([packed[p][0], packed[p + 1][0]], axis=0)
         o = jnp.concatenate([packed[p][1], packed[p + 1][1]], axis=0)
@@ -260,19 +254,34 @@
                 key_out[span, :] = ((key_add + sums[0][span, :]) * SCALE).astype(jnp.bfloat16)
             part = dot(keys_t[:, span], score_grad, 1, 0)
             query_part = part if query_part is None else query_part + part
-        outs[p - first][...] = query_part[:, :rows].astype(jnp.bfloat16)
-        outs[p + 1 - first][...] = query_part[:, rows:].astype(jnp.bfloat16)
-
-
-def query_kernel(n_t, *refs):
-    total = refs[0][...].astype(jnp.float32)
+        outs[p - first][:rows, :] = query_part[:, :rows].astype(jnp.bfloat16)
+        outs[p + 1 - first][:rows, :] = query_part[:, rows:].astype(jnp.bfloat16)
+
+
+def finish_kernel(n_t, chips, frames, hot, *refs):
+    parts, (query_out, gate_out, held) = refs[:n_t][::-1], refs[n_t:]
+    t = lax.axis_index("tm")
+    rows = query_out.shape[0]
+    total = parts[0][:rows, :].astype(jnp.float32)
     for k in range(1, n_t):
-        total = total + refs[k][...].astype(jnp.float32)
-    refs[n_t][...] = jnp.transpose(total * SCALE).astype(jnp.bfloat16)
-
-
-def half_results(n_t, chips, frames, hot, ref, packed, saved, held, tiles):
-    t, chip, _ = place()
+        total = total + parts[k][:rows, :].astype(jnp.float32)
+    query_out[...] = jnp.transpose(total * SCALE).astype(jnp.bfloat16)
+    for k in range(n_t):
+        held[t ^ k] = parts[k][rows:, :].astype(jnp.float32)
+    tiles = gate_out.shape[1] // (2 * chips * LANES)
+    for core in range(2):
+        for a in range(chips):
+            for j in range(tiles):
+                total = jnp.zeros(hot.shape[1:], jnp.float32)
+                for f in range(n_t * frames):
+                    row = ((core * chips + a) * frames + f % frames) * tiles + j
+                    total = total + hot[f] * held[f // frames, row : row + 1, :]
+                column = ((2 * a + core) * tiles + j) * LANES
+                gate_out[:, column : column + LANES] = total
+
+
+def half_result(n_t, chips, ref, packed, saved, tiles):
+    _, chip, _ = place()
     rows = saved.shape[1]
     part = rows // chips
     base = tiles * n_t * part
@@ -296,50 +305,22 @@
         ],
         axis=1,
     )
-    count = (ref.shape[0] - chips * base) // 2
-    each = count // n_t
-    terms = ref[chips * base : chips * base + count, :].astype(jnp.float32)
-    terms = terms + ref[chips * base + count :, :].astype(jnp.float32)
-    for k in range(n_t):
-        held[t ^ k] = terms[k * each : (k + 1) * each]
-
-    def gate_tile(a, j):
-        total = jnp.zeros(hot.shape[1:], jnp.float32)
-        for f in range(n_t * frames):
-            row = (a * frames + f % frames) * tiles + j
-            total = total + hot[f] * held[f // frames, row : row + 1, :]
-        return total
-
-    return dot(ordered, gated, 1, 0), gate_tile
-
-
-def own_kernel(n_t, chips, frames, hot, own, *refs):
-    packed, (weight_out, gate_out, saved, held) = refs[:n_t], refs[n_t:]
-    tiles = weight_out.shape[1] // LANES
-    result, gate_tile = half_results(n_t, chips, frames, hot, own, packed, saved, held, tiles)
-    weight_out[...] = result
-    for a in range(chips):
-        for j in range(tiles):
-            gate_out[:, (a * tiles + j) * LANES : (a * tiles + j + 1) * LANES] = gate_tile(a, j)
-
-
-def final_kernel(n_t, chips, frames, hot, other, own_weight, own_gate, *refs):
-    packed, (weight_out, gate_out, saved, held) = refs[:n_t], refs[n_t:]
+    return dot(ordered, gated, 1, 0)
+
+
+def own_kernel(n_t, chips, own, *refs):
+    packed, (weight_out, saved) = refs[:n_t], refs[n_t:]
+    weight_out[...] = half_result(n_t, chips, own, packed, saved, weight_out.shape[1] // LANES)
+
+
+def final_kernel(n_t, chips, other, own_weight, *refs):
+    packed, (weight_out, saved) = refs[:n_t], refs[n_t:]
     core = place()[2]
     width = own_weight.shape[1]
-    tiles = width // LANES
-    result, gate_tile = half_results(n_t, chips, frames, hot, other, packed, saved, held, tiles)
+    result = half_result(n_t, chips, other, packed, saved, width // LANES)
     mine = own_weight[...]
     weight_out[:, :width] = jnp.where(core == 0, mine, result)
     weight_out[:, width:] = jnp.where(core == 0, result, mine)
-    for a in range(chips):
-        for j in range(tiles):
-            first = gate_tile(a, j)
-            second = own_gate[:, (a * tiles + j) * LANES : (a * tiles + j + 1) * LANES]
-            column = 2 * a * width + j * LANES
-            gate_out[:, column : column + LANES] = jnp.where(core == 0, second, first)
-            column += width
-            gate_out[:, column : column + LANES] = jnp.where(core == 0, first, second)
 
 
 def call(kernel, args, out_shape, scratch=(), flops=0, in_place=False, in_smem=0):
@@ -389,10 +370,11 @@
     def shape(dtype, *dims):
         return jax.ShapeDtypeStruct(dims, dtype)
 
+    def over_chip(x, k):
+        return lax.ppermute(x, "space", [(s, s ^ (2 * k)) for s in range(n_s)])
+
     def over_chips(x):
-        return [x] + [
-            lax.ppermute(x, "space", [(s, s ^ (2 * k)) for s in range(n_s)]) for k in range(1, chips)
-        ]
+        return [x] + [over_chip(x, k) for k in range(1, chips)]
 
     def over_cores(x):
         return lax.ppermute(x, "space", [(s, s ^ 1) for s in range(n_s)])
@@ -403,7 +385,7 @@
     tiles = width // LANES
     part = rows // chips
     count = chips * frames * tiles
-    starts = sections(rows, chips, tiles, n_t, count)
+    starts = sections(rows, chips, tiles, n_t)
 
     def time_swaps(messages):
         got = {k: over_time(messages[k], k) for k in range(n_t - 1, 0, -1)}
@@ -435,7 +417,7 @@
         ],
         in_smem=2,
     )
-    mine, other, terms = call(
+    mine, other, own_terms = call(
         functools.partial(head_kernel, chips, frames),
         [packed, kept, received, gate_a] + pieces,
         [shape(f32, rows, HD), shape(f32, rows, HD), shape(f32, count, LANES)],
@@ -448,63 +430,71 @@
         shape(f32, 2 * n_t, LANES),
         flops=2 * n_t * rows * k_rows * HD,
     )
-    heads = call(
+    *heads, terms = call(
         functools.partial(join_kernel, n_t, chips, starts),
-        [mine, over_cores(other), stats, terms] + pieces,
-        [shape(bf16, starts[-1], LANES)] * n_t,
+        [mine, over_cores(other), stats, own_terms, over_cores(own_terms)] + pieces,
+        [shape(bf16, starts[-1], LANES)] * n_t + [shape(f32, 2 * count, LANES)],
         [pltpu.VMEM((rows, width), f32), pltpu.VMEM((chips, part, width), f32)],
     )
     heads_all = time_swaps(heads[::-1])
+    step = 1
+    while step < chips:
+        terms = terms + over_chip(terms, step)
+        step *= 2
     base = tiles * n_t * part
+    gate_b, _ = lax.optimization_barrier((gate_b, terms))
     bundle = call(
-        functools.partial(bundle_kernel, n_t, starts, count),
+        functools.partial(bundle_kernel, n_t, starts),
         [gate_b] + far_first(heads_all),
-        shape(bf16, base + n_t * count, LANES),
+        shape(bf16, base, LANES),
     )
     bundles = over_chips(bundle)
     later_bias, _ = lax.optimization_barrier((bias, bundle))
     accs = [pltpu.VMEM((k_rows, HD), f32)] * 2
+    message = shape(bf16, HD + 2 * count, rows)
     far = call(
         functools.partial(grads_kernel, n_t, starts, 2, n_t),
-        [later_bias, keys, values] + packed_all + heads_all[::-1],
-        [shape(f32, k_rows, HD)] * 2 + [shape(bf16, HD, rows)] * (n_t - 2),
+        [later_bias, keys, values, terms] + packed_all + heads_all[::-1],
+        [shape(f32, k_rows, HD)] * 2 + [message] * (n_t - 2),
         accs,
         flops=10 * (n_t - 2) * rows * k_rows * HD,
     )
     parts = {k: over_time(far[1 + n_t - k], k) for k in range(n_t - 1, 1, -1)}
     near = call(
         functools.partial(grads_kernel, n_t, starts, 0, 2),
-        [bias, keys, values] + packed_all + heads_all[::-1] + list(far[:2]),
-        [shape(bf16, k_rows, HD)] * 2 + [shape(bf16, HD, rows)] * 2,
+        [bias, keys, values, terms] + packed_all + heads_all[::-1] + list(far[:2]),
+        [shape(bf16, k_rows, HD)] * 2 + [message] * 2,
         flops=20 * rows * k_rows * HD,
     )
     key_grad, value_grad = near[:2]
     parts[0], parts[1] = near[3], over_time(near[2], 1)
     parts = [parts[k] for k in range(n_t)]
-    bundles, _ = lax.optimization_barrier((bundles, (key_grad, parts[n_t - 1])))
+    bundles, _ = lax.optimization_barrier((bundles, (key_grad, parts[: n_t // 2 - 1 : -1])))
     collected = call(
-        functools.partial(collect_kernel, chips, base),
-        bundles,
-        shape(bf16, chips * base + 2 * n_t * count, LANES),
-        [pltpu.VMEM((chips, n_t * count, LANES), f32)],
-    )
-    scratch = [pltpu.VMEM((n_t, rows, HD), f32), pltpu.VMEM((n_t, count, LANES), f32)]
-    own_halves = call(
-        functools.partial(own_kernel, n_t, chips, frames),
-        [hot, collected] + packed_all,
-        [shape(f32, HD, width), shape(f32, levels, chips * width)],
+        functools.partial(collect_kernel, chips), bundles, shape(bf16, chips * base, LANES)
+    )
+    scratch = [pltpu.VMEM((n_t, rows, HD), f32)]
+    own_half = call(
+        functools.partial(own_kernel, n_t, chips),
+        [collected] + packed_all,
+        shape(f32, HD, width),
         scratch,
         flops=2 * n_t * rows * width * HD,
     )
-    weight_grad, gate_grad = call(
-        functools.partial(final_kernel, n_t, chips, frames),
-        [hot, over_cores(collected), *own_halves] + packed_all,
-        [shape(f32, HD, 2 * width), shape(f32, levels, n_s * width)],
+    weight_grad = call(
+        functools.partial(final_kernel, n_t, chips),
+        [over_cores(collected), own_half] + packed_all,
+        shape(f32, HD, 2 * width),
         scratch,
         flops=2 * n_t * rows * width * HD,
     )
-    parts[0], _ = lax.optimization_barrier((parts[0], gate_grad))
-    query_grad = call(functools.partial(query_kernel, n_t), parts[::-1], shape(bf16, rows, HD))
+    hot, _ = lax.optimization_barrier((hot, weight_grad))
+    query_grad, gate_grad = call(
+        functools.partial(finish_kernel, n_t, chips, frames),
+        [hot] + parts[::-1],
+        [shape(bf16, rows, HD), shape(f32, levels, n_s * width)],
+        [pltpu.VMEM((n_t, 2 * count, LANES), f32)],
+    )
     if width != shard:
         weight_grad = without_padding(weight_grad, 2, shard)
         gate_grad = without_padding(gate_grad, n_s, shard)

time: 47.5 us -> 48 us (1.011)
  starting transfers between devices: 23.5 us -> 25 us
  waiting for transfers between devices: 13.3 us -> 12.3 us
    ppermute x9, waiting for transfers between devices: 10.8 us -> 7.21 us  [over_time(): return lax.ppermute(x, 'tm', [(t, t ^ k) for t in range(n_t)])]
    ppermute x6 -> x8, starting transfers between devices: 7.67 us -> 10.8 us  [over_chip(): return lax.ppermute(x, 'space', [(s, s ^ 2 * k) for s in range(n_s)])]
    ppermute x9, starting transfers between devices: 15.2 us -> 13 us  [over_time(): return lax.ppermute(x, 'tm', [(t, t ^ k) for t in range(n_t)])]
    ppermute x3 -> x4, waiting for transfers between devices: 0.01 us -> 1.68 us  [over_cores(): return lax.ppermute(x, 'space', [(s, s ^ 1) for s in range(n_s)])]
    ppermute x6 -> x8, waiting for transfers between devices: 2.45 us -> 3.41 us  [over_chip(): return lax.ppermute(x, 'space', [(s, s ^ 2 * k) for s in range(n_s)])]
    ppermute x3 -> x4, starting transfers between devices: 0.66 us -> 1.16 us  [over_cores(): return lax.ppermute(x, 'space', [(s, s ^ 1) for s in range(n_s)])]
  transfers between devices with their start and end apart: 18 -> 21, of which waited for: 9 -> 9; matrix products, arithmetic and copies ran while one was open for 0% -> 0% of each run, Pallas kernels for 14% -> 13%
where the time goes in v15:
time: 48 us; the launch traced here: 47.9 us
  starting transfers between devices  25 us (52%)
  waiting for transfers between devices  12.3 us (26%)
  Pallas kernels  8.94 us (19%)
  local copies, waits for them, and re-layouts  0.84 us (2%)
  between operations  0.81 us (2%)
    ppermute x9, starting transfers between devices, over_time(): return lax.ppermute(x, 'tm', [(t, t ^ k) for t in range(n_t)])  13 us
    ppermute x8, starting transfers between devices, over_chip(): return lax.ppermute(x, 'space', [(s, s ^ 2 * k) for s in range(n_s)])  10.8 us
    pallas_call x12, Pallas kernels, call(): pl.pallas_call(kernel, out_shape=out_shape, in_specs=[pl.BlockSpec(memory...  8.94 us
    ppermute x9, waiting for transfers between devices, over_time(): return lax.ppermute(x, 'tm', [(t, t ^ k) for t in range(n_t)])  7.21 us
    ppermute x8, waiting for transfers between devices, over_chip(): return lax.ppermute(x, 'space', [(s, s ^ 2 * k) for s in range(n_s)])  3.41 us
    ppermute x4, waiting for transfers between devices, over_cores(): return lax.ppermute(x, 'space', [(s, s ^ 1) for s in range(n_s)])  1.68 us
    ppermute x4, starting transfers between devices, over_cores(): return lax.ppermute(x, 'space', [(s, s ^ 1) for s in range(n_s)])  1.16 us
  transfers between devices with their start and end apart: 21, of which 9 were waited for; matrix products, arithmetic and copies ran while one was open for 0% of the time, Pallas kernels for 13%

profile of v15, /device:TPU:0, one launch (start us, length us, event | category | flops | bytes accessed | tf_op | source)
XLA Modules:
  0.0 47.9 jit_solution(17706491409741608143)
XLA Ops:
  1.5 1.5 %shard_map.128 = (bf16[4,128,640]{2,1,0:T(8,128)(2,1)S(1)}, bf16[128,2688]{1,0:T(8,128)(2,1)S(1)}) custom-call(bf16[128,5120]{1,0:T(8,128)(2,1)} %weight_in.1, bf16[128,128]{1,0:T(8,128)(2,1)S(1)} %copy-done.4), custom_call_target="tpu_custom_call" | custom-call | bytes 1343488 | tf_op jit(solution)/shard_map/pallas_call | solution.py:330
  3.5 2.6 %collective-permute-start.1 = (bf16[128,640]{1,0:T(8,128)(2,1)S(1)}, bf16[128,640]{1,0:T(8,128)(2,1)S(1)}, u32[]{:S(2)}, u32[]{:S(2)}) collective-permute-start(bf16[128,640]{1,0:T(8,128)(2,1)S(1)} %copy-done.1), channel_id=1, source_target_pairs={{0,2},{1,3},{2,0},{3,1},{4,6},{5,7},{6,4},{7,5},{8,10},{9,11},{10,... | collective-permute-start | bytes 491528 | tf_op jit(solution)/shard_map/ppermute | solution.py:374
  6.1 1.5 %collective-permute-start.2 = (bf16[128,640]{1,0:T(8,128)(2,1)S(1)}, bf16[128,640]{1,0:T(8,128)(2,1)S(1)}, u32[]{:S(2)}, u32[]{:S(2)}) collective-permute-start(bf16[128,640]{1,0:T(8,128)(2,1)S(1)} %copy-done.1), channel_id=1, source_target_pairs={{0,4},{1,5},{2,6},{3,7},{4,0},{5,1},{6,2},{7,3},{8,12},{9,13},{10,... | collective-permute-start | bytes 491528 | tf_op jit(solution)/shard_map/ppermute | solution.py:374
  7.7 3.1 %collective-permute-start.6 = (bf16[2,128,128]{2,1,0:T(8,128)(2,1)S(1)}, bf16[2,128,128]{2,1,0:T(8,128)(2,1)S(1)}, u32[]{:S(2)}, u32[]{:S(2)}) collective-permute-start(bf16[2,128,128]{2,1,0:T(8,128)(2,1)S(1)} %pad_maximum_fusion.packed.refs_0_), channel_id=1, source_target_pairs={{0,16},{8,24},{16,0},{24,8},{1,17},{9,25},{17,1},{25,9},{2,18},{10... | collective-permute-start | bytes 196616 | tf_op jit(solution)/shard_map/ppermute | solution.py:383
  10.8 1.6 %collective-permute-start.5 = (bf16[2,128,128]{2,1,0:T(8,128)(2,1)S(1)}, bf16[2,128,128]{2,1,0:T(8,128)(2,1)S(1)}, u32[]{:S(2)}, u32[]{:S(2)}) collective-permute-start(bf16[2,128,128]{2,1,0:T(8,128)(2,1)S(1)} %pad_maximum_fusion.packed.refs_0_), channel_id=1, source_target_pairs={{0,8},{8,0},{16,24},{24,16},{1,9},{9,1},{17,25},{25,17},{2,10},{10... | collective-permute-start | bytes 196616 | tf_op jit(solution)/shard_map/ppermute | solution.py:383
  13.8 1.2 %collective-permute-start.7 = (bf16[2,128,128]{2,1,0:T(8,128)(2,1)S(1)}, bf16[2,128,128]{2,1,0:T(8,128)(2,1)S(1)}, u32[]{:S(2)}, u32[]{:S(2)}) collective-permute-start(bf16[2,128,128]{2,1,0:T(8,128)(2,1)S(1)} %collective-permute-done.6.refs_2_), channel_id=1, source_target_pairs={{0,8},{8,0},{16,24},{24,16},{1,9},{9,1},{17,25},{25,17},{2,10},{10... | collective-permute-start | bytes 196616 | tf_op jit(solution)/shard_map/ppermute | solution.py:383
  15.0 0.9 %collective-permute-done.2.refs_2_ = bf16[128,640]{1,0:T(8,128)(2,1)S(1)} collective-permute-done((bf16[128,640]{1,0:T(8,128)(2,1)S(1)}, bf16[128,640]{1,0:T(8,128)(2,1)S(1)}, u32[]{:S(2)}, u32[]{:S(2)}) %collective-permute-start.2) | collective-permute-done | bytes 163872 | tf_op jit(solution)/shard_map/ppermute | solution.py:374
  19.0 1.6 %collective-permute-start.9 = (f32[80,128]{1,0:T(8,128)S(1)}, f32[80,128]{1,0:T(8,128)S(1)}, u32[]{:S(2)}, u32[]{:S(2)}) collective-permute-start(f32[80,128]{1,0:T(8,128)S(1)} %get-tuple-element.51), channel_id=1, source_target_pairs={{0,2},{1,3},{2,0},{3,1},{4,6},{5,7},{6,4},{7,5},{8,10},{9,11},{10,... | collective-permute-start | bytes 122888 | tf_op jit(solution)/shard_map/ppermute | solution.py:374
  20.6 3.8 %collective-permute-start.11 = (bf16[320,128]{1,0:T(8,128)(2,1)S(1)}, bf16[320,128]{1,0:T(8,128)(2,1)S(1)}, u32[]{:S(2)}, u32[]{:S(2)}) collective-permute-start(bf16[320,128]{1,0:T(8,128)(2,1)S(1)} %get-tuple-element.54), channel_id=1, source_target_pairs={{0,24},{8,16},{16,8},{24,0},{1,25},{9,17},{17,9},{25,1},{2,26},{10... | collective-permute-start | bytes 245768 | tf_op jit(solution)/shard_map/ppermute | solution.py:383
  25.0 1.6 %collective-permute-start.10 = (f32[80,128]{1,0:T(8,128)S(1)}, f32[80,128]{1,0:T(8,128)S(1)}, u32[]{:S(2)}, u32[]{:S(2)}) collective-permute-start(f32[80,128]{1,0:T(8,128)S(1)} %add.6), channel_id=1, source_target_pairs={{0,4},{1,5},{2,6},{3,7},{4,0},{5,1},{6,2},{7,3},{8,12},{9,13},{10,... | collective-permute-start | bytes 122888 | tf_op jit(solution)/shard_map/ppermute | solution.py:374
  26.6 2.5 %collective-permute-done.10 = f32[80,128]{1,0:T(8,128)S(1)} collective-permute-done((f32[80,128]{1,0:T(8,128)S(1)}, f32[80,128]{1,0:T(8,128)S(1)}, u32[]{:S(2)}, u32[]{:S(2)}) %collective-permute-start.10) | collective-permute-done | bytes 40992 | tf_op jit(solution)/shard_map/ppermute | solution.py:374
  29.1 1.2 %collective-permute-done.12.refs_2_.refs_5_ = bf16[320,128]{1,0:T(8,128)(2,1)S(1)} collective-permute-done((bf16[320,128]{1,0:T(8,128)(2,1)S(1)}, bf16[320,128]{1,0:T(8,128)(2,1)S(1)}, u32[]{:S(2)}, u32[]{:S(2)}) %collective-permute-start.12) | collective-permute-done | bytes 81952 | tf_op jit(solution)/shard_map/ppermute | solution.py:383
  30.3 0.8 %collective-permute-start.14 = (bf16[640,128]{1,0:T(8,128)(2,1)S(1)}, bf16[640,128]{1,0:T(8,128)(2,1)S(1)}, u32[]{:S(2)}, u32[]{:S(2)}) collective-permute-start(bf16[640,128]{1,0:T(8,128)(2,1)S(1)} %shard_map.133.refs_0_), channel_id=1, source_target_pairs={{0,2},{1,3},{2,0},{3,1},{4,6},{5,7},{6,4},{7,5},{8,10},{9,11},{10,... | collective-permute-start | bytes 491528 | tf_op jit(solution)/shard_map/ppermute | solution.py:374
  31.1 1.5 %collective-permute-start.15 = (bf16[640,128]{1,0:T(8,128)(2,1)S(1)}, bf16[640,128]{1,0:T(8,128)(2,1)S(1)}, u32[]{:S(2)}, u32[]{:S(2)}) collective-permute-start(bf16[640,128]{1,0:T(8,128)(2,1)S(1)} %shard_map.133.refs_0_), channel_id=1, source_target_pairs={{0,4},{1,5},{2,6},{3,7},{4,0},{5,1},{6,2},{7,3},{8,12},{9,13},{10,... | collective-permute-start | bytes 491528 | tf_op jit(solution)/shard_map/ppermute | solution.py:374
  32.6 1.2 %collective-permute-start.16 = (bf16[640,128]{1,0:T(8,128)(2,1)S(1)}, bf16[640,128]{1,0:T(8,128)(2,1)S(1)}, u32[]{:S(2)}, u32[]{:S(2)}) collective-permute-start(bf16[640,128]{1,0:T(8,128)(2,1)S(1)} %shard_map.133.refs_0_), channel_id=1, source_target_pairs={{0,6},{1,7},{2,4},{3,5},{4,2},{5,3},{6,0},{7,1},{8,14},{9,15},{10,... | collective-permute-start | bytes 491528 | tf_op jit(solution)/shard_map/ppermute | solution.py:374
  33.8 1.0 %shard_map.134 = (f32[1024,128]{1,0:T(8,128)S(1)}, f32[1024,128]{1,0:T(8,128)S(1)}, bf16[208,128]{1,0:T(8,128)(2,1)S(1)}, bf16[208,128]{1,0:T(8,128)(2,1)S(1)}) custom-call(f32[2,512]{1,0:T(2,128)S(1)} %get-tuple-element.57.bias, bf16[1024,128]{1,0:T(8,128)(2,1)S(1)} %copy-done, bf16[1024,128]{1,0:T(8,128)(2,1)S(1)} %copy-done.3, f32[80,128]{1,0:T(8,128)S(1)} %add.7.terms, ...), custom_call_target="tpu_custom_call" | custom-call | flops 335544320 | bytes 1159168 | tf_op jit(solution)/shard_map/pallas_call | solution.py:330
  34.8 2.7 %collective-permute-start.17 = (bf16[208,128]{1,0:T(8,128)(2,1)S(1)}, bf16[208,128]{1,0:T(8,128)(2,1)S(1)}, u32[]{:S(2)}, u32[]{:S(2)}) collective-permute-start(bf16[208,128]{1,0:T(8,128)(2,1)S(1)} %get-tuple-element.61), channel_id=1, source_target_pairs={{0,24},{8,16},{16,8},{24,0},{1,25},{9,17},{17,9},{25,1},{2,26},{10... | collective-permute-start | bytes 159752 | tf_op jit(solution)/shard_map/ppermute | solution.py:383
  37.5 1.6 %shard_map.135 = (bf16[1024,128]{1,0:T(8,128)(2,1)}, bf16[1024,128]{1,0:T(8,128)(2,1)}, bf16[208,128]{1,0:T(8,128)(2,1)S(1)}, bf16[208,128]{1,0:T(8,128)(2,1)S(1)}) custom-call(f32[2,512]{1,0:T(2,128)S(1)} %get-tuple-element.57.bias, bf16[1024,128]{1,0:T(8,128)(2,1)S(1)} %copy-done, bf16[1024,128]{1,0:T(8,128)(2,1)S(1)} %copy-done.3, ...), custom_call_target="tpu_custom_call" | custom-call | flops 335544320 | bytes 2207744 | tf_op jit(solution)/shard_map/pallas_call | solution.py:330
  39.1 1.7 %collective-permute-done.17.refs_0_ = bf16[208,128]{1,0:T(8,128)(2,1)S(1)} collective-permute-done((bf16[208,128]{1,0:T(8,128)(2,1)S(1)}, bf16[208,128]{1,0:T(8,128)(2,1)S(1)}, u32[]{:S(2)}, u32[]{:S(2)}) %collective-permute-start.17) | collective-permute-done | bytes 53280 | tf_op jit(solution)/shard_map/ppermute | solution.py:383
  40.8 1.7 %collective-permute-done.18.refs_1_ = bf16[208,128]{1,0:T(8,128)(2,1)S(1)} collective-permute-done((bf16[208,128]{1,0:T(8,128)(2,1)S(1)}, bf16[208,128]{1,0:T(8,128)(2,1)S(1)}, u32[]{:S(2)}, u32[]{:S(2)}) %collective-permute-start.18) | collective-permute-done | bytes 53280 | tf_op jit(solution)/shard_map/ppermute | solution.py:383
  43.1 1.7 %collective-permute-done.19.other = bf16[2560,128]{1,0:T(8,128)(2,1)S(1)} collective-permute-done((bf16[2560,128]{1,0:T(8,128)(2,1)S(1)}, bf16[2560,128]{1,0:T(8,128)(2,1)S(1)}, u32[]{:S(2)}, u32[]{:S(2)}) %collective-permute-start.19) | collective-permute-done | bytes 655392 | tf_op jit(solution)/shard_map/ppermute | solution.py:380
  44.8 1.2 %shard_map.138 = f32[128,1280]{1,0:T(8,128)} custom-call(bf16[2560,128]{1,0:T(8,128)(2,1)S(1)} %collective-permute-done.19.other, f32[128,640]{1,0:T(8,128)S(1)} %shard_map.137.own_weight, bf16[2,128,128]{2,1,0:T(8,128)(2,1)S(1)} %pad_maximum_fusion.packed.refs_0_, bf16[2,128,128]{2,1,0:T(8,128)(2,1)S(1)} %collective-permute-done.5.refs_1_, ...), custom_call_target="tpu_custom_call" | custom-call | flops 83886080 | bytes 1245184 | tf_op jit(solution)/shard_map/pallas_call | solution.py:330
  46.0 1.0 %collective-permute-done.20.refs_2_ = bf16[208,128]{1,0:T(8,128)(2,1)S(1)} collective-permute-done((bf16[208,128]{1,0:T(8,128)(2,1)S(1)}, bf16[208,128]{1,0:T(8,128)(2,1)S(1)}, u32[]{:S(2)}, u32[]{:S(2)}) %collective-permute-start.20) | collective-permute-done | bytes 53280 | tf_op jit(solution)/shard_map/ppermute | solution.py:383
  47.0 0.9 %shard_map.139 = (bf16[128,128]{1,0:T(8,128)(2,1)}, f32[16,5120]{1,0:T(8,128)}) custom-call(f32[8,16,128]{2,1,0:T(8,128)S(1)} %get-tuple-element.67.hot, bf16[208,128]{1,0:T(8,128)(2,1)S(1)} %collective-permute-done.17.refs_0_, bf16[208,128]{1,0:T(8,128)(2,1)S(1)} %collective-permute-done.18.refs_1_, bf16[208,128]{1,0:T(8,128)(2,1)S(1)} %collective-permute-done.20.refs_2_, ...), custom_call_target="tpu_custom_call" | custom-call | bytes 278528 | tf_op jit(solution)/shard_map/pallas_call | solution.py:330
  (49 shorter events, 7.1 us)
Async XLA Ops:
  0.6 11.7 %copy-start.2 = (f32[16,5120]{1,0:T(8,128)S(1)}, f32[16,5120]{1,0:T(8,128)}, u32[]{:S(2)}) copy-start(f32[16,5120]{1,0:T(8,128)} %gate) | copy-start | bytes 983044
  3.0 15.1 %copy-start = (bf16[1024,128]{1,0:T(8,128)(2,1)S(1)}, bf16[1024,128]{1,0:T(8,128)(2,1)}, u32[]{:S(2)}) copy-start(bf16[1024,128]{1,0:T(8,128)(2,1)} %keys.5) | copy-start | bytes 786436
  3.0 4.7 %collective-permute-start = (bf16[128,2688]{1,0:T(8,128)(2,1)S(1)}, bf16[128,2688]{1,0:T(8,128)(2,1)S(1)}, u32[]{:S(2)}, u32[]{:S(2)}) collective-permute-start(bf16[128,2688]{1,0:T(8,128)(2,1)S(1)} %get-tuple-element.39), channel_id=1, source_target_pairs={{0,1},{1,0},{2,3},{3,2},{4,5},{5,4},{6,7},{7,6},{8,9},{9,8},{10,11... | collective-permute-start | bytes 2064392 | tf_op jit(solution)/shard_map/ppermute | solution.py:380
  3.5 11.4 %collective-permute-start.1 = (bf16[128,640]{1,0:T(8,128)(2,1)S(1)}, bf16[128,640]{1,0:T(8,128)(2,1)S(1)}, u32[]{:S(2)}, u32[]{:S(2)}) collective-permute-start(bf16[128,640]{1,0:T(8,128)(2,1)S(1)} %copy-done.1), channel_id=1, source_target_pairs={{0,2},{1,3},{2,0},{3,1},{4,6},{5,7},{6,4},{7,5},{8,10},{9,11},{10,... | collective-permute-start | bytes 491528 | tf_op jit(solution)/shard_map/ppermute | solution.py:374
  6.1 9.8 %collective-permute-start.2 = (bf16[128,640]{1,0:T(8,128)(2,1)S(1)}, bf16[128,640]{1,0:T(8,128)(2,1)S(1)}, u32[]{:S(2)}, u32[]{:S(2)}) collective-permute-start(bf16[128,640]{1,0:T(8,128)(2,1)S(1)} %copy-done.1), channel_id=1, source_target_pairs={{0,4},{1,5},{2,6},{3,7},{4,0},{5,1},{6,2},{7,3},{8,12},{9,13},{10,... | collective-permute-start | bytes 491528 | tf_op jit(solution)/shard_map/ppermute | solution.py:374
  7.6 8.3 %collective-permute-start.3 = (bf16[128,640]{1,0:T(8,128)(2,1)S(1)}, bf16[128,640]{1,0:T(8,128)(2,1)S(1)}, u32[]{:S(2)}, u32[]{:S(2)}) collective-permute-start(bf16[128,640]{1,0:T(8,128)(2,1)S(1)} %copy-done.1), channel_id=1, source_target_pairs={{0,6},{1,7},{2,4},{3,5},{4,2},{5,3},{6,0},{7,1},{8,14},{9,15},{10,... | collective-permute-start | bytes 491528 | tf_op jit(solution)/shard_map/ppermute | solution.py:374
  7.7 6.1 %collective-permute-start.6 = (bf16[2,128,128]{2,1,0:T(8,128)(2,1)S(1)}, bf16[2,128,128]{2,1,0:T(8,128)(2,1)S(1)}, u32[]{:S(2)}, u32[]{:S(2)}) collective-permute-start(bf16[2,128,128]{2,1,0:T(8,128)(2,1)S(1)} %pad_maximum_fusion.packed.refs_0_), channel_id=1, source_target_pairs={{0,16},{8,24},{16,0},{24,8},{1,17},{9,25},{17,1},{25,9},{2,18},{10... | collective-permute-start | bytes 196616 | tf_op jit(solution)/shard_map/ppermute | solution.py:383
  10.8 6.5 %collective-permute-start.5 = (bf16[2,128,128]{2,1,0:T(8,128)(2,1)S(1)}, bf16[2,128,128]{2,1,0:T(8,128)(2,1)S(1)}, u32[]{:S(2)}, u32[]{:S(2)}) collective-permute-start(bf16[2,128,128]{2,1,0:T(8,128)(2,1)S(1)} %pad_maximum_fusion.packed.refs_0_), channel_id=1, source_target_pairs={{0,8},{8,0},{16,24},{24,16},{1,9},{9,1},{17,25},{25,17},{2,10},{10... | collective-permute-start | bytes 196616 | tf_op jit(solution)/shard_map/ppermute | solution.py:383
  13.8 4.3 %collective-permute-start.7 = (bf16[2,128,128]{2,1,0:T(8,128)(2,1)S(1)}, bf16[2,128,128]{2,1,0:T(8,128)(2,1)S(1)}, u32[]{:S(2)}, u32[]{:S(2)}) collective-permute-start(bf16[2,128,128]{2,1,0:T(8,128)(2,1)S(1)} %collective-permute-done.6.refs_2_), channel_id=1, source_target_pairs={{0,8},{8,0},{16,24},{24,16},{1,9},{9,1},{17,25},{25,17},{2,10},{10... | collective-permute-start | bytes 196616 | tf_op jit(solution)/shard_map/ppermute | solution.py:383
  16.6 17.2 %copy-start.3 = (bf16[1024,128]{1,0:T(8,128)(2,1)S(1)}, bf16[1024,128]{1,0:T(8,128)(2,1)}, u32[]{:S(2)}) copy-start(bf16[1024,128]{1,0:T(8,128)(2,1)} %values.3) | copy-start | bytes 786436
  16.7 2.2 %collective-permute-start.4 = (f32[128,128]{1,0:T(8,128)S(1)}, f32[128,128]{1,0:T(8,128)S(1)}, u32[]{:S(2)}, u32[]{:S(2)}) collective-permute-start(f32[128,128]{1,0:T(8,128)S(1)} %get-tuple-element.47), channel_id=1, source_target_pairs={{0,1},{1,0},{2,3},{3,2},{4,5},{5,4},{6,7},{7,6},{8,9},{9,8},{10,11... | collective-permute-start | bytes 196616 | tf_op jit(solution)/shard_map/ppermute | solution.py:380
  16.7 2.1 %collective-permute-start.8 = (f32[40,128]{1,0:T(8,128)S(1)}, f32[40,128]{1,0:T(8,128)S(1)}, u32[]{:S(2)}, u32[]{:S(2)}) collective-permute-start(f32[40,128]{1,0:T(8,128)S(1)} %get-tuple-element.50.own_terms), channel_id=1, source_target_pairs={{0,1},{1,0},{2,3},{3,2},{4,5},{5,4},{6,7},{7,6},{8,9},{9,8},{10,11... | collective-permute-start | bytes 61448 | tf_op jit(solution)/shard_map/ppermute | solution.py:380
  19.0 6.0 %collective-permute-start.9 = (f32[80,128]{1,0:T(8,128)S(1)}, f32[80,128]{1,0:T(8,128)S(1)}, u32[]{:S(2)}, u32[]{:S(2)}) collective-permute-start(f32[80,128]{1,0:T(8,128)S(1)} %get-tuple-element.51), channel_id=1, source_target_pairs={{0,2},{1,3},{2,0},{3,1},{4,6},{5,7},{6,4},{7,5},{8,10},{9,11},{10,... | collective-permute-start | bytes 122888 | tf_op jit(solution)/shard_map/ppermute | solution.py:374
  20.6 8.5 %collective-permute-start.11 = (bf16[320,128]{1,0:T(8,128)(2,1)S(1)}, bf16[320,128]{1,0:T(8,128)(2,1)S(1)}, u32[]{:S(2)}, u32[]{:S(2)}) collective-permute-start(bf16[320,128]{1,0:T(8,128)(2,1)S(1)} %get-tuple-element.54), channel_id=1, source_target_pairs={{0,24},{8,16},{16,8},{24,0},{1,25},{9,17},{17,9},{25,1},{2,26},{10... | collective-permute-start | bytes 245768 | tf_op jit(solution)/shard_map/ppermute | solution.py:383
  24.4 5.9 %collective-permute-start.12 = (bf16[320,128]{1,0:T(8,128)(2,1)S(1)}, bf16[320,128]{1,0:T(8,128)(2,1)S(1)}, u32[]{:S(2)}, u32[]{:S(2)}) collective-permute-start(bf16[320,128]{1,0:T(8,128)(2,1)S(1)} %get-tuple-element.55), channel_id=1, source_target_pairs={{0,16},{8,24},{16,0},{24,8},{1,17},{9,25},{17,1},{25,9},{2,18},{10... | collective-permute-start | bytes 245768 | tf_op jit(solution)/shard_map/ppermute | solution.py:383
  24.4 5.9 %collective-permute-start.13 = (bf16[320,128]{1,0:T(8,128)(2,1)S(1)}, bf16[320,128]{1,0:T(8,128)(2,1)S(1)}, u32[]{:S(2)}, u32[]{:S(2)}) collective-permute-start(bf16[320,128]{1,0:T(8,128)(2,1)S(1)} %get-tuple-element.56), channel_id=1, source_target_pairs={{0,8},{8,0},{16,24},{24,16},{1,9},{9,1},{17,25},{25,17},{2,10},{10... | collective-permute-start | bytes 245768 | tf_op jit(solution)/shard_map/ppermute | solution.py:383
  25.0 4.1 %collective-permute-start.10 = (f32[80,128]{1,0:T(8,128)S(1)}, f32[80,128]{1,0:T(8,128)S(1)}, u32[]{:S(2)}, u32[]{:S(2)}) collective-permute-start(f32[80,128]{1,0:T(8,128)S(1)} %add.6), channel_id=1, source_target_pairs={{0,4},{1,5},{2,6},{3,7},{4,0},{5,1},{6,2},{7,3},{8,12},{9,13},{10,... | collective-permute-start | bytes 122888 | tf_op jit(solution)/shard_map/ppermute | solution.py:374
  30.3 12.3 %collective-permute-start.14 = (bf16[640,128]{1,0:T(8,128)(2,1)S(1)}, bf16[640,128]{1,0:T(8,128)(2,1)S(1)}, u32[]{:S(2)}, u32[]{:S(2)}) collective-permute-start(bf16[640,128]{1,0:T(8,128)(2,1)S(1)} %shard_map.133.refs_0_), channel_id=1, source_target_pairs={{0,2},{1,3},{2,0},{3,1},{4,6},{5,7},{6,4},{7,5},{8,10},{9,11},{10,... | collective-permute-start | bytes 491528 | tf_op jit(solution)/shard_map/ppermute | solution.py:374
  31.1 11.4 %collective-permute-start.15 = (bf16[640,128]{1,0:T(8,128)(2,1)S(1)}, bf16[640,128]{1,0:T(8,128)(2,1)S(1)}, u32[]{:S(2)}, u32[]{:S(2)}) collective-permute-start(bf16[640,128]{1,0:T(8,128)(2,1)S(1)} %shard_map.133.refs_0_), channel_id=1, source_target_pairs={{0,4},{1,5},{2,6},{3,7},{4,0},{5,1},{6,2},{7,3},{8,12},{9,13},{10,... | collective-permute-start | bytes 491528 | tf_op jit(solution)/shard_map/ppermute | solution.py:374
  32.6 9.9 %collective-permute-start.16 = (bf16[640,128]{1,0:T(8,128)(2,1)S(1)}, bf16[640,128]{1,0:T(8,128)(2,1)S(1)}, u32[]{:S(2)}, u32[]{:S(2)}) collective-permute-start(bf16[640,128]{1,0:T(8,128)(2,1)S(1)} %shard_map.133.refs_0_), channel_id=1, source_target_pairs={{0,6},{1,7},{2,4},{3,5},{4,2},{5,3},{6,0},{7,1},{8,14},{9,15},{10,... | collective-permute-start | bytes 491528 | tf_op jit(solution)/shard_map/ppermute | solution.py:374
  34.8 6.0 %collective-permute-start.17 = (bf16[208,128]{1,0:T(8,128)(2,1)S(1)}, bf16[208,128]{1,0:T(8,128)(2,1)S(1)}, u32[]{:S(2)}, u32[]{:S(2)}) collective-permute-start(bf16[208,128]{1,0:T(8,128)(2,1)S(1)} %get-tuple-element.61), channel_id=1, source_target_pairs={{0,24},{8,16},{16,8},{24,0},{1,25},{9,17},{17,9},{25,1},{2,26},{10... | collective-permute-start | bytes 159752 | tf_op jit(solution)/shard_map/ppermute | solution.py:383
  37.5 5.0 %collective-permute-start.18 = (bf16[208,128]{1,0:T(8,128)(2,1)S(1)}, bf16[208,128]{1,0:T(8,128)(2,1)S(1)}, u32[]{:S(2)}, u32[]{:S(2)}) collective-permute-start(bf16[208,128]{1,0:T(8,128)(2,1)S(1)} %get-tuple-element.62), channel_id=1, source_target_pairs={{0,16},{8,24},{16,0},{24,8},{1,17},{9,25},{17,1},{25,9},{2,18},{10... | collective-permute-start | bytes 159752 | tf_op jit(solution)/shard_map/ppermute | solution.py:383
  42.6 2.2 %collective-permute-start.19 = (bf16[2560,128]{1,0:T(8,128)(2,1)S(1)}, bf16[2560,128]{1,0:T(8,128)(2,1)S(1)}, u32[]{:S(2)}, u32[]{:S(2)}) collective-permute-start(bf16[2560,128]{1,0:T(8,128)(2,1)S(1)} %shard_map.136.own), channel_id=1, source_target_pairs={{0,1},{1,0},{2,3},{3,2},{4,5},{5,4},{6,7},{7,6},{8,9},{9,8},{10,11... | collective-permute-start | bytes 1966088 | tf_op jit(solution)/shard_map/ppermute | solution.py:380
  42.7 4.2 %collective-permute-start.20 = (bf16[208,128]{1,0:T(8,128)(2,1)S(1)}, bf16[208,128]{1,0:T(8,128)(2,1)S(1)}, u32[]{:S(2)}, u32[]{:S(2)}) collective-permute-start(bf16[208,128]{1,0:T(8,128)(2,1)S(1)} %get-tuple-element.68), channel_id=1, source_target_pairs={{0,8},{8,0},{16,24},{24,16},{1,9},{9,1},{17,25},{25,17},{2,10},{10... | collective-permute-start | bytes 159752 | tf_op jit(solution)/shard_map/ppermute | solution.py:383
  (5 other events, 31.7 us)

commit v16 on v14

--- a/solution.py
+++ b/solution.py
@@ -188,21 +188,6 @@
     first = SPLIT * 2 * n_t
     terms = [heads[k][starts[2] :, :].astype(jnp.float32)[first : first + count] for k in range(n_t)]
     out[tiles * n_t * part :, :] = jnp.concatenate(terms, axis=0).astype(jnp.bfloat16)
-
-
-def collect_kernel(chips, base, *refs):
-    pieces, out, held = refs[:chips], refs[chips], refs[chips + 1]
-    chip = place()[1]
-    for k in range(chips):
-        out[k * base : (k + 1) * base, :] = pieces[k][:base, :]
-        held[chip ^ k] = pieces[k][base:, :].astype(jnp.float32)
-    total = held[0]
-    for k in range(1, chips):
-        total = total + held[k]
-    high = total.astype(jnp.bfloat16)
-    count = total.shape[0]
-    out[chips * base : chips * base + count, :] = high
-    out[chips * base + count :, :] = (total - high.astype(jnp.float32)).astype(jnp.bfloat16)
 
 
 def grads_kernel(n_t, starts, first, last, bias, keys, values, *refs):
@@ -271,7 +256,7 @@
     refs[n_t][...] = jnp.transpose(total * SCALE).astype(jnp.bfloat16)
 
 
-def half_results(n_t, chips, frames, hot, ref, packed, saved, held, tiles):
+def half_results(n_t, chips, frames, hot, gated_refs, packed, saved, held, tiles):
     t, chip, _ = place()
     rows = saved.shape[1]
     part = rows // chips
@@ -282,53 +267,52 @@
     for c in range(chips):
         mine = pl.ds(pl.multiple_of((chip ^ c) * part, part), part)
         ordered += [saved[k, mine, :] for k in range(n_t)]
+        held[chip ^ c] = gated_refs[c][base:, :].astype(jnp.float32)
     ordered = jnp.transpose(jnp.concatenate(ordered, axis=0)).astype(jnp.bfloat16)
     gated = jnp.concatenate(
         [
             jnp.concatenate(
-                [
-                    ref[c * base + j * n_t * part : c * base + (j + 1) * n_t * part, :]
-                    for c in range(chips)
-                ],
-                axis=0,
+                [ref[j * n_t * part : (j + 1) * n_t * part, :] for ref in gated_refs], axis=0
             )
             for j in range(tiles)
         ],
         axis=1,
     )
-    count = (ref.shape[0] - chips * base) // 2
-    each = count // n_t
-    terms = ref[chips * base : chips * base + count, :].astype(jnp.float32)
-    terms = terms + ref[chips * base + count :, :].astype(jnp.float32)
+    terms = held[0]
+    for c in range(1, chips):
+        terms = terms + held[c]
+    count = terms.shape[0] // n_t
     for k in range(n_t):
-        held[t ^ k] = terms[k * each : (k + 1) * each]
+        held[0, pl.ds(pl.multiple_of((t ^ k) * count, 8), count), :] = terms[k * count : (k + 1) * count]
 
     def gate_tile(a, j):
         total = jnp.zeros(hot.shape[1:], jnp.float32)
         for f in range(n_t * frames):
-            row = (a * frames + f % frames) * tiles + j
-            total = total + hot[f] * held[f // frames, row : row + 1, :]
+            row = (f // frames) * count + (a * frames + f % frames) * tiles + j
+            total = total + hot[f] * held[0, row : row + 1, :]
         return total
 
     return dot(ordered, gated, 1, 0), gate_tile
 
 
-def own_kernel(n_t, chips, frames, hot, own, *refs):
-    packed, (weight_out, gate_out, saved, held) = refs[:n_t], refs[n_t:]
+def own_kernel(n_t, chips, frames, hot, *refs):
+    gated, packed = refs[:chips], refs[chips : chips + n_t]
+    weight_out, gate_out, saved, held = refs[chips + n_t :]
     tiles = weight_out.shape[1] // LANES
-    result, gate_tile = half_results(n_t, chips, frames, hot, own, packed, saved, held, tiles)
+    result, gate_tile = half_results(n_t, chips, frames, hot, gated, packed, saved, held, tiles)
     weight_out[...] = result
     for a in range(chips):
         for j in range(tiles):
             gate_out[:, (a * tiles + j) * LANES : (a * tiles + j + 1) * LANES] = gate_tile(a, j)
 
 
-def final_kernel(n_t, chips, frames, hot, other, own_weight, own_gate, *refs):
-    packed, (weight_out, gate_out, saved, held) = refs[:n_t], refs[n_t:]
+def final_kernel(n_t, chips, frames, hot, own_weight, own_gate, *refs):
+    gated, packed = refs[:chips], refs[chips : chips + n_t]
+    weight_out, gate_out, saved, held = refs[chips + n_t :]
     core = place()[2]
     width = own_weight.shape[1]
     tiles = width // LANES
-    result, gate_tile = half_results(n_t, chips, frames, hot, other, packed, saved, held, tiles)
+    result, gate_tile = half_results(n_t, chips, frames, hot, gated, packed, saved, held, tiles)
     mine = own_weight[...]
     weight_out[:, :width] = jnp.where(core == 0, mine, result)
     weight_out[:, width:] = jnp.where(core == 0, result, mine)
@@ -481,24 +465,18 @@
     key_grad, value_grad = near[:2]
     parts[0], parts[1] = near[3], over_time(near[2], 1)
     parts = [parts[k] for k in range(n_t)]
-    bundles, _ = lax.optimization_barrier((bundles, (key_grad, parts[n_t - 1])))
-    collected = call(
-        functools.partial(collect_kernel, chips, base),
-        bundles,
-        shape(bf16, chips * base + 2 * n_t * count, LANES),
-        [pltpu.VMEM((chips, n_t * count, LANES), f32)],
-    )
-    scratch = [pltpu.VMEM((n_t, rows, HD), f32), pltpu.VMEM((n_t, count, LANES), f32)]
+    bundles, _ = lax.optimization_barrier((bundles, (key_grad, parts[: n_t // 2 - 1 : -1])))
+    scratch = [pltpu.VMEM((n_t, rows, HD), f32), pltpu.VMEM((chips, n_t * count, LANES), f32)]
     own_halves = call(
         functools.partial(own_kernel, n_t, chips, frames),
-        [hot, collected] + packed_all,
+        [hot] + bundles + packed_all,
         [shape(f32, HD, width), shape(f32, levels, chips * width)],
         scratch,
         flops=2 * n_t * rows * width * HD,
     )
     weight_grad, gate_grad = call(
         functools.partial(final_kernel, n_t, chips, frames),
-        [hot, over_cores(collected), *own_halves] + packed_all,
+        [hot, *own_halves] + [over_cores(x) for x in bundles] + packed_all,
         [shape(f32, HD, 2 * width), shape(f32, levels, n_s * width)],
         scratch,
         flops=2 * n_t * rows * width * HD,

time: 47.5 us -> 47.4 us (level)
  starting transfers between devices: 23.5 us -> 22.4 us
  waiting for transfers between devices: 13.3 us -> 14.3 us
    ppermute x9, starting transfers between devices: 15.2 us -> 13 us  [over_time(): return lax.ppermute(x, 'tm', [(t, t ^ k) for t in range(n_t)])]
    ppermute x9, waiting for transfers between devices: 10.8 us -> 12.7 us  [over_time(): return lax.ppermute(x, 'tm', [(t, t ^ k) for t in range(n_t)])]
    ppermute x6, waiting for transfers between devices: 2.45 us -> 0.71 us  [over_chips(): lax.ppermute(x, 'space', [(s, s ^ 2 * k) for s in range(n_s)])]
    ppermute x3 -> x6, starting transfers between devices: 0.66 us -> 1.67 us  [over_cores(): return lax.ppermute(x, 'space', [(s, s ^ 1) for s in range(n_s)])]
    ppermute x3 -> x6, waiting for transfers between devices: 0.01 us -> 0.86 us  [over_cores(): return lax.ppermute(x, 'space', [(s, s ^ 1) for s in range(n_s)])]
    pallas_call x12 -> x11, Pallas kernels: 8.98 us -> 8.98 us  [call(): pl.pallas_call(kernel, out_shape=out_shape, in_specs=[pl.BlockSpec(memory...]
  transfers between devices with their start and end apart: 18 -> 21, of which waited for: 9 -> 12; matrix products, arithmetic and copies ran while one was open for 0% -> 0% of each run, Pallas kernels for 14% -> 14%
where the time goes in v16:
time: 47.4 us; the launch traced here: 47.3 us
  starting transfers between devices  22.4 us (47%)
  waiting for transfers between devices  14.3 us (30%)
  Pallas kernels  8.98 us (19%)
  local copies, waits for them, and re-layouts  0.84 us (2%)
  between operations  0.79 us (2%)
    ppermute x9, starting transfers between devices, over_time(): return lax.ppermute(x, 'tm', [(t, t ^ k) for t in range(n_t)])  13 us
    ppermute x9, waiting for transfers between devices, over_time(): return lax.ppermute(x, 'tm', [(t, t ^ k) for t in range(n_t)])  12.7 us
    pallas_call x11, Pallas kernels, call(): pl.pallas_call(kernel, out_shape=out_shape, in_specs=[pl.BlockSpec(memory...  8.98 us
    ppermute x6, starting transfers between devices, over_chips(): lax.ppermute(x, 'space', [(s, s ^ 2 * k) for s in range(n_s)])  7.72 us
    ppermute x6, starting transfers between devices, over_cores(): return lax.ppermute(x, 'space', [(s, s ^ 1) for s in range(n_s)])  1.67 us
  transfers between devices with their start and end apart: 21, of which 12 were waited for; matrix products, arithmetic and copies ran while one was open for 0% of the time, Pallas kernels for 14%

profile of v16, /device:TPU:0, one launch (start us, length us, event | category | flops | bytes accessed | tf_op | source)
XLA Modules:
  0.0 47.3 jit_solution(6847081262903984776)
XLA Ops:
  0.7 0.8 %copy-done.4 = bf16[128,128]{1,0:T(8,128)(2,1)S(1)} copy-done((bf16[128,128]{1,0:T(8,128)(2,1)S(1)}, bf16[128,128]{1,0:T(8,128)(2,1)}, u32[]{:S(2)}) %copy-start.4) | copy-done | bytes 32792
  1.5 1.5 %shard_map.128 = (bf16[4,128,640]{2,1,0:T(8,128)(2,1)S(1)}, bf16[128,2688]{1,0:T(8,128)(2,1)S(1)}) custom-call(bf16[128,5120]{1,0:T(8,128)(2,1)} %weight_in.1, bf16[128,128]{1,0:T(8,128)(2,1)S(1)} %copy-done.4), custom_call_target="tpu_custom_call" | custom-call | bytes 1343488 | tf_op jit(solution)/shard_map/pallas_call | solution.py:333
  3.5 3.5 %collective-permute-start.3 = (bf16[128,640]{1,0:T(8,128)(2,1)S(1)}, bf16[128,640]{1,0:T(8,128)(2,1)S(1)}, u32[]{:S(2)}, u32[]{:S(2)}) collective-permute-start(bf16[128,640]{1,0:T(8,128)(2,1)S(1)} %copy-done.1), channel_id=1, source_target_pairs={{0,6},{1,7},{2,4},{3,5},{4,2},{5,3},{6,0},{7,1},{8,14},{9,15},{10,... | collective-permute-start | bytes 491528 | tf_op jit(solution)/shard_map/ppermute | solution.py:378
  7.7 3.1 %collective-permute-start.6 = (bf16[2,128,128]{2,1,0:T(8,128)(2,1)S(1)}, bf16[2,128,128]{2,1,0:T(8,128)(2,1)S(1)}, u32[]{:S(2)}, u32[]{:S(2)}) collective-permute-start(bf16[2,128,128]{2,1,0:T(8,128)(2,1)S(1)} %pad_maximum_fusion.packed.refs_0_.refs_4_), channel_id=1, source_target_pairs={{0,16},{8,24},{16,0},{24,8},{1,17},{9,25},{17,1},{25,9},{2,18},{10... | collective-permute-start | bytes 196616 | tf_op jit(solution)/shard_map/ppermute | solution.py:385
  10.8 1.6 %collective-permute-start.5 = (bf16[2,128,128]{2,1,0:T(8,128)(2,1)S(1)}, bf16[2,128,128]{2,1,0:T(8,128)(2,1)S(1)}, u32[]{:S(2)}, u32[]{:S(2)}) collective-permute-start(bf16[2,128,128]{2,1,0:T(8,128)(2,1)S(1)} %pad_maximum_fusion.packed.refs_0_.refs_4_), channel_id=1, source_target_pairs={{0,8},{8,0},{16,24},{24,16},{1,9},{9,1},{17,25},{25,17},{2,10},{10... | collective-permute-start | bytes 196616 | tf_op jit(solution)/shard_map/ppermute | solution.py:385
  12.4 0.6 %shard_map.129 = (f32[2,512]{1,0:T(2,128)S(1)}, f32[4,2,640]{2,1,0:T(2,128)S(1)}, f32[4,1,640]{2,1,0:T(1,128)S(1)}, f32[8,16,128]{2,1,0:T(8,128)S(1)}) custom-call(s32[8]{0:T(128)S(1)} %copy-done.5, s32[4]{0:T(128)S(1)} %copy-done.6, f32[16,5120]{1,0:T(8,128)S(1)} %copy-done.2), custom_call_target="tpu_custom_call" | custom-call | bytes 327728 | tf_op jit(solution)/shard_map/pallas_call | solution.py:333
  13.0 0.8 %collective-permute-done.6.refs_2_.refs_6_ = bf16[2,128,128]{2,1,0:T(8,128)(2,1)S(1)} collective-permute-done((bf16[2,128,128]{2,1,0:T(8,128)(2,1)S(1)}, bf16[2,128,128]{2,1,0:T(8,128)(2,1)S(1)}, u32[]{:S(2)}, u32[]{:S(2)}) %collective-permute-start.6) | collective-permute-done | bytes 65568 | tf_op jit(solution)/shard_map/ppermute | solution.py:385
  13.8 1.2 %collective-permute-start.7 = (bf16[2,128,128]{2,1,0:T(8,128)(2,1)S(1)}, bf16[2,128,128]{2,1,0:T(8,128)(2,1)S(1)}, u32[]{:S(2)}, u32[]{:S(2)}) collective-permute-start(bf16[2,128,128]{2,1,0:T(8,128)(2,1)S(1)} %collective-permute-done.6.refs_2_.refs_6_), channel_id=1, source_target_pairs={{0,8},{8,0},{16,24},{24,16},{1,9},{9,1},{17,25},{25,17},{2,10},{10... | collective-permute-start | bytes 196616 | tf_op jit(solution)/shard_map/ppermute | solution.py:385
  15.7 0.8 %shard_map.130 = (f32[128,128]{1,0:T(8,128)S(1)}, f32[128,128]{1,0:T(8,128)S(1)}, f32[40,128]{1,0:T(8,128)S(1)}) custom-call(bf16[2,128,128]{2,1,0:T(8,128)(2,1)S(1)} %pad_maximum_fusion.packed.refs_0_.refs_4_, bf16[4,128,640]{2,1,0:T(8,128)(2,1)S(1)} %get-tuple-element.44.kept, bf16[128,2688]{1,0:T(8,128)(2,1)S(1)} %collective-permute-done.received, ...), custom_call_target="tpu_custom_call" | custom-call | flops 335544320 | bytes 2084864 | tf_op jit(solution)/shard_map/pallas_call | solution.py:333
  16.5 1.5 %collective-permute-done.7.refs_3_.refs_7_ = bf16[2,128,128]{2,1,0:T(8,128)(2,1)S(1)} collective-permute-done((bf16[2,128,128]{2,1,0:T(8,128)(2,1)S(1)}, bf16[2,128,128]{2,1,0:T(8,128)(2,1)S(1)}, u32[]{:S(2)}, u32[]{:S(2)}) %collective-permute-start.7) | collective-permute-done | bytes 65568 | tf_op jit(solution)/shard_map/ppermute | solution.py:385
  18.1 0.8 %shard_map.131.stats = f32[8,128]{1,0:T(8,128)S(1)} custom-call(f32[2,512]{1,0:T(2,128)S(1)} %get-tuple-element.54.bias, bf16[1024,128]{1,0:T(8,128)(2,1)S(1)} %copy-done, bf16[2,128,128]{2,1,0:T(8,128)(2,1)S(1)} %pad_maximum_fusion.packed.refs_0_.refs_4_, bf16[2,128,128]{2,1,0:T(8,128)(2,1)S(1)} %collective-permute-done.5.refs_1_.refs_5_, ...), custom_call_target="tpu_custom_call" | custom-call | flops 134217728 | bytes 528384 | tf_op jit(solution)/shard_map/pallas_call | solution.py:333
  19.0 3.9 %collective-permute-start.8 = (bf16[352,128]{1,0:T(8,128)(2,1)S(1)}, bf16[352,128]{1,0:T(8,128)(2,1)S(1)}, u32[]{:S(2)}, u32[]{:S(2)}) collective-permute-start(bf16[352,128]{1,0:T(8,128)(2,1)S(1)} %get-tuple-element.51), channel_id=1, source_target_pairs={{0,24},{8,16},{16,8},{24,0},{1,25},{9,17},{17,9},{25,1},{2,26},{10... | collective-permute-start | bytes 270344 | tf_op jit(solution)/shard_map/ppermute | solution.py:385
  23.5 2.5 %collective-permute-done.8.refs_1_.refs_4_ = bf16[352,128]{1,0:T(8,128)(2,1)S(1)} collective-permute-done((bf16[352,128]{1,0:T(8,128)(2,1)S(1)}, bf16[352,128]{1,0:T(8,128)(2,1)S(1)}, u32[]{:S(2)}, u32[]{:S(2)}) %collective-permute-start.8) | collective-permute-done | bytes 90144 | tf_op jit(solution)/shard_map/ppermute | solution.py:385
  26.0 3.5 %collective-permute-done.9.refs_2_.refs_5_ = bf16[352,128]{1,0:T(8,128)(2,1)S(1)} collective-permute-done((bf16[352,128]{1,0:T(8,128)(2,1)S(1)}, bf16[352,128]{1,0:T(8,128)(2,1)S(1)}, u32[]{:S(2)}, u32[]{:S(2)}) %collective-permute-start.9) | collective-permute-done | bytes 90144 | tf_op jit(solution)/shard_map/ppermute | solution.py:385
  29.5 2.3 %collective-permute-start.16 = (bf16[800,128]{1,0:T(8,128)(2,1)S(1)}, bf16[800,128]{1,0:T(8,128)(2,1)S(1)}, u32[]{:S(2)}, u32[]{:S(2)}) collective-permute-start(bf16[800,128]{1,0:T(8,128)(2,1)S(1)} %shard_map.133.refs_0_), channel_id=1, source_target_pairs={{0,6},{1,7},{2,4},{3,5},{4,2},{5,3},{6,0},{7,1},{8,14},{9,15},{10,... | collective-permute-start | bytes 614408 | tf_op jit(solution)/shard_map/ppermute | solution.py:378
  31.8 0.7 %collective-permute-start.15 = (bf16[800,128]{1,0:T(8,128)(2,1)S(1)}, bf16[800,128]{1,0:T(8,128)(2,1)S(1)}, u32[]{:S(2)}, u32[]{:S(2)}) collective-permute-start(bf16[800,128]{1,0:T(8,128)(2,1)S(1)} %shard_map.133.refs_0_), channel_id=1, source_target_pairs={{0,4},{1,5},{2,6},{3,7},{4,0},{5,1},{6,2},{7,3},{8,12},{9,13},{10,... | collective-permute-start | bytes 614408 | tf_op jit(solution)/shard_map/ppermute | solution.py:378
  33.1 1.0 %shard_map.134 = (f32[1024,128]{1,0:T(8,128)S(1)}, f32[1024,128]{1,0:T(8,128)S(1)}, bf16[128,128]{1,0:T(8,128)(2,1)S(1)}, bf16[128,128]{1,0:T(8,128)(2,1)S(1)}) custom-call(f32[2,512]{1,0:T(2,128)S(1)} %get-tuple-element.54.bias, bf16[1024,128]{1,0:T(8,128)(2,1)S(1)} %copy-done, bf16[1024,128]{1,0:T(8,128)(2,1)S(1)} %copy-done.3, ...), custom_call_target="tpu_custom_call" | custom-call | flops 335544320 | bytes 1150976 | tf_op jit(solution)/shard_map/pallas_call | solution.py:333
  34.1 2.7 %collective-permute-start.11 = (bf16[128,128]{1,0:T(8,128)(2,1)S(1)}, bf16[128,128]{1,0:T(8,128)(2,1)S(1)}, u32[]{:S(2)}, u32[]{:S(2)}) collective-permute-start(bf16[128,128]{1,0:T(8,128)(2,1)S(1)} %get-tuple-element.55), channel_id=1, source_target_pairs={{0,24},{8,16},{16,8},{24,0},{1,25},{9,17},{17,9},{25,1},{2,26},{10... | collective-permute-start | bytes 98312 | tf_op jit(solution)/shard_map/ppermute | solution.py:385
  36.7 1.7 %shard_map.135 = (bf16[1024,128]{1,0:T(8,128)(2,1)}, bf16[1024,128]{1,0:T(8,128)(2,1)}, bf16[128,128]{1,0:T(8,128)(2,1)S(1)}, bf16[128,128]{1,0:T(8,128)(2,1)S(1)}) custom-call(f32[2,512]{1,0:T(2,128)S(1)} %get-tuple-element.54.bias, bf16[1024,128]{1,0:T(8,128)(2,1)S(1)} %copy-done, bf16[1024,128]{1,0:T(8,128)(2,1)S(1)} %copy-done.3, ...), custom_call_target="tpu_custom_call" | custom-call | flops 335544320 | bytes 2199552 | tf_op jit(solution)/shard_map/pallas_call | solution.py:333
  38.4 1.5 %collective-permute-done.11.refs_0_ = bf16[128,128]{1,0:T(8,128)(2,1)S(1)} collective-permute-done((bf16[128,128]{1,0:T(8,128)(2,1)S(1)}, bf16[128,128]{1,0:T(8,128)(2,1)S(1)}, u32[]{:S(2)}, u32[]{:S(2)}) %collective-permute-start.11) | collective-permute-done | bytes 32800 | tf_op jit(solution)/shard_map/ppermute | solution.py:385
  39.8 1.7 %collective-permute-done.12.refs_1_ = bf16[128,128]{1,0:T(8,128)(2,1)S(1)} collective-permute-done((bf16[128,128]{1,0:T(8,128)(2,1)S(1)}, bf16[128,128]{1,0:T(8,128)(2,1)S(1)}, u32[]{:S(2)}, u32[]{:S(2)}) %collective-permute-start.12) | collective-permute-done | bytes 32800 | tf_op jit(solution)/shard_map/ppermute | solution.py:385
  44.0 1.3 %shard_map.137 = (f32[128,1280]{1,0:T(8,128)}, f32[16,5120]{1,0:T(8,128)}) custom-call(f32[8,16,128]{2,1,0:T(8,128)S(1)} %get-tuple-element.61.hot, f32[128,640]{1,0:T(8,128)S(1)} %get-tuple-element.67.own_weight, f32[16,2560]{1,0:T(8,128)S(1)} %get-tuple-element.68.own_gate, bf16[800,128]{1,0:T(8,128)(2,1)S(1)} %collective-permute-done.17.refs_0_, ...), custom_call_target="tpu_custom_call" | custom-call | flops 83886080 | bytes 1638400 | tf_op jit(solution)/shard_map/pallas_call | solution.py:333
  45.2 1.3 %collective-permute-done.13.refs_2_ = bf16[128,128]{1,0:T(8,128)(2,1)S(1)} collective-permute-done((bf16[128,128]{1,0:T(8,128)(2,1)S(1)}, bf16[128,128]{1,0:T(8,128)(2,1)S(1)}, u32[]{:S(2)}, u32[]{:S(2)}) %collective-permute-start.13) | collective-permute-done | bytes 32800 | tf_op jit(solution)/shard_map/ppermute | solution.py:385
  46.6 0.7 %shard_map.138 = bf16[128,128]{1,0:T(8,128)(2,1)} custom-call(bf16[128,128]{1,0:T(8,128)(2,1)S(1)} %collective-permute-done.11.refs_0_, bf16[128,128]{1,0:T(8,128)(2,1)S(1)} %collective-permute-done.12.refs_1_, bf16[128,128]{1,0:T(8,128)(2,1)S(1)} %collective-permute-done.13.refs_2_, bf16[128,128]{1,0:T(8,128)(2,1)S(1)} %get-tuple-element.70.refs_3_), custom_call_target="tpu_custom_call" | custom-call | bytes 131072 | tf_op jit(solution)/shard_map/pallas_call | solution.py:333
  (46 shorter events, 5.7 us)
Async XLA Ops:
  0.6 11.7 %copy-start.2 = (f32[16,5120]{1,0:T(8,128)S(1)}, f32[16,5120]{1,0:T(8,128)}, u32[]{:S(2)}) copy-start(f32[16,5120]{1,0:T(8,128)} %gate) | copy-start | bytes 983044
  3.0 15.1 %copy-start = (bf16[1024,128]{1,0:T(8,128)(2,1)S(1)}, bf16[1024,128]{1,0:T(8,128)(2,1)}, u32[]{:S(2)}) copy-start(bf16[1024,128]{1,0:T(8,128)(2,1)} %keys.5) | copy-start | bytes 786436
  3.0 4.7 %collective-permute-start = (bf16[128,2688]{1,0:T(8,128)(2,1)S(1)}, bf16[128,2688]{1,0:T(8,128)(2,1)S(1)}, u32[]{:S(2)}, u32[]{:S(2)}) collective-permute-start(bf16[128,2688]{1,0:T(8,128)(2,1)S(1)} %get-tuple-element.39), channel_id=1, source_target_pairs={{0,1},{1,0},{2,3},{3,2},{4,5},{5,4},{6,7},{7,6},{8,9},{9,8},{10,11... | collective-permute-start | bytes 2064392 | tf_op jit(solution)/shard_map/ppermute | solution.py:382
  3.5 11.4 %collective-permute-start.3 = (bf16[128,640]{1,0:T(8,128)(2,1)S(1)}, bf16[128,640]{1,0:T(8,128)(2,1)S(1)}, u32[]{:S(2)}, u32[]{:S(2)}) collective-permute-start(bf16[128,640]{1,0:T(8,128)(2,1)S(1)} %copy-done.1), channel_id=1, source_target_pairs={{0,6},{1,7},{2,4},{3,5},{4,2},{5,3},{6,0},{7,1},{8,14},{9,15},{10,... | collective-permute-start | bytes 491528 | tf_op jit(solution)/shard_map/ppermute | solution.py:378
  7.1 8.3 %collective-permute-start.2 = (bf16[128,640]{1,0:T(8,128)(2,1)S(1)}, bf16[128,640]{1,0:T(8,128)(2,1)S(1)}, u32[]{:S(2)}, u32[]{:S(2)}) collective-permute-start(bf16[128,640]{1,0:T(8,128)(2,1)S(1)} %copy-done.1), channel_id=1, source_target_pairs={{0,4},{1,5},{2,6},{3,7},{4,0},{5,1},{6,2},{7,3},{8,12},{9,13},{10,... | collective-permute-start | bytes 491528 | tf_op jit(solution)/shard_map/ppermute | solution.py:378
  7.6 8.1 %collective-permute-start.1 = (bf16[128,640]{1,0:T(8,128)(2,1)S(1)}, bf16[128,640]{1,0:T(8,128)(2,1)S(1)}, u32[]{:S(2)}, u32[]{:S(2)}) collective-permute-start(bf16[128,640]{1,0:T(8,128)(2,1)S(1)} %copy-done.1), channel_id=1, source_target_pairs={{0,2},{1,3},{2,0},{3,1},{4,6},{5,7},{6,4},{7,5},{8,10},{9,11},{10,... | collective-permute-start | bytes 491528 | tf_op jit(solution)/shard_map/ppermute | solution.py:378
  7.7 6.1 %collective-permute-start.6 = (bf16[2,128,128]{2,1,0:T(8,128)(2,1)S(1)}, bf16[2,128,128]{2,1,0:T(8,128)(2,1)S(1)}, u32[]{:S(2)}, u32[]{:S(2)}) collective-permute-start(bf16[2,128,128]{2,1,0:T(8,128)(2,1)S(1)} %pad_maximum_fusion.packed.refs_0_.refs_4_), channel_id=1, source_target_pairs={{0,16},{8,24},{16,0},{24,8},{1,17},{9,25},{17,1},{25,9},{2,18},{10... | collective-permute-start | bytes 196616 | tf_op jit(solution)/shard_map/ppermute | solution.py:385
  10.8 5.7 %collective-permute-start.5 = (bf16[2,128,128]{2,1,0:T(8,128)(2,1)S(1)}, bf16[2,128,128]{2,1,0:T(8,128)(2,1)S(1)}, u32[]{:S(2)}, u32[]{:S(2)}) collective-permute-start(bf16[2,128,128]{2,1,0:T(8,128)(2,1)S(1)} %pad_maximum_fusion.packed.refs_0_.refs_4_), channel_id=1, source_target_pairs={{0,8},{8,0},{16,24},{24,16},{1,9},{9,1},{17,25},{25,17},{2,10},{10... | collective-permute-start | bytes 196616 | tf_op jit(solution)/shard_map/ppermute | solution.py:385
  13.8 4.3 %collective-permute-start.7 = (bf16[2,128,128]{2,1,0:T(8,128)(2,1)S(1)}, bf16[2,128,128]{2,1,0:T(8,128)(2,1)S(1)}, u32[]{:S(2)}, u32[]{:S(2)}) collective-permute-start(bf16[2,128,128]{2,1,0:T(8,128)(2,1)S(1)} %collective-permute-done.6.refs_2_.refs_6_), channel_id=1, source_target_pairs={{0,8},{8,0},{16,24},{24,16},{1,9},{9,1},{17,25},{25,17},{2,10},{10... | collective-permute-start | bytes 196616 | tf_op jit(solution)/shard_map/ppermute | solution.py:385
  16.4 16.6 %copy-start.3 = (bf16[1024,128]{1,0:T(8,128)(2,1)S(1)}, bf16[1024,128]{1,0:T(8,128)(2,1)}, u32[]{:S(2)}) copy-start(bf16[1024,128]{1,0:T(8,128)(2,1)} %values.3) | copy-start | bytes 786436
  16.4 2.4 %collective-permute-start.4 = (f32[128,128]{1,0:T(8,128)S(1)}, f32[128,128]{1,0:T(8,128)S(1)}, u32[]{:S(2)}, u32[]{:S(2)}) collective-permute-start(f32[128,128]{1,0:T(8,128)S(1)} %get-tuple-element.47), channel_id=1, source_target_pairs={{0,1},{1,0},{2,3},{3,2},{4,5},{5,4},{6,7},{7,6},{8,9},{9,8},{10,11... | collective-permute-start | bytes 196616 | tf_op jit(solution)/shard_map/ppermute | solution.py:382
  19.0 7.0 %collective-permute-start.8 = (bf16[352,128]{1,0:T(8,128)(2,1)S(1)}, bf16[352,128]{1,0:T(8,128)(2,1)S(1)}, u32[]{:S(2)}, u32[]{:S(2)}) collective-permute-start(bf16[352,128]{1,0:T(8,128)(2,1)S(1)} %get-tuple-element.51), channel_id=1, source_target_pairs={{0,24},{8,16},{16,8},{24,0},{1,25},{9,17},{17,9},{25,1},{2,26},{10... | collective-permute-start | bytes 270344 | tf_op jit(solution)/shard_map/ppermute | solution.py:385
  22.9 6.6 %collective-permute-start.9 = (bf16[352,128]{1,0:T(8,128)(2,1)S(1)}, bf16[352,128]{1,0:T(8,128)(2,1)S(1)}, u32[]{:S(2)}, u32[]{:S(2)}) collective-permute-start(bf16[352,128]{1,0:T(8,128)(2,1)S(1)} %get-tuple-element.52), channel_id=1, source_target_pairs={{0,16},{8,24},{16,0},{24,8},{1,17},{9,25},{17,1},{25,9},{2,18},{10... | collective-permute-start | bytes 270344 | tf_op jit(solution)/shard_map/ppermute | solution.py:385
  22.9 6.6 %collective-permute-start.10 = (bf16[352,128]{1,0:T(8,128)(2,1)S(1)}, bf16[352,128]{1,0:T(8,128)(2,1)S(1)}, u32[]{:S(2)}, u32[]{:S(2)}) collective-permute-start(bf16[352,128]{1,0:T(8,128)(2,1)S(1)} %get-tuple-element.53), channel_id=1, source_target_pairs={{0,8},{8,0},{16,24},{24,16},{1,9},{9,1},{17,25},{25,17},{2,10},{10... | collective-permute-start | bytes 270344 | tf_op jit(solution)/shard_map/ppermute | solution.py:385
  29.5 12.0 %collective-permute-start.16 = (bf16[800,128]{1,0:T(8,128)(2,1)S(1)}, bf16[800,128]{1,0:T(8,128)(2,1)S(1)}, u32[]{:S(2)}, u32[]{:S(2)}) collective-permute-start(bf16[800,128]{1,0:T(8,128)(2,1)S(1)} %shard_map.133.refs_0_), channel_id=1, source_target_pairs={{0,6},{1,7},{2,4},{3,5},{4,2},{5,3},{6,0},{7,1},{8,14},{9,15},{10,... | collective-permute-start | bytes 614408 | tf_op jit(solution)/shard_map/ppermute | solution.py:378
  31.8 9.7 %collective-permute-start.15 = (bf16[800,128]{1,0:T(8,128)(2,1)S(1)}, bf16[800,128]{1,0:T(8,128)(2,1)S(1)}, u32[]{:S(2)}, u32[]{:S(2)}) collective-permute-start(bf16[800,128]{1,0:T(8,128)(2,1)S(1)} %shard_map.133.refs_0_), channel_id=1, source_target_pairs={{0,4},{1,5},{2,6},{3,7},{4,0},{5,1},{6,2},{7,3},{8,12},{9,13},{10,... | collective-permute-start | bytes 614408 | tf_op jit(solution)/shard_map/ppermute | solution.py:378
  32.5 9.0 %collective-permute-start.14 = (bf16[800,128]{1,0:T(8,128)(2,1)S(1)}, bf16[800,128]{1,0:T(8,128)(2,1)S(1)}, u32[]{:S(2)}, u32[]{:S(2)}) collective-permute-start(bf16[800,128]{1,0:T(8,128)(2,1)S(1)} %shard_map.133.refs_0_), channel_id=1, source_target_pairs={{0,2},{1,3},{2,0},{3,1},{4,6},{5,7},{6,4},{7,5},{8,10},{9,11},{10,... | collective-permute-start | bytes 614408 | tf_op jit(solution)/shard_map/ppermute | solution.py:378
  34.1 5.8 %collective-permute-start.11 = (bf16[128,128]{1,0:T(8,128)(2,1)S(1)}, bf16[128,128]{1,0:T(8,128)(2,1)S(1)}, u32[]{:S(2)}, u32[]{:S(2)}) collective-permute-start(bf16[128,128]{1,0:T(8,128)(2,1)S(1)} %get-tuple-element.55), channel_id=1, source_target_pairs={{0,24},{8,16},{16,8},{24,0},{1,25},{9,17},{17,9},{25,1},{2,26},{10... | collective-permute-start | bytes 98312 | tf_op jit(solution)/shard_map/ppermute | solution.py:385
  36.7 4.8 %collective-permute-start.12 = (bf16[128,128]{1,0:T(8,128)(2,1)S(1)}, bf16[128,128]{1,0:T(8,128)(2,1)S(1)}, u32[]{:S(2)}, u32[]{:S(2)}) collective-permute-start(bf16[128,128]{1,0:T(8,128)(2,1)S(1)} %get-tuple-element.56), channel_id=1, source_target_pairs={{0,16},{8,24},{16,0},{24,8},{1,17},{9,25},{17,1},{25,9},{2,18},{10... | collective-permute-start | bytes 98312 | tf_op jit(solution)/shard_map/ppermute | solution.py:385
  41.6 1.5 %collective-permute-start.17 = (bf16[800,128]{1,0:T(8,128)(2,1)S(1)}, bf16[800,128]{1,0:T(8,128)(2,1)S(1)}, u32[]{:S(2)}, u32[]{:S(2)}) collective-permute-start(bf16[800,128]{1,0:T(8,128)(2,1)S(1)} %shard_map.133.refs_0_), channel_id=1, source_target_pairs={{0,1},{1,0},{2,3},{3,2},{4,5},{5,4},{6,7},{7,6},{8,9},{9,8},{10,11... | collective-permute-start | bytes 614408 | tf_op jit(solution)/shard_map/ppermute | solution.py:382
  41.6 1.7 %collective-permute-start.18 = (bf16[800,128]{1,0:T(8,128)(2,1)S(1)}, bf16[800,128]{1,0:T(8,128)(2,1)S(1)}, u32[]{:S(2)}, u32[]{:S(2)}) collective-permute-start(bf16[800,128]{1,0:T(8,128)(2,1)S(1)} %collective-permute-done.14.refs_1_), channel_id=1, source_target_pairs={{0,1},{1,0},{2,3},{3,2},{4,5},{5,4},{6,7},{7,6},{8,9},{9,8},{10,11... | collective-permute-start | bytes 614408 | tf_op jit(solution)/shard_map/ppermute | solution.py:382
  42.1 1.5 %collective-permute-start.19 = (bf16[800,128]{1,0:T(8,128)(2,1)S(1)}, bf16[800,128]{1,0:T(8,128)(2,1)S(1)}, u32[]{:S(2)}, u32[]{:S(2)}) collective-permute-start(bf16[800,128]{1,0:T(8,128)(2,1)S(1)} %collective-permute-done.15.refs_2_), channel_id=1, source_target_pairs={{0,1},{1,0},{2,3},{3,2},{4,5},{5,4},{6,7},{7,6},{8,9},{9,8},{10,11... | collective-permute-start | bytes 614408 | tf_op jit(solution)/shard_map/ppermute | solution.py:382
  42.2 1.7 %collective-permute-start.20 = (bf16[800,128]{1,0:T(8,128)(2,1)S(1)}, bf16[800,128]{1,0:T(8,128)(2,1)S(1)}, u32[]{:S(2)}, u32[]{:S(2)}) collective-permute-start(bf16[800,128]{1,0:T(8,128)(2,1)S(1)} %collective-permute-done.16.refs_3_), channel_id=1, source_target_pairs={{0,1},{1,0},{2,3},{3,2},{4,5},{5,4},{6,7},{7,6},{8,9},{9,8},{10,11... | collective-permute-start | bytes 614408 | tf_op jit(solution)/shard_map/ppermute | solution.py:382
  42.6 3.9 %collective-permute-start.13 = (bf16[128,128]{1,0:T(8,128)(2,1)S(1)}, bf16[128,128]{1,0:T(8,128)(2,1)S(1)}, u32[]{:S(2)}, u32[]{:S(2)}) collective-permute-start(bf16[128,128]{1,0:T(8,128)(2,1)S(1)} %get-tuple-element.59), channel_id=1, source_target_pairs={{0,8},{8,0},{16,24},{24,16},{1,9},{9,1},{17,25},{25,17},{2,10},{10... | collective-permute-start | bytes 98312 | tf_op jit(solution)/shard_map/ppermute | solution.py:385
  (5 other events, 31.7 us)

commit v17 on v13

--- a/solution.py
+++ b/solution.py
@@ -25,9 +25,9 @@
     )
 
 
-def two_first(blocks):
+def last_swapped(blocks):
     blocks = list(blocks)
-    return blocks[:1] + blocks[2:3] + blocks[1:2] + blocks[3:]
+    return blocks[:-2] + blocks[:-3:-1]
 
 
 def place():
@@ -44,15 +44,13 @@
     return lambda frame: sum((frame >= bound).astype(jnp.int32) for bound in bounds)
 
 
-def cut_kernel(chips, weight_in, saved_in, kept, sent, sems):
+def fetch_kernel(chips, weight_in, grad_in, kept, grad, sems):
     _, chip, core = place()
     width = kept.shape[2]
-    moves = [(saved_in, sent.at[:, chips * width : chips * width + HD])]
+    copies = [pltpu.make_async_copy(grad_in, grad, sems.at[chips])]
     for k in range(chips):
-        for c, out in ((1 - core, sent.at[:, k * width : (k + 1) * width]), (core, kept.at[k])):
-            columns = pl.ds(pl.multiple_of((2 * (chip ^ k) + c) * width, LANES), width)
-            moves.append((weight_in.at[:, columns], out))
-    copies = [pltpu.make_async_copy(a, b, sems.at[i]) for i, (a, b) in enumerate(moves)]
+        columns = pl.ds(pl.multiple_of((2 * (chip ^ k) + core) * width, LANES), width)
+        copies.append(pltpu.make_async_copy(weight_in.at[:, columns], kept.at[k], sems.at[k]))
     for copy in copies:
         copy.start()
     for copy in copies:
@@ -105,15 +103,16 @@
             out[n_t + p + i : n_t + p + i + 1, :] = total[:, i * rows : (i + 1) * rows]
 
 
-def head_kernel(chips, frames, packed, kept, received, gate_a, *refs):
+def head_kernel(chips, frames, packed, other_saved, kept, received, gate_a, *refs):
     pieces, (mine, other, terms) = refs[:chips], refs[chips:]
-    _, chip, _ = place()
+    _, chip, core = place()
     width = pieces[0].shape[1]
     tiles = width // LANES
-    saved = jnp.concatenate([packed[1], received[:, chips * width : chips * width + HD]], axis=1)
+    saved = jnp.concatenate([packed[1], other_saved[...]], axis=1)
     head = None
     for k in range(chips):
-        weight = jnp.concatenate([kept[k], received[:, k * width : (k + 1) * width]], axis=0)
+        columns = pl.ds(pl.multiple_of((2 * (chip ^ k) + core) * width, LANES), width)
+        weight = jnp.concatenate([kept[k], received[:, columns]], axis=0)
         wide = pieces[k][...].astype(jnp.float32)
         gated = jnp.concatenate(
             [
@@ -172,7 +171,7 @@
 
 
 def bundle_kernel(n_t, starts, count, gate_b, *refs):
-    heads, out = two_first(refs[:n_t]), refs[n_t]
+    heads, out = last_swapped(refs[:n_t]), refs[n_t]
     tiles = gate_b.shape[2] // LANES
     part = (starts[2] - starts[1]) // tiles
     wide = [heads[k][starts[1] : starts[2], :].astype(jnp.float32) for k in range(n_t)]
@@ -410,19 +409,22 @@
         return [messages[0]] + [got[k] for k in range(1, n_t)]
 
     pieces = over_chips(out_grad)
-    kept, sent = call(
-        functools.partial(cut_kernel, chips),
-        [proj_weight, saved_out],
-        [shape(bf16, chips, HD, width), shape(bf16, HD, chips * width + HD)],
-        [pltpu.SemaphoreType.DMA((2 * chips + 1,))],
-        in_place=True,
-    )
-    received = over_cores(sent)
-    packed, _ = lax.optimization_barrier((jnp.stack([queries, saved_out]), received))
+    received, other_saved = over_cores(proj_weight), over_cores(saved_out)
+    packed, _ = lax.optimization_barrier(
+        (jnp.stack([queries, saved_out]), (received, other_saved))
+    )
     packed_all = [packed]
     for k in range(1, n_t):
         low = k & -k
         packed_all.append(over_time(packed_all[k - low], low))
+    (to_fetch, own_grad), _ = lax.optimization_barrier(((proj_weight, out_grad), received))
+    kept, pieces[0] = call(
+        functools.partial(fetch_kernel, chips),
+        [to_fetch, own_grad],
+        [shape(bf16, chips, HD, width), shape(bf16, rows, width)],
+        [pltpu.SemaphoreType.DMA((chips + 1,))],
+        in_place=True,
+    )
     gate_table, _ = lax.optimization_barrier((gate_table, received))
     bias, gate_a, gate_b, hot = call(
         functools.partial(masks_kernel, n_t, chips, frames, rows),
@@ -437,7 +439,7 @@
     )
     mine, other, terms = call(
         functools.partial(head_kernel, chips, frames),
-        [packed, kept, received, gate_a] + pieces,
+        [packed, other_saved, kept, received, gate_a] + pieces,
         [shape(f32, rows, HD), shape(f32, rows, HD), shape(f32, count, LANES)],
         flops=4 * rows * chips * width * 2 * HD,
     )
@@ -458,7 +460,7 @@
     base = tiles * n_t * part
     bundle = call(
         functools.partial(bundle_kernel, n_t, starts, count),
-        [gate_b] + two_first(heads_all),
+        [gate_b] + last_swapped(heads_all),
         shape(bf16, base + n_t * count, LANES),
     )
     bundles = over_chips(bundle)

time: 46.8 us -> 46.5 us (level)
  other arithmetic: 0.01 us -> 0.78 us
  starting transfers between devices: 21.4 us -> 20.7 us
    ppermute x6, waiting for transfers between devices: 0.92 us -> 0.02 us  [over_chips(): lax.ppermute(x, 'space', [(s, s ^ 2 * k) for s in range(n_s)])]
    another operation x1, other arithmetic: 0.01 us -> 0.78 us  [body(): jnp.stack([queries, saved_out])]
    ppermute x9, starting transfers between devices: 13.1 us -> 12.4 us  [over_time(): return lax.ppermute(x, 'tm', [(t, t ^ k) for t in range(n_t)])]
    ppermute x3 -> x4, waiting for transfers between devices: 1.73 us -> 2.36 us  [over_cores(): return lax.ppermute(x, 'space', [(s, s ^ 1) for s in range(n_s)])]
    unnamed x16 -> x12, local copies, waits for them, and re-layouts: 0.84 us -> 0.94 us
  transfers between devices with their start and end apart: 18 -> 19, of which waited for: 9 -> 8; matrix products, arithmetic and copies ran while one was open for 0% -> 2% of each run, Pallas kernels for 14% -> 17%
where the time goes in v17:
time: 46.5 us; the launch traced here: 46.3 us
  starting transfers between devices  20.7 us (45%)
  waiting for transfers between devices  14.2 us (31%)
  Pallas kernels  8.87 us (19%)
  local copies, waits for them, and re-layouts  0.94 us (2%)
  between operations  0.81 us (2%)
  other arithmetic  0.78 us (2%)
    ppermute x9, starting transfers between devices, over_time(): return lax.ppermute(x, 'tm', [(t, t ^ k) for t in range(n_t)])  12.4 us
    ppermute x9, waiting for transfers between devices, over_time(): return lax.ppermute(x, 'tm', [(t, t ^ k) for t in range(n_t)])  11.8 us
    pallas_call x12, Pallas kernels, call(): pl.pallas_call(kernel, out_shape=out_shape, in_specs=[pl.BlockSpec(memory...  8.87 us
    ppermute x6, starting transfers between devices, over_chips(): lax.ppermute(x, 'space', [(s, s ^ 2 * k) for s in range(n_s)])  7.66 us
    ppermute x4, waiting for transfers between devices, over_cores(): return lax.ppermute(x, 'space', [(s, s ^ 1) for s in range(n_s)])  2.36 us
    unnamed x12, local copies, waits for them, and re-layouts  0.94 us
  transfers between devices with their start and end apart: 19, of which 8 were waited for; matrix products, arithmetic and copies ran while one was open for 2% of the time, Pallas kernels for 17%

profile of v17, /device:TPU:0, one launch (start us, length us, event | category | flops | bytes accessed | tf_op | source)
XLA Modules:
  0.0 46.3 jit_solution(11265390393784011871)
XLA Ops:
  1.2 2.6 %collective-permute-start.2 = (bf16[128,640]{1,0:T(8,128)(2,1)}, bf16[128,640]{1,0:T(8,128)(2,1)S(1)}, u32[]{:S(2)}, u32[]{:S(2)}) collective-permute-start(bf16[128,640]{1,0:T(8,128)(2,1)} %grad_in), channel_id=1, source_target_pairs={{0,2},{1,3},{2,0},{3,1},{4,6},{5,7},{6,4},{7,5},{8,10},{9,11},{10,... | collective-permute-start | bytes 491528 | tf_op jit(solution)/shard_map/ppermute | solution.py:393
  3.7 1.5 %collective-permute-start.3 = (bf16[128,640]{1,0:T(8,128)(2,1)}, bf16[128,640]{1,0:T(8,128)(2,1)S(1)}, u32[]{:S(2)}, u32[]{:S(2)}) collective-permute-start(bf16[128,640]{1,0:T(8,128)(2,1)} %grad_in), channel_id=1, source_target_pairs={{0,4},{1,5},{2,6},{3,7},{4,0},{5,1},{6,2},{7,3},{8,12},{9,13},{10,... | collective-permute-start | bytes 491528 | tf_op jit(solution)/shard_map/ppermute | solution.py:393
  5.3 0.8 %pad_maximum_fusion.packed.refs_0_ = bf16[2,128,128]{2,1,0:T(8,128)(2,1)S(1)} fusion(bf16[1,128,128]{2,1,0:T(8,128)(2,1)} %bitcast.3, bf16[1,128,128]{2,1,0:T(8,128)(2,1)} %bitcast.2), kind=kLoop, calls=%fused_computation | loop fusion | flops 32768 | bytes 131072 | tf_op jit(solution)/shard_map/stack | solution.py:414
  6.7 3.0 %collective-permute-start.7 = (bf16[2,128,128]{2,1,0:T(8,128)(2,1)S(1)}, bf16[2,128,128]{2,1,0:T(8,128)(2,1)S(1)}, u32[]{:S(2)}, u32[]{:S(2)}) collective-permute-start(bf16[2,128,128]{2,1,0:T(8,128)(2,1)S(1)} %pad_maximum_fusion.packed.refs_0_), channel_id=1, source_target_pairs={{0,16},{8,24},{16,0},{24,8},{1,17},{9,25},{17,1},{25,9},{2,18},{10... | collective-permute-start | bytes 196616 | tf_op jit(solution)/shard_map/ppermute | solution.py:400
  9.7 1.6 %collective-permute-start.6 = (bf16[2,128,128]{2,1,0:T(8,128)(2,1)S(1)}, bf16[2,128,128]{2,1,0:T(8,128)(2,1)S(1)}, u32[]{:S(2)}, u32[]{:S(2)}) collective-permute-start(bf16[2,128,128]{2,1,0:T(8,128)(2,1)S(1)} %pad_maximum_fusion.packed.refs_0_), channel_id=1, source_target_pairs={{0,8},{8,0},{16,24},{24,16},{1,9},{9,1},{17,25},{25,17},{2,10},{10... | collective-permute-start | bytes 196616 | tf_op jit(solution)/shard_map/ppermute | solution.py:400
  11.3 0.9 %copy-done.3 = bf16[128,640]{1,0:T(8,128)(2,1)S(1)} copy-done((bf16[128,640]{1,0:T(8,128)(2,1)S(1)}, bf16[128,640]{1,0:T(8,128)(2,1)}, u32[]{:S(2)}) %copy-start.3) | copy-done | bytes 163864
  12.2 1.4 %shard_map.129 = (bf16[4,128,640]{2,1,0:T(8,128)(2,1)S(1)}, bf16[128,640]{1,0:T(8,128)(2,1)S(1)}) custom-call(bf16[128,5120]{1,0:T(8,128)(2,1)} %weight_in, bf16[128,640]{1,0:T(8,128)(2,1)S(1)} %copy-done.3), custom_call_target="tpu_custom_call" | custom-call | bytes 1474560 | tf_op jit(solution)/shard_map/pallas_call | solution.py:348
  14.9 0.8 %shard_map.130 = (f32[128,128]{1,0:T(8,128)S(1)}, f32[128,128]{1,0:T(8,128)S(1)}, f32[40,128]{1,0:T(8,128)S(1)}) custom-call(bf16[2,128,128]{2,1,0:T(8,128)(2,1)S(1)} %pad_maximum_fusion.packed.refs_0_, bf16[128,128]{1,0:T(8,128)(2,1)S(1)} %collective-permute-done.1.other_saved, bf16[4,128,640]{2,1,0:T(8,128)(2,1)S(1)} %get-tuple-element.47.kept, ...), custom_call_target="tpu_custom_call" | custom-call | flops 335544320 | bytes 2740224 | tf_op jit(solution)/shard_map/pallas_call | solution.py:348
  15.7 2.9 %collective-permute-done.8.refs_3_ = bf16[2,128,128]{2,1,0:T(8,128)(2,1)S(1)} collective-permute-done((bf16[2,128,128]{2,1,0:T(8,128)(2,1)S(1)}, bf16[2,128,128]{2,1,0:T(8,128)(2,1)S(1)}, u32[]{:S(2)}, u32[]{:S(2)}) %collective-permute-start.8) | collective-permute-done | bytes 65568 | tf_op jit(solution)/shard_map/ppermute | solution.py:400
  18.7 0.8 %shard_map.131.stats = f32[8,128]{1,0:T(8,128)S(1)} custom-call(f32[2,512]{1,0:T(2,128)S(1)} %get-tuple-element.58.bias, bf16[1024,128]{1,0:T(8,128)(2,1)S(1)} %copy-done, bf16[2,128,128]{2,1,0:T(8,128)(2,1)S(1)} %pad_maximum_fusion.packed.refs_0_, bf16[2,128,128]{2,1,0:T(8,128)(2,1)S(1)} %collective-permute-done.6.refs_1_, ...), custom_call_target="tpu_custom_call" | custom-call | flops 134217728 | bytes 528384 | tf_op jit(solution)/shard_map/pallas_call | solution.py:348
  19.6 2.8 %collective-permute-start.10 = (bf16[352,128]{1,0:T(8,128)(2,1)S(1)}, bf16[352,128]{1,0:T(8,128)(2,1)S(1)}, u32[]{:S(2)}, u32[]{:S(2)}) collective-permute-start(bf16[352,128]{1,0:T(8,128)(2,1)S(1)} %get-tuple-element.56), channel_id=1, source_target_pairs={{0,24},{8,16},{16,8},{24,0},{1,25},{9,17},{17,9},{25,1},{2,26},{10... | collective-permute-start | bytes 270344 | tf_op jit(solution)/shard_map/ppermute | solution.py:400
  22.4 1.7 %collective-permute-start.9 = (bf16[352,128]{1,0:T(8,128)(2,1)S(1)}, bf16[352,128]{1,0:T(8,128)(2,1)S(1)}, u32[]{:S(2)}, u32[]{:S(2)}) collective-permute-start(bf16[352,128]{1,0:T(8,128)(2,1)S(1)} %get-tuple-element.55), channel_id=1, source_target_pairs={{0,8},{8,0},{16,24},{24,16},{1,9},{9,1},{17,25},{25,17},{2,10},{10... | collective-permute-start | bytes 270344 | tf_op jit(solution)/shard_map/ppermute | solution.py:400
  24.1 2.4 %collective-permute-done.10.refs_2_.refs_4_ = bf16[352,128]{1,0:T(8,128)(2,1)S(1)} collective-permute-done((bf16[352,128]{1,0:T(8,128)(2,1)S(1)}, bf16[352,128]{1,0:T(8,128)(2,1)S(1)}, u32[]{:S(2)}, u32[]{:S(2)}) %collective-permute-start.10) | collective-permute-done | bytes 90144 | tf_op jit(solution)/shard_map/ppermute | solution.py:400
  26.4 2.8 %collective-permute-done.11.refs_3_.refs_5_ = bf16[352,128]{1,0:T(8,128)(2,1)S(1)} collective-permute-done((bf16[352,128]{1,0:T(8,128)(2,1)S(1)}, bf16[352,128]{1,0:T(8,128)(2,1)S(1)}, u32[]{:S(2)}, u32[]{:S(2)}) %collective-permute-start.11) | collective-permute-done | bytes 90144 | tf_op jit(solution)/shard_map/ppermute | solution.py:400
  29.3 1.6 %collective-permute-start.15 = (bf16[800,128]{1,0:T(8,128)(2,1)S(1)}, bf16[800,128]{1,0:T(8,128)(2,1)S(1)}, u32[]{:S(2)}, u32[]{:S(2)}) collective-permute-start(bf16[800,128]{1,0:T(8,128)(2,1)S(1)} %shard_map.133.refs_0_), channel_id=1, source_target_pairs={{0,2},{1,3},{2,0},{3,1},{4,6},{5,7},{6,4},{7,5},{8,10},{9,11},{10,... | collective-permute-start | bytes 614408 | tf_op jit(solution)/shard_map/ppermute | solution.py:393
  30.9 1.5 %collective-permute-start.16 = (bf16[800,128]{1,0:T(8,128)(2,1)S(1)}, bf16[800,128]{1,0:T(8,128)(2,1)S(1)}, u32[]{:S(2)}, u32[]{:S(2)}) collective-permute-start(bf16[800,128]{1,0:T(8,128)(2,1)S(1)} %shard_map.133.refs_0_), channel_id=1, source_target_pairs={{0,4},{1,5},{2,6},{3,7},{4,0},{5,1},{6,2},{7,3},{8,12},{9,13},{10,... | collective-permute-start | bytes 614408 | tf_op jit(solution)/shard_map/ppermute | solution.py:393
  32.9 1.0 %shard_map.134 = (f32[1024,128]{1,0:T(8,128)S(1)}, f32[1024,128]{1,0:T(8,128)S(1)}, bf16[128,128]{1,0:T(8,128)(2,1)S(1)}, bf16[128,128]{1,0:T(8,128)(2,1)S(1)}) custom-call(f32[2,512]{1,0:T(2,128)S(1)} %get-tuple-element.58.bias, bf16[1024,128]{1,0:T(8,128)(2,1)S(1)} %copy-done, bf16[1024,128]{1,0:T(8,128)(2,1)S(1)} %copy-done.2, ...), custom_call_target="tpu_custom_call" | custom-call | flops 335544320 | bytes 1150976 | tf_op jit(solution)/shard_map/pallas_call | solution.py:348
  33.8 2.7 %collective-permute-start.12 = (bf16[128,128]{1,0:T(8,128)(2,1)S(1)}, bf16[128,128]{1,0:T(8,128)(2,1)S(1)}, u32[]{:S(2)}, u32[]{:S(2)}) collective-permute-start(bf16[128,128]{1,0:T(8,128)(2,1)S(1)} %get-tuple-element.59), channel_id=1, source_target_pairs={{0,24},{8,16},{16,8},{24,0},{1,25},{9,17},{17,9},{25,1},{2,26},{10... | collective-permute-start | bytes 98312 | tf_op jit(solution)/shard_map/ppermute | solution.py:400
  36.6 1.7 %shard_map.135 = (bf16[1024,128]{1,0:T(8,128)(2,1)}, bf16[1024,128]{1,0:T(8,128)(2,1)}, bf16[128,128]{1,0:T(8,128)(2,1)S(1)}, bf16[128,128]{1,0:T(8,128)(2,1)S(1)}) custom-call(f32[2,512]{1,0:T(2,128)S(1)} %get-tuple-element.58.bias, bf16[1024,128]{1,0:T(8,128)(2,1)S(1)} %copy-done, bf16[1024,128]{1,0:T(8,128)(2,1)S(1)} %copy-done.2, ...), custom_call_target="tpu_custom_call" | custom-call | flops 335544320 | bytes 2199552 | tf_op jit(solution)/shard_map/pallas_call | solution.py:348
  38.2 1.4 %collective-permute-done.12.refs_0_ = bf16[128,128]{1,0:T(8,128)(2,1)S(1)} collective-permute-done((bf16[128,128]{1,0:T(8,128)(2,1)S(1)}, bf16[128,128]{1,0:T(8,128)(2,1)S(1)}, u32[]{:S(2)}, u32[]{:S(2)}) %collective-permute-start.12) | collective-permute-done | bytes 32800 | tf_op jit(solution)/shard_map/ppermute | solution.py:400
  39.6 1.7 %collective-permute-done.13.refs_1_ = bf16[128,128]{1,0:T(8,128)(2,1)S(1)} collective-permute-done((bf16[128,128]{1,0:T(8,128)(2,1)S(1)}, bf16[128,128]{1,0:T(8,128)(2,1)S(1)}, u32[]{:S(2)}, u32[]{:S(2)}) %collective-permute-start.13) | collective-permute-done | bytes 32800 | tf_op jit(solution)/shard_map/ppermute | solution.py:400
  42.0 1.7 %collective-permute-done.18.other = bf16[2880,128]{1,0:T(8,128)(2,1)S(1)} collective-permute-done((bf16[2880,128]{1,0:T(8,128)(2,1)S(1)}, bf16[2880,128]{1,0:T(8,128)(2,1)S(1)}, u32[]{:S(2)}, u32[]{:S(2)}) %collective-permute-start.18) | collective-permute-done | bytes 737312 | tf_op jit(solution)/shard_map/ppermute | solution.py:397
  43.8 1.3 %shard_map.138 = (f32[128,1280]{1,0:T(8,128)}, f32[16,5120]{1,0:T(8,128)}) custom-call(f32[8,16,128]{2,1,0:T(8,128)S(1)} %get-tuple-element.65.hot, bf16[2880,128]{1,0:T(8,128)(2,1)S(1)} %collective-permute-done.18.other, f32[128,640]{1,0:T(8,128)S(1)} %get-tuple-element.71.own_weight, f32[16,2560]{1,0:T(8,128)S(1)} %get-tuple-element.72.own_gate, ...), custom_call_target="tpu_custom_call" | custom-call | flops 83886080 | bytes 1556480 | tf_op jit(solution)/shard_map/pallas_call | solution.py:348
  45.5 0.7 %shard_map.139 = bf16[128,128]{1,0:T(8,128)(2,1)} custom-call(bf16[128,128]{1,0:T(8,128)(2,1)S(1)} %collective-permute-done.12.refs_0_, bf16[128,128]{1,0:T(8,128)(2,1)S(1)} %collective-permute-done.13.refs_1_, bf16[128,128]{1,0:T(8,128)(2,1)S(1)} %collective-permute-done.14.refs_2_, bf16[128,128]{1,0:T(8,128)(2,1)S(1)} %get-tuple-element.74.refs_3_), custom_call_target="tpu_custom_call" | custom-call | bytes 131072 | tf_op jit(solution)/shard_map/pallas_call | solution.py:348
  (39 shorter events, 4.2 us)
Async XLA Ops:
  0.6 13.0 %copy-start.1 = (f32[16,5120]{1,0:T(8,128)S(1)}, f32[16,5120]{1,0:T(8,128)}, u32[]{:S(2)}) copy-start(f32[16,5120]{1,0:T(8,128)} %gate) | copy-start | bytes 983044
  0.6 6.1 %collective-permute-start = (bf16[128,5120]{1,0:T(8,128)(2,1)}, bf16[128,5120]{1,0:T(8,128)(2,1)S(1)}, u32[]{:S(2)}, u32[]{:S(2)}) collective-permute-start(bf16[128,5120]{1,0:T(8,128)(2,1)} %weight_in), channel_id=1, source_target_pairs={{0,1},{1,0},{2,3},{3,2},{4,5},{5,4},{6,7},{7,6},{8,9},{9,8},{10,11... | collective-permute-start | bytes 3932168 | tf_op jit(solution)/shard_map/ppermute | solution.py:397
  1.2 13.7 %collective-permute-start.2 = (bf16[128,640]{1,0:T(8,128)(2,1)}, bf16[128,640]{1,0:T(8,128)(2,1)S(1)}, u32[]{:S(2)}, u32[]{:S(2)}) collective-permute-start(bf16[128,640]{1,0:T(8,128)(2,1)} %grad_in), channel_id=1, source_target_pairs={{0,2},{1,3},{2,0},{3,1},{4,6},{5,7},{6,4},{7,5},{8,10},{9,11},{10,... | collective-permute-start | bytes 491528 | tf_op jit(solution)/shard_map/ppermute | solution.py:393
  3.7 11.1 %collective-permute-start.3 = (bf16[128,640]{1,0:T(8,128)(2,1)}, bf16[128,640]{1,0:T(8,128)(2,1)S(1)}, u32[]{:S(2)}, u32[]{:S(2)}) collective-permute-start(bf16[128,640]{1,0:T(8,128)(2,1)} %grad_in), channel_id=1, source_target_pairs={{0,4},{1,5},{2,6},{3,7},{4,0},{5,1},{6,2},{7,3},{8,12},{9,13},{10,... | collective-permute-start | bytes 491528 | tf_op jit(solution)/shard_map/ppermute | solution.py:393
  5.2 9.6 %collective-permute-start.4 = (bf16[128,640]{1,0:T(8,128)(2,1)}, bf16[128,640]{1,0:T(8,128)(2,1)S(1)}, u32[]{:S(2)}, u32[]{:S(2)}) collective-permute-start(bf16[128,640]{1,0:T(8,128)(2,1)} %grad_in), channel_id=1, source_target_pairs={{0,6},{1,7},{2,4},{3,5},{4,2},{5,3},{6,0},{7,1},{8,14},{9,15},{10,... | collective-permute-start | bytes 491528 | tf_op jit(solution)/shard_map/ppermute | solution.py:393
  5.3 1.4 %collective-permute-start.1 = (bf16[128,128]{1,0:T(8,128)(2,1)}, bf16[128,128]{1,0:T(8,128)(2,1)S(1)}, u32[]{:S(2)}, u32[]{:S(2)}) collective-permute-start(bf16[128,128]{1,0:T(8,128)(2,1)} %param.12), channel_id=1, source_target_pairs={{0,1},{1,0},{2,3},{3,2},{4,5},{5,4},{6,7},{7,6},{8,9},{9,8},{10,11... | collective-permute-start | bytes 98312 | tf_op jit(solution)/shard_map/ppermute | solution.py:397
  6.7 7.6 %collective-permute-start.7 = (bf16[2,128,128]{2,1,0:T(8,128)(2,1)S(1)}, bf16[2,128,128]{2,1,0:T(8,128)(2,1)S(1)}, u32[]{:S(2)}, u32[]{:S(2)}) collective-permute-start(bf16[2,128,128]{2,1,0:T(8,128)(2,1)S(1)} %pad_maximum_fusion.packed.refs_0_), channel_id=1, source_target_pairs={{0,16},{8,24},{16,0},{24,8},{1,17},{9,25},{17,1},{25,9},{2,18},{10... | collective-permute-start | bytes 196616 | tf_op jit(solution)/shard_map/ppermute | solution.py:400
  9.7 6.0 %collective-permute-start.6 = (bf16[2,128,128]{2,1,0:T(8,128)(2,1)S(1)}, bf16[2,128,128]{2,1,0:T(8,128)(2,1)S(1)}, u32[]{:S(2)}, u32[]{:S(2)}) collective-permute-start(bf16[2,128,128]{2,1,0:T(8,128)(2,1)S(1)} %pad_maximum_fusion.packed.refs_0_), channel_id=1, source_target_pairs={{0,8},{8,0},{16,24},{24,16},{1,9},{9,1},{17,25},{25,17},{2,10},{10... | collective-permute-start | bytes 196616 | tf_op jit(solution)/shard_map/ppermute | solution.py:400
  12.2 1.4 %copy-start.4 = (s32[8]{0:T(128)S(1)}, s32[8]{0:T(128)}, u32[]{:S(2)}) copy-start(s32[8]{0:T(128)} %levels.1) | copy-start | bytes 100
  12.2 1.4 %copy-start.5 = (s32[4]{0:T(128)S(1)}, s32[4]{0:T(128)}, u32[]{:S(2)}) copy-start(s32[4]{0:T(128)} %clips.1) | copy-start | bytes 52
  14.3 4.3 %collective-permute-start.8 = (bf16[2,128,128]{2,1,0:T(8,128)(2,1)S(1)}, bf16[2,128,128]{2,1,0:T(8,128)(2,1)S(1)}, u32[]{:S(2)}, u32[]{:S(2)}) collective-permute-start(bf16[2,128,128]{2,1,0:T(8,128)(2,1)S(1)} %collective-permute-done.7.refs_2_), channel_id=1, source_target_pairs={{0,8},{8,0},{16,24},{24,16},{1,9},{9,1},{17,25},{25,17},{2,10},{10... | collective-permute-start | bytes 196616 | tf_op jit(solution)/shard_map/ppermute | solution.py:400
  14.9 3.8 %copy-start = (bf16[1024,128]{1,0:T(8,128)(2,1)S(1)}, bf16[1024,128]{1,0:T(8,128)(2,1)}, u32[]{:S(2)}) copy-start(bf16[1024,128]{1,0:T(8,128)(2,1)} %keys.5) | copy-start | bytes 786436
  15.6 17.2 %copy-start.2 = (bf16[1024,128]{1,0:T(8,128)(2,1)S(1)}, bf16[1024,128]{1,0:T(8,128)(2,1)}, u32[]{:S(2)}) copy-start(bf16[1024,128]{1,0:T(8,128)(2,1)} %values.3) | copy-start | bytes 786436
  15.7 3.8 %collective-permute-start.5 = (f32[128,128]{1,0:T(8,128)S(1)}, f32[128,128]{1,0:T(8,128)S(1)}, u32[]{:S(2)}, u32[]{:S(2)}) collective-permute-start(f32[128,128]{1,0:T(8,128)S(1)} %get-tuple-element.51), channel_id=1, source_target_pairs={{0,1},{1,0},{2,3},{3,2},{4,5},{5,4},{6,7},{7,6},{8,9},{9,8},{10,11... | collective-permute-start | bytes 196616 | tf_op jit(solution)/shard_map/ppermute | solution.py:397
  19.6 6.8 %collective-permute-start.10 = (bf16[352,128]{1,0:T(8,128)(2,1)S(1)}, bf16[352,128]{1,0:T(8,128)(2,1)S(1)}, u32[]{:S(2)}, u32[]{:S(2)}) collective-permute-start(bf16[352,128]{1,0:T(8,128)(2,1)S(1)} %get-tuple-element.56), channel_id=1, source_target_pairs={{0,24},{8,16},{16,8},{24,0},{1,25},{9,17},{17,9},{25,1},{2,26},{10... | collective-permute-start | bytes 270344 | tf_op jit(solution)/shard_map/ppermute | solution.py:400
  22.4 6.9 %collective-permute-start.11 = (bf16[352,128]{1,0:T(8,128)(2,1)S(1)}, bf16[352,128]{1,0:T(8,128)(2,1)S(1)}, u32[]{:S(2)}, u32[]{:S(2)}) collective-permute-start(bf16[352,128]{1,0:T(8,128)(2,1)S(1)} %get-tuple-element.57), channel_id=1, source_target_pairs={{0,16},{8,24},{16,0},{24,8},{1,17},{9,25},{17,1},{25,9},{2,18},{10... | collective-permute-start | bytes 270344 | tf_op jit(solution)/shard_map/ppermute | solution.py:400
  22.4 6.9 %collective-permute-start.9 = (bf16[352,128]{1,0:T(8,128)(2,1)S(1)}, bf16[352,128]{1,0:T(8,128)(2,1)S(1)}, u32[]{:S(2)}, u32[]{:S(2)}) collective-permute-start(bf16[352,128]{1,0:T(8,128)(2,1)S(1)} %get-tuple-element.55), channel_id=1, source_target_pairs={{0,8},{8,0},{16,24},{24,16},{1,9},{9,1},{17,25},{25,17},{2,10},{10... | collective-permute-start | bytes 270344 | tf_op jit(solution)/shard_map/ppermute | solution.py:400
  29.3 12.1 %collective-permute-start.15 = (bf16[800,128]{1,0:T(8,128)(2,1)S(1)}, bf16[800,128]{1,0:T(8,128)(2,1)S(1)}, u32[]{:S(2)}, u32[]{:S(2)}) collective-permute-start(bf16[800,128]{1,0:T(8,128)(2,1)S(1)} %shard_map.133.refs_0_), channel_id=1, source_target_pairs={{0,2},{1,3},{2,0},{3,1},{4,6},{5,7},{6,4},{7,5},{8,10},{9,11},{10,... | collective-permute-start | bytes 614408 | tf_op jit(solution)/shard_map/ppermute | solution.py:393
  30.9 10.5 %collective-permute-start.16 = (bf16[800,128]{1,0:T(8,128)(2,1)S(1)}, bf16[800,128]{1,0:T(8,128)(2,1)S(1)}, u32[]{:S(2)}, u32[]{:S(2)}) collective-permute-start(bf16[800,128]{1,0:T(8,128)(2,1)S(1)} %shard_map.133.refs_0_), channel_id=1, source_target_pairs={{0,4},{1,5},{2,6},{3,7},{4,0},{5,1},{6,2},{7,3},{8,12},{9,13},{10,... | collective-permute-start | bytes 614408 | tf_op jit(solution)/shard_map/ppermute | solution.py:393
  32.4 9.0 %collective-permute-start.17 = (bf16[800,128]{1,0:T(8,128)(2,1)S(1)}, bf16[800,128]{1,0:T(8,128)(2,1)S(1)}, u32[]{:S(2)}, u32[]{:S(2)}) collective-permute-start(bf16[800,128]{1,0:T(8,128)(2,1)S(1)} %shard_map.133.refs_0_), channel_id=1, source_target_pairs={{0,6},{1,7},{2,4},{3,5},{4,2},{5,3},{6,0},{7,1},{8,14},{9,15},{10,... | collective-permute-start | bytes 614408 | tf_op jit(solution)/shard_map/ppermute | solution.py:393
  33.8 5.8 %collective-permute-start.12 = (bf16[128,128]{1,0:T(8,128)(2,1)S(1)}, bf16[128,128]{1,0:T(8,128)(2,1)S(1)}, u32[]{:S(2)}, u32[]{:S(2)}) collective-permute-start(bf16[128,128]{1,0:T(8,128)(2,1)S(1)} %get-tuple-element.59), channel_id=1, source_target_pairs={{0,24},{8,16},{16,8},{24,0},{1,25},{9,17},{17,9},{25,1},{2,26},{10... | collective-permute-start | bytes 98312 | tf_op jit(solution)/shard_map/ppermute | solution.py:400
  36.5 4.8 %collective-permute-start.13 = (bf16[128,128]{1,0:T(8,128)(2,1)S(1)}, bf16[128,128]{1,0:T(8,128)(2,1)S(1)}, u32[]{:S(2)}, u32[]{:S(2)}) collective-permute-start(bf16[128,128]{1,0:T(8,128)(2,1)S(1)} %get-tuple-element.60), channel_id=1, source_target_pairs={{0,16},{8,24},{16,0},{24,8},{1,17},{9,25},{17,1},{25,9},{2,18},{10... | collective-permute-start | bytes 98312 | tf_op jit(solution)/shard_map/ppermute | solution.py:400
  41.5 2.3 %collective-permute-start.18 = (bf16[2880,128]{1,0:T(8,128)(2,1)S(1)}, bf16[2880,128]{1,0:T(8,128)(2,1)S(1)}, u32[]{:S(2)}, u32[]{:S(2)}) collective-permute-start(bf16[2880,128]{1,0:T(8,128)(2,1)S(1)} %shard_map.136.own), channel_id=1, source_target_pairs={{0,1},{1,0},{2,3},{3,2},{4,5},{5,4},{6,7},{7,6},{8,9},{9,8},{10,11... | collective-permute-start | bytes 2211848 | tf_op jit(solution)/shard_map/ppermute | solution.py:397
  41.6 4.0 %collective-permute-start.14 = (bf16[128,128]{1,0:T(8,128)(2,1)S(1)}, bf16[128,128]{1,0:T(8,128)(2,1)S(1)}, u32[]{:S(2)}, u32[]{:S(2)}) collective-permute-start(bf16[128,128]{1,0:T(8,128)(2,1)S(1)} %get-tuple-element.63), channel_id=1, source_target_pairs={{0,8},{8,0},{16,24},{24,16},{1,9},{9,1},{17,25},{25,17},{2,10},{10... | collective-permute-start | bytes 98312 | tf_op jit(solution)/shard_map/ppermute | solution.py:400
  (1 other events, 0.9 us)

commit v18 on v17

--- a/solution.py
+++ b/solution.py
@@ -23,6 +23,11 @@
     return lax.dot_general(
         a, b, (((on_a,), (on_b,)), ((), ())), preferred_element_type=jnp.float32
     )
+
+
+def far_first(blocks):
+    blocks = list(blocks)
+    return blocks[:1] + blocks[:0:-1]
 
 
 def last_swapped(blocks):
@@ -88,7 +93,7 @@
 
 
 def stats_kernel(n_t, bias, keys, *refs):
-    packed, out = refs[:n_t], refs[n_t]
+    packed, out = far_first(refs[:n_t]), refs[n_t]
     rows = packed[0].shape[1]
     for p in range(0, n_t, 2):
         q = jnp.concatenate([packed[p][0], packed[p + 1][0]], axis=0)
@@ -413,10 +418,7 @@
     packed, _ = lax.optimization_barrier(
         (jnp.stack([queries, saved_out]), (received, other_saved))
     )
-    packed_all = [packed]
-    for k in range(1, n_t):
-        low = k & -k
-        packed_all.append(over_time(packed_all[k - low], low))
+    packed_all = time_swaps([packed] * n_t)
     (to_fetch, own_grad), _ = lax.optimization_barrier(((proj_weight, out_grad), received))
     kept, pieces[0] = call(
         functools.partial(fetch_kernel, chips),
@@ -446,7 +448,7 @@
     later_bias, _ = lax.optimization_barrier((bias, mine))
     stats = call(
         functools.partial(stats_kernel, n_t),
-        [later_bias, keys] + packed_all,
+        [later_bias, keys] + far_first(packed_all),
         shape(f32, 2 * n_t, LANES),
         flops=2 * n_t * rows * k_rows * HD,
     )

time: 46.5 us -> 46.6 us (level)
  starting transfers between devices: 20.7 us -> 20.2 us
  waiting for transfers between devices: 14.2 us -> 14.7 us
    ppermute x9, waiting for transfers between devices: 11.8 us -> 12.3 us  [over_time(): return lax.ppermute(x, 'tm', [(t, t ^ k) for t in range(n_t)])]
    ppermute x9, starting transfers between devices: 12.4 us -> 11.9 us  [over_time(): return lax.ppermute(x, 'tm', [(t, t ^ k) for t in range(n_t)])]
  transfers between devices with their start and end apart: 19 -> 19, of which waited for: 8 -> 9; matrix products, arithmetic and copies ran while one was open for 2% -> 2% of each run, Pallas kernels for 17% -> 17%
where the time goes in v18:
time: 46.6 us; the launch traced here: 46.3 us
  starting transfers between devices  20.2 us (43%)
  waiting for transfers between devices  14.7 us (32%)
  Pallas kernels  8.88 us (19%)
  local copies, waits for them, and re-layouts  0.94 us (2%)
  between operations  0.8 us (2%)
  other arithmetic  0.78 us (2%)
    ppermute x9, waiting for transfers between devices, over_time(): return lax.ppermute(x, 'tm', [(t, t ^ k) for t in range(n_t)])  12.3 us
    ppermute x9, starting transfers between devices, over_time(): return lax.ppermute(x, 'tm', [(t, t ^ k) for t in range(n_t)])  11.9 us
    pallas_call x12, Pallas kernels, call(): pl.pallas_call(kernel, out_shape=out_shape, in_specs=[pl.BlockSpec(memory...  8.88 us
    ppermute x6, starting transfers between devices, over_chips(): lax.ppermute(x, 'space', [(s, s ^ 2 * k) for s in range(n_s)])  7.66 us
    ppermute x4, waiting for transfers between devices, over_cores(): return lax.ppermute(x, 'space', [(s, s ^ 1) for s in range(n_s)])  2.36 us
    unnamed x12, local copies, waits for them, and re-layouts  0.94 us
  transfers between devices with their start and end apart: 19, of which 9 were waited for; matrix products, arithmetic and copies ran while one was open for 2% of the time, Pallas kernels for 17%

profile of v18, /device:TPU:0, one launch (start us, length us, event | category | flops | bytes accessed | tf_op | source)
XLA Modules:
  0.0 46.3 jit_solution(11180659176799703272)
XLA Ops:
  1.2 2.6 %collective-permute-start.2 = (bf16[128,640]{1,0:T(8,128)(2,1)}, bf16[128,640]{1,0:T(8,128)(2,1)S(1)}, u32[]{:S(2)}, u32[]{:S(2)}) collective-permute-start(bf16[128,640]{1,0:T(8,128)(2,1)} %grad_in), channel_id=1, source_target_pairs={{0,2},{1,3},{2,0},{3,1},{4,6},{5,7},{6,4},{7,5},{8,10},{9,11},{10,... | collective-permute-start | bytes 491528 | tf_op jit(solution)/shard_map/ppermute | solution.py:398
  3.7 1.5 %collective-permute-start.3 = (bf16[128,640]{1,0:T(8,128)(2,1)}, bf16[128,640]{1,0:T(8,128)(2,1)S(1)}, u32[]{:S(2)}, u32[]{:S(2)}) collective-permute-start(bf16[128,640]{1,0:T(8,128)(2,1)} %grad_in), channel_id=1, source_target_pairs={{0,4},{1,5},{2,6},{3,7},{4,0},{5,1},{6,2},{7,3},{8,12},{9,13},{10,... | collective-permute-start | bytes 491528 | tf_op jit(solution)/shard_map/ppermute | solution.py:398
  5.3 0.8 %pad_maximum_fusion.packed.refs_0_ = bf16[2,128,128]{2,1,0:T(8,128)(2,1)S(1)} fusion(bf16[1,128,128]{2,1,0:T(8,128)(2,1)} %bitcast.3, bf16[1,128,128]{2,1,0:T(8,128)(2,1)} %bitcast.2), kind=kLoop, calls=%fused_computation | loop fusion | flops 32768 | bytes 131072 | tf_op jit(solution)/shard_map/stack | solution.py:419
  6.7 4.1 %collective-permute-start.6 = (bf16[2,128,128]{2,1,0:T(8,128)(2,1)S(1)}, bf16[2,128,128]{2,1,0:T(8,128)(2,1)S(1)}, u32[]{:S(2)}, u32[]{:S(2)}) collective-permute-start(bf16[2,128,128]{2,1,0:T(8,128)(2,1)S(1)} %pad_maximum_fusion.packed.refs_0_), channel_id=1, source_target_pairs={{0,24},{8,16},{16,8},{24,0},{1,25},{9,17},{17,9},{25,1},{2,26},{10... | collective-permute-start | bytes 196616 | tf_op jit(solution)/shard_map/ppermute | solution.py:405
  10.8 0.9 %copy-done.3 = bf16[128,640]{1,0:T(8,128)(2,1)S(1)} copy-done((bf16[128,640]{1,0:T(8,128)(2,1)S(1)}, bf16[128,640]{1,0:T(8,128)(2,1)}, u32[]{:S(2)}) %copy-start.3) | copy-done | bytes 163864
  11.7 1.4 %shard_map.129 = (bf16[4,128,640]{2,1,0:T(8,128)(2,1)S(1)}, bf16[128,640]{1,0:T(8,128)(2,1)S(1)}) custom-call(bf16[128,5120]{1,0:T(8,128)(2,1)} %weight_in, bf16[128,640]{1,0:T(8,128)(2,1)S(1)} %copy-done.3), custom_call_target="tpu_custom_call" | custom-call | bytes 1474560 | tf_op jit(solution)/shard_map/pallas_call | solution.py:353
  14.4 0.8 %shard_map.130 = (f32[128,128]{1,0:T(8,128)S(1)}, f32[128,128]{1,0:T(8,128)S(1)}, f32[40,128]{1,0:T(8,128)S(1)}) custom-call(bf16[2,128,128]{2,1,0:T(8,128)(2,1)S(1)} %pad_maximum_fusion.packed.refs_0_, bf16[128,128]{1,0:T(8,128)(2,1)S(1)} %collective-permute-done.1.other_saved, bf16[4,128,640]{2,1,0:T(8,128)(2,1)S(1)} %get-tuple-element.47.kept, ...), custom_call_target="tpu_custom_call" | custom-call | flops 335544320 | bytes 2740224 | tf_op jit(solution)/shard_map/pallas_call | solution.py:353
  15.3 1.4 %collective-permute-done.7.refs_2_ = bf16[2,128,128]{2,1,0:T(8,128)(2,1)S(1)} collective-permute-done((bf16[2,128,128]{2,1,0:T(8,128)(2,1)S(1)}, bf16[2,128,128]{2,1,0:T(8,128)(2,1)S(1)}, u32[]{:S(2)}, u32[]{:S(2)}) %collective-permute-start.7) | collective-permute-done | bytes 65568 | tf_op jit(solution)/shard_map/ppermute | solution.py:405
  16.7 1.4 %collective-permute-done.8.refs_3_.refs_1_ = bf16[2,128,128]{2,1,0:T(8,128)(2,1)S(1)} collective-permute-done((bf16[2,128,128]{2,1,0:T(8,128)(2,1)S(1)}, bf16[2,128,128]{2,1,0:T(8,128)(2,1)S(1)}, u32[]{:S(2)}, u32[]{:S(2)}) %collective-permute-start.8) | collective-permute-done | bytes 65568 | tf_op jit(solution)/shard_map/ppermute | solution.py:405
  18.1 0.8 %shard_map.131.stats = f32[8,128]{1,0:T(8,128)S(1)} custom-call(f32[2,512]{1,0:T(2,128)S(1)} %get-tuple-element.58.bias, bf16[1024,128]{1,0:T(8,128)(2,1)S(1)} %copy-done, bf16[2,128,128]{2,1,0:T(8,128)(2,1)S(1)} %pad_maximum_fusion.packed.refs_0_, bf16[2,128,128]{2,1,0:T(8,128)(2,1)S(1)} %collective-permute-done.6.refs_1_.refs_3_, ...), custom_call_target="tpu_custom_call" | custom-call | flops 134217728 | bytes 528384 | tf_op jit(solution)/shard_map/pallas_call | solution.py:353
  19.0 2.5 %collective-permute-start.10 = (bf16[352,128]{1,0:T(8,128)(2,1)S(1)}, bf16[352,128]{1,0:T(8,128)(2,1)S(1)}, u32[]{:S(2)}, u32[]{:S(2)}) collective-permute-start(bf16[352,128]{1,0:T(8,128)(2,1)S(1)} %get-tuple-element.56), channel_id=1, source_target_pairs={{0,24},{8,16},{16,8},{24,0},{1,25},{9,17},{17,9},{25,1},{2,26},{10... | collective-permute-start | bytes 270344 | tf_op jit(solution)/shard_map/ppermute | solution.py:405
  22.1 1.4 %collective-permute-start.9 = (bf16[352,128]{1,0:T(8,128)(2,1)S(1)}, bf16[352,128]{1,0:T(8,128)(2,1)S(1)}, u32[]{:S(2)}, u32[]{:S(2)}) collective-permute-start(bf16[352,128]{1,0:T(8,128)(2,1)S(1)} %get-tuple-element.55), channel_id=1, source_target_pairs={{0,8},{8,0},{16,24},{24,16},{1,9},{9,1},{17,25},{25,17},{2,10},{10... | collective-permute-start | bytes 270344 | tf_op jit(solution)/shard_map/ppermute | solution.py:405
  23.5 2.5 %collective-permute-done.10.refs_2_.refs_4_ = bf16[352,128]{1,0:T(8,128)(2,1)S(1)} collective-permute-done((bf16[352,128]{1,0:T(8,128)(2,1)S(1)}, bf16[352,128]{1,0:T(8,128)(2,1)S(1)}, u32[]{:S(2)}, u32[]{:S(2)}) %collective-permute-start.10) | collective-permute-done | bytes 90144 | tf_op jit(solution)/shard_map/ppermute | solution.py:405
  26.0 3.3 %collective-permute-done.11.refs_3_.refs_5_ = bf16[352,128]{1,0:T(8,128)(2,1)S(1)} collective-permute-done((bf16[352,128]{1,0:T(8,128)(2,1)S(1)}, bf16[352,128]{1,0:T(8,128)(2,1)S(1)}, u32[]{:S(2)}, u32[]{:S(2)}) %collective-permute-start.11) | collective-permute-done | bytes 90144 | tf_op jit(solution)/shard_map/ppermute | solution.py:405
  29.4 1.6 %collective-permute-start.15 = (bf16[800,128]{1,0:T(8,128)(2,1)S(1)}, bf16[800,128]{1,0:T(8,128)(2,1)S(1)}, u32[]{:S(2)}, u32[]{:S(2)}) collective-permute-start(bf16[800,128]{1,0:T(8,128)(2,1)S(1)} %shard_map.133.refs_0_), channel_id=1, source_target_pairs={{0,2},{1,3},{2,0},{3,1},{4,6},{5,7},{6,4},{7,5},{8,10},{9,11},{10,... | collective-permute-start | bytes 614408 | tf_op jit(solution)/shard_map/ppermute | solution.py:398
  31.0 1.5 %collective-permute-start.16 = (bf16[800,128]{1,0:T(8,128)(2,1)S(1)}, bf16[800,128]{1,0:T(8,128)(2,1)S(1)}, u32[]{:S(2)}, u32[]{:S(2)}) collective-permute-start(bf16[800,128]{1,0:T(8,128)(2,1)S(1)} %shard_map.133.refs_0_), channel_id=1, source_target_pairs={{0,4},{1,5},{2,6},{3,7},{4,0},{5,1},{6,2},{7,3},{8,12},{9,13},{10,... | collective-permute-start | bytes 614408 | tf_op jit(solution)/shard_map/ppermute | solution.py:398
  33.0 1.0 %shard_map.134 = (f32[1024,128]{1,0:T(8,128)S(1)}, f32[1024,128]{1,0:T(8,128)S(1)}, bf16[128,128]{1,0:T(8,128)(2,1)S(1)}, bf16[128,128]{1,0:T(8,128)(2,1)S(1)}) custom-call(f32[2,512]{1,0:T(2,128)S(1)} %get-tuple-element.58.bias, bf16[1024,128]{1,0:T(8,128)(2,1)S(1)} %copy-done, bf16[1024,128]{1,0:T(8,128)(2,1)S(1)} %copy-done.2, ...), custom_call_target="tpu_custom_call" | custom-call | flops 335544320 | bytes 1150976 | tf_op jit(solution)/shard_map/pallas_call | solution.py:353
  34.0 2.7 %collective-permute-start.12 = (bf16[128,128]{1,0:T(8,128)(2,1)S(1)}, bf16[128,128]{1,0:T(8,128)(2,1)S(1)}, u32[]{:S(2)}, u32[]{:S(2)}) collective-permute-start(bf16[128,128]{1,0:T(8,128)(2,1)S(1)} %get-tuple-element.59), channel_id=1, source_target_pairs={{0,24},{8,16},{16,8},{24,0},{1,25},{9,17},{17,9},{25,1},{2,26},{10... | collective-permute-start | bytes 98312 | tf_op jit(solution)/shard_map/ppermute | solution.py:405
  36.6 1.7 %shard_map.135 = (bf16[1024,128]{1,0:T(8,128)(2,1)}, bf16[1024,128]{1,0:T(8,128)(2,1)}, bf16[128,128]{1,0:T(8,128)(2,1)S(1)}, bf16[128,128]{1,0:T(8,128)(2,1)S(1)}) custom-call(f32[2,512]{1,0:T(2,128)S(1)} %get-tuple-element.58.bias, bf16[1024,128]{1,0:T(8,128)(2,1)S(1)} %copy-done, bf16[1024,128]{1,0:T(8,128)(2,1)S(1)} %copy-done.2, ...), custom_call_target="tpu_custom_call" | custom-call | flops 335544320 | bytes 2199552 | tf_op jit(solution)/shard_map/pallas_call | solution.py:353
  38.3 1.5 %collective-permute-done.12.refs_0_ = bf16[128,128]{1,0:T(8,128)(2,1)S(1)} collective-permute-done((bf16[128,128]{1,0:T(8,128)(2,1)S(1)}, bf16[128,128]{1,0:T(8,128)(2,1)S(1)}, u32[]{:S(2)}, u32[]{:S(2)}) %collective-permute-start.12) | collective-permute-done | bytes 32800 | tf_op jit(solution)/shard_map/ppermute | solution.py:405
  39.7 1.7 %collective-permute-done.13.refs_1_ = bf16[128,128]{1,0:T(8,128)(2,1)S(1)} collective-permute-done((bf16[128,128]{1,0:T(8,128)(2,1)S(1)}, bf16[128,128]{1,0:T(8,128)(2,1)S(1)}, u32[]{:S(2)}, u32[]{:S(2)}) %collective-permute-start.13) | collective-permute-done | bytes 32800 | tf_op jit(solution)/shard_map/ppermute | solution.py:405
  42.1 1.7 %collective-permute-done.18.other = bf16[2880,128]{1,0:T(8,128)(2,1)S(1)} collective-permute-done((bf16[2880,128]{1,0:T(8,128)(2,1)S(1)}, bf16[2880,128]{1,0:T(8,128)(2,1)S(1)}, u32[]{:S(2)}, u32[]{:S(2)}) %collective-permute-start.18) | collective-permute-done | bytes 737312 | tf_op jit(solution)/shard_map/ppermute | solution.py:402
  43.8 1.3 %shard_map.138 = (f32[128,1280]{1,0:T(8,128)}, f32[16,5120]{1,0:T(8,128)}) custom-call(f32[8,16,128]{2,1,0:T(8,128)S(1)} %get-tuple-element.65.hot, bf16[2880,128]{1,0:T(8,128)(2,1)S(1)} %collective-permute-done.18.other, f32[128,640]{1,0:T(8,128)S(1)} %get-tuple-element.71.own_weight, f32[16,2560]{1,0:T(8,128)S(1)} %get-tuple-element.72.own_gate, ...), custom_call_target="tpu_custom_call" | custom-call | flops 83886080 | bytes 1556480 | tf_op jit(solution)/shard_map/pallas_call | solution.py:353
  45.6 0.7 %shard_map.139 = bf16[128,128]{1,0:T(8,128)(2,1)} custom-call(bf16[128,128]{1,0:T(8,128)(2,1)S(1)} %collective-permute-done.12.refs_0_, bf16[128,128]{1,0:T(8,128)(2,1)S(1)} %collective-permute-done.13.refs_1_, bf16[128,128]{1,0:T(8,128)(2,1)S(1)} %collective-permute-done.14.refs_2_, bf16[128,128]{1,0:T(8,128)(2,1)S(1)} %get-tuple-element.74.refs_3_), custom_call_target="tpu_custom_call" | custom-call | bytes 131072 | tf_op jit(solution)/shard_map/pallas_call | solution.py:353
  (39 shorter events, 4.9 us)
Async XLA Ops:
  0.6 12.4 %copy-start.1 = (f32[16,5120]{1,0:T(8,128)S(1)}, f32[16,5120]{1,0:T(8,128)}, u32[]{:S(2)}) copy-start(f32[16,5120]{1,0:T(8,128)} %gate) | copy-start | bytes 983044
  0.6 6.1 %collective-permute-start = (bf16[128,5120]{1,0:T(8,128)(2,1)}, bf16[128,5120]{1,0:T(8,128)(2,1)S(1)}, u32[]{:S(2)}, u32[]{:S(2)}) collective-permute-start(bf16[128,5120]{1,0:T(8,128)(2,1)} %weight_in), channel_id=1, source_target_pairs={{0,1},{1,0},{2,3},{3,2},{4,5},{5,4},{6,7},{7,6},{8,9},{9,8},{10,11... | collective-permute-start | bytes 3932168 | tf_op jit(solution)/shard_map/ppermute | solution.py:402
  1.2 12.6 %collective-permute-start.2 = (bf16[128,640]{1,0:T(8,128)(2,1)}, bf16[128,640]{1,0:T(8,128)(2,1)S(1)}, u32[]{:S(2)}, u32[]{:S(2)}) collective-permute-start(bf16[128,640]{1,0:T(8,128)(2,1)} %grad_in), channel_id=1, source_target_pairs={{0,2},{1,3},{2,0},{3,1},{4,6},{5,7},{6,4},{7,5},{8,10},{9,11},{10,... | collective-permute-start | bytes 491528 | tf_op jit(solution)/shard_map/ppermute | solution.py:398
  3.7 10.7 %collective-permute-start.3 = (bf16[128,640]{1,0:T(8,128)(2,1)}, bf16[128,640]{1,0:T(8,128)(2,1)S(1)}, u32[]{:S(2)}, u32[]{:S(2)}) collective-permute-start(bf16[128,640]{1,0:T(8,128)(2,1)} %grad_in), channel_id=1, source_target_pairs={{0,4},{1,5},{2,6},{3,7},{4,0},{5,1},{6,2},{7,3},{8,12},{9,13},{10,... | collective-permute-start | bytes 491528 | tf_op jit(solution)/shard_map/ppermute | solution.py:398
  5.2 9.2 %collective-permute-start.4 = (bf16[128,640]{1,0:T(8,128)(2,1)}, bf16[128,640]{1,0:T(8,128)(2,1)S(1)}, u32[]{:S(2)}, u32[]{:S(2)}) collective-permute-start(bf16[128,640]{1,0:T(8,128)(2,1)} %grad_in), channel_id=1, source_target_pairs={{0,6},{1,7},{2,4},{3,5},{4,2},{5,3},{6,0},{7,1},{8,14},{9,15},{10,... | collective-permute-start | bytes 491528 | tf_op jit(solution)/shard_map/ppermute | solution.py:398
  5.3 1.4 %collective-permute-start.1 = (bf16[128,128]{1,0:T(8,128)(2,1)}, bf16[128,128]{1,0:T(8,128)(2,1)S(1)}, u32[]{:S(2)}, u32[]{:S(2)}) collective-permute-start(bf16[128,128]{1,0:T(8,128)(2,1)} %param.12), channel_id=1, source_target_pairs={{0,1},{1,0},{2,3},{3,2},{4,5},{5,4},{6,7},{7,6},{8,9},{9,8},{10,11... | collective-permute-start | bytes 98312 | tf_op jit(solution)/shard_map/ppermute | solution.py:402
  6.7 8.6 %collective-permute-start.6 = (bf16[2,128,128]{2,1,0:T(8,128)(2,1)S(1)}, bf16[2,128,128]{2,1,0:T(8,128)(2,1)S(1)}, u32[]{:S(2)}, u32[]{:S(2)}) collective-permute-start(bf16[2,128,128]{2,1,0:T(8,128)(2,1)S(1)} %pad_maximum_fusion.packed.refs_0_), channel_id=1, source_target_pairs={{0,24},{8,16},{16,8},{24,0},{1,25},{9,17},{17,9},{25,1},{2,26},{10... | collective-permute-start | bytes 196616 | tf_op jit(solution)/shard_map/ppermute | solution.py:405
  10.7 5.9 %collective-permute-start.7 = (bf16[2,128,128]{2,1,0:T(8,128)(2,1)S(1)}, bf16[2,128,128]{2,1,0:T(8,128)(2,1)S(1)}, u32[]{:S(2)}, u32[]{:S(2)}) collective-permute-start(bf16[2,128,128]{2,1,0:T(8,128)(2,1)S(1)} %pad_maximum_fusion.packed.refs_0_), channel_id=1, source_target_pairs={{0,16},{8,24},{16,0},{24,8},{1,17},{9,25},{17,1},{25,9},{2,18},{10... | collective-permute-start | bytes 196616 | tf_op jit(solution)/shard_map/ppermute | solution.py:405
  11.7 1.4 %copy-start.4 = (s32[8]{0:T(128)S(1)}, s32[8]{0:T(128)}, u32[]{:S(2)}) copy-start(s32[8]{0:T(128)} %levels.1) | copy-start | bytes 100
  11.7 1.4 %copy-start.5 = (s32[4]{0:T(128)S(1)}, s32[4]{0:T(128)}, u32[]{:S(2)}) copy-start(s32[4]{0:T(128)} %clips.1) | copy-start | bytes 52
  13.8 4.3 %collective-permute-start.8 = (bf16[2,128,128]{2,1,0:T(8,128)(2,1)S(1)}, bf16[2,128,128]{2,1,0:T(8,128)(2,1)S(1)}, u32[]{:S(2)}, u32[]{:S(2)}) collective-permute-start(bf16[2,128,128]{2,1,0:T(8,128)(2,1)S(1)} %pad_maximum_fusion.packed.refs_0_), channel_id=1, source_target_pairs={{0,8},{8,0},{16,24},{24,16},{1,9},{9,1},{17,25},{25,17},{2,10},{10... | collective-permute-start | bytes 196616 | tf_op jit(solution)/shard_map/ppermute | solution.py:405
  14.4 3.7 %copy-start = (bf16[1024,128]{1,0:T(8,128)(2,1)S(1)}, bf16[1024,128]{1,0:T(8,128)(2,1)}, u32[]{:S(2)}) copy-start(bf16[1024,128]{1,0:T(8,128)(2,1)} %keys.5) | copy-start | bytes 786436
  15.2 17.8 %copy-start.2 = (bf16[1024,128]{1,0:T(8,128)(2,1)S(1)}, bf16[1024,128]{1,0:T(8,128)(2,1)}, u32[]{:S(2)}) copy-start(bf16[1024,128]{1,0:T(8,128)(2,1)} %values.3) | copy-start | bytes 786436
  15.2 3.7 %collective-permute-start.5 = (f32[128,128]{1,0:T(8,128)S(1)}, f32[128,128]{1,0:T(8,128)S(1)}, u32[]{:S(2)}, u32[]{:S(2)}) collective-permute-start(f32[128,128]{1,0:T(8,128)S(1)} %get-tuple-element.51), channel_id=1, source_target_pairs={{0,1},{1,0},{2,3},{3,2},{4,5},{5,4},{6,7},{7,6},{8,9},{9,8},{10,11... | collective-permute-start | bytes 196616 | tf_op jit(solution)/shard_map/ppermute | solution.py:402
  19.0 7.0 %collective-permute-start.10 = (bf16[352,128]{1,0:T(8,128)(2,1)S(1)}, bf16[352,128]{1,0:T(8,128)(2,1)S(1)}, u32[]{:S(2)}, u32[]{:S(2)}) collective-permute-start(bf16[352,128]{1,0:T(8,128)(2,1)S(1)} %get-tuple-element.56), channel_id=1, source_target_pairs={{0,24},{8,16},{16,8},{24,0},{1,25},{9,17},{17,9},{25,1},{2,26},{10... | collective-permute-start | bytes 270344 | tf_op jit(solution)/shard_map/ppermute | solution.py:405
  21.5 7.8 %collective-permute-start.11 = (bf16[352,128]{1,0:T(8,128)(2,1)S(1)}, bf16[352,128]{1,0:T(8,128)(2,1)S(1)}, u32[]{:S(2)}, u32[]{:S(2)}) collective-permute-start(bf16[352,128]{1,0:T(8,128)(2,1)S(1)} %get-tuple-element.57), channel_id=1, source_target_pairs={{0,16},{8,24},{16,0},{24,8},{1,17},{9,25},{17,1},{25,9},{2,18},{10... | collective-permute-start | bytes 270344 | tf_op jit(solution)/shard_map/ppermute | solution.py:405
  22.1 7.3 %collective-permute-start.9 = (bf16[352,128]{1,0:T(8,128)(2,1)S(1)}, bf16[352,128]{1,0:T(8,128)(2,1)S(1)}, u32[]{:S(2)}, u32[]{:S(2)}) collective-permute-start(bf16[352,128]{1,0:T(8,128)(2,1)S(1)} %get-tuple-element.55), channel_id=1, source_target_pairs={{0,8},{8,0},{16,24},{24,16},{1,9},{9,1},{17,25},{25,17},{2,10},{10... | collective-permute-start | bytes 270344 | tf_op jit(solution)/shard_map/ppermute | solution.py:405
  29.4 12.0 %collective-permute-start.15 = (bf16[800,128]{1,0:T(8,128)(2,1)S(1)}, bf16[800,128]{1,0:T(8,128)(2,1)S(1)}, u32[]{:S(2)}, u32[]{:S(2)}) collective-permute-start(bf16[800,128]{1,0:T(8,128)(2,1)S(1)} %shard_map.133.refs_0_), channel_id=1, source_target_pairs={{0,2},{1,3},{2,0},{3,1},{4,6},{5,7},{6,4},{7,5},{8,10},{9,11},{10,... | collective-permute-start | bytes 614408 | tf_op jit(solution)/shard_map/ppermute | solution.py:398
  31.0 10.5 %collective-permute-start.16 = (bf16[800,128]{1,0:T(8,128)(2,1)S(1)}, bf16[800,128]{1,0:T(8,128)(2,1)S(1)}, u32[]{:S(2)}, u32[]{:S(2)}) collective-permute-start(bf16[800,128]{1,0:T(8,128)(2,1)S(1)} %shard_map.133.refs_0_), channel_id=1, source_target_pairs={{0,4},{1,5},{2,6},{3,7},{4,0},{5,1},{6,2},{7,3},{8,12},{9,13},{10,... | collective-permute-start | bytes 614408 | tf_op jit(solution)/shard_map/ppermute | solution.py:398
  32.5 9.0 %collective-permute-start.17 = (bf16[800,128]{1,0:T(8,128)(2,1)S(1)}, bf16[800,128]{1,0:T(8,128)(2,1)S(1)}, u32[]{:S(2)}, u32[]{:S(2)}) collective-permute-start(bf16[800,128]{1,0:T(8,128)(2,1)S(1)} %shard_map.133.refs_0_), channel_id=1, source_target_pairs={{0,6},{1,7},{2,4},{3,5},{4,2},{5,3},{6,0},{7,1},{8,14},{9,15},{10,... | collective-permute-start | bytes 614408 | tf_op jit(solution)/shard_map/ppermute | solution.py:398
  34.0 5.8 %collective-permute-start.12 = (bf16[128,128]{1,0:T(8,128)(2,1)S(1)}, bf16[128,128]{1,0:T(8,128)(2,1)S(1)}, u32[]{:S(2)}, u32[]{:S(2)}) collective-permute-start(bf16[128,128]{1,0:T(8,128)(2,1)S(1)} %get-tuple-element.59), channel_id=1, source_target_pairs={{0,24},{8,16},{16,8},{24,0},{1,25},{9,17},{17,9},{25,1},{2,26},{10... | collective-permute-start | bytes 98312 | tf_op jit(solution)/shard_map/ppermute | solution.py:405
  36.6 4.8 %collective-permute-start.13 = (bf16[128,128]{1,0:T(8,128)(2,1)S(1)}, bf16[128,128]{1,0:T(8,128)(2,1)S(1)}, u32[]{:S(2)}, u32[]{:S(2)}) collective-permute-start(bf16[128,128]{1,0:T(8,128)(2,1)S(1)} %get-tuple-element.60), channel_id=1, source_target_pairs={{0,16},{8,24},{16,0},{24,8},{1,17},{9,25},{17,1},{25,9},{2,18},{10... | collective-permute-start | bytes 98312 | tf_op jit(solution)/shard_map/ppermute | solution.py:405
  41.5 2.3 %collective-permute-start.18 = (bf16[2880,128]{1,0:T(8,128)(2,1)S(1)}, bf16[2880,128]{1,0:T(8,128)(2,1)S(1)}, u32[]{:S(2)}, u32[]{:S(2)}) collective-permute-start(bf16[2880,128]{1,0:T(8,128)(2,1)S(1)} %shard_map.136.own), channel_id=1, source_target_pairs={{0,1},{1,0},{2,3},{3,2},{4,5},{5,4},{6,7},{7,6},{8,9},{9,8},{10,11... | collective-permute-start | bytes 2211848 | tf_op jit(solution)/shard_map/ppermute | solution.py:402
  41.6 4.0 %collective-permute-start.14 = (bf16[128,128]{1,0:T(8,128)(2,1)S(1)}, bf16[128,128]{1,0:T(8,128)(2,1)S(1)}, u32[]{:S(2)}, u32[]{:S(2)}) collective-permute-start(bf16[128,128]{1,0:T(8,128)(2,1)S(1)} %get-tuple-element.63), channel_id=1, source_target_pairs={{0,8},{8,0},{16,24},{24,16},{1,9},{9,1},{17,25},{25,17},{2,10},{10... | collective-permute-start | bytes 98312 | tf_op jit(solution)/shard_map/ppermute | solution.py:405
  (1 other events, 0.9 us)

commit v19 on v18

--- a/solution.py
+++ b/solution.py
@@ -275,18 +275,23 @@
     refs[n_t][...] = jnp.transpose(total * SCALE).astype(jnp.bfloat16)
 
 
-def half_results(n_t, chips, frames, hot, ref, packed, saved, held, tiles):
-    t, chip, _ = place()
-    rows = saved.shape[1]
-    part = rows // chips
-    base = tiles * n_t * part
+def order_kernel(n_t, chips, *refs):
+    packed, (out, saved) = refs[:n_t], refs[n_t:]
+    chip = place()[1]
+    part = saved.shape[1] // chips
     for k in range(n_t):
         saved[k] = packed[k][1].astype(jnp.float32)
     ordered = []
     for c in range(chips):
         mine = pl.ds(pl.multiple_of((chip ^ c) * part, part), part)
         ordered += [saved[k, mine, :] for k in range(n_t)]
-    ordered = jnp.transpose(jnp.concatenate(ordered, axis=0)).astype(jnp.bfloat16)
+    out[...] = jnp.transpose(jnp.concatenate(ordered, axis=0)).astype(jnp.bfloat16)
+
+
+def half_results(n_t, chips, frames, hot, ref, ordered, held, tiles):
+    t = lax.axis_index("tm")
+    part = ordered.shape[1] // (n_t * chips)
+    base = tiles * n_t * part
     gated = jnp.concatenate(
         [
             jnp.concatenate(
@@ -314,25 +319,25 @@
             total = total + hot[f] * held[f // frames, row : row + 1, :]
         return total
 
-    return dot(ordered, gated, 1, 0), gate_tile
-
-
-def own_kernel(n_t, chips, frames, hot, own, *refs):
-    packed, (weight_out, gate_out, saved, held) = refs[:n_t], refs[n_t:]
+    return dot(ordered[...], gated, 1, 0), gate_tile
+
+
+def own_kernel(n_t, chips, frames, hot, own, ordered, weight_out, gate_out, held):
     tiles = weight_out.shape[1] // LANES
-    result, gate_tile = half_results(n_t, chips, frames, hot, own, packed, saved, held, tiles)
+    result, gate_tile = half_results(n_t, chips, frames, hot, own, ordered, held, tiles)
     weight_out[...] = result
     for a in range(chips):
         for j in range(tiles):
             gate_out[:, (a * tiles + j) * LANES : (a * tiles + j + 1) * LANES] = gate_tile(a, j)
 
 
-def final_kernel(n_t, chips, frames, hot, other, own_weight, own_gate, *refs):
-    packed, (weight_out, gate_out, saved, held) = refs[:n_t], refs[n_t:]
+def final_kernel(
+    n_t, chips, frames, hot, other, own_weight, own_gate, ordered, weight_out, gate_out, held
+):
     core = place()[2]
     width = own_weight.shape[1]
     tiles = width // LANES
-    result, gate_tile = half_results(n_t, chips, frames, hot, other, packed, saved, held, tiles)
+    result, gate_tile = half_results(n_t, chips, frames, hot, other, ordered, held, tiles)
     mine = own_weight[...]
     weight_out[:, :width] = jnp.where(core == 0, mine, result)
     weight_out[:, width:] = jnp.where(core == 0, result, mine)
@@ -485,24 +490,31 @@
     key_grad, value_grad = near[:2]
     parts[0], parts[1] = near[3], over_time(near[2], 1)
     parts = [parts[k] for k in range(n_t)]
-    bundles, _ = lax.optimization_barrier((bundles, (key_grad, parts[: n_t // 2 - 1 : -1])))
+    to_order, _ = lax.optimization_barrier((packed_all, key_grad))
+    ordered = call(
+        functools.partial(order_kernel, n_t, chips),
+        to_order,
+        shape(bf16, HD, n_t * rows),
+        [pltpu.VMEM((n_t, rows, HD), f32)],
+    )
+    bundles, _ = lax.optimization_barrier((bundles, (ordered, key_grad, parts[: n_t // 2 - 1 : -1])))
     collected = call(
         functools.partial(collect_kernel, chips, base),
         bundles,
         shape(bf16, chips * base + 2 * n_t * count, LANES),
         [pltpu.VMEM((chips, n_t * count, LANES), f32)],
     )
-    scratch = [pltpu.VMEM((n_t, rows, HD), f32), pltpu.VMEM((n_t, count, LANES), f32)]
+    scratch = [pltpu.VMEM((n_t, count, LANES), f32)]
     own_halves = call(
         functools.partial(own_kernel, n_t, chips, frames),
-        [hot, collected] + packed_all,
+        [hot, collected, ordered],
         [shape(f32, HD, width), shape(f32, levels, chips * width)],
         scratch,
         flops=2 * n_t * rows * width * HD,
     )
     weight_grad, gate_grad = call(
         functools.partial(final_kernel, n_t, chips, frames),
-        [hot, over_cores(collected), *own_halves] + packed_all,
+        [hot, over_cores(collected), *own_halves, ordered],
         [shape(f32, HD, 2 * width), shape(f32, levels, n_s * width)],
         scratch,
         flops=2 * n_t * rows * width * HD,

time: 46.6 us -> 46.5 us (level)
    pallas_call x12 -> x13, Pallas kernels: 8.88 us -> 8.82 us  [call(): pl.pallas_call(kernel, out_shape=out_shape, in_specs=[pl.BlockSpec(memory...]
where the time goes in v19:
time: 46.5 us; the launch traced here: 46.3 us
  starting transfers between devices  20.2 us (43%)
  waiting for transfers between devices  14.8 us (32%)
  Pallas kernels  8.82 us (19%)
  local copies, waits for them, and re-layouts  0.94 us (2%)
  between operations  0.81 us (2%)
  other arithmetic  0.78 us (2%)
    ppermute x9, waiting for transfers between devices, over_time(): return lax.ppermute(x, 'tm', [(t, t ^ k) for t in range(n_t)])  12.3 us
    ppermute x9, starting transfers between devices, over_time(): return lax.ppermute(x, 'tm', [(t, t ^ k) for t in range(n_t)])  11.9 us
    pallas_call x13, Pallas kernels, call(): pl.pallas_call(kernel, out_shape=out_shape, in_specs=[pl.BlockSpec(memory...  8.82 us
    ppermute x6, starting transfers between devices, over_chips(): lax.ppermute(x, 'space', [(s, s ^ 2 * k) for s in range(n_s)])  7.66 us
    ppermute x4, waiting for transfers between devices, over_cores(): return lax.ppermute(x, 'space', [(s, s ^ 1) for s in range(n_s)])  2.47 us
    unnamed x12, local copies, waits for them, and re-layouts  0.94 us
  transfers between devices with their start and end apart: 19, of which 9 were waited for; matrix products, arithmetic and copies ran while one was open for 2% of the time, Pallas kernels for 17%

profile of v19, /device:TPU:0, one launch (start us, length us, event | category | flops | bytes accessed | tf_op | source)
XLA Modules:
  0.0 46.3 jit_solution(10156831409690556983)
XLA Ops:
  1.2 2.6 %collective-permute-start.2 = (bf16[128,640]{1,0:T(8,128)(2,1)}, bf16[128,640]{1,0:T(8,128)(2,1)S(1)}, u32[]{:S(2)}, u32[]{:S(2)}) collective-permute-start(bf16[128,640]{1,0:T(8,128)(2,1)} %grad_in), channel_id=1, source_target_pairs={{0,2},{1,3},{2,0},{3,1},{4,6},{5,7},{6,4},{7,5},{8,10},{9,11},{10,... | collective-permute-start | bytes 491528 | tf_op jit(solution)/shard_map/ppermute | solution.py:403
  3.7 1.5 %collective-permute-start.3 = (bf16[128,640]{1,0:T(8,128)(2,1)}, bf16[128,640]{1,0:T(8,128)(2,1)S(1)}, u32[]{:S(2)}, u32[]{:S(2)}) collective-permute-start(bf16[128,640]{1,0:T(8,128)(2,1)} %grad_in), channel_id=1, source_target_pairs={{0,4},{1,5},{2,6},{3,7},{4,0},{5,1},{6,2},{7,3},{8,12},{9,13},{10,... | collective-permute-start | bytes 491528 | tf_op jit(solution)/shard_map/ppermute | solution.py:403
  5.3 0.8 %pad_maximum_fusion.packed.refs_0_ = bf16[2,128,128]{2,1,0:T(8,128)(2,1)S(1)} fusion(bf16[1,128,128]{2,1,0:T(8,128)(2,1)} %bitcast.3, bf16[1,128,128]{2,1,0:T(8,128)(2,1)} %bitcast.2), kind=kLoop, calls=%fused_computation | loop fusion | flops 32768 | bytes 131072 | tf_op jit(solution)/shard_map/stack | solution.py:424
  6.7 4.1 %collective-permute-start.6 = (bf16[2,128,128]{2,1,0:T(8,128)(2,1)S(1)}, bf16[2,128,128]{2,1,0:T(8,128)(2,1)S(1)}, u32[]{:S(2)}, u32[]{:S(2)}) collective-permute-start(bf16[2,128,128]{2,1,0:T(8,128)(2,1)S(1)} %pad_maximum_fusion.packed.refs_0_), channel_id=1, source_target_pairs={{0,24},{8,16},{16,8},{24,0},{1,25},{9,17},{17,9},{25,1},{2,26},{10... | collective-permute-start | bytes 196616 | tf_op jit(solution)/shard_map/ppermute | solution.py:410
  10.8 0.9 %copy-done.3 = bf16[128,640]{1,0:T(8,128)(2,1)S(1)} copy-done((bf16[128,640]{1,0:T(8,128)(2,1)S(1)}, bf16[128,640]{1,0:T(8,128)(2,1)}, u32[]{:S(2)}) %copy-start.3) | copy-done | bytes 163864
  11.7 1.4 %shard_map.129 = (bf16[4,128,640]{2,1,0:T(8,128)(2,1)S(1)}, bf16[128,640]{1,0:T(8,128)(2,1)S(1)}) custom-call(bf16[128,5120]{1,0:T(8,128)(2,1)} %weight_in, bf16[128,640]{1,0:T(8,128)(2,1)S(1)} %copy-done.3), custom_call_target="tpu_custom_call" | custom-call | bytes 1474560 | tf_op jit(solution)/shard_map/pallas_call | solution.py:358
  14.4 0.8 %shard_map.130 = (f32[128,128]{1,0:T(8,128)S(1)}, f32[128,128]{1,0:T(8,128)S(1)}, f32[40,128]{1,0:T(8,128)S(1)}) custom-call(bf16[2,128,128]{2,1,0:T(8,128)(2,1)S(1)} %pad_maximum_fusion.packed.refs_0_, bf16[128,128]{1,0:T(8,128)(2,1)S(1)} %collective-permute-done.1.other_saved, bf16[4,128,640]{2,1,0:T(8,128)(2,1)S(1)} %get-tuple-element.51.kept, ...), custom_call_target="tpu_custom_call" | custom-call | flops 335544320 | bytes 2740224 | tf_op jit(solution)/shard_map/pallas_call | solution.py:358
  15.3 1.4 %collective-permute-done.7.refs_2_ = bf16[2,128,128]{2,1,0:T(8,128)(2,1)S(1)} collective-permute-done((bf16[2,128,128]{2,1,0:T(8,128)(2,1)S(1)}, bf16[2,128,128]{2,1,0:T(8,128)(2,1)S(1)}, u32[]{:S(2)}, u32[]{:S(2)}) %collective-permute-start.7) | collective-permute-done | bytes 65568 | tf_op jit(solution)/shard_map/ppermute | solution.py:410
  16.7 1.4 %collective-permute-done.8.refs_3_.refs_1_ = bf16[2,128,128]{2,1,0:T(8,128)(2,1)S(1)} collective-permute-done((bf16[2,128,128]{2,1,0:T(8,128)(2,1)S(1)}, bf16[2,128,128]{2,1,0:T(8,128)(2,1)S(1)}, u32[]{:S(2)}, u32[]{:S(2)}) %collective-permute-start.8) | collective-permute-done | bytes 65568 | tf_op jit(solution)/shard_map/ppermute | solution.py:410
  18.1 0.8 %shard_map.131.stats = f32[8,128]{1,0:T(8,128)S(1)} custom-call(f32[2,512]{1,0:T(2,128)S(1)} %get-tuple-element.62.bias, bf16[1024,128]{1,0:T(8,128)(2,1)S(1)} %copy-done, bf16[2,128,128]{2,1,0:T(8,128)(2,1)S(1)} %pad_maximum_fusion.packed.refs_0_, bf16[2,128,128]{2,1,0:T(8,128)(2,1)S(1)} %collective-permute-done.6.refs_1_.refs_3_, ...), custom_call_target="tpu_custom_call" | custom-call | flops 134217728 | bytes 528384 | tf_op jit(solution)/shard_map/pallas_call | solution.py:358
  19.0 2.5 %collective-permute-start.10 = (bf16[352,128]{1,0:T(8,128)(2,1)S(1)}, bf16[352,128]{1,0:T(8,128)(2,1)S(1)}, u32[]{:S(2)}, u32[]{:S(2)}) collective-permute-start(bf16[352,128]{1,0:T(8,128)(2,1)S(1)} %get-tuple-element.60), channel_id=1, source_target_pairs={{0,24},{8,16},{16,8},{24,0},{1,25},{9,17},{17,9},{25,1},{2,26},{10... | collective-permute-start | bytes 270344 | tf_op jit(solution)/shard_map/ppermute | solution.py:410
  22.1 1.4 %collective-permute-start.9 = (bf16[352,128]{1,0:T(8,128)(2,1)S(1)}, bf16[352,128]{1,0:T(8,128)(2,1)S(1)}, u32[]{:S(2)}, u32[]{:S(2)}) collective-permute-start(bf16[352,128]{1,0:T(8,128)(2,1)S(1)} %get-tuple-element.59), channel_id=1, source_target_pairs={{0,8},{8,0},{16,24},{24,16},{1,9},{9,1},{17,25},{25,17},{2,10},{10... | collective-permute-start | bytes 270344 | tf_op jit(solution)/shard_map/ppermute | solution.py:410
  23.5 2.5 %collective-permute-done.10.refs_2_.refs_4_ = bf16[352,128]{1,0:T(8,128)(2,1)S(1)} collective-permute-done((bf16[352,128]{1,0:T(8,128)(2,1)S(1)}, bf16[352,128]{1,0:T(8,128)(2,1)S(1)}, u32[]{:S(2)}, u32[]{:S(2)}) %collective-permute-start.10) | collective-permute-done | bytes 90144 | tf_op jit(solution)/shard_map/ppermute | solution.py:410
  26.0 3.3 %collective-permute-done.11.refs_3_.refs_5_ = bf16[352,128]{1,0:T(8,128)(2,1)S(1)} collective-permute-done((bf16[352,128]{1,0:T(8,128)(2,1)S(1)}, bf16[352,128]{1,0:T(8,128)(2,1)S(1)}, u32[]{:S(2)}, u32[]{:S(2)}) %collective-permute-start.11) | collective-permute-done | bytes 90144 | tf_op jit(solution)/shard_map/ppermute | solution.py:410
  29.4 1.6 %collective-permute-start.15 = (bf16[800,128]{1,0:T(8,128)(2,1)S(1)}, bf16[800,128]{1,0:T(8,128)(2,1)S(1)}, u32[]{:S(2)}, u32[]{:S(2)}) collective-permute-start(bf16[800,128]{1,0:T(8,128)(2,1)S(1)} %shard_map.133.refs_0_), channel_id=1, source_target_pairs={{0,2},{1,3},{2,0},{3,1},{4,6},{5,7},{6,4},{7,5},{8,10},{9,11},{10,... | collective-permute-start | bytes 614408 | tf_op jit(solution)/shard_map/ppermute | solution.py:403
  31.0 1.5 %collective-permute-start.16 = (bf16[800,128]{1,0:T(8,128)(2,1)S(1)}, bf16[800,128]{1,0:T(8,128)(2,1)S(1)}, u32[]{:S(2)}, u32[]{:S(2)}) collective-permute-start(bf16[800,128]{1,0:T(8,128)(2,1)S(1)} %shard_map.133.refs_0_), channel_id=1, source_target_pairs={{0,4},{1,5},{2,6},{3,7},{4,0},{5,1},{6,2},{7,3},{8,12},{9,13},{10,... | collective-permute-start | bytes 614408 | tf_op jit(solution)/shard_map/ppermute | solution.py:403
  33.0 1.0 %shard_map.134 = (f32[1024,128]{1,0:T(8,128)S(1)}, f32[1024,128]{1,0:T(8,128)S(1)}, bf16[128,128]{1,0:T(8,128)(2,1)S(1)}, bf16[128,128]{1,0:T(8,128)(2,1)S(1)}) custom-call(f32[2,512]{1,0:T(2,128)S(1)} %get-tuple-element.62.bias, bf16[1024,128]{1,0:T(8,128)(2,1)S(1)} %copy-done, bf16[1024,128]{1,0:T(8,128)(2,1)S(1)} %copy-done.2, ...), custom_call_target="tpu_custom_call" | custom-call | flops 335544320 | bytes 1150976 | tf_op jit(solution)/shard_map/pallas_call | solution.py:358
  33.9 2.7 %collective-permute-start.12 = (bf16[128,128]{1,0:T(8,128)(2,1)S(1)}, bf16[128,128]{1,0:T(8,128)(2,1)S(1)}, u32[]{:S(2)}, u32[]{:S(2)}) collective-permute-start(bf16[128,128]{1,0:T(8,128)(2,1)S(1)} %get-tuple-element.63), channel_id=1, source_target_pairs={{0,24},{8,16},{16,8},{24,0},{1,25},{9,17},{17,9},{25,1},{2,26},{10... | collective-permute-start | bytes 98312 | tf_op jit(solution)/shard_map/ppermute | solution.py:410
  36.6 1.7 %shard_map.135 = (bf16[1024,128]{1,0:T(8,128)(2,1)}, bf16[1024,128]{1,0:T(8,128)(2,1)}, bf16[128,128]{1,0:T(8,128)(2,1)S(1)}, bf16[128,128]{1,0:T(8,128)(2,1)S(1)}) custom-call(f32[2,512]{1,0:T(2,128)S(1)} %get-tuple-element.62.bias, bf16[1024,128]{1,0:T(8,128)(2,1)S(1)} %copy-done, bf16[1024,128]{1,0:T(8,128)(2,1)S(1)} %copy-done.2, ...), custom_call_target="tpu_custom_call" | custom-call | flops 335544320 | bytes 2199552 | tf_op jit(solution)/shard_map/pallas_call | solution.py:358
  38.4 1.3 %collective-permute-done.12.refs_0_ = bf16[128,128]{1,0:T(8,128)(2,1)S(1)} collective-permute-done((bf16[128,128]{1,0:T(8,128)(2,1)S(1)}, bf16[128,128]{1,0:T(8,128)(2,1)S(1)}, u32[]{:S(2)}, u32[]{:S(2)}) %collective-permute-start.12) | collective-permute-done | bytes 32800 | tf_op jit(solution)/shard_map/ppermute | solution.py:410
  39.7 1.7 %collective-permute-done.13.refs_1_ = bf16[128,128]{1,0:T(8,128)(2,1)S(1)} collective-permute-done((bf16[128,128]{1,0:T(8,128)(2,1)S(1)}, bf16[128,128]{1,0:T(8,128)(2,1)S(1)}, u32[]{:S(2)}, u32[]{:S(2)}) %collective-permute-start.13) | collective-permute-done | bytes 32800 | tf_op jit(solution)/shard_map/ppermute | solution.py:410
  42.0 1.8 %collective-permute-done.18.other = bf16[2880,128]{1,0:T(8,128)(2,1)S(1)} collective-permute-done((bf16[2880,128]{1,0:T(8,128)(2,1)S(1)}, bf16[2880,128]{1,0:T(8,128)(2,1)S(1)}, u32[]{:S(2)}, u32[]{:S(2)}) %collective-permute-start.18) | collective-permute-done | bytes 737312 | tf_op jit(solution)/shard_map/ppermute | solution.py:407
  43.8 1.2 %shard_map.139 = (f32[128,1280]{1,0:T(8,128)}, f32[16,5120]{1,0:T(8,128)}) custom-call(f32[8,16,128]{2,1,0:T(8,128)S(1)} %get-tuple-element.69.hot, bf16[2880,128]{1,0:T(8,128)(2,1)S(1)} %collective-permute-done.18.other, f32[128,640]{1,0:T(8,128)S(1)} %get-tuple-element.79.own_weight, f32[16,2560]{1,0:T(8,128)S(1)} %get-tuple-element.80.own_gate, ...), custom_call_target="tpu_custom_call" | custom-call | flops 83886080 | bytes 1425408 | tf_op jit(solution)/shard_map/pallas_call | solution.py:358
  45.6 0.7 %shard_map.140 = bf16[128,128]{1,0:T(8,128)(2,1)} custom-call(bf16[128,128]{1,0:T(8,128)(2,1)S(1)} %collective-permute-done.12.refs_0_, bf16[128,128]{1,0:T(8,128)(2,1)S(1)} %collective-permute-done.13.refs_1_, bf16[128,128]{1,0:T(8,128)(2,1)S(1)} %collective-permute-done.14.refs_2_, bf16[128,128]{1,0:T(8,128)(2,1)S(1)} %get-tuple-element.82.refs_3_), custom_call_target="tpu_custom_call" | custom-call | bytes 131072 | tf_op jit(solution)/shard_map/pallas_call | solution.py:358
  (40 shorter events, 5.0 us)
Async XLA Ops:
  0.6 12.4 %copy-start.1 = (f32[16,5120]{1,0:T(8,128)S(1)}, f32[16,5120]{1,0:T(8,128)}, u32[]{:S(2)}) copy-start(f32[16,5120]{1,0:T(8,128)} %gate) | copy-start | bytes 983044
  0.6 6.1 %collective-permute-start = (bf16[128,5120]{1,0:T(8,128)(2,1)}, bf16[128,5120]{1,0:T(8,128)(2,1)S(1)}, u32[]{:S(2)}, u32[]{:S(2)}) collective-permute-start(bf16[128,5120]{1,0:T(8,128)(2,1)} %weight_in), channel_id=1, source_target_pairs={{0,1},{1,0},{2,3},{3,2},{4,5},{5,4},{6,7},{7,6},{8,9},{9,8},{10,11... | collective-permute-start | bytes 3932168 | tf_op jit(solution)/shard_map/ppermute | solution.py:407
  1.2 12.6 %collective-permute-start.2 = (bf16[128,640]{1,0:T(8,128)(2,1)}, bf16[128,640]{1,0:T(8,128)(2,1)S(1)}, u32[]{:S(2)}, u32[]{:S(2)}) collective-permute-start(bf16[128,640]{1,0:T(8,128)(2,1)} %grad_in), channel_id=1, source_target_pairs={{0,2},{1,3},{2,0},{3,1},{4,6},{5,7},{6,4},{7,5},{8,10},{9,11},{10,... | collective-permute-start | bytes 491528 | tf_op jit(solution)/shard_map/ppermute | solution.py:403
  3.7 10.7 %collective-permute-start.3 = (bf16[128,640]{1,0:T(8,128)(2,1)}, bf16[128,640]{1,0:T(8,128)(2,1)S(1)}, u32[]{:S(2)}, u32[]{:S(2)}) collective-permute-start(bf16[128,640]{1,0:T(8,128)(2,1)} %grad_in), channel_id=1, source_target_pairs={{0,4},{1,5},{2,6},{3,7},{4,0},{5,1},{6,2},{7,3},{8,12},{9,13},{10,... | collective-permute-start | bytes 491528 | tf_op jit(solution)/shard_map/ppermute | solution.py:403
  5.2 9.2 %collective-permute-start.4 = (bf16[128,640]{1,0:T(8,128)(2,1)}, bf16[128,640]{1,0:T(8,128)(2,1)S(1)}, u32[]{:S(2)}, u32[]{:S(2)}) collective-permute-start(bf16[128,640]{1,0:T(8,128)(2,1)} %grad_in), channel_id=1, source_target_pairs={{0,6},{1,7},{2,4},{3,5},{4,2},{5,3},{6,0},{7,1},{8,14},{9,15},{10,... | collective-permute-start | bytes 491528 | tf_op jit(solution)/shard_map/ppermute | solution.py:403
  5.3 1.4 %collective-permute-start.1 = (bf16[128,128]{1,0:T(8,128)(2,1)}, bf16[128,128]{1,0:T(8,128)(2,1)S(1)}, u32[]{:S(2)}, u32[]{:S(2)}) collective-permute-start(bf16[128,128]{1,0:T(8,128)(2,1)} %param.12), channel_id=1, source_target_pairs={{0,1},{1,0},{2,3},{3,2},{4,5},{5,4},{6,7},{7,6},{8,9},{9,8},{10,11... | collective-permute-start | bytes 98312 | tf_op jit(solution)/shard_map/ppermute | solution.py:407
  6.7 8.6 %collective-permute-start.6 = (bf16[2,128,128]{2,1,0:T(8,128)(2,1)S(1)}, bf16[2,128,128]{2,1,0:T(8,128)(2,1)S(1)}, u32[]{:S(2)}, u32[]{:S(2)}) collective-permute-start(bf16[2,128,128]{2,1,0:T(8,128)(2,1)S(1)} %pad_maximum_fusion.packed.refs_0_), channel_id=1, source_target_pairs={{0,24},{8,16},{16,8},{24,0},{1,25},{9,17},{17,9},{25,1},{2,26},{10... | collective-permute-start | bytes 196616 | tf_op jit(solution)/shard_map/ppermute | solution.py:410
  10.7 5.9 %collective-permute-start.7 = (bf16[2,128,128]{2,1,0:T(8,128)(2,1)S(1)}, bf16[2,128,128]{2,1,0:T(8,128)(2,1)S(1)}, u32[]{:S(2)}, u32[]{:S(2)}) collective-permute-start(bf16[2,128,128]{2,1,0:T(8,128)(2,1)S(1)} %pad_maximum_fusion.packed.refs_0_), channel_id=1, source_target_pairs={{0,16},{8,24},{16,0},{24,8},{1,17},{9,25},{17,1},{25,9},{2,18},{10... | collective-permute-start | bytes 196616 | tf_op jit(solution)/shard_map/ppermute | solution.py:410
  11.7 1.4 %copy-start.4 = (s32[8]{0:T(128)S(1)}, s32[8]{0:T(128)}, u32[]{:S(2)}) copy-start(s32[8]{0:T(128)} %levels.1) | copy-start | bytes 100
  11.7 1.4 %copy-start.5 = (s32[4]{0:T(128)S(1)}, s32[4]{0:T(128)}, u32[]{:S(2)}) copy-start(s32[4]{0:T(128)} %clips.1) | copy-start | bytes 52
  13.8 4.3 %collective-permute-start.8 = (bf16[2,128,128]{2,1,0:T(8,128)(2,1)S(1)}, bf16[2,128,128]{2,1,0:T(8,128)(2,1)S(1)}, u32[]{:S(2)}, u32[]{:S(2)}) collective-permute-start(bf16[2,128,128]{2,1,0:T(8,128)(2,1)S(1)} %pad_maximum_fusion.packed.refs_0_), channel_id=1, source_target_pairs={{0,8},{8,0},{16,24},{24,16},{1,9},{9,1},{17,25},{25,17},{2,10},{10... | collective-permute-start | bytes 196616 | tf_op jit(solution)/shard_map/ppermute | solution.py:410
  14.4 3.7 %copy-start = (bf16[1024,128]{1,0:T(8,128)(2,1)S(1)}, bf16[1024,128]{1,0:T(8,128)(2,1)}, u32[]{:S(2)}) copy-start(bf16[1024,128]{1,0:T(8,128)(2,1)} %keys.5) | copy-start | bytes 786436
  15.2 17.8 %copy-start.2 = (bf16[1024,128]{1,0:T(8,128)(2,1)S(1)}, bf16[1024,128]{1,0:T(8,128)(2,1)}, u32[]{:S(2)}) copy-start(bf16[1024,128]{1,0:T(8,128)(2,1)} %values.3) | copy-start | bytes 786436
  15.2 3.7 %collective-permute-start.5 = (f32[128,128]{1,0:T(8,128)S(1)}, f32[128,128]{1,0:T(8,128)S(1)}, u32[]{:S(2)}, u32[]{:S(2)}) collective-permute-start(f32[128,128]{1,0:T(8,128)S(1)} %get-tuple-element.55), channel_id=1, source_target_pairs={{0,1},{1,0},{2,3},{3,2},{4,5},{5,4},{6,7},{7,6},{8,9},{9,8},{10,11... | collective-permute-start | bytes 196616 | tf_op jit(solution)/shard_map/ppermute | solution.py:407
  19.0 7.0 %collective-permute-start.10 = (bf16[352,128]{1,0:T(8,128)(2,1)S(1)}, bf16[352,128]{1,0:T(8,128)(2,1)S(1)}, u32[]{:S(2)}, u32[]{:S(2)}) collective-permute-start(bf16[352,128]{1,0:T(8,128)(2,1)S(1)} %get-tuple-element.60), channel_id=1, source_target_pairs={{0,24},{8,16},{16,8},{24,0},{1,25},{9,17},{17,9},{25,1},{2,26},{10... | collective-permute-start | bytes 270344 | tf_op jit(solution)/shard_map/ppermute | solution.py:410
  21.5 7.8 %collective-permute-start.11 = (bf16[352,128]{1,0:T(8,128)(2,1)S(1)}, bf16[352,128]{1,0:T(8,128)(2,1)S(1)}, u32[]{:S(2)}, u32[]{:S(2)}) collective-permute-start(bf16[352,128]{1,0:T(8,128)(2,1)S(1)} %get-tuple-element.61), channel_id=1, source_target_pairs={{0,16},{8,24},{16,0},{24,8},{1,17},{9,25},{17,1},{25,9},{2,18},{10... | collective-permute-start | bytes 270344 | tf_op jit(solution)/shard_map/ppermute | solution.py:410
  22.1 7.3 %collective-permute-start.9 = (bf16[352,128]{1,0:T(8,128)(2,1)S(1)}, bf16[352,128]{1,0:T(8,128)(2,1)S(1)}, u32[]{:S(2)}, u32[]{:S(2)}) collective-permute-start(bf16[352,128]{1,0:T(8,128)(2,1)S(1)} %get-tuple-element.59), channel_id=1, source_target_pairs={{0,8},{8,0},{16,24},{24,16},{1,9},{9,1},{17,25},{25,17},{2,10},{10... | collective-permute-start | bytes 270344 | tf_op jit(solution)/shard_map/ppermute | solution.py:410
  29.4 12.0 %collective-permute-start.15 = (bf16[800,128]{1,0:T(8,128)(2,1)S(1)}, bf16[800,128]{1,0:T(8,128)(2,1)S(1)}, u32[]{:S(2)}, u32[]{:S(2)}) collective-permute-start(bf16[800,128]{1,0:T(8,128)(2,1)S(1)} %shard_map.133.refs_0_), channel_id=1, source_target_pairs={{0,2},{1,3},{2,0},{3,1},{4,6},{5,7},{6,4},{7,5},{8,10},{9,11},{10,... | collective-permute-start | bytes 614408 | tf_op jit(solution)/shard_map/ppermute | solution.py:403
  31.0 10.5 %collective-permute-start.16 = (bf16[800,128]{1,0:T(8,128)(2,1)S(1)}, bf16[800,128]{1,0:T(8,128)(2,1)S(1)}, u32[]{:S(2)}, u32[]{:S(2)}) collective-permute-start(bf16[800,128]{1,0:T(8,128)(2,1)S(1)} %shard_map.133.refs_0_), channel_id=1, source_target_pairs={{0,4},{1,5},{2,6},{3,7},{4,0},{5,1},{6,2},{7,3},{8,12},{9,13},{10,... | collective-permute-start | bytes 614408 | tf_op jit(solution)/shard_map/ppermute | solution.py:403
  32.5 9.0 %collective-permute-start.17 = (bf16[800,128]{1,0:T(8,128)(2,1)S(1)}, bf16[800,128]{1,0:T(8,128)(2,1)S(1)}, u32[]{:S(2)}, u32[]{:S(2)}) collective-permute-start(bf16[800,128]{1,0:T(8,128)(2,1)S(1)} %shard_map.133.refs_0_), channel_id=1, source_target_pairs={{0,6},{1,7},{2,4},{3,5},{4,2},{5,3},{6,0},{7,1},{8,14},{9,15},{10,... | collective-permute-start | bytes 614408 | tf_op jit(solution)/shard_map/ppermute | solution.py:403
  33.9 5.8 %collective-permute-start.12 = (bf16[128,128]{1,0:T(8,128)(2,1)S(1)}, bf16[128,128]{1,0:T(8,128)(2,1)S(1)}, u32[]{:S(2)}, u32[]{:S(2)}) collective-permute-start(bf16[128,128]{1,0:T(8,128)(2,1)S(1)} %get-tuple-element.63), channel_id=1, source_target_pairs={{0,24},{8,16},{16,8},{24,0},{1,25},{9,17},{17,9},{25,1},{2,26},{10... | collective-permute-start | bytes 98312 | tf_op jit(solution)/shard_map/ppermute | solution.py:410
  36.6 4.8 %collective-permute-start.13 = (bf16[128,128]{1,0:T(8,128)(2,1)S(1)}, bf16[128,128]{1,0:T(8,128)(2,1)S(1)}, u32[]{:S(2)}, u32[]{:S(2)}) collective-permute-start(bf16[128,128]{1,0:T(8,128)(2,1)S(1)} %get-tuple-element.64), channel_id=1, source_target_pairs={{0,16},{8,24},{16,0},{24,8},{1,17},{9,25},{17,1},{25,9},{2,18},{10... | collective-permute-start | bytes 98312 | tf_op jit(solution)/shard_map/ppermute | solution.py:410
  41.5 2.3 %collective-permute-start.18 = (bf16[2880,128]{1,0:T(8,128)(2,1)S(1)}, bf16[2880,128]{1,0:T(8,128)(2,1)S(1)}, u32[]{:S(2)}, u32[]{:S(2)}) collective-permute-start(bf16[2880,128]{1,0:T(8,128)(2,1)S(1)} %shard_map.137.own), channel_id=1, source_target_pairs={{0,1},{1,0},{2,3},{3,2},{4,5},{5,4},{6,7},{7,6},{8,9},{9,8},{10,11... | collective-permute-start | bytes 2211848 | tf_op jit(solution)/shard_map/ppermute | solution.py:407
  41.6 4.0 %collective-permute-start.14 = (bf16[128,128]{1,0:T(8,128)(2,1)S(1)}, bf16[128,128]{1,0:T(8,128)(2,1)S(1)}, u32[]{:S(2)}, u32[]{:S(2)}) collective-permute-start(bf16[128,128]{1,0:T(8,128)(2,1)S(1)} %get-tuple-element.67), channel_id=1, source_target_pairs={{0,8},{8,0},{16,24},{24,16},{1,9},{9,1},{17,25},{25,17},{2,10},{10... | collective-permute-start | bytes 98312 | tf_op jit(solution)/shard_map/ppermute | solution.py:410
  (1 other events, 0.9 us)

commit v20 on v18

--- a/solution.py
+++ b/solution.py
@@ -210,12 +210,12 @@
 
 
 def grads_kernel(n_t, starts, first, last, bias, keys, values, *refs):
-    packed, heads = refs[:n_t], refs[n_t : 2 * n_t][::-1]
+    packed, heads = far_first(refs[:n_t]), last_swapped(refs[n_t : 2 * n_t])
     refs = refs[2 * n_t :]
     if first == 0:
         sums, refs = refs[:2], refs[2:]
     key_out, value_out = refs[:2]
-    outs = refs[2 : 2 + last - first][::-1]
+    outs = refs[2 : 2 + last - first]
     accs = refs[2 + last - first :]
     rows = packed[0].shape[1]
     ones = jnp.ones((8, HD), jnp.float32)
@@ -470,22 +470,22 @@
     accs = [pltpu.VMEM((k_rows, HD), f32)] * 2
     far = call(
         functools.partial(grads_kernel, n_t, starts, 2, n_t),
-        [later_bias, keys, values] + packed_all + heads_all[::-1],
+        [later_bias, keys, values] + far_first(packed_all) + last_swapped(heads_all),
         [shape(f32, k_rows, HD)] * 2 + [shape(bf16, HD, rows)] * (n_t - 2),
         accs,
         flops=10 * (n_t - 2) * rows * k_rows * HD,
     )
-    parts = {k: over_time(far[1 + n_t - k], k) for k in range(n_t - 1, 1, -1)}
+    parts = {k: over_time(far[k], k) for k in range(2, n_t)}
     near = call(
         functools.partial(grads_kernel, n_t, starts, 0, 2),
-        [bias, keys, values] + packed_all + heads_all[::-1] + list(far[:2]),
+        [bias, keys, values] + far_first(packed_all) + last_swapped(heads_all) + list(far[:2]),
         [shape(bf16, k_rows, HD)] * 2 + [shape(bf16, HD, rows)] * 2,
         flops=20 * rows * k_rows * HD,
     )
     key_grad, value_grad = near[:2]
-    parts[0], parts[1] = near[3], over_time(near[2], 1)
+    parts[0], parts[1] = near[2], over_time(near[3], 1)
     parts = [parts[k] for k in range(n_t)]
-    bundles, _ = lax.optimization_barrier((bundles, (key_grad, parts[: n_t // 2 - 1 : -1])))
+    bundles, _ = lax.optimization_barrier((bundles, (key_grad, parts[n_t // 2 :])))
     collected = call(
         functools.partial(collect_kernel, chips, base),
         bundles,
@@ -508,7 +508,7 @@
         flops=2 * n_t * rows * width * HD,
     )
     parts[0], _ = lax.optimization_barrier((parts[0], gate_grad))
-    query_grad = call(functools.partial(query_kernel, n_t), parts[::-1], shape(bf16, rows, HD))
+    query_grad = call(functools.partial(query_kernel, n_t), parts, shape(bf16, rows, HD))
     if width != shard:
         weight_grad = without_padding(weight_grad, 2, shard)
         gate_grad = without_padding(gate_grad, n_s, shard)

time: 46.6 us -> 46.5 us (level)
    ppermute x9, waiting for transfers between devices: 12.3 us -> 11.3 us  [over_time(): return lax.ppermute(x, 'tm', [(t, t ^ k) for t in range(n_t)])]
    ppermute x6, waiting for transfers between devices: 0.02 us -> 0.94 us  [over_chips(): lax.ppermute(x, 'space', [(s, s ^ 2 * k) for s in range(n_s)])]
  transfers between devices with their start and end apart: 19 -> 19, of which waited for: 9 -> 10; matrix products, arithmetic and copies ran while one was open for 2% -> 2% of each run, Pallas kernels for 17% -> 17%
where the time goes in v20:
time: 46.5 us; the launch traced here: 46.3 us
  starting transfers between devices  20.3 us (44%)
  waiting for transfers between devices  14.6 us (31%)
  Pallas kernels  8.88 us (19%)
  local copies, waits for them, and re-layouts  0.94 us (2%)
  between operations  0.8 us (2%)
  other arithmetic  0.78 us (2%)
    ppermute x9, starting transfers between devices, over_time(): return lax.ppermute(x, 'tm', [(t, t ^ k) for t in range(n_t)])  12 us
    ppermute x9, waiting for transfers between devices, over_time(): return lax.ppermute(x, 'tm', [(t, t ^ k) for t in range(n_t)])  11.3 us
    pallas_call x12, Pallas kernels, call(): pl.pallas_call(kernel, out_shape=out_shape, in_specs=[pl.BlockSpec(memory...  8.88 us
    ppermute x6, starting transfers between devices, over_chips(): lax.ppermute(x, 'space', [(s, s ^ 2 * k) for s in range(n_s)])  7.66 us
    ppermute x4, waiting for transfers between devices, over_cores(): return lax.ppermute(x, 'space', [(s, s ^ 1) for s in range(n_s)])  2.36 us
    ppermute x6, waiting for transfers between devices, over_chips(): lax.ppermute(x, 'space', [(s, s ^ 2 * k) for s in range(n_s)])  0.94 us
    unnamed x12, local copies, waits for them, and re-layouts  0.94 us
  transfers between devices with their start and end apart: 19, of which 10 were waited for; matrix products, arithmetic and copies ran while one was open for 2% of the time, Pallas kernels for 17%

profile of v20, /device:TPU:0, one launch (start us, length us, event | category | flops | bytes accessed | tf_op | source)
XLA Modules:
  0.0 46.3 jit_solution(7590833088507302622)
XLA Ops:
  1.2 2.6 %collective-permute-start.5 = (bf16[128,640]{1,0:T(8,128)(2,1)}, bf16[128,640]{1,0:T(8,128)(2,1)S(1)}, u32[]{:S(2)}, u32[]{:S(2)}) collective-permute-start(bf16[128,640]{1,0:T(8,128)(2,1)} %grad_in), channel_id=1, source_target_pairs={{0,2},{1,3},{2,0},{3,1},{4,6},{5,7},{6,4},{7,5},{8,10},{9,11},{10,... | collective-permute-start | bytes 491528 | tf_op jit(solution)/shard_map/ppermute | solution.py:398
  3.7 1.5 %collective-permute-start.6 = (bf16[128,640]{1,0:T(8,128)(2,1)}, bf16[128,640]{1,0:T(8,128)(2,1)S(1)}, u32[]{:S(2)}, u32[]{:S(2)}) collective-permute-start(bf16[128,640]{1,0:T(8,128)(2,1)} %grad_in), channel_id=1, source_target_pairs={{0,4},{1,5},{2,6},{3,7},{4,0},{5,1},{6,2},{7,3},{8,12},{9,13},{10,... | collective-permute-start | bytes 491528 | tf_op jit(solution)/shard_map/ppermute | solution.py:398
  5.3 0.8 %pad_maximum_fusion.packed.refs_0_ = bf16[2,128,128]{2,1,0:T(8,128)(2,1)S(1)} fusion(bf16[1,128,128]{2,1,0:T(8,128)(2,1)} %bitcast.3, bf16[1,128,128]{2,1,0:T(8,128)(2,1)} %bitcast.2), kind=kLoop, calls=%fused_computation | loop fusion | flops 32768 | bytes 131072 | tf_op jit(solution)/shard_map/stack | solution.py:419
  6.7 4.1 %collective-permute-start.2 = (bf16[2,128,128]{2,1,0:T(8,128)(2,1)S(1)}, bf16[2,128,128]{2,1,0:T(8,128)(2,1)S(1)}, u32[]{:S(2)}, u32[]{:S(2)}) collective-permute-start(bf16[2,128,128]{2,1,0:T(8,128)(2,1)S(1)} %pad_maximum_fusion.packed.refs_0_), channel_id=1, source_target_pairs={{0,24},{8,16},{16,8},{24,0},{1,25},{9,17},{17,9},{25,1},{2,26},{10... | collective-permute-start | bytes 196616 | tf_op jit(solution)/shard_map/ppermute | solution.py:405
  10.8 0.9 %copy-done.3 = bf16[128,640]{1,0:T(8,128)(2,1)S(1)} copy-done((bf16[128,640]{1,0:T(8,128)(2,1)S(1)}, bf16[128,640]{1,0:T(8,128)(2,1)}, u32[]{:S(2)}) %copy-start.3) | copy-done | bytes 163864
  11.7 1.4 %shard_map.129 = (bf16[4,128,640]{2,1,0:T(8,128)(2,1)S(1)}, bf16[128,640]{1,0:T(8,128)(2,1)S(1)}) custom-call(bf16[128,5120]{1,0:T(8,128)(2,1)} %weight_in, bf16[128,640]{1,0:T(8,128)(2,1)S(1)} %copy-done.3), custom_call_target="tpu_custom_call" | custom-call | bytes 1474560 | tf_op jit(solution)/shard_map/pallas_call | solution.py:353
  14.4 0.8 %shard_map.130 = (f32[128,128]{1,0:T(8,128)S(1)}, f32[128,128]{1,0:T(8,128)S(1)}, f32[40,128]{1,0:T(8,128)S(1)}) custom-call(bf16[2,128,128]{2,1,0:T(8,128)(2,1)S(1)} %pad_maximum_fusion.packed.refs_0_, bf16[128,128]{1,0:T(8,128)(2,1)S(1)} %collective-permute-done.1.other_saved, bf16[4,128,640]{2,1,0:T(8,128)(2,1)S(1)} %get-tuple-element.46.kept, ...), custom_call_target="tpu_custom_call" | custom-call | flops 335544320 | bytes 2740224 | tf_op jit(solution)/shard_map/pallas_call | solution.py:353
  15.3 1.4 %collective-permute-done.3.refs_2_ = bf16[2,128,128]{2,1,0:T(8,128)(2,1)S(1)} collective-permute-done((bf16[2,128,128]{2,1,0:T(8,128)(2,1)S(1)}, bf16[2,128,128]{2,1,0:T(8,128)(2,1)S(1)}, u32[]{:S(2)}, u32[]{:S(2)}) %collective-permute-start.3) | collective-permute-done | bytes 65568 | tf_op jit(solution)/shard_map/ppermute | solution.py:405
  16.7 1.4 %collective-permute-done.4.refs_3_.refs_1_ = bf16[2,128,128]{2,1,0:T(8,128)(2,1)S(1)} collective-permute-done((bf16[2,128,128]{2,1,0:T(8,128)(2,1)S(1)}, bf16[2,128,128]{2,1,0:T(8,128)(2,1)S(1)}, u32[]{:S(2)}, u32[]{:S(2)}) %collective-permute-start.4) | collective-permute-done | bytes 65568 | tf_op jit(solution)/shard_map/ppermute | solution.py:405
  18.1 0.8 %shard_map.131.stats = f32[8,128]{1,0:T(8,128)S(1)} custom-call(f32[2,512]{1,0:T(2,128)S(1)} %get-tuple-element.58.bias, bf16[1024,128]{1,0:T(8,128)(2,1)S(1)} %copy-done, bf16[2,128,128]{2,1,0:T(8,128)(2,1)S(1)} %pad_maximum_fusion.packed.refs_0_, bf16[2,128,128]{2,1,0:T(8,128)(2,1)S(1)} %collective-permute-done.2.refs_1_.refs_3_, ...), custom_call_target="tpu_custom_call" | custom-call | flops 134217728 | bytes 528384 | tf_op jit(solution)/shard_map/pallas_call | solution.py:353
  19.0 2.5 %collective-permute-start.10 = (bf16[352,128]{1,0:T(8,128)(2,1)S(1)}, bf16[352,128]{1,0:T(8,128)(2,1)S(1)}, u32[]{:S(2)}, u32[]{:S(2)}) collective-permute-start(bf16[352,128]{1,0:T(8,128)(2,1)S(1)} %get-tuple-element.55), channel_id=1, source_target_pairs={{0,24},{8,16},{16,8},{24,0},{1,25},{9,17},{17,9},{25,1},{2,26},{10... | collective-permute-start | bytes 270344 | tf_op jit(solution)/shard_map/ppermute | solution.py:405
  22.1 1.4 %collective-permute-start.9 = (bf16[352,128]{1,0:T(8,128)(2,1)S(1)}, bf16[352,128]{1,0:T(8,128)(2,1)S(1)}, u32[]{:S(2)}, u32[]{:S(2)}) collective-permute-start(bf16[352,128]{1,0:T(8,128)(2,1)S(1)} %get-tuple-element.54), channel_id=1, source_target_pairs={{0,8},{8,0},{16,24},{24,16},{1,9},{9,1},{17,25},{25,17},{2,10},{10... | collective-permute-start | bytes 270344 | tf_op jit(solution)/shard_map/ppermute | solution.py:405
  23.5 2.5 %collective-permute-done.10.refs_2_.refs_6_ = bf16[352,128]{1,0:T(8,128)(2,1)S(1)} collective-permute-done((bf16[352,128]{1,0:T(8,128)(2,1)S(1)}, bf16[352,128]{1,0:T(8,128)(2,1)S(1)}, u32[]{:S(2)}, u32[]{:S(2)}) %collective-permute-start.10) | collective-permute-done | bytes 90144 | tf_op jit(solution)/shard_map/ppermute | solution.py:405
  26.0 3.3 %collective-permute-done.11.refs_3_.refs_7_ = bf16[352,128]{1,0:T(8,128)(2,1)S(1)} collective-permute-done((bf16[352,128]{1,0:T(8,128)(2,1)S(1)}, bf16[352,128]{1,0:T(8,128)(2,1)S(1)}, u32[]{:S(2)}, u32[]{:S(2)}) %collective-permute-start.11) | collective-permute-done | bytes 90144 | tf_op jit(solution)/shard_map/ppermute | solution.py:405
  29.4 1.6 %collective-permute-start.12 = (bf16[800,128]{1,0:T(8,128)(2,1)S(1)}, bf16[800,128]{1,0:T(8,128)(2,1)S(1)}, u32[]{:S(2)}, u32[]{:S(2)}) collective-permute-start(bf16[800,128]{1,0:T(8,128)(2,1)S(1)} %shard_map.133.refs_0_), channel_id=1, source_target_pairs={{0,2},{1,3},{2,0},{3,1},{4,6},{5,7},{6,4},{7,5},{8,10},{9,11},{10,... | collective-permute-start | bytes 614408 | tf_op jit(solution)/shard_map/ppermute | solution.py:398
  31.0 1.5 %collective-permute-start.13 = (bf16[800,128]{1,0:T(8,128)(2,1)S(1)}, bf16[800,128]{1,0:T(8,128)(2,1)S(1)}, u32[]{:S(2)}, u32[]{:S(2)}) collective-permute-start(bf16[800,128]{1,0:T(8,128)(2,1)S(1)} %shard_map.133.refs_0_), channel_id=1, source_target_pairs={{0,4},{1,5},{2,6},{3,7},{4,0},{5,1},{6,2},{7,3},{8,12},{9,13},{10,... | collective-permute-start | bytes 614408 | tf_op jit(solution)/shard_map/ppermute | solution.py:398
  33.0 1.0 %shard_map.134 = (f32[1024,128]{1,0:T(8,128)S(1)}, f32[1024,128]{1,0:T(8,128)S(1)}, bf16[128,128]{1,0:T(8,128)(2,1)S(1)}, bf16[128,128]{1,0:T(8,128)(2,1)S(1)}) custom-call(f32[2,512]{1,0:T(2,128)S(1)} %get-tuple-element.58.bias, bf16[1024,128]{1,0:T(8,128)(2,1)S(1)} %copy-done, bf16[1024,128]{1,0:T(8,128)(2,1)S(1)} %copy-done.2, ...), custom_call_target="tpu_custom_call" | custom-call | flops 335544320 | bytes 1150976 | tf_op jit(solution)/shard_map/pallas_call | solution.py:353
  34.0 0.8 %collective-permute-start.15 = (bf16[128,128]{1,0:T(8,128)(2,1)S(1)}, bf16[128,128]{1,0:T(8,128)(2,1)S(1)}, u32[]{:S(2)}, u32[]{:S(2)}) collective-permute-start(bf16[128,128]{1,0:T(8,128)(2,1)S(1)} %get-tuple-element.64), channel_id=1, source_target_pairs={{0,16},{8,24},{16,0},{24,8},{1,17},{9,25},{17,1},{25,9},{2,18},{10... | collective-permute-start | bytes 98312 | tf_op jit(solution)/shard_map/ppermute | solution.py:405
  34.8 1.9 %collective-permute-start.16 = (bf16[128,128]{1,0:T(8,128)(2,1)S(1)}, bf16[128,128]{1,0:T(8,128)(2,1)S(1)}, u32[]{:S(2)}, u32[]{:S(2)}) collective-permute-start(bf16[128,128]{1,0:T(8,128)(2,1)S(1)} %get-tuple-element.65), channel_id=1, source_target_pairs={{0,24},{8,16},{16,8},{24,0},{1,25},{9,17},{17,9},{25,1},{2,26},{10... | collective-permute-start | bytes 98312 | tf_op jit(solution)/shard_map/ppermute | solution.py:405
  36.7 1.7 %shard_map.135 = (bf16[1024,128]{1,0:T(8,128)(2,1)}, bf16[1024,128]{1,0:T(8,128)(2,1)}, bf16[128,128]{1,0:T(8,128)(2,1)S(1)}, bf16[128,128]{1,0:T(8,128)(2,1)S(1)}) custom-call(f32[2,512]{1,0:T(2,128)S(1)} %get-tuple-element.58.bias, bf16[1024,128]{1,0:T(8,128)(2,1)S(1)} %copy-done, bf16[1024,128]{1,0:T(8,128)(2,1)S(1)} %copy-done.2, ...), custom_call_target="tpu_custom_call" | custom-call | flops 335544320 | bytes 2199552 | tf_op jit(solution)/shard_map/pallas_call | solution.py:353
  38.9 1.6 %collective-permute-done.16.refs_3_ = bf16[128,128]{1,0:T(8,128)(2,1)S(1)} collective-permute-done((bf16[128,128]{1,0:T(8,128)(2,1)S(1)}, bf16[128,128]{1,0:T(8,128)(2,1)S(1)}, u32[]{:S(2)}, u32[]{:S(2)}) %collective-permute-start.16) | collective-permute-done | bytes 32800 | tf_op jit(solution)/shard_map/ppermute | solution.py:405
  40.5 0.9 %collective-permute-done.13.refs_2_ = bf16[800,128]{1,0:T(8,128)(2,1)S(1)} collective-permute-done((bf16[800,128]{1,0:T(8,128)(2,1)S(1)}, bf16[800,128]{1,0:T(8,128)(2,1)S(1)}, u32[]{:S(2)}, u32[]{:S(2)}) %collective-permute-start.13) | collective-permute-done | bytes 204832 | tf_op jit(solution)/shard_map/ppermute | solution.py:398
  42.1 1.7 %collective-permute-done.17.other = bf16[2880,128]{1,0:T(8,128)(2,1)S(1)} collective-permute-done((bf16[2880,128]{1,0:T(8,128)(2,1)S(1)}, bf16[2880,128]{1,0:T(8,128)(2,1)S(1)}, u32[]{:S(2)}, u32[]{:S(2)}) %collective-permute-start.17) | collective-permute-done | bytes 737312 | tf_op jit(solution)/shard_map/ppermute | solution.py:402
  43.8 1.3 %shard_map.138 = (f32[128,1280]{1,0:T(8,128)}, f32[16,5120]{1,0:T(8,128)}) custom-call(f32[8,16,128]{2,1,0:T(8,128)S(1)} %get-tuple-element.62.hot, bf16[2880,128]{1,0:T(8,128)(2,1)S(1)} %collective-permute-done.17.other, f32[128,640]{1,0:T(8,128)S(1)} %get-tuple-element.70.own_weight, f32[16,2560]{1,0:T(8,128)S(1)} %get-tuple-element.71.own_gate, ...), custom_call_target="tpu_custom_call" | custom-call | flops 83886080 | bytes 1556480 | tf_op jit(solution)/shard_map/pallas_call | solution.py:353
  (39 shorter events, 6.2 us)
Async XLA Ops:
  0.6 12.4 %copy-start.1 = (f32[16,5120]{1,0:T(8,128)S(1)}, f32[16,5120]{1,0:T(8,128)}, u32[]{:S(2)}) copy-start(f32[16,5120]{1,0:T(8,128)} %gate) | copy-start | bytes 983044
  0.6 6.1 %collective-permute-start = (bf16[128,5120]{1,0:T(8,128)(2,1)}, bf16[128,5120]{1,0:T(8,128)(2,1)S(1)}, u32[]{:S(2)}, u32[]{:S(2)}) collective-permute-start(bf16[128,5120]{1,0:T(8,128)(2,1)} %weight_in), channel_id=1, source_target_pairs={{0,1},{1,0},{2,3},{3,2},{4,5},{5,4},{6,7},{7,6},{8,9},{9,8},{10,11... | collective-permute-start | bytes 3932168 | tf_op jit(solution)/shard_map/ppermute | solution.py:402
  1.2 12.6 %collective-permute-start.5 = (bf16[128,640]{1,0:T(8,128)(2,1)}, bf16[128,640]{1,0:T(8,128)(2,1)S(1)}, u32[]{:S(2)}, u32[]{:S(2)}) collective-permute-start(bf16[128,640]{1,0:T(8,128)(2,1)} %grad_in), channel_id=1, source_target_pairs={{0,2},{1,3},{2,0},{3,1},{4,6},{5,7},{6,4},{7,5},{8,10},{9,11},{10,... | collective-permute-start | bytes 491528 | tf_op jit(solution)/shard_map/ppermute | solution.py:398
  3.7 10.7 %collective-permute-start.6 = (bf16[128,640]{1,0:T(8,128)(2,1)}, bf16[128,640]{1,0:T(8,128)(2,1)S(1)}, u32[]{:S(2)}, u32[]{:S(2)}) collective-permute-start(bf16[128,640]{1,0:T(8,128)(2,1)} %grad_in), channel_id=1, source_target_pairs={{0,4},{1,5},{2,6},{3,7},{4,0},{5,1},{6,2},{7,3},{8,12},{9,13},{10,... | collective-permute-start | bytes 491528 | tf_op jit(solution)/shard_map/ppermute | solution.py:398
  5.2 9.2 %collective-permute-start.7 = (bf16[128,640]{1,0:T(8,128)(2,1)}, bf16[128,640]{1,0:T(8,128)(2,1)S(1)}, u32[]{:S(2)}, u32[]{:S(2)}) collective-permute-start(bf16[128,640]{1,0:T(8,128)(2,1)} %grad_in), channel_id=1, source_target_pairs={{0,6},{1,7},{2,4},{3,5},{4,2},{5,3},{6,0},{7,1},{8,14},{9,15},{10,... | collective-permute-start | bytes 491528 | tf_op jit(solution)/shard_map/ppermute | solution.py:398
  5.3 1.4 %collective-permute-start.1 = (bf16[128,128]{1,0:T(8,128)(2,1)}, bf16[128,128]{1,0:T(8,128)(2,1)S(1)}, u32[]{:S(2)}, u32[]{:S(2)}) collective-permute-start(bf16[128,128]{1,0:T(8,128)(2,1)} %param.12), channel_id=1, source_target_pairs={{0,1},{1,0},{2,3},{3,2},{4,5},{5,4},{6,7},{7,6},{8,9},{9,8},{10,11... | collective-permute-start | bytes 98312 | tf_op jit(solution)/shard_map/ppermute | solution.py:402
  6.7 8.6 %collective-permute-start.2 = (bf16[2,128,128]{2,1,0:T(8,128)(2,1)S(1)}, bf16[2,128,128]{2,1,0:T(8,128)(2,1)S(1)}, u32[]{:S(2)}, u32[]{:S(2)}) collective-permute-start(bf16[2,128,128]{2,1,0:T(8,128)(2,1)S(1)} %pad_maximum_fusion.packed.refs_0_), channel_id=1, source_target_pairs={{0,24},{8,16},{16,8},{24,0},{1,25},{9,17},{17,9},{25,1},{2,26},{10... | collective-permute-start | bytes 196616 | tf_op jit(solution)/shard_map/ppermute | solution.py:405
  10.7 5.9 %collective-permute-start.3 = (bf16[2,128,128]{2,1,0:T(8,128)(2,1)S(1)}, bf16[2,128,128]{2,1,0:T(8,128)(2,1)S(1)}, u32[]{:S(2)}, u32[]{:S(2)}) collective-permute-start(bf16[2,128,128]{2,1,0:T(8,128)(2,1)S(1)} %pad_maximum_fusion.packed.refs_0_), channel_id=1, source_target_pairs={{0,16},{8,24},{16,0},{24,8},{1,17},{9,25},{17,1},{25,9},{2,18},{10... | collective-permute-start | bytes 196616 | tf_op jit(solution)/shard_map/ppermute | solution.py:405
  11.7 1.4 %copy-start.4 = (s32[8]{0:T(128)S(1)}, s32[8]{0:T(128)}, u32[]{:S(2)}) copy-start(s32[8]{0:T(128)} %levels.1) | copy-start | bytes 100
  11.7 1.4 %copy-start.5 = (s32[4]{0:T(128)S(1)}, s32[4]{0:T(128)}, u32[]{:S(2)}) copy-start(s32[4]{0:T(128)} %clips.1) | copy-start | bytes 52
  13.8 4.3 %collective-permute-start.4 = (bf16[2,128,128]{2,1,0:T(8,128)(2,1)S(1)}, bf16[2,128,128]{2,1,0:T(8,128)(2,1)S(1)}, u32[]{:S(2)}, u32[]{:S(2)}) collective-permute-start(bf16[2,128,128]{2,1,0:T(8,128)(2,1)S(1)} %pad_maximum_fusion.packed.refs_0_), channel_id=1, source_target_pairs={{0,8},{8,0},{16,24},{24,16},{1,9},{9,1},{17,25},{25,17},{2,10},{10... | collective-permute-start | bytes 196616 | tf_op jit(solution)/shard_map/ppermute | solution.py:405
  14.4 3.7 %copy-start = (bf16[1024,128]{1,0:T(8,128)(2,1)S(1)}, bf16[1024,128]{1,0:T(8,128)(2,1)}, u32[]{:S(2)}) copy-start(bf16[1024,128]{1,0:T(8,128)(2,1)} %keys.5) | copy-start | bytes 786436
  15.2 17.8 %copy-start.2 = (bf16[1024,128]{1,0:T(8,128)(2,1)S(1)}, bf16[1024,128]{1,0:T(8,128)(2,1)}, u32[]{:S(2)}) copy-start(bf16[1024,128]{1,0:T(8,128)(2,1)} %values.3) | copy-start | bytes 786436
  15.2 3.7 %collective-permute-start.8 = (f32[128,128]{1,0:T(8,128)S(1)}, f32[128,128]{1,0:T(8,128)S(1)}, u32[]{:S(2)}, u32[]{:S(2)}) collective-permute-start(f32[128,128]{1,0:T(8,128)S(1)} %get-tuple-element.50), channel_id=1, source_target_pairs={{0,1},{1,0},{2,3},{3,2},{4,5},{5,4},{6,7},{7,6},{8,9},{9,8},{10,11... | collective-permute-start | bytes 196616 | tf_op jit(solution)/shard_map/ppermute | solution.py:402
  19.0 7.0 %collective-permute-start.10 = (bf16[352,128]{1,0:T(8,128)(2,1)S(1)}, bf16[352,128]{1,0:T(8,128)(2,1)S(1)}, u32[]{:S(2)}, u32[]{:S(2)}) collective-permute-start(bf16[352,128]{1,0:T(8,128)(2,1)S(1)} %get-tuple-element.55), channel_id=1, source_target_pairs={{0,24},{8,16},{16,8},{24,0},{1,25},{9,17},{17,9},{25,1},{2,26},{10... | collective-permute-start | bytes 270344 | tf_op jit(solution)/shard_map/ppermute | solution.py:405
  21.5 7.8 %collective-permute-start.11 = (bf16[352,128]{1,0:T(8,128)(2,1)S(1)}, bf16[352,128]{1,0:T(8,128)(2,1)S(1)}, u32[]{:S(2)}, u32[]{:S(2)}) collective-permute-start(bf16[352,128]{1,0:T(8,128)(2,1)S(1)} %get-tuple-element.56), channel_id=1, source_target_pairs={{0,16},{8,24},{16,0},{24,8},{1,17},{9,25},{17,1},{25,9},{2,18},{10... | collective-permute-start | bytes 270344 | tf_op jit(solution)/shard_map/ppermute | solution.py:405
  22.1 7.3 %collective-permute-start.9 = (bf16[352,128]{1,0:T(8,128)(2,1)S(1)}, bf16[352,128]{1,0:T(8,128)(2,1)S(1)}, u32[]{:S(2)}, u32[]{:S(2)}) collective-permute-start(bf16[352,128]{1,0:T(8,128)(2,1)S(1)} %get-tuple-element.54), channel_id=1, source_target_pairs={{0,8},{8,0},{16,24},{24,16},{1,9},{9,1},{17,25},{25,17},{2,10},{10... | collective-permute-start | bytes 270344 | tf_op jit(solution)/shard_map/ppermute | solution.py:405
  29.4 11.1 %collective-permute-start.12 = (bf16[800,128]{1,0:T(8,128)(2,1)S(1)}, bf16[800,128]{1,0:T(8,128)(2,1)S(1)}, u32[]{:S(2)}, u32[]{:S(2)}) collective-permute-start(bf16[800,128]{1,0:T(8,128)(2,1)S(1)} %shard_map.133.refs_0_), channel_id=1, source_target_pairs={{0,2},{1,3},{2,0},{3,1},{4,6},{5,7},{6,4},{7,5},{8,10},{9,11},{10,... | collective-permute-start | bytes 614408 | tf_op jit(solution)/shard_map/ppermute | solution.py:398
  31.0 10.5 %collective-permute-start.13 = (bf16[800,128]{1,0:T(8,128)(2,1)S(1)}, bf16[800,128]{1,0:T(8,128)(2,1)S(1)}, u32[]{:S(2)}, u32[]{:S(2)}) collective-permute-start(bf16[800,128]{1,0:T(8,128)(2,1)S(1)} %shard_map.133.refs_0_), channel_id=1, source_target_pairs={{0,4},{1,5},{2,6},{3,7},{4,0},{5,1},{6,2},{7,3},{8,12},{9,13},{10,... | collective-permute-start | bytes 614408 | tf_op jit(solution)/shard_map/ppermute | solution.py:398
  32.5 8.9 %collective-permute-start.14 = (bf16[800,128]{1,0:T(8,128)(2,1)S(1)}, bf16[800,128]{1,0:T(8,128)(2,1)S(1)}, u32[]{:S(2)}, u32[]{:S(2)}) collective-permute-start(bf16[800,128]{1,0:T(8,128)(2,1)S(1)} %shard_map.133.refs_0_), channel_id=1, source_target_pairs={{0,6},{1,7},{2,4},{3,5},{4,2},{5,3},{6,0},{7,1},{8,14},{9,15},{10,... | collective-permute-start | bytes 614408 | tf_op jit(solution)/shard_map/ppermute | solution.py:398
  34.0 4.9 %collective-permute-start.15 = (bf16[128,128]{1,0:T(8,128)(2,1)S(1)}, bf16[128,128]{1,0:T(8,128)(2,1)S(1)}, u32[]{:S(2)}, u32[]{:S(2)}) collective-permute-start(bf16[128,128]{1,0:T(8,128)(2,1)S(1)} %get-tuple-element.64), channel_id=1, source_target_pairs={{0,16},{8,24},{16,0},{24,8},{1,17},{9,25},{17,1},{25,9},{2,18},{10... | collective-permute-start | bytes 98312 | tf_op jit(solution)/shard_map/ppermute | solution.py:405
  34.8 5.7 %collective-permute-start.16 = (bf16[128,128]{1,0:T(8,128)(2,1)S(1)}, bf16[128,128]{1,0:T(8,128)(2,1)S(1)}, u32[]{:S(2)}, u32[]{:S(2)}) collective-permute-start(bf16[128,128]{1,0:T(8,128)(2,1)S(1)} %get-tuple-element.65), channel_id=1, source_target_pairs={{0,24},{8,16},{16,8},{24,0},{1,25},{9,17},{17,9},{25,1},{2,26},{10... | collective-permute-start | bytes 98312 | tf_op jit(solution)/shard_map/ppermute | solution.py:405
  41.5 2.3 %collective-permute-start.17 = (bf16[2880,128]{1,0:T(8,128)(2,1)S(1)}, bf16[2880,128]{1,0:T(8,128)(2,1)S(1)}, u32[]{:S(2)}, u32[]{:S(2)}) collective-permute-start(bf16[2880,128]{1,0:T(8,128)(2,1)S(1)} %shard_map.136.own), channel_id=1, source_target_pairs={{0,1},{1,0},{2,3},{3,2},{4,5},{5,4},{6,7},{7,6},{8,9},{9,8},{10,11... | collective-permute-start | bytes 2211848 | tf_op jit(solution)/shard_map/ppermute | solution.py:402
  41.6 4.0 %collective-permute-start.18 = (bf16[128,128]{1,0:T(8,128)(2,1)S(1)}, bf16[128,128]{1,0:T(8,128)(2,1)S(1)}, u32[]{:S(2)}, u32[]{:S(2)}) collective-permute-start(bf16[128,128]{1,0:T(8,128)(2,1)S(1)} %get-tuple-element.74), channel_id=1, source_target_pairs={{0,8},{8,0},{16,24},{24,16},{1,9},{9,1},{17,25},{25,17},{2,10},{10... | collective-permute-start | bytes 98312 | tf_op jit(solution)/shard_map/ppermute | solution.py:405
  (1 other events, 0.9 us)

commit v21 on v20

--- a/solution.py
+++ b/solution.py
@@ -195,7 +195,7 @@
 
 
 def collect_kernel(chips, base, *refs):
-    pieces, out, held = refs[:chips], refs[chips], refs[chips + 1]
+    pieces, out, held = far_first(refs[:chips]), refs[chips], refs[chips + 1]
     chip = place()[1]
     for k in range(chips):
         out[k * base : (k + 1) * base, :] = pieces[k][:base, :]
@@ -466,6 +466,7 @@
         shape(bf16, base + n_t * count, LANES),
     )
     bundles = over_chips(bundle)
+    bundles = far_first(bundles)
     later_bias, _ = lax.optimization_barrier((bias, bundle))
     accs = [pltpu.VMEM((k_rows, HD), f32)] * 2
     far = call(

time: 46.5 us -> 46.3 us (level)
  transfers between devices with their start and end apart: 19 -> 19, of which waited for: 10 -> 11; matrix products, arithmetic and copies ran while one was open for 2% -> 2% of each run, Pallas kernels for 17% -> 17%
where the time goes in v21:
time: 46.3 us; the launch traced here: 46.1 us
  starting transfers between devices  20.5 us (44%)
  waiting for transfers between devices  14.2 us (31%)
  Pallas kernels  8.87 us (19%)
  local copies, waits for them, and re-layouts  0.94 us (2%)
  between operations  0.79 us (2%)
  other arithmetic  0.78 us (2%)
    ppermute x9, starting transfers between devices, over_time(): return lax.ppermute(x, 'tm', [(t, t ^ k) for t in range(n_t)])  12.1 us
    ppermute x9, waiting for transfers between devices, over_time(): return lax.ppermute(x, 'tm', [(t, t ^ k) for t in range(n_t)])  11.3 us
    pallas_call x12, Pallas kernels, call(): pl.pallas_call(kernel, out_shape=out_shape, in_specs=[pl.BlockSpec(memory...  8.87 us
    ppermute x6, starting transfers between devices, over_chips(): lax.ppermute(x, 'space', [(s, s ^ 2 * k) for s in range(n_s)])  7.66 us
    ppermute x4, waiting for transfers between devices, over_cores(): return lax.ppermute(x, 'space', [(s, s ^ 1) for s in range(n_s)])  2.18 us
    unnamed x12, local copies, waits for them, and re-layouts  0.94 us
  transfers between devices with their start and end apart: 19, of which 11 were waited for; matrix products, arithmetic and copies ran while one was open for 2% of the time, Pallas kernels for 17%

profile of v21, /device:TPU:0, one launch (start us, length us, event | category | flops | bytes accessed | tf_op | source)
XLA Modules:
  0.0 46.1 jit_solution(15122429237193293105)
XLA Ops:
  1.2 2.6 %collective-permute-start.5 = (bf16[128,640]{1,0:T(8,128)(2,1)}, bf16[128,640]{1,0:T(8,128)(2,1)S(1)}, u32[]{:S(2)}, u32[]{:S(2)}) collective-permute-start(bf16[128,640]{1,0:T(8,128)(2,1)} %grad_in), channel_id=1, source_target_pairs={{0,2},{1,3},{2,0},{3,1},{4,6},{5,7},{6,4},{7,5},{8,10},{9,11},{10,... | collective-permute-start | bytes 491528 | tf_op jit(solution)/shard_map/ppermute | solution.py:398
  3.7 1.5 %collective-permute-start.6 = (bf16[128,640]{1,0:T(8,128)(2,1)}, bf16[128,640]{1,0:T(8,128)(2,1)S(1)}, u32[]{:S(2)}, u32[]{:S(2)}) collective-permute-start(bf16[128,640]{1,0:T(8,128)(2,1)} %grad_in), channel_id=1, source_target_pairs={{0,4},{1,5},{2,6},{3,7},{4,0},{5,1},{6,2},{7,3},{8,12},{9,13},{10,... | collective-permute-start | bytes 491528 | tf_op jit(solution)/shard_map/ppermute | solution.py:398
  5.3 0.8 %pad_maximum_fusion.packed.refs_0_ = bf16[2,128,128]{2,1,0:T(8,128)(2,1)S(1)} fusion(bf16[1,128,128]{2,1,0:T(8,128)(2,1)} %bitcast.3, bf16[1,128,128]{2,1,0:T(8,128)(2,1)} %bitcast.2), kind=kLoop, calls=%fused_computation | loop fusion | flops 32768 | bytes 131072 | tf_op jit(solution)/shard_map/stack | solution.py:419
  6.7 4.1 %collective-permute-start.2 = (bf16[2,128,128]{2,1,0:T(8,128)(2,1)S(1)}, bf16[2,128,128]{2,1,0:T(8,128)(2,1)S(1)}, u32[]{:S(2)}, u32[]{:S(2)}) collective-permute-start(bf16[2,128,128]{2,1,0:T(8,128)(2,1)S(1)} %pad_maximum_fusion.packed.refs_0_), channel_id=1, source_target_pairs={{0,24},{8,16},{16,8},{24,0},{1,25},{9,17},{17,9},{25,1},{2,26},{10... | collective-permute-start | bytes 196616 | tf_op jit(solution)/shard_map/ppermute | solution.py:405
  10.8 0.9 %copy-done.3 = bf16[128,640]{1,0:T(8,128)(2,1)S(1)} copy-done((bf16[128,640]{1,0:T(8,128)(2,1)S(1)}, bf16[128,640]{1,0:T(8,128)(2,1)}, u32[]{:S(2)}) %copy-start.3) | copy-done | bytes 163864
  11.7 1.4 %shard_map.129 = (bf16[4,128,640]{2,1,0:T(8,128)(2,1)S(1)}, bf16[128,640]{1,0:T(8,128)(2,1)S(1)}) custom-call(bf16[128,5120]{1,0:T(8,128)(2,1)} %weight_in, bf16[128,640]{1,0:T(8,128)(2,1)S(1)} %copy-done.3), custom_call_target="tpu_custom_call" | custom-call | bytes 1474560 | tf_op jit(solution)/shard_map/pallas_call | solution.py:353
  13.1 0.7 %shard_map.128 = (f32[2,512]{1,0:T(2,128)S(1)}, f32[4,2,640]{2,1,0:T(2,128)S(1)}, f32[4,1,640]{2,1,0:T(1,128)S(1)}, f32[8,16,128]{2,1,0:T(8,128)S(1)}) custom-call(s32[8]{0:T(128)S(1)} %copy-done.4, s32[4]{0:T(128)S(1)} %copy-done.5, f32[16,5120]{1,0:T(8,128)S(1)} %copy-done.1), custom_call_target="tpu_custom_call" | custom-call | bytes 327728 | tf_op jit(solution)/shard_map/pallas_call | solution.py:353
  14.4 0.8 %shard_map.130 = (f32[128,128]{1,0:T(8,128)S(1)}, f32[128,128]{1,0:T(8,128)S(1)}, f32[40,128]{1,0:T(8,128)S(1)}) custom-call(bf16[2,128,128]{2,1,0:T(8,128)(2,1)S(1)} %pad_maximum_fusion.packed.refs_0_, bf16[128,128]{1,0:T(8,128)(2,1)S(1)} %collective-permute-done.1.other_saved, bf16[4,128,640]{2,1,0:T(8,128)(2,1)S(1)} %get-tuple-element.46.kept, ...), custom_call_target="tpu_custom_call" | custom-call | flops 335544320 | bytes 2740224 | tf_op jit(solution)/shard_map/pallas_call | solution.py:353
  15.3 1.4 %collective-permute-done.3.refs_2_ = bf16[2,128,128]{2,1,0:T(8,128)(2,1)S(1)} collective-permute-done((bf16[2,128,128]{2,1,0:T(8,128)(2,1)S(1)}, bf16[2,128,128]{2,1,0:T(8,128)(2,1)S(1)}, u32[]{:S(2)}, u32[]{:S(2)}) %collective-permute-start.3) | collective-permute-done | bytes 65568 | tf_op jit(solution)/shard_map/ppermute | solution.py:405
  16.7 1.4 %collective-permute-done.4.refs_3_.refs_1_ = bf16[2,128,128]{2,1,0:T(8,128)(2,1)S(1)} collective-permute-done((bf16[2,128,128]{2,1,0:T(8,128)(2,1)S(1)}, bf16[2,128,128]{2,1,0:T(8,128)(2,1)S(1)}, u32[]{:S(2)}, u32[]{:S(2)}) %collective-permute-start.4) | collective-permute-done | bytes 65568 | tf_op jit(solution)/shard_map/ppermute | solution.py:405
  18.1 0.8 %shard_map.131.stats = f32[8,128]{1,0:T(8,128)S(1)} custom-call(f32[2,512]{1,0:T(2,128)S(1)} %get-tuple-element.58.bias, bf16[1024,128]{1,0:T(8,128)(2,1)S(1)} %copy-done, bf16[2,128,128]{2,1,0:T(8,128)(2,1)S(1)} %pad_maximum_fusion.packed.refs_0_, bf16[2,128,128]{2,1,0:T(8,128)(2,1)S(1)} %collective-permute-done.2.refs_1_.refs_3_, ...), custom_call_target="tpu_custom_call" | custom-call | flops 134217728 | bytes 528384 | tf_op jit(solution)/shard_map/pallas_call | solution.py:353
  19.0 2.5 %collective-permute-start.10 = (bf16[352,128]{1,0:T(8,128)(2,1)S(1)}, bf16[352,128]{1,0:T(8,128)(2,1)S(1)}, u32[]{:S(2)}, u32[]{:S(2)}) collective-permute-start(bf16[352,128]{1,0:T(8,128)(2,1)S(1)} %get-tuple-element.55), channel_id=1, source_target_pairs={{0,24},{8,16},{16,8},{24,0},{1,25},{9,17},{17,9},{25,1},{2,26},{10... | collective-permute-start | bytes 270344 | tf_op jit(solution)/shard_map/ppermute | solution.py:405
  22.1 1.4 %collective-permute-start.9 = (bf16[352,128]{1,0:T(8,128)(2,1)S(1)}, bf16[352,128]{1,0:T(8,128)(2,1)S(1)}, u32[]{:S(2)}, u32[]{:S(2)}) collective-permute-start(bf16[352,128]{1,0:T(8,128)(2,1)S(1)} %get-tuple-element.54), channel_id=1, source_target_pairs={{0,8},{8,0},{16,24},{24,16},{1,9},{9,1},{17,25},{25,17},{2,10},{10... | collective-permute-start | bytes 270344 | tf_op jit(solution)/shard_map/ppermute | solution.py:405
  23.5 2.5 %collective-permute-done.10.refs_2_.refs_6_ = bf16[352,128]{1,0:T(8,128)(2,1)S(1)} collective-permute-done((bf16[352,128]{1,0:T(8,128)(2,1)S(1)}, bf16[352,128]{1,0:T(8,128)(2,1)S(1)}, u32[]{:S(2)}, u32[]{:S(2)}) %collective-permute-start.10) | collective-permute-done | bytes 90144 | tf_op jit(solution)/shard_map/ppermute | solution.py:405
  26.0 3.3 %collective-permute-done.11.refs_3_.refs_7_ = bf16[352,128]{1,0:T(8,128)(2,1)S(1)} collective-permute-done((bf16[352,128]{1,0:T(8,128)(2,1)S(1)}, bf16[352,128]{1,0:T(8,128)(2,1)S(1)}, u32[]{:S(2)}, u32[]{:S(2)}) %collective-permute-start.11) | collective-permute-done | bytes 90144 | tf_op jit(solution)/shard_map/ppermute | solution.py:405
  29.4 2.5 %collective-permute-start.12 = (bf16[800,128]{1,0:T(8,128)(2,1)S(1)}, bf16[800,128]{1,0:T(8,128)(2,1)S(1)}, u32[]{:S(2)}, u32[]{:S(2)}) collective-permute-start(bf16[800,128]{1,0:T(8,128)(2,1)S(1)} %shard_map.133.refs_0_), channel_id=1, source_target_pairs={{0,6},{1,7},{2,4},{3,5},{4,2},{5,3},{6,0},{7,1},{8,14},{9,15},{10,... | collective-permute-start | bytes 614408 | tf_op jit(solution)/shard_map/ppermute | solution.py:398
  33.0 1.0 %shard_map.134 = (f32[1024,128]{1,0:T(8,128)S(1)}, f32[1024,128]{1,0:T(8,128)S(1)}, bf16[128,128]{1,0:T(8,128)(2,1)S(1)}, bf16[128,128]{1,0:T(8,128)(2,1)S(1)}) custom-call(f32[2,512]{1,0:T(2,128)S(1)} %get-tuple-element.58.bias, bf16[1024,128]{1,0:T(8,128)(2,1)S(1)} %copy-done, bf16[1024,128]{1,0:T(8,128)(2,1)S(1)} %copy-done.2, ...), custom_call_target="tpu_custom_call" | custom-call | flops 335544320 | bytes 1150976 | tf_op jit(solution)/shard_map/pallas_call | solution.py:353
  33.9 0.8 %collective-permute-start.15 = (bf16[128,128]{1,0:T(8,128)(2,1)S(1)}, bf16[128,128]{1,0:T(8,128)(2,1)S(1)}, u32[]{:S(2)}, u32[]{:S(2)}) collective-permute-start(bf16[128,128]{1,0:T(8,128)(2,1)S(1)} %get-tuple-element.64), channel_id=1, source_target_pairs={{0,16},{8,24},{16,0},{24,8},{1,17},{9,25},{17,1},{25,9},{2,18},{10... | collective-permute-start | bytes 98312 | tf_op jit(solution)/shard_map/ppermute | solution.py:405
  34.8 1.9 %collective-permute-start.16 = (bf16[128,128]{1,0:T(8,128)(2,1)S(1)}, bf16[128,128]{1,0:T(8,128)(2,1)S(1)}, u32[]{:S(2)}, u32[]{:S(2)}) collective-permute-start(bf16[128,128]{1,0:T(8,128)(2,1)S(1)} %get-tuple-element.65), channel_id=1, source_target_pairs={{0,24},{8,16},{16,8},{24,0},{1,25},{9,17},{17,9},{25,1},{2,26},{10... | collective-permute-start | bytes 98312 | tf_op jit(solution)/shard_map/ppermute | solution.py:405
  36.7 1.7 %shard_map.135 = (bf16[1024,128]{1,0:T(8,128)(2,1)}, bf16[1024,128]{1,0:T(8,128)(2,1)}, bf16[128,128]{1,0:T(8,128)(2,1)S(1)}, bf16[128,128]{1,0:T(8,128)(2,1)S(1)}) custom-call(f32[2,512]{1,0:T(2,128)S(1)} %get-tuple-element.58.bias, bf16[1024,128]{1,0:T(8,128)(2,1)S(1)} %copy-done, bf16[1024,128]{1,0:T(8,128)(2,1)S(1)} %copy-done.2, ...), custom_call_target="tpu_custom_call" | custom-call | flops 335544320 | bytes 2199552 | tf_op jit(solution)/shard_map/pallas_call | solution.py:353
  38.9 1.6 %collective-permute-done.16.refs_3_ = bf16[128,128]{1,0:T(8,128)(2,1)S(1)} collective-permute-done((bf16[128,128]{1,0:T(8,128)(2,1)S(1)}, bf16[128,128]{1,0:T(8,128)(2,1)S(1)}, u32[]{:S(2)}, u32[]{:S(2)}) %collective-permute-start.16) | collective-permute-done | bytes 32800 | tf_op jit(solution)/shard_map/ppermute | solution.py:405
  42.0 1.5 %collective-permute-done.17.other = bf16[2880,128]{1,0:T(8,128)(2,1)S(1)} collective-permute-done((bf16[2880,128]{1,0:T(8,128)(2,1)S(1)}, bf16[2880,128]{1,0:T(8,128)(2,1)S(1)}, u32[]{:S(2)}, u32[]{:S(2)}) %collective-permute-start.17) | collective-permute-done | bytes 737312 | tf_op jit(solution)/shard_map/ppermute | solution.py:402
  43.6 1.3 %shard_map.138 = (f32[128,1280]{1,0:T(8,128)}, f32[16,5120]{1,0:T(8,128)}) custom-call(f32[8,16,128]{2,1,0:T(8,128)S(1)} %get-tuple-element.62.hot, bf16[2880,128]{1,0:T(8,128)(2,1)S(1)} %collective-permute-done.17.other, f32[128,640]{1,0:T(8,128)S(1)} %get-tuple-element.70.own_weight, f32[16,2560]{1,0:T(8,128)S(1)} %get-tuple-element.71.own_gate, ...), custom_call_target="tpu_custom_call" | custom-call | flops 83886080 | bytes 1556480 | tf_op jit(solution)/shard_map/pallas_call | solution.py:353
  45.4 0.7 %shard_map.139 = bf16[128,128]{1,0:T(8,128)(2,1)} custom-call(bf16[128,128]{1,0:T(8,128)(2,1)S(1)} %get-tuple-element.73.refs_0_, bf16[128,128]{1,0:T(8,128)(2,1)S(1)} %collective-permute-done.18.refs_1_, bf16[128,128]{1,0:T(8,128)(2,1)S(1)} %collective-permute-done.15.refs_2_, bf16[128,128]{1,0:T(8,128)(2,1)S(1)} %collective-permute-done.16.refs_3_), custom_call_target="tpu_custom_call" | custom-call | bytes 131072 | tf_op jit(solution)/shard_map/pallas_call | solution.py:353
  (39 shorter events, 6.2 us)
Async XLA Ops:
  0.6 12.4 %copy-start.1 = (f32[16,5120]{1,0:T(8,128)S(1)}, f32[16,5120]{1,0:T(8,128)}, u32[]{:S(2)}) copy-start(f32[16,5120]{1,0:T(8,128)} %gate) | copy-start | bytes 983044
  0.6 6.1 %collective-permute-start = (bf16[128,5120]{1,0:T(8,128)(2,1)}, bf16[128,5120]{1,0:T(8,128)(2,1)S(1)}, u32[]{:S(2)}, u32[]{:S(2)}) collective-permute-start(bf16[128,5120]{1,0:T(8,128)(2,1)} %weight_in), channel_id=1, source_target_pairs={{0,1},{1,0},{2,3},{3,2},{4,5},{5,4},{6,7},{7,6},{8,9},{9,8},{10,11... | collective-permute-start | bytes 3932168 | tf_op jit(solution)/shard_map/ppermute | solution.py:402
  1.2 12.6 %collective-permute-start.5 = (bf16[128,640]{1,0:T(8,128)(2,1)}, bf16[128,640]{1,0:T(8,128)(2,1)S(1)}, u32[]{:S(2)}, u32[]{:S(2)}) collective-permute-start(bf16[128,640]{1,0:T(8,128)(2,1)} %grad_in), channel_id=1, source_target_pairs={{0,2},{1,3},{2,0},{3,1},{4,6},{5,7},{6,4},{7,5},{8,10},{9,11},{10,... | collective-permute-start | bytes 491528 | tf_op jit(solution)/shard_map/ppermute | solution.py:398
  3.7 10.7 %collective-permute-start.6 = (bf16[128,640]{1,0:T(8,128)(2,1)}, bf16[128,640]{1,0:T(8,128)(2,1)S(1)}, u32[]{:S(2)}, u32[]{:S(2)}) collective-permute-start(bf16[128,640]{1,0:T(8,128)(2,1)} %grad_in), channel_id=1, source_target_pairs={{0,4},{1,5},{2,6},{3,7},{4,0},{5,1},{6,2},{7,3},{8,12},{9,13},{10,... | collective-permute-start | bytes 491528 | tf_op jit(solution)/shard_map/ppermute | solution.py:398
  5.2 9.2 %collective-permute-start.7 = (bf16[128,640]{1,0:T(8,128)(2,1)}, bf16[128,640]{1,0:T(8,128)(2,1)S(1)}, u32[]{:S(2)}, u32[]{:S(2)}) collective-permute-start(bf16[128,640]{1,0:T(8,128)(2,1)} %grad_in), channel_id=1, source_target_pairs={{0,6},{1,7},{2,4},{3,5},{4,2},{5,3},{6,0},{7,1},{8,14},{9,15},{10,... | collective-permute-start | bytes 491528 | tf_op jit(solution)/shard_map/ppermute | solution.py:398
  5.3 1.4 %collective-permute-start.1 = (bf16[128,128]{1,0:T(8,128)(2,1)}, bf16[128,128]{1,0:T(8,128)(2,1)S(1)}, u32[]{:S(2)}, u32[]{:S(2)}) collective-permute-start(bf16[128,128]{1,0:T(8,128)(2,1)} %param.12), channel_id=1, source_target_pairs={{0,1},{1,0},{2,3},{3,2},{4,5},{5,4},{6,7},{7,6},{8,9},{9,8},{10,11... | collective-permute-start | bytes 98312 | tf_op jit(solution)/shard_map/ppermute | solution.py:402
  6.7 8.6 %collective-permute-start.2 = (bf16[2,128,128]{2,1,0:T(8,128)(2,1)S(1)}, bf16[2,128,128]{2,1,0:T(8,128)(2,1)S(1)}, u32[]{:S(2)}, u32[]{:S(2)}) collective-permute-start(bf16[2,128,128]{2,1,0:T(8,128)(2,1)S(1)} %pad_maximum_fusion.packed.refs_0_), channel_id=1, source_target_pairs={{0,24},{8,16},{16,8},{24,0},{1,25},{9,17},{17,9},{25,1},{2,26},{10... | collective-permute-start | bytes 196616 | tf_op jit(solution)/shard_map/ppermute | solution.py:405
  10.7 5.9 %collective-permute-start.3 = (bf16[2,128,128]{2,1,0:T(8,128)(2,1)S(1)}, bf16[2,128,128]{2,1,0:T(8,128)(2,1)S(1)}, u32[]{:S(2)}, u32[]{:S(2)}) collective-permute-start(bf16[2,128,128]{2,1,0:T(8,128)(2,1)S(1)} %pad_maximum_fusion.packed.refs_0_), channel_id=1, source_target_pairs={{0,16},{8,24},{16,0},{24,8},{1,17},{9,25},{17,1},{25,9},{2,18},{10... | collective-permute-start | bytes 196616 | tf_op jit(solution)/shard_map/ppermute | solution.py:405
  11.7 1.4 %copy-start.4 = (s32[8]{0:T(128)S(1)}, s32[8]{0:T(128)}, u32[]{:S(2)}) copy-start(s32[8]{0:T(128)} %levels.1) | copy-start | bytes 100
  11.7 1.4 %copy-start.5 = (s32[4]{0:T(128)S(1)}, s32[4]{0:T(128)}, u32[]{:S(2)}) copy-start(s32[4]{0:T(128)} %clips.1) | copy-start | bytes 52
  13.8 4.3 %collective-permute-start.4 = (bf16[2,128,128]{2,1,0:T(8,128)(2,1)S(1)}, bf16[2,128,128]{2,1,0:T(8,128)(2,1)S(1)}, u32[]{:S(2)}, u32[]{:S(2)}) collective-permute-start(bf16[2,128,128]{2,1,0:T(8,128)(2,1)S(1)} %pad_maximum_fusion.packed.refs_0_), channel_id=1, source_target_pairs={{0,8},{8,0},{16,24},{24,16},{1,9},{9,1},{17,25},{25,17},{2,10},{10... | collective-permute-start | bytes 196616 | tf_op jit(solution)/shard_map/ppermute | solution.py:405
  14.4 3.7 %copy-start = (bf16[1024,128]{1,0:T(8,128)(2,1)S(1)}, bf16[1024,128]{1,0:T(8,128)(2,1)}, u32[]{:S(2)}) copy-start(bf16[1024,128]{1,0:T(8,128)(2,1)} %keys.5) | copy-start | bytes 786436
  15.2 17.8 %copy-start.2 = (bf16[1024,128]{1,0:T(8,128)(2,1)S(1)}, bf16[1024,128]{1,0:T(8,128)(2,1)}, u32[]{:S(2)}) copy-start(bf16[1024,128]{1,0:T(8,128)(2,1)} %values.3) | copy-start | bytes 786436
  15.2 3.7 %collective-permute-start.8 = (f32[128,128]{1,0:T(8,128)S(1)}, f32[128,128]{1,0:T(8,128)S(1)}, u32[]{:S(2)}, u32[]{:S(2)}) collective-permute-start(f32[128,128]{1,0:T(8,128)S(1)} %get-tuple-element.50), channel_id=1, source_target_pairs={{0,1},{1,0},{2,3},{3,2},{4,5},{5,4},{6,7},{7,6},{8,9},{9,8},{10,11... | collective-permute-start | bytes 196616 | tf_op jit(solution)/shard_map/ppermute | solution.py:402
  19.0 7.0 %collective-permute-start.10 = (bf16[352,128]{1,0:T(8,128)(2,1)S(1)}, bf16[352,128]{1,0:T(8,128)(2,1)S(1)}, u32[]{:S(2)}, u32[]{:S(2)}) collective-permute-start(bf16[352,128]{1,0:T(8,128)(2,1)S(1)} %get-tuple-element.55), channel_id=1, source_target_pairs={{0,24},{8,16},{16,8},{24,0},{1,25},{9,17},{17,9},{25,1},{2,26},{10... | collective-permute-start | bytes 270344 | tf_op jit(solution)/shard_map/ppermute | solution.py:405
  21.5 7.8 %collective-permute-start.11 = (bf16[352,128]{1,0:T(8,128)(2,1)S(1)}, bf16[352,128]{1,0:T(8,128)(2,1)S(1)}, u32[]{:S(2)}, u32[]{:S(2)}) collective-permute-start(bf16[352,128]{1,0:T(8,128)(2,1)S(1)} %get-tuple-element.56), channel_id=1, source_target_pairs={{0,16},{8,24},{16,0},{24,8},{1,17},{9,25},{17,1},{25,9},{2,18},{10... | collective-permute-start | bytes 270344 | tf_op jit(solution)/shard_map/ppermute | solution.py:405
  22.1 7.3 %collective-permute-start.9 = (bf16[352,128]{1,0:T(8,128)(2,1)S(1)}, bf16[352,128]{1,0:T(8,128)(2,1)S(1)}, u32[]{:S(2)}, u32[]{:S(2)}) collective-permute-start(bf16[352,128]{1,0:T(8,128)(2,1)S(1)} %get-tuple-element.54), channel_id=1, source_target_pairs={{0,8},{8,0},{16,24},{24,16},{1,9},{9,1},{17,25},{25,17},{2,10},{10... | collective-permute-start | bytes 270344 | tf_op jit(solution)/shard_map/ppermute | solution.py:405
  29.4 11.1 %collective-permute-start.12 = (bf16[800,128]{1,0:T(8,128)(2,1)S(1)}, bf16[800,128]{1,0:T(8,128)(2,1)S(1)}, u32[]{:S(2)}, u32[]{:S(2)}) collective-permute-start(bf16[800,128]{1,0:T(8,128)(2,1)S(1)} %shard_map.133.refs_0_), channel_id=1, source_target_pairs={{0,6},{1,7},{2,4},{3,5},{4,2},{5,3},{6,0},{7,1},{8,14},{9,15},{10,... | collective-permute-start | bytes 614408 | tf_op jit(solution)/shard_map/ppermute | solution.py:398
  31.9 9.2 %collective-permute-start.13 = (bf16[800,128]{1,0:T(8,128)(2,1)S(1)}, bf16[800,128]{1,0:T(8,128)(2,1)S(1)}, u32[]{:S(2)}, u32[]{:S(2)}) collective-permute-start(bf16[800,128]{1,0:T(8,128)(2,1)S(1)} %shard_map.133.refs_0_), channel_id=1, source_target_pairs={{0,4},{1,5},{2,6},{3,7},{4,0},{5,1},{6,2},{7,3},{8,12},{9,13},{10,... | collective-permute-start | bytes 614408 | tf_op jit(solution)/shard_map/ppermute | solution.py:398
  32.4 8.8 %collective-permute-start.14 = (bf16[800,128]{1,0:T(8,128)(2,1)S(1)}, bf16[800,128]{1,0:T(8,128)(2,1)S(1)}, u32[]{:S(2)}, u32[]{:S(2)}) collective-permute-start(bf16[800,128]{1,0:T(8,128)(2,1)S(1)} %shard_map.133.refs_0_), channel_id=1, source_target_pairs={{0,2},{1,3},{2,0},{3,1},{4,6},{5,7},{6,4},{7,5},{8,10},{9,11},{10,... | collective-permute-start | bytes 614408 | tf_op jit(solution)/shard_map/ppermute | solution.py:398
  33.9 4.9 %collective-permute-start.15 = (bf16[128,128]{1,0:T(8,128)(2,1)S(1)}, bf16[128,128]{1,0:T(8,128)(2,1)S(1)}, u32[]{:S(2)}, u32[]{:S(2)}) collective-permute-start(bf16[128,128]{1,0:T(8,128)(2,1)S(1)} %get-tuple-element.64), channel_id=1, source_target_pairs={{0,16},{8,24},{16,0},{24,8},{1,17},{9,25},{17,1},{25,9},{2,18},{10... | collective-permute-start | bytes 98312 | tf_op jit(solution)/shard_map/ppermute | solution.py:405
  34.8 5.7 %collective-permute-start.16 = (bf16[128,128]{1,0:T(8,128)(2,1)S(1)}, bf16[128,128]{1,0:T(8,128)(2,1)S(1)}, u32[]{:S(2)}, u32[]{:S(2)}) collective-permute-start(bf16[128,128]{1,0:T(8,128)(2,1)S(1)} %get-tuple-element.65), channel_id=1, source_target_pairs={{0,24},{8,16},{16,8},{24,0},{1,25},{9,17},{17,9},{25,1},{2,26},{10... | collective-permute-start | bytes 98312 | tf_op jit(solution)/shard_map/ppermute | solution.py:405
  41.3 2.3 %collective-permute-start.17 = (bf16[2880,128]{1,0:T(8,128)(2,1)S(1)}, bf16[2880,128]{1,0:T(8,128)(2,1)S(1)}, u32[]{:S(2)}, u32[]{:S(2)}) collective-permute-start(bf16[2880,128]{1,0:T(8,128)(2,1)S(1)} %shard_map.136.own), channel_id=1, source_target_pairs={{0,1},{1,0},{2,3},{3,2},{4,5},{5,4},{6,7},{7,6},{8,9},{9,8},{10,11... | collective-permute-start | bytes 2211848 | tf_op jit(solution)/shard_map/ppermute | solution.py:402
  41.4 4.0 %collective-permute-start.18 = (bf16[128,128]{1,0:T(8,128)(2,1)S(1)}, bf16[128,128]{1,0:T(8,128)(2,1)S(1)}, u32[]{:S(2)}, u32[]{:S(2)}) collective-permute-start(bf16[128,128]{1,0:T(8,128)(2,1)S(1)} %get-tuple-element.74), channel_id=1, source_target_pairs={{0,8},{8,0},{16,24},{24,16},{1,9},{9,1},{17,25},{25,17},{2,10},{10... | collective-permute-start | bytes 98312 | tf_op jit(solution)/shard_map/ppermute | solution.py:405
  (1 other events, 0.9 us)

commit v22 on v21

--- a/solution.py
+++ b/solution.py
@@ -92,20 +92,21 @@
         gate_b[k] = gate[pl.ds(level, 1), mine]
 
 
-def stats_kernel(n_t, bias, keys, *refs):
-    packed, out = far_first(refs[:n_t]), refs[n_t]
+def stats_kernel(first, last, bias, keys, *refs):
+    packed, out = refs[:-1], refs[-1]
     rows = packed[0].shape[1]
-    for p in range(0, n_t, 2):
+    count = last - first
+    for p in range(0, count, 2):
         q = jnp.concatenate([packed[p][0], packed[p + 1][0]], axis=0)
         scores = []
         for kf in range(bias.shape[0]):
-            mask = bias[kf : kf + 1, p * rows : (p + 2) * rows]
+            mask = bias[kf : kf + 1, (first + p) * rows : (first + p + 2) * rows]
             scores.append(dot(keys[kf * SPF : (kf + 1) * SPF, :], q, 1, 1) * SCALE + mask)
         top = functools.reduce(jnp.maximum, [jnp.max(x, axis=0, keepdims=True) for x in scores])
         total = sum(jnp.sum(jnp.exp(x - top), axis=0, keepdims=True) for x in scores)
         for i in range(2):
             out[p + i : p + i + 1, :] = top[:, i * rows : (i + 1) * rows]
-            out[n_t + p + i : n_t + p + i + 1, :] = total[:, i * rows : (i + 1) * rows]
+            out[count + p + i : count + p + i + 1, :] = total[:, i * rows : (i + 1) * rows]
 
 
 def head_kernel(chips, frames, packed, other_saved, kept, received, gate_a, *refs):
@@ -151,7 +152,7 @@
     return jnp.concatenate([x, jnp.zeros((rows - x.shape[0], x.shape[1]), x.dtype)], axis=0)
 
 
-def join_kernel(n_t, chips, starts, mine, received, stats, terms, *refs):
+def join_kernel(n_t, chips, starts, mine, received, near_stats, far_stats, terms, *refs):
     pieces, outs, (wide, held) = refs[:chips], refs[chips : chips + n_t][::-1], refs[chips + n_t :]
     t, chip, _ = place()
     part, tiles = held.shape[1], held.shape[2] // LANES
@@ -159,7 +160,9 @@
         wide[...] = pieces[k][...].astype(jnp.float32)
         held[k] = wide[pl.ds(pl.multiple_of(chip * part, part), part), :]
     head = (mine[...] + received[...]).astype(jnp.bfloat16)
-    rest = stats[...]
+    near, far = near_stats[...], far_stats[...]
+    each = far.shape[0] // 2
+    rest = jnp.concatenate([near[:2], far[:each], near[2:], far[each:]], axis=0)
     split = []
     for _ in range(SPLIT):
         piece = rest.astype(jnp.bfloat16).astype(jnp.float32)
@@ -446,15 +449,22 @@
         flops=4 * rows * chips * width * 2 * HD,
     )
     later_bias, _ = lax.optimization_barrier((bias, mine))
-    stats = call(
-        functools.partial(stats_kernel, n_t),
-        [later_bias, keys] + far_first(packed_all),
-        shape(f32, 2 * n_t, LANES),
-        flops=2 * n_t * rows * k_rows * HD,
+    far_stats = call(
+        functools.partial(stats_kernel, 2, n_t),
+        [later_bias, keys] + packed_all[2:],
+        shape(f32, 2 * (n_t - 2), LANES),
+        flops=2 * (n_t - 2) * rows * k_rows * HD,
+    )
+    last_bias, _ = lax.optimization_barrier((bias, far_stats))
+    near_stats = call(
+        functools.partial(stats_kernel, 0, 2),
+        [last_bias, keys] + packed_all[:2],
+        shape(f32, 4, LANES),
+        flops=4 * rows * k_rows * HD,
     )
     heads = call(
         functools.partial(join_kernel, n_t, chips, starts),
-        [mine, over_cores(other), stats, terms] + pieces,
+        [mine, over_cores(other), near_stats, far_stats, terms] + pieces,
         [shape(bf16, starts[-1], LANES)] * n_t,
         [pltpu.VMEM((rows, width), f32), pltpu.VMEM((chips, part, width), f32)],
     )

time: 46.3 us -> 46 us (level)
  waiting for transfers between devices: 14.2 us -> 13.7 us
    ppermute x9, waiting for transfers between devices: 11.3 us -> 10.8 us  [over_time(): return lax.ppermute(x, 'tm', [(t, t ^ k) for t in range(n_t)])]
    pallas_call x12 -> x13, Pallas kernels: 8.87 us -> 9.08 us  [call(): pl.pallas_call(kernel, out_shape=out_shape, in_specs=[pl.BlockSpec(memory...]
  transfers between devices with their start and end apart: 19 -> 19, of which waited for: 11 -> 11; matrix products, arithmetic and copies ran while one was open for 2% -> 2% of each run, Pallas kernels for 17% -> 18%
where the time goes in v22:
time: 46 us; the launch traced here: 45.8 us
  starting transfers between devices  20.5 us (45%)
  waiting for transfers between devices  13.7 us (30%)
  Pallas kernels  9.08 us (20%)
  local copies, waits for them, and re-layouts  0.94 us (2%)
  between operations  0.79 us (2%)
  other arithmetic  0.78 us (2%)
    ppermute x9, starting transfers between devices, over_time(): return lax.ppermute(x, 'tm', [(t, t ^ k) for t in range(n_t)])  12.2 us
    ppermute x9, waiting for transfers between devices, over_time(): return lax.ppermute(x, 'tm', [(t, t ^ k) for t in range(n_t)])  10.8 us
    pallas_call x13, Pallas kernels, call(): pl.pallas_call(kernel, out_shape=out_shape, in_specs=[pl.BlockSpec(memory...  9.08 us
    ppermute x6, starting transfers between devices, over_chips(): lax.ppermute(x, 'space', [(s, s ^ 2 * k) for s in range(n_s)])  7.66 us
    ppermute x4, waiting for transfers between devices, over_cores(): return lax.ppermute(x, 'space', [(s, s ^ 1) for s in range(n_s)])  2.17 us
    unnamed x12, local copies, waits for them, and re-layouts  0.94 us
  transfers between devices with their start and end apart: 19, of which 11 were waited for; matrix products, arithmetic and copies ran while one was open for 2% of the time, Pallas kernels for 18%

profile of v22, /device:TPU:0, one launch (start us, length us, event | category | flops | bytes accessed | tf_op | source)
XLA Modules:
  0.0 45.8 jit_solution(6758638082327140)
XLA Ops:
  1.2 2.6 %collective-permute-start.5 = (bf16[128,640]{1,0:T(8,128)(2,1)}, bf16[128,640]{1,0:T(8,128)(2,1)S(1)}, u32[]{:S(2)}, u32[]{:S(2)}) collective-permute-start(bf16[128,640]{1,0:T(8,128)(2,1)} %grad_in), channel_id=1, source_target_pairs={{0,2},{1,3},{2,0},{3,1},{4,6},{5,7},{6,4},{7,5},{8,10},{9,11},{10,... | collective-permute-start | bytes 491528 | tf_op jit(solution)/shard_map/ppermute | solution.py:401
  3.7 1.5 %collective-permute-start.6 = (bf16[128,640]{1,0:T(8,128)(2,1)}, bf16[128,640]{1,0:T(8,128)(2,1)S(1)}, u32[]{:S(2)}, u32[]{:S(2)}) collective-permute-start(bf16[128,640]{1,0:T(8,128)(2,1)} %grad_in), channel_id=1, source_target_pairs={{0,4},{1,5},{2,6},{3,7},{4,0},{5,1},{6,2},{7,3},{8,12},{9,13},{10,... | collective-permute-start | bytes 491528 | tf_op jit(solution)/shard_map/ppermute | solution.py:401
  5.3 0.8 %pad_maximum_fusion.packed.refs_0_ = bf16[2,128,128]{2,1,0:T(8,128)(2,1)S(1)} fusion(bf16[1,128,128]{2,1,0:T(8,128)(2,1)} %bitcast.3, bf16[1,128,128]{2,1,0:T(8,128)(2,1)} %bitcast.2), kind=kLoop, calls=%fused_computation | loop fusion | flops 32768 | bytes 131072 | tf_op jit(solution)/shard_map/stack | solution.py:422
  6.1 0.6 %collective-permute-done.1.other_saved = bf16[128,128]{1,0:T(8,128)(2,1)S(1)} collective-permute-done((bf16[128,128]{1,0:T(8,128)(2,1)}, bf16[128,128]{1,0:T(8,128)(2,1)S(1)}, u32[]{:S(2)}, u32[]{:S(2)}) %collective-permute-start.1) | collective-permute-done | bytes 32800 | tf_op jit(solution)/shard_map/ppermute | solution.py:405
  6.7 4.1 %collective-permute-start.2 = (bf16[2,128,128]{2,1,0:T(8,128)(2,1)S(1)}, bf16[2,128,128]{2,1,0:T(8,128)(2,1)S(1)}, u32[]{:S(2)}, u32[]{:S(2)}) collective-permute-start(bf16[2,128,128]{2,1,0:T(8,128)(2,1)S(1)} %pad_maximum_fusion.packed.refs_0_), channel_id=1, source_target_pairs={{0,24},{8,16},{16,8},{24,0},{1,25},{9,17},{17,9},{25,1},{2,26},{10... | collective-permute-start | bytes 196616 | tf_op jit(solution)/shard_map/ppermute | solution.py:408
  10.8 0.9 %copy-done.3 = bf16[128,640]{1,0:T(8,128)(2,1)S(1)} copy-done((bf16[128,640]{1,0:T(8,128)(2,1)S(1)}, bf16[128,640]{1,0:T(8,128)(2,1)}, u32[]{:S(2)}) %copy-start.3) | copy-done | bytes 163864
  11.7 1.4 %shard_map.129 = (bf16[4,128,640]{2,1,0:T(8,128)(2,1)S(1)}, bf16[128,640]{1,0:T(8,128)(2,1)S(1)}) custom-call(bf16[128,5120]{1,0:T(8,128)(2,1)} %weight_in, bf16[128,640]{1,0:T(8,128)(2,1)S(1)} %copy-done.3), custom_call_target="tpu_custom_call" | custom-call | bytes 1474560 | tf_op jit(solution)/shard_map/pallas_call | solution.py:356
  13.1 0.7 %shard_map.128 = (f32[2,512]{1,0:T(2,128)S(1)}, f32[4,2,640]{2,1,0:T(2,128)S(1)}, f32[4,1,640]{2,1,0:T(1,128)S(1)}, f32[8,16,128]{2,1,0:T(8,128)S(1)}) custom-call(s32[8]{0:T(128)S(1)} %copy-done.4, s32[4]{0:T(128)S(1)} %copy-done.5, f32[16,5120]{1,0:T(8,128)S(1)} %copy-done.1), custom_call_target="tpu_custom_call" | custom-call | bytes 327728 | tf_op jit(solution)/shard_map/pallas_call | solution.py:356
  14.4 0.8 %shard_map.130 = (f32[128,128]{1,0:T(8,128)S(1)}, f32[128,128]{1,0:T(8,128)S(1)}, f32[40,128]{1,0:T(8,128)S(1)}) custom-call(bf16[2,128,128]{2,1,0:T(8,128)(2,1)S(1)} %pad_maximum_fusion.packed.refs_0_, bf16[128,128]{1,0:T(8,128)(2,1)S(1)} %collective-permute-done.1.other_saved, bf16[4,128,640]{2,1,0:T(8,128)(2,1)S(1)} %get-tuple-element.47.kept, ...), custom_call_target="tpu_custom_call" | custom-call | flops 335544320 | bytes 2740224 | tf_op jit(solution)/shard_map/pallas_call | solution.py:356
  15.3 1.4 %collective-permute-done.3.refs_0_.refs_2_ = bf16[2,128,128]{2,1,0:T(8,128)(2,1)S(1)} collective-permute-done((bf16[2,128,128]{2,1,0:T(8,128)(2,1)S(1)}, bf16[2,128,128]{2,1,0:T(8,128)(2,1)S(1)}, u32[]{:S(2)}, u32[]{:S(2)}) %collective-permute-start.3) | collective-permute-done | bytes 65568 | tf_op jit(solution)/shard_map/ppermute | solution.py:408
  17.2 0.9 %collective-permute-done.4.refs_1_.refs_3_ = bf16[2,128,128]{2,1,0:T(8,128)(2,1)S(1)} collective-permute-done((bf16[2,128,128]{2,1,0:T(8,128)(2,1)S(1)}, bf16[2,128,128]{2,1,0:T(8,128)(2,1)S(1)}, u32[]{:S(2)}, u32[]{:S(2)}) %collective-permute-start.4) | collective-permute-done | bytes 65568 | tf_op jit(solution)/shard_map/ppermute | solution.py:408
  18.7 2.5 %collective-permute-start.10 = (bf16[352,128]{1,0:T(8,128)(2,1)S(1)}, bf16[352,128]{1,0:T(8,128)(2,1)S(1)}, u32[]{:S(2)}, u32[]{:S(2)}) collective-permute-start(bf16[352,128]{1,0:T(8,128)(2,1)S(1)} %get-tuple-element.57), channel_id=1, source_target_pairs={{0,24},{8,16},{16,8},{24,0},{1,25},{9,17},{17,9},{25,1},{2,26},{10... | collective-permute-start | bytes 270344 | tf_op jit(solution)/shard_map/ppermute | solution.py:408
  21.8 1.4 %collective-permute-start.9 = (bf16[352,128]{1,0:T(8,128)(2,1)S(1)}, bf16[352,128]{1,0:T(8,128)(2,1)S(1)}, u32[]{:S(2)}, u32[]{:S(2)}) collective-permute-start(bf16[352,128]{1,0:T(8,128)(2,1)S(1)} %get-tuple-element.56), channel_id=1, source_target_pairs={{0,8},{8,0},{16,24},{24,16},{1,9},{9,1},{17,25},{25,17},{2,10},{10... | collective-permute-start | bytes 270344 | tf_op jit(solution)/shard_map/ppermute | solution.py:408
  23.2 2.3 %collective-permute-done.10.refs_2_.refs_6_ = bf16[352,128]{1,0:T(8,128)(2,1)S(1)} collective-permute-done((bf16[352,128]{1,0:T(8,128)(2,1)S(1)}, bf16[352,128]{1,0:T(8,128)(2,1)S(1)}, u32[]{:S(2)}, u32[]{:S(2)}) %collective-permute-start.10) | collective-permute-done | bytes 90144 | tf_op jit(solution)/shard_map/ppermute | solution.py:408
  25.5 3.5 %collective-permute-done.11.refs_3_.refs_7_ = bf16[352,128]{1,0:T(8,128)(2,1)S(1)} collective-permute-done((bf16[352,128]{1,0:T(8,128)(2,1)S(1)}, bf16[352,128]{1,0:T(8,128)(2,1)S(1)}, u32[]{:S(2)}, u32[]{:S(2)}) %collective-permute-start.11) | collective-permute-done | bytes 90144 | tf_op jit(solution)/shard_map/ppermute | solution.py:408
  29.1 2.5 %collective-permute-start.12 = (bf16[800,128]{1,0:T(8,128)(2,1)S(1)}, bf16[800,128]{1,0:T(8,128)(2,1)S(1)}, u32[]{:S(2)}, u32[]{:S(2)}) collective-permute-start(bf16[800,128]{1,0:T(8,128)(2,1)S(1)} %shard_map.134.refs_0_), channel_id=1, source_target_pairs={{0,6},{1,7},{2,4},{3,5},{4,2},{5,3},{6,0},{7,1},{8,14},{9,15},{10,... | collective-permute-start | bytes 614408 | tf_op jit(solution)/shard_map/ppermute | solution.py:401
  32.7 1.0 %shard_map.135 = (f32[1024,128]{1,0:T(8,128)S(1)}, f32[1024,128]{1,0:T(8,128)S(1)}, bf16[128,128]{1,0:T(8,128)(2,1)S(1)}, bf16[128,128]{1,0:T(8,128)(2,1)S(1)}) custom-call(f32[2,512]{1,0:T(2,128)S(1)} %get-tuple-element.60.bias, bf16[1024,128]{1,0:T(8,128)(2,1)S(1)} %copy-done, bf16[1024,128]{1,0:T(8,128)(2,1)S(1)} %copy-done.2, ...), custom_call_target="tpu_custom_call" | custom-call | flops 335544320 | bytes 1150976 | tf_op jit(solution)/shard_map/pallas_call | solution.py:356
  33.7 0.8 %collective-permute-start.15 = (bf16[128,128]{1,0:T(8,128)(2,1)S(1)}, bf16[128,128]{1,0:T(8,128)(2,1)S(1)}, u32[]{:S(2)}, u32[]{:S(2)}) collective-permute-start(bf16[128,128]{1,0:T(8,128)(2,1)S(1)} %get-tuple-element.66), channel_id=1, source_target_pairs={{0,16},{8,24},{16,0},{24,8},{1,17},{9,25},{17,1},{25,9},{2,18},{10... | collective-permute-start | bytes 98312 | tf_op jit(solution)/shard_map/ppermute | solution.py:408
  34.5 1.9 %collective-permute-start.16 = (bf16[128,128]{1,0:T(8,128)(2,1)S(1)}, bf16[128,128]{1,0:T(8,128)(2,1)S(1)}, u32[]{:S(2)}, u32[]{:S(2)}) collective-permute-start(bf16[128,128]{1,0:T(8,128)(2,1)S(1)} %get-tuple-element.67), channel_id=1, source_target_pairs={{0,24},{8,16},{16,8},{24,0},{1,25},{9,17},{17,9},{25,1},{2,26},{10... | collective-permute-start | bytes 98312 | tf_op jit(solution)/shard_map/ppermute | solution.py:408
  36.4 1.7 %shard_map.136 = (bf16[1024,128]{1,0:T(8,128)(2,1)}, bf16[1024,128]{1,0:T(8,128)(2,1)}, bf16[128,128]{1,0:T(8,128)(2,1)S(1)}, bf16[128,128]{1,0:T(8,128)(2,1)S(1)}) custom-call(f32[2,512]{1,0:T(2,128)S(1)} %get-tuple-element.60.bias, bf16[1024,128]{1,0:T(8,128)(2,1)S(1)} %copy-done, bf16[1024,128]{1,0:T(8,128)(2,1)S(1)} %copy-done.2, ...), custom_call_target="tpu_custom_call" | custom-call | flops 335544320 | bytes 2199552 | tf_op jit(solution)/shard_map/pallas_call | solution.py:356
  38.6 1.6 %collective-permute-done.16.refs_3_ = bf16[128,128]{1,0:T(8,128)(2,1)S(1)} collective-permute-done((bf16[128,128]{1,0:T(8,128)(2,1)S(1)}, bf16[128,128]{1,0:T(8,128)(2,1)S(1)}, u32[]{:S(2)}, u32[]{:S(2)}) %collective-permute-start.16) | collective-permute-done | bytes 32800 | tf_op jit(solution)/shard_map/ppermute | solution.py:408
  41.8 1.5 %collective-permute-done.17.other = bf16[2880,128]{1,0:T(8,128)(2,1)S(1)} collective-permute-done((bf16[2880,128]{1,0:T(8,128)(2,1)S(1)}, bf16[2880,128]{1,0:T(8,128)(2,1)S(1)}, u32[]{:S(2)}, u32[]{:S(2)}) %collective-permute-start.17) | collective-permute-done | bytes 737312 | tf_op jit(solution)/shard_map/ppermute | solution.py:405
  43.3 1.3 %shard_map.139 = (f32[128,1280]{1,0:T(8,128)}, f32[16,5120]{1,0:T(8,128)}) custom-call(f32[8,16,128]{2,1,0:T(8,128)S(1)} %get-tuple-element.64.hot, bf16[2880,128]{1,0:T(8,128)(2,1)S(1)} %collective-permute-done.17.other, f32[128,640]{1,0:T(8,128)S(1)} %get-tuple-element.72.own_weight, f32[16,2560]{1,0:T(8,128)S(1)} %get-tuple-element.73.own_gate, ...), custom_call_target="tpu_custom_call" | custom-call | flops 83886080 | bytes 1556480 | tf_op jit(solution)/shard_map/pallas_call | solution.py:356
  45.1 0.7 %shard_map.140 = bf16[128,128]{1,0:T(8,128)(2,1)} custom-call(bf16[128,128]{1,0:T(8,128)(2,1)S(1)} %get-tuple-element.75.refs_0_, bf16[128,128]{1,0:T(8,128)(2,1)S(1)} %collective-permute-done.18.refs_1_, bf16[128,128]{1,0:T(8,128)(2,1)S(1)} %collective-permute-done.15.refs_2_, bf16[128,128]{1,0:T(8,128)(2,1)S(1)} %collective-permute-done.16.refs_3_), custom_call_target="tpu_custom_call" | custom-call | bytes 131072 | tf_op jit(solution)/shard_map/pallas_call | solution.py:356
  (40 shorter events, 6.6 us)
Async XLA Ops:
  0.6 12.4 %copy-start.1 = (f32[16,5120]{1,0:T(8,128)S(1)}, f32[16,5120]{1,0:T(8,128)}, u32[]{:S(2)}) copy-start(f32[16,5120]{1,0:T(8,128)} %gate) | copy-start | bytes 983044
  0.6 6.1 %collective-permute-start = (bf16[128,5120]{1,0:T(8,128)(2,1)}, bf16[128,5120]{1,0:T(8,128)(2,1)S(1)}, u32[]{:S(2)}, u32[]{:S(2)}) collective-permute-start(bf16[128,5120]{1,0:T(8,128)(2,1)} %weight_in), channel_id=1, source_target_pairs={{0,1},{1,0},{2,3},{3,2},{4,5},{5,4},{6,7},{7,6},{8,9},{9,8},{10,11... | collective-permute-start | bytes 3932168 | tf_op jit(solution)/shard_map/ppermute | solution.py:405
  1.2 12.6 %collective-permute-start.5 = (bf16[128,640]{1,0:T(8,128)(2,1)}, bf16[128,640]{1,0:T(8,128)(2,1)S(1)}, u32[]{:S(2)}, u32[]{:S(2)}) collective-permute-start(bf16[128,640]{1,0:T(8,128)(2,1)} %grad_in), channel_id=1, source_target_pairs={{0,2},{1,3},{2,0},{3,1},{4,6},{5,7},{6,4},{7,5},{8,10},{9,11},{10,... | collective-permute-start | bytes 491528 | tf_op jit(solution)/shard_map/ppermute | solution.py:401
  3.7 10.7 %collective-permute-start.6 = (bf16[128,640]{1,0:T(8,128)(2,1)}, bf16[128,640]{1,0:T(8,128)(2,1)S(1)}, u32[]{:S(2)}, u32[]{:S(2)}) collective-permute-start(bf16[128,640]{1,0:T(8,128)(2,1)} %grad_in), channel_id=1, source_target_pairs={{0,4},{1,5},{2,6},{3,7},{4,0},{5,1},{6,2},{7,3},{8,12},{9,13},{10,... | collective-permute-start | bytes 491528 | tf_op jit(solution)/shard_map/ppermute | solution.py:401
  5.2 9.2 %collective-permute-start.7 = (bf16[128,640]{1,0:T(8,128)(2,1)}, bf16[128,640]{1,0:T(8,128)(2,1)S(1)}, u32[]{:S(2)}, u32[]{:S(2)}) collective-permute-start(bf16[128,640]{1,0:T(8,128)(2,1)} %grad_in), channel_id=1, source_target_pairs={{0,6},{1,7},{2,4},{3,5},{4,2},{5,3},{6,0},{7,1},{8,14},{9,15},{10,... | collective-permute-start | bytes 491528 | tf_op jit(solution)/shard_map/ppermute | solution.py:401
  5.3 1.4 %collective-permute-start.1 = (bf16[128,128]{1,0:T(8,128)(2,1)}, bf16[128,128]{1,0:T(8,128)(2,1)S(1)}, u32[]{:S(2)}, u32[]{:S(2)}) collective-permute-start(bf16[128,128]{1,0:T(8,128)(2,1)} %param.12), channel_id=1, source_target_pairs={{0,1},{1,0},{2,3},{3,2},{4,5},{5,4},{6,7},{7,6},{8,9},{9,8},{10,11... | collective-permute-start | bytes 98312 | tf_op jit(solution)/shard_map/ppermute | solution.py:405
  6.7 8.6 %collective-permute-start.2 = (bf16[2,128,128]{2,1,0:T(8,128)(2,1)S(1)}, bf16[2,128,128]{2,1,0:T(8,128)(2,1)S(1)}, u32[]{:S(2)}, u32[]{:S(2)}) collective-permute-start(bf16[2,128,128]{2,1,0:T(8,128)(2,1)S(1)} %pad_maximum_fusion.packed.refs_0_), channel_id=1, source_target_pairs={{0,24},{8,16},{16,8},{24,0},{1,25},{9,17},{17,9},{25,1},{2,26},{10... | collective-permute-start | bytes 196616 | tf_op jit(solution)/shard_map/ppermute | solution.py:408
  10.7 5.9 %collective-permute-start.3 = (bf16[2,128,128]{2,1,0:T(8,128)(2,1)S(1)}, bf16[2,128,128]{2,1,0:T(8,128)(2,1)S(1)}, u32[]{:S(2)}, u32[]{:S(2)}) collective-permute-start(bf16[2,128,128]{2,1,0:T(8,128)(2,1)S(1)} %pad_maximum_fusion.packed.refs_0_), channel_id=1, source_target_pairs={{0,16},{8,24},{16,0},{24,8},{1,17},{9,25},{17,1},{25,9},{2,18},{10... | collective-permute-start | bytes 196616 | tf_op jit(solution)/shard_map/ppermute | solution.py:408
  11.7 1.4 %copy-start.4 = (s32[8]{0:T(128)S(1)}, s32[8]{0:T(128)}, u32[]{:S(2)}) copy-start(s32[8]{0:T(128)} %levels.1) | copy-start | bytes 100
  11.7 1.4 %copy-start.5 = (s32[4]{0:T(128)S(1)}, s32[4]{0:T(128)}, u32[]{:S(2)}) copy-start(s32[4]{0:T(128)} %clips.1) | copy-start | bytes 52
  13.8 4.3 %collective-permute-start.4 = (bf16[2,128,128]{2,1,0:T(8,128)(2,1)S(1)}, bf16[2,128,128]{2,1,0:T(8,128)(2,1)S(1)}, u32[]{:S(2)}, u32[]{:S(2)}) collective-permute-start(bf16[2,128,128]{2,1,0:T(8,128)(2,1)S(1)} %pad_maximum_fusion.packed.refs_0_), channel_id=1, source_target_pairs={{0,8},{8,0},{16,24},{24,16},{1,9},{9,1},{17,25},{25,17},{2,10},{10... | collective-permute-start | bytes 196616 | tf_op jit(solution)/shard_map/ppermute | solution.py:408
  14.4 2.3 %copy-start = (bf16[1024,128]{1,0:T(8,128)(2,1)S(1)}, bf16[1024,128]{1,0:T(8,128)(2,1)}, u32[]{:S(2)}) copy-start(bf16[1024,128]{1,0:T(8,128)(2,1)} %keys.7) | copy-start | bytes 786436
  15.2 17.5 %copy-start.2 = (bf16[1024,128]{1,0:T(8,128)(2,1)S(1)}, bf16[1024,128]{1,0:T(8,128)(2,1)}, u32[]{:S(2)}) copy-start(bf16[1024,128]{1,0:T(8,128)(2,1)} %values.3) | copy-start | bytes 786436
  15.2 3.4 %collective-permute-start.8 = (f32[128,128]{1,0:T(8,128)S(1)}, f32[128,128]{1,0:T(8,128)S(1)}, u32[]{:S(2)}, u32[]{:S(2)}) collective-permute-start(f32[128,128]{1,0:T(8,128)S(1)} %get-tuple-element.51), channel_id=1, source_target_pairs={{0,1},{1,0},{2,3},{3,2},{4,5},{5,4},{6,7},{7,6},{8,9},{9,8},{10,11... | collective-permute-start | bytes 196616 | tf_op jit(solution)/shard_map/ppermute | solution.py:405
  18.7 6.8 %collective-permute-start.10 = (bf16[352,128]{1,0:T(8,128)(2,1)S(1)}, bf16[352,128]{1,0:T(8,128)(2,1)S(1)}, u32[]{:S(2)}, u32[]{:S(2)}) collective-permute-start(bf16[352,128]{1,0:T(8,128)(2,1)S(1)} %get-tuple-element.57), channel_id=1, source_target_pairs={{0,24},{8,16},{16,8},{24,0},{1,25},{9,17},{17,9},{25,1},{2,26},{10... | collective-permute-start | bytes 270344 | tf_op jit(solution)/shard_map/ppermute | solution.py:408
  21.2 7.8 %collective-permute-start.11 = (bf16[352,128]{1,0:T(8,128)(2,1)S(1)}, bf16[352,128]{1,0:T(8,128)(2,1)S(1)}, u32[]{:S(2)}, u32[]{:S(2)}) collective-permute-start(bf16[352,128]{1,0:T(8,128)(2,1)S(1)} %get-tuple-element.58), channel_id=1, source_target_pairs={{0,16},{8,24},{16,0},{24,8},{1,17},{9,25},{17,1},{25,9},{2,18},{10... | collective-permute-start | bytes 270344 | tf_op jit(solution)/shard_map/ppermute | solution.py:408
  21.8 7.3 %collective-permute-start.9 = (bf16[352,128]{1,0:T(8,128)(2,1)S(1)}, bf16[352,128]{1,0:T(8,128)(2,1)S(1)}, u32[]{:S(2)}, u32[]{:S(2)}) collective-permute-start(bf16[352,128]{1,0:T(8,128)(2,1)S(1)} %get-tuple-element.56), channel_id=1, source_target_pairs={{0,8},{8,0},{16,24},{24,16},{1,9},{9,1},{17,25},{25,17},{2,10},{10... | collective-permute-start | bytes 270344 | tf_op jit(solution)/shard_map/ppermute | solution.py:408
  29.1 11.1 %collective-permute-start.12 = (bf16[800,128]{1,0:T(8,128)(2,1)S(1)}, bf16[800,128]{1,0:T(8,128)(2,1)S(1)}, u32[]{:S(2)}, u32[]{:S(2)}) collective-permute-start(bf16[800,128]{1,0:T(8,128)(2,1)S(1)} %shard_map.134.refs_0_), channel_id=1, source_target_pairs={{0,6},{1,7},{2,4},{3,5},{4,2},{5,3},{6,0},{7,1},{8,14},{9,15},{10,... | collective-permute-start | bytes 614408 | tf_op jit(solution)/shard_map/ppermute | solution.py:401
  31.6 9.2 %collective-permute-start.13 = (bf16[800,128]{1,0:T(8,128)(2,1)S(1)}, bf16[800,128]{1,0:T(8,128)(2,1)S(1)}, u32[]{:S(2)}, u32[]{:S(2)}) collective-permute-start(bf16[800,128]{1,0:T(8,128)(2,1)S(1)} %shard_map.134.refs_0_), channel_id=1, source_target_pairs={{0,4},{1,5},{2,6},{3,7},{4,0},{5,1},{6,2},{7,3},{8,12},{9,13},{10,... | collective-permute-start | bytes 614408 | tf_op jit(solution)/shard_map/ppermute | solution.py:401
  32.1 8.8 %collective-permute-start.14 = (bf16[800,128]{1,0:T(8,128)(2,1)S(1)}, bf16[800,128]{1,0:T(8,128)(2,1)S(1)}, u32[]{:S(2)}, u32[]{:S(2)}) collective-permute-start(bf16[800,128]{1,0:T(8,128)(2,1)S(1)} %shard_map.134.refs_0_), channel_id=1, source_target_pairs={{0,2},{1,3},{2,0},{3,1},{4,6},{5,7},{6,4},{7,5},{8,10},{9,11},{10,... | collective-permute-start | bytes 614408 | tf_op jit(solution)/shard_map/ppermute | solution.py:401
  33.7 4.9 %collective-permute-start.15 = (bf16[128,128]{1,0:T(8,128)(2,1)S(1)}, bf16[128,128]{1,0:T(8,128)(2,1)S(1)}, u32[]{:S(2)}, u32[]{:S(2)}) collective-permute-start(bf16[128,128]{1,0:T(8,128)(2,1)S(1)} %get-tuple-element.66), channel_id=1, source_target_pairs={{0,16},{8,24},{16,0},{24,8},{1,17},{9,25},{17,1},{25,9},{2,18},{10... | collective-permute-start | bytes 98312 | tf_op jit(solution)/shard_map/ppermute | solution.py:408
  34.5 5.7 %collective-permute-start.16 = (bf16[128,128]{1,0:T(8,128)(2,1)S(1)}, bf16[128,128]{1,0:T(8,128)(2,1)S(1)}, u32[]{:S(2)}, u32[]{:S(2)}) collective-permute-start(bf16[128,128]{1,0:T(8,128)(2,1)S(1)} %get-tuple-element.67), channel_id=1, source_target_pairs={{0,24},{8,16},{16,8},{24,0},{1,25},{9,17},{17,9},{25,1},{2,26},{10... | collective-permute-start | bytes 98312 | tf_op jit(solution)/shard_map/ppermute | solution.py:408
  41.0 2.3 %collective-permute-start.17 = (bf16[2880,128]{1,0:T(8,128)(2,1)S(1)}, bf16[2880,128]{1,0:T(8,128)(2,1)S(1)}, u32[]{:S(2)}, u32[]{:S(2)}) collective-permute-start(bf16[2880,128]{1,0:T(8,128)(2,1)S(1)} %shard_map.137.own), channel_id=1, source_target_pairs={{0,1},{1,0},{2,3},{3,2},{4,5},{5,4},{6,7},{7,6},{8,9},{9,8},{10,11... | collective-permute-start | bytes 2211848 | tf_op jit(solution)/shard_map/ppermute | solution.py:405
  41.1 4.0 %collective-permute-start.18 = (bf16[128,128]{1,0:T(8,128)(2,1)S(1)}, bf16[128,128]{1,0:T(8,128)(2,1)S(1)}, u32[]{:S(2)}, u32[]{:S(2)}) collective-permute-start(bf16[128,128]{1,0:T(8,128)(2,1)S(1)} %get-tuple-element.76), channel_id=1, source_target_pairs={{0,8},{8,0},{16,24},{24,16},{1,9},{9,1},{17,25},{25,17},{2,10},{10... | collective-permute-start | bytes 98312 | tf_op jit(solution)/shard_map/ppermute | solution.py:408
  (1 other events, 0.9 us)

commit v23 on v22

--- a/solution.py
+++ b/solution.py
@@ -278,18 +278,23 @@
     refs[n_t][...] = jnp.transpose(total * SCALE).astype(jnp.bfloat16)
 
 
-def half_results(n_t, chips, frames, hot, ref, packed, saved, held, tiles):
-    t, chip, _ = place()
-    rows = saved.shape[1]
-    part = rows // chips
-    base = tiles * n_t * part
+def order_kernel(n_t, chips, *refs):
+    packed, (out, saved) = refs[:n_t], refs[n_t:]
+    chip = place()[1]
+    part = saved.shape[1] // chips
     for k in range(n_t):
         saved[k] = packed[k][1].astype(jnp.float32)
     ordered = []
     for c in range(chips):
         mine = pl.ds(pl.multiple_of((chip ^ c) * part, part), part)
         ordered += [saved[k, mine, :] for k in range(n_t)]
-    ordered = jnp.transpose(jnp.concatenate(ordered, axis=0)).astype(jnp.bfloat16)
+    out[...] = jnp.transpose(jnp.concatenate(ordered, axis=0)).astype(jnp.bfloat16)
+
+
+def half_results(n_t, chips, frames, hot, ref, ordered, held, tiles):
+    t = lax.axis_index("tm")
+    part = ordered.shape[1] // (n_t * chips)
+    base = tiles * n_t * part
     gated = jnp.concatenate(
         [
             jnp.concatenate(
@@ -317,25 +322,25 @@
             total = total + hot[f] * held[f // frames, row : row + 1, :]
         return total
 
-    return dot(ordered, gated, 1, 0), gate_tile
-
-
-def own_kernel(n_t, chips, frames, hot, own, *refs):
-    packed, (weight_out, gate_out, saved, held) = refs[:n_t], refs[n_t:]
+    return dot(ordered[...], gated, 1, 0), gate_tile
+
+
+def own_kernel(n_t, chips, frames, hot, own, ordered, weight_out, gate_out, held):
     tiles = weight_out.shape[1] // LANES
-    result, gate_tile = half_results(n_t, chips, frames, hot, own, packed, saved, held, tiles)
+    result, gate_tile = half_results(n_t, chips, frames, hot, own, ordered, held, tiles)
     weight_out[...] = result
     for a in range(chips):
         for j in range(tiles):
             gate_out[:, (a * tiles + j) * LANES : (a * tiles + j + 1) * LANES] = gate_tile(a, j)
 
 
-def final_kernel(n_t, chips, frames, hot, other, own_weight, own_gate, *refs):
-    packed, (weight_out, gate_out, saved, held) = refs[:n_t], refs[n_t:]
+def final_kernel(
+    n_t, chips, frames, hot, other, own_weight, own_gate, ordered, weight_out, gate_out, held
+):
     core = place()[2]
     width = own_weight.shape[1]
     tiles = width // LANES
-    result, gate_tile = half_results(n_t, chips, frames, hot, other, packed, saved, held, tiles)
+    result, gate_tile = half_results(n_t, chips, frames, hot, other, ordered, held, tiles)
     mine = own_weight[...]
     weight_out[:, :width] = jnp.where(core == 0, mine, result)
     weight_out[:, width:] = jnp.where(core == 0, result, mine)
@@ -496,24 +501,31 @@
     key_grad, value_grad = near[:2]
     parts[0], parts[1] = near[2], over_time(near[3], 1)
     parts = [parts[k] for k in range(n_t)]
-    bundles, _ = lax.optimization_barrier((bundles, (key_grad, parts[n_t // 2 :])))
+    to_order, _ = lax.optimization_barrier((packed_all, key_grad))
+    ordered = call(
+        functools.partial(order_kernel, n_t, chips),
+        to_order,
+        shape(bf16, HD, n_t * rows),
+        [pltpu.VMEM((n_t, rows, HD), f32)],
+    )
+    bundles, _ = lax.optimization_barrier((bundles, (ordered, key_grad, parts[n_t // 2 :])))
     collected = call(
         functools.partial(collect_kernel, chips, base),
         bundles,
         shape(bf16, chips * base + 2 * n_t * count, LANES),
         [pltpu.VMEM((chips, n_t * count, LANES), f32)],
     )
-    scratch = [pltpu.VMEM((n_t, rows, HD), f32), pltpu.VMEM((n_t, count, LANES), f32)]
+    scratch = [pltpu.VMEM((n_t, count, LANES), f32)]
     own_halves = call(
         functools.partial(own_kernel, n_t, chips, frames),
-        [hot, collected] + packed_all,
+        [hot, collected, ordered],
         [shape(f32, HD, width), shape(f32, levels, chips * width)],
         scratch,
         flops=2 * n_t * rows * width * HD,
     )
     weight_grad, gate_grad = call(
         functools.partial(final_kernel, n_t, chips, frames),
-        [hot, over_cores(collected), *own_halves] + packed_all,
+        [hot, over_cores(collected), *own_halves, ordered],
         [shape(f32, HD, 2 * width), shape(f32, levels, n_s * width)],
         scratch,
         flops=2 * n_t * rows * width * HD,

time: 46 us -> 46 us (level)
    pallas_call x13 -> x14, Pallas kernels: 9.08 us -> 9.01 us  [call(): pl.pallas_call(kernel, out_shape=out_shape, in_specs=[pl.BlockSpec(memory...]
where the time goes in v23:
time: 46 us; the launch traced here: 45.8 us
  starting transfers between devices  20.5 us (45%)
  waiting for transfers between devices  13.8 us (30%)
  Pallas kernels  9.01 us (20%)
  local copies, waits for them, and re-layouts  0.94 us (2%)
  between operations  0.79 us (2%)
  other arithmetic  0.78 us (2%)
    ppermute x9, starting transfers between devices, over_time(): return lax.ppermute(x, 'tm', [(t, t ^ k) for t in range(n_t)])  12.2 us
    ppermute x9, waiting for transfers between devices, over_time(): return lax.ppermute(x, 'tm', [(t, t ^ k) for t in range(n_t)])  10.8 us
    pallas_call x14, Pallas kernels, call(): pl.pallas_call(kernel, out_shape=out_shape, in_specs=[pl.BlockSpec(memory...  9.01 us
    ppermute x6, starting transfers between devices, over_chips(): lax.ppermute(x, 'space', [(s, s ^ 2 * k) for s in range(n_s)])  7.66 us
    ppermute x4, waiting for transfers between devices, over_cores(): return lax.ppermute(x, 'space', [(s, s ^ 1) for s in range(n_s)])  2.28 us
    unnamed x12, local copies, waits for them, and re-layouts  0.94 us
  transfers between devices with their start and end apart: 19, of which 11 were waited for; matrix products, arithmetic and copies ran while one was open for 2% of the time, Pallas kernels for 18%

profile of v23, /device:TPU:0, one launch (start us, length us, event | category | flops | bytes accessed | tf_op | source)
XLA Modules:
  0.0 45.8 jit_solution(14033027826345113051)
XLA Ops:
  1.2 2.6 %collective-permute-start.5 = (bf16[128,640]{1,0:T(8,128)(2,1)}, bf16[128,640]{1,0:T(8,128)(2,1)S(1)}, u32[]{:S(2)}, u32[]{:S(2)}) collective-permute-start(bf16[128,640]{1,0:T(8,128)(2,1)} %grad_in), channel_id=1, source_target_pairs={{0,2},{1,3},{2,0},{3,1},{4,6},{5,7},{6,4},{7,5},{8,10},{9,11},{10,... | collective-permute-start | bytes 491528 | tf_op jit(solution)/shard_map/ppermute | solution.py:406
  3.7 1.5 %collective-permute-start.6 = (bf16[128,640]{1,0:T(8,128)(2,1)}, bf16[128,640]{1,0:T(8,128)(2,1)S(1)}, u32[]{:S(2)}, u32[]{:S(2)}) collective-permute-start(bf16[128,640]{1,0:T(8,128)(2,1)} %grad_in), channel_id=1, source_target_pairs={{0,4},{1,5},{2,6},{3,7},{4,0},{5,1},{6,2},{7,3},{8,12},{9,13},{10,... | collective-permute-start | bytes 491528 | tf_op jit(solution)/shard_map/ppermute | solution.py:406
  5.3 0.8 %pad_maximum_fusion.packed.refs_0_ = bf16[2,128,128]{2,1,0:T(8,128)(2,1)S(1)} fusion(bf16[1,128,128]{2,1,0:T(8,128)(2,1)} %bitcast.3, bf16[1,128,128]{2,1,0:T(8,128)(2,1)} %bitcast.2), kind=kLoop, calls=%fused_computation | loop fusion | flops 32768 | bytes 131072 | tf_op jit(solution)/shard_map/stack | solution.py:427
  6.1 0.6 %collective-permute-done.1.other_saved = bf16[128,128]{1,0:T(8,128)(2,1)S(1)} collective-permute-done((bf16[128,128]{1,0:T(8,128)(2,1)}, bf16[128,128]{1,0:T(8,128)(2,1)S(1)}, u32[]{:S(2)}, u32[]{:S(2)}) %collective-permute-start.1) | collective-permute-done | bytes 32800 | tf_op jit(solution)/shard_map/ppermute | solution.py:410
  6.7 4.1 %collective-permute-start.2 = (bf16[2,128,128]{2,1,0:T(8,128)(2,1)S(1)}, bf16[2,128,128]{2,1,0:T(8,128)(2,1)S(1)}, u32[]{:S(2)}, u32[]{:S(2)}) collective-permute-start(bf16[2,128,128]{2,1,0:T(8,128)(2,1)S(1)} %pad_maximum_fusion.packed.refs_0_), channel_id=1, source_target_pairs={{0,24},{8,16},{16,8},{24,0},{1,25},{9,17},{17,9},{25,1},{2,26},{10... | collective-permute-start | bytes 196616 | tf_op jit(solution)/shard_map/ppermute | solution.py:413
  10.8 0.9 %copy-done.3 = bf16[128,640]{1,0:T(8,128)(2,1)S(1)} copy-done((bf16[128,640]{1,0:T(8,128)(2,1)S(1)}, bf16[128,640]{1,0:T(8,128)(2,1)}, u32[]{:S(2)}) %copy-start.3) | copy-done | bytes 163864
  11.7 1.4 %shard_map.129 = (bf16[4,128,640]{2,1,0:T(8,128)(2,1)S(1)}, bf16[128,640]{1,0:T(8,128)(2,1)S(1)}) custom-call(bf16[128,5120]{1,0:T(8,128)(2,1)} %weight_in, bf16[128,640]{1,0:T(8,128)(2,1)S(1)} %copy-done.3), custom_call_target="tpu_custom_call" | custom-call | bytes 1474560 | tf_op jit(solution)/shard_map/pallas_call | solution.py:361
  13.1 0.7 %shard_map.128 = (f32[2,512]{1,0:T(2,128)S(1)}, f32[4,2,640]{2,1,0:T(2,128)S(1)}, f32[4,1,640]{2,1,0:T(1,128)S(1)}, f32[8,16,128]{2,1,0:T(8,128)S(1)}) custom-call(s32[8]{0:T(128)S(1)} %copy-done.4, s32[4]{0:T(128)S(1)} %copy-done.5, f32[16,5120]{1,0:T(8,128)S(1)} %copy-done.1), custom_call_target="tpu_custom_call" | custom-call | bytes 327728 | tf_op jit(solution)/shard_map/pallas_call | solution.py:361
  14.4 0.8 %shard_map.130 = (f32[128,128]{1,0:T(8,128)S(1)}, f32[128,128]{1,0:T(8,128)S(1)}, f32[40,128]{1,0:T(8,128)S(1)}) custom-call(bf16[2,128,128]{2,1,0:T(8,128)(2,1)S(1)} %pad_maximum_fusion.packed.refs_0_, bf16[128,128]{1,0:T(8,128)(2,1)S(1)} %collective-permute-done.1.other_saved, bf16[4,128,640]{2,1,0:T(8,128)(2,1)S(1)} %get-tuple-element.51.kept, ...), custom_call_target="tpu_custom_call" | custom-call | flops 335544320 | bytes 2740224 | tf_op jit(solution)/shard_map/pallas_call | solution.py:361
  15.3 1.4 %collective-permute-done.3.refs_0_.refs_2_ = bf16[2,128,128]{2,1,0:T(8,128)(2,1)S(1)} collective-permute-done((bf16[2,128,128]{2,1,0:T(8,128)(2,1)S(1)}, bf16[2,128,128]{2,1,0:T(8,128)(2,1)S(1)}, u32[]{:S(2)}, u32[]{:S(2)}) %collective-permute-start.3) | collective-permute-done | bytes 65568 | tf_op jit(solution)/shard_map/ppermute | solution.py:413
  17.2 0.9 %collective-permute-done.4.refs_1_.refs_3_ = bf16[2,128,128]{2,1,0:T(8,128)(2,1)S(1)} collective-permute-done((bf16[2,128,128]{2,1,0:T(8,128)(2,1)S(1)}, bf16[2,128,128]{2,1,0:T(8,128)(2,1)S(1)}, u32[]{:S(2)}, u32[]{:S(2)}) %collective-permute-start.4) | collective-permute-done | bytes 65568 | tf_op jit(solution)/shard_map/ppermute | solution.py:413
  18.7 2.5 %collective-permute-start.10 = (bf16[352,128]{1,0:T(8,128)(2,1)S(1)}, bf16[352,128]{1,0:T(8,128)(2,1)S(1)}, u32[]{:S(2)}, u32[]{:S(2)}) collective-permute-start(bf16[352,128]{1,0:T(8,128)(2,1)S(1)} %get-tuple-element.61), channel_id=1, source_target_pairs={{0,24},{8,16},{16,8},{24,0},{1,25},{9,17},{17,9},{25,1},{2,26},{10... | collective-permute-start | bytes 270344 | tf_op jit(solution)/shard_map/ppermute | solution.py:413
  21.8 1.4 %collective-permute-start.9 = (bf16[352,128]{1,0:T(8,128)(2,1)S(1)}, bf16[352,128]{1,0:T(8,128)(2,1)S(1)}, u32[]{:S(2)}, u32[]{:S(2)}) collective-permute-start(bf16[352,128]{1,0:T(8,128)(2,1)S(1)} %get-tuple-element.60), channel_id=1, source_target_pairs={{0,8},{8,0},{16,24},{24,16},{1,9},{9,1},{17,25},{25,17},{2,10},{10... | collective-permute-start | bytes 270344 | tf_op jit(solution)/shard_map/ppermute | solution.py:413
  23.2 2.4 %collective-permute-done.10.refs_2_.refs_6_ = bf16[352,128]{1,0:T(8,128)(2,1)S(1)} collective-permute-done((bf16[352,128]{1,0:T(8,128)(2,1)S(1)}, bf16[352,128]{1,0:T(8,128)(2,1)S(1)}, u32[]{:S(2)}, u32[]{:S(2)}) %collective-permute-start.10) | collective-permute-done | bytes 90144 | tf_op jit(solution)/shard_map/ppermute | solution.py:413
  25.6 3.5 %collective-permute-done.11.refs_3_.refs_7_ = bf16[352,128]{1,0:T(8,128)(2,1)S(1)} collective-permute-done((bf16[352,128]{1,0:T(8,128)(2,1)S(1)}, bf16[352,128]{1,0:T(8,128)(2,1)S(1)}, u32[]{:S(2)}, u32[]{:S(2)}) %collective-permute-start.11) | collective-permute-done | bytes 90144 | tf_op jit(solution)/shard_map/ppermute | solution.py:413
  29.1 2.5 %collective-permute-start.12 = (bf16[800,128]{1,0:T(8,128)(2,1)S(1)}, bf16[800,128]{1,0:T(8,128)(2,1)S(1)}, u32[]{:S(2)}, u32[]{:S(2)}) collective-permute-start(bf16[800,128]{1,0:T(8,128)(2,1)S(1)} %shard_map.134.refs_0_), channel_id=1, source_target_pairs={{0,6},{1,7},{2,4},{3,5},{4,2},{5,3},{6,0},{7,1},{8,14},{9,15},{10,... | collective-permute-start | bytes 614408 | tf_op jit(solution)/shard_map/ppermute | solution.py:406
  32.7 1.0 %shard_map.135 = (f32[1024,128]{1,0:T(8,128)S(1)}, f32[1024,128]{1,0:T(8,128)S(1)}, bf16[128,128]{1,0:T(8,128)(2,1)S(1)}, bf16[128,128]{1,0:T(8,128)(2,1)S(1)}) custom-call(f32[2,512]{1,0:T(2,128)S(1)} %get-tuple-element.64.bias, bf16[1024,128]{1,0:T(8,128)(2,1)S(1)} %copy-done, bf16[1024,128]{1,0:T(8,128)(2,1)S(1)} %copy-done.2, ...), custom_call_target="tpu_custom_call" | custom-call | flops 335544320 | bytes 1150976 | tf_op jit(solution)/shard_map/pallas_call | solution.py:361
  33.7 0.8 %collective-permute-start.15 = (bf16[128,128]{1,0:T(8,128)(2,1)S(1)}, bf16[128,128]{1,0:T(8,128)(2,1)S(1)}, u32[]{:S(2)}, u32[]{:S(2)}) collective-permute-start(bf16[128,128]{1,0:T(8,128)(2,1)S(1)} %get-tuple-element.74), channel_id=1, source_target_pairs={{0,16},{8,24},{16,0},{24,8},{1,17},{9,25},{17,1},{25,9},{2,18},{10... | collective-permute-start | bytes 98312 | tf_op jit(solution)/shard_map/ppermute | solution.py:413
  34.5 1.9 %collective-permute-start.16 = (bf16[128,128]{1,0:T(8,128)(2,1)S(1)}, bf16[128,128]{1,0:T(8,128)(2,1)S(1)}, u32[]{:S(2)}, u32[]{:S(2)}) collective-permute-start(bf16[128,128]{1,0:T(8,128)(2,1)S(1)} %get-tuple-element.75), channel_id=1, source_target_pairs={{0,24},{8,16},{16,8},{24,0},{1,25},{9,17},{17,9},{25,1},{2,26},{10... | collective-permute-start | bytes 98312 | tf_op jit(solution)/shard_map/ppermute | solution.py:413
  36.4 1.7 %shard_map.136 = (bf16[1024,128]{1,0:T(8,128)(2,1)}, bf16[1024,128]{1,0:T(8,128)(2,1)}, bf16[128,128]{1,0:T(8,128)(2,1)S(1)}, bf16[128,128]{1,0:T(8,128)(2,1)S(1)}) custom-call(f32[2,512]{1,0:T(2,128)S(1)} %get-tuple-element.64.bias, bf16[1024,128]{1,0:T(8,128)(2,1)S(1)} %copy-done, bf16[1024,128]{1,0:T(8,128)(2,1)S(1)} %copy-done.2, ...), custom_call_target="tpu_custom_call" | custom-call | flops 335544320 | bytes 2199552 | tf_op jit(solution)/shard_map/pallas_call | solution.py:361
  38.6 1.6 %collective-permute-done.16.refs_3_ = bf16[128,128]{1,0:T(8,128)(2,1)S(1)} collective-permute-done((bf16[128,128]{1,0:T(8,128)(2,1)S(1)}, bf16[128,128]{1,0:T(8,128)(2,1)S(1)}, u32[]{:S(2)}, u32[]{:S(2)}) %collective-permute-start.16) | collective-permute-done | bytes 32800 | tf_op jit(solution)/shard_map/ppermute | solution.py:413
  41.6 1.6 %collective-permute-done.17.other = bf16[2880,128]{1,0:T(8,128)(2,1)S(1)} collective-permute-done((bf16[2880,128]{1,0:T(8,128)(2,1)S(1)}, bf16[2880,128]{1,0:T(8,128)(2,1)S(1)}, u32[]{:S(2)}, u32[]{:S(2)}) %collective-permute-start.17) | collective-permute-done | bytes 737312 | tf_op jit(solution)/shard_map/ppermute | solution.py:410
  43.3 1.2 %shard_map.140 = (f32[128,1280]{1,0:T(8,128)}, f32[16,5120]{1,0:T(8,128)}) custom-call(f32[8,16,128]{2,1,0:T(8,128)S(1)} %get-tuple-element.68.hot, bf16[2880,128]{1,0:T(8,128)(2,1)S(1)} %collective-permute-done.17.other, f32[128,640]{1,0:T(8,128)S(1)} %get-tuple-element.80.own_weight, f32[16,2560]{1,0:T(8,128)S(1)} %get-tuple-element.81.own_gate, ...), custom_call_target="tpu_custom_call" | custom-call | flops 83886080 | bytes 1425408 | tf_op jit(solution)/shard_map/pallas_call | solution.py:361
  45.1 0.7 %shard_map.141 = bf16[128,128]{1,0:T(8,128)(2,1)} custom-call(bf16[128,128]{1,0:T(8,128)(2,1)S(1)} %get-tuple-element.83.refs_0_, bf16[128,128]{1,0:T(8,128)(2,1)S(1)} %collective-permute-done.18.refs_1_, bf16[128,128]{1,0:T(8,128)(2,1)S(1)} %collective-permute-done.15.refs_2_, bf16[128,128]{1,0:T(8,128)(2,1)S(1)} %collective-permute-done.16.refs_3_), custom_call_target="tpu_custom_call" | custom-call | bytes 131072 | tf_op jit(solution)/shard_map/pallas_call | solution.py:361
  (41 shorter events, 6.5 us)
Async XLA Ops:
  0.6 12.4 %copy-start.1 = (f32[16,5120]{1,0:T(8,128)S(1)}, f32[16,5120]{1,0:T(8,128)}, u32[]{:S(2)}) copy-start(f32[16,5120]{1,0:T(8,128)} %gate) | copy-start | bytes 983044
  0.6 6.1 %collective-permute-start = (bf16[128,5120]{1,0:T(8,128)(2,1)}, bf16[128,5120]{1,0:T(8,128)(2,1)S(1)}, u32[]{:S(2)}, u32[]{:S(2)}) collective-permute-start(bf16[128,5120]{1,0:T(8,128)(2,1)} %weight_in), channel_id=1, source_target_pairs={{0,1},{1,0},{2,3},{3,2},{4,5},{5,4},{6,7},{7,6},{8,9},{9,8},{10,11... | collective-permute-start | bytes 3932168 | tf_op jit(solution)/shard_map/ppermute | solution.py:410
  1.2 12.6 %collective-permute-start.5 = (bf16[128,640]{1,0:T(8,128)(2,1)}, bf16[128,640]{1,0:T(8,128)(2,1)S(1)}, u32[]{:S(2)}, u32[]{:S(2)}) collective-permute-start(bf16[128,640]{1,0:T(8,128)(2,1)} %grad_in), channel_id=1, source_target_pairs={{0,2},{1,3},{2,0},{3,1},{4,6},{5,7},{6,4},{7,5},{8,10},{9,11},{10,... | collective-permute-start | bytes 491528 | tf_op jit(solution)/shard_map/ppermute | solution.py:406
  3.7 10.7 %collective-permute-start.6 = (bf16[128,640]{1,0:T(8,128)(2,1)}, bf16[128,640]{1,0:T(8,128)(2,1)S(1)}, u32[]{:S(2)}, u32[]{:S(2)}) collective-permute-start(bf16[128,640]{1,0:T(8,128)(2,1)} %grad_in), channel_id=1, source_target_pairs={{0,4},{1,5},{2,6},{3,7},{4,0},{5,1},{6,2},{7,3},{8,12},{9,13},{10,... | collective-permute-start | bytes 491528 | tf_op jit(solution)/shard_map/ppermute | solution.py:406
  5.2 9.2 %collective-permute-start.7 = (bf16[128,640]{1,0:T(8,128)(2,1)}, bf16[128,640]{1,0:T(8,128)(2,1)S(1)}, u32[]{:S(2)}, u32[]{:S(2)}) collective-permute-start(bf16[128,640]{1,0:T(8,128)(2,1)} %grad_in), channel_id=1, source_target_pairs={{0,6},{1,7},{2,4},{3,5},{4,2},{5,3},{6,0},{7,1},{8,14},{9,15},{10,... | collective-permute-start | bytes 491528 | tf_op jit(solution)/shard_map/ppermute | solution.py:406
  5.3 1.4 %collective-permute-start.1 = (bf16[128,128]{1,0:T(8,128)(2,1)}, bf16[128,128]{1,0:T(8,128)(2,1)S(1)}, u32[]{:S(2)}, u32[]{:S(2)}) collective-permute-start(bf16[128,128]{1,0:T(8,128)(2,1)} %param.12), channel_id=1, source_target_pairs={{0,1},{1,0},{2,3},{3,2},{4,5},{5,4},{6,7},{7,6},{8,9},{9,8},{10,11... | collective-permute-start | bytes 98312 | tf_op jit(solution)/shard_map/ppermute | solution.py:410
  6.7 8.6 %collective-permute-start.2 = (bf16[2,128,128]{2,1,0:T(8,128)(2,1)S(1)}, bf16[2,128,128]{2,1,0:T(8,128)(2,1)S(1)}, u32[]{:S(2)}, u32[]{:S(2)}) collective-permute-start(bf16[2,128,128]{2,1,0:T(8,128)(2,1)S(1)} %pad_maximum_fusion.packed.refs_0_), channel_id=1, source_target_pairs={{0,24},{8,16},{16,8},{24,0},{1,25},{9,17},{17,9},{25,1},{2,26},{10... | collective-permute-start | bytes 196616 | tf_op jit(solution)/shard_map/ppermute | solution.py:413
  10.7 5.9 %collective-permute-start.3 = (bf16[2,128,128]{2,1,0:T(8,128)(2,1)S(1)}, bf16[2,128,128]{2,1,0:T(8,128)(2,1)S(1)}, u32[]{:S(2)}, u32[]{:S(2)}) collective-permute-start(bf16[2,128,128]{2,1,0:T(8,128)(2,1)S(1)} %pad_maximum_fusion.packed.refs_0_), channel_id=1, source_target_pairs={{0,16},{8,24},{16,0},{24,8},{1,17},{9,25},{17,1},{25,9},{2,18},{10... | collective-permute-start | bytes 196616 | tf_op jit(solution)/shard_map/ppermute | solution.py:413
  11.7 1.4 %copy-start.4 = (s32[8]{0:T(128)S(1)}, s32[8]{0:T(128)}, u32[]{:S(2)}) copy-start(s32[8]{0:T(128)} %levels.1) | copy-start | bytes 100
  11.7 1.4 %copy-start.5 = (s32[4]{0:T(128)S(1)}, s32[4]{0:T(128)}, u32[]{:S(2)}) copy-start(s32[4]{0:T(128)} %clips.1) | copy-start | bytes 52
  13.8 4.3 %collective-permute-start.4 = (bf16[2,128,128]{2,1,0:T(8,128)(2,1)S(1)}, bf16[2,128,128]{2,1,0:T(8,128)(2,1)S(1)}, u32[]{:S(2)}, u32[]{:S(2)}) collective-permute-start(bf16[2,128,128]{2,1,0:T(8,128)(2,1)S(1)} %pad_maximum_fusion.packed.refs_0_), channel_id=1, source_target_pairs={{0,8},{8,0},{16,24},{24,16},{1,9},{9,1},{17,25},{25,17},{2,10},{10... | collective-permute-start | bytes 196616 | tf_op jit(solution)/shard_map/ppermute | solution.py:413
  14.4 2.3 %copy-start = (bf16[1024,128]{1,0:T(8,128)(2,1)S(1)}, bf16[1024,128]{1,0:T(8,128)(2,1)}, u32[]{:S(2)}) copy-start(bf16[1024,128]{1,0:T(8,128)(2,1)} %keys.7) | copy-start | bytes 786436
  15.2 17.5 %copy-start.2 = (bf16[1024,128]{1,0:T(8,128)(2,1)S(1)}, bf16[1024,128]{1,0:T(8,128)(2,1)}, u32[]{:S(2)}) copy-start(bf16[1024,128]{1,0:T(8,128)(2,1)} %values.3) | copy-start | bytes 786436
  15.2 3.4 %collective-permute-start.8 = (f32[128,128]{1,0:T(8,128)S(1)}, f32[128,128]{1,0:T(8,128)S(1)}, u32[]{:S(2)}, u32[]{:S(2)}) collective-permute-start(f32[128,128]{1,0:T(8,128)S(1)} %get-tuple-element.55), channel_id=1, source_target_pairs={{0,1},{1,0},{2,3},{3,2},{4,5},{5,4},{6,7},{7,6},{8,9},{9,8},{10,11... | collective-permute-start | bytes 196616 | tf_op jit(solution)/shard_map/ppermute | solution.py:410
  18.7 6.9 %collective-permute-start.10 = (bf16[352,128]{1,0:T(8,128)(2,1)S(1)}, bf16[352,128]{1,0:T(8,128)(2,1)S(1)}, u32[]{:S(2)}, u32[]{:S(2)}) collective-permute-start(bf16[352,128]{1,0:T(8,128)(2,1)S(1)} %get-tuple-element.61), channel_id=1, source_target_pairs={{0,24},{8,16},{16,8},{24,0},{1,25},{9,17},{17,9},{25,1},{2,26},{10... | collective-permute-start | bytes 270344 | tf_op jit(solution)/shard_map/ppermute | solution.py:413
  21.2 7.8 %collective-permute-start.11 = (bf16[352,128]{1,0:T(8,128)(2,1)S(1)}, bf16[352,128]{1,0:T(8,128)(2,1)S(1)}, u32[]{:S(2)}, u32[]{:S(2)}) collective-permute-start(bf16[352,128]{1,0:T(8,128)(2,1)S(1)} %get-tuple-element.62), channel_id=1, source_target_pairs={{0,16},{8,24},{16,0},{24,8},{1,17},{9,25},{17,1},{25,9},{2,18},{10... | collective-permute-start | bytes 270344 | tf_op jit(solution)/shard_map/ppermute | solution.py:413
  21.8 7.3 %collective-permute-start.9 = (bf16[352,128]{1,0:T(8,128)(2,1)S(1)}, bf16[352,128]{1,0:T(8,128)(2,1)S(1)}, u32[]{:S(2)}, u32[]{:S(2)}) collective-permute-start(bf16[352,128]{1,0:T(8,128)(2,1)S(1)} %get-tuple-element.60), channel_id=1, source_target_pairs={{0,8},{8,0},{16,24},{24,16},{1,9},{9,1},{17,25},{25,17},{2,10},{10... | collective-permute-start | bytes 270344 | tf_op jit(solution)/shard_map/ppermute | solution.py:413
  29.1 11.1 %collective-permute-start.12 = (bf16[800,128]{1,0:T(8,128)(2,1)S(1)}, bf16[800,128]{1,0:T(8,128)(2,1)S(1)}, u32[]{:S(2)}, u32[]{:S(2)}) collective-permute-start(bf16[800,128]{1,0:T(8,128)(2,1)S(1)} %shard_map.134.refs_0_), channel_id=1, source_target_pairs={{0,6},{1,7},{2,4},{3,5},{4,2},{5,3},{6,0},{7,1},{8,14},{9,15},{10,... | collective-permute-start | bytes 614408 | tf_op jit(solution)/shard_map/ppermute | solution.py:406
  31.6 9.2 %collective-permute-start.13 = (bf16[800,128]{1,0:T(8,128)(2,1)S(1)}, bf16[800,128]{1,0:T(8,128)(2,1)S(1)}, u32[]{:S(2)}, u32[]{:S(2)}) collective-permute-start(bf16[800,128]{1,0:T(8,128)(2,1)S(1)} %shard_map.134.refs_0_), channel_id=1, source_target_pairs={{0,4},{1,5},{2,6},{3,7},{4,0},{5,1},{6,2},{7,3},{8,12},{9,13},{10,... | collective-permute-start | bytes 614408 | tf_op jit(solution)/shard_map/ppermute | solution.py:406
  32.1 8.8 %collective-permute-start.14 = (bf16[800,128]{1,0:T(8,128)(2,1)S(1)}, bf16[800,128]{1,0:T(8,128)(2,1)S(1)}, u32[]{:S(2)}, u32[]{:S(2)}) collective-permute-start(bf16[800,128]{1,0:T(8,128)(2,1)S(1)} %shard_map.134.refs_0_), channel_id=1, source_target_pairs={{0,2},{1,3},{2,0},{3,1},{4,6},{5,7},{6,4},{7,5},{8,10},{9,11},{10,... | collective-permute-start | bytes 614408 | tf_op jit(solution)/shard_map/ppermute | solution.py:406
  33.7 4.9 %collective-permute-start.15 = (bf16[128,128]{1,0:T(8,128)(2,1)S(1)}, bf16[128,128]{1,0:T(8,128)(2,1)S(1)}, u32[]{:S(2)}, u32[]{:S(2)}) collective-permute-start(bf16[128,128]{1,0:T(8,128)(2,1)S(1)} %get-tuple-element.74), channel_id=1, source_target_pairs={{0,16},{8,24},{16,0},{24,8},{1,17},{9,25},{17,1},{25,9},{2,18},{10... | collective-permute-start | bytes 98312 | tf_op jit(solution)/shard_map/ppermute | solution.py:413
  34.5 5.7 %collective-permute-start.16 = (bf16[128,128]{1,0:T(8,128)(2,1)S(1)}, bf16[128,128]{1,0:T(8,128)(2,1)S(1)}, u32[]{:S(2)}, u32[]{:S(2)}) collective-permute-start(bf16[128,128]{1,0:T(8,128)(2,1)S(1)} %get-tuple-element.75), channel_id=1, source_target_pairs={{0,24},{8,16},{16,8},{24,0},{1,25},{9,17},{17,9},{25,1},{2,26},{10... | collective-permute-start | bytes 98312 | tf_op jit(solution)/shard_map/ppermute | solution.py:413
  41.0 2.3 %collective-permute-start.17 = (bf16[2880,128]{1,0:T(8,128)(2,1)S(1)}, bf16[2880,128]{1,0:T(8,128)(2,1)S(1)}, u32[]{:S(2)}, u32[]{:S(2)}) collective-permute-start(bf16[2880,128]{1,0:T(8,128)(2,1)S(1)} %shard_map.138.own), channel_id=1, source_target_pairs={{0,1},{1,0},{2,3},{3,2},{4,5},{5,4},{6,7},{7,6},{8,9},{9,8},{10,11... | collective-permute-start | bytes 2211848 | tf_op jit(solution)/shard_map/ppermute | solution.py:410
  41.1 4.0 %collective-permute-start.18 = (bf16[128,128]{1,0:T(8,128)(2,1)S(1)}, bf16[128,128]{1,0:T(8,128)(2,1)S(1)}, u32[]{:S(2)}, u32[]{:S(2)}) collective-permute-start(bf16[128,128]{1,0:T(8,128)(2,1)S(1)} %get-tuple-element.84), channel_id=1, source_target_pairs={{0,8},{8,0},{16,24},{24,16},{1,9},{9,1},{17,25},{25,17},{2,10},{10... | collective-permute-start | bytes 98312 | tf_op jit(solution)/shard_map/ppermute | solution.py:413
  (1 other events, 0.9 us)
